TPU v7x, 32 devices: a whole 2x2x4 slice. The times are simulated.
32 devices in a mesh: grp: 2 (over x), row: 16 (over z, y, core).
Axes of the slice: x: 2, y: 2, z: 4, core: 2. Of those that a mesh axis runs over, the one named last changes fastest.
Arguments:
- q_latent: bfloat16 [128, 1536], P(('grp', 'row')), parts along dimension 0, may hold values from -96 to 96
- new_latent: bfloat16 [128, 576], P(('grp', 'row')), parts along dimension 0, may hold values from -18 to 18
- cache: bfloat16 [128, 1536, 576], P(('grp', 'row')), parts along dimension 0, may hold values from -6 to 6
- lengths: int32 [128], P(('grp', 'row')), parts along dimension 0, may hold values from 128 to 1536, as said below
- w_uq: bfloat16 [1536, 24576], P(None, 'row'), may hold values from -0.15625 to 0.15625
- w_uk: bfloat16 [128, 128, 512], P('row'), may hold values from -0.5 to 0.5
- w_uv: bfloat16 [128, 512, 128], P('row'), may hold values from -0.25 to 0.25
- w_o: bfloat16 [16384, 7168], P('row'), may hold values from -0.046875 to 0.046875
Outputs:
- attended: bfloat16 [128, 7168], P(('grp', 'row')), parts along dimension 0
There are 2 independent parts, one for each index of `grp`. A program takes and returns all parts, laid end to end along the dimension named above; an argument that names none is the same for every part. Nothing has to cross between parts.
Inputs may be any that keep to these rules, and one draw needn't show every extreme that they name: `lengths`: each is a multiple of 128.
All inputs are finite; a program needn't handle non-finite values.
Results may differ from a plain program's by a relative error of at most 0.013.
The roundings to bfloat16 on the way count: a program that leaves them out, or rounds other values in their place, can miss the bound.
Values may be sent and summed in bfloat16 or wider, within the bound.
No kernel may reach another device: no remote copies, remote signals or barrier semaphores. Data moves between devices by JAX's collectives and lax.ppermute only.
A program may use at most 128 MiB of HBM per device.

v0:
```python
import math

import jax
import jax.numpy as jnp
from jax import lax
from jax.sharding import PartitionSpec as P

LAT = 512
ROPE = 64
NOPE = 128
VD = 128
KBLK = 512


def rotate(pe_part, lengths):
    half = pe_part.shape[-1] // 2
    steps = jnp.arange(half, dtype=jnp.float32)
    frequency = jnp.exp(steps * (-math.log(10000.0) / half))
    angles = lengths.astype(jnp.float32)[:, None] * frequency[None, :]
    cosine = jnp.cos(angles)[:, None, :]
    sine_part = jnp.sin(angles)[:, None, :]
    values_in = pe_part.astype(jnp.float32)
    first_half = values_in[..., :half]
    second_half = values_in[..., half:]
    joined = jnp.concatenate(
        [
            first_half * cosine - second_half * sine_part,
            second_half * cosine + first_half * sine_part,
        ],
        axis=-1,
    )
    return joined.astype(jnp.bfloat16)


def on_device(q_latent, new_latent, cache, lengths, w_uq, w_uk, w_uv, w_o):
    heads_here = w_uk.shape[0]
    head_width = NOPE + ROPE
    factor = head_width ** (-0.5)
    piece = lax.all_gather(q_latent, "row", axis=0, tiled=True)
    row_count = piece.shape[0]
    projected = jnp.dot(piece, w_uq, preferred_element_type=jnp.float32).astype(jnp.bfloat16)
    projected = projected.reshape(row_count, heads_here, head_width)
    absorbed = jnp.einsum(
        "rhn,hnc->rhc", projected[..., :NOPE], w_uk, preferred_element_type=jnp.float32
    ).astype(jnp.bfloat16)
    queries = jnp.concatenate([absorbed, projected[..., NOPE:]], axis=-1)
    owner_query = lax.all_to_all(queries, "row", split_axis=0, concat_axis=1, tiled=True)
    owner_query = jnp.concatenate(
        [owner_query[..., :LAT], rotate(owner_query[..., LAT:], lengths)], axis=-1
    )
    rows_here = cache.shape[0]
    maxlen = cache.shape[1]
    heads_all = owner_query.shape[1]
    block_count = maxlen // KBLK

    def score_pass(index, buffer):
        first_key = index * KBLK
        key_block = lax.dynamic_slice_in_dim(cache, first_key, KBLK, 1)
        block_scores = (
            jnp.einsum("rhc,rtc->rht", owner_query, key_block, preferred_element_type=jnp.float32)
            * factor
        )
        position = first_key + jnp.arange(KBLK)
        block_scores = jnp.where(
            position[None, None, :] < lengths[:, None, None], block_scores, -jnp.inf
        )
        return lax.dynamic_update_slice_in_dim(buffer, block_scores, first_key, 2)

    scores = lax.fori_loop(
        0, block_count, score_pass, jnp.full((rows_here, heads_all, maxlen), -jnp.inf, jnp.float32)
    )
    own = (
        jnp.einsum("rhc,rc->rh", owner_query, new_latent, preferred_element_type=jnp.float32)
        * factor
    )
    peak = jnp.maximum(jnp.max(scores, axis=-1), own)
    expo = jnp.exp(scores - peak[..., None])
    own_expo = jnp.exp(own - peak)
    total = jnp.sum(expo, axis=-1) + own_expo
    weights = (expo / total[..., None]).astype(jnp.bfloat16)
    own_weight = (own_expo / total).astype(jnp.bfloat16)

    def value_pass(index, summed):
        first_key = index * KBLK
        key_block = lax.dynamic_slice_in_dim(cache, first_key, KBLK, 1)
        weight_block = lax.dynamic_slice_in_dim(weights, first_key, KBLK, 2)
        return summed + jnp.einsum(
            "rht,rtc->rhc", weight_block, key_block[..., :LAT], preferred_element_type=jnp.float32
        )

    summed = lax.fori_loop(
        0, block_count, value_pass, jnp.zeros((rows_here, heads_all, LAT), jnp.float32)
    )
    summed = summed + own_weight.astype(jnp.float32)[..., None] * new_latent[:, None, :LAT].astype(
        jnp.float32
    )
    latent_out = summed.astype(jnp.bfloat16)
    head_latent = lax.all_to_all(latent_out, "row", split_axis=1, concat_axis=0, tiled=True)
    values = jnp.einsum(
        "rhc,hcv->rhv", head_latent, w_uv, preferred_element_type=jnp.float32
    ).astype(jnp.bfloat16)
    values = values.reshape(values.shape[0], heads_here * VD)
    partial_terms = jnp.dot(values, w_o, preferred_element_type=jnp.float32)
    attended = lax.psum_scatter(partial_terms, "row", scatter_dimension=0, tiled=True)
    return attended.astype(jnp.bfloat16)


def solution(mesh):
    placed = (
        P(("grp", "row"), None),
        P(("grp", "row"), None),
        P(("grp", "row"), None, None),
        P(("grp", "row")),
        P(None, "row"),
        P("row", None, None),
        P("row", None, None),
        P("row", None),
    )
    return jax.shard_map(
        on_device, mesh=mesh, in_specs=placed, out_specs=P(("grp", "row"), None), check_vma=False
    )
```

profile of v0, /device:TPU:0, one launch (start us, length us, event | category | flops | bytes accessed | tf_op | source)
XLA Modules:
  0.0 186.6 jit_solution(14958461425533161721)
XLA Ops:
  0.0 24.0 %all-gather = bf16[16,4,1536]{2,1,0:T(4,128)(2,1)S(1)} all-gather(bf16[1,4,1536]{2,1,0:T(4,128)(2,1)} %bitcast.49), channel_id=1, replica_groups=mesh['grp'=2,'row'=16] {'row'}, dimensions={0}, use_global_device_ids=true | all-gather | bytes 208896 | tf_op jit(solution)/shard_map/all_gather | solution.py:39
  24.0 3.3 %convolution_convert_fusion = bf16[64,1536]{1,0:T(8,128)(2,1)S(1)} fusion(bf16[64,1536]{1,0:T(8,128)(2,1)S(1)} %reshape.99, bf16[1536,1536]{1,0:T(8,128)(2,1)} %param.16), kind=kOutput, calls=%fused_computation.17 | convolution fusion | flops 302088192 | bytes 5111808 | tf_op jit(solution)/shard_map/dot_general | solution.py:41
  27.3 0.2 reshape.96
  27.6 0.3 fusion.23
  28.0 1.2 copy.37
  29.2 3.6 %all-to-all-start = ((bf16[64,8,576]{2,1,0:T(8,128)(2,1)}), bf16[64,8,576]{2,1,0:T(8,128)(2,1)S(1)}, u32[]{:S(2)}, u32[]{:S(2)}) async-start(bf16[64,8,576]{2,1,0:T(8,128)(2,1)} %copy.37), calls=%async_computation | async-start | bytes 1310720 | tf_op jit(solution)/shard_map/all_to_all | solution.py:47
  33.0 16.4 %all-to-all-done = bf16[64,8,576]{2,1,0:T(8,128)(2,1)S(1)} async-done(((bf16[64,8,576]{2,1,0:T(8,128)(2,1)}), bf16[64,8,576]{2,1,0:T(8,128)(2,1)S(1)}, u32[]{:S(2)}, u32[]{:S(2)}) %all-to-all-start) | async-done | bytes 589856 | tf_op jit(solution)/shard_map/all_to_all | solution.py:47
  49.5 0.1 subtract_convert_fusion
  49.8 0.3 copy.39
  50.1 1.9 broadcast_in_dim.47
  52.0 11.4 %while.27 = (s32[]{:T(128)}, f32[4,128,1536]{1,2,0:T(8,128)}, s32[4]{0:T(128)S(1)}, bf16[4,1536,576]{1,2,0:T(8,128)(2,1)}, bf16[4,128,576]{1,2,0:T(8,128)(2,1)S(...) while((s32[]{:T(128)}, f32[4,128,1536]{1,2,0:T(8,128)}, s32[4]{0:T(128)S(1)}, ...), condition=%wide.region_1.2_spmd, body=%wide.region_0.1_spmd.sunk | while | flops 302516736 | bytes 4007071 | solution.py:69
  52.1 3.7 %fusion.50 = f32[4,128,1536]{1,2,0:T(8,128)} fusion(f32[4,128,1536]{1,2,0:T(8,128)} %get-tuple-element.316, s32[]{:T(128)S(6)} %select_n.37, bf16[4,128,576]{1,2,0:T(8,128)(2,1)S(1)} %get-tuple-element.328, bf16[4,1536,576]{1,2,0:T(8,128)(2,1)} %get-tuple-element.327, pred[4,512]{1,0:T(4,128)(4,1)S(1)} %broadcast_compare_fusion.2), kind=kOutput, calls=%fused_computation.5.clone.1 | convolution fusion | flops 302514176 | bytes 4000768 | tf_op jit(solution)/shard_map/while/body/eval_jaxpr/rhc,rtc->rht/dot_general | solution.py:60
  55.8 3.7 %fusion.50 = f32[4,128,1536]{1,2,0:T(8,128)} fusion(f32[4,128,1536]{1,2,0:T(8,128)} %get-tuple-element.316, s32[]{:T(128)S(6)} %select_n.37, bf16[4,128,576]{1,2,0:T(8,128)(2,1)S(1)} %get-tuple-element.328, bf16[4,1536,576]{1,2,0:T(8,128)(2,1)} %get-tuple-element.327, pred[4,512]{1,0:T(4,128)(4,1)S(1)} %broadcast_compare_fusion.2), kind=kOutput, calls=%fused_computation.5.clone.1 | convolution fusion | flops 302514176 | bytes 4000768 | tf_op jit(solution)/shard_map/while/body/eval_jaxpr/rhc,rtc->rht/dot_general | solution.py:60
  59.7 3.7 %fusion.50 = f32[4,128,1536]{1,2,0:T(8,128)} fusion(f32[4,128,1536]{1,2,0:T(8,128)} %get-tuple-element.316, s32[]{:T(128)S(6)} %select_n.37, bf16[4,128,576]{1,2,0:T(8,128)(2,1)S(1)} %get-tuple-element.328, bf16[4,1536,576]{1,2,0:T(8,128)(2,1)} %get-tuple-element.327, pred[4,512]{1,0:T(4,128)(4,1)S(1)} %broadcast_compare_fusion.2), kind=kOutput, calls=%fused_computation.5.clone.1 | convolution fusion | flops 302514176 | bytes 4000768 | tf_op jit(solution)/shard_map/while/body/eval_jaxpr/rhc,rtc->rht/dot_general | solution.py:60
  63.4 2.1 %reduce_max.9 = f32[4,128]{1,0:T(4,128)S(1)} reduce(f32[4,128,1536]{1,2,0:T(8,128)} %get-tuple-element.178, f32[]{:T(128)} %constant.77.clone.1), dimensions={2}, to_apply=%region_2.3 | reduce | flops 785920 | bytes 3147780 | tf_op jit(solution)/shard_map/reduce_max | solution.py:76
  65.5 3.6 %copy.40 = f32[4,128,1536]{2,1,0:T(8,128)} copy(f32[4,128,1536]{1,2,0:T(8,128)} %get-tuple-element.178) | data formatting | bytes 6291456 | tf_op jit(solution)/shard_map/while | solution.py:69
  69.1 0.3 fusion.30
  69.4 2.6 %fusion.22 = f32[4,128]{1,0:T(4,128)S(1)} fusion(f32[4,128,1536]{2,1,0:T(8,128)} %copy.40, f32[4,128]{1,0:T(4,128)S(1)} %multiply_maximum_fusion), kind=kLoop, calls=%fused_computation.16 | loop fusion | flops 1572352 | bytes 3149824 | tf_op jit(solution)/shard_map/reduce_sum | solution.py:79
  72.1 1.7 divide_convert_fusion
  73.8 8.2 %while.28 = (s32[]{:T(128)}, f32[4,128,512]{2,1,0:T(8,128)S(1)}, bf16[4,128,1536]{2,1,0:T(8,128)(2,1)}, bf16[4,1536,576]{1,2,0:T(8,128)(2,1)}, s32[]{:T(128)}, /*index=5*/s32[]{:T(128)}, s32[]{:T(128)}, s32[]{:T(128)}) while((s32[]{:T(128)}, f32[4,128,512]{2,1,0:T(8,128)S(1)}, bf16[4,128,1536]{2,1,0:T(8,128)(2,1)}, ...), condition=%wide.region_5.6_spmd.clone, body=%wide.region_4.5_spmd.clone.sunk | while | flops 268959744 | bytes 4720268 | solution.py:91
  73.8 2.7 %fusion.53 = f32[4,128,512]{2,1,0:T(8,128)S(1)} fusion(bf16[4,1536,576]{1,2,0:T(8,128)(2,1)} %get-tuple-element.352, s32[]{:T(128)S(6)} %select_n.38, f32[4,128,512]{2,1,0:T(8,128)S(1)} %get-tuple-element.342, bf16[4,128,1536]{2,1,0:T(8,128)(2,1)} %get-tuple-element.351, pred[]{:T(512)S(6)} %compare.3), kind=kOutput, calls=%fused_computation.11.clone.1 | convolution fusion | flops 268959744 | bytes 4720128 | tf_op jit(solution)/shard_map/while/body/eval_jaxpr/rht,rtc->rhc/dot_general | solution.py:87
  76.6 2.7 %fusion.53 = f32[4,128,512]{2,1,0:T(8,128)S(1)} fusion(bf16[4,1536,576]{1,2,0:T(8,128)(2,1)} %get-tuple-element.352, s32[]{:T(128)S(6)} %select_n.38, f32[4,128,512]{2,1,0:T(8,128)S(1)} %get-tuple-element.342, bf16[4,128,1536]{2,1,0:T(8,128)(2,1)} %get-tuple-element.351, pred[]{:T(512)S(6)} %compare.3), kind=kOutput, calls=%fused_computation.11.clone.1 | convolution fusion | flops 268959744 | bytes 4720128 | tf_op jit(solution)/shard_map/while/body/eval_jaxpr/rht,rtc->rhc/dot_general | solution.py:87
  79.3 2.7 %fusion.53 = f32[4,128,512]{2,1,0:T(8,128)S(1)} fusion(bf16[4,1536,576]{1,2,0:T(8,128)(2,1)} %get-tuple-element.352, s32[]{:T(128)S(6)} %select_n.38, f32[4,128,512]{2,1,0:T(8,128)S(1)} %get-tuple-element.342, bf16[4,128,1536]{2,1,0:T(8,128)(2,1)} %get-tuple-element.351, pred[]{:T(512)S(6)} %compare.3), kind=kOutput, calls=%fused_computation.11.clone.1 | convolution fusion | flops 268959744 | bytes 4720128 | tf_op jit(solution)/shard_map/while/body/eval_jaxpr/rht,rtc->rhc/dot_general | solution.py:87
  82.2 1.5 fusion.25
  83.7 4.7 %all-to-all-start.1 = ((bf16[4,128,512]{2,0,1:T(4,128)(2,1)}), bf16[4,128,512]{2,0,1:T(4,128)(2,1)S(1)}, u32[]{:S(2)}, u32[]{:S(2)}) async-start(bf16[4,128,512]{2,0,1:T(4,128)(2,1)} %fusion.25), calls=%async_computation.1 | async-start | bytes 1048576 | tf_op jit(solution)/shard_map/all_to_all | solution.py:98
  88.5 0.6 dynamic-slice
  89.7 13.2 %all-to-all-done.1 = bf16[4,128,512]{2,0,1:T(4,128)(2,1)S(1)} async-done(((bf16[4,128,512]{2,0,1:T(4,128)(2,1)}), bf16[4,128,512]{2,0,1:T(4,128)(2,1)S(1)}, u32[]{:S(2)}, u32[]{:S(2)}) %all-to-all-start.1) | async-done | bytes 524320 | tf_op jit(solution)/shard_map/all_to_all | solution.py:98
  102.9 0.2 copy.67
  103.2 0.3 fusion.24
  103.6 7.9 %fusion.26 = f32[64,7168]{1,0:T(8,128)S(1)} fusion(bf16[1024,7168]{1,0:T(8,128)(2,1)} %param.19, bf16[8,8,8,128]{3,2,1,0:T(8,128)(2,1)S(1)} %fusion.24), kind=kOutput, calls=%fused_computation.30 | convolution fusion | flops 939524096 | bytes 16646144 | tf_op jit(solution)/shard_map/dot_general | solution.py:103
  111.5 73.6 %all-reduce.2 = bf16[64,7168]{1,0:T(8,128)(2,1)} all-reduce(f32[64,7168]{1,0:T(8,128)S(1)} %fusion.26), channel_id=2, replica_groups=mesh['grp'=2,'row'=16] {'row'}, use_global_device_ids=true, to_apply=%region_6.7.clone | all-reduce | flops 458752 | bytes 2752512
  185.1 1.6 dynamic-slice_convert_fusion
  (36 shorter events, 1.1 us)
Async XLA Ops:
  0.0 27.6 %copy-start = (bf16[8,128,512]{2,1,0:T(8,128)(2,1)S(1)}, bf16[8,128,512]{2,1,0:T(8,128)(2,1)}, u32[]{:S(2)}) copy-start(bf16[8,128,512]{2,1,0:T(8,128)(2,1)} %param.17) | copy-start | bytes 3145732
  27.6 5.3 %copy-start.4 = (s32[4]{0:T(128)S(1)}, s32[4]{0:T(128)}, u32[]{:S(2)}) copy-start(s32[4]{0:T(128)} %param.15) | copy-start | bytes 52
  27.6 5.4 %copy-start.3 = (bf16[4,576]{1,0:T(4,128)(2,1)S(1)}, bf16[4,576]{1,0:T(4,128)(2,1)}, u32[]{:S(2)}) copy-start(bf16[4,576]{1,0:T(4,128)(2,1)} %param.13) | copy-start | bytes 13828
  29.2 20.2 %all-to-all-start = ((bf16[64,8,576]{2,1,0:T(8,128)(2,1)}), bf16[64,8,576]{2,1,0:T(8,128)(2,1)S(1)}, u32[]{:S(2)}, u32[]{:S(2)}) async-start(bf16[64,8,576]{2,1,0:T(8,128)(2,1)} %copy.37), calls=%async_computation | async-start | bytes 1310720 | tf_op jit(solution)/shard_map/all_to_all | solution.py:47
  69.1 3.0 %copy-start.1 = (f32[4,128,1536]{2,1,0:T(8,128)S(1)}, f32[4,128,1536]{2,1,0:T(8,128)}, u32[]{:S(2)}) copy-start(f32[4,128,1536]{2,1,0:T(8,128)} %copy.40) | copy-start | bytes 9437188
  73.8 14.7 %copy-start.5 = (u32[32]{0:T(128)S(1)}, u32[32]{0:T(128)}, u32[]{:S(2)}) copy-start(u32[32]{0:T(128)} %constant.88) | copy-start | bytes 388
  82.0 21.2 %copy-start.2 = (bf16[8,512,128]{2,1,0:T(8,128)(2,1)S(1)}, bf16[8,512,128]{2,1,0:T(8,128)(2,1)}, u32[]{:S(2)}) copy-start(bf16[8,512,128]{2,1,0:T(8,128)(2,1)} %param.18) | copy-start | bytes 3145732
  83.7 19.2 %all-to-all-start.1 = ((bf16[4,128,512]{2,0,1:T(4,128)(2,1)}), bf16[4,128,512]{2,0,1:T(4,128)(2,1)S(1)}, u32[]{:S(2)}, u32[]{:S(2)}) async-start(bf16[4,128,512]{2,0,1:T(4,128)(2,1)} %fusion.25), calls=%async_computation.1 | async-start | bytes 1048576 | tf_op jit(solution)/shard_map/all_to_all | solution.py:98
where the time goes:
time: 187 us
  blocking collectives  97.6 us (52%)
  matrix products  31.4 us (17%)
  waiting for transfers between devices  29.6 us (16%)
  local copies, waits for them, and re-layouts  9.96 us (5%)
  other arithmetic  8.76 us (5%)
  starting transfers between devices  8.32 us (4%)
    unnamed x1, blocking collectives  73.6 us
    all_gather x1, blocking collectives, on_device(): piece = lax.all_gather(q_latent, 'row', axis=0, tiled=True)  24 us
    all_to_all x1, waiting for transfers between devices, on_device(): lax.all_to_all(queries, 'row', split_axis=0, concat_axis=1, tiled=True)  16.4 us
    all_to_all x1, waiting for transfers between devices, on_device(): lax.all_to_all(latent_out, 'row', split_axis=1, concat_axis=0, tiled=True)  13.2 us
    dot_general x3, matrix products, score_pass(): jnp.einsum('rhc,rtc->rht', owner_query, key_block, preferred_element_type...  11.2 us
    dot_general x3, matrix products, value_pass(): jnp.einsum('rht,rtc->rhc', weight_block, key_block[..., :LAT], preferred_...  8.17 us
    dot_general x1, matrix products, on_device(): partial_terms = jnp.dot(values, w_o, preferred_element_type=jnp.float32)  7.91 us
    all_to_all x1, starting transfers between devices, on_device(): lax.all_to_all(latent_out, 'row', split_axis=1, concat_axis=0, tiled=True)  4.73 us
  transfers between devices with their start and end apart: 2, of which 2 were waited for; matrix products, arithmetic and copies ran while one was open for 0% of the time, Pallas kernels for 0%

commit v1 on v0

v1 whole, which is shorter than its diff:
```python
import functools
import math

import jax
import jax.numpy as jnp
from jax import lax
from jax.experimental import pallas as pl
from jax.experimental.pallas import tpu as pltpu
from jax.sharding import PartitionSpec as P

LAT = 512
ROPE = 64
NOPE = 128
VD = 128
LANES = 128
FACTOR = (NOPE + ROPE) ** -0.5


def resident(x):
    return pltpu.with_memory_space_constraint(x, pltpu.VMEM)


def in_vmem():
    return pl.BlockSpec(memory_space=pltpu.VMEM)


def project_kernel(q_ref, wq_ref, wk_ref, out_ref, lat_ref, rot_ref):
    heads = wk_ref.shape[0]
    devices = out_ref.shape[0]
    count = q_ref.shape[0]
    rows = count // devices
    wide = rows * heads
    width = NOPE + ROPE
    projected = jnp.dot(q_ref[...], wq_ref[...], preferred_element_type=jnp.float32)
    for h in range(heads):
        mine = projected[:, h * width : (h + 1) * width]
        absorbed = jnp.dot(
            mine[:, :NOPE].astype(jnp.bfloat16), wk_ref[h], preferred_element_type=jnp.float32
        )
        for c in range(LAT // LANES):
            lat_ref[c, pl.ds(h, count, stride=heads), :] = absorbed[:, c * LANES : (c + 1) * LANES]
        pe = mine[:, NOPE:]
        rot_ref[pl.ds(h, count, stride=heads), :] = jnp.concatenate([pe, pe], axis=-1)
    for c in range(LAT // LANES):
        piece = lat_ref[c].reshape(devices, wide, LANES)
        out_ref[:, c * wide : (c + 1) * wide, :] = piece.astype(jnp.bfloat16)
    pair = rot_ref[...].reshape(devices, wide, LANES)
    lane = lax.broadcasted_iota(jnp.int32, (devices, wide // 2, LANES), 2)
    packed = jnp.where(lane < ROPE, pair[:, : wide // 2], pair[:, wide // 2 :])
    out_ref[:, LAT // LANES * wide :, :] = packed.astype(jnp.bfloat16)


def project(piece, w_uq, w_uk, devices):
    count = piece.shape[0]
    heads = w_uk.shape[0]
    wide = count // devices * heads
    return pl.pallas_call(
        project_kernel,
        out_shape=jax.ShapeDtypeStruct((devices, LAT // LANES * wide + wide // 2, LANES), jnp.bfloat16),
        in_specs=[in_vmem()] * 3,
        out_specs=in_vmem(),
        scratch_shapes=[
            pltpu.VMEM((LAT // LANES, count * heads, LANES), jnp.float32),
            pltpu.VMEM((count * heads, LANES), jnp.float32),
        ],
        compiler_params=pltpu.CompilerParams(vmem_limit_bytes=16 * 2**20),
        name="project",
    )(piece, resident(w_uq), resident(w_uk))


def attend_kernel(len_ref, q_ref, key_ref, new_ref, cos_ref, sin_ref, out_ref):
    devices = q_ref.shape[0]
    rows, _, maxlen = key_ref.shape
    wide = out_ref.shape[1]
    heads = wide // rows
    total_heads = devices * heads
    half = ROPE // 2
    pieces = LAT // LANES
    for r in range(rows):
        parts = []
        for c in range(pieces):
            first = c * wide + r * heads
            part = q_ref[:, first : first + heads, :].astype(jnp.float32)
            parts.append(part.reshape(total_heads, LANES))
        latent = jnp.concatenate(parts, axis=-1)
        first = pieces * wide + (r % (rows // 2)) * heads
        pe = q_ref[:, first : first + heads, :].astype(jnp.float32).reshape(total_heads, LANES)
        side = r // (rows // 2) * ROPE
        pe = pe[:, side : side + ROPE]
        swapped = jnp.concatenate([pe[:, half:], pe[:, :half]], axis=-1)
        rotated = (pe * cos_ref[r : r + 1, :] + swapped * sin_ref[r : r + 1, :]).astype(jnp.bfloat16)
        newest = new_ref[r : r + 1, :].astype(jnp.float32)
        own = (
            jnp.sum(latent * newest[:, :LAT], axis=-1, keepdims=True)
            + jnp.sum(rotated.astype(jnp.float32) * newest[:, LAT:], axis=-1, keepdims=True)
        ) * FACTOR
        scores = jnp.dot(
            latent.astype(jnp.bfloat16), key_ref[r, :LAT, :], preferred_element_type=jnp.float32
        )
        scores += jnp.dot(rotated, key_ref[r, LAT:, :], preferred_element_type=jnp.float32)
        position = lax.broadcasted_iota(jnp.int32, (1, maxlen), 1)
        scores = jnp.where(position < len_ref[r], scores * FACTOR, -jnp.inf)
        peak = jnp.maximum(jnp.max(scores, axis=-1, keepdims=True), own)
        expo = jnp.exp(scores - peak)
        own_expo = jnp.exp(own - peak)
        total = jnp.sum(expo, axis=-1, keepdims=True) + own_expo
        weights = (expo / total).astype(jnp.bfloat16)
        own_weight = (own_expo / total).astype(jnp.bfloat16).astype(jnp.float32)
        summed = lax.dot_general(
            weights,
            key_ref[r, :LAT, :],
            (((1,), (1,)), ((), ())),
            preferred_element_type=jnp.float32,
        )
        summed += own_weight * newest[:, :LAT]
        out_ref[:, r * heads : (r + 1) * heads, :] = summed.reshape(devices, heads, LAT).astype(
            jnp.bfloat16
        )


def attend(lengths, queries, keys, new_latent, cosine, sine, heads):
    devices = queries.shape[0]
    rows = keys.shape[0]
    return pl.pallas_call(
        attend_kernel,
        out_shape=jax.ShapeDtypeStruct((devices, rows * heads, LAT), jnp.bfloat16),
        in_specs=[pl.BlockSpec(memory_space=pltpu.SMEM)] + [in_vmem()] * 5,
        out_specs=in_vmem(),
        compiler_params=pltpu.CompilerParams(vmem_limit_bytes=16 * 2**20),
        name="attend",
    )(lengths, queries, resident(keys), new_latent, cosine, sine)


def output_kernel(core_ref, y_ref, wv_ref, wo_ref, mine_ref, other_ref, rows_ref, val_ref, block):
    heads = wv_ref.shape[0]
    devices, wide, _ = y_ref.shape
    core = core_ref[0]
    half = devices // 2 * wide
    for place in range(devices // 2):
        for side in range(2):
            device = 2 * place + (core if side == 0 else 1 - core)
            first = side * half + place * wide
            received = y_ref[device].astype(jnp.float32)
            for c in range(LAT // LANES):
                rows_ref[c, first : first + wide, :] = received[:, c * LANES : (c + 1) * LANES]
    count = devices * wide // heads
    for h in range(heads):
        chosen = jnp.concatenate(
            [rows_ref[c, pl.ds(h, count, stride=heads), :] for c in range(LAT // LANES)],
            axis=-1,
        )
        val_ref[:, h * VD : (h + 1) * VD] = jnp.dot(
            chosen.astype(jnp.bfloat16), wv_ref[h], preferred_element_type=jnp.float32
        ).astype(jnp.bfloat16)

    def step(index, carry):
        columns = pl.ds(pl.multiple_of(index * block, block), block)
        terms = jnp.dot(val_ref[...], wo_ref[:, columns], preferred_element_type=jnp.float32)
        mine_ref[:, columns] = terms[: count // 2]
        other_ref[:, columns] = terms[count // 2 :].astype(jnp.bfloat16)
        return carry

    lax.fori_loop(0, wo_ref.shape[1] // block, step, 0)


def output_terms(core, received, w_uv, w_o):
    devices, wide, _ = received.shape
    heads = w_uv.shape[0]
    count = devices * wide // heads
    depth = w_o.shape[1]
    return pl.pallas_call(
        functools.partial(output_kernel, block=1024),
        out_shape=(
            jax.ShapeDtypeStruct((count // 2, depth), jnp.float32),
            jax.ShapeDtypeStruct((count // 2, depth), jnp.bfloat16),
        ),
        in_specs=[pl.BlockSpec(memory_space=pltpu.SMEM)] + [in_vmem()] * 3,
        out_specs=(in_vmem(), in_vmem()),
        scratch_shapes=[
            pltpu.VMEM((LAT // LANES, devices * wide, LANES), jnp.float32),
            pltpu.VMEM((count, heads * VD), jnp.bfloat16),
        ],
        compiler_params=pltpu.CompilerParams(vmem_limit_bytes=16 * 2**20),
        name="output_terms",
    )(core, received, resident(w_uv), resident(w_o))


def on_device(q_latent, new_latent, cache, lengths, w_uq, w_uk, w_uv, w_o, devices):
    heads = w_uk.shape[0]
    rows = cache.shape[0]
    me = lax.axis_index("row")
    half = ROPE // 2
    frequency = jnp.exp(jnp.arange(half, dtype=jnp.float32) * (-math.log(10000.0) / half))
    angles = lengths.astype(jnp.float32)[:, None] * frequency[None, :]
    cosine = jnp.cos(angles)
    sine = jnp.sin(angles)
    cosine = jnp.concatenate([cosine, cosine], axis=-1)
    sine = jnp.concatenate([-sine, sine], axis=-1)

    copies = jnp.broadcast_to(q_latent[None], (devices,) + q_latent.shape)
    gathered = lax.all_to_all(copies, "row", split_axis=0, concat_axis=0, tiled=True)
    piece = gathered.reshape(devices * rows, -1)

    queries = project(piece, w_uq, w_uk, devices)
    queries = lax.all_to_all(queries, "row", split_axis=0, concat_axis=0, tiled=True)
    keys = jnp.swapaxes(cache, 1, 2)
    latents = attend(lengths, queries, keys, new_latent, cosine, sine, heads)
    latents = lax.all_to_all(latents, "row", split_axis=0, concat_axis=0, tiled=True)

    core = lax.rem(me, 2).astype(jnp.int32).reshape(1)
    mine, other = output_terms(core, latents, w_uv, w_o)
    partner = [(i, i ^ 1) for i in range(devices)]
    summed = mine + lax.ppermute(other, "row", partner).astype(jnp.float32)
    summed = summed.astype(jnp.bfloat16).reshape(devices // 2, rows, -1)
    groups = [list(range(c, devices, 2)) for c in range(2)]
    shares = lax.all_to_all(
        summed, "row", split_axis=0, concat_axis=0, tiled=True, axis_index_groups=groups
    )
    return jnp.sum(shares.astype(jnp.float32), axis=0).astype(jnp.bfloat16)


def solution(mesh):
    placed = (
        P(("grp", "row"), None),
        P(("grp", "row"), None),
        P(("grp", "row"), None, None),
        P(("grp", "row")),
        P(None, "row"),
        P("row", None, None),
        P("row", None, None),
        P("row", None),
    )
    body = functools.partial(on_device, devices=mesh.shape["row"])
    return jax.shard_map(
        body, mesh=mesh, in_specs=placed, out_specs=P(("grp", "row"), None), check_vma=False
    )
```

time: 187 us -> 99.8 us (0.53)
  blocking collectives: 97.6 us -> 33.6 us
  matrix products: 31.4 us -> 0 us
  Pallas kernels: 0 us -> 12 us
  other arithmetic: 8.76 us -> 1.14 us
  local copies, waits for them, and re-layouts: 9.96 us -> 12.8 us
  waiting for transfers between devices: 29.6 us -> 31.5 us
    unnamed x1 -> x0, blocking collectives: 73.6 us -> none
    all_to_all x0 -> x2, blocking collectives: none -> 33.6 us  [the longest x1 17.4 us: on_device(): lax.all_to_all(summed, 'row', split_axis=0, concat_axis=0, tiled=True, ax...]
    dot_general x11 -> x0, matrix products: 31.4 us -> none  [the longest x3 11.2 us: score_pass(): jnp.einsum('rhc,rtc->rht', owner_query, key_block, preferred_element_type...]
    all_gather x1 -> x0, blocking collectives: 24 us -> none  [on_device(): piece = lax.all_gather(q_latent, 'row', axis=0, tiled=True)]
    pallas_call x0 -> x3, Pallas kernels: none -> 12 us  [the longest x1 5.97 us: attend(): pl.pallas_call(attend_kernel, out_shape=jax.ShapeDtypeStruct((devices, ro...]
    unnamed x15 -> x14, local copies, waits for them, and re-layouts: 0.69 us -> 11.7 us
    while x2 -> x0, local copies, waits for them, and re-layouts: 3.88 us -> none  [on_device(): lax.fori_loop(0, block_count, score_pass, jnp.full((rows_here, heads_all,...]
    convert_element_type x6 -> x2, other arithmetic: 3.32 us -> 0.12 us  [the longest x1 0.12 us: on_device(): summed = summed.astype(jnp.bfloat16).reshape(devices // 2, rows, -1)]
  transfers between devices with their start and end apart: 2 -> 3, of which waited for: 2 -> 3; matrix products, arithmetic and copies ran while one was open for 0% -> 0% of each run, Pallas kernels for 0% -> 0%
where the time goes in v1:
time: 99.8 us; the launch traced here: 99.2 us
  blocking collectives  33.6 us (34%)
  waiting for transfers between devices  31.5 us (32%)
  local copies, waits for them, and re-layouts  12.8 us (13%)
  Pallas kernels  12 us (12%)
  starting transfers between devices  8.03 us (8%)
  other arithmetic  1.14 us (1%)
    all_to_all x1, blocking collectives, on_device(): lax.all_to_all(summed, 'row', split_axis=0, concat_axis=0, tiled=True, ax...  17.4 us
    all_to_all x1, blocking collectives, on_device(): lax.all_to_all(copies, 'row', split_axis=0, concat_axis=0, tiled=True)  16.2 us
    all_to_all x1, waiting for transfers between devices, on_device(): lax.all_to_all(queries, 'row', split_axis=0, concat_axis=0, tiled=True)  15.3 us
    all_to_all x1, waiting for transfers between devices, on_device(): lax.all_to_all(latents, 'row', split_axis=0, concat_axis=0, tiled=True)  14.5 us
    unnamed x14, local copies, waits for them, and re-layouts  11.7 us
    pallas_call x1, Pallas kernels, attend(): pl.pallas_call(attend_kernel, out_shape=jax.ShapeDtypeStruct((devices, ro...  5.97 us
    all_to_all x1, starting transfers between devices, on_device(): lax.all_to_all(latents, 'row', split_axis=0, concat_axis=0, tiled=True)  4.37 us
    pallas_call x1, Pallas kernels, output_terms(): pl.pallas_call(functools.partial(output_kernel, block=1024), out_shape=(j...  3.87 us
  transfers between devices with their start and end apart: 3, of which 3 were waited for; matrix products, arithmetic and copies ran while one was open for 0% of the time, Pallas kernels for 0%

profile of v1, /device:TPU:0, one launch (start us, length us, event | category | flops | bytes accessed | tf_op | source)
XLA Modules:
  0.0 99.2 jit_solution(15260079248214147766)
XLA Ops:
  0.0 0.0 copy-start.6
  0.0 0.0 copy-start.5
  0.0 0.8 broadcast_in_dim.2
  0.8 16.2 %all_to_all.20 = bf16[16,4,1536]{2,1,0:T(4,128)(2,1)S(1)} all-to-all(bf16[16,4,1536]{2,1,0:T(4,128)(2,1)S(1)} %broadcast_in_dim.2), channel_id=1, replica_groups=mesh['grp'=2,'row'=16] {'row'}, dimensions={0} | all-to-all | bytes 393216 | tf_op jit(solution)/shard_map/all_to_all | solution.py:201
  17.0 0.1 reshape.17.q_ref
  17.0 0.0 copy-start.2
  17.0 2.3 %copy-done.2 = bf16[1536,1536]{1,0:T(8,128)(2,1)S(1)} copy-done((bf16[1536,1536]{1,0:T(8,128)(2,1)S(1)}, bf16[1536,1536]{1,0:T(8,128)(2,1)}, u32[]{:S(2)}) %copy-start.2) | copy-done | bytes 4718616
  19.4 0.0 copy-start.3
  19.4 1.2 %copy-done.3 = bf16[8,128,512]{2,1,0:T(8,128)(2,1)S(1)} copy-done((bf16[8,128,512]{2,1,0:T(8,128)(2,1)S(1)}, bf16[8,128,512]{2,1,0:T(8,128)(2,1)}, u32[]{:S(2)}) %copy-start.3) | copy-done | bytes 1048600
  20.6 0.0 copy-start.4
  20.6 2.2 %project.1 = bf16[16,144,128]{2,1,0:T(8,128)(2,1)} custom-call(bf16[64,1536]{1,0:T(8,128)(2,1)S(1)} %reshape.17.q_ref, bf16[1536,1536]{1,0:T(8,128)(2,1)S(1)} %copy-done.2, bf16[8,128,512]{2,1,0:T(8,128)(2,1)S(1)} %copy-done.3), custom_call_target="tpu_custom_call" | custom-call | tf_op jit(solution)/shard_map/project/pallas_call | solution.py:57
  22.8 3.6 %all-to-all-start.1 = ((bf16[16,144,128]{2,1,0:T(8,128)(2,1)}), bf16[16,144,128]{2,1,0:T(8,128)(2,1)S(1)}, u32[]{:S(2)}, u32[]{:S(2)}) async-start(bf16[16,144,128]{2,1,0:T(8,128)(2,1)} %project.1), calls=%async_computation.1 | async-start | bytes 1179648 | tf_op jit(solution)/shard_map/all_to_all | solution.py:205
  26.4 0.0 copy-done.6
  26.4 0.1 fusion
  26.5 0.1 pad_maximum_fusion
  26.6 15.3 %all-to-all-done.1.q_ref = bf16[16,144,128]{2,1,0:T(8,128)(2,1)S(1)} async-done(((bf16[16,144,128]{2,1,0:T(8,128)(2,1)}), bf16[16,144,128]{2,1,0:T(8,128)(2,1)S(1)}, u32[]{:S(2)}, u32[]{:S(2)}) %all-to-all-start.1) | async-done | bytes 589856 | tf_op jit(solution)/shard_map/all_to_all | solution.py:205
  41.9 0.0 copy-done.5
  41.9 0.0 copy-start.1
  41.9 3.0 %copy-done.1 = bf16[4,1536,576]{1,2,0:T(8,128)(2,1)S(1)} copy-done((bf16[4,1536,576]{1,2,0:T(8,128)(2,1)S(1)}, bf16[4,1536,576]{1,2,0:T(8,128)(2,1)}, u32[]{:S(2)}) %copy-start.1) | copy-done | bytes 7077912
  44.9 6.0 %attend.1 = bf16[16,32,512]{2,1,0:T(8,128)(2,1)} custom-call(s32[4]{0:T(128)S(1)} %copy-done.6, bf16[16,144,128]{2,1,0:T(8,128)(2,1)S(1)} %all-to-all-done.1.q_ref, bf16[4,576,1536]{2,1,0:T(8,128)(2,1)S(1)} %bitcast.2, bf16[4,576]{1,0:T(4,128)(2,1)S(1)} %copy-done.5, f32[4,64]{1,0:T(4,128)S(1)} %get-tuple-element.12.cos_ref, ...), custom_call_target="tpu_custom_call" | custom-call | tf_op jit(solution)/shard_map/attend/pallas_call | solution.py:124
  50.9 4.4 %all-to-all-start.2 = ((bf16[16,32,512]{2,1,0:T(8,128)(2,1)}), bf16[16,32,512]{2,1,0:T(8,128)(2,1)S(1)}, u32[]{:S(2)}, u32[]{:S(2)}) async-start(bf16[16,32,512]{2,1,0:T(8,128)(2,1)} %attend.1), calls=%async_computation.2 | async-start | bytes 1048576 | tf_op jit(solution)/shard_map/all_to_all | solution.py:208
  55.3 14.5 %all-to-all-done.2.y_ref = bf16[16,32,512]{2,1,0:T(8,128)(2,1)S(1)} async-done(((bf16[16,32,512]{2,1,0:T(8,128)(2,1)}), bf16[16,32,512]{2,1,0:T(8,128)(2,1)S(1)}, u32[]{:S(2)}, u32[]{:S(2)}) %all-to-all-start.2) | async-done | bytes 524320 | tf_op jit(solution)/shard_map/all_to_all | solution.py:208
  69.7 0.0 copy-done.4
  69.7 0.0 copy-start
  69.7 5.2 %copy-done = bf16[1024,7168]{1,0:T(8,128)(2,1)S(1)} copy-done((bf16[1024,7168]{1,0:T(8,128)(2,1)S(1)}, bf16[1024,7168]{1,0:T(8,128)(2,1)}, u32[]{:S(2)}) %copy-start) | copy-done | bytes 14680088
  74.9 3.9 %output_terms.1 = (f32[32,7168]{1,0:T(8,128)S(1)}, bf16[32,7168]{1,0:T(8,128)(2,1)S(1)}) custom-call(s32[1]{0:T(128)} %bitcast.core_ref, bf16[16,32,512]{2,1,0:T(8,128)(2,1)S(1)} %all-to-all-done.2.y_ref, bf16[8,512,128]{2,1,0:T(8,128)(2,1)S(1)} %copy-done.4, bf16[1024,7168]{1,0:T(8,128)(2,1)S(1)} %copy-done), custom_call_target="tpu_custom_call" | custom-call | tf_op jit(solution)/shard_map/output_terms/pallas_call | solution.py:171
  78.8 0.1 collective-permute-start
  78.9 1.8 %collective-permute-done = bf16[32,7168]{1,0:T(8,128)(2,1)S(1)} collective-permute-done((bf16[32,7168]{1,0:T(8,128)(2,1)S(1)}, bf16[32,7168]{1,0:T(8,128)(2,1)S(1)}, u32[]{:S(2)}, u32[]{:S(2)}) %collective-permute-start) | collective-permute-done | bytes 458784 | tf_op jit(solution)/shard_map/ppermute | solution.py:213
  80.7 0.1 add_convert_fusion
  80.8 0.2 reshape.18
  81.0 17.4 %all_to_all.21 = bf16[8,4,7168]{2,1,0:T(4,128)(2,1)S(1)} all-to-all(bf16[8,4,7168]{2,1,0:T(4,128)(2,1)S(1)} %reshape.18), channel_id=1, replica_groups={{0,2,4,6,8,10,12,14},{1,3,5,7,9,11,13,15},{16,18,20,22,24,26,28,30},{17..., dimensions={0} | all-to-all | bytes 917504 | tf_op jit(solution)/shard_map/all_to_all | solution.py:216
  98.4 0.8 reduce_sum.12
  (2 shorter events, 0.0 us)
Async XLA Ops:
  0.0 26.4 %copy-start.6 = (s32[4]{0:T(128)S(1)}, s32[4]{0:T(128)}, u32[]{:S(2)}) copy-start(s32[4]{0:T(128)} %len_ref.1) | copy-start | bytes 52
  0.0 41.9 %copy-start.5 = (bf16[4,576]{1,0:T(4,128)(2,1)S(1)}, bf16[4,576]{1,0:T(4,128)(2,1)}, u32[]{:S(2)}) copy-start(bf16[4,576]{1,0:T(4,128)(2,1)} %new_ref.1) | copy-start | bytes 13828
  17.0 2.3 %copy-start.2 = (bf16[1536,1536]{1,0:T(8,128)(2,1)S(1)}, bf16[1536,1536]{1,0:T(8,128)(2,1)}, u32[]{:S(2)}) copy-start(bf16[1536,1536]{1,0:T(8,128)(2,1)} %wq_ref.1) | copy-start | bytes 14155780
  19.4 1.2 %copy-start.3 = (bf16[8,128,512]{2,1,0:T(8,128)(2,1)S(1)}, bf16[8,128,512]{2,1,0:T(8,128)(2,1)}, u32[]{:S(2)}) copy-start(bf16[8,128,512]{2,1,0:T(8,128)(2,1)} %wk_ref.1) | copy-start | bytes 3145732
  20.6 49.1 %copy-start.4 = (bf16[8,512,128]{2,1,0:T(8,128)(2,1)S(1)}, bf16[8,512,128]{2,1,0:T(8,128)(2,1)}, u32[]{:S(2)}) copy-start(bf16[8,512,128]{2,1,0:T(8,128)(2,1)} %wv_ref.1) | copy-start | bytes 3145732
  22.8 19.1 %all-to-all-start.1 = ((bf16[16,144,128]{2,1,0:T(8,128)(2,1)}), bf16[16,144,128]{2,1,0:T(8,128)(2,1)S(1)}, u32[]{:S(2)}, u32[]{:S(2)}) async-start(bf16[16,144,128]{2,1,0:T(8,128)(2,1)} %project.1), calls=%async_computation.1 | async-start | bytes 1179648 | tf_op jit(solution)/shard_map/all_to_all | solution.py:205
  41.9 3.0 %copy-start.1 = (bf16[4,1536,576]{1,2,0:T(8,128)(2,1)S(1)}, bf16[4,1536,576]{1,2,0:T(8,128)(2,1)}, u32[]{:S(2)}) copy-start(bf16[4,1536,576]{1,2,0:T(8,128)(2,1)} %param.10) | copy-start | bytes 21233668
  50.9 18.8 %all-to-all-start.2 = ((bf16[16,32,512]{2,1,0:T(8,128)(2,1)}), bf16[16,32,512]{2,1,0:T(8,128)(2,1)S(1)}, u32[]{:S(2)}, u32[]{:S(2)}) async-start(bf16[16,32,512]{2,1,0:T(8,128)(2,1)} %attend.1), calls=%async_computation.2 | async-start | bytes 1048576 | tf_op jit(solution)/shard_map/all_to_all | solution.py:208
  69.7 5.2 %copy-start = (bf16[1024,7168]{1,0:T(8,128)(2,1)S(1)}, bf16[1024,7168]{1,0:T(8,128)(2,1)}, u32[]{:S(2)}) copy-start(bf16[1024,7168]{1,0:T(8,128)(2,1)} %wo_ref.1) | copy-start | bytes 44040196
  78.8 1.9 %collective-permute-start = (bf16[32,7168]{1,0:T(8,128)(2,1)S(1)}, bf16[32,7168]{1,0:T(8,128)(2,1)S(1)}, u32[]{:S(2)}, u32[]{:S(2)}) collective-permute-start(bf16[32,7168]{1,0:T(8,128)(2,1)S(1)} %get-tuple-element.8), channel_id=1, source_target_pairs={{0,1},{1,0},{2,3},{3,2},{4,5},{5,4},{6,7},{7,6},{8,9},{9,8},{10,11... | collective-permute-start | bytes 1376264 | tf_op jit(solution)/shard_map/ppermute | solution.py:213

commit v2 on v1

v2 whole, which is shorter than its diff:
```python
import functools
import math

import jax
import jax.numpy as jnp
from jax import lax
from jax.experimental import pallas as pl
from jax.experimental.pallas import tpu as pltpu
from jax.sharding import PartitionSpec as P

LAT = 512
ROPE = 64
NOPE = 128
VD = 128
LANES = 128
PIECES = LAT // LANES
FACTOR = (NOPE + ROPE) ** -0.5
LIMIT = 16 * 2**20


def resident(x):
    return pltpu.with_memory_space_constraint(x, pltpu.VMEM)


def in_vmem():
    return pl.BlockSpec(memory_space=pltpu.VMEM)


def params():
    return pltpu.CompilerParams(vmem_limit_bytes=LIMIT)


def cost(microseconds):
    return pl.CostEstimate(
        flops=int(microseconds * 1.15e9), bytes_accessed=0, transcendentals=0
    )


def project_kernel(devices, *refs):
    q_refs = refs[:devices]
    wq_ref, wk_ref = refs[devices : devices + 2]
    out_refs = refs[devices + 2 : 2 * devices + 2]
    all_ref, lat_ref, rot_ref = refs[2 * devices + 2 :]
    heads = wk_ref.shape[0]
    rows = q_refs[0].shape[0]
    count = devices * rows
    wide = rows * heads
    width = NOPE + ROPE
    for k in range(devices):
        all_ref[k * rows : (k + 1) * rows, :] = q_refs[k][...].astype(jnp.float32)
    projected = jnp.dot(
        all_ref[...].astype(jnp.bfloat16), wq_ref[...], preferred_element_type=jnp.float32
    )
    for h in range(heads):
        mine = projected[:, h * width : (h + 1) * width]
        absorbed = jnp.dot(
            mine[:, :NOPE].astype(jnp.bfloat16), wk_ref[h], preferred_element_type=jnp.float32
        )
        for c in range(PIECES):
            lat_ref[c, pl.ds(h, count, stride=heads), :] = absorbed[:, c * LANES : (c + 1) * LANES]
        pe = mine[:, NOPE:]
        rot_ref[pl.ds(h, count, stride=heads), :] = jnp.concatenate([pe, pe], axis=-1)
    lane = lax.broadcasted_iota(jnp.int32, (wide // 2, LANES), 1)
    for k in range(devices):
        for c in range(PIECES):
            out_refs[k][c * wide : (c + 1) * wide, :] = lat_ref[
                c, k * wide : (k + 1) * wide, :
            ].astype(jnp.bfloat16)
        low = rot_ref[k * wide : k * wide + wide // 2, :]
        high = rot_ref[k * wide + wide // 2 : (k + 1) * wide, :]
        out_refs[k][PIECES * wide :, :] = jnp.where(lane < ROPE, low, high).astype(jnp.bfloat16)


def project(pieces, w_uq, w_uk):
    devices = len(pieces)
    rows, depth = pieces[0].shape
    heads = w_uk.shape[0]
    wide = rows * heads
    block = jax.ShapeDtypeStruct((PIECES * wide + wide // 2, LANES), jnp.bfloat16)
    return pl.pallas_call(
        functools.partial(project_kernel, devices),
        out_shape=[block] * devices,
        in_specs=[in_vmem()] * (devices + 2),
        out_specs=[in_vmem()] * devices,
        scratch_shapes=[
            pltpu.VMEM((devices * rows, depth), jnp.float32),
            pltpu.VMEM((PIECES, devices * wide, LANES), jnp.float32),
            pltpu.VMEM((devices * wide, LANES), jnp.float32),
        ],
        compiler_params=params(),
        cost_estimate=cost(20),
        name="project",
    )(*pieces, resident(w_uq), resident(w_uk))


def attend_kernel(devices, len_ref, *refs):
    q_refs = refs[:devices]
    key_ref, new_ref = refs[devices : devices + 2]
    out_refs = refs[devices + 2 :]
    rows, _, maxlen = key_ref.shape
    wide = out_refs[0].shape[0]
    heads = wide // rows
    half = ROPE // 2

    lane = lax.broadcasted_iota(jnp.int32, (rows, ROPE), 1)
    place = lax.broadcasted_iota(jnp.int32, (rows, ROPE), 0)
    step = jnp.where(lane < half, lane, lane - half).astype(jnp.float32)
    frequency = jnp.exp(step * (-math.log(10000.0) / half))
    length = jnp.zeros((rows, ROPE), jnp.float32)
    for r in range(rows):
        length = jnp.where(place == r, len_ref[r].astype(jnp.float32), length)
    cosine = jnp.cos(length * frequency)
    sine = jnp.sin(length * frequency)
    sine = jnp.where(lane < half, -sine, sine)

    def query_block(first):
        blocks = [ref[first : first + heads, :].astype(jnp.float32) for ref in q_refs]
        return jnp.concatenate(blocks, axis=0)

    for r in range(rows):
        latent = jnp.concatenate(
            [query_block(c * wide + r * heads) for c in range(PIECES)], axis=-1
        )
        pe = query_block(PIECES * wide + (r % (rows // 2)) * heads)
        side = r // (rows // 2) * ROPE
        pe = pe[:, side : side + ROPE]
        swapped = jnp.concatenate([pe[:, half:], pe[:, :half]], axis=-1)
        rotated = (pe * cosine[r : r + 1, :] + swapped * sine[r : r + 1, :]).astype(jnp.bfloat16)
        newest = new_ref[r : r + 1, :].astype(jnp.float32)
        own = (
            jnp.sum(latent * newest[:, :LAT], axis=-1, keepdims=True)
            + jnp.sum(rotated.astype(jnp.float32) * newest[:, LAT:], axis=-1, keepdims=True)
        ) * FACTOR
        scores = jnp.dot(
            latent.astype(jnp.bfloat16), key_ref[r, :LAT, :], preferred_element_type=jnp.float32
        )
        scores += jnp.dot(rotated, key_ref[r, LAT:, :], preferred_element_type=jnp.float32)
        position = lax.broadcasted_iota(jnp.int32, (1, maxlen), 1)
        scores = jnp.where(position < len_ref[r], scores * FACTOR, -jnp.inf)
        peak = jnp.maximum(jnp.max(scores, axis=-1, keepdims=True), own)
        expo = jnp.exp(scores - peak)
        own_expo = jnp.exp(own - peak)
        total = jnp.sum(expo, axis=-1, keepdims=True) + own_expo
        weights = (expo / total).astype(jnp.bfloat16)
        own_weight = (own_expo / total).astype(jnp.bfloat16).astype(jnp.float32)
        summed = lax.dot_general(
            weights,
            key_ref[r, :LAT, :],
            (((1,), (1,)), ((), ())),
            preferred_element_type=jnp.float32,
        )
        summed += own_weight * newest[:, :LAT]
        for k in range(devices):
            out_refs[k][r * heads : (r + 1) * heads, :] = summed[
                k * heads : (k + 1) * heads, :
            ].astype(jnp.bfloat16)


def attend(lengths, queries, keys, new_latent, heads):
    devices = len(queries)
    rows = keys.shape[0]
    block = jax.ShapeDtypeStruct((rows * heads, LAT), jnp.bfloat16)
    return pl.pallas_call(
        functools.partial(attend_kernel, devices),
        out_shape=[block] * devices,
        in_specs=[pl.BlockSpec(memory_space=pltpu.SMEM)] + [in_vmem()] * (devices + 2),
        out_specs=[in_vmem()] * devices,
        compiler_params=params(),
        cost_estimate=cost(20),
        name="attend",
    )(lengths, *queries, resident(keys), new_latent)


def output_kernel(devices, block, *refs):
    y_refs = refs[:devices]
    wv_ref, wo_ref, mine_ref, other_ref, rows_ref, val_ref = refs[devices:]
    heads = wv_ref.shape[0]
    wide = y_refs[0].shape[0]
    for place, k in enumerate([*range(0, devices, 2), *range(1, devices, 2)]):
        received = y_refs[k][...].astype(jnp.float32)
        for c in range(PIECES):
            rows_ref[c, place * wide : (place + 1) * wide, :] = received[:, c * LANES : (c + 1) * LANES]
    count = devices * wide // heads
    for h in range(heads):
        chosen = jnp.concatenate(
            [rows_ref[c, pl.ds(h, count, stride=heads), :] for c in range(PIECES)], axis=-1
        )
        val_ref[:, h * VD : (h + 1) * VD] = jnp.dot(
            chosen.astype(jnp.bfloat16), wv_ref[h], preferred_element_type=jnp.float32
        ).astype(jnp.bfloat16)

    def step(index, carry):
        columns = pl.ds(pl.multiple_of(index * block, block), block)
        terms = jnp.dot(val_ref[...], wo_ref[:, columns], preferred_element_type=jnp.float32)
        mine_ref[:, columns] = terms[: count // 2]
        other_ref[:, columns] = terms[count // 2 :].astype(jnp.bfloat16)
        return carry

    lax.fori_loop(0, wo_ref.shape[1] // block, step, 0)


def output_terms(received, w_uv, w_o):
    devices = len(received)
    wide = received[0].shape[0]
    heads = w_uv.shape[0]
    count = devices * wide // heads
    depth = w_o.shape[1]
    return pl.pallas_call(
        functools.partial(output_kernel, devices, 1024),
        out_shape=(
            jax.ShapeDtypeStruct((count // 2, depth), jnp.float32),
            jax.ShapeDtypeStruct((count // 2, depth), jnp.bfloat16),
        ),
        in_specs=[in_vmem()] * (devices + 2),
        out_specs=(in_vmem(), in_vmem()),
        scratch_shapes=[
            pltpu.VMEM((PIECES, devices * wide, LANES), jnp.float32),
            pltpu.VMEM((count, heads * VD), jnp.bfloat16),
        ],
        compiler_params=params(),
        cost_estimate=cost(20),
        name="output_terms",
    )(*received, resident(w_uv), resident(w_o))


def pair_kernel(rows, mine_ref, other_ref, *out_refs):
    total = mine_ref[...] + other_ref[...].astype(jnp.float32)
    for j, out_ref in enumerate(out_refs):
        out_ref[...] = total[j * rows : (j + 1) * rows].astype(out_ref.dtype)


def pair_sum(mine, other, rows):
    count, depth = mine.shape
    shapes = [jax.ShapeDtypeStruct((rows, depth), jnp.float32)]
    shapes += [jax.ShapeDtypeStruct((rows, depth), jnp.bfloat16)] * (count // rows - 1)
    return pl.pallas_call(
        functools.partial(pair_kernel, rows),
        out_shape=shapes,
        in_specs=[in_vmem()] * 2,
        out_specs=[in_vmem()] * len(shapes),
        compiler_params=params(),
        cost_estimate=cost(1),
        name="pair_sum",
    )(mine, other)


def on_device(q_latent, new_latent, cache, lengths, w_uq, w_uk, w_uv, w_o, devices):
    heads = w_uk.shape[0]
    rows = cache.shape[0]
    def swap(block, k):
        if k == 0:
            return block
        return lax.ppermute(block, "row", [(i, i ^ k) for i in range(devices)])

    pieces = [swap(q_latent, k) for k in range(devices)]
    queries = project(pieces, w_uq, w_uk)
    queries = [swap(block, k) for k, block in enumerate(queries)]
    keys = jnp.swapaxes(cache, 1, 2)
    latents = attend(lengths, queries, keys, new_latent, heads)
    latents = [swap(block, k) for k, block in enumerate(latents)]
    mine, other = output_terms(latents, w_uv, w_o)
    shares = pair_sum(mine, swap(other, 1), rows)
    shares = [swap(block, 2 * j).astype(jnp.float32) for j, block in enumerate(shares)]
    return sum(shares[1:], shares[0]).astype(jnp.bfloat16)


def solution(mesh):
    placed = (
        P(("grp", "row"), None),
        P(("grp", "row"), None),
        P(("grp", "row"), None, None),
        P(("grp", "row")),
        P(None, "row"),
        P("row", None, None),
        P("row", None, None),
        P("row", None),
    )
    body = functools.partial(on_device, devices=mesh.shape["row"])
    return jax.shard_map(
        body, mesh=mesh, in_specs=placed, out_specs=P(("grp", "row"), None), check_vma=False
    )
```

time: 99.8 us -> 110 us (1.10)
  starting transfers between devices: 8.03 us -> 75.1 us
  blocking collectives: 33.6 us -> 0 us
  waiting for transfers between devices: 31.5 us -> 19 us
  local copies, waits for them, and re-layouts: 12.8 us -> 4.3 us
  Pallas kernels: 12 us -> 10.6 us
    ppermute x1 -> x53, starting transfers between devices: 0.07 us -> 75.1 us  [swap(): return lax.ppermute(block, 'row', [(i, i ^ k) for i in range(devices)])]
    all_to_all x2 -> x0, blocking collectives: 33.6 us -> none  [the longest x1 17.4 us: on_device(): lax.all_to_all(summed, 'row', split_axis=0, concat_axis=0, tiled=True, ax...]
    all_to_all x2 -> x0, waiting for transfers between devices: 29.7 us -> none  [the longest x1 15.3 us: on_device(): lax.all_to_all(queries, 'row', split_axis=0, concat_axis=0, tiled=True)]
    ppermute x1 -> x53, waiting for transfers between devices: 1.8 us -> 19 us  [swap(): return lax.ppermute(block, 'row', [(i, i ^ k) for i in range(devices)])]
    all_to_all x2 -> x0, starting transfers between devices: 7.96 us -> none  [the longest x1 4.37 us: on_device(): lax.all_to_all(latents, 'row', split_axis=0, concat_axis=0, tiled=True)]
    unnamed x14 -> x22, local copies, waits for them, and re-layouts: 11.7 us -> 4.3 us
    pallas_call x3 -> x4, Pallas kernels: 12 us -> 10.6 us  [the longest x1 5.22 us: attend(): pl.pallas_call(functools.partial(attend_kernel, devices), out_shape=[bloc...]
  transfers between devices with their start and end apart: 3 -> 53, of which waited for: 3 -> 11; matrix products, arithmetic and copies ran while one was open for 0% -> 0% of each run, Pallas kernels for 0% -> 0%
where the time goes in v2:
time: 110 us
  starting transfers between devices  75.1 us (68%)
  waiting for transfers between devices  19 us (17%)
  Pallas kernels  10.6 us (10%)
  local copies, waits for them, and re-layouts  4.3 us (4%)
    ppermute x53, starting transfers between devices, swap(): return lax.ppermute(block, 'row', [(i, i ^ k) for i in range(devices)])  75.1 us
    ppermute x53, waiting for transfers between devices, swap(): return lax.ppermute(block, 'row', [(i, i ^ k) for i in range(devices)])  19 us
    pallas_call x1, Pallas kernels, attend(): pl.pallas_call(functools.partial(attend_kernel, devices), out_shape=[bloc...  5.22 us
    unnamed x22, local copies, waits for them, and re-layouts  4.3 us
    pallas_call x1, Pallas kernels, output_terms(): pl.pallas_call(functools.partial(output_kernel, devices, 1024), out_shape...  3.87 us
  transfers between devices with their start and end apart: 53, of which 11 were waited for; matrix products, arithmetic and copies ran while one was open for 0% of the time, Pallas kernels for 0%

profile of v2, /device:TPU:0, one launch (start us, length us, event | category | flops | bytes accessed | tf_op | source)
XLA Modules:
  0.0 109.8 jit_solution(17540905809825942322)
XLA Ops:
  0.0 6.0 %collective-permute-start.13 = (bf16[4,1536]{1,0:T(4,128)(2,1)}, bf16[4,1536]{1,0:T(4,128)(2,1)S(1)}, u32[]{:S(2)}, u32[]{:S(2)}) collective-permute-start(bf16[4,1536]{1,0:T(4,128)(2,1)} %refs_0_.1), channel_id=1, source_target_pairs={{0,14},{1,15},{2,12},{3,13},{4,10},{5,11},{6,8},{7,9},{8,6},{9,7},... | collective-permute-start | bytes 36872 | tf_op jit(solution)/shard_map/ppermute | solution.py:253
  6.0 3.0 %collective-permute-start.11 = (bf16[4,1536]{1,0:T(4,128)(2,1)}, bf16[4,1536]{1,0:T(4,128)(2,1)S(1)}, u32[]{:S(2)}, u32[]{:S(2)}) collective-permute-start(bf16[4,1536]{1,0:T(4,128)(2,1)} %refs_0_.1), channel_id=1, source_target_pairs={{0,12},{1,13},{2,14},{3,15},{4,8},{5,9},{6,10},{7,11},{8,4},{9,5},... | collective-permute-start | bytes 36872 | tf_op jit(solution)/shard_map/ppermute | solution.py:253
  9.0 4.1 %collective-permute-start.9 = (bf16[4,1536]{1,0:T(4,128)(2,1)}, bf16[4,1536]{1,0:T(4,128)(2,1)S(1)}, u32[]{:S(2)}, u32[]{:S(2)}) collective-permute-start(bf16[4,1536]{1,0:T(4,128)(2,1)} %refs_0_.1), channel_id=1, source_target_pairs={{0,10},{1,11},{2,8},{3,9},{4,14},{5,15},{6,12},{7,13},{8,2},{9,3},... | collective-permute-start | bytes 36872 | tf_op jit(solution)/shard_map/ppermute | solution.py:253
  13.1 2.1 %collective-permute-start.7 = (bf16[4,1536]{1,0:T(4,128)(2,1)}, bf16[4,1536]{1,0:T(4,128)(2,1)S(1)}, u32[]{:S(2)}, u32[]{:S(2)}) collective-permute-start(bf16[4,1536]{1,0:T(4,128)(2,1)} %refs_0_.1), channel_id=1, source_target_pairs={{0,8},{1,9},{2,10},{3,11},{4,12},{5,13},{6,14},{7,15},{8,0},{9,1},... | collective-permute-start | bytes 36872 | tf_op jit(solution)/shard_map/ppermute | solution.py:253
  15.2 3.2 %collective-permute-start.5 = (bf16[4,1536]{1,0:T(4,128)(2,1)}, bf16[4,1536]{1,0:T(4,128)(2,1)S(1)}, u32[]{:S(2)}, u32[]{:S(2)}) collective-permute-start(bf16[4,1536]{1,0:T(4,128)(2,1)} %refs_0_.1), channel_id=1, source_target_pairs={{0,6},{1,7},{2,4},{3,5},{4,2},{5,3},{6,0},{7,1},{8,14},{9,15},{10,... | collective-permute-start | bytes 36872 | tf_op jit(solution)/shard_map/ppermute | solution.py:253
  20.4 1.5 %collective-permute-start.1 = (bf16[4,1536]{1,0:T(4,128)(2,1)}, bf16[4,1536]{1,0:T(4,128)(2,1)S(1)}, u32[]{:S(2)}, u32[]{:S(2)}) collective-permute-start(bf16[4,1536]{1,0:T(4,128)(2,1)} %refs_0_.1), channel_id=1, source_target_pairs={{0,2},{1,3},{2,0},{3,1},{4,6},{5,7},{6,4},{7,5},{8,10},{9,11},{10,... | collective-permute-start | bytes 36872 | tf_op jit(solution)/shard_map/ppermute | solution.py:253
  21.9 1.2 %collective-permute-start.14 = (bf16[4,1536]{1,0:T(4,128)(2,1)}, bf16[4,1536]{1,0:T(4,128)(2,1)S(1)}, u32[]{:S(2)}, u32[]{:S(2)}) collective-permute-start(bf16[4,1536]{1,0:T(4,128)(2,1)} %refs_0_.1), channel_id=1, source_target_pairs={{0,15},{1,14},{2,13},{3,12},{4,11},{5,10},{6,9},{7,8},{8,7},{9,6},... | collective-permute-start | bytes 36872 | tf_op jit(solution)/shard_map/ppermute | solution.py:253
  24.3 3.7 %collective-permute-done.14.refs_15_ = bf16[4,1536]{1,0:T(4,128)(2,1)S(1)} collective-permute-done((bf16[4,1536]{1,0:T(4,128)(2,1)}, bf16[4,1536]{1,0:T(4,128)(2,1)S(1)}, u32[]{:S(2)}, u32[]{:S(2)}) %collective-permute-start.14) | collective-permute-done | bytes 12320 | tf_op jit(solution)/shard_map/ppermute | solution.py:253
  28.0 2.3 %copy-done.1 = bf16[1536,1536]{1,0:T(8,128)(2,1)S(1)} copy-done((bf16[1536,1536]{1,0:T(8,128)(2,1)S(1)}, bf16[1536,1536]{1,0:T(8,128)(2,1)}, u32[]{:S(2)}) %copy-start.1) | copy-done | bytes 4718616
  32.3 1.4 %project.1 = (bf16[144,128]{1,0:T(8,128)(2,1)S(1)}, bf16[144,128]{1,0:T(8,128)(2,1)S(1)}, bf16[144,128]{1,0:T(8,128)(2,1)S(1)}, bf16[144,128]{1,0:T(8,128)(2,1)S...) custom-call(bf16[4,1536]{1,0:T(4,128)(2,1)S(1)} %copy-done.4, ...), custom_call_target="tpu_custom_call" | custom-call | flops 23000000512 | tf_op jit(solution)/shard_map/project/pallas_call | solution.py:80
  35.7 2.1 %collective-permute-start.19 = (bf16[144,128]{1,0:T(8,128)(2,1)S(1)}, bf16[144,128]{1,0:T(8,128)(2,1)S(1)}, u32[]{:S(2)}, u32[]{:S(2)}) collective-permute-start(bf16[144,128]{1,0:T(8,128)(2,1)S(1)} %get-tuple-element.52), channel_id=1, source_target_pairs={{0,5},{1,4},{2,7},{3,6},{4,1},{5,0},{6,3},{7,2},{8,13},{9,12},{10,... | collective-permute-start | bytes 110600 | tf_op jit(solution)/shard_map/ppermute | solution.py:253
  38.5 1.5 %collective-permute-start.21 = (bf16[144,128]{1,0:T(8,128)(2,1)S(1)}, bf16[144,128]{1,0:T(8,128)(2,1)S(1)}, u32[]{:S(2)}, u32[]{:S(2)}) collective-permute-start(bf16[144,128]{1,0:T(8,128)(2,1)S(1)} %get-tuple-element.54), channel_id=1, source_target_pairs={{0,7},{1,6},{2,5},{3,4},{4,3},{5,2},{6,1},{7,0},{8,15},{9,14},{10,... | collective-permute-start | bytes 110600 | tf_op jit(solution)/shard_map/ppermute | solution.py:253
  40.1 3.0 %collective-permute-start.23 = (bf16[144,128]{1,0:T(8,128)(2,1)S(1)}, bf16[144,128]{1,0:T(8,128)(2,1)S(1)}, u32[]{:S(2)}, u32[]{:S(2)}) collective-permute-start(bf16[144,128]{1,0:T(8,128)(2,1)S(1)} %get-tuple-element.56), channel_id=1, source_target_pairs={{0,9},{1,8},{2,11},{3,10},{4,13},{5,12},{6,15},{7,14},{8,1},{9,0},... | collective-permute-start | bytes 110600 | tf_op jit(solution)/shard_map/ppermute | solution.py:253
  43.3 2.9 %collective-permute-start.25 = (bf16[144,128]{1,0:T(8,128)(2,1)S(1)}, bf16[144,128]{1,0:T(8,128)(2,1)S(1)}, u32[]{:S(2)}, u32[]{:S(2)}) collective-permute-start(bf16[144,128]{1,0:T(8,128)(2,1)S(1)} %get-tuple-element.58), channel_id=1, source_target_pairs={{0,11},{1,10},{2,9},{3,8},{4,15},{5,14},{6,13},{7,12},{8,3},{9,2},... | collective-permute-start | bytes 110600 | tf_op jit(solution)/shard_map/ppermute | solution.py:253
  46.6 3.5 %collective-permute-start.27 = (bf16[144,128]{1,0:T(8,128)(2,1)S(1)}, bf16[144,128]{1,0:T(8,128)(2,1)S(1)}, u32[]{:S(2)}, u32[]{:S(2)}) collective-permute-start(bf16[144,128]{1,0:T(8,128)(2,1)S(1)} %get-tuple-element.60), channel_id=1, source_target_pairs={{0,13},{1,12},{2,15},{3,14},{4,9},{5,8},{6,11},{7,10},{8,5},{9,4},... | collective-permute-start | bytes 110600 | tf_op jit(solution)/shard_map/ppermute | solution.py:253
  51.3 3.0 %collective-permute-start.29 = (bf16[144,128]{1,0:T(8,128)(2,1)S(1)}, bf16[144,128]{1,0:T(8,128)(2,1)S(1)}, u32[]{:S(2)}, u32[]{:S(2)}) collective-permute-start(bf16[144,128]{1,0:T(8,128)(2,1)S(1)} %get-tuple-element.62), channel_id=1, source_target_pairs={{0,15},{1,14},{2,13},{3,12},{4,11},{5,10},{6,9},{7,8},{8,7},{9,6},... | collective-permute-start | bytes 110600 | tf_op jit(solution)/shard_map/ppermute | solution.py:253
  54.3 2.5 %collective-permute-done.28.refs_14_ = bf16[144,128]{1,0:T(8,128)(2,1)S(1)} collective-permute-done((bf16[144,128]{1,0:T(8,128)(2,1)S(1)}, bf16[144,128]{1,0:T(8,128)(2,1)S(1)}, u32[]{:S(2)}, u32[]{:S(2)}) %collective-permute-start.28) | collective-permute-done | bytes 36896 | tf_op jit(solution)/shard_map/ppermute | solution.py:253
  57.8 5.2 %attend.1 = (bf16[32,512]{1,0:T(8,128)(2,1)S(1)}, bf16[32,512]{1,0:T(8,128)(2,1)S(1)}, bf16[32,512]{1,0:T(8,128)(2,1)S(1)}, bf16[32,512]{1,0:T(8,128)(2,1)S(1)},...) custom-call(s32[4]{0:T(128)S(1)} %copy-done.6, ...), custom_call_target="tpu_custom_call" | custom-call | flops 23000000512 | tf_op jit(solution)/shard_map/attend/pallas_call | solution.py:163
  64.9 1.7 %collective-permute-start.34 = (bf16[32,512]{1,0:T(8,128)(2,1)S(1)}, bf16[32,512]{1,0:T(8,128)(2,1)S(1)}, u32[]{:S(2)}, u32[]{:S(2)}) collective-permute-start(bf16[32,512]{1,0:T(8,128)(2,1)S(1)} %get-tuple-element.68), channel_id=1, source_target_pairs={{0,5},{1,4},{2,7},{3,6},{4,1},{5,0},{6,3},{7,2},{8,13},{9,12},{10,... | collective-permute-start | bytes 98312 | tf_op jit(solution)/shard_map/ppermute | solution.py:253
  67.2 2.2 %collective-permute-start.36 = (bf16[32,512]{1,0:T(8,128)(2,1)S(1)}, bf16[32,512]{1,0:T(8,128)(2,1)S(1)}, u32[]{:S(2)}, u32[]{:S(2)}) collective-permute-start(bf16[32,512]{1,0:T(8,128)(2,1)S(1)} %get-tuple-element.70), channel_id=1, source_target_pairs={{0,7},{1,6},{2,5},{3,4},{4,3},{5,2},{6,1},{7,0},{8,15},{9,14},{10,... | collective-permute-start | bytes 98312 | tf_op jit(solution)/shard_map/ppermute | solution.py:253
  69.3 1.6 %collective-permute-start.37 = (bf16[32,512]{1,0:T(8,128)(2,1)S(1)}, bf16[32,512]{1,0:T(8,128)(2,1)S(1)}, u32[]{:S(2)}, u32[]{:S(2)}) collective-permute-start(bf16[32,512]{1,0:T(8,128)(2,1)S(1)} %get-tuple-element.71), channel_id=1, source_target_pairs={{0,8},{1,9},{2,10},{3,11},{4,12},{5,13},{6,14},{7,15},{8,0},{9,1},... | collective-permute-start | bytes 98312 | tf_op jit(solution)/shard_map/ppermute | solution.py:253
  71.9 2.5 %collective-permute-start.39 = (bf16[32,512]{1,0:T(8,128)(2,1)S(1)}, bf16[32,512]{1,0:T(8,128)(2,1)S(1)}, u32[]{:S(2)}, u32[]{:S(2)}) collective-permute-start(bf16[32,512]{1,0:T(8,128)(2,1)S(1)} %get-tuple-element.73), channel_id=1, source_target_pairs={{0,10},{1,11},{2,8},{3,9},{4,14},{5,15},{6,12},{7,13},{8,2},{9,3},... | collective-permute-start | bytes 98312 | tf_op jit(solution)/shard_map/ppermute | solution.py:253
  75.5 2.6 %collective-permute-start.41 = (bf16[32,512]{1,0:T(8,128)(2,1)S(1)}, bf16[32,512]{1,0:T(8,128)(2,1)S(1)}, u32[]{:S(2)}, u32[]{:S(2)}) collective-permute-start(bf16[32,512]{1,0:T(8,128)(2,1)S(1)} %get-tuple-element.75), channel_id=1, source_target_pairs={{0,12},{1,13},{2,14},{3,15},{4,8},{5,9},{6,10},{7,11},{8,4},{9,5},... | collective-permute-start | bytes 98312 | tf_op jit(solution)/shard_map/ppermute | solution.py:253
  79.0 3.6 %collective-permute-start.43 = (bf16[32,512]{1,0:T(8,128)(2,1)S(1)}, bf16[32,512]{1,0:T(8,128)(2,1)S(1)}, u32[]{:S(2)}, u32[]{:S(2)}) collective-permute-start(bf16[32,512]{1,0:T(8,128)(2,1)S(1)} %get-tuple-element.77), channel_id=1, source_target_pairs={{0,14},{1,15},{2,12},{3,13},{4,10},{5,11},{6,8},{7,9},{8,6},{9,7},... | collective-permute-start | bytes 98312 | tf_op jit(solution)/shard_map/ppermute | solution.py:253
  83.6 2.1 %collective-permute-done.43.refs_14_ = bf16[32,512]{1,0:T(8,128)(2,1)S(1)} collective-permute-done((bf16[32,512]{1,0:T(8,128)(2,1)S(1)}, bf16[32,512]{1,0:T(8,128)(2,1)S(1)}, u32[]{:S(2)}, u32[]{:S(2)}) %collective-permute-start.43) | collective-permute-done | bytes 32800 | tf_op jit(solution)/shard_map/ppermute | solution.py:253
  85.7 3.0 %collective-permute-done.44.refs_15_ = bf16[32,512]{1,0:T(8,128)(2,1)S(1)} collective-permute-done((bf16[32,512]{1,0:T(8,128)(2,1)S(1)}, bf16[32,512]{1,0:T(8,128)(2,1)S(1)}, u32[]{:S(2)}, u32[]{:S(2)}) %collective-permute-start.44) | collective-permute-done | bytes 32800 | tf_op jit(solution)/shard_map/ppermute | solution.py:253
  88.7 3.9 %output_terms.1 = (f32[32,7168]{1,0:T(8,128)S(1)}, bf16[32,7168]{1,0:T(8,128)(2,1)S(1)}) custom-call(bf16[32,512]{1,0:T(8,128)(2,1)S(1)} %get-tuple-element.63.refs_0_, bf16[32,512]{1,0:T(8,128)(2,1)S(1)} %collective-permute-done.30.refs_1_, bf16[32,512]{1,0:T(8,128)(2,1)S(1)} %collective-permute-done.31.refs_2_, ...), custom_call_target="tpu_custom_call" | custom-call | flops 23000000512 | tf_op jit(solution)/shard_map/output_terms/pallas_call | solution.py:208
  92.8 1.6 %collective-permute-done.45.other_ref = bf16[32,7168]{1,0:T(8,128)(2,1)S(1)} collective-permute-done((bf16[32,7168]{1,0:T(8,128)(2,1)S(1)}, bf16[32,7168]{1,0:T(8,128)(2,1)S(1)}, u32[]{:S(2)}, u32[]{:S(2)}) %collective-permute-start.45) | collective-permute-done | bytes 458784 | tf_op jit(solution)/shard_map/ppermute | solution.py:253
  95.1 3.0 %collective-permute-start.48 = (bf16[4,7168]{1,0:T(4,128)(2,1)S(1)}, bf16[4,7168]{1,0:T(4,128)(2,1)S(1)}, u32[]{:S(2)}, u32[]{:S(2)}) collective-permute-start(bf16[4,7168]{1,0:T(4,128)(2,1)S(1)} %get-tuple-element.84), channel_id=1, source_target_pairs={{0,6},{1,7},{2,4},{3,5},{4,2},{5,3},{6,0},{7,1},{8,14},{9,15},{10,... | collective-permute-start | bytes 172040 | tf_op jit(solution)/shard_map/ppermute | solution.py:253
  98.1 2.8 %collective-permute-start.50 = (bf16[4,7168]{1,0:T(4,128)(2,1)S(1)}, bf16[4,7168]{1,0:T(4,128)(2,1)S(1)}, u32[]{:S(2)}, u32[]{:S(2)}) collective-permute-start(bf16[4,7168]{1,0:T(4,128)(2,1)S(1)} %get-tuple-element.86), channel_id=1, source_target_pairs={{0,10},{1,11},{2,8},{3,9},{4,14},{5,15},{6,12},{7,13},{8,2},{9,3},... | collective-permute-start | bytes 172040 | tf_op jit(solution)/shard_map/ppermute | solution.py:253
  102.2 3.6 %collective-permute-start.52 = (bf16[4,7168]{1,0:T(4,128)(2,1)S(1)}, bf16[4,7168]{1,0:T(4,128)(2,1)S(1)}, u32[]{:S(2)}, u32[]{:S(2)}) collective-permute-start(bf16[4,7168]{1,0:T(4,128)(2,1)S(1)} %get-tuple-element.88), channel_id=1, source_target_pairs={{0,14},{1,15},{2,12},{3,13},{4,10},{5,11},{6,8},{7,9},{8,6},{9,7},... | collective-permute-start | bytes 172040 | tf_op jit(solution)/shard_map/ppermute | solution.py:253
  106.2 2.2 %collective-permute-done.50 = bf16[4,7168]{1,0:T(4,128)(2,1)S(1)} collective-permute-done((bf16[4,7168]{1,0:T(4,128)(2,1)S(1)}, bf16[4,7168]{1,0:T(4,128)(2,1)S(1)}, u32[]{:S(2)}, u32[]{:S(2)}) %collective-permute-start.50) | collective-permute-done | bytes 57376 | tf_op jit(solution)/shard_map/ppermute | solution.py:253
  (102 shorter events, 21.0 us)
Async XLA Ops:
  0.0 13.1 %collective-permute-start.13 = (bf16[4,1536]{1,0:T(4,128)(2,1)}, bf16[4,1536]{1,0:T(4,128)(2,1)S(1)}, u32[]{:S(2)}, u32[]{:S(2)}) collective-permute-start(bf16[4,1536]{1,0:T(4,128)(2,1)} %refs_0_.1), channel_id=1, source_target_pairs={{0,14},{1,15},{2,12},{3,13},{4,10},{5,11},{6,8},{7,9},{8,6},{9,7},... | collective-permute-start | bytes 36872 | tf_op jit(solution)/shard_map/ppermute | solution.py:253
  6.0 7.1 %collective-permute-start.12 = (bf16[4,1536]{1,0:T(4,128)(2,1)}, bf16[4,1536]{1,0:T(4,128)(2,1)S(1)}, u32[]{:S(2)}, u32[]{:S(2)}) collective-permute-start(bf16[4,1536]{1,0:T(4,128)(2,1)} %refs_0_.1), channel_id=1, source_target_pairs={{0,13},{1,12},{2,15},{3,14},{4,9},{5,8},{6,11},{7,10},{8,5},{9,4},... | collective-permute-start | bytes 36872 | tf_op jit(solution)/shard_map/ppermute | solution.py:253
  6.0 9.2 %collective-permute-start.11 = (bf16[4,1536]{1,0:T(4,128)(2,1)}, bf16[4,1536]{1,0:T(4,128)(2,1)S(1)}, u32[]{:S(2)}, u32[]{:S(2)}) collective-permute-start(bf16[4,1536]{1,0:T(4,128)(2,1)} %refs_0_.1), channel_id=1, source_target_pairs={{0,12},{1,13},{2,14},{3,15},{4,8},{5,9},{6,10},{7,11},{8,4},{9,5},... | collective-permute-start | bytes 36872 | tf_op jit(solution)/shard_map/ppermute | solution.py:253
  9.0 9.4 %collective-permute-start.9 = (bf16[4,1536]{1,0:T(4,128)(2,1)}, bf16[4,1536]{1,0:T(4,128)(2,1)S(1)}, u32[]{:S(2)}, u32[]{:S(2)}) collective-permute-start(bf16[4,1536]{1,0:T(4,128)(2,1)} %refs_0_.1), channel_id=1, source_target_pairs={{0,10},{1,11},{2,8},{3,9},{4,14},{5,15},{6,12},{7,13},{8,2},{9,3},... | collective-permute-start | bytes 36872 | tf_op jit(solution)/shard_map/ppermute | solution.py:253
  13.1 6.5 %collective-permute-start.7 = (bf16[4,1536]{1,0:T(4,128)(2,1)}, bf16[4,1536]{1,0:T(4,128)(2,1)S(1)}, u32[]{:S(2)}, u32[]{:S(2)}) collective-permute-start(bf16[4,1536]{1,0:T(4,128)(2,1)} %refs_0_.1), channel_id=1, source_target_pairs={{0,8},{1,9},{2,10},{3,11},{4,12},{5,13},{6,14},{7,15},{8,0},{9,1},... | collective-permute-start | bytes 36872 | tf_op jit(solution)/shard_map/ppermute | solution.py:253
  15.2 6.7 %collective-permute-start.5 = (bf16[4,1536]{1,0:T(4,128)(2,1)}, bf16[4,1536]{1,0:T(4,128)(2,1)S(1)}, u32[]{:S(2)}, u32[]{:S(2)}) collective-permute-start(bf16[4,1536]{1,0:T(4,128)(2,1)} %refs_0_.1), channel_id=1, source_target_pairs={{0,6},{1,7},{2,4},{3,5},{4,2},{5,3},{6,0},{7,1},{8,14},{9,15},{10,... | collective-permute-start | bytes 36872 | tf_op jit(solution)/shard_map/ppermute | solution.py:253
  35.7 7.4 %collective-permute-start.19 = (bf16[144,128]{1,0:T(8,128)(2,1)S(1)}, bf16[144,128]{1,0:T(8,128)(2,1)S(1)}, u32[]{:S(2)}, u32[]{:S(2)}) collective-permute-start(bf16[144,128]{1,0:T(8,128)(2,1)S(1)} %get-tuple-element.52), channel_id=1, source_target_pairs={{0,5},{1,4},{2,7},{3,6},{4,1},{5,0},{6,3},{7,2},{8,13},{9,12},{10,... | collective-permute-start | bytes 110600 | tf_op jit(solution)/shard_map/ppermute | solution.py:253
  38.5 7.8 %collective-permute-start.21 = (bf16[144,128]{1,0:T(8,128)(2,1)S(1)}, bf16[144,128]{1,0:T(8,128)(2,1)S(1)}, u32[]{:S(2)}, u32[]{:S(2)}) collective-permute-start(bf16[144,128]{1,0:T(8,128)(2,1)S(1)} %get-tuple-element.54), channel_id=1, source_target_pairs={{0,7},{1,6},{2,5},{3,4},{4,3},{5,2},{6,1},{7,0},{8,15},{9,14},{10,... | collective-permute-start | bytes 110600 | tf_op jit(solution)/shard_map/ppermute | solution.py:253
  40.1 6.6 %collective-permute-start.22 = (bf16[144,128]{1,0:T(8,128)(2,1)S(1)}, bf16[144,128]{1,0:T(8,128)(2,1)S(1)}, u32[]{:S(2)}, u32[]{:S(2)}) collective-permute-start(bf16[144,128]{1,0:T(8,128)(2,1)S(1)} %get-tuple-element.55), channel_id=1, source_target_pairs={{0,8},{1,9},{2,10},{3,11},{4,12},{5,13},{6,14},{7,15},{8,0},{9,1},... | collective-permute-start | bytes 110600 | tf_op jit(solution)/shard_map/ppermute | solution.py:253
  40.1 10.1 %collective-permute-start.23 = (bf16[144,128]{1,0:T(8,128)(2,1)S(1)}, bf16[144,128]{1,0:T(8,128)(2,1)S(1)}, u32[]{:S(2)}, u32[]{:S(2)}) collective-permute-start(bf16[144,128]{1,0:T(8,128)(2,1)S(1)} %get-tuple-element.56), channel_id=1, source_target_pairs={{0,9},{1,8},{2,11},{3,10},{4,13},{5,12},{6,15},{7,14},{8,1},{9,0},... | collective-permute-start | bytes 110600 | tf_op jit(solution)/shard_map/ppermute | solution.py:253
  43.0 8.2 %collective-permute-start.24 = (bf16[144,128]{1,0:T(8,128)(2,1)S(1)}, bf16[144,128]{1,0:T(8,128)(2,1)S(1)}, u32[]{:S(2)}, u32[]{:S(2)}) collective-permute-start(bf16[144,128]{1,0:T(8,128)(2,1)S(1)} %get-tuple-element.57), channel_id=1, source_target_pairs={{0,10},{1,11},{2,8},{3,9},{4,14},{5,15},{6,12},{7,13},{8,2},{9,3},... | collective-permute-start | bytes 110600 | tf_op jit(solution)/shard_map/ppermute | solution.py:253
  43.3 10.9 %collective-permute-start.25 = (bf16[144,128]{1,0:T(8,128)(2,1)S(1)}, bf16[144,128]{1,0:T(8,128)(2,1)S(1)}, u32[]{:S(2)}, u32[]{:S(2)}) collective-permute-start(bf16[144,128]{1,0:T(8,128)(2,1)S(1)} %get-tuple-element.58), channel_id=1, source_target_pairs={{0,11},{1,10},{2,9},{3,8},{4,15},{5,14},{6,13},{7,12},{8,3},{9,2},... | collective-permute-start | bytes 110600 | tf_op jit(solution)/shard_map/ppermute | solution.py:253
  46.3 8.0 %collective-permute-start.26 = (bf16[144,128]{1,0:T(8,128)(2,1)S(1)}, bf16[144,128]{1,0:T(8,128)(2,1)S(1)}, u32[]{:S(2)}, u32[]{:S(2)}) collective-permute-start(bf16[144,128]{1,0:T(8,128)(2,1)S(1)} %get-tuple-element.59), channel_id=1, source_target_pairs={{0,12},{1,13},{2,14},{3,15},{4,8},{5,9},{6,10},{7,11},{8,4},{9,5},... | collective-permute-start | bytes 110600 | tf_op jit(solution)/shard_map/ppermute | solution.py:253
  46.6 7.6 %collective-permute-start.27 = (bf16[144,128]{1,0:T(8,128)(2,1)S(1)}, bf16[144,128]{1,0:T(8,128)(2,1)S(1)}, u32[]{:S(2)}, u32[]{:S(2)}) collective-permute-start(bf16[144,128]{1,0:T(8,128)(2,1)S(1)} %get-tuple-element.60), channel_id=1, source_target_pairs={{0,13},{1,12},{2,15},{3,14},{4,9},{5,8},{6,11},{7,10},{8,5},{9,4},... | collective-permute-start | bytes 110600 | tf_op jit(solution)/shard_map/ppermute | solution.py:253
  50.1 6.7 %collective-permute-start.28 = (bf16[144,128]{1,0:T(8,128)(2,1)S(1)}, bf16[144,128]{1,0:T(8,128)(2,1)S(1)}, u32[]{:S(2)}, u32[]{:S(2)}) collective-permute-start(bf16[144,128]{1,0:T(8,128)(2,1)S(1)} %get-tuple-element.61), channel_id=1, source_target_pairs={{0,14},{1,15},{2,12},{3,13},{4,10},{5,11},{6,8},{7,9},{8,6},{9,7},... | collective-permute-start | bytes 110600 | tf_op jit(solution)/shard_map/ppermute | solution.py:253
  51.3 6.4 %collective-permute-start.29 = (bf16[144,128]{1,0:T(8,128)(2,1)S(1)}, bf16[144,128]{1,0:T(8,128)(2,1)S(1)}, u32[]{:S(2)}, u32[]{:S(2)}) collective-permute-start(bf16[144,128]{1,0:T(8,128)(2,1)S(1)} %get-tuple-element.62), channel_id=1, source_target_pairs={{0,15},{1,14},{2,13},{3,12},{4,11},{5,10},{6,9},{7,8},{8,7},{9,6},... | collective-permute-start | bytes 110600 | tf_op jit(solution)/shard_map/ppermute | solution.py:253
  64.9 7.0 %collective-permute-start.34 = (bf16[32,512]{1,0:T(8,128)(2,1)S(1)}, bf16[32,512]{1,0:T(8,128)(2,1)S(1)}, u32[]{:S(2)}, u32[]{:S(2)}) collective-permute-start(bf16[32,512]{1,0:T(8,128)(2,1)S(1)} %get-tuple-element.68), channel_id=1, source_target_pairs={{0,5},{1,4},{2,7},{3,6},{4,1},{5,0},{6,3},{7,2},{8,13},{9,12},{10,... | collective-permute-start | bytes 98312 | tf_op jit(solution)/shard_map/ppermute | solution.py:253
  66.6 7.8 %collective-permute-start.35 = (bf16[32,512]{1,0:T(8,128)(2,1)S(1)}, bf16[32,512]{1,0:T(8,128)(2,1)S(1)}, u32[]{:S(2)}, u32[]{:S(2)}) collective-permute-start(bf16[32,512]{1,0:T(8,128)(2,1)S(1)} %get-tuple-element.69), channel_id=1, source_target_pairs={{0,6},{1,7},{2,4},{3,5},{4,2},{5,3},{6,0},{7,1},{8,14},{9,15},{10,... | collective-permute-start | bytes 98312 | tf_op jit(solution)/shard_map/ppermute | solution.py:253
  67.2 8.4 %collective-permute-start.36 = (bf16[32,512]{1,0:T(8,128)(2,1)S(1)}, bf16[32,512]{1,0:T(8,128)(2,1)S(1)}, u32[]{:S(2)}, u32[]{:S(2)}) collective-permute-start(bf16[32,512]{1,0:T(8,128)(2,1)S(1)} %get-tuple-element.70), channel_id=1, source_target_pairs={{0,7},{1,6},{2,5},{3,4},{4,3},{5,2},{6,1},{7,0},{8,15},{9,14},{10,... | collective-permute-start | bytes 98312 | tf_op jit(solution)/shard_map/ppermute | solution.py:253
  69.3 8.8 %collective-permute-start.37 = (bf16[32,512]{1,0:T(8,128)(2,1)S(1)}, bf16[32,512]{1,0:T(8,128)(2,1)S(1)}, u32[]{:S(2)}, u32[]{:S(2)}) collective-permute-start(bf16[32,512]{1,0:T(8,128)(2,1)S(1)} %get-tuple-element.71), channel_id=1, source_target_pairs={{0,8},{1,9},{2,10},{3,11},{4,12},{5,13},{6,14},{7,15},{8,0},{9,1},... | collective-permute-start | bytes 98312 | tf_op jit(solution)/shard_map/ppermute | solution.py:253
  70.9 8.1 %collective-permute-start.38 = (bf16[32,512]{1,0:T(8,128)(2,1)S(1)}, bf16[32,512]{1,0:T(8,128)(2,1)S(1)}, u32[]{:S(2)}, u32[]{:S(2)}) collective-permute-start(bf16[32,512]{1,0:T(8,128)(2,1)S(1)} %get-tuple-element.72), channel_id=1, source_target_pairs={{0,9},{1,8},{2,11},{3,10},{4,13},{5,12},{6,15},{7,14},{8,1},{9,0},... | collective-permute-start | bytes 98312 | tf_op jit(solution)/shard_map/ppermute | solution.py:253
  71.9 10.7 %collective-permute-start.39 = (bf16[32,512]{1,0:T(8,128)(2,1)S(1)}, bf16[32,512]{1,0:T(8,128)(2,1)S(1)}, u32[]{:S(2)}, u32[]{:S(2)}) collective-permute-start(bf16[32,512]{1,0:T(8,128)(2,1)S(1)} %get-tuple-element.73), channel_id=1, source_target_pairs={{0,10},{1,11},{2,8},{3,9},{4,14},{5,15},{6,12},{7,13},{8,2},{9,3},... | collective-permute-start | bytes 98312 | tf_op jit(solution)/shard_map/ppermute | solution.py:253
  74.4 9.1 %collective-permute-start.40 = (bf16[32,512]{1,0:T(8,128)(2,1)S(1)}, bf16[32,512]{1,0:T(8,128)(2,1)S(1)}, u32[]{:S(2)}, u32[]{:S(2)}) collective-permute-start(bf16[32,512]{1,0:T(8,128)(2,1)S(1)} %get-tuple-element.74), channel_id=1, source_target_pairs={{0,11},{1,10},{2,9},{3,8},{4,15},{5,14},{6,13},{7,12},{8,3},{9,2},... | collective-permute-start | bytes 98312 | tf_op jit(solution)/shard_map/ppermute | solution.py:253
  75.5 8.0 %collective-permute-start.41 = (bf16[32,512]{1,0:T(8,128)(2,1)S(1)}, bf16[32,512]{1,0:T(8,128)(2,1)S(1)}, u32[]{:S(2)}, u32[]{:S(2)}) collective-permute-start(bf16[32,512]{1,0:T(8,128)(2,1)S(1)} %get-tuple-element.75), channel_id=1, source_target_pairs={{0,12},{1,13},{2,14},{3,15},{4,8},{5,9},{6,10},{7,11},{8,4},{9,5},... | collective-permute-start | bytes 98312 | tf_op jit(solution)/shard_map/ppermute | solution.py:253
  79.0 6.6 %collective-permute-start.43 = (bf16[32,512]{1,0:T(8,128)(2,1)S(1)}, bf16[32,512]{1,0:T(8,128)(2,1)S(1)}, u32[]{:S(2)}, u32[]{:S(2)}) collective-permute-start(bf16[32,512]{1,0:T(8,128)(2,1)S(1)} %get-tuple-element.77), channel_id=1, source_target_pairs={{0,14},{1,15},{2,12},{3,13},{4,10},{5,11},{6,8},{7,9},{8,6},{9,7},... | collective-permute-start | bytes 98312 | tf_op jit(solution)/shard_map/ppermute | solution.py:253
  94.6 6.4 %collective-permute-start.46 = (bf16[4,7168]{1,0:T(4,128)(2,1)S(1)}, bf16[4,7168]{1,0:T(4,128)(2,1)S(1)}, u32[]{:S(2)}, u32[]{:S(2)}) collective-permute-start(bf16[4,7168]{1,0:T(4,128)(2,1)S(1)} %get-tuple-element.82), channel_id=1, source_target_pairs={{0,2},{1,3},{2,0},{3,1},{4,6},{5,7},{6,4},{7,5},{8,10},{9,11},{10,... | collective-permute-start | bytes 172040 | tf_op jit(solution)/shard_map/ppermute | solution.py:253
  95.1 7.1 %collective-permute-start.47 = (bf16[4,7168]{1,0:T(4,128)(2,1)S(1)}, bf16[4,7168]{1,0:T(4,128)(2,1)S(1)}, u32[]{:S(2)}, u32[]{:S(2)}) collective-permute-start(bf16[4,7168]{1,0:T(4,128)(2,1)S(1)} %get-tuple-element.83), channel_id=1, source_target_pairs={{0,4},{1,5},{2,6},{3,7},{4,0},{5,1},{6,2},{7,3},{8,12},{9,13},{10,... | collective-permute-start | bytes 172040 | tf_op jit(solution)/shard_map/ppermute | solution.py:253
  95.1 10.7 %collective-permute-start.48 = (bf16[4,7168]{1,0:T(4,128)(2,1)S(1)}, bf16[4,7168]{1,0:T(4,128)(2,1)S(1)}, u32[]{:S(2)}, u32[]{:S(2)}) collective-permute-start(bf16[4,7168]{1,0:T(4,128)(2,1)S(1)} %get-tuple-element.84), channel_id=1, source_target_pairs={{0,6},{1,7},{2,4},{3,5},{4,2},{5,3},{6,0},{7,1},{8,14},{9,15},{10,... | collective-permute-start | bytes 172040 | tf_op jit(solution)/shard_map/ppermute | solution.py:253
  98.1 8.0 %collective-permute-start.49 = (bf16[4,7168]{1,0:T(4,128)(2,1)S(1)}, bf16[4,7168]{1,0:T(4,128)(2,1)S(1)}, u32[]{:S(2)}, u32[]{:S(2)}) collective-permute-start(bf16[4,7168]{1,0:T(4,128)(2,1)S(1)} %get-tuple-element.85), channel_id=1, source_target_pairs={{0,8},{1,9},{2,10},{3,11},{4,12},{5,13},{6,14},{7,15},{8,0},{9,1},... | collective-permute-start | bytes 172040 | tf_op jit(solution)/shard_map/ppermute | solution.py:253
  98.1 10.2 %collective-permute-start.50 = (bf16[4,7168]{1,0:T(4,128)(2,1)S(1)}, bf16[4,7168]{1,0:T(4,128)(2,1)S(1)}, u32[]{:S(2)}, u32[]{:S(2)}) collective-permute-start(bf16[4,7168]{1,0:T(4,128)(2,1)S(1)} %get-tuple-element.86), channel_id=1, source_target_pairs={{0,10},{1,11},{2,8},{3,9},{4,14},{5,15},{6,12},{7,13},{8,2},{9,3},... | collective-permute-start | bytes 172040 | tf_op jit(solution)/shard_map/ppermute | solution.py:253
  101.0 7.4 %collective-permute-start.51 = (bf16[4,7168]{1,0:T(4,128)(2,1)S(1)}, bf16[4,7168]{1,0:T(4,128)(2,1)S(1)}, u32[]{:S(2)}, u32[]{:S(2)}) collective-permute-start(bf16[4,7168]{1,0:T(4,128)(2,1)S(1)} %get-tuple-element.87), channel_id=1, source_target_pairs={{0,12},{1,13},{2,14},{3,15},{4,8},{5,9},{6,10},{7,11},{8,4},{9,5},... | collective-permute-start | bytes 172040 | tf_op jit(solution)/shard_map/ppermute | solution.py:253
  102.2 6.9 %collective-permute-start.52 = (bf16[4,7168]{1,0:T(4,128)(2,1)S(1)}, bf16[4,7168]{1,0:T(4,128)(2,1)S(1)}, u32[]{:S(2)}, u32[]{:S(2)}) collective-permute-start(bf16[4,7168]{1,0:T(4,128)(2,1)S(1)} %get-tuple-element.88), channel_id=1, source_target_pairs={{0,14},{1,15},{2,12},{3,13},{4,10},{5,11},{6,8},{7,9},{8,6},{9,7},... | collective-permute-start | bytes 172040 | tf_op jit(solution)/shard_map/ppermute | solution.py:253
  (32 other events, 415.5 us)

commit v3 on v2

v3 whole, which is shorter than its diff:
```python
import functools
import math

import jax
import jax.numpy as jnp
from jax import lax
from jax.experimental import pallas as pl
from jax.experimental.pallas import tpu as pltpu
from jax.sharding import PartitionSpec as P

LAT = 512
ROPE = 64
NOPE = 128
VD = 128
LANES = 128
PIECES = LAT // LANES
FACTOR = (NOPE + ROPE) ** -0.5
LIMIT = 16 * 2**20
GROUPS = 2


def resident(x):
    return pltpu.with_memory_space_constraint(x, pltpu.VMEM)


def in_vmem():
    return pl.BlockSpec(memory_space=pltpu.VMEM)


def params():
    return pltpu.CompilerParams(vmem_limit_bytes=LIMIT)


def cost(microseconds):
    return pl.CostEstimate(
        flops=int(microseconds * 1.15e9), bytes_accessed=0, transcendentals=0
    )


def join_kernel(*refs):
    *in_refs, out_ref = refs
    out_ref[...] = jnp.concatenate(
        [ref[...].astype(jnp.float32) for ref in in_refs], axis=0
    ).astype(out_ref.dtype)


def join(blocks):
    rows, depth = blocks[0].shape
    return pl.pallas_call(
        join_kernel,
        out_shape=jax.ShapeDtypeStruct((len(blocks) * rows, depth), blocks[0].dtype),
        in_specs=[in_vmem()] * len(blocks),
        out_specs=in_vmem(),
        compiler_params=params(),
        cost_estimate=cost(10),
        name="join",
    )(*blocks)


def gathered_order(devices):
    return [z + y + c for c in range(2) for z in range(0, devices, 4) for y in (0, 2)]


def project_kernel(devices, groups, q_ref, far_ref, wq_ref, wk_ref, *refs):
    out_refs = refs[:groups]
    lat_ref, rot_ref = refs[groups:]
    heads = wk_ref.shape[0]
    count = 2 * q_ref.shape[0]
    rows = count // devices // groups
    wide = rows * heads
    width = NOPE + ROPE
    me = lax.axis_index("row")
    piece = jnp.concatenate([q_ref[...], far_ref[...]], axis=0)
    projected = jnp.dot(piece, wq_ref[...], preferred_element_type=jnp.float32)
    for h in range(heads):
        mine = projected[:, h * width : (h + 1) * width]
        absorbed = jnp.dot(
            mine[:, :NOPE].astype(jnp.bfloat16), wk_ref[h], preferred_element_type=jnp.float32
        )
        for c in range(PIECES):
            lat_ref[c, pl.ds(h, count, stride=heads), :] = absorbed[:, c * LANES : (c + 1) * LANES]
        pe = mine[:, NOPE:]
        rot_ref[pl.ds(h, count, stride=heads), :] = jnp.concatenate([pe, pe], axis=-1)
    lane = lax.broadcasted_iota(jnp.int32, (wide // 2, LANES), 1)
    for place, k in enumerate(gathered_order(devices)):
        owner = jnp.bitwise_xor(me, k)
        for g, out_ref in enumerate(out_refs):
            first = (place * groups + g) * wide
            for c in range(PIECES):
                out_ref[owner, c * wide : (c + 1) * wide, :] = lat_ref[
                    c, first : first + wide, :
                ].astype(jnp.bfloat16)
            low = rot_ref[first : first + wide // 2, :]
            high = rot_ref[first + wide // 2 : first + wide, :]
            out_ref[owner, PIECES * wide :, :] = jnp.where(lane < ROPE, low, high).astype(
                jnp.bfloat16
            )


def project(near, far, w_uq, w_uk, devices, groups):
    heads = w_uk.shape[0]
    count = 2 * near.shape[0]
    wide = count // devices // groups * heads
    block = jax.ShapeDtypeStruct((devices, PIECES * wide + wide // 2, LANES), jnp.bfloat16)
    return pl.pallas_call(
        functools.partial(project_kernel, devices, groups),
        out_shape=[block] * groups,
        in_specs=[in_vmem()] * 4,
        out_specs=[in_vmem()] * groups,
        scratch_shapes=[
            pltpu.VMEM((PIECES, count * heads, LANES), jnp.float32),
            pltpu.VMEM((count * heads, LANES), jnp.float32),
        ],
        compiler_params=params(),
        cost_estimate=cost(20),
        name="project",
    )(near, far, resident(w_uq), resident(w_uk))


def attend_kernel(start, rows, len_ref, q_ref, key_ref, new_ref, out_ref):
    devices, wide, _ = out_ref.shape
    maxlen = key_ref.shape[2]
    heads = wide // rows
    half = ROPE // 2
    total_heads = devices * heads
    lane = lax.broadcasted_iota(jnp.int32, (rows, ROPE), 1)
    place = lax.broadcasted_iota(jnp.int32, (rows, ROPE), 0)
    step = jnp.where(lane < half, lane, lane - half).astype(jnp.float32)
    frequency = jnp.exp(step * (-math.log(10000.0) / half))
    length = jnp.zeros((rows, ROPE), jnp.float32)
    for r in range(rows):
        length = jnp.where(place == r, len_ref[start + r].astype(jnp.float32), length)
    cosine = jnp.cos(length * frequency)
    sine = jnp.sin(length * frequency)
    sine = jnp.where(lane < half, -sine, sine)

    def query_block(first):
        block = q_ref[:, first : first + heads, :].astype(jnp.float32)
        return block.reshape(total_heads, LANES)

    for r in range(rows):
        latent = jnp.concatenate(
            [query_block(c * wide + r * heads) for c in range(PIECES)], axis=-1
        )
        pe = query_block(PIECES * wide + (r % (rows // 2)) * heads)
        side = r // (rows // 2) * ROPE
        pe = pe[:, side : side + ROPE]
        swapped = jnp.concatenate([pe[:, half:], pe[:, :half]], axis=-1)
        rotated = (pe * cosine[r : r + 1, :] + swapped * sine[r : r + 1, :]).astype(jnp.bfloat16)
        newest = new_ref[start + r : start + r + 1, :].astype(jnp.float32)
        own = (
            jnp.sum(latent * newest[:, :LAT], axis=-1, keepdims=True)
            + jnp.sum(rotated.astype(jnp.float32) * newest[:, LAT:], axis=-1, keepdims=True)
        ) * FACTOR
        scores = jnp.dot(
            latent.astype(jnp.bfloat16),
            key_ref[start + r, :LAT, :],
            preferred_element_type=jnp.float32,
        )
        scores += jnp.dot(rotated, key_ref[start + r, LAT:, :], preferred_element_type=jnp.float32)
        position = lax.broadcasted_iota(jnp.int32, (1, maxlen), 1)
        scores = jnp.where(position < len_ref[start + r], scores * FACTOR, -jnp.inf)
        peak = jnp.maximum(jnp.max(scores, axis=-1, keepdims=True), own)
        expo = jnp.exp(scores - peak)
        own_expo = jnp.exp(own - peak)
        total = jnp.sum(expo, axis=-1, keepdims=True) + own_expo
        weights = (expo / total).astype(jnp.bfloat16)
        own_weight = (own_expo / total).astype(jnp.bfloat16).astype(jnp.float32)
        summed = lax.dot_general(
            weights,
            key_ref[start + r, :LAT, :],
            (((1,), (1,)), ((), ())),
            preferred_element_type=jnp.float32,
        )
        summed += own_weight * newest[:, :LAT]
        out_ref[:, r * heads : (r + 1) * heads, :] = summed.reshape(devices, heads, LAT).astype(
            jnp.bfloat16
        )


def attend(lengths, queries, keys, new_latent, heads, start, rows):
    devices = queries.shape[0]
    return pl.pallas_call(
        functools.partial(attend_kernel, start, rows),
        out_shape=jax.ShapeDtypeStruct((devices, rows * heads, LAT), jnp.bfloat16),
        in_specs=[pl.BlockSpec(memory_space=pltpu.SMEM)] + [in_vmem()] * 3,
        out_specs=in_vmem(),
        compiler_params=params(),
        cost_estimate=cost(10),
        name="attend",
    )(lengths, queries, resident(keys), new_latent)


def output_kernel(groups, block, *refs):
    y_refs = refs[:groups]
    wv_ref, wo_ref, mine_ref, other_ref, rows_ref, val_ref = refs[groups:]
    heads = wv_ref.shape[0]
    devices, wide, _ = y_refs[0].shape
    me = lax.axis_index("row")
    for place, k in enumerate([*range(0, devices, 2), *range(1, devices, 2)]):
        for g, y_ref in enumerate(y_refs):
            first = (place * groups + g) * wide
            received = y_ref[jnp.bitwise_xor(me, k)].astype(jnp.float32)
            for c in range(PIECES):
                rows_ref[c, first : first + wide, :] = received[:, c * LANES : (c + 1) * LANES]
    count = rows_ref.shape[1] // heads
    for h in range(heads):
        chosen = jnp.concatenate(
            [rows_ref[c, pl.ds(h, count, stride=heads), :] for c in range(PIECES)], axis=-1
        )
        val_ref[:, h * VD : (h + 1) * VD] = jnp.dot(
            chosen.astype(jnp.bfloat16), wv_ref[h], preferred_element_type=jnp.float32
        ).astype(jnp.bfloat16)

    def step(index, carry):
        columns = pl.ds(pl.multiple_of(index * block, block), block)
        terms = jnp.dot(val_ref[...], wo_ref[:, columns], preferred_element_type=jnp.float32)
        mine_ref[:, columns] = terms[: count // 2]
        other_ref[:, columns] = terms[count // 2 :].astype(jnp.bfloat16)
        return carry

    lax.fori_loop(0, wo_ref.shape[1] // block, step, 0)


def output_terms(received, w_uv, w_o):
    groups = len(received)
    devices, wide, _ = received[0].shape
    heads = w_uv.shape[0]
    count = devices * groups * wide // heads
    depth = w_o.shape[1]
    return pl.pallas_call(
        functools.partial(output_kernel, groups, 1024),
        out_shape=(
            jax.ShapeDtypeStruct((count // 2, depth), jnp.float32),
            jax.ShapeDtypeStruct((count // 2, depth), jnp.bfloat16),
        ),
        in_specs=[in_vmem()] * (groups + 2),
        out_specs=(in_vmem(), in_vmem()),
        scratch_shapes=[
            pltpu.VMEM((PIECES, count * heads, LANES), jnp.float32),
            pltpu.VMEM((count, heads * VD), jnp.bfloat16),
        ],
        compiler_params=params(),
        cost_estimate=cost(20),
        name="output_terms",
    )(*received, resident(w_uv), resident(w_o))


def pair_kernel(rows, mine_ref, other_ref, *out_refs):
    total = mine_ref[...] + other_ref[...].astype(jnp.float32)
    for j, out_ref in enumerate(out_refs):
        out_ref[...] = total[j * rows : (j + 1) * rows].astype(out_ref.dtype)


def pair_sum(mine, other, rows):
    count, depth = mine.shape
    shapes = [jax.ShapeDtypeStruct((rows, depth), jnp.float32)]
    shapes += [jax.ShapeDtypeStruct((rows, depth), jnp.bfloat16)] * (count // rows - 1)
    return pl.pallas_call(
        functools.partial(pair_kernel, rows),
        out_shape=shapes,
        in_specs=[in_vmem()] * 2,
        out_specs=[in_vmem()] * len(shapes),
        compiler_params=params(),
        cost_estimate=cost(1),
        name="pair_sum",
    )(mine, other)


def on_device(q_latent, new_latent, cache, lengths, w_uq, w_uk, w_uv, w_o, devices):
    heads = w_uk.shape[0]
    rows = cache.shape[0]
    def swap(block, k):
        if k == 0:
            return block
        return lax.ppermute(block, "row", [(i, i ^ k) for i in range(devices)])

    def exchange(block):
        return lax.all_to_all(block, "row", split_axis=0, concat_axis=0, tiled=True)

    near = join([q_latent, swap(q_latent, 2)])
    near = join([swap(near, z) for z in range(0, devices, 4)])
    queries = project(near, swap(near, 1), w_uq, w_uk, devices, GROUPS)
    queries = [exchange(block) for block in queries]
    keys = jnp.swapaxes(cache, 1, 2)
    part = rows // GROUPS
    latents = [
        exchange(attend(lengths, block, keys, new_latent, heads, g * part, part))
        for g, block in enumerate(queries)
    ]
    mine, other = output_terms(latents, w_uv, w_o)
    shares = pair_sum(mine, swap(other, 1), rows)
    shares = [swap(block, 2 * j).astype(jnp.float32) for j, block in enumerate(shares)]
    return sum(shares[1:], shares[0]).astype(jnp.bfloat16)


def solution(mesh):
    placed = (
        P(("grp", "row"), None),
        P(("grp", "row"), None),
        P(("grp", "row"), None, None),
        P(("grp", "row")),
        P(None, "row"),
        P("row", None, None),
        P("row", None, None),
        P("row", None),
    )
    body = functools.partial(on_device, devices=mesh.shape["row"])
    return jax.shard_map(
        body, mesh=mesh, in_specs=placed, out_specs=P(("grp", "row"), None), check_vma=False
    )
```

time: 110 us -> 101 us (0.918)
  starting transfers between devices: 75.1 us -> 26.2 us
  blocking collectives: 0 us -> 27.5 us
  local copies, waits for them, and re-layouts: 4.3 us -> 11.9 us
  Pallas kernels: 10.6 us -> 12.6 us
  waiting for transfers between devices: 19 us -> 20.8 us
    ppermute x53 -> x13, starting transfers between devices: 75.1 us -> 19.1 us  [swap(): return lax.ppermute(block, 'row', [(i, i ^ k) for i in range(devices)])]
    all_to_all x0 -> x2, blocking collectives: none -> 27.5 us  [exchange(): return lax.all_to_all(block, 'row', split_axis=0, concat_axis=0, tiled=True)]
    all_to_all x0 -> x2, waiting for transfers between devices: none -> 7.92 us  [exchange(): return lax.all_to_all(block, 'row', split_axis=0, concat_axis=0, tiled=True)]
    unnamed x22 -> x20, local copies, waits for them, and re-layouts: 4.3 us -> 11.9 us
    all_to_all x0 -> x2, starting transfers between devices: none -> 7.07 us  [exchange(): return lax.all_to_all(block, 'row', split_axis=0, concat_axis=0, tiled=True)]
    ppermute x53 -> x13, waiting for transfers between devices: 19 us -> 12.9 us  [swap(): return lax.ppermute(block, 'row', [(i, i ^ k) for i in range(devices)])]
    pallas_call x3 -> x6, Pallas kernels: 10.5 us -> 12.5 us  [the longest x2 6.56 us: attend(): pl.pallas_call(functools.partial(attend_kernel, start, rows), out_shape=j...]
  transfers between devices with their start and end apart: 53 -> 15, of which waited for: 11 -> 10; matrix products, arithmetic and copies ran while one was open for 0% -> 0% of each run, Pallas kernels for 0% -> 7%
where the time goes in v3:
time: 101 us; the launch traced here: 100 us
  blocking collectives  27.5 us (27%)
  starting transfers between devices  26.2 us (26%)
  waiting for transfers between devices  20.8 us (21%)
  Pallas kernels  12.6 us (12%)
  local copies, waits for them, and re-layouts  11.9 us (12%)
    all_to_all x2, blocking collectives, exchange(): return lax.all_to_all(block, 'row', split_axis=0, concat_axis=0, tiled=True)  27.5 us
    ppermute x13, starting transfers between devices, swap(): return lax.ppermute(block, 'row', [(i, i ^ k) for i in range(devices)])  19.1 us
    ppermute x13, waiting for transfers between devices, swap(): return lax.ppermute(block, 'row', [(i, i ^ k) for i in range(devices)])  12.9 us
    unnamed x20, local copies, waits for them, and re-layouts  11.9 us
    all_to_all x2, waiting for transfers between devices, exchange(): return lax.all_to_all(block, 'row', split_axis=0, concat_axis=0, tiled=True)  7.92 us
    all_to_all x2, starting transfers between devices, exchange(): return lax.all_to_all(block, 'row', split_axis=0, concat_axis=0, tiled=True)  7.07 us
    pallas_call x2, Pallas kernels, attend(): pl.pallas_call(functools.partial(attend_kernel, start, rows), out_shape=j...  6.56 us
    pallas_call x1, Pallas kernels, output_terms(): pl.pallas_call(functools.partial(output_kernel, groups, 1024), out_shape=...  3.86 us
  transfers between devices with their start and end apart: 15, of which 10 were waited for; matrix products, arithmetic and copies ran while one was open for 0% of the time, Pallas kernels for 7%

profile of v3, /device:TPU:0, one launch (start us, length us, event | category | flops | bytes accessed | tf_op | source)
XLA Modules:
  0.0 100.0 jit_solution(5432139103125918430)
XLA Ops:
  0.0 3.0 %collective-permute-start = (bf16[4,1536]{1,0:T(4,128)(2,1)}, bf16[4,1536]{1,0:T(4,128)(2,1)S(1)}, u32[]{:S(2)}, u32[]{:S(2)}) collective-permute-start(bf16[4,1536]{1,0:T(4,128)(2,1)} %refs_0_.1), channel_id=1, source_target_pairs={{0,2},{1,3},{2,0},{3,1},{4,6},{5,7},{6,4},{7,5},{8,10},{9,11},{10,... | collective-permute-start | bytes 36872 | tf_op jit(solution)/shard_map/ppermute | solution.py:276
  3.0 1.9 %collective-permute-done.refs_1_ = bf16[4,1536]{1,0:T(4,128)(2,1)S(1)} collective-permute-done((bf16[4,1536]{1,0:T(4,128)(2,1)}, bf16[4,1536]{1,0:T(4,128)(2,1)S(1)}, u32[]{:S(2)}, u32[]{:S(2)}) %collective-permute-start) | collective-permute-done | bytes 12320 | tf_op jit(solution)/shard_map/ppermute | solution.py:276
  4.9 0.7 copy-done.5
  5.6 4.2 %collective-permute-start.3 = (bf16[8,1536]{1,0:T(8,128)(2,1)S(1)}, bf16[8,1536]{1,0:T(8,128)(2,1)S(1)}, u32[]{:S(2)}, u32[]{:S(2)}) collective-permute-start(bf16[8,1536]{1,0:T(8,128)(2,1)S(1)} %join.2.refs_0_), channel_id=1, source_target_pairs={{0,12},{1,13},{2,14},{3,15},{4,8},{5,9},{6,10},{7,11},{8,4},{9,5},... | collective-permute-start | bytes 73736 | tf_op jit(solution)/shard_map/ppermute | solution.py:276
  9.8 0.6 collective-permute-start.1
  10.4 1.2 %collective-permute-done.3.refs_3_ = bf16[8,1536]{1,0:T(8,128)(2,1)S(1)} collective-permute-done((bf16[8,1536]{1,0:T(8,128)(2,1)S(1)}, bf16[8,1536]{1,0:T(8,128)(2,1)S(1)}, u32[]{:S(2)}, u32[]{:S(2)}) %collective-permute-start.3) | collective-permute-done | bytes 24608 | tf_op jit(solution)/shard_map/ppermute | solution.py:276
  11.6 2.9 %collective-permute-done.2.refs_2_ = bf16[8,1536]{1,0:T(8,128)(2,1)S(1)} collective-permute-done((bf16[8,1536]{1,0:T(8,128)(2,1)S(1)}, bf16[8,1536]{1,0:T(8,128)(2,1)S(1)}, u32[]{:S(2)}, u32[]{:S(2)}) %collective-permute-start.2) | collective-permute-done | bytes 24608 | tf_op jit(solution)/shard_map/ppermute | solution.py:276
  14.6 1.3 %collective-permute-done.4.far_ref = bf16[32,1536]{1,0:T(8,128)(2,1)S(1)} collective-permute-done((bf16[32,1536]{1,0:T(8,128)(2,1)S(1)}, bf16[32,1536]{1,0:T(8,128)(2,1)S(1)}, u32[]{:S(2)}, u32[]{:S(2)}) %collective-permute-start.4) | collective-permute-done | bytes 98336 | tf_op jit(solution)/shard_map/ppermute | solution.py:276
  15.9 2.1 %project.1 = (bf16[16,72,128]{2,1,0:T(8,128)(2,1)S(1)}, bf16[16,72,128]{2,1,0:T(8,128)(2,1)}) custom-call(bf16[32,1536]{1,0:T(8,128)(2,1)S(1)} %join.3.q_ref, bf16[32,1536]{1,0:T(8,128)(2,1)S(1)} %collective-permute-done.4.far_ref, bf16[1536,1536]{1,0:T(8,128)(2,1)S(1)} %bitcast.4, bf16[8,128,512]{2,1,0:T(8,128)(2,1)S(1)} %copy-done.3), custom_call_target="tpu_custom_call" | custom-call | flops 23000000512 | tf_op jit(solution)/shard_map/project/pallas_call | solution.py:105
  18.0 14.7 %all_to_all.20.q_ref = bf16[16,72,128]{2,1,0:T(8,128)(2,1)S(1)} all-to-all(bf16[16,72,128]{2,1,0:T(8,128)(2,1)S(1)} %get-tuple-element.17), channel_id=1, replica_groups=mesh['grp'=2,'row'=16] {'row'}, dimensions={0} | all-to-all | bytes 589824 | tf_op jit(solution)/shard_map/all_to_all | solution.py:279
  32.7 3.5 %all-to-all-start.2 = ((bf16[16,72,128]{2,1,0:T(8,128)(2,1)}), bf16[16,72,128]{2,1,0:T(8,128)(2,1)S(1)}, u32[]{:S(2)}, u32[]{:S(2)}) async-start(bf16[16,72,128]{2,1,0:T(8,128)(2,1)} %get-tuple-element.18), calls=%async_computation.2 | async-start | bytes 589824 | tf_op jit(solution)/shard_map/all_to_all | solution.py:279
  36.3 3.0 %copy-done.1 = bf16[4,1536,576]{1,2,0:T(8,128)(2,1)S(1)} copy-done((bf16[4,1536,576]{1,2,0:T(8,128)(2,1)S(1)}, bf16[4,1536,576]{1,2,0:T(8,128)(2,1)}, u32[]{:S(2)}) %copy-start.1) | copy-done | bytes 7077912
  39.3 3.6 %attend.2 = bf16[16,16,512]{2,1,0:T(8,128)(2,1)} custom-call(s32[4]{0:T(128)S(1)} %copy-done.7, bf16[16,72,128]{2,1,0:T(8,128)(2,1)S(1)} %all_to_all.20.q_ref, bf16[4,576,1536]{2,1,0:T(8,128)(2,1)S(1)} %bitcast.1, bf16[4,576]{1,0:T(4,128)(2,1)S(1)} %copy-done.6), custom_call_target="tpu_custom_call" | custom-call | flops 11500000256 | tf_op jit(solution)/shard_map/attend/pallas_call | solution.py:183
  42.9 3.9 %all-to-all-done.2.q_ref = bf16[16,72,128]{2,1,0:T(8,128)(2,1)S(1)} async-done(((bf16[16,72,128]{2,1,0:T(8,128)(2,1)}), bf16[16,72,128]{2,1,0:T(8,128)(2,1)S(1)}, u32[]{:S(2)}, u32[]{:S(2)}) %all-to-all-start.2) | async-done | bytes 294944 | tf_op jit(solution)/shard_map/all_to_all | solution.py:279
  46.8 3.5 %all-to-all-start.1 = ((bf16[16,16,512]{2,1,0:T(8,128)(2,1)}), bf16[16,16,512]{2,1,0:T(8,128)(2,1)S(1)}, u32[]{:S(2)}, u32[]{:S(2)}) async-start(bf16[16,16,512]{2,1,0:T(8,128)(2,1)} %attend.2), calls=%async_computation.1 | async-start | bytes 524288 | tf_op jit(solution)/shard_map/all_to_all | solution.py:279
  50.3 3.0 %copy-done.2 = bf16[4,1536,576]{1,2,0:T(8,128)(2,1)S(1)} copy-done((bf16[4,1536,576]{1,2,0:T(8,128)(2,1)S(1)}, bf16[4,1536,576]{1,2,0:T(8,128)(2,1)}, u32[]{:S(2)}) %copy-start.2) | copy-done | bytes 7077912
  53.3 2.9 %attend.3 = bf16[16,16,512]{2,1,0:T(8,128)(2,1)S(1)} custom-call(s32[4]{0:T(128)S(1)} %copy-done.7, bf16[16,72,128]{2,1,0:T(8,128)(2,1)S(1)} %all-to-all-done.2.q_ref, bf16[4,576,1536]{2,1,0:T(8,128)(2,1)S(1)} %bitcast.2, bf16[4,576]{1,0:T(4,128)(2,1)S(1)} %copy-done.6), custom_call_target="tpu_custom_call" | custom-call | flops 11500000256 | tf_op jit(solution)/shard_map/attend/pallas_call | solution.py:183
  56.3 4.1 %all-to-all-done.1.refs_0_ = bf16[16,16,512]{2,1,0:T(8,128)(2,1)S(1)} async-done(((bf16[16,16,512]{2,1,0:T(8,128)(2,1)}), bf16[16,16,512]{2,1,0:T(8,128)(2,1)S(1)}, u32[]{:S(2)}, u32[]{:S(2)}) %all-to-all-start.1) | async-done | bytes 262176 | tf_op jit(solution)/shard_map/all_to_all | solution.py:279
  60.3 12.8 %all_to_all.21.refs_1_ = bf16[16,16,512]{2,1,0:T(8,128)(2,1)S(1)} all-to-all(bf16[16,16,512]{2,1,0:T(8,128)(2,1)S(1)} %attend.3), channel_id=1, replica_groups=mesh['grp'=2,'row'=16] {'row'}, dimensions={0} | all-to-all | bytes 524288 | tf_op jit(solution)/shard_map/all_to_all | solution.py:279
  73.2 5.2 %copy-done = bf16[1024,7168]{1,0:T(8,128)(2,1)S(1)} copy-done((bf16[1024,7168]{1,0:T(8,128)(2,1)S(1)}, bf16[1024,7168]{1,0:T(8,128)(2,1)}, u32[]{:S(2)}) %copy-start) | copy-done | bytes 14680088
  78.3 3.9 %output_terms.1 = (f32[32,7168]{1,0:T(8,128)S(1)}, bf16[32,7168]{1,0:T(8,128)(2,1)S(1)}) custom-call(bf16[16,16,512]{2,1,0:T(8,128)(2,1)S(1)} %all-to-all-done.1.refs_0_, bf16[16,16,512]{2,1,0:T(8,128)(2,1)S(1)} %all_to_all.21.refs_1_, bf16[8,512,128]{2,1,0:T(8,128)(2,1)S(1)} %copy-done.4, bf16[1024,7168]{1,0:T(8,128)(2,1)S(1)} %copy-done), custom_call_target="tpu_custom_call" | custom-call | flops 23000000512 | tf_op jit(solution)/shard_map/output_terms/pallas_call | solution.py:231
  82.3 1.8 %collective-permute-done.5.other_ref = bf16[32,7168]{1,0:T(8,128)(2,1)S(1)} collective-permute-done((bf16[32,7168]{1,0:T(8,128)(2,1)S(1)}, bf16[32,7168]{1,0:T(8,128)(2,1)S(1)}, u32[]{:S(2)}, u32[]{:S(2)}) %collective-permute-start.5) | collective-permute-done | bytes 458784 | tf_op jit(solution)/shard_map/ppermute | solution.py:276
  84.4 1.0 collective-permute-start.7
  85.4 2.3 %collective-permute-start.8 = (bf16[4,7168]{1,0:T(4,128)(2,1)S(1)}, bf16[4,7168]{1,0:T(4,128)(2,1)S(1)}, u32[]{:S(2)}, u32[]{:S(2)}) collective-permute-start(bf16[4,7168]{1,0:T(4,128)(2,1)S(1)} %get-tuple-element.24), channel_id=1, source_target_pairs={{0,6},{1,7},{2,4},{3,5},{4,2},{5,3},{6,0},{7,1},{8,14},{9,15},{10,... | collective-permute-start | bytes 172040 | tf_op jit(solution)/shard_map/ppermute | solution.py:276
  87.8 1.1 %collective-permute-start.9 = (bf16[4,7168]{1,0:T(4,128)(2,1)S(1)}, bf16[4,7168]{1,0:T(4,128)(2,1)S(1)}, u32[]{:S(2)}, u32[]{:S(2)}) collective-permute-start(bf16[4,7168]{1,0:T(4,128)(2,1)S(1)} %get-tuple-element.25), channel_id=1, source_target_pairs={{0,8},{1,9},{2,10},{3,11},{4,12},{5,13},{6,14},{7,15},{8,0},{9,1},... | collective-permute-start | bytes 172040 | tf_op jit(solution)/shard_map/ppermute | solution.py:276
  88.8 1.5 %collective-permute-start.10 = (bf16[4,7168]{1,0:T(4,128)(2,1)S(1)}, bf16[4,7168]{1,0:T(4,128)(2,1)S(1)}, u32[]{:S(2)}, u32[]{:S(2)}) collective-permute-start(bf16[4,7168]{1,0:T(4,128)(2,1)S(1)} %get-tuple-element.26), channel_id=1, source_target_pairs={{0,10},{1,11},{2,8},{3,9},{4,14},{5,15},{6,12},{7,13},{8,2},{9,3},... | collective-permute-start | bytes 172040 | tf_op jit(solution)/shard_map/ppermute | solution.py:276
  90.3 2.0 %collective-permute-start.11 = (bf16[4,7168]{1,0:T(4,128)(2,1)S(1)}, bf16[4,7168]{1,0:T(4,128)(2,1)S(1)}, u32[]{:S(2)}, u32[]{:S(2)}) collective-permute-start(bf16[4,7168]{1,0:T(4,128)(2,1)S(1)} %get-tuple-element.27), channel_id=1, source_target_pairs={{0,12},{1,13},{2,14},{3,15},{4,8},{5,9},{6,10},{7,11},{8,4},{9,5},... | collective-permute-start | bytes 172040 | tf_op jit(solution)/shard_map/ppermute | solution.py:276
  92.3 3.1 %collective-permute-start.12 = (bf16[4,7168]{1,0:T(4,128)(2,1)S(1)}, bf16[4,7168]{1,0:T(4,128)(2,1)S(1)}, u32[]{:S(2)}, u32[]{:S(2)}) collective-permute-start(bf16[4,7168]{1,0:T(4,128)(2,1)S(1)} %get-tuple-element.28), channel_id=1, source_target_pairs={{0,14},{1,15},{2,12},{3,13},{4,10},{5,11},{6,8},{7,9},{8,6},{9,7},... | collective-permute-start | bytes 172040 | tf_op jit(solution)/shard_map/ppermute | solution.py:276
  95.4 0.2 collective-permute-done.9
  95.7 2.3 %collective-permute-done.10 = bf16[4,7168]{1,0:T(4,128)(2,1)S(1)} collective-permute-done((bf16[4,7168]{1,0:T(4,128)(2,1)S(1)}, bf16[4,7168]{1,0:T(4,128)(2,1)S(1)}, u32[]{:S(2)}, u32[]{:S(2)}) %collective-permute-start.10) | collective-permute-done | bytes 57376 | tf_op jit(solution)/shard_map/ppermute | solution.py:276
  97.9 1.3 %collective-permute-done.12 = bf16[4,7168]{1,0:T(4,128)(2,1)S(1)} collective-permute-done((bf16[4,7168]{1,0:T(4,128)(2,1)S(1)}, bf16[4,7168]{1,0:T(4,128)(2,1)S(1)}, u32[]{:S(2)}, u32[]{:S(2)}) %collective-permute-start.12) | collective-permute-done | bytes 57376 | tf_op jit(solution)/shard_map/ppermute | solution.py:276
  99.3 0.7 add_convert_fusion
  (29 shorter events, 0.6 us)
Async XLA Ops:
  0.0 4.8 %collective-permute-start = (bf16[4,1536]{1,0:T(4,128)(2,1)}, bf16[4,1536]{1,0:T(4,128)(2,1)S(1)}, u32[]{:S(2)}, u32[]{:S(2)}) collective-permute-start(bf16[4,1536]{1,0:T(4,128)(2,1)} %refs_0_.1), channel_id=1, source_target_pairs={{0,2},{1,3},{2,0},{3,1},{4,6},{5,7},{6,4},{7,5},{8,10},{9,11},{10,... | collective-permute-start | bytes 36872 | tf_op jit(solution)/shard_map/ppermute | solution.py:276
  4.9 0.7 copy-start.5
  5.6 10.3 %slice-start = ((s8[4718592]{0:T(1024)(128)(4,1)}), s8[4194304]{0:T(1024)(128)(4,1)S(1)}, s32[]{:S(2)}) async-start(s8[4718592]{0:T(1024)(128)(4,1)} %bitcast.3), calls=%async_computation.4 | async-start | bytes 8388608
  5.6 10.3 %slice-start.1 = ((s8[4718592]{0:T(1024)(128)(4,1)}), s8[524288]{0:T(1024)(128)(4,1)S(1)}, s32[]{:S(2)}) async-start(s8[4718592]{0:T(1024)(128)(4,1)} %bitcast.3), calls=%async_computation.5 | async-start | bytes 1048576
  5.6 10.3 %copy-start.3 = (bf16[8,128,512]{2,1,0:T(8,128)(2,1)S(1)}, bf16[8,128,512]{2,1,0:T(8,128)(2,1)}, u32[]{:S(2)}) copy-start(bf16[8,128,512]{2,1,0:T(8,128)(2,1)} %wk_ref.1) | copy-start | bytes 3145732
  5.6 6.0 %collective-permute-start.3 = (bf16[8,1536]{1,0:T(8,128)(2,1)S(1)}, bf16[8,1536]{1,0:T(8,128)(2,1)S(1)}, u32[]{:S(2)}, u32[]{:S(2)}) collective-permute-start(bf16[8,1536]{1,0:T(8,128)(2,1)S(1)} %join.2.refs_0_), channel_id=1, source_target_pairs={{0,12},{1,13},{2,14},{3,15},{4,8},{5,9},{6,10},{7,11},{8,4},{9,5},... | collective-permute-start | bytes 73736 | tf_op jit(solution)/shard_map/ppermute | solution.py:276
  9.8 4.7 %collective-permute-start.2 = (bf16[8,1536]{1,0:T(8,128)(2,1)S(1)}, bf16[8,1536]{1,0:T(8,128)(2,1)S(1)}, u32[]{:S(2)}, u32[]{:S(2)}) collective-permute-start(bf16[8,1536]{1,0:T(8,128)(2,1)S(1)} %join.2.refs_0_), channel_id=1, source_target_pairs={{0,8},{1,9},{2,10},{3,11},{4,12},{5,13},{6,14},{7,15},{8,0},{9,1},... | collective-permute-start | bytes 73736 | tf_op jit(solution)/shard_map/ppermute | solution.py:276
  9.8 4.7 %collective-permute-start.1 = (bf16[8,1536]{1,0:T(8,128)(2,1)S(1)}, bf16[8,1536]{1,0:T(8,128)(2,1)S(1)}, u32[]{:S(2)}, u32[]{:S(2)}) collective-permute-start(bf16[8,1536]{1,0:T(8,128)(2,1)S(1)} %join.2.refs_0_), channel_id=1, source_target_pairs={{0,4},{1,5},{2,6},{3,7},{4,0},{5,1},{6,2},{7,3},{8,12},{9,13},{10,... | collective-permute-start | bytes 73736 | tf_op jit(solution)/shard_map/ppermute | solution.py:276
  14.5 21.8 %copy-start.6 = (bf16[4,576]{1,0:T(4,128)(2,1)S(1)}, bf16[4,576]{1,0:T(4,128)(2,1)}, u32[]{:S(2)}) copy-start(bf16[4,576]{1,0:T(4,128)(2,1)} %new_ref.3) | copy-start | bytes 13828
  14.5 21.7 %copy-start.7 = (s32[4]{0:T(128)S(1)}, s32[4]{0:T(128)}, u32[]{:S(2)}) copy-start(s32[4]{0:T(128)} %len_ref.3) | copy-start | bytes 52
  14.5 1.4 %collective-permute-start.4 = (bf16[32,1536]{1,0:T(8,128)(2,1)S(1)}, bf16[32,1536]{1,0:T(8,128)(2,1)S(1)}, u32[]{:S(2)}, u32[]{:S(2)}) collective-permute-start(bf16[32,1536]{1,0:T(8,128)(2,1)S(1)} %join.3.q_ref), channel_id=1, source_target_pairs={{0,1},{1,0},{2,3},{3,2},{4,5},{5,4},{6,7},{7,6},{8,9},{9,8},{10,11... | collective-permute-start | bytes 294920 | tf_op jit(solution)/shard_map/ppermute | solution.py:276
  32.7 14.1 %all-to-all-start.2 = ((bf16[16,72,128]{2,1,0:T(8,128)(2,1)}), bf16[16,72,128]{2,1,0:T(8,128)(2,1)S(1)}, u32[]{:S(2)}, u32[]{:S(2)}) async-start(bf16[16,72,128]{2,1,0:T(8,128)(2,1)} %get-tuple-element.18), calls=%async_computation.2 | async-start | bytes 589824 | tf_op jit(solution)/shard_map/all_to_all | solution.py:279
  36.3 3.0 %copy-start.1 = (bf16[4,1536,576]{1,2,0:T(8,128)(2,1)S(1)}, bf16[4,1536,576]{1,2,0:T(8,128)(2,1)}, u32[]{:S(2)}) copy-start(bf16[4,1536,576]{1,2,0:T(8,128)(2,1)} %param.10) | copy-start | bytes 21233668
  46.8 13.5 %all-to-all-start.1 = ((bf16[16,16,512]{2,1,0:T(8,128)(2,1)}), bf16[16,16,512]{2,1,0:T(8,128)(2,1)S(1)}, u32[]{:S(2)}, u32[]{:S(2)}) async-start(bf16[16,16,512]{2,1,0:T(8,128)(2,1)} %attend.2), calls=%async_computation.1 | async-start | bytes 524288 | tf_op jit(solution)/shard_map/all_to_all | solution.py:279
  50.3 3.0 %copy-start.2 = (bf16[4,1536,576]{1,2,0:T(8,128)(2,1)S(1)}, bf16[4,1536,576]{1,2,0:T(8,128)(2,1)}, u32[]{:S(2)}) copy-start(bf16[4,1536,576]{1,2,0:T(8,128)(2,1)} %param.10) | copy-start | bytes 21233668
  53.3 19.8 %copy-start.4 = (bf16[8,512,128]{2,1,0:T(8,128)(2,1)S(1)}, bf16[8,512,128]{2,1,0:T(8,128)(2,1)}, u32[]{:S(2)}) copy-start(bf16[8,512,128]{2,1,0:T(8,128)(2,1)} %refs_2_.1) | copy-start | bytes 3145732
  73.2 5.2 %copy-start = (bf16[1024,7168]{1,0:T(8,128)(2,1)S(1)}, bf16[1024,7168]{1,0:T(8,128)(2,1)}, u32[]{:S(2)}) copy-start(bf16[1024,7168]{1,0:T(8,128)(2,1)} %refs_3_.1) | copy-start | bytes 44040196
  82.2 1.9 %collective-permute-start.5 = (bf16[32,7168]{1,0:T(8,128)(2,1)S(1)}, bf16[32,7168]{1,0:T(8,128)(2,1)S(1)}, u32[]{:S(2)}, u32[]{:S(2)}) collective-permute-start(bf16[32,7168]{1,0:T(8,128)(2,1)S(1)} %get-tuple-element.20), channel_id=1, source_target_pairs={{0,1},{1,0},{2,3},{3,2},{4,5},{5,4},{6,7},{7,6},{8,9},{9,8},{10,11... | collective-permute-start | bytes 1376264 | tf_op jit(solution)/shard_map/ppermute | solution.py:276
  84.2 6.1 %collective-permute-start.6 = (bf16[4,7168]{1,0:T(4,128)(2,1)S(1)}, bf16[4,7168]{1,0:T(4,128)(2,1)S(1)}, u32[]{:S(2)}, u32[]{:S(2)}) collective-permute-start(bf16[4,7168]{1,0:T(4,128)(2,1)S(1)} %get-tuple-element.22), channel_id=1, source_target_pairs={{0,2},{1,3},{2,0},{3,1},{4,6},{5,7},{6,4},{7,5},{8,10},{9,11},{10,... | collective-permute-start | bytes 172040 | tf_op jit(solution)/shard_map/ppermute | solution.py:276
  84.4 7.8 %collective-permute-start.7 = (bf16[4,7168]{1,0:T(4,128)(2,1)S(1)}, bf16[4,7168]{1,0:T(4,128)(2,1)S(1)}, u32[]{:S(2)}, u32[]{:S(2)}) collective-permute-start(bf16[4,7168]{1,0:T(4,128)(2,1)S(1)} %get-tuple-element.23), channel_id=1, source_target_pairs={{0,4},{1,5},{2,6},{3,7},{4,0},{5,1},{6,2},{7,3},{8,12},{9,13},{10,... | collective-permute-start | bytes 172040 | tf_op jit(solution)/shard_map/ppermute | solution.py:276
  85.4 10.0 %collective-permute-start.8 = (bf16[4,7168]{1,0:T(4,128)(2,1)S(1)}, bf16[4,7168]{1,0:T(4,128)(2,1)S(1)}, u32[]{:S(2)}, u32[]{:S(2)}) collective-permute-start(bf16[4,7168]{1,0:T(4,128)(2,1)S(1)} %get-tuple-element.24), channel_id=1, source_target_pairs={{0,6},{1,7},{2,4},{3,5},{4,2},{5,3},{6,0},{7,1},{8,14},{9,15},{10,... | collective-permute-start | bytes 172040 | tf_op jit(solution)/shard_map/ppermute | solution.py:276
  87.8 7.9 %collective-permute-start.9 = (bf16[4,7168]{1,0:T(4,128)(2,1)S(1)}, bf16[4,7168]{1,0:T(4,128)(2,1)S(1)}, u32[]{:S(2)}, u32[]{:S(2)}) collective-permute-start(bf16[4,7168]{1,0:T(4,128)(2,1)S(1)} %get-tuple-element.25), channel_id=1, source_target_pairs={{0,8},{1,9},{2,10},{3,11},{4,12},{5,13},{6,14},{7,15},{8,0},{9,1},... | collective-permute-start | bytes 172040 | tf_op jit(solution)/shard_map/ppermute | solution.py:276
  88.8 9.1 %collective-permute-start.10 = (bf16[4,7168]{1,0:T(4,128)(2,1)S(1)}, bf16[4,7168]{1,0:T(4,128)(2,1)S(1)}, u32[]{:S(2)}, u32[]{:S(2)}) collective-permute-start(bf16[4,7168]{1,0:T(4,128)(2,1)S(1)} %get-tuple-element.26), channel_id=1, source_target_pairs={{0,10},{1,11},{2,8},{3,9},{4,14},{5,15},{6,12},{7,13},{8,2},{9,3},... | collective-permute-start | bytes 172040 | tf_op jit(solution)/shard_map/ppermute | solution.py:276
  90.3 7.6 %collective-permute-start.11 = (bf16[4,7168]{1,0:T(4,128)(2,1)S(1)}, bf16[4,7168]{1,0:T(4,128)(2,1)S(1)}, u32[]{:S(2)}, u32[]{:S(2)}) collective-permute-start(bf16[4,7168]{1,0:T(4,128)(2,1)S(1)} %get-tuple-element.27), channel_id=1, source_target_pairs={{0,12},{1,13},{2,14},{3,15},{4,8},{5,9},{6,10},{7,11},{8,4},{9,5},... | collective-permute-start | bytes 172040 | tf_op jit(solution)/shard_map/ppermute | solution.py:276
  92.3 7.0 %collective-permute-start.12 = (bf16[4,7168]{1,0:T(4,128)(2,1)S(1)}, bf16[4,7168]{1,0:T(4,128)(2,1)S(1)}, u32[]{:S(2)}, u32[]{:S(2)}) collective-permute-start(bf16[4,7168]{1,0:T(4,128)(2,1)S(1)} %get-tuple-element.28), channel_id=1, source_target_pairs={{0,14},{1,15},{2,12},{3,13},{4,10},{5,11},{6,8},{7,9},{8,6},{9,7},... | collective-permute-start | bytes 172040 | tf_op jit(solution)/shard_map/ppermute | solution.py:276

commit v4 on v2

v4 whole, which is shorter than its diff:
```python
import functools
import math

import jax
import jax.numpy as jnp
from jax import lax
from jax.experimental import pallas as pl
from jax.experimental.pallas import tpu as pltpu
from jax.sharding import PartitionSpec as P

LAT = 512
ROPE = 64
HALF = ROPE // 2
NOPE = 128
VD = 128
LANES = 128
PIECES = LAT // LANES
FACTOR = (NOPE + ROPE) ** -0.5
LIMIT = 16 * 2**20
PARTS = 2
BLOCK = 512


def resident(x):
    return pltpu.with_memory_space_constraint(x, pltpu.VMEM)


def in_vmem():
    return pl.BlockSpec(memory_space=pltpu.VMEM)


def call(kernel, out_shape, microseconds, name, scratch=(), scalars=0):
    def run(*args):
        smem = [pl.BlockSpec(memory_space=pltpu.SMEM)] * scalars
        return pl.pallas_call(
            kernel,
            out_shape=out_shape,
            in_specs=smem + [in_vmem()] * (len(args) - scalars),
            out_specs=jax.tree.map(lambda _: in_vmem(), out_shape),
            scratch_shapes=list(scratch),
            compiler_params=pltpu.CompilerParams(vmem_limit_bytes=LIMIT),
            cost_estimate=pl.CostEstimate(
                flops=int(microseconds * 1.15e9), bytes_accessed=0, transcendentals=0
            ),
            name=name,
        )(*args)

    return run


def shape(*dims, dtype=jnp.bfloat16):
    return jax.ShapeDtypeStruct(dims, dtype)


def chip_order(devices):
    return sorted(range(0, devices, 2), key=lambda k: -k.bit_length())


def gathered_order(devices):
    return [z + y + c for c in range(2) for z in range(0, devices, 4) for y in (0, 2)]


def rotary_kernel(len_ref, cos_ref, sin_ref):
    rows, width = cos_ref.shape
    lane = lax.broadcasted_iota(jnp.int32, (rows, width), 1)
    place = lax.broadcasted_iota(jnp.int32, (rows, width), 0)
    step = jnp.where(lane < HALF, lane, lane - HALF).astype(jnp.float32)
    frequency = jnp.exp(step * (-math.log(10000.0) / HALF))
    length = jnp.zeros((rows, width), jnp.float32)
    for r in range(rows):
        length = jnp.where(place == r, len_ref[r].astype(jnp.float32), length)
    angle = length * frequency
    sine = jnp.sin(angle)
    cos_ref[...] = jnp.cos(angle)
    sin_ref[...] = jnp.where(lane < HALF, -sine, sine)


def rotary(lengths):
    table = shape(lengths.shape[0], ROPE, dtype=jnp.float32)
    return call(rotary_kernel, (table, table), 3, "rotary", scalars=1)(lengths)


def join_kernel(*refs):
    *in_refs, out_ref = refs
    out_ref[...] = jnp.concatenate(
        [ref[...].astype(jnp.float32) for ref in in_refs], axis=0
    ).astype(out_ref.dtype)


def join(blocks):
    rows, depth = blocks[0].shape
    return call(join_kernel, shape(len(blocks) * rows, depth), 5, "join")(*blocks)


def project_kernel(devices, q_ref, far_ref, wq_ref, wk_ref, mine_ref, other_ref, lat_ref, rot_ref):
    heads = wk_ref.shape[0]
    count = 2 * q_ref.shape[0]
    wide = count // devices * heads
    width = NOPE + ROPE
    piece = jnp.concatenate([q_ref[...], far_ref[...]], axis=0)
    projected = jnp.dot(piece, wq_ref[...], preferred_element_type=jnp.float32)
    for h in range(heads):
        mine = projected[:, h * width : (h + 1) * width]
        absorbed = jnp.dot(
            mine[:, :NOPE].astype(jnp.bfloat16), wk_ref[h], preferred_element_type=jnp.float32
        )
        for c in range(PIECES):
            lat_ref[c, pl.ds(h, count, stride=heads), :] = absorbed[:, c * LANES : (c + 1) * LANES]
        pe = mine[:, NOPE:]
        rot_ref[pl.ds(h, count, stride=heads), :] = jnp.concatenate([pe, pe], axis=-1)
    lane = lax.broadcasted_iota(jnp.int32, (wide // 2, LANES), 1)
    order = chip_order(devices)
    for place, k in enumerate(gathered_order(devices)):
        out_ref = other_ref if k % 2 else mine_ref
        at = order.index(k - k % 2)
        first = place * wide
        for c in range(PIECES):
            out_ref[at, c * wide : (c + 1) * wide, :] = lat_ref[c, first : first + wide, :].astype(
                jnp.bfloat16
            )
        low = rot_ref[first : first + wide // 2, :]
        high = rot_ref[first + wide // 2 : first + wide, :]
        out_ref[at, PIECES * wide :, :] = jnp.where(lane < ROPE, low, high).astype(jnp.bfloat16)


def project(near, far, w_uq, w_uk, devices):
    heads = w_uk.shape[0]
    count = 2 * near.shape[0]
    wide = count // devices * heads
    half = shape(devices // 2, PIECES * wide + wide // 2, LANES)
    scratch = [
        pltpu.VMEM((PIECES, count * heads, LANES), jnp.float32),
        pltpu.VMEM((count * heads, LANES), jnp.float32),
    ]
    kernel = functools.partial(project_kernel, devices)
    return call(kernel, (half, half), 20, "project", scratch)(
        near, far, resident(w_uq), resident(w_uk)
    )


def pack_kernel(mine_ref, other_ref, *out_refs):
    for j, out_ref in enumerate(out_refs):
        out_ref[0] = mine_ref[j]
        out_ref[1] = other_ref[j]


def pack(mine, other):
    chips, count, width = mine.shape
    return call(pack_kernel, [shape(2, count, width)] * chips, 1, "pack")(mine, other)


def attend_kernel(chips, len_ref, cos_ref, sin_ref, key_ref, new_ref, *refs):
    q_refs = refs[:chips]
    out_refs = refs[chips:]
    rows, _, maxlen = key_ref.shape
    wide = out_refs[0].shape[1]
    heads = wide // rows

    def query_block(first):
        blocks = [
            ref[core, first : first + heads, :].astype(jnp.float32)
            for ref in q_refs
            for core in range(2)
        ]
        return jnp.concatenate(blocks, axis=0)

    for r in range(rows):
        latent = jnp.concatenate(
            [query_block(c * wide + r * heads) for c in range(PIECES)], axis=-1
        )
        pe = query_block(PIECES * wide + (r % (rows // 2)) * heads)
        side = r // (rows // 2) * ROPE
        pe = pe[:, side : side + ROPE]
        swapped = jnp.concatenate([pe[:, HALF:], pe[:, :HALF]], axis=-1)
        rotated = (pe * cos_ref[r : r + 1, :] + swapped * sin_ref[r : r + 1, :]).astype(jnp.bfloat16)
        newest = new_ref[r : r + 1, :].astype(jnp.float32)
        own = (
            jnp.sum(latent * newest[:, :LAT], axis=-1, keepdims=True)
            + jnp.sum(rotated.astype(jnp.float32) * newest[:, LAT:], axis=-1, keepdims=True)
        ) * FACTOR
        scores = jnp.dot(
            latent.astype(jnp.bfloat16), key_ref[r, :LAT, :], preferred_element_type=jnp.float32
        )
        scores += jnp.dot(rotated, key_ref[r, LAT:, :], preferred_element_type=jnp.float32)
        position = lax.broadcasted_iota(jnp.int32, (1, maxlen), 1)
        scores = jnp.where(position < len_ref[r], scores * FACTOR, -jnp.inf)
        peak = jnp.maximum(jnp.max(scores, axis=-1, keepdims=True), own)
        expo = jnp.exp(scores - peak)
        own_expo = jnp.exp(own - peak)
        total = jnp.sum(expo, axis=-1, keepdims=True) + own_expo
        weights = (expo / total).astype(jnp.bfloat16)
        own_weight = (own_expo / total).astype(jnp.bfloat16).astype(jnp.float32)
        summed = lax.dot_general(
            weights,
            key_ref[r, :LAT, :],
            (((1,), (1,)), ((), ())),
            preferred_element_type=jnp.float32,
        )
        summed += own_weight * newest[:, :LAT]
        for k in range(2 * chips):
            out_refs[k // 2][k % 2, r * heads : (r + 1) * heads, :] = summed[
                k * heads : (k + 1) * heads, :
            ].astype(jnp.bfloat16)


def attend(lengths, tables, keys, new_latent, messages, heads):
    chips = len(messages)
    kernel = functools.partial(attend_kernel, chips)
    block = shape(2, keys.shape[0] * heads, LAT)
    return call(kernel, [block] * chips, 2 + chips, "attend", scalars=1)(
        lengths, *tables, resident(keys), new_latent, *messages
    )


def regroup_kernel(*refs):
    *in_refs, out_ref = refs
    for j, ref in enumerate(in_refs):
        out_ref[j] = ref[1]


def regroup(messages):
    _, wide, width = messages[0].shape
    return call(regroup_kernel, shape(len(messages), wide, width), 1, "regroup")(*messages)


def values_kernel(chips, *refs):
    mine_refs = refs[:chips]
    other_ref, wv_ref, val_ref, rows_ref = refs[chips:]
    heads = wv_ref.shape[0]
    wide = other_ref.shape[1]
    for place in range(2 * chips):
        block = mine_refs[place][0] if place < chips else other_ref[place - chips]
        block = block.astype(jnp.float32)
        for c in range(PIECES):
            rows_ref[c, place * wide : (place + 1) * wide, :] = block[:, c * LANES : (c + 1) * LANES]
    count = val_ref.shape[0]
    for h in range(heads):
        chosen = jnp.concatenate(
            [rows_ref[c, pl.ds(h, count, stride=heads), :] for c in range(PIECES)], axis=-1
        )
        val_ref[:, h * VD : (h + 1) * VD] = jnp.dot(
            chosen.astype(jnp.bfloat16), wv_ref[h], preferred_element_type=jnp.float32
        ).astype(jnp.bfloat16)


def head_values(messages, other, w_uv):
    chips, wide, _ = other.shape
    heads = w_uv.shape[0]
    count = 2 * chips * wide // heads
    scratch = [pltpu.VMEM((PIECES, count * heads, LANES), jnp.float32)]
    kernel = functools.partial(values_kernel, chips)
    return call(kernel, shape(count, heads * VD), 3, "values", scratch)(
        *messages, other, resident(w_uv)
    )


def terms_kernel(start, val_ref, wo_ref, mine_ref, other_ref):
    half, width = mine_ref.shape

    def step(index, carry):
        here = pl.ds(pl.multiple_of(index * BLOCK, BLOCK), BLOCK)
        there = pl.ds(pl.multiple_of(start + index * BLOCK, BLOCK), BLOCK)
        terms = jnp.dot(val_ref[...], wo_ref[:, there], preferred_element_type=jnp.float32)
        mine_ref[:, here] = terms[:half]
        other_ref[:, here] = terms[half:].astype(jnp.bfloat16)
        return carry

    lax.fori_loop(0, width // BLOCK, step, 0)


def output_terms(values, w_o, part):
    half = values.shape[0] // 2
    width = w_o.shape[1] // PARTS
    out = (shape(half, width, dtype=jnp.float32), shape(half, width))
    kernel = functools.partial(terms_kernel, part * width)
    return call(kernel, out, 6, "terms")(values, resident(w_o))


def pair_kernel(rows, *refs):
    mine_refs = refs[:PARTS]
    other_refs = refs[PARTS : 2 * PARTS]
    out_refs = refs[2 * PARTS :]
    for p, (mine_ref, other_ref) in enumerate(zip(mine_refs, other_refs)):
        width = mine_ref.shape[1]
        total = mine_ref[...] + other_ref[...].astype(jnp.float32)
        for j, out_ref in enumerate(out_refs):
            out_ref[:, p * width : (p + 1) * width] = total[j * rows : (j + 1) * rows].astype(
                out_ref.dtype
            )


def pair_sum(mine, other, rows):
    count, width = mine[0].shape
    chips = count // rows
    out = [shape(rows, PARTS * width)] * (chips - 1)
    out += [shape(rows, PARTS * width, dtype=jnp.float32)]
    return call(functools.partial(pair_kernel, rows), out, 1, "pair_sum")(*mine, *other)


def on_device(q_latent, new_latent, cache, lengths, w_uq, w_uk, w_uv, w_o, devices):
    heads = w_uk.shape[0]
    rows = cache.shape[0]
    order = chip_order(devices)
    chips = len(order)
    quarter = chips // 4

    def swap(block, k):
        if k == 0:
            return block
        return lax.ppermute(block, "row", [(i, i ^ k) for i in range(devices)])

    near = join([q_latent, swap(q_latent, 2)])
    tables = rotary(lengths)
    near = join([swap(near, z) for z in range(0, devices, 4)])
    mine, other = project(near, swap(near, 1), w_uq, w_uk, devices)
    messages = pack(mine, swap(other, 1))
    messages = [swap(block, k) for k, block in zip(order, messages)]
    keys = jnp.swapaxes(cache, 1, 2)
    latents = []
    for first, last in ((0, quarter), (quarter, 2 * quarter), (2 * quarter, chips)):
        done = attend(lengths, tables, keys, new_latent, messages[first:last], heads)
        latents += [swap(block, k) for k, block in zip(order[first:last], done)]
    values = head_values(latents, swap(regroup(latents), 1), w_uv)
    terms = [output_terms(values, w_o, part) for part in range(PARTS)]
    shares = pair_sum([a for a, _ in terms], [swap(b, 1) for _, b in terms], rows)
    shares = [swap(block, k).astype(jnp.float32) for k, block in zip(order, shares)]
    return sum(shares[:-1], shares[-1]).astype(jnp.bfloat16)


def solution(mesh):
    placed = (
        P(("grp", "row"), None),
        P(("grp", "row"), None),
        P(("grp", "row"), None, None),
        P(("grp", "row")),
        P(None, "row"),
        P("row", None, None),
        P("row", None, None),
        P("row", None),
    )
    body = functools.partial(on_device, devices=mesh.shape["row"])
    return jax.shard_map(
        body, mesh=mesh, in_specs=placed, out_specs=P(("grp", "row"), None), check_vma=False
    )
```

time: 110 us -> 87.7 us (0.80)
  starting transfers between devices: 75.1 us -> 40.5 us
  Pallas kernels: 10.6 us -> 21.5 us
  waiting for transfers between devices: 19 us -> 23.7 us
  local copies, waits for them, and re-layouts: 4.3 us -> 0.77 us
    ppermute x53 -> x30, starting transfers between devices: 75.1 us -> 40.5 us  [swap(): return lax.ppermute(block, 'row', [(i, i ^ k) for i in range(devices)])]
    pallas_call x4 -> x13, Pallas kernels: 10.6 us -> 21.5 us  [run(): pl.pallas_call(kernel, out_shape=out_shape, in_specs=smem + [in_vmem()] *...]
    ppermute x53 -> x30, waiting for transfers between devices: 19 us -> 23.7 us  [swap(): return lax.ppermute(block, 'row', [(i, i ^ k) for i in range(devices)])]
    unnamed x22 -> x26, local copies, waits for them, and re-layouts: 4.3 us -> 0.77 us
  transfers between devices with their start and end apart: 53 -> 30, of which waited for: 11 -> 16; matrix products, arithmetic and copies ran while one was open for 0% -> 0% of each run, Pallas kernels for 0% -> 17%
where the time goes in v4:
time: 87.7 us; the launch traced here: 87.5 us
  starting transfers between devices  40.5 us (46%)
  waiting for transfers between devices  23.7 us (27%)
  Pallas kernels  21.5 us (25%)
    ppermute x30, starting transfers between devices, swap(): return lax.ppermute(block, 'row', [(i, i ^ k) for i in range(devices)])  40.5 us
    ppermute x30, waiting for transfers between devices, swap(): return lax.ppermute(block, 'row', [(i, i ^ k) for i in range(devices)])  23.7 us
    pallas_call x13, Pallas kernels, run(): pl.pallas_call(kernel, out_shape=out_shape, in_specs=smem + [in_vmem()] *...  21.5 us
  transfers between devices with their start and end apart: 30, of which 16 were waited for; matrix products, arithmetic and copies ran while one was open for 0% of the time, Pallas kernels for 17%

profile of v4, /device:TPU:0, one launch (start us, length us, event | category | flops | bytes accessed | tf_op | source)
XLA Modules:
  0.0 87.5 jit_solution(13325575958351547297)
XLA Ops:
  0.0 3.0 %collective-permute-start = (bf16[4,1536]{1,0:T(4,128)(2,1)}, bf16[4,1536]{1,0:T(4,128)(2,1)S(1)}, u32[]{:S(2)}, u32[]{:S(2)}) collective-permute-start(bf16[4,1536]{1,0:T(4,128)(2,1)} %refs_0_.1), channel_id=1, source_target_pairs={{0,2},{1,3},{2,0},{3,1},{4,6},{5,7},{6,4},{7,5},{8,10},{9,11},{10,... | collective-permute-start | bytes 36872 | tf_op jit(solution)/shard_map/ppermute | solution.py:310
  3.0 1.9 %collective-permute-done.refs_1_ = bf16[4,1536]{1,0:T(4,128)(2,1)S(1)} collective-permute-done((bf16[4,1536]{1,0:T(4,128)(2,1)}, bf16[4,1536]{1,0:T(4,128)(2,1)S(1)}, u32[]{:S(2)}, u32[]{:S(2)}) %collective-permute-start) | collective-permute-done | bytes 12320 | tf_op jit(solution)/shard_map/ppermute | solution.py:310
  5.6 4.2 %collective-permute-start.3 = (bf16[8,1536]{1,0:T(8,128)(2,1)S(1)}, bf16[8,1536]{1,0:T(8,128)(2,1)S(1)}, u32[]{:S(2)}, u32[]{:S(2)}) collective-permute-start(bf16[8,1536]{1,0:T(8,128)(2,1)S(1)} %join.2.refs_0_), channel_id=1, source_target_pairs={{0,12},{1,13},{2,14},{3,15},{4,8},{5,9},{6,10},{7,11},{8,4},{9,5},... | collective-permute-start | bytes 73736 | tf_op jit(solution)/shard_map/ppermute | solution.py:310
  11.6 2.9 %collective-permute-done.2.refs_2_ = bf16[8,1536]{1,0:T(8,128)(2,1)S(1)} collective-permute-done((bf16[8,1536]{1,0:T(8,128)(2,1)S(1)}, bf16[8,1536]{1,0:T(8,128)(2,1)S(1)}, u32[]{:S(2)}, u32[]{:S(2)}) %collective-permute-start.2) | collective-permute-done | bytes 24608 | tf_op jit(solution)/shard_map/ppermute | solution.py:310
  14.6 1.3 %collective-permute-done.4.far_ref = bf16[32,1536]{1,0:T(8,128)(2,1)S(1)} collective-permute-done((bf16[32,1536]{1,0:T(8,128)(2,1)S(1)}, bf16[32,1536]{1,0:T(8,128)(2,1)S(1)}, u32[]{:S(2)}, u32[]{:S(2)}) %collective-permute-start.4) | collective-permute-done | bytes 98336 | tf_op jit(solution)/shard_map/ppermute | solution.py:310
  15.9 1.4 %project.1 = (bf16[8,144,128]{2,1,0:T(8,128)(2,1)S(1)}, bf16[8,144,128]{2,1,0:T(8,128)(2,1)S(1)}) custom-call(bf16[32,1536]{1,0:T(8,128)(2,1)S(1)} %join.3.q_ref, bf16[32,1536]{1,0:T(8,128)(2,1)S(1)} %collective-permute-done.4.far_ref, bf16[1536,1536]{1,0:T(8,128)(2,1)S(1)} %bitcast.9, bf16[8,128,512]{2,1,0:T(8,128)(2,1)S(1)} %copy-done), custom_call_target="tpu_custom_call" | custom-call | flops 23000000512 | tf_op jit(solution)/shard_map/project/pallas_call | solution.py:35
  17.5 1.4 %collective-permute-done.5.other_ref = bf16[8,144,128]{2,1,0:T(8,128)(2,1)S(1)} collective-permute-done((bf16[8,144,128]{2,1,0:T(8,128)(2,1)S(1)}, bf16[8,144,128]{2,1,0:T(8,128)(2,1)S(1)}, u32[]{:S(2)}, u32[]{:S(2)}) %collective-permute-start.5) | collective-permute-done | bytes 294944 | tf_op jit(solution)/shard_map/ppermute | solution.py:310
  19.0 2.1 %collective-permute-start.6 = (bf16[2,144,128]{2,1,0:T(8,128)(2,1)S(1)}, bf16[2,144,128]{2,1,0:T(8,128)(2,1)S(1)}, u32[]{:S(2)}, u32[]{:S(2)}) collective-permute-start(bf16[2,144,128]{2,1,0:T(8,128)(2,1)S(1)} %get-tuple-element.41), channel_id=1, source_target_pairs={{0,8},{1,9},{2,10},{3,11},{4,12},{5,13},{6,14},{7,15},{8,0},{9,1},... | collective-permute-start | bytes 221192 | tf_op jit(solution)/shard_map/ppermute | solution.py:310
  21.1 1.9 %collective-permute-start.7 = (bf16[2,144,128]{2,1,0:T(8,128)(2,1)S(1)}, bf16[2,144,128]{2,1,0:T(8,128)(2,1)S(1)}, u32[]{:S(2)}, u32[]{:S(2)}) collective-permute-start(bf16[2,144,128]{2,1,0:T(8,128)(2,1)S(1)} %get-tuple-element.42), channel_id=1, source_target_pairs={{0,10},{1,11},{2,8},{3,9},{4,14},{5,15},{6,12},{7,13},{8,2},{9,3},... | collective-permute-start | bytes 221192 | tf_op jit(solution)/shard_map/ppermute | solution.py:310
  23.5 1.5 %collective-permute-start.10 = (bf16[2,144,128]{2,1,0:T(8,128)(2,1)S(1)}, bf16[2,144,128]{2,1,0:T(8,128)(2,1)S(1)}, u32[]{:S(2)}, u32[]{:S(2)}) collective-permute-start(bf16[2,144,128]{2,1,0:T(8,128)(2,1)S(1)} %get-tuple-element.45), channel_id=1, source_target_pairs={{0,12},{1,13},{2,14},{3,15},{4,8},{5,9},{6,10},{7,11},{8,4},{9,5},... | collective-permute-start | bytes 221192 | tf_op jit(solution)/shard_map/ppermute | solution.py:310
  25.1 2.3 %collective-permute-start.11 = (bf16[2,144,128]{2,1,0:T(8,128)(2,1)S(1)}, bf16[2,144,128]{2,1,0:T(8,128)(2,1)S(1)}, u32[]{:S(2)}, u32[]{:S(2)}) collective-permute-start(bf16[2,144,128]{2,1,0:T(8,128)(2,1)S(1)} %get-tuple-element.46), channel_id=1, source_target_pairs={{0,14},{1,15},{2,12},{3,13},{4,10},{5,11},{6,8},{7,9},{8,6},{9,7},... | collective-permute-start | bytes 221192 | tf_op jit(solution)/shard_map/ppermute | solution.py:310
  27.4 3.0 %collective-permute-start.15 = (bf16[2,144,128]{2,1,0:T(8,128)(2,1)S(1)}, bf16[2,144,128]{2,1,0:T(8,128)(2,1)S(1)}, u32[]{:S(2)}, u32[]{:S(2)}) collective-permute-start(bf16[2,144,128]{2,1,0:T(8,128)(2,1)S(1)} %get-tuple-element.50), channel_id=1, source_target_pairs={{0,6},{1,7},{2,4},{3,5},{4,2},{5,3},{6,0},{7,1},{8,14},{9,15},{10,... | collective-permute-start | bytes 221192 | tf_op jit(solution)/shard_map/ppermute | solution.py:310
  30.4 1.8 %collective-permute-done.7.refs_1_ = bf16[2,144,128]{2,1,0:T(8,128)(2,1)S(1)} collective-permute-done((bf16[2,144,128]{2,1,0:T(8,128)(2,1)S(1)}, bf16[2,144,128]{2,1,0:T(8,128)(2,1)S(1)}, u32[]{:S(2)}, u32[]{:S(2)}) %collective-permute-start.7) | collective-permute-done | bytes 73760 | tf_op jit(solution)/shard_map/ppermute | solution.py:310
  32.4 4.8 %attend.3 = (bf16[2,32,512]{2,1,0:T(8,128)(2,1)S(1)}, bf16[2,32,512]{2,1,0:T(8,128)(2,1)S(1)}) custom-call(s32[4]{0:T(128)S(1)} %copy-done.4, f32[4,64]{1,0:T(4,128)S(1)} %get-tuple-element.37.cos_ref, f32[4,64]{1,0:T(4,128)S(1)} %get-tuple-element.38.sin_ref, bf16[4,576,1536]{2,1,0:T(8,128)(2,1)S(1)} %bitcast.5, bf16[4,576]{1,0:T(4,128)(2,1)S(1)} %copy-done.3, ...), custom_call_target="tpu_custom_call" | custom-call | flops 4600000000 | tf_op jit(solution)/shard_map/attend/pallas_call | solution.py:35
  37.2 1.4 %collective-permute-start.8 = (bf16[2,32,512]{2,1,0:T(8,128)(2,1)S(1)}, bf16[2,32,512]{2,1,0:T(8,128)(2,1)S(1)}, u32[]{:S(2)}, u32[]{:S(2)}) collective-permute-start(bf16[2,32,512]{2,1,0:T(8,128)(2,1)S(1)} %get-tuple-element.43), channel_id=1, source_target_pairs={{0,8},{1,9},{2,10},{3,11},{4,12},{5,13},{6,14},{7,15},{8,0},{9,1},... | collective-permute-start | bytes 196616 | tf_op jit(solution)/shard_map/ppermute | solution.py:310
  38.6 2.9 %collective-permute-start.9 = (bf16[2,32,512]{2,1,0:T(8,128)(2,1)S(1)}, bf16[2,32,512]{2,1,0:T(8,128)(2,1)S(1)}, u32[]{:S(2)}, u32[]{:S(2)}) collective-permute-start(bf16[2,32,512]{2,1,0:T(8,128)(2,1)S(1)} %get-tuple-element.44), channel_id=1, source_target_pairs={{0,10},{1,11},{2,8},{3,9},{4,14},{5,15},{6,12},{7,13},{8,2},{9,3},... | collective-permute-start | bytes 196616 | tf_op jit(solution)/shard_map/ppermute | solution.py:310
  41.5 4.8 %attend.4 = (bf16[2,32,512]{2,1,0:T(8,128)(2,1)S(1)}, bf16[2,32,512]{2,1,0:T(8,128)(2,1)S(1)}) custom-call(s32[4]{0:T(128)S(1)} %copy-done.4, f32[4,64]{1,0:T(4,128)S(1)} %get-tuple-element.37.cos_ref, f32[4,64]{1,0:T(4,128)S(1)} %get-tuple-element.38.sin_ref, bf16[4,576,1536]{2,1,0:T(8,128)(2,1)S(1)} %bitcast.6, bf16[4,576]{1,0:T(4,128)(2,1)S(1)} %copy-done.3, ...), custom_call_target="tpu_custom_call" | custom-call | flops 4600000000 | tf_op jit(solution)/shard_map/attend/pallas_call | solution.py:35
  46.3 3.3 %collective-permute-start.12 = (bf16[2,32,512]{2,1,0:T(8,128)(2,1)S(1)}, bf16[2,32,512]{2,1,0:T(8,128)(2,1)S(1)}, u32[]{:S(2)}, u32[]{:S(2)}) collective-permute-start(bf16[2,32,512]{2,1,0:T(8,128)(2,1)S(1)} %get-tuple-element.47), channel_id=1, source_target_pairs={{0,12},{1,13},{2,14},{3,15},{4,8},{5,9},{6,10},{7,11},{8,4},{9,5},... | collective-permute-start | bytes 196616 | tf_op jit(solution)/shard_map/ppermute | solution.py:310
  49.9 5.1 %attend.5 = (bf16[2,32,512]{2,1,0:T(8,128)(2,1)S(1)}, bf16[2,32,512]{2,1,0:T(8,128)(2,1)S(1)}, bf16[2,32,512]{2,1,0:T(8,128)(2,1)S(1)}, bf16[2,32,512]{2,1,0:T(8,128)(2,1)S(1)}) custom-call(s32[4]{0:T(128)S(1)} %copy-done.4, f32[4,64]{1,0:T(4,128)S(1)} %get-tuple-element.37.cos_ref, f32[4,64]{1,0:T(4,128)S(1)} %get-tuple-element.38.sin_ref, ...), custom_call_target="tpu_custom_call" | custom-call | flops 6899999744 | tf_op jit(solution)/shard_map/attend/pallas_call | solution.py:35
  55.0 3.3 %collective-permute-start.18 = (bf16[2,32,512]{2,1,0:T(8,128)(2,1)S(1)}, bf16[2,32,512]{2,1,0:T(8,128)(2,1)S(1)}, u32[]{:S(2)}, u32[]{:S(2)}) collective-permute-start(bf16[2,32,512]{2,1,0:T(8,128)(2,1)S(1)} %get-tuple-element.54), channel_id=1, source_target_pairs={{0,6},{1,7},{2,4},{3,5},{4,2},{5,3},{6,0},{7,1},{8,14},{9,15},{10,... | collective-permute-start | bytes 196616 | tf_op jit(solution)/shard_map/ppermute | solution.py:310
  59.3 2.0 %collective-permute-done.18.refs_5_ = bf16[2,32,512]{2,1,0:T(8,128)(2,1)S(1)} collective-permute-done((bf16[2,32,512]{2,1,0:T(8,128)(2,1)S(1)}, bf16[2,32,512]{2,1,0:T(8,128)(2,1)S(1)}, u32[]{:S(2)}, u32[]{:S(2)}) %collective-permute-start.18) | collective-permute-done | bytes 65568 | tf_op jit(solution)/shard_map/ppermute | solution.py:310
  61.2 1.3 %collective-permute-done.19.refs_6_ = bf16[2,32,512]{2,1,0:T(8,128)(2,1)S(1)} collective-permute-done((bf16[2,32,512]{2,1,0:T(8,128)(2,1)S(1)}, bf16[2,32,512]{2,1,0:T(8,128)(2,1)S(1)}, u32[]{:S(2)}, u32[]{:S(2)}) %collective-permute-start.19) | collective-permute-done | bytes 65568 | tf_op jit(solution)/shard_map/ppermute | solution.py:310
  62.7 1.5 %collective-permute-done.20.refs_8_ = bf16[8,32,512]{2,1,0:T(8,128)(2,1)S(1)} collective-permute-done((bf16[8,32,512]{2,1,0:T(8,128)(2,1)S(1)}, bf16[8,32,512]{2,1,0:T(8,128)(2,1)S(1)}, u32[]{:S(2)}, u32[]{:S(2)}) %collective-permute-start.20) | collective-permute-done | bytes 262176 | tf_op jit(solution)/shard_map/ppermute | solution.py:310
  64.7 2.1 %terms.3 = (f32[32,3584]{1,0:T(8,128)S(1)}, bf16[32,3584]{1,0:T(8,128)(2,1)S(1)}) custom-call(bf16[64,1024]{1,0:T(8,128)(2,1)S(1)} %values.1.val_ref, bf16[1024,7168]{1,0:T(8,128)(2,1)S(1)} %bitcast.2), custom_call_target="tpu_custom_call" | custom-call | flops 6899999744 | tf_op jit(solution)/shard_map/terms/pallas_call | solution.py:35
  66.8 2.1 %terms.2 = (f32[32,3584]{1,0:T(8,128)S(1)}, bf16[32,3584]{1,0:T(8,128)(2,1)S(1)}) custom-call(bf16[64,1024]{1,0:T(8,128)(2,1)S(1)} %values.1.val_ref, bf16[1024,7168]{1,0:T(8,128)(2,1)S(1)} %bitcast.2), custom_call_target="tpu_custom_call" | custom-call | flops 6899999744 | tf_op jit(solution)/shard_map/terms/pallas_call | solution.py:35
  71.0 2.0 %collective-permute-start.23 = (bf16[4,7168]{1,0:T(4,128)(2,1)S(1)}, bf16[4,7168]{1,0:T(4,128)(2,1)S(1)}, u32[]{:S(2)}, u32[]{:S(2)}) collective-permute-start(bf16[4,7168]{1,0:T(4,128)(2,1)S(1)} %get-tuple-element.62), channel_id=1, source_target_pairs={{0,8},{1,9},{2,10},{3,11},{4,12},{5,13},{6,14},{7,15},{8,0},{9,1},... | collective-permute-start | bytes 172040 | tf_op jit(solution)/shard_map/ppermute | solution.py:310
  73.8 3.1 %collective-permute-start.25 = (bf16[4,7168]{1,0:T(4,128)(2,1)S(1)}, bf16[4,7168]{1,0:T(4,128)(2,1)S(1)}, u32[]{:S(2)}, u32[]{:S(2)}) collective-permute-start(bf16[4,7168]{1,0:T(4,128)(2,1)S(1)} %get-tuple-element.64), channel_id=1, source_target_pairs={{0,12},{1,13},{2,14},{3,15},{4,8},{5,9},{6,10},{7,11},{8,4},{9,5},... | collective-permute-start | bytes 172040 | tf_op jit(solution)/shard_map/ppermute | solution.py:310
  76.8 1.9 %collective-permute-start.26 = (bf16[4,7168]{1,0:T(4,128)(2,1)S(1)}, bf16[4,7168]{1,0:T(4,128)(2,1)S(1)}, u32[]{:S(2)}, u32[]{:S(2)}) collective-permute-start(bf16[4,7168]{1,0:T(4,128)(2,1)S(1)} %get-tuple-element.65), channel_id=1, source_target_pairs={{0,14},{1,15},{2,12},{3,13},{4,10},{5,11},{6,8},{7,9},{8,6},{9,7},... | collective-permute-start | bytes 172040 | tf_op jit(solution)/shard_map/ppermute | solution.py:310
  78.7 1.8 %collective-permute-start.28 = (bf16[4,7168]{1,0:T(4,128)(2,1)S(1)}, bf16[4,7168]{1,0:T(4,128)(2,1)S(1)}, u32[]{:S(2)}, u32[]{:S(2)}) collective-permute-start(bf16[4,7168]{1,0:T(4,128)(2,1)S(1)} %get-tuple-element.67), channel_id=1, source_target_pairs={{0,6},{1,7},{2,4},{3,5},{4,2},{5,3},{6,0},{7,1},{8,14},{9,15},{10,... | collective-permute-start | bytes 172040 | tf_op jit(solution)/shard_map/ppermute | solution.py:310
  80.5 2.1 %collective-permute-done.24 = bf16[4,7168]{1,0:T(4,128)(2,1)S(1)} collective-permute-done((bf16[4,7168]{1,0:T(4,128)(2,1)S(1)}, bf16[4,7168]{1,0:T(4,128)(2,1)S(1)}, u32[]{:S(2)}, u32[]{:S(2)}) %collective-permute-start.24) | collective-permute-done | bytes 57376 | tf_op jit(solution)/shard_map/ppermute | solution.py:310
  83.9 1.3 %collective-permute-done.28 = bf16[4,7168]{1,0:T(4,128)(2,1)S(1)} collective-permute-done((bf16[4,7168]{1,0:T(4,128)(2,1)S(1)}, bf16[4,7168]{1,0:T(4,128)(2,1)S(1)}, u32[]{:S(2)}, u32[]{:S(2)}) %collective-permute-start.28) | collective-permute-done | bytes 57376 | tf_op jit(solution)/shard_map/ppermute | solution.py:310
  85.2 1.5 %collective-permute-done.29 = bf16[4,7168]{1,0:T(4,128)(2,1)S(1)} collective-permute-done((bf16[4,7168]{1,0:T(4,128)(2,1)S(1)}, bf16[4,7168]{1,0:T(4,128)(2,1)S(1)}, u32[]{:S(2)}, u32[]{:S(2)}) %collective-permute-start.29) | collective-permute-done | bytes 57376 | tf_op jit(solution)/shard_map/ppermute | solution.py:310
  (71 shorter events, 10.5 us)
Async XLA Ops:
  0.0 4.8 %collective-permute-start = (bf16[4,1536]{1,0:T(4,128)(2,1)}, bf16[4,1536]{1,0:T(4,128)(2,1)S(1)}, u32[]{:S(2)}, u32[]{:S(2)}) collective-permute-start(bf16[4,1536]{1,0:T(4,128)(2,1)} %refs_0_.1), channel_id=1, source_target_pairs={{0,2},{1,3},{2,0},{3,1},{4,6},{5,7},{6,4},{7,5},{8,10},{9,11},{10,... | collective-permute-start | bytes 36872 | tf_op jit(solution)/shard_map/ppermute | solution.py:310
  5.6 6.0 %collective-permute-start.3 = (bf16[8,1536]{1,0:T(8,128)(2,1)S(1)}, bf16[8,1536]{1,0:T(8,128)(2,1)S(1)}, u32[]{:S(2)}, u32[]{:S(2)}) collective-permute-start(bf16[8,1536]{1,0:T(8,128)(2,1)S(1)} %join.2.refs_0_), channel_id=1, source_target_pairs={{0,12},{1,13},{2,14},{3,15},{4,8},{5,9},{6,10},{7,11},{8,4},{9,5},... | collective-permute-start | bytes 73736 | tf_op jit(solution)/shard_map/ppermute | solution.py:310
  9.8 4.7 %collective-permute-start.2 = (bf16[8,1536]{1,0:T(8,128)(2,1)S(1)}, bf16[8,1536]{1,0:T(8,128)(2,1)S(1)}, u32[]{:S(2)}, u32[]{:S(2)}) collective-permute-start(bf16[8,1536]{1,0:T(8,128)(2,1)S(1)} %join.2.refs_0_), channel_id=1, source_target_pairs={{0,8},{1,9},{2,10},{3,11},{4,12},{5,13},{6,14},{7,15},{8,0},{9,1},... | collective-permute-start | bytes 73736 | tf_op jit(solution)/shard_map/ppermute | solution.py:310
  9.8 4.7 %collective-permute-start.1 = (bf16[8,1536]{1,0:T(8,128)(2,1)S(1)}, bf16[8,1536]{1,0:T(8,128)(2,1)S(1)}, u32[]{:S(2)}, u32[]{:S(2)}) collective-permute-start(bf16[8,1536]{1,0:T(8,128)(2,1)S(1)} %join.2.refs_0_), channel_id=1, source_target_pairs={{0,4},{1,5},{2,6},{3,7},{4,0},{5,1},{6,2},{7,3},{8,12},{9,13},{10,... | collective-permute-start | bytes 73736 | tf_op jit(solution)/shard_map/ppermute | solution.py:310
  14.5 1.4 %collective-permute-start.4 = (bf16[32,1536]{1,0:T(8,128)(2,1)S(1)}, bf16[32,1536]{1,0:T(8,128)(2,1)S(1)}, u32[]{:S(2)}, u32[]{:S(2)}) collective-permute-start(bf16[32,1536]{1,0:T(8,128)(2,1)S(1)} %join.3.q_ref), channel_id=1, source_target_pairs={{0,1},{1,0},{2,3},{3,2},{4,5},{5,4},{6,7},{7,6},{8,9},{9,8},{10,11... | collective-permute-start | bytes 294920 | tf_op jit(solution)/shard_map/ppermute | solution.py:310
  17.3 1.6 %collective-permute-start.5 = (bf16[8,144,128]{2,1,0:T(8,128)(2,1)S(1)}, bf16[8,144,128]{2,1,0:T(8,128)(2,1)S(1)}, u32[]{:S(2)}, u32[]{:S(2)}) collective-permute-start(bf16[8,144,128]{2,1,0:T(8,128)(2,1)S(1)} %get-tuple-element.40), channel_id=1, source_target_pairs={{0,1},{1,0},{2,3},{3,2},{4,5},{5,4},{6,7},{7,6},{8,9},{9,8},{10,11... | collective-permute-start | bytes 884744 | tf_op jit(solution)/shard_map/ppermute | solution.py:310
  19.0 8.4 %collective-permute-start.6 = (bf16[2,144,128]{2,1,0:T(8,128)(2,1)S(1)}, bf16[2,144,128]{2,1,0:T(8,128)(2,1)S(1)}, u32[]{:S(2)}, u32[]{:S(2)}) collective-permute-start(bf16[2,144,128]{2,1,0:T(8,128)(2,1)S(1)} %get-tuple-element.41), channel_id=1, source_target_pairs={{0,8},{1,9},{2,10},{3,11},{4,12},{5,13},{6,14},{7,15},{8,0},{9,1},... | collective-permute-start | bytes 221192 | tf_op jit(solution)/shard_map/ppermute | solution.py:310
  21.1 11.1 %collective-permute-start.7 = (bf16[2,144,128]{2,1,0:T(8,128)(2,1)S(1)}, bf16[2,144,128]{2,1,0:T(8,128)(2,1)S(1)}, u32[]{:S(2)}, u32[]{:S(2)}) collective-permute-start(bf16[2,144,128]{2,1,0:T(8,128)(2,1)S(1)} %get-tuple-element.42), channel_id=1, source_target_pairs={{0,10},{1,11},{2,8},{3,9},{4,14},{5,15},{6,12},{7,13},{8,2},{9,3},... | collective-permute-start | bytes 221192 | tf_op jit(solution)/shard_map/ppermute | solution.py:310
  23.5 13.7 %collective-permute-start.10 = (bf16[2,144,128]{2,1,0:T(8,128)(2,1)S(1)}, bf16[2,144,128]{2,1,0:T(8,128)(2,1)S(1)}, u32[]{:S(2)}, u32[]{:S(2)}) collective-permute-start(bf16[2,144,128]{2,1,0:T(8,128)(2,1)S(1)} %get-tuple-element.45), channel_id=1, source_target_pairs={{0,12},{1,13},{2,14},{3,15},{4,8},{5,9},{6,10},{7,11},{8,4},{9,5},... | collective-permute-start | bytes 221192 | tf_op jit(solution)/shard_map/ppermute | solution.py:310
  25.1 13.5 %collective-permute-start.11 = (bf16[2,144,128]{2,1,0:T(8,128)(2,1)S(1)}, bf16[2,144,128]{2,1,0:T(8,128)(2,1)S(1)}, u32[]{:S(2)}, u32[]{:S(2)}) collective-permute-start(bf16[2,144,128]{2,1,0:T(8,128)(2,1)S(1)} %get-tuple-element.46), channel_id=1, source_target_pairs={{0,14},{1,15},{2,12},{3,13},{4,10},{5,11},{6,8},{7,9},{8,6},{9,7},... | collective-permute-start | bytes 221192 | tf_op jit(solution)/shard_map/ppermute | solution.py:310
  27.4 18.9 %collective-permute-start.14 = (bf16[2,144,128]{2,1,0:T(8,128)(2,1)S(1)}, bf16[2,144,128]{2,1,0:T(8,128)(2,1)S(1)}, u32[]{:S(2)}, u32[]{:S(2)}) collective-permute-start(bf16[2,144,128]{2,1,0:T(8,128)(2,1)S(1)} %get-tuple-element.49), channel_id=1, source_target_pairs={{0,4},{1,5},{2,6},{3,7},{4,0},{5,1},{6,2},{7,3},{8,12},{9,13},{10,... | collective-permute-start | bytes 221192 | tf_op jit(solution)/shard_map/ppermute | solution.py:310
  27.4 22.2 %collective-permute-start.15 = (bf16[2,144,128]{2,1,0:T(8,128)(2,1)S(1)}, bf16[2,144,128]{2,1,0:T(8,128)(2,1)S(1)}, u32[]{:S(2)}, u32[]{:S(2)}) collective-permute-start(bf16[2,144,128]{2,1,0:T(8,128)(2,1)S(1)} %get-tuple-element.50), channel_id=1, source_target_pairs={{0,6},{1,7},{2,4},{3,5},{4,2},{5,3},{6,0},{7,1},{8,14},{9,15},{10,... | collective-permute-start | bytes 221192 | tf_op jit(solution)/shard_map/ppermute | solution.py:310
  32.2 17.6 %collective-permute-start.16 = (bf16[2,144,128]{2,1,0:T(8,128)(2,1)S(1)}, bf16[2,144,128]{2,1,0:T(8,128)(2,1)S(1)}, u32[]{:S(2)}, u32[]{:S(2)}) collective-permute-start(bf16[2,144,128]{2,1,0:T(8,128)(2,1)S(1)} %get-tuple-element.51), channel_id=1, source_target_pairs={{0,2},{1,3},{2,0},{3,1},{4,6},{5,7},{6,4},{7,5},{8,10},{9,11},{10,... | collective-permute-start | bytes 221192 | tf_op jit(solution)/shard_map/ppermute | solution.py:310
  37.2 17.8 %collective-permute-start.8 = (bf16[2,32,512]{2,1,0:T(8,128)(2,1)S(1)}, bf16[2,32,512]{2,1,0:T(8,128)(2,1)S(1)}, u32[]{:S(2)}, u32[]{:S(2)}) collective-permute-start(bf16[2,32,512]{2,1,0:T(8,128)(2,1)S(1)} %get-tuple-element.43), channel_id=1, source_target_pairs={{0,8},{1,9},{2,10},{3,11},{4,12},{5,13},{6,14},{7,15},{8,0},{9,1},... | collective-permute-start | bytes 196616 | tf_op jit(solution)/shard_map/ppermute | solution.py:310
  38.6 19.7 %collective-permute-start.9 = (bf16[2,32,512]{2,1,0:T(8,128)(2,1)S(1)}, bf16[2,32,512]{2,1,0:T(8,128)(2,1)S(1)}, u32[]{:S(2)}, u32[]{:S(2)}) collective-permute-start(bf16[2,32,512]{2,1,0:T(8,128)(2,1)S(1)} %get-tuple-element.44), channel_id=1, source_target_pairs={{0,10},{1,11},{2,8},{3,9},{4,14},{5,15},{6,12},{7,13},{8,2},{9,3},... | collective-permute-start | bytes 196616 | tf_op jit(solution)/shard_map/ppermute | solution.py:310
  46.3 12.2 %collective-permute-start.12 = (bf16[2,32,512]{2,1,0:T(8,128)(2,1)S(1)}, bf16[2,32,512]{2,1,0:T(8,128)(2,1)S(1)}, u32[]{:S(2)}, u32[]{:S(2)}) collective-permute-start(bf16[2,32,512]{2,1,0:T(8,128)(2,1)S(1)} %get-tuple-element.47), channel_id=1, source_target_pairs={{0,12},{1,13},{2,14},{3,15},{4,8},{5,9},{6,10},{7,11},{8,4},{9,5},... | collective-permute-start | bytes 196616 | tf_op jit(solution)/shard_map/ppermute | solution.py:310
  49.6 8.9 %collective-permute-start.13 = (bf16[2,32,512]{2,1,0:T(8,128)(2,1)S(1)}, bf16[2,32,512]{2,1,0:T(8,128)(2,1)S(1)}, u32[]{:S(2)}, u32[]{:S(2)}) collective-permute-start(bf16[2,32,512]{2,1,0:T(8,128)(2,1)S(1)} %get-tuple-element.48), channel_id=1, source_target_pairs={{0,14},{1,15},{2,12},{3,13},{4,10},{5,11},{6,8},{7,9},{8,6},{9,7},... | collective-permute-start | bytes 196616 | tf_op jit(solution)/shard_map/ppermute | solution.py:310
  49.8 14.8 %slice-start.1 = ((s8[14680064]{0:T(1024)(128)(4,1)}), s8[4194304]{0:T(1024)(128)(4,1)S(1)}, s32[]{:S(2)}) async-start(s8[14680064]{0:T(1024)(128)(4,1)} %bitcast.1), calls=%async_computation.1 | async-start | bytes 8388608
  49.9 14.8 %slice-start.2 = ((s8[14680064]{0:T(1024)(128)(4,1)}), s8[4194304]{0:T(1024)(128)(4,1)S(1)}, s32[]{:S(2)}) async-start(s8[14680064]{0:T(1024)(128)(4,1)} %bitcast.1), calls=%async_computation.2 | async-start | bytes 8388608
  54.9 4.3 %collective-permute-start.17 = (bf16[2,32,512]{2,1,0:T(8,128)(2,1)S(1)}, bf16[2,32,512]{2,1,0:T(8,128)(2,1)S(1)}, u32[]{:S(2)}, u32[]{:S(2)}) collective-permute-start(bf16[2,32,512]{2,1,0:T(8,128)(2,1)S(1)} %get-tuple-element.53), channel_id=1, source_target_pairs={{0,4},{1,5},{2,6},{3,7},{4,0},{5,1},{6,2},{7,3},{8,12},{9,13},{10,... | collective-permute-start | bytes 196616 | tf_op jit(solution)/shard_map/ppermute | solution.py:310
  55.0 6.2 %collective-permute-start.18 = (bf16[2,32,512]{2,1,0:T(8,128)(2,1)S(1)}, bf16[2,32,512]{2,1,0:T(8,128)(2,1)S(1)}, u32[]{:S(2)}, u32[]{:S(2)}) collective-permute-start(bf16[2,32,512]{2,1,0:T(8,128)(2,1)S(1)} %get-tuple-element.54), channel_id=1, source_target_pairs={{0,6},{1,7},{2,4},{3,5},{4,2},{5,3},{6,0},{7,1},{8,14},{9,15},{10,... | collective-permute-start | bytes 196616 | tf_op jit(solution)/shard_map/ppermute | solution.py:310
  58.3 4.3 %collective-permute-start.19 = (bf16[2,32,512]{2,1,0:T(8,128)(2,1)S(1)}, bf16[2,32,512]{2,1,0:T(8,128)(2,1)S(1)}, u32[]{:S(2)}, u32[]{:S(2)}) collective-permute-start(bf16[2,32,512]{2,1,0:T(8,128)(2,1)S(1)} %get-tuple-element.55), channel_id=1, source_target_pairs={{0,2},{1,3},{2,0},{3,1},{4,6},{5,7},{6,4},{7,5},{8,10},{9,11},{10,... | collective-permute-start | bytes 196616 | tf_op jit(solution)/shard_map/ppermute | solution.py:310
  62.6 1.6 %collective-permute-start.20 = (bf16[8,32,512]{2,1,0:T(8,128)(2,1)S(1)}, bf16[8,32,512]{2,1,0:T(8,128)(2,1)S(1)}, u32[]{:S(2)}, u32[]{:S(2)}) collective-permute-start(bf16[8,32,512]{2,1,0:T(8,128)(2,1)S(1)} %regroup.1), channel_id=1, source_target_pairs={{0,1},{1,0},{2,3},{3,2},{4,5},{5,4},{6,7},{7,6},{8,9},{9,8},{10,11... | collective-permute-start | bytes 786440 | tf_op jit(solution)/shard_map/ppermute | solution.py:310
  69.0 1.6 %collective-permute-start.22 = (bf16[32,3584]{1,0:T(8,128)(2,1)S(1)}, bf16[32,3584]{1,0:T(8,128)(2,1)S(1)}, u32[]{:S(2)}, u32[]{:S(2)}) collective-permute-start(bf16[32,3584]{1,0:T(8,128)(2,1)S(1)} %get-tuple-element.60), channel_id=1, source_target_pairs={{0,1},{1,0},{2,3},{3,2},{4,5},{5,4},{6,7},{7,6},{8,9},{9,8},{10,11... | collective-permute-start | bytes 688136 | tf_op jit(solution)/shard_map/ppermute | solution.py:310
  69.2 1.7 %collective-permute-start.21 = (bf16[32,3584]{1,0:T(8,128)(2,1)S(1)}, bf16[32,3584]{1,0:T(8,128)(2,1)S(1)}, u32[]{:S(2)}, u32[]{:S(2)}) collective-permute-start(bf16[32,3584]{1,0:T(8,128)(2,1)S(1)} %get-tuple-element.59), channel_id=1, source_target_pairs={{0,1},{1,0},{2,3},{3,2},{4,5},{5,4},{6,7},{7,6},{8,9},{9,8},{10,11... | collective-permute-start | bytes 688136 | tf_op jit(solution)/shard_map/ppermute | solution.py:310
  71.0 7.7 %collective-permute-start.23 = (bf16[4,7168]{1,0:T(4,128)(2,1)S(1)}, bf16[4,7168]{1,0:T(4,128)(2,1)S(1)}, u32[]{:S(2)}, u32[]{:S(2)}) collective-permute-start(bf16[4,7168]{1,0:T(4,128)(2,1)S(1)} %get-tuple-element.62), channel_id=1, source_target_pairs={{0,8},{1,9},{2,10},{3,11},{4,12},{5,13},{6,14},{7,15},{8,0},{9,1},... | collective-permute-start | bytes 172040 | tf_op jit(solution)/shard_map/ppermute | solution.py:310
  72.9 9.6 %collective-permute-start.24 = (bf16[4,7168]{1,0:T(4,128)(2,1)S(1)}, bf16[4,7168]{1,0:T(4,128)(2,1)S(1)}, u32[]{:S(2)}, u32[]{:S(2)}) collective-permute-start(bf16[4,7168]{1,0:T(4,128)(2,1)S(1)} %get-tuple-element.63), channel_id=1, source_target_pairs={{0,10},{1,11},{2,8},{3,9},{4,14},{5,15},{6,12},{7,13},{8,2},{9,3},... | collective-permute-start | bytes 172040 | tf_op jit(solution)/shard_map/ppermute | solution.py:310
  73.8 8.8 %collective-permute-start.25 = (bf16[4,7168]{1,0:T(4,128)(2,1)S(1)}, bf16[4,7168]{1,0:T(4,128)(2,1)S(1)}, u32[]{:S(2)}, u32[]{:S(2)}) collective-permute-start(bf16[4,7168]{1,0:T(4,128)(2,1)S(1)} %get-tuple-element.64), channel_id=1, source_target_pairs={{0,12},{1,13},{2,14},{3,15},{4,8},{5,9},{6,10},{7,11},{8,4},{9,5},... | collective-permute-start | bytes 172040 | tf_op jit(solution)/shard_map/ppermute | solution.py:310
  76.8 7.0 %collective-permute-start.26 = (bf16[4,7168]{1,0:T(4,128)(2,1)S(1)}, bf16[4,7168]{1,0:T(4,128)(2,1)S(1)}, u32[]{:S(2)}, u32[]{:S(2)}) collective-permute-start(bf16[4,7168]{1,0:T(4,128)(2,1)S(1)} %get-tuple-element.65), channel_id=1, source_target_pairs={{0,14},{1,15},{2,12},{3,13},{4,10},{5,11},{6,8},{7,9},{8,6},{9,7},... | collective-permute-start | bytes 172040 | tf_op jit(solution)/shard_map/ppermute | solution.py:310
  78.7 5.2 %collective-permute-start.27 = (bf16[4,7168]{1,0:T(4,128)(2,1)S(1)}, bf16[4,7168]{1,0:T(4,128)(2,1)S(1)}, u32[]{:S(2)}, u32[]{:S(2)}) collective-permute-start(bf16[4,7168]{1,0:T(4,128)(2,1)S(1)} %get-tuple-element.66), channel_id=1, source_target_pairs={{0,4},{1,5},{2,6},{3,7},{4,0},{5,1},{6,2},{7,3},{8,12},{9,13},{10,... | collective-permute-start | bytes 172040 | tf_op jit(solution)/shard_map/ppermute | solution.py:310
  78.7 6.5 %collective-permute-start.28 = (bf16[4,7168]{1,0:T(4,128)(2,1)S(1)}, bf16[4,7168]{1,0:T(4,128)(2,1)S(1)}, u32[]{:S(2)}, u32[]{:S(2)}) collective-permute-start(bf16[4,7168]{1,0:T(4,128)(2,1)S(1)} %get-tuple-element.67), channel_id=1, source_target_pairs={{0,6},{1,7},{2,4},{3,5},{4,2},{5,3},{6,0},{7,1},{8,14},{9,15},{10,... | collective-permute-start | bytes 172040 | tf_op jit(solution)/shard_map/ppermute | solution.py:310
  82.6 4.2 %collective-permute-start.29 = (bf16[4,7168]{1,0:T(4,128)(2,1)S(1)}, bf16[4,7168]{1,0:T(4,128)(2,1)S(1)}, u32[]{:S(2)}, u32[]{:S(2)}) collective-permute-start(bf16[4,7168]{1,0:T(4,128)(2,1)S(1)} %get-tuple-element.68), channel_id=1, source_target_pairs={{0,2},{1,3},{2,0},{3,1},{4,6},{5,7},{6,4},{7,5},{8,10},{9,11},{10,... | collective-permute-start | bytes 172040 | tf_op jit(solution)/shard_map/ppermute | solution.py:310
  (11 other events, 109.6 us)

commit v5 on v4

--- a/solution.py
+++ b/solution.py
@@ -52,12 +52,12 @@
     return jax.ShapeDtypeStruct(dims, dtype)
 
 
-def chip_order(devices):
-    return sorted(range(0, devices, 2), key=lambda k: -k.bit_length())
+def far_first(devices, step):
+    return sorted(range(0, devices, step), key=lambda k: -k.bit_length())
 
 
 def gathered_order(devices):
-    return [z + y + c for c in range(2) for z in range(0, devices, 4) for y in (0, 2)]
+    return [z + y for z in range(0, devices, 4) for y in (0, 2)]
 
 
 def rotary_kernel(len_ref, cos_ref, sin_ref):
@@ -92,61 +92,53 @@
     return call(join_kernel, shape(len(blocks) * rows, depth), 5, "join")(*blocks)
 
 
-def project_kernel(devices, q_ref, far_ref, wq_ref, wk_ref, mine_ref, other_ref, lat_ref, rot_ref):
-    heads = wk_ref.shape[0]
-    count = 2 * q_ref.shape[0]
-    wide = count // devices * heads
+def project_kernel(devices, q_ref, *refs):
+    weights = (refs[0:2], refs[2:4])
+    lat_ref, rot_ref = refs[-2:]
+    out_refs = refs[4:-2]
+    heads = weights[0][1].shape[0]
+    count = q_ref.shape[0]
+    wide = 2 * count // devices * heads
     width = NOPE + ROPE
-    piece = jnp.concatenate([q_ref[...], far_ref[...]], axis=0)
-    projected = jnp.dot(piece, wq_ref[...], preferred_element_type=jnp.float32)
-    for h in range(heads):
-        mine = projected[:, h * width : (h + 1) * width]
-        absorbed = jnp.dot(
-            mine[:, :NOPE].astype(jnp.bfloat16), wk_ref[h], preferred_element_type=jnp.float32
-        )
-        for c in range(PIECES):
-            lat_ref[c, pl.ds(h, count, stride=heads), :] = absorbed[:, c * LANES : (c + 1) * LANES]
-        pe = mine[:, NOPE:]
-        rot_ref[pl.ds(h, count, stride=heads), :] = jnp.concatenate([pe, pe], axis=-1)
     lane = lax.broadcasted_iota(jnp.int32, (wide // 2, LANES), 1)
-    order = chip_order(devices)
-    for place, k in enumerate(gathered_order(devices)):
-        out_ref = other_ref if k % 2 else mine_ref
-        at = order.index(k - k % 2)
-        first = place * wide
-        for c in range(PIECES):
-            out_ref[at, c * wide : (c + 1) * wide, :] = lat_ref[c, first : first + wide, :].astype(
+    order = far_first(devices, 2)
+    for core, (wq_ref, wk_ref) in enumerate(weights):
+        projected = jnp.dot(q_ref[...], wq_ref[...], preferred_element_type=jnp.float32)
+        for h in range(heads):
+            mine = projected[:, h * width : (h + 1) * width]
+            absorbed = jnp.dot(
+                mine[:, :NOPE].astype(jnp.bfloat16), wk_ref[h], preferred_element_type=jnp.float32
+            )
+            at = pl.ds(h, count, stride=heads)
+            for c in range(PIECES):
+                lat_ref[core * PIECES + c, at, :] = absorbed[:, c * LANES : (c + 1) * LANES]
+            pe = mine[:, NOPE:]
+            rot_ref[core, at, :] = jnp.concatenate([pe, pe], axis=-1)
+        for place, k in enumerate(gathered_order(devices)):
+            out_ref = out_refs[order.index(k)]
+            first = place * wide
+            for c in range(PIECES):
+                out_ref[core, c * wide : (c + 1) * wide, :] = lat_ref[
+                    core * PIECES + c, first : first + wide, :
+                ].astype(jnp.bfloat16)
+            low = rot_ref[core, first : first + wide // 2, :]
+            high = rot_ref[core, first + wide // 2 : first + wide, :]
+            out_ref[core, PIECES * wide :, :] = jnp.where(lane < ROPE, low, high).astype(
                 jnp.bfloat16
             )
-        low = rot_ref[first : first + wide // 2, :]
-        high = rot_ref[first + wide // 2 : first + wide, :]
-        out_ref[at, PIECES * wide :, :] = jnp.where(lane < ROPE, low, high).astype(jnp.bfloat16)
-
-
-def project(near, far, w_uq, w_uk, devices):
-    heads = w_uk.shape[0]
-    count = 2 * near.shape[0]
-    wide = count // devices * heads
-    half = shape(devices // 2, PIECES * wide + wide // 2, LANES)
+
+
+def project(piece, weights, devices):
+    heads = weights[1].shape[0]
+    count = piece.shape[0]
+    wide = 2 * count // devices * heads
     scratch = [
-        pltpu.VMEM((PIECES, count * heads, LANES), jnp.float32),
-        pltpu.VMEM((count * heads, LANES), jnp.float32),
+        pltpu.VMEM((2 * PIECES, count * heads, LANES), jnp.float32),
+        pltpu.VMEM((2, count * heads, LANES), jnp.float32),
     ]
+    out = [shape(2, PIECES * wide + wide // 2, LANES)] * (devices // 2)
     kernel = functools.partial(project_kernel, devices)
-    return call(kernel, (half, half), 20, "project", scratch)(
-        near, far, resident(w_uq), resident(w_uk)
-    )
-
-
-def pack_kernel(mine_ref, other_ref, *out_refs):
-    for j, out_ref in enumerate(out_refs):
-        out_ref[0] = mine_ref[j]
-        out_ref[1] = other_ref[j]
-
-
-def pack(mine, other):
-    chips, count, width = mine.shape
-    return call(pack_kernel, [shape(2, count, width)] * chips, 1, "pack")(mine, other)
+    return call(kernel, out, 20, "project", scratch)(piece, *[resident(w) for w in weights])
 
 
 def attend_kernel(chips, len_ref, cos_ref, sin_ref, key_ref, new_ref, *refs):
@@ -276,55 +268,80 @@
     return call(kernel, out, 6, "terms")(values, resident(w_o))
 
 
-def pair_kernel(rows, *refs):
-    mine_refs = refs[:PARTS]
-    other_refs = refs[PARTS : 2 * PARTS]
-    out_refs = refs[2 * PARTS :]
-    for p, (mine_ref, other_ref) in enumerate(zip(mine_refs, other_refs)):
-        width = mine_ref.shape[1]
-        total = mine_ref[...] + other_ref[...].astype(jnp.float32)
-        for j, out_ref in enumerate(out_refs):
-            out_ref[:, p * width : (p + 1) * width] = total[j * rows : (j + 1) * rows].astype(
-                out_ref.dtype
-            )
-
-
-def pair_sum(mine, other, rows):
-    count, width = mine[0].shape
-    chips = count // rows
-    out = [shape(rows, PARTS * width)] * (chips - 1)
-    out += [shape(rows, PARTS * width, dtype=jnp.float32)]
-    return call(functools.partial(pair_kernel, rows), out, 1, "pair_sum")(*mine, *other)
+def core_sum_kernel(keep, give, mine_ref, other_ref, keep_ref, give_ref):
+    rows = keep_ref.shape[0] // len(keep)
+    total = mine_ref[...] + other_ref[...].astype(jnp.float32)
+    for out_ref, places in ((keep_ref, keep), (give_ref, give)):
+        blocks = [total[j * rows : (j + 1) * rows] for j in places]
+        out_ref[...] = jnp.concatenate(blocks, axis=0).astype(out_ref.dtype)
+
+
+def core_sum(mine, other, devices):
+    count, width = mine.shape
+    order = far_first(devices, 2)
+    zs = far_first(devices, 4)
+    keep = [order.index(z) for z in zs]
+    give = [order.index(z + 2) for z in zs]
+    out = (shape(count // 2, width, dtype=jnp.float32), shape(count // 2, width))
+    return call(functools.partial(core_sum_kernel, keep, give), out, 1, "core_sum")(mine, other)
+
+
+def chip_sum_kernel(mine_ref, other_ref, *out_refs):
+    rows = out_refs[0].shape[0]
+    total = mine_ref[...] + other_ref[...].astype(jnp.float32)
+    for j, out_ref in enumerate(out_refs):
+        out_ref[...] = total[j * rows : (j + 1) * rows].astype(out_ref.dtype)
+
+
+def chip_sum(mine, other, rows):
+    count, width = mine.shape
+    out = [shape(rows, width)] * (count // rows - 1) + [shape(rows, width, dtype=jnp.float32)]
+    return call(chip_sum_kernel, out, 1, "chip_sum")(mine, other)
+
+
+def last_sum_kernel(*refs):
+    *in_refs, out_ref = refs
+    each = len(in_refs) // PARTS
+    width = out_ref.shape[1] // PARTS
+    for p in range(PARTS):
+        terms = [ref[...].astype(jnp.float32) for ref in in_refs[p * each : (p + 1) * each]]
+        out_ref[:, p * width : (p + 1) * width] = sum(terms[1:], terms[0]).astype(out_ref.dtype)
+
+
+def last_sum(shares):
+    rows, width = shares[0][0].shape
+    blocks = [block for part in shares for block in part]
+    return call(last_sum_kernel, shape(rows, PARTS * width), 1, "last_sum")(*blocks)
 
 
 def on_device(q_latent, new_latent, cache, lengths, w_uq, w_uk, w_uv, w_o, devices):
     heads = w_uk.shape[0]
     rows = cache.shape[0]
-    order = chip_order(devices)
-    chips = len(order)
-    quarter = chips // 4
+    order = far_first(devices, 2)
+    zs = far_first(devices, 4)
 
     def swap(block, k):
         if k == 0:
             return block
         return lax.ppermute(block, "row", [(i, i ^ k) for i in range(devices)])
 
+    far_weights = [swap(w_uq, 1), swap(w_uk, 1)]
     near = join([q_latent, swap(q_latent, 2)])
     tables = rotary(lengths)
     near = join([swap(near, z) for z in range(0, devices, 4)])
-    mine, other = project(near, swap(near, 1), w_uq, w_uk, devices)
-    messages = pack(mine, swap(other, 1))
+    messages = project(near, [w_uq, w_uk, *far_weights], devices)
     messages = [swap(block, k) for k, block in zip(order, messages)]
     keys = jnp.swapaxes(cache, 1, 2)
-    latents = []
-    for first, last in ((0, quarter), (quarter, 2 * quarter), (2 * quarter, chips)):
-        done = attend(lengths, tables, keys, new_latent, messages[first:last], heads)
-        latents += [swap(block, k) for k, block in zip(order[first:last], done)]
+    latents = attend(lengths, tables, keys, new_latent, messages, heads)
+    latents = [swap(block, k) for k, block in zip(order, latents)]
     values = head_values(latents, swap(regroup(latents), 1), w_uv)
-    terms = [output_terms(values, w_o, part) for part in range(PARTS)]
-    shares = pair_sum([a for a, _ in terms], [swap(b, 1) for _, b in terms], rows)
-    shares = [swap(block, k).astype(jnp.float32) for k, block in zip(order, shares)]
-    return sum(shares[:-1], shares[-1]).astype(jnp.bfloat16)
+    shares = []
+    for part in range(PARTS):
+        mine, other = output_terms(values, w_o, part)
+        mine, other = core_sum(mine, swap(other, 1), devices)
+        blocks = chip_sum(mine, swap(other, 2), rows)
+        shares.append([swap(block, z) for z, block in zip(zs, blocks)])
+    return last_sum(shares)
 
 
 def solution(mesh):

time: 87.7 us -> 80.7 us (0.920)
  Pallas kernels: 21.5 us -> 13.7 us
  waiting for transfers between devices: 23.7 us -> 25 us
    pallas_call x13 -> x14, Pallas kernels: 21.5 us -> 13.7 us  [run(): pl.pallas_call(kernel, out_shape=out_shape, in_specs=smem + [in_vmem()] *...]
    ppermute x30 -> x31, waiting for transfers between devices: 23.7 us -> 25 us  [swap(): return lax.ppermute(block, 'row', [(i, i ^ k) for i in range(devices)])]
    ppermute x30 -> x31, starting transfers between devices: 40.5 us -> 40.7 us  [swap(): return lax.ppermute(block, 'row', [(i, i ^ k) for i in range(devices)])]
  transfers between devices with their start and end apart: 30 -> 31, of which waited for: 16 -> 15; matrix products, arithmetic and copies ran while one was open for 0% -> 0% of each run, Pallas kernels for 17% -> 4%
where the time goes in v5:
time: 80.7 us; the launch traced here: 80.5 us
  starting transfers between devices  40.7 us (50%)
  waiting for transfers between devices  25 us (31%)
  Pallas kernels  13.7 us (17%)
    ppermute x31, starting transfers between devices, swap(): return lax.ppermute(block, 'row', [(i, i ^ k) for i in range(devices)])  40.7 us
    ppermute x31, waiting for transfers between devices, swap(): return lax.ppermute(block, 'row', [(i, i ^ k) for i in range(devices)])  25 us
    pallas_call x14, Pallas kernels, run(): pl.pallas_call(kernel, out_shape=out_shape, in_specs=smem + [in_vmem()] *...  13.7 us
  transfers between devices with their start and end apart: 31, of which 15 were waited for; matrix products, arithmetic and copies ran while one was open for 0% of the time, Pallas kernels for 4%

profile of v5, /device:TPU:0, one launch (start us, length us, event | category | flops | bytes accessed | tf_op | source)
XLA Modules:
  0.0 80.5 jit_solution(5536923555754863806)
XLA Ops:
  0.5 2.5 %collective-permute-start = (bf16[4,1536]{1,0:T(4,128)(2,1)}, bf16[4,1536]{1,0:T(4,128)(2,1)S(1)}, u32[]{:S(2)}, u32[]{:S(2)}) collective-permute-start(bf16[4,1536]{1,0:T(4,128)(2,1)} %refs_0_.2), channel_id=1, source_target_pairs={{0,2},{1,3},{2,0},{3,1},{4,6},{5,7},{6,4},{7,5},{8,10},{9,11},{10,... | collective-permute-start | bytes 36872 | tf_op jit(solution)/shard_map/ppermute | solution.py:326
  3.2 1.7 %collective-permute-done.refs_1_ = bf16[4,1536]{1,0:T(4,128)(2,1)S(1)} collective-permute-done((bf16[4,1536]{1,0:T(4,128)(2,1)}, bf16[4,1536]{1,0:T(4,128)(2,1)S(1)}, u32[]{:S(2)}, u32[]{:S(2)}) %collective-permute-start) | collective-permute-done | bytes 12320 | tf_op jit(solution)/shard_map/ppermute | solution.py:326
  5.6 2.1 %collective-permute-start.1 = (bf16[8,1536]{1,0:T(8,128)(2,1)S(1)}, bf16[8,1536]{1,0:T(8,128)(2,1)S(1)}, u32[]{:S(2)}, u32[]{:S(2)}) collective-permute-start(bf16[8,1536]{1,0:T(8,128)(2,1)S(1)} %join.2.refs_0_), channel_id=1, source_target_pairs={{0,4},{1,5},{2,6},{3,7},{4,0},{5,1},{6,2},{7,3},{8,12},{9,13},{10,... | collective-permute-start | bytes 73736 | tf_op jit(solution)/shard_map/ppermute | solution.py:326
  7.7 2.6 %collective-permute-start.2 = (bf16[8,1536]{1,0:T(8,128)(2,1)S(1)}, bf16[8,1536]{1,0:T(8,128)(2,1)S(1)}, u32[]{:S(2)}, u32[]{:S(2)}) collective-permute-start(bf16[8,1536]{1,0:T(8,128)(2,1)S(1)} %join.2.refs_0_), channel_id=1, source_target_pairs={{0,8},{1,9},{2,10},{3,11},{4,12},{5,13},{6,14},{7,15},{8,0},{9,1},... | collective-permute-start | bytes 73736 | tf_op jit(solution)/shard_map/ppermute | solution.py:326
  10.3 2.2 %collective-permute-done.2.refs_2_ = bf16[8,1536]{1,0:T(8,128)(2,1)S(1)} collective-permute-done((bf16[8,1536]{1,0:T(8,128)(2,1)S(1)}, bf16[8,1536]{1,0:T(8,128)(2,1)S(1)}, u32[]{:S(2)}, u32[]{:S(2)}) %collective-permute-start.2) | collective-permute-done | bytes 24608 | tf_op jit(solution)/shard_map/ppermute | solution.py:326
  12.5 3.4 %collective-permute-done.3.refs_3_ = bf16[8,1536]{1,0:T(8,128)(2,1)S(1)} collective-permute-done((bf16[8,1536]{1,0:T(8,128)(2,1)S(1)}, bf16[8,1536]{1,0:T(8,128)(2,1)S(1)}, u32[]{:S(2)}, u32[]{:S(2)}) %collective-permute-start.3) | collective-permute-done | bytes 24608 | tf_op jit(solution)/shard_map/ppermute | solution.py:326
  16.0 2.3 %project.1 = (bf16[2,144,128]{2,1,0:T(8,128)(2,1)S(1)}, bf16[2,144,128]{2,1,0:T(8,128)(2,1)S(1)}, bf16[2,144,128]{2,1,0:T(8,128)(2,1)S(1)}, bf16[2,144,128]{2,1,...) custom-call(bf16[32,1536]{1,0:T(8,128)(2,1)S(1)} %join.3.q_ref, ...), custom_call_target="tpu_custom_call" | custom-call | flops 23000000512 | tf_op jit(solution)/shard_map/project/pallas_call | solution.py:35
  18.5 3.0 %collective-permute-start.11 = (bf16[2,144,128]{2,1,0:T(8,128)(2,1)S(1)}, bf16[2,144,128]{2,1,0:T(8,128)(2,1)S(1)}, u32[]{:S(2)}, u32[]{:S(2)}) collective-permute-start(bf16[2,144,128]{2,1,0:T(8,128)(2,1)S(1)} %get-tuple-element.46), channel_id=1, source_target_pairs={{0,6},{1,7},{2,4},{3,5},{4,2},{5,3},{6,0},{7,1},{8,14},{9,15},{10,... | collective-permute-start | bytes 221192 | tf_op jit(solution)/shard_map/ppermute | solution.py:326
  21.9 3.9 %collective-permute-start.7 = (bf16[2,144,128]{2,1,0:T(8,128)(2,1)S(1)}, bf16[2,144,128]{2,1,0:T(8,128)(2,1)S(1)}, u32[]{:S(2)}, u32[]{:S(2)}) collective-permute-start(bf16[2,144,128]{2,1,0:T(8,128)(2,1)S(1)} %get-tuple-element.42), channel_id=1, source_target_pairs={{0,10},{1,11},{2,8},{3,9},{4,14},{5,15},{6,12},{7,13},{8,2},{9,3},... | collective-permute-start | bytes 221192 | tf_op jit(solution)/shard_map/ppermute | solution.py:326
  26.1 3.5 %collective-permute-start.9 = (bf16[2,144,128]{2,1,0:T(8,128)(2,1)S(1)}, bf16[2,144,128]{2,1,0:T(8,128)(2,1)S(1)}, u32[]{:S(2)}, u32[]{:S(2)}) collective-permute-start(bf16[2,144,128]{2,1,0:T(8,128)(2,1)S(1)} %get-tuple-element.44), channel_id=1, source_target_pairs={{0,14},{1,15},{2,12},{3,13},{4,10},{5,11},{6,8},{7,9},{8,6},{9,7},... | collective-permute-start | bytes 221192 | tf_op jit(solution)/shard_map/ppermute | solution.py:326
  30.8 3.3 %collective-permute-done.7.refs_1_ = bf16[2,144,128]{2,1,0:T(8,128)(2,1)S(1)} collective-permute-done((bf16[2,144,128]{2,1,0:T(8,128)(2,1)S(1)}, bf16[2,144,128]{2,1,0:T(8,128)(2,1)S(1)}, u32[]{:S(2)}, u32[]{:S(2)}) %collective-permute-start.7) | collective-permute-done | bytes 73760 | tf_op jit(solution)/shard_map/ppermute | solution.py:326
  34.1 5.2 %attend.1 = (bf16[2,32,512]{2,1,0:T(8,128)(2,1)S(1)}, bf16[2,32,512]{2,1,0:T(8,128)(2,1)S(1)}, bf16[2,32,512]{2,1,0:T(8,128)(2,1)S(1)}, bf16[2,32,512]{2,1,0:T(8...) custom-call(s32[4]{0:T(128)S(1)} %copy-done.4, ...), custom_call_target="tpu_custom_call" | custom-call | flops 11500000256 | tf_op jit(solution)/shard_map/attend/pallas_call | solution.py:35
  39.3 2.0 %collective-permute-start.13 = (bf16[2,32,512]{2,1,0:T(8,128)(2,1)S(1)}, bf16[2,32,512]{2,1,0:T(8,128)(2,1)S(1)}, u32[]{:S(2)}, u32[]{:S(2)}) collective-permute-start(bf16[2,32,512]{2,1,0:T(8,128)(2,1)S(1)} %get-tuple-element.49), channel_id=1, source_target_pairs={{0,8},{1,9},{2,10},{3,11},{4,12},{5,13},{6,14},{7,15},{8,0},{9,1},... | collective-permute-start | bytes 196616 | tf_op jit(solution)/shard_map/ppermute | solution.py:326
  41.4 0.9 %collective-permute-start.14 = (bf16[2,32,512]{2,1,0:T(8,128)(2,1)S(1)}, bf16[2,32,512]{2,1,0:T(8,128)(2,1)S(1)}, u32[]{:S(2)}, u32[]{:S(2)}) collective-permute-start(bf16[2,32,512]{2,1,0:T(8,128)(2,1)S(1)} %get-tuple-element.50), channel_id=1, source_target_pairs={{0,10},{1,11},{2,8},{3,9},{4,14},{5,15},{6,12},{7,13},{8,2},{9,3},... | collective-permute-start | bytes 196616 | tf_op jit(solution)/shard_map/ppermute | solution.py:326
  42.3 2.7 %collective-permute-start.15 = (bf16[2,32,512]{2,1,0:T(8,128)(2,1)S(1)}, bf16[2,32,512]{2,1,0:T(8,128)(2,1)S(1)}, u32[]{:S(2)}, u32[]{:S(2)}) collective-permute-start(bf16[2,32,512]{2,1,0:T(8,128)(2,1)S(1)} %get-tuple-element.51), channel_id=1, source_target_pairs={{0,12},{1,13},{2,14},{3,15},{4,8},{5,9},{6,10},{7,11},{8,4},{9,5},... | collective-permute-start | bytes 196616 | tf_op jit(solution)/shard_map/ppermute | solution.py:326
  45.0 2.0 %collective-permute-start.16 = (bf16[2,32,512]{2,1,0:T(8,128)(2,1)S(1)}, bf16[2,32,512]{2,1,0:T(8,128)(2,1)S(1)}, u32[]{:S(2)}, u32[]{:S(2)}) collective-permute-start(bf16[2,32,512]{2,1,0:T(8,128)(2,1)S(1)} %get-tuple-element.52), channel_id=1, source_target_pairs={{0,14},{1,15},{2,12},{3,13},{4,10},{5,11},{6,8},{7,9},{8,6},{9,7},... | collective-permute-start | bytes 196616 | tf_op jit(solution)/shard_map/ppermute | solution.py:326
  48.0 1.1 %collective-permute-start.18 = (bf16[2,32,512]{2,1,0:T(8,128)(2,1)S(1)}, bf16[2,32,512]{2,1,0:T(8,128)(2,1)S(1)}, u32[]{:S(2)}, u32[]{:S(2)}) collective-permute-start(bf16[2,32,512]{2,1,0:T(8,128)(2,1)S(1)} %get-tuple-element.54), channel_id=1, source_target_pairs={{0,6},{1,7},{2,4},{3,5},{4,2},{5,3},{6,0},{7,1},{8,14},{9,15},{10,... | collective-permute-start | bytes 196616 | tf_op jit(solution)/shard_map/ppermute | solution.py:326
  49.0 1.1 %collective-permute-done.14.refs_1_ = bf16[2,32,512]{2,1,0:T(8,128)(2,1)S(1)} collective-permute-done((bf16[2,32,512]{2,1,0:T(8,128)(2,1)S(1)}, bf16[2,32,512]{2,1,0:T(8,128)(2,1)S(1)}, u32[]{:S(2)}, u32[]{:S(2)}) %collective-permute-start.14) | collective-permute-done | bytes 65568 | tf_op jit(solution)/shard_map/ppermute | solution.py:326
  50.2 1.4 %collective-permute-start.19 = (bf16[2,32,512]{2,1,0:T(8,128)(2,1)S(1)}, bf16[2,32,512]{2,1,0:T(8,128)(2,1)S(1)}, u32[]{:S(2)}, u32[]{:S(2)}) collective-permute-start(bf16[2,32,512]{2,1,0:T(8,128)(2,1)S(1)} %get-tuple-element.55), channel_id=1, source_target_pairs={{0,2},{1,3},{2,0},{3,1},{4,6},{5,7},{6,4},{7,5},{8,10},{9,11},{10,... | collective-permute-start | bytes 196616 | tf_op jit(solution)/shard_map/ppermute | solution.py:326
  52.1 1.1 %collective-permute-done.18.refs_5_ = bf16[2,32,512]{2,1,0:T(8,128)(2,1)S(1)} collective-permute-done((bf16[2,32,512]{2,1,0:T(8,128)(2,1)S(1)}, bf16[2,32,512]{2,1,0:T(8,128)(2,1)S(1)}, u32[]{:S(2)}, u32[]{:S(2)}) %collective-permute-start.18) | collective-permute-done | bytes 65568 | tf_op jit(solution)/shard_map/ppermute | solution.py:326
  53.1 1.3 %collective-permute-done.19.refs_6_ = bf16[2,32,512]{2,1,0:T(8,128)(2,1)S(1)} collective-permute-done((bf16[2,32,512]{2,1,0:T(8,128)(2,1)S(1)}, bf16[2,32,512]{2,1,0:T(8,128)(2,1)S(1)}, u32[]{:S(2)}, u32[]{:S(2)}) %collective-permute-start.19) | collective-permute-done | bytes 65568 | tf_op jit(solution)/shard_map/ppermute | solution.py:326
  54.5 1.5 %collective-permute-done.20.refs_8_ = bf16[8,32,512]{2,1,0:T(8,128)(2,1)S(1)} collective-permute-done((bf16[8,32,512]{2,1,0:T(8,128)(2,1)S(1)}, bf16[8,32,512]{2,1,0:T(8,128)(2,1)S(1)}, u32[]{:S(2)}, u32[]{:S(2)}) %collective-permute-start.20) | collective-permute-done | bytes 262176 | tf_op jit(solution)/shard_map/ppermute | solution.py:326
  56.6 2.1 %terms.3 = (f32[32,3584]{1,0:T(8,128)S(1)}, bf16[32,3584]{1,0:T(8,128)(2,1)S(1)}) custom-call(bf16[64,1024]{1,0:T(8,128)(2,1)S(1)} %values.1.val_ref, bf16[1024,7168]{1,0:T(8,128)(2,1)S(1)} %bitcast.2), custom_call_target="tpu_custom_call" | custom-call | flops 6899999744 | tf_op jit(solution)/shard_map/terms/pallas_call | solution.py:35
  58.9 2.1 %terms.2 = (f32[32,3584]{1,0:T(8,128)S(1)}, bf16[32,3584]{1,0:T(8,128)(2,1)S(1)}) custom-call(bf16[64,1024]{1,0:T(8,128)(2,1)S(1)} %values.1.val_ref, bf16[1024,7168]{1,0:T(8,128)(2,1)S(1)} %bitcast.2), custom_call_target="tpu_custom_call" | custom-call | flops 6899999744 | tf_op jit(solution)/shard_map/terms/pallas_call | solution.py:35
  61.5 1.4 %collective-permute-start.27 = (bf16[16,3584]{1,0:T(8,128)(2,1)S(1)}, bf16[16,3584]{1,0:T(8,128)(2,1)S(1)}, u32[]{:S(2)}, u32[]{:S(2)}) collective-permute-start(bf16[16,3584]{1,0:T(8,128)(2,1)S(1)} %get-tuple-element.68), channel_id=1, source_target_pairs={{0,2},{1,3},{2,0},{3,1},{4,6},{5,7},{6,4},{7,5},{8,10},{9,11},{10,... | collective-permute-start | bytes 344072 | tf_op jit(solution)/shard_map/ppermute | solution.py:326
  63.0 1.1 %collective-permute-start.22 = (bf16[16,3584]{1,0:T(8,128)(2,1)S(1)}, bf16[16,3584]{1,0:T(8,128)(2,1)S(1)}, u32[]{:S(2)}, u32[]{:S(2)}) collective-permute-start(bf16[16,3584]{1,0:T(8,128)(2,1)S(1)} %get-tuple-element.60), channel_id=1, source_target_pairs={{0,2},{1,3},{2,0},{3,1},{4,6},{5,7},{6,4},{7,5},{8,10},{9,11},{10,... | collective-permute-start | bytes 344072 | tf_op jit(solution)/shard_map/ppermute | solution.py:326
  64.1 3.5 %collective-permute-done.27.other_ref = bf16[16,3584]{1,0:T(8,128)(2,1)S(1)} collective-permute-done((bf16[16,3584]{1,0:T(8,128)(2,1)S(1)}, bf16[16,3584]{1,0:T(8,128)(2,1)S(1)}, u32[]{:S(2)}, u32[]{:S(2)}) %collective-permute-start.27) | collective-permute-done | bytes 114720 | tf_op jit(solution)/shard_map/ppermute | solution.py:326
  67.6 1.8 %collective-permute-start.28 = (bf16[4,3584]{1,0:T(4,128)(2,1)S(1)}, bf16[4,3584]{1,0:T(4,128)(2,1)S(1)}, u32[]{:S(2)}, u32[]{:S(2)}) collective-permute-start(bf16[4,3584]{1,0:T(4,128)(2,1)S(1)} %get-tuple-element.69), channel_id=1, source_target_pairs={{0,8},{1,9},{2,10},{3,11},{4,12},{5,13},{6,14},{7,15},{8,0},{9,1},... | collective-permute-start | bytes 86024 | tf_op jit(solution)/shard_map/ppermute | solution.py:326
  69.5 1.7 %collective-permute-start.29 = (bf16[4,3584]{1,0:T(4,128)(2,1)S(1)}, bf16[4,3584]{1,0:T(4,128)(2,1)S(1)}, u32[]{:S(2)}, u32[]{:S(2)}) collective-permute-start(bf16[4,3584]{1,0:T(4,128)(2,1)S(1)} %get-tuple-element.70), channel_id=1, source_target_pairs={{0,12},{1,13},{2,14},{3,15},{4,8},{5,9},{6,10},{7,11},{8,4},{9,5},... | collective-permute-start | bytes 86024 | tf_op jit(solution)/shard_map/ppermute | solution.py:326
  71.6 2.3 %collective-permute-start.23 = (bf16[4,3584]{1,0:T(4,128)(2,1)S(1)}, bf16[4,3584]{1,0:T(4,128)(2,1)S(1)}, u32[]{:S(2)}, u32[]{:S(2)}) collective-permute-start(bf16[4,3584]{1,0:T(4,128)(2,1)S(1)} %get-tuple-element.61), channel_id=1, source_target_pairs={{0,8},{1,9},{2,10},{3,11},{4,12},{5,13},{6,14},{7,15},{8,0},{9,1},... | collective-permute-start | bytes 86024 | tf_op jit(solution)/shard_map/ppermute | solution.py:326
  74.0 1.7 %collective-permute-start.24 = (bf16[4,3584]{1,0:T(4,128)(2,1)S(1)}, bf16[4,3584]{1,0:T(4,128)(2,1)S(1)}, u32[]{:S(2)}, u32[]{:S(2)}) collective-permute-start(bf16[4,3584]{1,0:T(4,128)(2,1)S(1)} %get-tuple-element.62), channel_id=1, source_target_pairs={{0,12},{1,13},{2,14},{3,15},{4,8},{5,9},{6,10},{7,11},{8,4},{9,5},... | collective-permute-start | bytes 86024 | tf_op jit(solution)/shard_map/ppermute | solution.py:326
  76.5 3.2 %collective-permute-done.24.refs_1_ = bf16[4,3584]{1,0:T(4,128)(2,1)S(1)} collective-permute-done((bf16[4,3584]{1,0:T(4,128)(2,1)S(1)}, bf16[4,3584]{1,0:T(4,128)(2,1)S(1)}, u32[]{:S(2)}, u32[]{:S(2)}) %collective-permute-start.24) | collective-permute-done | bytes 28704 | tf_op jit(solution)/shard_map/ppermute | solution.py:326
  (73 shorter events, 8.5 us)
Async XLA Ops:
  0.0 16.0 %collective-permute-start.4 = (bf16[1536,1536]{1,0:T(8,128)(2,1)}, bf16[1536,1536]{1,0:T(8,128)(2,1)S(1)}, u32[]{:S(2)}, u32[]{:S(2)}) collective-permute-start(bf16[1536,1536]{1,0:T(8,128)(2,1)} %refs_0_.3), channel_id=1, source_target_pairs={{0,1},{1,0},{2,3},{3,2},{4,5},{5,4},{6,7},{7,6},{8,9},{9,8},{10,11... | collective-permute-start | bytes 14155784 | tf_op jit(solution)/shard_map/ppermute | solution.py:326
  0.5 4.4 %collective-permute-start = (bf16[4,1536]{1,0:T(4,128)(2,1)}, bf16[4,1536]{1,0:T(4,128)(2,1)S(1)}, u32[]{:S(2)}, u32[]{:S(2)}) collective-permute-start(bf16[4,1536]{1,0:T(4,128)(2,1)} %refs_0_.2), channel_id=1, source_target_pairs={{0,2},{1,3},{2,0},{3,1},{4,6},{5,7},{6,4},{7,5},{8,10},{9,11},{10,... | collective-permute-start | bytes 36872 | tf_op jit(solution)/shard_map/ppermute | solution.py:326
  3.0 13.0 %collective-permute-start.5 = (bf16[8,128,512]{2,1,0:T(8,128)(2,1)}, bf16[8,128,512]{2,1,0:T(8,128)(2,1)S(1)}, u32[]{:S(2)}, u32[]{:S(2)}) collective-permute-start(bf16[8,128,512]{2,1,0:T(8,128)(2,1)} %refs_1_.1), channel_id=1, source_target_pairs={{0,1},{1,0},{2,3},{3,2},{4,5},{5,4},{6,7},{7,6},{8,9},{9,8},{10,11... | collective-permute-start | bytes 3145736 | tf_op jit(solution)/shard_map/ppermute | solution.py:326
  5.6 4.7 %collective-permute-start.1 = (bf16[8,1536]{1,0:T(8,128)(2,1)S(1)}, bf16[8,1536]{1,0:T(8,128)(2,1)S(1)}, u32[]{:S(2)}, u32[]{:S(2)}) collective-permute-start(bf16[8,1536]{1,0:T(8,128)(2,1)S(1)} %join.2.refs_0_), channel_id=1, source_target_pairs={{0,4},{1,5},{2,6},{3,7},{4,0},{5,1},{6,2},{7,3},{8,12},{9,13},{10,... | collective-permute-start | bytes 73736 | tf_op jit(solution)/shard_map/ppermute | solution.py:326
  7.7 4.8 %collective-permute-start.2 = (bf16[8,1536]{1,0:T(8,128)(2,1)S(1)}, bf16[8,1536]{1,0:T(8,128)(2,1)S(1)}, u32[]{:S(2)}, u32[]{:S(2)}) collective-permute-start(bf16[8,1536]{1,0:T(8,128)(2,1)S(1)} %join.2.refs_0_), channel_id=1, source_target_pairs={{0,8},{1,9},{2,10},{3,11},{4,12},{5,13},{6,14},{7,15},{8,0},{9,1},... | collective-permute-start | bytes 73736 | tf_op jit(solution)/shard_map/ppermute | solution.py:326
  10.3 5.6 %collective-permute-start.3 = (bf16[8,1536]{1,0:T(8,128)(2,1)S(1)}, bf16[8,1536]{1,0:T(8,128)(2,1)S(1)}, u32[]{:S(2)}, u32[]{:S(2)}) collective-permute-start(bf16[8,1536]{1,0:T(8,128)(2,1)S(1)} %join.2.refs_0_), channel_id=1, source_target_pairs={{0,12},{1,13},{2,14},{3,15},{4,8},{5,9},{6,10},{7,11},{8,4},{9,5},... | collective-permute-start | bytes 73736 | tf_op jit(solution)/shard_map/ppermute | solution.py:326
  18.4 7.4 %collective-permute-start.10 = (bf16[2,144,128]{2,1,0:T(8,128)(2,1)S(1)}, bf16[2,144,128]{2,1,0:T(8,128)(2,1)S(1)}, u32[]{:S(2)}, u32[]{:S(2)}) collective-permute-start(bf16[2,144,128]{2,1,0:T(8,128)(2,1)S(1)} %get-tuple-element.45), channel_id=1, source_target_pairs={{0,4},{1,5},{2,6},{3,7},{4,0},{5,1},{6,2},{7,3},{8,12},{9,13},{10,... | collective-permute-start | bytes 221192 | tf_op jit(solution)/shard_map/ppermute | solution.py:326
  18.5 7.6 %collective-permute-start.11 = (bf16[2,144,128]{2,1,0:T(8,128)(2,1)S(1)}, bf16[2,144,128]{2,1,0:T(8,128)(2,1)S(1)}, u32[]{:S(2)}, u32[]{:S(2)}) collective-permute-start(bf16[2,144,128]{2,1,0:T(8,128)(2,1)S(1)} %get-tuple-element.46), channel_id=1, source_target_pairs={{0,6},{1,7},{2,4},{3,5},{4,2},{5,3},{6,0},{7,1},{8,14},{9,15},{10,... | collective-permute-start | bytes 221192 | tf_op jit(solution)/shard_map/ppermute | solution.py:326
  21.4 8.8 %collective-permute-start.12 = (bf16[2,144,128]{2,1,0:T(8,128)(2,1)S(1)}, bf16[2,144,128]{2,1,0:T(8,128)(2,1)S(1)}, u32[]{:S(2)}, u32[]{:S(2)}) collective-permute-start(bf16[2,144,128]{2,1,0:T(8,128)(2,1)S(1)} %get-tuple-element.47), channel_id=1, source_target_pairs={{0,2},{1,3},{2,0},{3,1},{4,6},{5,7},{6,4},{7,5},{8,10},{9,11},{10,... | collective-permute-start | bytes 221192 | tf_op jit(solution)/shard_map/ppermute | solution.py:326
  21.9 8.8 %collective-permute-start.6 = (bf16[2,144,128]{2,1,0:T(8,128)(2,1)S(1)}, bf16[2,144,128]{2,1,0:T(8,128)(2,1)S(1)}, u32[]{:S(2)}, u32[]{:S(2)}) collective-permute-start(bf16[2,144,128]{2,1,0:T(8,128)(2,1)S(1)} %get-tuple-element.41), channel_id=1, source_target_pairs={{0,8},{1,9},{2,10},{3,11},{4,12},{5,13},{6,14},{7,15},{8,0},{9,1},... | collective-permute-start | bytes 221192 | tf_op jit(solution)/shard_map/ppermute | solution.py:326
  21.9 12.1 %collective-permute-start.7 = (bf16[2,144,128]{2,1,0:T(8,128)(2,1)S(1)}, bf16[2,144,128]{2,1,0:T(8,128)(2,1)S(1)}, u32[]{:S(2)}, u32[]{:S(2)}) collective-permute-start(bf16[2,144,128]{2,1,0:T(8,128)(2,1)S(1)} %get-tuple-element.42), channel_id=1, source_target_pairs={{0,10},{1,11},{2,8},{3,9},{4,14},{5,15},{6,12},{7,13},{8,2},{9,3},... | collective-permute-start | bytes 221192 | tf_op jit(solution)/shard_map/ppermute | solution.py:326
  25.8 8.2 %collective-permute-start.8 = (bf16[2,144,128]{2,1,0:T(8,128)(2,1)S(1)}, bf16[2,144,128]{2,1,0:T(8,128)(2,1)S(1)}, u32[]{:S(2)}, u32[]{:S(2)}) collective-permute-start(bf16[2,144,128]{2,1,0:T(8,128)(2,1)S(1)} %get-tuple-element.43), channel_id=1, source_target_pairs={{0,12},{1,13},{2,14},{3,15},{4,8},{5,9},{6,10},{7,11},{8,4},{9,5},... | collective-permute-start | bytes 221192 | tf_op jit(solution)/shard_map/ppermute | solution.py:326
  26.1 8.0 %collective-permute-start.9 = (bf16[2,144,128]{2,1,0:T(8,128)(2,1)S(1)}, bf16[2,144,128]{2,1,0:T(8,128)(2,1)S(1)}, u32[]{:S(2)}, u32[]{:S(2)}) collective-permute-start(bf16[2,144,128]{2,1,0:T(8,128)(2,1)S(1)} %get-tuple-element.44), channel_id=1, source_target_pairs={{0,14},{1,15},{2,12},{3,13},{4,10},{5,11},{6,8},{7,9},{8,6},{9,7},... | collective-permute-start | bytes 221192 | tf_op jit(solution)/shard_map/ppermute | solution.py:326
  34.1 22.4 %slice-start = ((s8[14680064]{0:T(1024)(128)(4,1)}), s8[4194304]{0:T(1024)(128)(4,1)S(1)}, s32[]{:S(2)}) async-start(s8[14680064]{0:T(1024)(128)(4,1)} %bitcast.1), calls=%async_computation | async-start | bytes 8388608
  39.3 8.7 %collective-permute-start.13 = (bf16[2,32,512]{2,1,0:T(8,128)(2,1)S(1)}, bf16[2,32,512]{2,1,0:T(8,128)(2,1)S(1)}, u32[]{:S(2)}, u32[]{:S(2)}) collective-permute-start(bf16[2,32,512]{2,1,0:T(8,128)(2,1)S(1)} %get-tuple-element.49), channel_id=1, source_target_pairs={{0,8},{1,9},{2,10},{3,11},{4,12},{5,13},{6,14},{7,15},{8,0},{9,1},... | collective-permute-start | bytes 196616 | tf_op jit(solution)/shard_map/ppermute | solution.py:326
  41.4 8.8 %collective-permute-start.14 = (bf16[2,32,512]{2,1,0:T(8,128)(2,1)S(1)}, bf16[2,32,512]{2,1,0:T(8,128)(2,1)S(1)}, u32[]{:S(2)}, u32[]{:S(2)}) collective-permute-start(bf16[2,32,512]{2,1,0:T(8,128)(2,1)S(1)} %get-tuple-element.50), channel_id=1, source_target_pairs={{0,10},{1,11},{2,8},{3,9},{4,14},{5,15},{6,12},{7,13},{8,2},{9,3},... | collective-permute-start | bytes 196616 | tf_op jit(solution)/shard_map/ppermute | solution.py:326
  42.3 9.2 %collective-permute-start.15 = (bf16[2,32,512]{2,1,0:T(8,128)(2,1)S(1)}, bf16[2,32,512]{2,1,0:T(8,128)(2,1)S(1)}, u32[]{:S(2)}, u32[]{:S(2)}) collective-permute-start(bf16[2,32,512]{2,1,0:T(8,128)(2,1)S(1)} %get-tuple-element.51), channel_id=1, source_target_pairs={{0,12},{1,13},{2,14},{3,15},{4,8},{5,9},{6,10},{7,11},{8,4},{9,5},... | collective-permute-start | bytes 196616 | tf_op jit(solution)/shard_map/ppermute | solution.py:326
  45.0 7.1 %collective-permute-start.16 = (bf16[2,32,512]{2,1,0:T(8,128)(2,1)S(1)}, bf16[2,32,512]{2,1,0:T(8,128)(2,1)S(1)}, u32[]{:S(2)}, u32[]{:S(2)}) collective-permute-start(bf16[2,32,512]{2,1,0:T(8,128)(2,1)S(1)} %get-tuple-element.52), channel_id=1, source_target_pairs={{0,14},{1,15},{2,12},{3,13},{4,10},{5,11},{6,8},{7,9},{8,6},{9,7},... | collective-permute-start | bytes 196616 | tf_op jit(solution)/shard_map/ppermute | solution.py:326
  47.0 5.0 %collective-permute-start.17 = (bf16[2,32,512]{2,1,0:T(8,128)(2,1)S(1)}, bf16[2,32,512]{2,1,0:T(8,128)(2,1)S(1)}, u32[]{:S(2)}, u32[]{:S(2)}) collective-permute-start(bf16[2,32,512]{2,1,0:T(8,128)(2,1)S(1)} %get-tuple-element.53), channel_id=1, source_target_pairs={{0,4},{1,5},{2,6},{3,7},{4,0},{5,1},{6,2},{7,3},{8,12},{9,13},{10,... | collective-permute-start | bytes 196616 | tf_op jit(solution)/shard_map/ppermute | solution.py:326
  48.0 5.2 %collective-permute-start.18 = (bf16[2,32,512]{2,1,0:T(8,128)(2,1)S(1)}, bf16[2,32,512]{2,1,0:T(8,128)(2,1)S(1)}, u32[]{:S(2)}, u32[]{:S(2)}) collective-permute-start(bf16[2,32,512]{2,1,0:T(8,128)(2,1)S(1)} %get-tuple-element.54), channel_id=1, source_target_pairs={{0,6},{1,7},{2,4},{3,5},{4,2},{5,3},{6,0},{7,1},{8,14},{9,15},{10,... | collective-permute-start | bytes 196616 | tf_op jit(solution)/shard_map/ppermute | solution.py:326
  50.2 4.3 %collective-permute-start.19 = (bf16[2,32,512]{2,1,0:T(8,128)(2,1)S(1)}, bf16[2,32,512]{2,1,0:T(8,128)(2,1)S(1)}, u32[]{:S(2)}, u32[]{:S(2)}) collective-permute-start(bf16[2,32,512]{2,1,0:T(8,128)(2,1)S(1)} %get-tuple-element.55), channel_id=1, source_target_pairs={{0,2},{1,3},{2,0},{3,1},{4,6},{5,7},{6,4},{7,5},{8,10},{9,11},{10,... | collective-permute-start | bytes 196616 | tf_op jit(solution)/shard_map/ppermute | solution.py:326
  54.5 1.6 %collective-permute-start.20 = (bf16[8,32,512]{2,1,0:T(8,128)(2,1)S(1)}, bf16[8,32,512]{2,1,0:T(8,128)(2,1)S(1)}, u32[]{:S(2)}, u32[]{:S(2)}) collective-permute-start(bf16[8,32,512]{2,1,0:T(8,128)(2,1)S(1)} %regroup.1), channel_id=1, source_target_pairs={{0,1},{1,0},{2,3},{3,2},{4,5},{5,4},{6,7},{7,6},{8,9},{9,8},{10,11... | collective-permute-start | bytes 786440 | tf_op jit(solution)/shard_map/ppermute | solution.py:326
  58.7 2.8 %collective-permute-start.26 = (bf16[32,3584]{1,0:T(8,128)(2,1)S(1)}, bf16[32,3584]{1,0:T(8,128)(2,1)S(1)}, u32[]{:S(2)}, u32[]{:S(2)}) collective-permute-start(bf16[32,3584]{1,0:T(8,128)(2,1)S(1)} %get-tuple-element.66), channel_id=1, source_target_pairs={{0,1},{1,0},{2,3},{3,2},{4,5},{5,4},{6,7},{7,6},{8,9},{9,8},{10,11... | collective-permute-start | bytes 688136 | tf_op jit(solution)/shard_map/ppermute | solution.py:326
  61.0 1.9 %collective-permute-start.21 = (bf16[32,3584]{1,0:T(8,128)(2,1)S(1)}, bf16[32,3584]{1,0:T(8,128)(2,1)S(1)}, u32[]{:S(2)}, u32[]{:S(2)}) collective-permute-start(bf16[32,3584]{1,0:T(8,128)(2,1)S(1)} %get-tuple-element.58), channel_id=1, source_target_pairs={{0,1},{1,0},{2,3},{3,2},{4,5},{5,4},{6,7},{7,6},{8,9},{9,8},{10,11... | collective-permute-start | bytes 688136 | tf_op jit(solution)/shard_map/ppermute | solution.py:326
  61.5 6.1 %collective-permute-start.27 = (bf16[16,3584]{1,0:T(8,128)(2,1)S(1)}, bf16[16,3584]{1,0:T(8,128)(2,1)S(1)}, u32[]{:S(2)}, u32[]{:S(2)}) collective-permute-start(bf16[16,3584]{1,0:T(8,128)(2,1)S(1)} %get-tuple-element.68), channel_id=1, source_target_pairs={{0,2},{1,3},{2,0},{3,1},{4,6},{5,7},{6,4},{7,5},{8,10},{9,11},{10,... | collective-permute-start | bytes 344072 | tf_op jit(solution)/shard_map/ppermute | solution.py:326
  63.0 8.6 %collective-permute-start.22 = (bf16[16,3584]{1,0:T(8,128)(2,1)S(1)}, bf16[16,3584]{1,0:T(8,128)(2,1)S(1)}, u32[]{:S(2)}, u32[]{:S(2)}) collective-permute-start(bf16[16,3584]{1,0:T(8,128)(2,1)S(1)} %get-tuple-element.60), channel_id=1, source_target_pairs={{0,2},{1,3},{2,0},{3,1},{4,6},{5,7},{6,4},{7,5},{8,10},{9,11},{10,... | collective-permute-start | bytes 344072 | tf_op jit(solution)/shard_map/ppermute | solution.py:326
  67.6 8.0 %collective-permute-start.28 = (bf16[4,3584]{1,0:T(4,128)(2,1)S(1)}, bf16[4,3584]{1,0:T(4,128)(2,1)S(1)}, u32[]{:S(2)}, u32[]{:S(2)}) collective-permute-start(bf16[4,3584]{1,0:T(4,128)(2,1)S(1)} %get-tuple-element.69), channel_id=1, source_target_pairs={{0,8},{1,9},{2,10},{3,11},{4,12},{5,13},{6,14},{7,15},{8,0},{9,1},... | collective-permute-start | bytes 86024 | tf_op jit(solution)/shard_map/ppermute | solution.py:326
  69.5 6.2 %collective-permute-start.29 = (bf16[4,3584]{1,0:T(4,128)(2,1)S(1)}, bf16[4,3584]{1,0:T(4,128)(2,1)S(1)}, u32[]{:S(2)}, u32[]{:S(2)}) collective-permute-start(bf16[4,3584]{1,0:T(4,128)(2,1)S(1)} %get-tuple-element.70), channel_id=1, source_target_pairs={{0,12},{1,13},{2,14},{3,15},{4,8},{5,9},{6,10},{7,11},{8,4},{9,5},... | collective-permute-start | bytes 86024 | tf_op jit(solution)/shard_map/ppermute | solution.py:326
  71.1 4.5 %collective-permute-start.30 = (bf16[4,3584]{1,0:T(4,128)(2,1)S(1)}, bf16[4,3584]{1,0:T(4,128)(2,1)S(1)}, u32[]{:S(2)}, u32[]{:S(2)}) collective-permute-start(bf16[4,3584]{1,0:T(4,128)(2,1)S(1)} %get-tuple-element.71), channel_id=1, source_target_pairs={{0,4},{1,5},{2,6},{3,7},{4,0},{5,1},{6,2},{7,3},{8,12},{9,13},{10,... | collective-permute-start | bytes 86024 | tf_op jit(solution)/shard_map/ppermute | solution.py:326
  71.6 4.9 %collective-permute-start.23 = (bf16[4,3584]{1,0:T(4,128)(2,1)S(1)}, bf16[4,3584]{1,0:T(4,128)(2,1)S(1)}, u32[]{:S(2)}, u32[]{:S(2)}) collective-permute-start(bf16[4,3584]{1,0:T(4,128)(2,1)S(1)} %get-tuple-element.61), channel_id=1, source_target_pairs={{0,8},{1,9},{2,10},{3,11},{4,12},{5,13},{6,14},{7,15},{8,0},{9,1},... | collective-permute-start | bytes 86024 | tf_op jit(solution)/shard_map/ppermute | solution.py:326
  74.0 5.8 %collective-permute-start.24 = (bf16[4,3584]{1,0:T(4,128)(2,1)S(1)}, bf16[4,3584]{1,0:T(4,128)(2,1)S(1)}, u32[]{:S(2)}, u32[]{:S(2)}) collective-permute-start(bf16[4,3584]{1,0:T(4,128)(2,1)S(1)} %get-tuple-element.62), channel_id=1, source_target_pairs={{0,12},{1,13},{2,14},{3,15},{4,8},{5,9},{6,10},{7,11},{8,4},{9,5},... | collective-permute-start | bytes 86024 | tf_op jit(solution)/shard_map/ppermute | solution.py:326
  75.6 4.2 %collective-permute-start.25 = (bf16[4,3584]{1,0:T(4,128)(2,1)S(1)}, bf16[4,3584]{1,0:T(4,128)(2,1)S(1)}, u32[]{:S(2)}, u32[]{:S(2)}) collective-permute-start(bf16[4,3584]{1,0:T(4,128)(2,1)S(1)} %get-tuple-element.63), channel_id=1, source_target_pairs={{0,4},{1,5},{2,6},{3,7},{4,0},{5,1},{6,2},{7,3},{8,12},{9,13},{10,... | collective-permute-start | bytes 86024 | tf_op jit(solution)/shard_map/ppermute | solution.py:326
  (12 other events, 154.0 us)

commit v6 on v5

--- a/solution.py
+++ b/solution.py
@@ -57,7 +57,7 @@
 
 
 def gathered_order(devices):
-    return [z + y for z in range(0, devices, 4) for y in (0, 2)]
+    return [z + y for y in (0, 2) for z in far_first(devices, 4)]
 
 
 def rotary_kernel(len_ref, cos_ref, sin_ref):
@@ -80,30 +80,35 @@
     return call(rotary_kernel, (table, table), 3, "rotary", scalars=1)(lengths)
 
 
-def join_kernel(*refs):
-    *in_refs, out_ref = refs
+def join_kernel(cos_ref, sin_ref, *refs):
+    *in_refs, cos_out_ref, sin_out_ref, out_ref = refs
+    cos_out_ref[...] = cos_ref[...]
+    sin_out_ref[...] = sin_ref[...]
     out_ref[...] = jnp.concatenate(
         [ref[...].astype(jnp.float32) for ref in in_refs], axis=0
     ).astype(out_ref.dtype)
 
 
-def join(blocks):
+def join(tables, blocks):
     rows, depth = blocks[0].shape
-    return call(join_kernel, shape(len(blocks) * rows, depth), 5, "join")(*blocks)
-
-
-def project_kernel(devices, q_ref, *refs):
+    out = (*[shape(*t.shape, dtype=t.dtype) for t in tables], shape(len(blocks) * rows, depth))
+    cosine, sine, joined = call(join_kernel, out, 3, "join")(*tables, *blocks)
+    return (cosine, sine), joined
+
+
+def project_kernel(devices, q_ref, far_ref, *refs):
     weights = (refs[0:2], refs[2:4])
     lat_ref, rot_ref = refs[-2:]
     out_refs = refs[4:-2]
     heads = weights[0][1].shape[0]
-    count = q_ref.shape[0]
+    piece = jnp.concatenate([q_ref[...], far_ref[...]], axis=0)
+    count = piece.shape[0]
     wide = 2 * count // devices * heads
     width = NOPE + ROPE
     lane = lax.broadcasted_iota(jnp.int32, (wide // 2, LANES), 1)
     order = far_first(devices, 2)
     for core, (wq_ref, wk_ref) in enumerate(weights):
-        projected = jnp.dot(q_ref[...], wq_ref[...], preferred_element_type=jnp.float32)
+        projected = jnp.dot(piece, wq_ref[...], preferred_element_type=jnp.float32)
         for h in range(heads):
             mine = projected[:, h * width : (h + 1) * width]
             absorbed = jnp.dot(
@@ -128,9 +133,9 @@
             )
 
 
-def project(piece, weights, devices):
+def project(near, far, weights, devices):
     heads = weights[1].shape[0]
-    count = piece.shape[0]
+    count = 2 * near.shape[0]
     wide = 2 * count // devices * heads
     scratch = [
         pltpu.VMEM((2 * PIECES, count * heads, LANES), jnp.float32),
@@ -138,7 +143,7 @@
     ]
     out = [shape(2, PIECES * wide + wide // 2, LANES)] * (devices // 2)
     kernel = functools.partial(project_kernel, devices)
-    return call(kernel, out, 20, "project", scratch)(piece, *[resident(w) for w in weights])
+    return call(kernel, out, 20, "project", scratch)(near, far, *[resident(w) for w in weights])
 
 
 def attend_kernel(chips, len_ref, cos_ref, sin_ref, key_ref, new_ref, *refs):
@@ -286,32 +291,35 @@
     return call(functools.partial(core_sum_kernel, keep, give), out, 1, "core_sum")(mine, other)
 
 
-def chip_sum_kernel(mine_ref, other_ref, *out_refs):
+def chip_sum_kernel(*refs):
+    mine_refs = refs[:PARTS]
+    other_refs = refs[PARTS : 2 * PARTS]
+    out_refs = refs[2 * PARTS :]
     rows = out_refs[0].shape[0]
-    total = mine_ref[...] + other_ref[...].astype(jnp.float32)
-    for j, out_ref in enumerate(out_refs):
-        out_ref[...] = total[j * rows : (j + 1) * rows].astype(out_ref.dtype)
+    for p, (mine_ref, other_ref) in enumerate(zip(mine_refs, other_refs)):
+        width = mine_ref.shape[1]
+        total = mine_ref[...] + other_ref[...].astype(jnp.float32)
+        for j, out_ref in enumerate(out_refs):
+            out_ref[:, p * width : (p + 1) * width] = total[j * rows : (j + 1) * rows].astype(
+                out_ref.dtype
+            )
 
 
 def chip_sum(mine, other, rows):
-    count, width = mine.shape
+    count, width = mine[0].shape
+    width *= PARTS
     out = [shape(rows, width)] * (count // rows - 1) + [shape(rows, width, dtype=jnp.float32)]
-    return call(chip_sum_kernel, out, 1, "chip_sum")(mine, other)
+    return call(chip_sum_kernel, out, 1, "chip_sum")(*mine, *other)
 
 
 def last_sum_kernel(*refs):
     *in_refs, out_ref = refs
-    each = len(in_refs) // PARTS
-    width = out_ref.shape[1] // PARTS
-    for p in range(PARTS):
-        terms = [ref[...].astype(jnp.float32) for ref in in_refs[p * each : (p + 1) * each]]
-        out_ref[:, p * width : (p + 1) * width] = sum(terms[1:], terms[0]).astype(out_ref.dtype)
-
-
-def last_sum(shares):
-    rows, width = shares[0][0].shape
-    blocks = [block for part in shares for block in part]
-    return call(last_sum_kernel, shape(rows, PARTS * width), 1, "last_sum")(*blocks)
+    terms = [ref[...].astype(jnp.float32) for ref in in_refs]
+    out_ref[...] = sum(terms[1:], terms[0]).astype(out_ref.dtype)
+
+
+def last_sum(blocks):
+    return call(last_sum_kernel, shape(*blocks[0].shape), 1, "last_sum")(*blocks)
 
 
 def on_device(q_latent, new_latent, cache, lengths, w_uq, w_uk, w_uv, w_o, devices):
@@ -326,22 +334,21 @@
         return lax.ppermute(block, "row", [(i, i ^ k) for i in range(devices)])
 
     far_weights = [swap(w_uq, 1), swap(w_uk, 1)]
-    near = join([q_latent, swap(q_latent, 2)])
-    tables = rotary(lengths)
-    near = join([swap(near, z) for z in range(0, devices, 4)])
-    messages = project(near, [w_uq, w_uk, *far_weights], devices)
+    tables, near = join(rotary(lengths), [swap(q_latent, z) for z in zs])
+    messages = project(near, swap(near, 2), [w_uq, w_uk, *far_weights], devices)
     messages = [swap(block, k) for k, block in zip(order, messages)]
     keys = jnp.swapaxes(cache, 1, 2)
     latents = attend(lengths, tables, keys, new_latent, messages, heads)
     latents = [swap(block, k) for k, block in zip(order, latents)]
     values = head_values(latents, swap(regroup(latents), 1), w_uv)
-    shares = []
+    keep, got = [], []
     for part in range(PARTS):
         mine, other = output_terms(values, w_o, part)
         mine, other = core_sum(mine, swap(other, 1), devices)
-        blocks = chip_sum(mine, swap(other, 2), rows)
-        shares.append([swap(block, z) for z, block in zip(zs, blocks)])
-    return last_sum(shares)
+        keep.append(mine)
+        got.append(swap(other, 2))
+    blocks = chip_sum(keep, got, rows)
+    return last_sum([swap(block, z) for z, block in zip(zs, blocks)])
 
 
 def solution(mesh):

time: 80.7 us -> 77.6 us (0.962)
  starting transfers between devices: 40.7 us -> 35.6 us
  waiting for transfers between devices: 25 us -> 27.2 us
    ppermute x31 -> x28, starting transfers between devices: 40.7 us -> 35.6 us  [swap(): return lax.ppermute(block, 'row', [(i, i ^ k) for i in range(devices)])]
    ppermute x31 -> x28, waiting for transfers between devices: 25 us -> 27.2 us  [swap(): return lax.ppermute(block, 'row', [(i, i ^ k) for i in range(devices)])]
    pallas_call x14 -> x12, Pallas kernels: 13.7 us -> 13.6 us  [run(): pl.pallas_call(kernel, out_shape=out_shape, in_specs=smem + [in_vmem()] *...]
  transfers between devices with their start and end apart: 31 -> 28, of which waited for: 15 -> 16; matrix products, arithmetic and copies ran while one was open for 0% -> 0% of each run, Pallas kernels for 4% -> 4%
where the time goes in v6:
time: 77.6 us; the launch traced here: 77.4 us
  starting transfers between devices  35.6 us (46%)
  waiting for transfers between devices  27.2 us (35%)
  Pallas kernels  13.6 us (18%)
    ppermute x28, starting transfers between devices, swap(): return lax.ppermute(block, 'row', [(i, i ^ k) for i in range(devices)])  35.6 us
    ppermute x28, waiting for transfers between devices, swap(): return lax.ppermute(block, 'row', [(i, i ^ k) for i in range(devices)])  27.2 us
    pallas_call x12, Pallas kernels, run(): pl.pallas_call(kernel, out_shape=out_shape, in_specs=smem + [in_vmem()] *...  13.6 us
  transfers between devices with their start and end apart: 28, of which 16 were waited for; matrix products, arithmetic and copies ran while one was open for 0% of the time, Pallas kernels for 4%

profile of v6, /device:TPU:0, one launch (start us, length us, event | category | flops | bytes accessed | tf_op | source)
XLA Modules:
  0.0 77.4 jit_solution(13888180709701552056)
XLA Ops:
  0.5 5.0 %collective-permute-start.1 = (bf16[4,1536]{1,0:T(4,128)(2,1)}, bf16[4,1536]{1,0:T(4,128)(2,1)S(1)}, u32[]{:S(2)}, u32[]{:S(2)}) collective-permute-start(bf16[4,1536]{1,0:T(4,128)(2,1)} %refs_3_.1), channel_id=1, source_target_pairs={{0,12},{1,13},{2,14},{3,15},{4,8},{5,9},{6,10},{7,11},{8,4},{9,5},... | collective-permute-start | bytes 36872 | tf_op jit(solution)/shard_map/ppermute | solution.py:334
  7.4 2.9 %collective-permute-done.refs_0_ = bf16[4,1536]{1,0:T(4,128)(2,1)S(1)} collective-permute-done((bf16[4,1536]{1,0:T(4,128)(2,1)}, bf16[4,1536]{1,0:T(4,128)(2,1)S(1)}, u32[]{:S(2)}, u32[]{:S(2)}) %collective-permute-start) | collective-permute-done | bytes 12320 | tf_op jit(solution)/shard_map/ppermute | solution.py:334
  10.5 1.6 %collective-permute-start.3 = (bf16[16,1536]{1,0:T(8,128)(2,1)S(1)}, bf16[16,1536]{1,0:T(8,128)(2,1)S(1)}, u32[]{:S(2)}, u32[]{:S(2)}) collective-permute-start(bf16[16,1536]{1,0:T(8,128)(2,1)S(1)} %get-tuple-element.42.q_ref), channel_id=1, source_target_pairs={{0,2},{1,3},{2,0},{3,1},{4,6},{5,7},{6,4},{7,5},{8,10},{9,11},{10,... | collective-permute-start | bytes 147464 | tf_op jit(solution)/shard_map/ppermute | solution.py:334
  12.0 2.6 %collective-permute-done.3.far_ref = bf16[16,1536]{1,0:T(8,128)(2,1)S(1)} collective-permute-done((bf16[16,1536]{1,0:T(8,128)(2,1)S(1)}, bf16[16,1536]{1,0:T(8,128)(2,1)S(1)}, u32[]{:S(2)}, u32[]{:S(2)}) %collective-permute-start.3) | collective-permute-done | bytes 49184 | tf_op jit(solution)/shard_map/ppermute | solution.py:334
  14.6 2.3 %project.1 = (bf16[2,144,128]{2,1,0:T(8,128)(2,1)S(1)}, bf16[2,144,128]{2,1,0:T(8,128)(2,1)S(1)}, bf16[2,144,128]{2,1,0:T(8,128)(2,1)S(1)}, bf16[2,144,128]{2,1,...) custom-call(bf16[16,1536]{1,0:T(8,128)(2,1)S(1)} %get-tuple-element., ...), custom_call_target="tpu_custom_call" | custom-call | flops 23000000512 | tf_op jit(solution)/shard_map/project/pallas_call | solution.py:35
  17.0 2.1 %collective-permute-start.6 = (bf16[2,144,128]{2,1,0:T(8,128)(2,1)S(1)}, bf16[2,144,128]{2,1,0:T(8,128)(2,1)S(1)}, u32[]{:S(2)}, u32[]{:S(2)}) collective-permute-start(bf16[2,144,128]{2,1,0:T(8,128)(2,1)S(1)} %get-tuple-element.43), channel_id=1, source_target_pairs={{0,8},{1,9},{2,10},{3,11},{4,12},{5,13},{6,14},{7,15},{8,0},{9,1},... | collective-permute-start | bytes 221192 | tf_op jit(solution)/shard_map/ppermute | solution.py:334
  19.0 1.9 %collective-permute-start.7 = (bf16[2,144,128]{2,1,0:T(8,128)(2,1)S(1)}, bf16[2,144,128]{2,1,0:T(8,128)(2,1)S(1)}, u32[]{:S(2)}, u32[]{:S(2)}) collective-permute-start(bf16[2,144,128]{2,1,0:T(8,128)(2,1)S(1)} %get-tuple-element.44), channel_id=1, source_target_pairs={{0,10},{1,11},{2,8},{3,9},{4,14},{5,15},{6,12},{7,13},{8,2},{9,3},... | collective-permute-start | bytes 221192 | tf_op jit(solution)/shard_map/ppermute | solution.py:334
  20.9 1.5 %collective-permute-start.8 = (bf16[2,144,128]{2,1,0:T(8,128)(2,1)S(1)}, bf16[2,144,128]{2,1,0:T(8,128)(2,1)S(1)}, u32[]{:S(2)}, u32[]{:S(2)}) collective-permute-start(bf16[2,144,128]{2,1,0:T(8,128)(2,1)S(1)} %get-tuple-element.45), channel_id=1, source_target_pairs={{0,12},{1,13},{2,14},{3,15},{4,8},{5,9},{6,10},{7,11},{8,4},{9,5},... | collective-permute-start | bytes 221192 | tf_op jit(solution)/shard_map/ppermute | solution.py:334
  22.4 2.3 %collective-permute-start.9 = (bf16[2,144,128]{2,1,0:T(8,128)(2,1)S(1)}, bf16[2,144,128]{2,1,0:T(8,128)(2,1)S(1)}, u32[]{:S(2)}, u32[]{:S(2)}) collective-permute-start(bf16[2,144,128]{2,1,0:T(8,128)(2,1)S(1)} %get-tuple-element.46), channel_id=1, source_target_pairs={{0,14},{1,15},{2,12},{3,13},{4,10},{5,11},{6,8},{7,9},{8,6},{9,7},... | collective-permute-start | bytes 221192 | tf_op jit(solution)/shard_map/ppermute | solution.py:334
  24.7 1.5 %collective-permute-done.6.refs_0_ = bf16[2,144,128]{2,1,0:T(8,128)(2,1)S(1)} collective-permute-done((bf16[2,144,128]{2,1,0:T(8,128)(2,1)S(1)}, bf16[2,144,128]{2,1,0:T(8,128)(2,1)S(1)}, u32[]{:S(2)}, u32[]{:S(2)}) %collective-permute-start.6) | collective-permute-done | bytes 73760 | tf_op jit(solution)/shard_map/ppermute | solution.py:334
  26.2 1.5 %collective-permute-start.11 = (bf16[2,144,128]{2,1,0:T(8,128)(2,1)S(1)}, bf16[2,144,128]{2,1,0:T(8,128)(2,1)S(1)}, u32[]{:S(2)}, u32[]{:S(2)}) collective-permute-start(bf16[2,144,128]{2,1,0:T(8,128)(2,1)S(1)} %get-tuple-element.48), channel_id=1, source_target_pairs={{0,6},{1,7},{2,4},{3,5},{4,2},{5,3},{6,0},{7,1},{8,14},{9,15},{10,... | collective-permute-start | bytes 221192 | tf_op jit(solution)/shard_map/ppermute | solution.py:334
  27.7 2.4 %collective-permute-done.7.refs_1_ = bf16[2,144,128]{2,1,0:T(8,128)(2,1)S(1)} collective-permute-done((bf16[2,144,128]{2,1,0:T(8,128)(2,1)S(1)}, bf16[2,144,128]{2,1,0:T(8,128)(2,1)S(1)}, u32[]{:S(2)}, u32[]{:S(2)}) %collective-permute-start.7) | collective-permute-done | bytes 73760 | tf_op jit(solution)/shard_map/ppermute | solution.py:334
  30.8 0.9 %collective-permute-done.11.refs_5_ = bf16[2,144,128]{2,1,0:T(8,128)(2,1)S(1)} collective-permute-done((bf16[2,144,128]{2,1,0:T(8,128)(2,1)S(1)}, bf16[2,144,128]{2,1,0:T(8,128)(2,1)S(1)}, u32[]{:S(2)}, u32[]{:S(2)}) %collective-permute-start.11) | collective-permute-done | bytes 73760 | tf_op jit(solution)/shard_map/ppermute | solution.py:334
  31.7 2.7 %collective-permute-done.12.refs_6_ = bf16[2,144,128]{2,1,0:T(8,128)(2,1)S(1)} collective-permute-done((bf16[2,144,128]{2,1,0:T(8,128)(2,1)S(1)}, bf16[2,144,128]{2,1,0:T(8,128)(2,1)S(1)}, u32[]{:S(2)}, u32[]{:S(2)}) %collective-permute-start.12) | collective-permute-done | bytes 73760 | tf_op jit(solution)/shard_map/ppermute | solution.py:334
  34.5 5.1 %attend.1 = (bf16[2,32,512]{2,1,0:T(8,128)(2,1)S(1)}, bf16[2,32,512]{2,1,0:T(8,128)(2,1)S(1)}, bf16[2,32,512]{2,1,0:T(8,128)(2,1)S(1)}, bf16[2,32,512]{2,1,0:T(8...) custom-call(s32[4]{0:T(128)S(1)} %copy-done.5, ...), custom_call_target="tpu_custom_call" | custom-call | flops 11500000256 | tf_op jit(solution)/shard_map/attend/pallas_call | solution.py:35
  39.8 3.0 %collective-permute-start.14 = (bf16[2,32,512]{2,1,0:T(8,128)(2,1)S(1)}, bf16[2,32,512]{2,1,0:T(8,128)(2,1)S(1)}, u32[]{:S(2)}, u32[]{:S(2)}) collective-permute-start(bf16[2,32,512]{2,1,0:T(8,128)(2,1)S(1)} %get-tuple-element.52), channel_id=1, source_target_pairs={{0,10},{1,11},{2,8},{3,9},{4,14},{5,15},{6,12},{7,13},{8,2},{9,3},... | collective-permute-start | bytes 196616 | tf_op jit(solution)/shard_map/ppermute | solution.py:334
  42.8 2.0 %collective-permute-start.15 = (bf16[2,32,512]{2,1,0:T(8,128)(2,1)S(1)}, bf16[2,32,512]{2,1,0:T(8,128)(2,1)S(1)}, u32[]{:S(2)}, u32[]{:S(2)}) collective-permute-start(bf16[2,32,512]{2,1,0:T(8,128)(2,1)S(1)} %get-tuple-element.53), channel_id=1, source_target_pairs={{0,12},{1,13},{2,14},{3,15},{4,8},{5,9},{6,10},{7,11},{8,4},{9,5},... | collective-permute-start | bytes 196616 | tf_op jit(solution)/shard_map/ppermute | solution.py:334
  44.8 2.5 %collective-permute-start.16 = (bf16[2,32,512]{2,1,0:T(8,128)(2,1)S(1)}, bf16[2,32,512]{2,1,0:T(8,128)(2,1)S(1)}, u32[]{:S(2)}, u32[]{:S(2)}) collective-permute-start(bf16[2,32,512]{2,1,0:T(8,128)(2,1)S(1)} %get-tuple-element.54), channel_id=1, source_target_pairs={{0,14},{1,15},{2,12},{3,13},{4,10},{5,11},{6,8},{7,9},{8,6},{9,7},... | collective-permute-start | bytes 196616 | tf_op jit(solution)/shard_map/ppermute | solution.py:334
  47.4 2.2 %collective-permute-start.18 = (bf16[2,32,512]{2,1,0:T(8,128)(2,1)S(1)}, bf16[2,32,512]{2,1,0:T(8,128)(2,1)S(1)}, u32[]{:S(2)}, u32[]{:S(2)}) collective-permute-start(bf16[2,32,512]{2,1,0:T(8,128)(2,1)S(1)} %get-tuple-element.56), channel_id=1, source_target_pairs={{0,6},{1,7},{2,4},{3,5},{4,2},{5,3},{6,0},{7,1},{8,14},{9,15},{10,... | collective-permute-start | bytes 196616 | tf_op jit(solution)/shard_map/ppermute | solution.py:334
  49.6 1.2 %collective-permute-start.19 = (bf16[2,32,512]{2,1,0:T(8,128)(2,1)S(1)}, bf16[2,32,512]{2,1,0:T(8,128)(2,1)S(1)}, u32[]{:S(2)}, u32[]{:S(2)}) collective-permute-start(bf16[2,32,512]{2,1,0:T(8,128)(2,1)S(1)} %get-tuple-element.57), channel_id=1, source_target_pairs={{0,2},{1,3},{2,0},{3,1},{4,6},{5,7},{6,4},{7,5},{8,10},{9,11},{10,... | collective-permute-start | bytes 196616 | tf_op jit(solution)/shard_map/ppermute | solution.py:334
  50.9 1.1 %collective-permute-done.16.refs_3_ = bf16[2,32,512]{2,1,0:T(8,128)(2,1)S(1)} collective-permute-done((bf16[2,32,512]{2,1,0:T(8,128)(2,1)S(1)}, bf16[2,32,512]{2,1,0:T(8,128)(2,1)S(1)}, u32[]{:S(2)}, u32[]{:S(2)}) %collective-permute-start.16) | collective-permute-done | bytes 65568 | tf_op jit(solution)/shard_map/ppermute | solution.py:334
  52.2 1.1 %collective-permute-done.18.refs_5_ = bf16[2,32,512]{2,1,0:T(8,128)(2,1)S(1)} collective-permute-done((bf16[2,32,512]{2,1,0:T(8,128)(2,1)S(1)}, bf16[2,32,512]{2,1,0:T(8,128)(2,1)S(1)}, u32[]{:S(2)}, u32[]{:S(2)}) %collective-permute-start.18) | collective-permute-done | bytes 65568 | tf_op jit(solution)/shard_map/ppermute | solution.py:334
  54.0 1.5 %collective-permute-done.20.refs_8_ = bf16[8,32,512]{2,1,0:T(8,128)(2,1)S(1)} collective-permute-done((bf16[8,32,512]{2,1,0:T(8,128)(2,1)S(1)}, bf16[8,32,512]{2,1,0:T(8,128)(2,1)S(1)}, u32[]{:S(2)}, u32[]{:S(2)}) %collective-permute-start.20) | collective-permute-done | bytes 262176 | tf_op jit(solution)/shard_map/ppermute | solution.py:334
  56.1 2.1 %terms.3 = (f32[32,3584]{1,0:T(8,128)S(1)}, bf16[32,3584]{1,0:T(8,128)(2,1)S(1)}) custom-call(bf16[64,1024]{1,0:T(8,128)(2,1)S(1)} %values.1.val_ref, bf16[1024,7168]{1,0:T(8,128)(2,1)S(1)} %bitcast.2), custom_call_target="tpu_custom_call" | custom-call | flops 6899999744 | tf_op jit(solution)/shard_map/terms/pallas_call | solution.py:35
  58.4 2.1 %terms.2 = (f32[32,3584]{1,0:T(8,128)S(1)}, bf16[32,3584]{1,0:T(8,128)(2,1)S(1)}) custom-call(bf16[64,1024]{1,0:T(8,128)(2,1)S(1)} %values.1.val_ref, bf16[1024,7168]{1,0:T(8,128)(2,1)S(1)} %bitcast.2), custom_call_target="tpu_custom_call" | custom-call | flops 6899999744 | tf_op jit(solution)/shard_map/terms/pallas_call | solution.py:35
  61.0 1.3 %collective-permute-start.24 = (bf16[16,3584]{1,0:T(8,128)(2,1)S(1)}, bf16[16,3584]{1,0:T(8,128)(2,1)S(1)}, u32[]{:S(2)}, u32[]{:S(2)}) collective-permute-start(bf16[16,3584]{1,0:T(8,128)(2,1)S(1)} %get-tuple-element.66), channel_id=1, source_target_pairs={{0,2},{1,3},{2,0},{3,1},{4,6},{5,7},{6,4},{7,5},{8,10},{9,11},{10,... | collective-permute-start | bytes 344072 | tf_op jit(solution)/shard_map/ppermute | solution.py:334
  62.4 1.0 %collective-permute-start.23 = (bf16[16,3584]{1,0:T(8,128)(2,1)S(1)}, bf16[16,3584]{1,0:T(8,128)(2,1)S(1)}, u32[]{:S(2)}, u32[]{:S(2)}) collective-permute-start(bf16[16,3584]{1,0:T(8,128)(2,1)S(1)} %get-tuple-element.65), channel_id=1, source_target_pairs={{0,2},{1,3},{2,0},{3,1},{4,6},{5,7},{6,4},{7,5},{8,10},{9,11},{10,... | collective-permute-start | bytes 344072 | tf_op jit(solution)/shard_map/ppermute | solution.py:334
  63.4 3.7 %collective-permute-done.24.refs_3_ = bf16[16,3584]{1,0:T(8,128)(2,1)S(1)} collective-permute-done((bf16[16,3584]{1,0:T(8,128)(2,1)S(1)}, bf16[16,3584]{1,0:T(8,128)(2,1)S(1)}, u32[]{:S(2)}, u32[]{:S(2)}) %collective-permute-start.24) | collective-permute-done | bytes 114720 | tf_op jit(solution)/shard_map/ppermute | solution.py:334
  67.1 1.7 %collective-permute-done.23.refs_2_ = bf16[16,3584]{1,0:T(8,128)(2,1)S(1)} collective-permute-done((bf16[16,3584]{1,0:T(8,128)(2,1)S(1)}, bf16[16,3584]{1,0:T(8,128)(2,1)S(1)}, u32[]{:S(2)}, u32[]{:S(2)}) %collective-permute-start.23) | collective-permute-done | bytes 114720 | tf_op jit(solution)/shard_map/ppermute | solution.py:334
  68.8 1.2 %collective-permute-start.25 = (bf16[4,7168]{1,0:T(4,128)(2,1)S(1)}, bf16[4,7168]{1,0:T(4,128)(2,1)S(1)}, u32[]{:S(2)}, u32[]{:S(2)}) collective-permute-start(bf16[4,7168]{1,0:T(4,128)(2,1)S(1)} %get-tuple-element.67), channel_id=1, source_target_pairs={{0,8},{1,9},{2,10},{3,11},{4,12},{5,13},{6,14},{7,15},{8,0},{9,1},... | collective-permute-start | bytes 172040 | tf_op jit(solution)/shard_map/ppermute | solution.py:334
  70.0 2.5 %collective-permute-start.26 = (bf16[4,7168]{1,0:T(4,128)(2,1)S(1)}, bf16[4,7168]{1,0:T(4,128)(2,1)S(1)}, u32[]{:S(2)}, u32[]{:S(2)}) collective-permute-start(bf16[4,7168]{1,0:T(4,128)(2,1)S(1)} %get-tuple-element.68), channel_id=1, source_target_pairs={{0,12},{1,13},{2,14},{3,15},{4,8},{5,9},{6,10},{7,11},{8,4},{9,5},... | collective-permute-start | bytes 172040 | tf_op jit(solution)/shard_map/ppermute | solution.py:334
  72.6 3.5 %collective-permute-done.25.refs_0_ = bf16[4,7168]{1,0:T(4,128)(2,1)S(1)} collective-permute-done((bf16[4,7168]{1,0:T(4,128)(2,1)S(1)}, bf16[4,7168]{1,0:T(4,128)(2,1)S(1)}, u32[]{:S(2)}, u32[]{:S(2)}) %collective-permute-start.25) | collective-permute-done | bytes 57376 | tf_op jit(solution)/shard_map/ppermute | solution.py:334
  (67 shorter events, 7.0 us)
Async XLA Ops:
  0.0 14.6 %collective-permute-start.4 = (bf16[1536,1536]{1,0:T(8,128)(2,1)}, bf16[1536,1536]{1,0:T(8,128)(2,1)S(1)}, u32[]{:S(2)}, u32[]{:S(2)}) collective-permute-start(bf16[1536,1536]{1,0:T(8,128)(2,1)} %refs_0_.1), channel_id=1, source_target_pairs={{0,1},{1,0},{2,3},{3,2},{4,5},{5,4},{6,7},{7,6},{8,9},{9,8},{10,11... | collective-permute-start | bytes 14155784 | tf_op jit(solution)/shard_map/ppermute | solution.py:334
  0.5 14.2 %collective-permute-start.5 = (bf16[8,128,512]{2,1,0:T(8,128)(2,1)}, bf16[8,128,512]{2,1,0:T(8,128)(2,1)S(1)}, u32[]{:S(2)}, u32[]{:S(2)}) collective-permute-start(bf16[8,128,512]{2,1,0:T(8,128)(2,1)} %refs_1_.1), channel_id=1, source_target_pairs={{0,1},{1,0},{2,3},{3,2},{4,5},{5,4},{6,7},{7,6},{8,9},{9,8},{10,11... | collective-permute-start | bytes 3145736 | tf_op jit(solution)/shard_map/ppermute | solution.py:334
  0.5 6.9 %collective-permute-start.1 = (bf16[4,1536]{1,0:T(4,128)(2,1)}, bf16[4,1536]{1,0:T(4,128)(2,1)S(1)}, u32[]{:S(2)}, u32[]{:S(2)}) collective-permute-start(bf16[4,1536]{1,0:T(4,128)(2,1)} %refs_3_.1), channel_id=1, source_target_pairs={{0,12},{1,13},{2,14},{3,15},{4,8},{5,9},{6,10},{7,11},{8,4},{9,5},... | collective-permute-start | bytes 36872 | tf_op jit(solution)/shard_map/ppermute | solution.py:334
  5.6 4.8 %collective-permute-start = (bf16[4,1536]{1,0:T(4,128)(2,1)}, bf16[4,1536]{1,0:T(4,128)(2,1)S(1)}, u32[]{:S(2)}, u32[]{:S(2)}) collective-permute-start(bf16[4,1536]{1,0:T(4,128)(2,1)} %refs_3_.1), channel_id=1, source_target_pairs={{0,8},{1,9},{2,10},{3,11},{4,12},{5,13},{6,14},{7,15},{8,0},{9,1},... | collective-permute-start | bytes 36872 | tf_op jit(solution)/shard_map/ppermute | solution.py:334
  5.6 4.8 %collective-permute-start.2 = (bf16[4,1536]{1,0:T(4,128)(2,1)}, bf16[4,1536]{1,0:T(4,128)(2,1)S(1)}, u32[]{:S(2)}, u32[]{:S(2)}) collective-permute-start(bf16[4,1536]{1,0:T(4,128)(2,1)} %refs_3_.1), channel_id=1, source_target_pairs={{0,4},{1,5},{2,6},{3,7},{4,0},{5,1},{6,2},{7,3},{8,12},{9,13},{10,... | collective-permute-start | bytes 36872 | tf_op jit(solution)/shard_map/ppermute | solution.py:334
  10.4 24.0 %slice-start.4 = ((s8[7077888]{0:T(1024)(128)(4,1)}), s8[4194304]{0:T(1024)(128)(4,1)S(1)}, s32[]{:S(2)}) async-start(s8[7077888]{0:T(1024)(128)(4,1)} %bitcast.3), calls=%async_computation.4 | async-start | bytes 8388608
  10.4 24.0 %slice-start.5 = ((s8[7077888]{0:T(1024)(128)(4,1)}), s8[2883584]{0:T(1024)(128)(4,1)S(1)}, s32[]{:S(2)}) async-start(s8[7077888]{0:T(1024)(128)(4,1)} %bitcast.3), calls=%async_computation.5 | async-start | bytes 5767168
  10.4 24.0 %copy-start.3 = (bf16[4,576]{1,0:T(4,128)(2,1)S(1)}, bf16[4,576]{1,0:T(4,128)(2,1)}, u32[]{:S(2)}) copy-start(bf16[4,576]{1,0:T(4,128)(2,1)} %new_ref.1) | copy-start | bytes 13828
  10.4 24.0 %copy-start.5 = (s32[4]{0:T(128)S(1)}, s32[4]{0:T(128)}, u32[]{:S(2)}) copy-start(s32[4]{0:T(128)} %len_ref.3) | copy-start | bytes 52
  10.5 4.2 %collective-permute-start.3 = (bf16[16,1536]{1,0:T(8,128)(2,1)S(1)}, bf16[16,1536]{1,0:T(8,128)(2,1)S(1)}, u32[]{:S(2)}, u32[]{:S(2)}) collective-permute-start(bf16[16,1536]{1,0:T(8,128)(2,1)S(1)} %get-tuple-element.42.q_ref), channel_id=1, source_target_pairs={{0,2},{1,3},{2,0},{3,1},{4,6},{5,7},{6,4},{7,5},{8,10},{9,11},{10,... | collective-permute-start | bytes 147464 | tf_op jit(solution)/shard_map/ppermute | solution.py:334
  17.0 9.2 %collective-permute-start.6 = (bf16[2,144,128]{2,1,0:T(8,128)(2,1)S(1)}, bf16[2,144,128]{2,1,0:T(8,128)(2,1)S(1)}, u32[]{:S(2)}, u32[]{:S(2)}) collective-permute-start(bf16[2,144,128]{2,1,0:T(8,128)(2,1)S(1)} %get-tuple-element.43), channel_id=1, source_target_pairs={{0,8},{1,9},{2,10},{3,11},{4,12},{5,13},{6,14},{7,15},{8,0},{9,1},... | collective-permute-start | bytes 221192 | tf_op jit(solution)/shard_map/ppermute | solution.py:334
  19.0 11.0 %collective-permute-start.7 = (bf16[2,144,128]{2,1,0:T(8,128)(2,1)S(1)}, bf16[2,144,128]{2,1,0:T(8,128)(2,1)S(1)}, u32[]{:S(2)}, u32[]{:S(2)}) collective-permute-start(bf16[2,144,128]{2,1,0:T(8,128)(2,1)S(1)} %get-tuple-element.44), channel_id=1, source_target_pairs={{0,10},{1,11},{2,8},{3,9},{4,14},{5,15},{6,12},{7,13},{8,2},{9,3},... | collective-permute-start | bytes 221192 | tf_op jit(solution)/shard_map/ppermute | solution.py:334
  20.9 9.9 %collective-permute-start.8 = (bf16[2,144,128]{2,1,0:T(8,128)(2,1)S(1)}, bf16[2,144,128]{2,1,0:T(8,128)(2,1)S(1)}, u32[]{:S(2)}, u32[]{:S(2)}) collective-permute-start(bf16[2,144,128]{2,1,0:T(8,128)(2,1)S(1)} %get-tuple-element.45), channel_id=1, source_target_pairs={{0,12},{1,13},{2,14},{3,15},{4,8},{5,9},{6,10},{7,11},{8,4},{9,5},... | collective-permute-start | bytes 221192 | tf_op jit(solution)/shard_map/ppermute | solution.py:334
  22.4 8.4 %collective-permute-start.9 = (bf16[2,144,128]{2,1,0:T(8,128)(2,1)S(1)}, bf16[2,144,128]{2,1,0:T(8,128)(2,1)S(1)}, u32[]{:S(2)}, u32[]{:S(2)}) collective-permute-start(bf16[2,144,128]{2,1,0:T(8,128)(2,1)S(1)} %get-tuple-element.46), channel_id=1, source_target_pairs={{0,14},{1,15},{2,12},{3,13},{4,10},{5,11},{6,8},{7,9},{8,6},{9,7},... | collective-permute-start | bytes 221192 | tf_op jit(solution)/shard_map/ppermute | solution.py:334
  24.7 6.2 %collective-permute-start.10 = (bf16[2,144,128]{2,1,0:T(8,128)(2,1)S(1)}, bf16[2,144,128]{2,1,0:T(8,128)(2,1)S(1)}, u32[]{:S(2)}, u32[]{:S(2)}) collective-permute-start(bf16[2,144,128]{2,1,0:T(8,128)(2,1)S(1)} %get-tuple-element.47), channel_id=1, source_target_pairs={{0,4},{1,5},{2,6},{3,7},{4,0},{5,1},{6,2},{7,3},{8,12},{9,13},{10,... | collective-permute-start | bytes 221192 | tf_op jit(solution)/shard_map/ppermute | solution.py:334
  26.2 5.5 %collective-permute-start.11 = (bf16[2,144,128]{2,1,0:T(8,128)(2,1)S(1)}, bf16[2,144,128]{2,1,0:T(8,128)(2,1)S(1)}, u32[]{:S(2)}, u32[]{:S(2)}) collective-permute-start(bf16[2,144,128]{2,1,0:T(8,128)(2,1)S(1)} %get-tuple-element.48), channel_id=1, source_target_pairs={{0,6},{1,7},{2,4},{3,5},{4,2},{5,3},{6,0},{7,1},{8,14},{9,15},{10,... | collective-permute-start | bytes 221192 | tf_op jit(solution)/shard_map/ppermute | solution.py:334
  30.1 4.4 %collective-permute-start.12 = (bf16[2,144,128]{2,1,0:T(8,128)(2,1)S(1)}, bf16[2,144,128]{2,1,0:T(8,128)(2,1)S(1)}, u32[]{:S(2)}, u32[]{:S(2)}) collective-permute-start(bf16[2,144,128]{2,1,0:T(8,128)(2,1)S(1)} %get-tuple-element.49), channel_id=1, source_target_pairs={{0,2},{1,3},{2,0},{3,1},{4,6},{5,7},{6,4},{7,5},{8,10},{9,11},{10,... | collective-permute-start | bytes 221192 | tf_op jit(solution)/shard_map/ppermute | solution.py:334
  39.6 7.7 %collective-permute-start.13 = (bf16[2,32,512]{2,1,0:T(8,128)(2,1)S(1)}, bf16[2,32,512]{2,1,0:T(8,128)(2,1)S(1)}, u32[]{:S(2)}, u32[]{:S(2)}) collective-permute-start(bf16[2,32,512]{2,1,0:T(8,128)(2,1)S(1)} %get-tuple-element.51), channel_id=1, source_target_pairs={{0,8},{1,9},{2,10},{3,11},{4,12},{5,13},{6,14},{7,15},{8,0},{9,1},... | collective-permute-start | bytes 196616 | tf_op jit(solution)/shard_map/ppermute | solution.py:334
  39.8 9.8 %collective-permute-start.14 = (bf16[2,32,512]{2,1,0:T(8,128)(2,1)S(1)}, bf16[2,32,512]{2,1,0:T(8,128)(2,1)S(1)}, u32[]{:S(2)}, u32[]{:S(2)}) collective-permute-start(bf16[2,32,512]{2,1,0:T(8,128)(2,1)S(1)} %get-tuple-element.52), channel_id=1, source_target_pairs={{0,10},{1,11},{2,8},{3,9},{4,14},{5,15},{6,12},{7,13},{8,2},{9,3},... | collective-permute-start | bytes 196616 | tf_op jit(solution)/shard_map/ppermute | solution.py:334
  42.8 8.0 %collective-permute-start.15 = (bf16[2,32,512]{2,1,0:T(8,128)(2,1)S(1)}, bf16[2,32,512]{2,1,0:T(8,128)(2,1)S(1)}, u32[]{:S(2)}, u32[]{:S(2)}) collective-permute-start(bf16[2,32,512]{2,1,0:T(8,128)(2,1)S(1)} %get-tuple-element.53), channel_id=1, source_target_pairs={{0,12},{1,13},{2,14},{3,15},{4,8},{5,9},{6,10},{7,11},{8,4},{9,5},... | collective-permute-start | bytes 196616 | tf_op jit(solution)/shard_map/ppermute | solution.py:334
  44.8 7.2 %collective-permute-start.16 = (bf16[2,32,512]{2,1,0:T(8,128)(2,1)S(1)}, bf16[2,32,512]{2,1,0:T(8,128)(2,1)S(1)}, u32[]{:S(2)}, u32[]{:S(2)}) collective-permute-start(bf16[2,32,512]{2,1,0:T(8,128)(2,1)S(1)} %get-tuple-element.54), channel_id=1, source_target_pairs={{0,14},{1,15},{2,12},{3,13},{4,10},{5,11},{6,8},{7,9},{8,6},{9,7},... | collective-permute-start | bytes 196616 | tf_op jit(solution)/shard_map/ppermute | solution.py:334
  47.4 4.8 %collective-permute-start.17 = (bf16[2,32,512]{2,1,0:T(8,128)(2,1)S(1)}, bf16[2,32,512]{2,1,0:T(8,128)(2,1)S(1)}, u32[]{:S(2)}, u32[]{:S(2)}) collective-permute-start(bf16[2,32,512]{2,1,0:T(8,128)(2,1)S(1)} %get-tuple-element.55), channel_id=1, source_target_pairs={{0,4},{1,5},{2,6},{3,7},{4,0},{5,1},{6,2},{7,3},{8,12},{9,13},{10,... | collective-permute-start | bytes 196616 | tf_op jit(solution)/shard_map/ppermute | solution.py:334
  47.4 5.8 %collective-permute-start.18 = (bf16[2,32,512]{2,1,0:T(8,128)(2,1)S(1)}, bf16[2,32,512]{2,1,0:T(8,128)(2,1)S(1)}, u32[]{:S(2)}, u32[]{:S(2)}) collective-permute-start(bf16[2,32,512]{2,1,0:T(8,128)(2,1)S(1)} %get-tuple-element.56), channel_id=1, source_target_pairs={{0,6},{1,7},{2,4},{3,5},{4,2},{5,3},{6,0},{7,1},{8,14},{9,15},{10,... | collective-permute-start | bytes 196616 | tf_op jit(solution)/shard_map/ppermute | solution.py:334
  49.6 4.3 %collective-permute-start.19 = (bf16[2,32,512]{2,1,0:T(8,128)(2,1)S(1)}, bf16[2,32,512]{2,1,0:T(8,128)(2,1)S(1)}, u32[]{:S(2)}, u32[]{:S(2)}) collective-permute-start(bf16[2,32,512]{2,1,0:T(8,128)(2,1)S(1)} %get-tuple-element.57), channel_id=1, source_target_pairs={{0,2},{1,3},{2,0},{3,1},{4,6},{5,7},{6,4},{7,5},{8,10},{9,11},{10,... | collective-permute-start | bytes 196616 | tf_op jit(solution)/shard_map/ppermute | solution.py:334
  53.9 1.6 %collective-permute-start.20 = (bf16[8,32,512]{2,1,0:T(8,128)(2,1)S(1)}, bf16[8,32,512]{2,1,0:T(8,128)(2,1)S(1)}, u32[]{:S(2)}, u32[]{:S(2)}) collective-permute-start(bf16[8,32,512]{2,1,0:T(8,128)(2,1)S(1)} %regroup.1), channel_id=1, source_target_pairs={{0,1},{1,0},{2,3},{3,2},{4,5},{5,4},{6,7},{7,6},{8,9},{9,8},{10,11... | collective-permute-start | bytes 786440 | tf_op jit(solution)/shard_map/ppermute | solution.py:334
  58.2 2.8 %collective-permute-start.22 = (bf16[32,3584]{1,0:T(8,128)(2,1)S(1)}, bf16[32,3584]{1,0:T(8,128)(2,1)S(1)}, u32[]{:S(2)}, u32[]{:S(2)}) collective-permute-start(bf16[32,3584]{1,0:T(8,128)(2,1)S(1)} %get-tuple-element.63), channel_id=1, source_target_pairs={{0,1},{1,0},{2,3},{3,2},{4,5},{5,4},{6,7},{7,6},{8,9},{9,8},{10,11... | collective-permute-start | bytes 688136 | tf_op jit(solution)/shard_map/ppermute | solution.py:334
  60.5 1.8 %collective-permute-start.21 = (bf16[32,3584]{1,0:T(8,128)(2,1)S(1)}, bf16[32,3584]{1,0:T(8,128)(2,1)S(1)}, u32[]{:S(2)}, u32[]{:S(2)}) collective-permute-start(bf16[32,3584]{1,0:T(8,128)(2,1)S(1)} %get-tuple-element.60), channel_id=1, source_target_pairs={{0,1},{1,0},{2,3},{3,2},{4,5},{5,4},{6,7},{7,6},{8,9},{9,8},{10,11... | collective-permute-start | bytes 688136 | tf_op jit(solution)/shard_map/ppermute | solution.py:334
  61.0 6.1 %collective-permute-start.24 = (bf16[16,3584]{1,0:T(8,128)(2,1)S(1)}, bf16[16,3584]{1,0:T(8,128)(2,1)S(1)}, u32[]{:S(2)}, u32[]{:S(2)}) collective-permute-start(bf16[16,3584]{1,0:T(8,128)(2,1)S(1)} %get-tuple-element.66), channel_id=1, source_target_pairs={{0,2},{1,3},{2,0},{3,1},{4,6},{5,7},{6,4},{7,5},{8,10},{9,11},{10,... | collective-permute-start | bytes 344072 | tf_op jit(solution)/shard_map/ppermute | solution.py:334
  62.4 6.4 %collective-permute-start.23 = (bf16[16,3584]{1,0:T(8,128)(2,1)S(1)}, bf16[16,3584]{1,0:T(8,128)(2,1)S(1)}, u32[]{:S(2)}, u32[]{:S(2)}) collective-permute-start(bf16[16,3584]{1,0:T(8,128)(2,1)S(1)} %get-tuple-element.65), channel_id=1, source_target_pairs={{0,2},{1,3},{2,0},{3,1},{4,6},{5,7},{6,4},{7,5},{8,10},{9,11},{10,... | collective-permute-start | bytes 344072 | tf_op jit(solution)/shard_map/ppermute | solution.py:334
  68.8 7.3 %collective-permute-start.25 = (bf16[4,7168]{1,0:T(4,128)(2,1)S(1)}, bf16[4,7168]{1,0:T(4,128)(2,1)S(1)}, u32[]{:S(2)}, u32[]{:S(2)}) collective-permute-start(bf16[4,7168]{1,0:T(4,128)(2,1)S(1)} %get-tuple-element.67), channel_id=1, source_target_pairs={{0,8},{1,9},{2,10},{3,11},{4,12},{5,13},{6,14},{7,15},{8,0},{9,1},... | collective-permute-start | bytes 172040 | tf_op jit(solution)/shard_map/ppermute | solution.py:334
  70.0 6.1 %collective-permute-start.26 = (bf16[4,7168]{1,0:T(4,128)(2,1)S(1)}, bf16[4,7168]{1,0:T(4,128)(2,1)S(1)}, u32[]{:S(2)}, u32[]{:S(2)}) collective-permute-start(bf16[4,7168]{1,0:T(4,128)(2,1)S(1)} %get-tuple-element.68), channel_id=1, source_target_pairs={{0,12},{1,13},{2,14},{3,15},{4,8},{5,9},{6,10},{7,11},{8,4},{9,5},... | collective-permute-start | bytes 172040 | tf_op jit(solution)/shard_map/ppermute | solution.py:334
  72.6 4.2 %collective-permute-start.27 = (bf16[4,7168]{1,0:T(4,128)(2,1)S(1)}, bf16[4,7168]{1,0:T(4,128)(2,1)S(1)}, u32[]{:S(2)}, u32[]{:S(2)}) collective-permute-start(bf16[4,7168]{1,0:T(4,128)(2,1)S(1)} %get-tuple-element.69), channel_id=1, source_target_pairs={{0,4},{1,5},{2,6},{3,7},{4,0},{5,1},{6,2},{7,3},{8,12},{9,13},{10,... | collective-permute-start | bytes 172040 | tf_op jit(solution)/shard_map/ppermute | solution.py:334
  (10 other events, 117.6 us)

commit v7 on v6

--- a/solution.py
+++ b/solution.py
@@ -18,7 +18,8 @@
 FACTOR = (NOPE + ROPE) ** -0.5
 LIMIT = 16 * 2**20
 PARTS = 2
-BLOCK = 512
+Y = 2
+Z1 = 4
 
 
 def resident(x):
@@ -57,7 +58,7 @@
 
 
 def gathered_order(devices):
-    return [z + y for y in (0, 2) for z in far_first(devices, 4)]
+    return [z + y for z in far_first(devices, 4) for y in (0, 2)]
 
 
 def rotary_kernel(len_ref, cos_ref, sin_ref):
@@ -96,12 +97,15 @@
     return (cosine, sine), joined
 
 
-def project_kernel(devices, q_ref, far_ref, *refs):
-    weights = (refs[0:2], refs[2:4])
+def project_kernel(devices, *refs):
+    pieces = devices // 4
+    q_refs = refs[:pieces]
+    weights = (refs[pieces : pieces + 2], refs[pieces + 2 : pieces + 4])
     lat_ref, rot_ref = refs[-2:]
-    out_refs = refs[4:-2]
+    out_refs = refs[pieces + 4 : -2]
     heads = weights[0][1].shape[0]
-    piece = jnp.concatenate([q_ref[...], far_ref[...]], axis=0)
+    piece = jnp.concatenate([ref[...].astype(jnp.float32) for ref in q_refs], axis=0)
+    piece = piece.astype(jnp.bfloat16)
     count = piece.shape[0]
     wide = 2 * count // devices * heads
     width = NOPE + ROPE
@@ -133,9 +137,9 @@
             )
 
 
-def project(near, far, weights, devices):
+def project(pieces, weights, devices):
     heads = weights[1].shape[0]
-    count = 2 * near.shape[0]
+    count = len(pieces) * pieces[0].shape[0]
     wide = 2 * count // devices * heads
     scratch = [
         pltpu.VMEM((2 * PIECES, count * heads, LANES), jnp.float32),
@@ -143,7 +147,7 @@
     ]
     out = [shape(2, PIECES * wide + wide // 2, LANES)] * (devices // 2)
     kernel = functools.partial(project_kernel, devices)
-    return call(kernel, out, 20, "project", scratch)(near, far, *[resident(w) for w in weights])
+    return call(kernel, out, 20, "project", scratch)(*pieces, *[resident(w) for w in weights])
 
 
 def attend_kernel(chips, len_ref, cos_ref, sin_ref, key_ref, new_ref, *refs):
@@ -253,16 +257,11 @@
 
 def terms_kernel(start, val_ref, wo_ref, mine_ref, other_ref):
     half, width = mine_ref.shape
-
-    def step(index, carry):
-        here = pl.ds(pl.multiple_of(index * BLOCK, BLOCK), BLOCK)
-        there = pl.ds(pl.multiple_of(start + index * BLOCK, BLOCK), BLOCK)
-        terms = jnp.dot(val_ref[...], wo_ref[:, there], preferred_element_type=jnp.float32)
-        mine_ref[:, here] = terms[:half]
-        other_ref[:, here] = terms[half:].astype(jnp.bfloat16)
-        return carry
-
-    lax.fori_loop(0, width // BLOCK, step, 0)
+    terms = jnp.dot(
+        val_ref[...], wo_ref[:, start : start + width], preferred_element_type=jnp.float32
+    )
+    mine_ref[...] = terms[:half]
+    other_ref[...] = terms[half:].astype(jnp.bfloat16)
 
 
 def output_terms(values, w_o, part):
@@ -273,25 +272,56 @@
     return call(kernel, out, 6, "terms")(values, resident(w_o))
 
 
-def core_sum_kernel(keep, give, mine_ref, other_ref, keep_ref, give_ref):
-    rows = keep_ref.shape[0] // len(keep)
+def far_z(devices):
+    return [z for z in far_first(devices, Z1) if z > Z1]
+
+
+def places(devices, chips):
+    order = far_first(devices, 2)
+    return [order.index(k) for k in chips]
+
+
+def pick(total, rows, where):
+    return jnp.concatenate([total[j * rows : (j + 1) * rows] for j in where], axis=0)
+
+
+def first_sum_kernel(rows, keep, give, near, mine_ref, other_ref, keep_ref, give_ref, near_ref):
     total = mine_ref[...] + other_ref[...].astype(jnp.float32)
-    for out_ref, places in ((keep_ref, keep), (give_ref, give)):
-        blocks = [total[j * rows : (j + 1) * rows] for j in places]
-        out_ref[...] = jnp.concatenate(blocks, axis=0).astype(out_ref.dtype)
-
-
-def core_sum(mine, other, devices):
+    keep_ref[...] = pick(total, rows, keep)
+    give_ref[...] = pick(total, rows, give).astype(give_ref.dtype)
+    near_ref[...] = pick(total, rows, near)
+
+
+def last_part_kernel(rows, keep, give, near, mine_ref, other_ref, before_ref, *out_refs):
+    keep_ref, give_ref, local_ref, pair_ref = out_refs
+    total = mine_ref[...] + other_ref[...].astype(jnp.float32)
+    keep_ref[...] = pick(total, rows, keep)
+    give_ref[...] = pick(total, rows, give).astype(give_ref.dtype)
+    here = pick(total, rows, near)
+    half, width = local_ref.shape[0], before_ref.shape[1]
+    for columns, block in ((slice(0, width), before_ref[...]), (slice(width, None), here)):
+        local_ref[:, columns] = block[:half]
+        pair_ref[:, columns] = block[half:].astype(pair_ref.dtype)
+
+
+def core_sum(mine, other, before, rows, devices):
     count, width = mine.shape
-    order = far_first(devices, 2)
-    zs = far_first(devices, 4)
-    keep = [order.index(z) for z in zs]
-    give = [order.index(z + 2) for z in zs]
-    out = (shape(count // 2, width, dtype=jnp.float32), shape(count // 2, width))
-    return call(functools.partial(core_sum_kernel, keep, give), out, 1, "core_sum")(mine, other)
-
-
-def chip_sum_kernel(*refs):
+    keep = places(devices, far_z(devices))
+    give = places(devices, [z + Y for z in far_z(devices)])
+    near = places(devices, [0, Y, Z1, Z1 + Y])
+    far = len(keep) * rows
+    out = (shape(far, width, dtype=jnp.float32), shape(far, width))
+    if before is None:
+        kernel = functools.partial(first_sum_kernel, rows, keep, give, near)
+        out += (shape(4 * rows, width, dtype=jnp.float32),)
+        return call(kernel, out, 1, "core_sum")(mine, other)
+    kernel = functools.partial(last_part_kernel, rows, keep, give, near)
+    full = before.shape[1] + width
+    out += (shape(2 * rows, full, dtype=jnp.float32), shape(2 * rows, full))
+    return call(kernel, out, 1, "core_sum")(mine, other, before)
+
+
+def far_sum_kernel(*refs):
     mine_refs = refs[:PARTS]
     other_refs = refs[PARTS : 2 * PARTS]
     out_refs = refs[2 * PARTS :]
@@ -305,11 +335,23 @@
             )
 
 
-def chip_sum(mine, other, rows):
+def far_sum(mine, other, rows):
     count, width = mine[0].shape
-    width *= PARTS
-    out = [shape(rows, width)] * (count // rows - 1) + [shape(rows, width, dtype=jnp.float32)]
-    return call(chip_sum_kernel, out, 1, "chip_sum")(*mine, *other)
+    out = [shape(rows, PARTS * width)] * (count // rows)
+    return call(far_sum_kernel, out, 1, "far_sum")(*mine, *other)
+
+
+def near_sum_kernel(mine_ref, other_ref, keep_ref, give_ref):
+    total = mine_ref[...] + other_ref[...].astype(jnp.float32)
+    rows = keep_ref.shape[0]
+    keep_ref[...] = total[:rows]
+    give_ref[...] = total[rows:].astype(give_ref.dtype)
+
+
+def near_sum(mine, other):
+    rows, width = mine.shape[0] // 2, mine.shape[1]
+    out = (shape(rows, width, dtype=jnp.float32), shape(rows, width))
+    return call(near_sum_kernel, out, 1, "near_sum")(mine, other)
 
 
 def last_sum_kernel(*refs):
@@ -334,21 +376,23 @@
         return lax.ppermute(block, "row", [(i, i ^ k) for i in range(devices)])
 
     far_weights = [swap(w_uq, 1), swap(w_uk, 1)]
-    tables, near = join(rotary(lengths), [swap(q_latent, z) for z in zs])
-    messages = project(near, swap(near, 2), [w_uq, w_uk, *far_weights], devices)
+    tables, near = join(rotary(lengths), [q_latent, swap(q_latent, 2)])
+    messages = project([swap(near, z) for z in zs], [w_uq, w_uk, *far_weights], devices)
     messages = [swap(block, k) for k, block in zip(order, messages)]
     keys = jnp.swapaxes(cache, 1, 2)
     latents = attend(lengths, tables, keys, new_latent, messages, heads)
     latents = [swap(block, k) for k, block in zip(order, latents)]
     values = head_values(latents, swap(regroup(latents), 1), w_uv)
-    keep, got = [], []
+    keep, got, near = [], [], None
     for part in range(PARTS):
         mine, other = output_terms(values, w_o, part)
-        mine, other = core_sum(mine, swap(other, 1), devices)
-        keep.append(mine)
-        got.append(swap(other, 2))
-    blocks = chip_sum(keep, got, rows)
-    return last_sum([swap(block, z) for z, block in zip(zs, blocks)])
+        far_mine, far_other, near, *pair = core_sum(mine, swap(other, 1), near, rows, devices)
+        keep.append(far_mine)
+        got.append(swap(far_other, Y))
+    local, across = near_sum(near, swap(pair[0], Z1))
+    far = far_sum(keep, got, rows)
+    far = [swap(block, z) for z, block in zip(far_z(devices), far)]
+    return last_sum([local, swap(across, Y), *far])
 
 
 def solution(mesh):

time: 77.6 us -> 74 us (0.954)
  waiting for transfers between devices: 27.2 us -> 24 us
  Pallas kernels: 13.6 us -> 12.1 us
  starting transfers between devices: 35.6 us -> 36.7 us
    ppermute x28 -> x29, waiting for transfers between devices: 27.2 us -> 24 us  [swap(): return lax.ppermute(block, 'row', [(i, i ^ k) for i in range(devices)])]
    pallas_call x12 -> x13, Pallas kernels: 13.6 us -> 12.1 us  [run(): pl.pallas_call(kernel, out_shape=out_shape, in_specs=smem + [in_vmem()] *...]
    ppermute x28 -> x29, starting transfers between devices: 35.6 us -> 36.7 us  [swap(): return lax.ppermute(block, 'row', [(i, i ^ k) for i in range(devices)])]
  transfers between devices with their start and end apart: 28 -> 29, of which waited for: 16 -> 16; matrix products, arithmetic and copies ran while one was open for 0% -> 0% of each run, Pallas kernels for 4% -> 3%
where the time goes in v7:
time: 74 us; the launch traced here: 73.8 us
  starting transfers between devices  36.7 us (50%)
  waiting for transfers between devices  24 us (32%)
  Pallas kernels  12.1 us (16%)
    ppermute x29, starting transfers between devices, swap(): return lax.ppermute(block, 'row', [(i, i ^ k) for i in range(devices)])  36.7 us
    ppermute x29, waiting for transfers between devices, swap(): return lax.ppermute(block, 'row', [(i, i ^ k) for i in range(devices)])  24 us
    pallas_call x13, Pallas kernels, run(): pl.pallas_call(kernel, out_shape=out_shape, in_specs=smem + [in_vmem()] *...  12.1 us
  transfers between devices with their start and end apart: 29, of which 16 were waited for; matrix products, arithmetic and copies ran while one was open for 0% of the time, Pallas kernels for 3%

profile of v7, /device:TPU:0, one launch (start us, length us, event | category | flops | bytes accessed | tf_op | source)
XLA Modules:
  0.0 73.8 jit_solution(13923380532915113766)
XLA Ops:
  0.5 3.0 %collective-permute-start = (bf16[4,1536]{1,0:T(4,128)(2,1)}, bf16[4,1536]{1,0:T(4,128)(2,1)S(1)}, u32[]{:S(2)}, u32[]{:S(2)}) collective-permute-start(bf16[4,1536]{1,0:T(4,128)(2,1)} %refs_0_.1), channel_id=1, source_target_pairs={{0,2},{1,3},{2,0},{3,1},{4,6},{5,7},{6,4},{7,5},{8,10},{9,11},{10,... | collective-permute-start | bytes 36872 | tf_op jit(solution)/shard_map/ppermute | solution.py:376
  5.4 2.1 %collective-permute-start.3 = (bf16[8,1536]{1,0:T(8,128)(2,1)S(1)}, bf16[8,1536]{1,0:T(8,128)(2,1)S(1)}, u32[]{:S(2)}, u32[]{:S(2)}) collective-permute-start(bf16[8,1536]{1,0:T(8,128)(2,1)S(1)} %get-tuple-element.45.refs_3_), channel_id=1, source_target_pairs={{0,4},{1,5},{2,6},{3,7},{4,0},{5,1},{6,2},{7,3},{8,12},{9,13},{10,... | collective-permute-start | bytes 73736 | tf_op jit(solution)/shard_map/ppermute | solution.py:376
  7.6 2.5 %collective-permute-start.2 = (bf16[8,1536]{1,0:T(8,128)(2,1)S(1)}, bf16[8,1536]{1,0:T(8,128)(2,1)S(1)}, u32[]{:S(2)}, u32[]{:S(2)}) collective-permute-start(bf16[8,1536]{1,0:T(8,128)(2,1)S(1)} %get-tuple-element.45.refs_3_), channel_id=1, source_target_pairs={{0,12},{1,13},{2,14},{3,15},{4,8},{5,9},{6,10},{7,11},{8,4},{9,5},... | collective-permute-start | bytes 73736 | tf_op jit(solution)/shard_map/ppermute | solution.py:376
  10.2 3.0 %collective-permute-done.2.refs_1_ = bf16[8,1536]{1,0:T(8,128)(2,1)S(1)} collective-permute-done((bf16[8,1536]{1,0:T(8,128)(2,1)S(1)}, bf16[8,1536]{1,0:T(8,128)(2,1)S(1)}, u32[]{:S(2)}, u32[]{:S(2)}) %collective-permute-start.2) | collective-permute-done | bytes 24608 | tf_op jit(solution)/shard_map/ppermute | solution.py:376
  13.2 1.8 %collective-permute-done.1.refs_0_ = bf16[8,1536]{1,0:T(8,128)(2,1)S(1)} collective-permute-done((bf16[8,1536]{1,0:T(8,128)(2,1)S(1)}, bf16[8,1536]{1,0:T(8,128)(2,1)S(1)}, u32[]{:S(2)}, u32[]{:S(2)}) %collective-permute-start.1) | collective-permute-done | bytes 24608 | tf_op jit(solution)/shard_map/ppermute | solution.py:376
  15.1 2.3 %project.1 = (bf16[2,144,128]{2,1,0:T(8,128)(2,1)S(1)}, bf16[2,144,128]{2,1,0:T(8,128)(2,1)S(1)}, bf16[2,144,128]{2,1,0:T(8,128)(2,1)S(1)}, bf16[2,144,128]{2,1,...) custom-call(bf16[8,1536]{1,0:T(8,128)(2,1)S(1)} %collective-permute-, ...), custom_call_target="tpu_custom_call" | custom-call | flops 23000000512 | tf_op jit(solution)/shard_map/project/pallas_call | solution.py:36
  17.5 3.9 %collective-permute-start.7 = (bf16[2,144,128]{2,1,0:T(8,128)(2,1)S(1)}, bf16[2,144,128]{2,1,0:T(8,128)(2,1)S(1)}, u32[]{:S(2)}, u32[]{:S(2)}) collective-permute-start(bf16[2,144,128]{2,1,0:T(8,128)(2,1)S(1)} %get-tuple-element.47), channel_id=1, source_target_pairs={{0,10},{1,11},{2,8},{3,9},{4,14},{5,15},{6,12},{7,13},{8,2},{9,3},... | collective-permute-start | bytes 221192 | tf_op jit(solution)/shard_map/ppermute | solution.py:376
  21.3 1.2 %collective-permute-start.8 = (bf16[2,144,128]{2,1,0:T(8,128)(2,1)S(1)}, bf16[2,144,128]{2,1,0:T(8,128)(2,1)S(1)}, u32[]{:S(2)}, u32[]{:S(2)}) collective-permute-start(bf16[2,144,128]{2,1,0:T(8,128)(2,1)S(1)} %get-tuple-element.48), channel_id=1, source_target_pairs={{0,12},{1,13},{2,14},{3,15},{4,8},{5,9},{6,10},{7,11},{8,4},{9,5},... | collective-permute-start | bytes 221192 | tf_op jit(solution)/shard_map/ppermute | solution.py:376
  22.5 2.6 %collective-permute-start.9 = (bf16[2,144,128]{2,1,0:T(8,128)(2,1)S(1)}, bf16[2,144,128]{2,1,0:T(8,128)(2,1)S(1)}, u32[]{:S(2)}, u32[]{:S(2)}) collective-permute-start(bf16[2,144,128]{2,1,0:T(8,128)(2,1)S(1)} %get-tuple-element.49), channel_id=1, source_target_pairs={{0,14},{1,15},{2,12},{3,13},{4,10},{5,11},{6,8},{7,9},{8,6},{9,7},... | collective-permute-start | bytes 221192 | tf_op jit(solution)/shard_map/ppermute | solution.py:376
  25.1 2.6 %collective-permute-done.6.refs_0_ = bf16[2,144,128]{2,1,0:T(8,128)(2,1)S(1)} collective-permute-done((bf16[2,144,128]{2,1,0:T(8,128)(2,1)S(1)}, bf16[2,144,128]{2,1,0:T(8,128)(2,1)S(1)}, u32[]{:S(2)}, u32[]{:S(2)}) %collective-permute-start.6) | collective-permute-done | bytes 73760 | tf_op jit(solution)/shard_map/ppermute | solution.py:376
  28.1 2.0 %collective-permute-done.7.refs_1_ = bf16[2,144,128]{2,1,0:T(8,128)(2,1)S(1)} collective-permute-done((bf16[2,144,128]{2,1,0:T(8,128)(2,1)S(1)}, bf16[2,144,128]{2,1,0:T(8,128)(2,1)S(1)}, u32[]{:S(2)}, u32[]{:S(2)}) %collective-permute-start.7) | collective-permute-done | bytes 73760 | tf_op jit(solution)/shard_map/ppermute | solution.py:376
  30.1 1.2 %collective-permute-start.12 = (bf16[2,144,128]{2,1,0:T(8,128)(2,1)S(1)}, bf16[2,144,128]{2,1,0:T(8,128)(2,1)S(1)}, u32[]{:S(2)}, u32[]{:S(2)}) collective-permute-start(bf16[2,144,128]{2,1,0:T(8,128)(2,1)S(1)} %get-tuple-element.52), channel_id=1, source_target_pairs={{0,2},{1,3},{2,0},{3,1},{4,6},{5,7},{6,4},{7,5},{8,10},{9,11},{10,... | collective-permute-start | bytes 221192 | tf_op jit(solution)/shard_map/ppermute | solution.py:376
  31.3 1.6 %collective-permute-done.11.refs_5_ = bf16[2,144,128]{2,1,0:T(8,128)(2,1)S(1)} collective-permute-done((bf16[2,144,128]{2,1,0:T(8,128)(2,1)S(1)}, bf16[2,144,128]{2,1,0:T(8,128)(2,1)S(1)}, u32[]{:S(2)}, u32[]{:S(2)}) %collective-permute-start.11) | collective-permute-done | bytes 73760 | tf_op jit(solution)/shard_map/ppermute | solution.py:376
  33.0 1.5 %collective-permute-done.12.refs_6_ = bf16[2,144,128]{2,1,0:T(8,128)(2,1)S(1)} collective-permute-done((bf16[2,144,128]{2,1,0:T(8,128)(2,1)S(1)}, bf16[2,144,128]{2,1,0:T(8,128)(2,1)S(1)}, u32[]{:S(2)}, u32[]{:S(2)}) %collective-permute-start.12) | collective-permute-done | bytes 73760 | tf_op jit(solution)/shard_map/ppermute | solution.py:376
  34.5 5.1 %attend.1 = (bf16[2,32,512]{2,1,0:T(8,128)(2,1)S(1)}, bf16[2,32,512]{2,1,0:T(8,128)(2,1)S(1)}, bf16[2,32,512]{2,1,0:T(8,128)(2,1)S(1)}, bf16[2,32,512]{2,1,0:T(8...) custom-call(s32[4]{0:T(128)S(1)} %copy-done.5, ...), custom_call_target="tpu_custom_call" | custom-call | flops 11500000256 | tf_op jit(solution)/shard_map/attend/pallas_call | solution.py:36
  39.8 3.6 %collective-permute-start.14 = (bf16[2,32,512]{2,1,0:T(8,128)(2,1)S(1)}, bf16[2,32,512]{2,1,0:T(8,128)(2,1)S(1)}, u32[]{:S(2)}, u32[]{:S(2)}) collective-permute-start(bf16[2,32,512]{2,1,0:T(8,128)(2,1)S(1)} %get-tuple-element.55), channel_id=1, source_target_pairs={{0,10},{1,11},{2,8},{3,9},{4,14},{5,15},{6,12},{7,13},{8,2},{9,3},... | collective-permute-start | bytes 196616 | tf_op jit(solution)/shard_map/ppermute | solution.py:376
  43.3 1.7 %collective-permute-start.15 = (bf16[2,32,512]{2,1,0:T(8,128)(2,1)S(1)}, bf16[2,32,512]{2,1,0:T(8,128)(2,1)S(1)}, u32[]{:S(2)}, u32[]{:S(2)}) collective-permute-start(bf16[2,32,512]{2,1,0:T(8,128)(2,1)S(1)} %get-tuple-element.56), channel_id=1, source_target_pairs={{0,12},{1,13},{2,14},{3,15},{4,8},{5,9},{6,10},{7,11},{8,4},{9,5},... | collective-permute-start | bytes 196616 | tf_op jit(solution)/shard_map/ppermute | solution.py:376
  45.0 2.4 %collective-permute-start.16 = (bf16[2,32,512]{2,1,0:T(8,128)(2,1)S(1)}, bf16[2,32,512]{2,1,0:T(8,128)(2,1)S(1)}, u32[]{:S(2)}, u32[]{:S(2)}) collective-permute-start(bf16[2,32,512]{2,1,0:T(8,128)(2,1)S(1)} %get-tuple-element.57), channel_id=1, source_target_pairs={{0,14},{1,15},{2,12},{3,13},{4,10},{5,11},{6,8},{7,9},{8,6},{9,7},... | collective-permute-start | bytes 196616 | tf_op jit(solution)/shard_map/ppermute | solution.py:376
  47.4 2.7 %collective-permute-start.18 = (bf16[2,32,512]{2,1,0:T(8,128)(2,1)S(1)}, bf16[2,32,512]{2,1,0:T(8,128)(2,1)S(1)}, u32[]{:S(2)}, u32[]{:S(2)}) collective-permute-start(bf16[2,32,512]{2,1,0:T(8,128)(2,1)S(1)} %get-tuple-element.59), channel_id=1, source_target_pairs={{0,6},{1,7},{2,4},{3,5},{4,2},{5,3},{6,0},{7,1},{8,14},{9,15},{10,... | collective-permute-start | bytes 196616 | tf_op jit(solution)/shard_map/ppermute | solution.py:376
  50.9 1.1 %collective-permute-done.16.refs_3_ = bf16[2,32,512]{2,1,0:T(8,128)(2,1)S(1)} collective-permute-done((bf16[2,32,512]{2,1,0:T(8,128)(2,1)S(1)}, bf16[2,32,512]{2,1,0:T(8,128)(2,1)S(1)}, u32[]{:S(2)}, u32[]{:S(2)}) %collective-permute-start.16) | collective-permute-done | bytes 65568 | tf_op jit(solution)/shard_map/ppermute | solution.py:376
  52.0 1.4 %collective-permute-done.18.refs_5_ = bf16[2,32,512]{2,1,0:T(8,128)(2,1)S(1)} collective-permute-done((bf16[2,32,512]{2,1,0:T(8,128)(2,1)S(1)}, bf16[2,32,512]{2,1,0:T(8,128)(2,1)S(1)}, u32[]{:S(2)}, u32[]{:S(2)}) %collective-permute-start.18) | collective-permute-done | bytes 65568 | tf_op jit(solution)/shard_map/ppermute | solution.py:376
  53.4 1.0 %collective-permute-done.19.refs_6_ = bf16[2,32,512]{2,1,0:T(8,128)(2,1)S(1)} collective-permute-done((bf16[2,32,512]{2,1,0:T(8,128)(2,1)S(1)}, bf16[2,32,512]{2,1,0:T(8,128)(2,1)S(1)}, u32[]{:S(2)}, u32[]{:S(2)}) %collective-permute-start.19) | collective-permute-done | bytes 65568 | tf_op jit(solution)/shard_map/ppermute | solution.py:376
  54.5 1.5 %collective-permute-done.20.refs_8_ = bf16[8,32,512]{2,1,0:T(8,128)(2,1)S(1)} collective-permute-done((bf16[8,32,512]{2,1,0:T(8,128)(2,1)S(1)}, bf16[8,32,512]{2,1,0:T(8,128)(2,1)S(1)}, u32[]{:S(2)}, u32[]{:S(2)}) %collective-permute-start.20) | collective-permute-done | bytes 262176 | tf_op jit(solution)/shard_map/ppermute | solution.py:376
  56.5 1.4 %terms.3 = (f32[32,3584]{1,0:T(8,128)S(1)}, bf16[32,3584]{1,0:T(8,128)(2,1)S(1)}) custom-call(bf16[64,1024]{1,0:T(8,128)(2,1)S(1)} %values.1.val_ref, bf16[1024,7168]{1,0:T(8,128)(2,1)S(1)} %bitcast.2), custom_call_target="tpu_custom_call" | custom-call | flops 6899999744 | tf_op jit(solution)/shard_map/terms/pallas_call | solution.py:36
  58.1 1.4 %terms.2 = (f32[32,3584]{1,0:T(8,128)S(1)}, bf16[32,3584]{1,0:T(8,128)(2,1)S(1)}) custom-call(bf16[64,1024]{1,0:T(8,128)(2,1)S(1)} %values.1.val_ref, bf16[1024,7168]{1,0:T(8,128)(2,1)S(1)} %bitcast.2), custom_call_target="tpu_custom_call" | custom-call | flops 6899999744 | tf_op jit(solution)/shard_map/terms/pallas_call | solution.py:36
  61.1 1.1 %collective-permute-start.26 = (bf16[8,3584]{1,0:T(8,128)(2,1)S(1)}, bf16[8,3584]{1,0:T(8,128)(2,1)S(1)}, u32[]{:S(2)}, u32[]{:S(2)}) collective-permute-start(bf16[8,3584]{1,0:T(8,128)(2,1)S(1)} %get-tuple-element.74), channel_id=1, source_target_pairs={{0,2},{1,3},{2,0},{3,1},{4,6},{5,7},{6,4},{7,5},{8,10},{9,11},{10,... | collective-permute-start | bytes 172040 | tf_op jit(solution)/shard_map/ppermute | solution.py:376
  62.2 0.9 %collective-permute-start.23 = (bf16[8,7168]{1,0:T(8,128)(2,1)S(1)}, bf16[8,7168]{1,0:T(8,128)(2,1)S(1)}, u32[]{:S(2)}, u32[]{:S(2)}) collective-permute-start(bf16[8,7168]{1,0:T(8,128)(2,1)S(1)} %get-tuple-element.68), channel_id=1, source_target_pairs={{0,4},{1,5},{2,6},{3,7},{4,0},{5,1},{6,2},{7,3},{8,12},{9,13},{10,... | collective-permute-start | bytes 344072 | tf_op jit(solution)/shard_map/ppermute | solution.py:376
  63.1 1.2 %collective-permute-done.25.refs_2_ = bf16[8,3584]{1,0:T(8,128)(2,1)S(1)} collective-permute-done((bf16[8,3584]{1,0:T(8,128)(2,1)S(1)}, bf16[8,3584]{1,0:T(8,128)(2,1)S(1)}, u32[]{:S(2)}, u32[]{:S(2)}) %collective-permute-start.25) | collective-permute-done | bytes 57376 | tf_op jit(solution)/shard_map/ppermute | solution.py:376
  64.4 1.1 %collective-permute-done.26.refs_3_ = bf16[8,3584]{1,0:T(8,128)(2,1)S(1)} collective-permute-done((bf16[8,3584]{1,0:T(8,128)(2,1)S(1)}, bf16[8,3584]{1,0:T(8,128)(2,1)S(1)}, u32[]{:S(2)}, u32[]{:S(2)}) %collective-permute-start.26) | collective-permute-done | bytes 57376 | tf_op jit(solution)/shard_map/ppermute | solution.py:376
  66.1 2.7 %collective-permute-start.28 = (bf16[4,7168]{1,0:T(4,128)(2,1)S(1)}, bf16[4,7168]{1,0:T(4,128)(2,1)S(1)}, u32[]{:S(2)}, u32[]{:S(2)}) collective-permute-start(bf16[4,7168]{1,0:T(4,128)(2,1)S(1)} %get-tuple-element.76), channel_id=1, source_target_pairs={{0,12},{1,13},{2,14},{3,15},{4,8},{5,9},{6,10},{7,11},{8,4},{9,5},... | collective-permute-start | bytes 172040 | tf_op jit(solution)/shard_map/ppermute | solution.py:376
  68.9 1.0 %collective-permute-start.24 = (bf16[4,7168]{1,0:T(4,128)(2,1)S(1)}, bf16[4,7168]{1,0:T(4,128)(2,1)S(1)}, u32[]{:S(2)}, u32[]{:S(2)}) collective-permute-start(bf16[4,7168]{1,0:T(4,128)(2,1)S(1)} %get-tuple-element.70), channel_id=1, source_target_pairs={{0,2},{1,3},{2,0},{3,1},{4,6},{5,7},{6,4},{7,5},{8,10},{9,11},{10,... | collective-permute-start | bytes 172040 | tf_op jit(solution)/shard_map/ppermute | solution.py:376
  69.9 3.0 %collective-permute-done.27.refs_2_ = bf16[4,7168]{1,0:T(4,128)(2,1)S(1)} collective-permute-done((bf16[4,7168]{1,0:T(4,128)(2,1)S(1)}, bf16[4,7168]{1,0:T(4,128)(2,1)S(1)}, u32[]{:S(2)}, u32[]{:S(2)}) %collective-permute-start.27) | collective-permute-done | bytes 57376 | tf_op jit(solution)/shard_map/ppermute | solution.py:376
  (70 shorter events, 7.9 us)
Async XLA Ops:
  0.0 15.0 %collective-permute-start.4 = (bf16[1536,1536]{1,0:T(8,128)(2,1)}, bf16[1536,1536]{1,0:T(8,128)(2,1)S(1)}, u32[]{:S(2)}, u32[]{:S(2)}) collective-permute-start(bf16[1536,1536]{1,0:T(8,128)(2,1)} %refs_4_.1), channel_id=1, source_target_pairs={{0,1},{1,0},{2,3},{3,2},{4,5},{5,4},{6,7},{7,6},{8,9},{9,8},{10,11... | collective-permute-start | bytes 14155784 | tf_op jit(solution)/shard_map/ppermute | solution.py:376
  0.5 14.6 %collective-permute-start.5 = (bf16[8,128,512]{2,1,0:T(8,128)(2,1)}, bf16[8,128,512]{2,1,0:T(8,128)(2,1)S(1)}, u32[]{:S(2)}, u32[]{:S(2)}) collective-permute-start(bf16[8,128,512]{2,1,0:T(8,128)(2,1)} %refs_5_.1), channel_id=1, source_target_pairs={{0,1},{1,0},{2,3},{3,2},{4,5},{5,4},{6,7},{7,6},{8,9},{9,8},{10,11... | collective-permute-start | bytes 3145736 | tf_op jit(solution)/shard_map/ppermute | solution.py:376
  0.5 4.8 %collective-permute-start = (bf16[4,1536]{1,0:T(4,128)(2,1)}, bf16[4,1536]{1,0:T(4,128)(2,1)S(1)}, u32[]{:S(2)}, u32[]{:S(2)}) collective-permute-start(bf16[4,1536]{1,0:T(4,128)(2,1)} %refs_0_.1), channel_id=1, source_target_pairs={{0,2},{1,3},{2,0},{3,1},{4,6},{5,7},{6,4},{7,5},{8,10},{9,11},{10,... | collective-permute-start | bytes 36872 | tf_op jit(solution)/shard_map/ppermute | solution.py:376
  5.4 29.1 %slice-start.4 = ((s8[7077888]{0:T(1024)(128)(4,1)}), s8[4194304]{0:T(1024)(128)(4,1)S(1)}, s32[]{:S(2)}) async-start(s8[7077888]{0:T(1024)(128)(4,1)} %bitcast.3), calls=%async_computation.4 | async-start | bytes 8388608
  5.4 29.1 %slice-start.5 = ((s8[7077888]{0:T(1024)(128)(4,1)}), s8[2883584]{0:T(1024)(128)(4,1)S(1)}, s32[]{:S(2)}) async-start(s8[7077888]{0:T(1024)(128)(4,1)} %bitcast.3), calls=%async_computation.5 | async-start | bytes 5767168
  5.4 29.1 %copy-start.3 = (bf16[4,576]{1,0:T(4,128)(2,1)S(1)}, bf16[4,576]{1,0:T(4,128)(2,1)}, u32[]{:S(2)}) copy-start(bf16[4,576]{1,0:T(4,128)(2,1)} %new_ref.1) | copy-start | bytes 13828
  5.4 4.7 %collective-permute-start.3 = (bf16[8,1536]{1,0:T(8,128)(2,1)S(1)}, bf16[8,1536]{1,0:T(8,128)(2,1)S(1)}, u32[]{:S(2)}, u32[]{:S(2)}) collective-permute-start(bf16[8,1536]{1,0:T(8,128)(2,1)S(1)} %get-tuple-element.45.refs_3_), channel_id=1, source_target_pairs={{0,4},{1,5},{2,6},{3,7},{4,0},{5,1},{6,2},{7,3},{8,12},{9,13},{10,... | collective-permute-start | bytes 73736 | tf_op jit(solution)/shard_map/ppermute | solution.py:376
  7.6 5.6 %collective-permute-start.2 = (bf16[8,1536]{1,0:T(8,128)(2,1)S(1)}, bf16[8,1536]{1,0:T(8,128)(2,1)S(1)}, u32[]{:S(2)}, u32[]{:S(2)}) collective-permute-start(bf16[8,1536]{1,0:T(8,128)(2,1)S(1)} %get-tuple-element.45.refs_3_), channel_id=1, source_target_pairs={{0,12},{1,13},{2,14},{3,15},{4,8},{5,9},{6,10},{7,11},{8,4},{9,5},... | collective-permute-start | bytes 73736 | tf_op jit(solution)/shard_map/ppermute | solution.py:376
  10.1 5.0 %collective-permute-start.1 = (bf16[8,1536]{1,0:T(8,128)(2,1)S(1)}, bf16[8,1536]{1,0:T(8,128)(2,1)S(1)}, u32[]{:S(2)}, u32[]{:S(2)}) collective-permute-start(bf16[8,1536]{1,0:T(8,128)(2,1)S(1)} %get-tuple-element.45.refs_3_), channel_id=1, source_target_pairs={{0,8},{1,9},{2,10},{3,11},{4,12},{5,13},{6,14},{7,15},{8,0},{9,1},... | collective-permute-start | bytes 73736 | tf_op jit(solution)/shard_map/ppermute | solution.py:376
  17.4 10.4 %collective-permute-start.6 = (bf16[2,144,128]{2,1,0:T(8,128)(2,1)S(1)}, bf16[2,144,128]{2,1,0:T(8,128)(2,1)S(1)}, u32[]{:S(2)}, u32[]{:S(2)}) collective-permute-start(bf16[2,144,128]{2,1,0:T(8,128)(2,1)S(1)} %get-tuple-element.46), channel_id=1, source_target_pairs={{0,8},{1,9},{2,10},{3,11},{4,12},{5,13},{6,14},{7,15},{8,0},{9,1},... | collective-permute-start | bytes 221192 | tf_op jit(solution)/shard_map/ppermute | solution.py:376
  17.5 12.7 %collective-permute-start.7 = (bf16[2,144,128]{2,1,0:T(8,128)(2,1)S(1)}, bf16[2,144,128]{2,1,0:T(8,128)(2,1)S(1)}, u32[]{:S(2)}, u32[]{:S(2)}) collective-permute-start(bf16[2,144,128]{2,1,0:T(8,128)(2,1)S(1)} %get-tuple-element.47), channel_id=1, source_target_pairs={{0,10},{1,11},{2,8},{3,9},{4,14},{5,15},{6,12},{7,13},{8,2},{9,3},... | collective-permute-start | bytes 221192 | tf_op jit(solution)/shard_map/ppermute | solution.py:376
  21.3 10.0 %collective-permute-start.8 = (bf16[2,144,128]{2,1,0:T(8,128)(2,1)S(1)}, bf16[2,144,128]{2,1,0:T(8,128)(2,1)S(1)}, u32[]{:S(2)}, u32[]{:S(2)}) collective-permute-start(bf16[2,144,128]{2,1,0:T(8,128)(2,1)S(1)} %get-tuple-element.48), channel_id=1, source_target_pairs={{0,12},{1,13},{2,14},{3,15},{4,8},{5,9},{6,10},{7,11},{8,4},{9,5},... | collective-permute-start | bytes 221192 | tf_op jit(solution)/shard_map/ppermute | solution.py:376
  22.5 8.9 %collective-permute-start.9 = (bf16[2,144,128]{2,1,0:T(8,128)(2,1)S(1)}, bf16[2,144,128]{2,1,0:T(8,128)(2,1)S(1)}, u32[]{:S(2)}, u32[]{:S(2)}) collective-permute-start(bf16[2,144,128]{2,1,0:T(8,128)(2,1)S(1)} %get-tuple-element.49), channel_id=1, source_target_pairs={{0,14},{1,15},{2,12},{3,13},{4,10},{5,11},{6,8},{7,9},{8,6},{9,7},... | collective-permute-start | bytes 221192 | tf_op jit(solution)/shard_map/ppermute | solution.py:376
  25.1 6.2 %collective-permute-start.10 = (bf16[2,144,128]{2,1,0:T(8,128)(2,1)S(1)}, bf16[2,144,128]{2,1,0:T(8,128)(2,1)S(1)}, u32[]{:S(2)}, u32[]{:S(2)}) collective-permute-start(bf16[2,144,128]{2,1,0:T(8,128)(2,1)S(1)} %get-tuple-element.50), channel_id=1, source_target_pairs={{0,4},{1,5},{2,6},{3,7},{4,0},{5,1},{6,2},{7,3},{8,12},{9,13},{10,... | collective-permute-start | bytes 221192 | tf_op jit(solution)/shard_map/ppermute | solution.py:376
  27.7 5.3 %collective-permute-start.11 = (bf16[2,144,128]{2,1,0:T(8,128)(2,1)S(1)}, bf16[2,144,128]{2,1,0:T(8,128)(2,1)S(1)}, u32[]{:S(2)}, u32[]{:S(2)}) collective-permute-start(bf16[2,144,128]{2,1,0:T(8,128)(2,1)S(1)} %get-tuple-element.51), channel_id=1, source_target_pairs={{0,6},{1,7},{2,4},{3,5},{4,2},{5,3},{6,0},{7,1},{8,14},{9,15},{10,... | collective-permute-start | bytes 221192 | tf_op jit(solution)/shard_map/ppermute | solution.py:376
  30.1 4.4 %collective-permute-start.12 = (bf16[2,144,128]{2,1,0:T(8,128)(2,1)S(1)}, bf16[2,144,128]{2,1,0:T(8,128)(2,1)S(1)}, u32[]{:S(2)}, u32[]{:S(2)}) collective-permute-start(bf16[2,144,128]{2,1,0:T(8,128)(2,1)S(1)} %get-tuple-element.52), channel_id=1, source_target_pairs={{0,2},{1,3},{2,0},{3,1},{4,6},{5,7},{6,4},{7,5},{8,10},{9,11},{10,... | collective-permute-start | bytes 221192 | tf_op jit(solution)/shard_map/ppermute | solution.py:376
  39.7 7.7 %collective-permute-start.13 = (bf16[2,32,512]{2,1,0:T(8,128)(2,1)S(1)}, bf16[2,32,512]{2,1,0:T(8,128)(2,1)S(1)}, u32[]{:S(2)}, u32[]{:S(2)}) collective-permute-start(bf16[2,32,512]{2,1,0:T(8,128)(2,1)S(1)} %get-tuple-element.54), channel_id=1, source_target_pairs={{0,8},{1,9},{2,10},{3,11},{4,12},{5,13},{6,14},{7,15},{8,0},{9,1},... | collective-permute-start | bytes 196616 | tf_op jit(solution)/shard_map/ppermute | solution.py:376
  39.8 10.3 %collective-permute-start.14 = (bf16[2,32,512]{2,1,0:T(8,128)(2,1)S(1)}, bf16[2,32,512]{2,1,0:T(8,128)(2,1)S(1)}, u32[]{:S(2)}, u32[]{:S(2)}) collective-permute-start(bf16[2,32,512]{2,1,0:T(8,128)(2,1)S(1)} %get-tuple-element.55), channel_id=1, source_target_pairs={{0,10},{1,11},{2,8},{3,9},{4,14},{5,15},{6,12},{7,13},{8,2},{9,3},... | collective-permute-start | bytes 196616 | tf_op jit(solution)/shard_map/ppermute | solution.py:376
  43.3 7.6 %collective-permute-start.15 = (bf16[2,32,512]{2,1,0:T(8,128)(2,1)S(1)}, bf16[2,32,512]{2,1,0:T(8,128)(2,1)S(1)}, u32[]{:S(2)}, u32[]{:S(2)}) collective-permute-start(bf16[2,32,512]{2,1,0:T(8,128)(2,1)S(1)} %get-tuple-element.56), channel_id=1, source_target_pairs={{0,12},{1,13},{2,14},{3,15},{4,8},{5,9},{6,10},{7,11},{8,4},{9,5},... | collective-permute-start | bytes 196616 | tf_op jit(solution)/shard_map/ppermute | solution.py:376
  45.0 7.0 %collective-permute-start.16 = (bf16[2,32,512]{2,1,0:T(8,128)(2,1)S(1)}, bf16[2,32,512]{2,1,0:T(8,128)(2,1)S(1)}, u32[]{:S(2)}, u32[]{:S(2)}) collective-permute-start(bf16[2,32,512]{2,1,0:T(8,128)(2,1)S(1)} %get-tuple-element.57), channel_id=1, source_target_pairs={{0,14},{1,15},{2,12},{3,13},{4,10},{5,11},{6,8},{7,9},{8,6},{9,7},... | collective-permute-start | bytes 196616 | tf_op jit(solution)/shard_map/ppermute | solution.py:376
  47.4 4.6 %collective-permute-start.17 = (bf16[2,32,512]{2,1,0:T(8,128)(2,1)S(1)}, bf16[2,32,512]{2,1,0:T(8,128)(2,1)S(1)}, u32[]{:S(2)}, u32[]{:S(2)}) collective-permute-start(bf16[2,32,512]{2,1,0:T(8,128)(2,1)S(1)} %get-tuple-element.58), channel_id=1, source_target_pairs={{0,4},{1,5},{2,6},{3,7},{4,0},{5,1},{6,2},{7,3},{8,12},{9,13},{10,... | collective-permute-start | bytes 196616 | tf_op jit(solution)/shard_map/ppermute | solution.py:376
  47.4 6.0 %collective-permute-start.18 = (bf16[2,32,512]{2,1,0:T(8,128)(2,1)S(1)}, bf16[2,32,512]{2,1,0:T(8,128)(2,1)S(1)}, u32[]{:S(2)}, u32[]{:S(2)}) collective-permute-start(bf16[2,32,512]{2,1,0:T(8,128)(2,1)S(1)} %get-tuple-element.59), channel_id=1, source_target_pairs={{0,6},{1,7},{2,4},{3,5},{4,2},{5,3},{6,0},{7,1},{8,14},{9,15},{10,... | collective-permute-start | bytes 196616 | tf_op jit(solution)/shard_map/ppermute | solution.py:376
  50.1 4.3 %collective-permute-start.19 = (bf16[2,32,512]{2,1,0:T(8,128)(2,1)S(1)}, bf16[2,32,512]{2,1,0:T(8,128)(2,1)S(1)}, u32[]{:S(2)}, u32[]{:S(2)}) collective-permute-start(bf16[2,32,512]{2,1,0:T(8,128)(2,1)S(1)} %get-tuple-element.60), channel_id=1, source_target_pairs={{0,2},{1,3},{2,0},{3,1},{4,6},{5,7},{6,4},{7,5},{8,10},{9,11},{10,... | collective-permute-start | bytes 196616 | tf_op jit(solution)/shard_map/ppermute | solution.py:376
  54.4 1.6 %collective-permute-start.20 = (bf16[8,32,512]{2,1,0:T(8,128)(2,1)S(1)}, bf16[8,32,512]{2,1,0:T(8,128)(2,1)S(1)}, u32[]{:S(2)}, u32[]{:S(2)}) collective-permute-start(bf16[8,32,512]{2,1,0:T(8,128)(2,1)S(1)} %regroup.1), channel_id=1, source_target_pairs={{0,1},{1,0},{2,3},{3,2},{4,5},{5,4},{6,7},{7,6},{8,9},{9,8},{10,11... | collective-permute-start | bytes 786440 | tf_op jit(solution)/shard_map/ppermute | solution.py:376
  57.9 2.0 %collective-permute-start.22 = (bf16[32,3584]{1,0:T(8,128)(2,1)S(1)}, bf16[32,3584]{1,0:T(8,128)(2,1)S(1)}, u32[]{:S(2)}, u32[]{:S(2)}) collective-permute-start(bf16[32,3584]{1,0:T(8,128)(2,1)S(1)} %get-tuple-element.65), channel_id=1, source_target_pairs={{0,1},{1,0},{2,3},{3,2},{4,5},{5,4},{6,7},{7,6},{8,9},{9,8},{10,11... | collective-permute-start | bytes 688136 | tf_op jit(solution)/shard_map/ppermute | solution.py:376
  59.5 1.6 %collective-permute-start.21 = (bf16[32,3584]{1,0:T(8,128)(2,1)S(1)}, bf16[32,3584]{1,0:T(8,128)(2,1)S(1)}, u32[]{:S(2)}, u32[]{:S(2)}) collective-permute-start(bf16[32,3584]{1,0:T(8,128)(2,1)S(1)} %get-tuple-element.63), channel_id=1, source_target_pairs={{0,1},{1,0},{2,3},{3,2},{4,5},{5,4},{6,7},{7,6},{8,9},{9,8},{10,11... | collective-permute-start | bytes 688136 | tf_op jit(solution)/shard_map/ppermute | solution.py:376
  60.0 4.4 %collective-permute-start.25 = (bf16[8,3584]{1,0:T(8,128)(2,1)S(1)}, bf16[8,3584]{1,0:T(8,128)(2,1)S(1)}, u32[]{:S(2)}, u32[]{:S(2)}) collective-permute-start(bf16[8,3584]{1,0:T(8,128)(2,1)S(1)} %get-tuple-element.73), channel_id=1, source_target_pairs={{0,2},{1,3},{2,0},{3,1},{4,6},{5,7},{6,4},{7,5},{8,10},{9,11},{10,... | collective-permute-start | bytes 172040 | tf_op jit(solution)/shard_map/ppermute | solution.py:376
  61.1 4.4 %collective-permute-start.26 = (bf16[8,3584]{1,0:T(8,128)(2,1)S(1)}, bf16[8,3584]{1,0:T(8,128)(2,1)S(1)}, u32[]{:S(2)}, u32[]{:S(2)}) collective-permute-start(bf16[8,3584]{1,0:T(8,128)(2,1)S(1)} %get-tuple-element.74), channel_id=1, source_target_pairs={{0,2},{1,3},{2,0},{3,1},{4,6},{5,7},{6,4},{7,5},{8,10},{9,11},{10,... | collective-permute-start | bytes 172040 | tf_op jit(solution)/shard_map/ppermute | solution.py:376
  62.2 6.7 %collective-permute-start.23 = (bf16[8,7168]{1,0:T(8,128)(2,1)S(1)}, bf16[8,7168]{1,0:T(8,128)(2,1)S(1)}, u32[]{:S(2)}, u32[]{:S(2)}) collective-permute-start(bf16[8,7168]{1,0:T(8,128)(2,1)S(1)} %get-tuple-element.68), channel_id=1, source_target_pairs={{0,4},{1,5},{2,6},{3,7},{4,0},{5,1},{6,2},{7,3},{8,12},{9,13},{10,... | collective-permute-start | bytes 344072 | tf_op jit(solution)/shard_map/ppermute | solution.py:376
  65.5 7.4 %collective-permute-start.27 = (bf16[4,7168]{1,0:T(4,128)(2,1)S(1)}, bf16[4,7168]{1,0:T(4,128)(2,1)S(1)}, u32[]{:S(2)}, u32[]{:S(2)}) collective-permute-start(bf16[4,7168]{1,0:T(4,128)(2,1)S(1)} %get-tuple-element.75), channel_id=1, source_target_pairs={{0,8},{1,9},{2,10},{3,11},{4,12},{5,13},{6,14},{7,15},{8,0},{9,1},... | collective-permute-start | bytes 172040 | tf_op jit(solution)/shard_map/ppermute | solution.py:376
  66.1 6.7 %collective-permute-start.28 = (bf16[4,7168]{1,0:T(4,128)(2,1)S(1)}, bf16[4,7168]{1,0:T(4,128)(2,1)S(1)}, u32[]{:S(2)}, u32[]{:S(2)}) collective-permute-start(bf16[4,7168]{1,0:T(4,128)(2,1)S(1)} %get-tuple-element.76), channel_id=1, source_target_pairs={{0,12},{1,13},{2,14},{3,15},{4,8},{5,9},{6,10},{7,11},{8,4},{9,5},... | collective-permute-start | bytes 172040 | tf_op jit(solution)/shard_map/ppermute | solution.py:376
  68.9 4.2 %collective-permute-start.24 = (bf16[4,7168]{1,0:T(4,128)(2,1)S(1)}, bf16[4,7168]{1,0:T(4,128)(2,1)S(1)}, u32[]{:S(2)}, u32[]{:S(2)}) collective-permute-start(bf16[4,7168]{1,0:T(4,128)(2,1)S(1)} %get-tuple-element.70), channel_id=1, source_target_pairs={{0,2},{1,3},{2,0},{3,1},{4,6},{5,7},{6,4},{7,5},{8,10},{9,11},{10,... | collective-permute-start | bytes 172040 | tf_op jit(solution)/shard_map/ppermute | solution.py:376
  (11 other events, 154.9 us)

commit v8 on v7

--- a/solution.py
+++ b/solution.py
@@ -15,7 +15,7 @@
 VD = 128
 LANES = 128
 PIECES = LAT // LANES
-FACTOR = (NOPE + ROPE) ** -0.5
+SCALE = (NOPE + ROPE) ** -0.5 * math.log2(math.e)
 LIMIT = 16 * 2**20
 PARTS = 2
 Y = 2
@@ -57,8 +57,18 @@
     return sorted(range(0, devices, step), key=lambda k: -k.bit_length())
 
 
+def chip_order(devices):
+    chips = far_first(devices, 2)
+    far = chips[: len(chips) // 2]
+    near = sorted(chips[len(chips) // 2 :])[1:]
+    mixed = far[:1]
+    for k, other in zip(far[1:], near):
+        mixed += [k, other]
+    return mixed + [0]
+
+
 def gathered_order(devices):
-    return [z + y for z in far_first(devices, 4) for y in (0, 2)]
+    return [z + y for z in reversed(far_first(devices, 4)) for y in (0, 2)]
 
 
 def rotary_kernel(len_ref, cos_ref, sin_ref):
@@ -110,7 +120,7 @@
     wide = 2 * count // devices * heads
     width = NOPE + ROPE
     lane = lax.broadcasted_iota(jnp.int32, (wide // 2, LANES), 1)
-    order = far_first(devices, 2)
+    order = chip_order(devices)
     for core, (wq_ref, wk_ref) in enumerate(weights):
         projected = jnp.dot(piece, wq_ref[...], preferred_element_type=jnp.float32)
         for h in range(heads):
@@ -150,7 +160,17 @@
     return call(kernel, out, 20, "project", scratch)(*pieces, *[resident(w) for w in weights])
 
 
-def attend_kernel(chips, len_ref, cos_ref, sin_ref, key_ref, new_ref, *refs):
+def flip_kernel(key_ref, after_ref, out_ref):
+    for r in range(key_ref.shape[0]):
+        out_ref[r] = key_ref[r, :LAT, :].T
+
+
+def flip(keys, after):
+    rows, _, maxlen = keys.shape
+    return call(flip_kernel, shape(rows, maxlen, LAT), 4, "flip")(resident(keys), after)
+
+
+def attend_kernel(chips, len_ref, cos_ref, sin_ref, key_ref, flip_ref, new_ref, *refs):
     q_refs = refs[:chips]
     out_refs = refs[chips:]
     rows, _, maxlen = key_ref.shape
@@ -175,28 +195,22 @@
         swapped = jnp.concatenate([pe[:, HALF:], pe[:, :HALF]], axis=-1)
         rotated = (pe * cos_ref[r : r + 1, :] + swapped * sin_ref[r : r + 1, :]).astype(jnp.bfloat16)
         newest = new_ref[r : r + 1, :].astype(jnp.float32)
-        own = (
-            jnp.sum(latent * newest[:, :LAT], axis=-1, keepdims=True)
-            + jnp.sum(rotated.astype(jnp.float32) * newest[:, LAT:], axis=-1, keepdims=True)
-        ) * FACTOR
+        own = jnp.sum(latent * newest[:, :LAT], axis=-1, keepdims=True) + jnp.sum(
+            rotated.astype(jnp.float32) * newest[:, LAT:], axis=-1, keepdims=True
+        )
         scores = jnp.dot(
             latent.astype(jnp.bfloat16), key_ref[r, :LAT, :], preferred_element_type=jnp.float32
         )
         scores += jnp.dot(rotated, key_ref[r, LAT:, :], preferred_element_type=jnp.float32)
         position = lax.broadcasted_iota(jnp.int32, (1, maxlen), 1)
-        scores = jnp.where(position < len_ref[r], scores * FACTOR, -jnp.inf)
+        scores = jnp.where(position < len_ref[r], scores, -jnp.inf)
         peak = jnp.maximum(jnp.max(scores, axis=-1, keepdims=True), own)
-        expo = jnp.exp(scores - peak)
-        own_expo = jnp.exp(own - peak)
-        total = jnp.sum(expo, axis=-1, keepdims=True) + own_expo
-        weights = (expo / total).astype(jnp.bfloat16)
-        own_weight = (own_expo / total).astype(jnp.bfloat16).astype(jnp.float32)
-        summed = lax.dot_general(
-            weights,
-            key_ref[r, :LAT, :],
-            (((1,), (1,)), ((), ())),
-            preferred_element_type=jnp.float32,
-        )
+        expo = jnp.exp2((scores - peak) * SCALE)
+        own_expo = jnp.exp2((own - peak) * SCALE)
+        inverse = 1.0 / (jnp.sum(expo, axis=-1, keepdims=True) + own_expo)
+        weights = (expo * inverse).astype(jnp.bfloat16)
+        own_weight = (own_expo * inverse).astype(jnp.bfloat16).astype(jnp.float32)
+        summed = jnp.dot(weights, flip_ref[r], preferred_element_type=jnp.float32)
         summed += own_weight * newest[:, :LAT]
         for k in range(2 * chips):
             out_refs[k // 2][k % 2, r * heads : (r + 1) * heads, :] = summed[
@@ -204,12 +218,12 @@
             ].astype(jnp.bfloat16)
 
 
-def attend(lengths, tables, keys, new_latent, messages, heads):
+def attend(lengths, tables, keys, flipped, new_latent, messages, heads):
     chips = len(messages)
     kernel = functools.partial(attend_kernel, chips)
     block = shape(2, keys.shape[0] * heads, LAT)
     return call(kernel, [block] * chips, 2 + chips, "attend", scalars=1)(
-        lengths, *tables, resident(keys), new_latent, *messages
+        lengths, *tables, resident(keys), resident(flipped), new_latent, *messages
     )
 
 
@@ -277,7 +291,7 @@
 
 
 def places(devices, chips):
-    order = far_first(devices, 2)
+    order = chip_order(devices)
     return [order.index(k) for k in chips]
 
 
@@ -367,8 +381,8 @@
 def on_device(q_latent, new_latent, cache, lengths, w_uq, w_uk, w_uv, w_o, devices):
     heads = w_uk.shape[0]
     rows = cache.shape[0]
-    order = far_first(devices, 2)
-    zs = far_first(devices, 4)
+    order = chip_order(devices)
+    zs = far_first(devices, 4)[::-1]
 
     def swap(block, k):
         if k == 0:
@@ -378,9 +392,10 @@
     far_weights = [swap(w_uq, 1), swap(w_uk, 1)]
     tables, near = join(rotary(lengths), [q_latent, swap(q_latent, 2)])
     messages = project([swap(near, z) for z in zs], [w_uq, w_uk, *far_weights], devices)
+    keys = jnp.swapaxes(cache, 1, 2)
+    flipped = flip(keys, messages[-1])
     messages = [swap(block, k) for k, block in zip(order, messages)]
-    keys = jnp.swapaxes(cache, 1, 2)
-    latents = attend(lengths, tables, keys, new_latent, messages, heads)
+    latents = attend(lengths, tables, keys, flipped, new_latent, messages, heads)
     latents = [swap(block, k) for k, block in zip(order, latents)]
     values = head_values(latents, swap(regroup(latents), 1), w_uv)
     keep, got, near = [], [], None

time: 74 us -> 72.8 us (0.984)
  starting transfers between devices: 36.7 us -> 34.8 us
  Pallas kernels: 12.1 us -> 13 us
    ppermute x29, starting transfers between devices: 36.7 us -> 34.8 us  [swap(): return lax.ppermute(block, 'row', [(i, i ^ k) for i in range(devices)])]
    pallas_call x13 -> x14, Pallas kernels: 12.1 us -> 13 us  [run(): pl.pallas_call(kernel, out_shape=out_shape, in_specs=smem + [in_vmem()] *...]
  transfers between devices with their start and end apart: 29 -> 29, of which waited for: 16 -> 16; matrix products, arithmetic and copies ran while one was open for 0% -> 0% of each run, Pallas kernels for 3% -> 5%
where the time goes in v8:
time: 72.8 us; the launch traced here: 72.7 us
  starting transfers between devices  34.8 us (48%)
  waiting for transfers between devices  23.9 us (33%)
  Pallas kernels  13 us (18%)
    ppermute x29, starting transfers between devices, swap(): return lax.ppermute(block, 'row', [(i, i ^ k) for i in range(devices)])  34.8 us
    ppermute x29, waiting for transfers between devices, swap(): return lax.ppermute(block, 'row', [(i, i ^ k) for i in range(devices)])  23.9 us
    pallas_call x14, Pallas kernels, run(): pl.pallas_call(kernel, out_shape=out_shape, in_specs=smem + [in_vmem()] *...  13 us
  transfers between devices with their start and end apart: 29, of which 16 were waited for; matrix products, arithmetic and copies ran while one was open for 0% of the time, Pallas kernels for 5%

profile of v8, /device:TPU:0, one launch (start us, length us, event | category | flops | bytes accessed | tf_op | source)
XLA Modules:
  0.0 72.7 jit_solution(1361971768279475075)
XLA Ops:
  0.5 3.0 %collective-permute-start = (bf16[4,1536]{1,0:T(4,128)(2,1)}, bf16[4,1536]{1,0:T(4,128)(2,1)S(1)}, u32[]{:S(2)}, u32[]{:S(2)}) collective-permute-start(bf16[4,1536]{1,0:T(4,128)(2,1)} %refs_0_.1), channel_id=1, source_target_pairs={{0,2},{1,3},{2,0},{3,1},{4,6},{5,7},{6,4},{7,5},{8,10},{9,11},{10,... | collective-permute-start | bytes 36872 | tf_op jit(solution)/shard_map/ppermute | solution.py:390
  5.4 3.2 %collective-permute-start.3 = (bf16[8,1536]{1,0:T(8,128)(2,1)S(1)}, bf16[8,1536]{1,0:T(8,128)(2,1)S(1)}, u32[]{:S(2)}, u32[]{:S(2)}) collective-permute-start(bf16[8,1536]{1,0:T(8,128)(2,1)S(1)} %get-tuple-element.45.refs_0_), channel_id=1, source_target_pairs={{0,8},{1,9},{2,10},{3,11},{4,12},{5,13},{6,14},{7,15},{8,0},{9,1},... | collective-permute-start | bytes 73736 | tf_op jit(solution)/shard_map/ppermute | solution.py:390
  8.6 1.3 %collective-permute-start.2 = (bf16[8,1536]{1,0:T(8,128)(2,1)S(1)}, bf16[8,1536]{1,0:T(8,128)(2,1)S(1)}, u32[]{:S(2)}, u32[]{:S(2)}) collective-permute-start(bf16[8,1536]{1,0:T(8,128)(2,1)S(1)} %get-tuple-element.45.refs_0_), channel_id=1, source_target_pairs={{0,12},{1,13},{2,14},{3,15},{4,8},{5,9},{6,10},{7,11},{8,4},{9,5},... | collective-permute-start | bytes 73736 | tf_op jit(solution)/shard_map/ppermute | solution.py:390
  10.4 3.8 %collective-permute-done.2.refs_2_ = bf16[8,1536]{1,0:T(8,128)(2,1)S(1)} collective-permute-done((bf16[8,1536]{1,0:T(8,128)(2,1)S(1)}, bf16[8,1536]{1,0:T(8,128)(2,1)S(1)}, u32[]{:S(2)}, u32[]{:S(2)}) %collective-permute-start.2) | collective-permute-done | bytes 24608 | tf_op jit(solution)/shard_map/ppermute | solution.py:390
  14.2 2.3 %project.1 = (bf16[2,144,128]{2,1,0:T(8,128)(2,1)S(1)}, bf16[2,144,128]{2,1,0:T(8,128)(2,1)S(1)}, bf16[2,144,128]{2,1,0:T(8,128)(2,1)S(1)}, bf16[2,144,128]{2,1,...) custom-call(bf16[8,1536]{1,0:T(8,128)(2,1)S(1)} %get-tuple-element.4, ...), custom_call_target="tpu_custom_call" | custom-call | flops 23000000512 | tf_op jit(solution)/shard_map/project/pallas_call | solution.py:36
  16.5 1.3 %collective-permute-start.6 = (bf16[2,144,128]{2,1,0:T(8,128)(2,1)S(1)}, bf16[2,144,128]{2,1,0:T(8,128)(2,1)S(1)}, u32[]{:S(2)}, u32[]{:S(2)}) collective-permute-start(bf16[2,144,128]{2,1,0:T(8,128)(2,1)S(1)} %get-tuple-element.47), channel_id=1, source_target_pairs={{0,8},{1,9},{2,10},{3,11},{4,12},{5,13},{6,14},{7,15},{8,0},{9,1},... | collective-permute-start | bytes 221192 | tf_op jit(solution)/shard_map/ppermute | solution.py:390
  17.8 2.6 %collective-permute-start.7 = (bf16[2,144,128]{2,1,0:T(8,128)(2,1)S(1)}, bf16[2,144,128]{2,1,0:T(8,128)(2,1)S(1)}, u32[]{:S(2)}, u32[]{:S(2)}) collective-permute-start(bf16[2,144,128]{2,1,0:T(8,128)(2,1)S(1)} %get-tuple-element.48), channel_id=1, source_target_pairs={{0,10},{1,11},{2,8},{3,9},{4,14},{5,15},{6,12},{7,13},{8,2},{9,3},... | collective-permute-start | bytes 221192 | tf_op jit(solution)/shard_map/ppermute | solution.py:390
  21.0 2.0 %collective-permute-start.9 = (bf16[2,144,128]{2,1,0:T(8,128)(2,1)S(1)}, bf16[2,144,128]{2,1,0:T(8,128)(2,1)S(1)}, u32[]{:S(2)}, u32[]{:S(2)}) collective-permute-start(bf16[2,144,128]{2,1,0:T(8,128)(2,1)S(1)} %get-tuple-element.50), channel_id=1, source_target_pairs={{0,12},{1,13},{2,14},{3,15},{4,8},{5,9},{6,10},{7,11},{8,4},{9,5},... | collective-permute-start | bytes 221192 | tf_op jit(solution)/shard_map/ppermute | solution.py:390
  23.0 2.1 %collective-permute-done.6.refs_0_ = bf16[2,144,128]{2,1,0:T(8,128)(2,1)S(1)} collective-permute-done((bf16[2,144,128]{2,1,0:T(8,128)(2,1)S(1)}, bf16[2,144,128]{2,1,0:T(8,128)(2,1)S(1)}, u32[]{:S(2)}, u32[]{:S(2)}) %collective-permute-start.6) | collective-permute-done | bytes 73760 | tf_op jit(solution)/shard_map/ppermute | solution.py:390
  25.1 2.9 %collective-permute-start.11 = (bf16[2,144,128]{2,1,0:T(8,128)(2,1)S(1)}, bf16[2,144,128]{2,1,0:T(8,128)(2,1)S(1)}, u32[]{:S(2)}, u32[]{:S(2)}) collective-permute-start(bf16[2,144,128]{2,1,0:T(8,128)(2,1)S(1)} %get-tuple-element.52), channel_id=1, source_target_pairs={{0,14},{1,15},{2,12},{3,13},{4,10},{5,11},{6,8},{7,9},{8,6},{9,7},... | collective-permute-start | bytes 221192 | tf_op jit(solution)/shard_map/ppermute | solution.py:390
  28.0 1.1 %collective-permute-done.7.refs_1_ = bf16[2,144,128]{2,1,0:T(8,128)(2,1)S(1)} collective-permute-done((bf16[2,144,128]{2,1,0:T(8,128)(2,1)S(1)}, bf16[2,144,128]{2,1,0:T(8,128)(2,1)S(1)}, u32[]{:S(2)}, u32[]{:S(2)}) %collective-permute-start.7) | collective-permute-done | bytes 73760 | tf_op jit(solution)/shard_map/ppermute | solution.py:390
  29.2 1.7 %flip.1.flip_ref = bf16[4,1536,512]{2,1,0:T(8,128)(2,1)S(1)} custom-call(bf16[4,576,1536]{2,1,0:T(8,128)(2,1)S(1)} %bitcast.5, bf16[2,144,128]{2,1,0:T(8,128)(2,1)S(1)} %get-tuple-element.46.after_ref.refs_7_), custom_call_target="tpu_custom_call" | custom-call | flops 4600000000 | tf_op jit(solution)/shard_map/flip/pallas_call | solution.py:36
  30.9 1.2 %collective-permute-done.11.refs_5_ = bf16[2,144,128]{2,1,0:T(8,128)(2,1)S(1)} collective-permute-done((bf16[2,144,128]{2,1,0:T(8,128)(2,1)S(1)}, bf16[2,144,128]{2,1,0:T(8,128)(2,1)S(1)}, u32[]{:S(2)}, u32[]{:S(2)}) %collective-permute-start.11) | collective-permute-done | bytes 73760 | tf_op jit(solution)/shard_map/ppermute | solution.py:390
  32.2 2.3 %collective-permute-done.12.refs_6_ = bf16[2,144,128]{2,1,0:T(8,128)(2,1)S(1)} collective-permute-done((bf16[2,144,128]{2,1,0:T(8,128)(2,1)S(1)}, bf16[2,144,128]{2,1,0:T(8,128)(2,1)S(1)}, u32[]{:S(2)}, u32[]{:S(2)}) %collective-permute-start.12) | collective-permute-done | bytes 73760 | tf_op jit(solution)/shard_map/ppermute | solution.py:390
  34.4 4.3 %attend.1 = (bf16[2,32,512]{2,1,0:T(8,128)(2,1)S(1)}, bf16[2,32,512]{2,1,0:T(8,128)(2,1)S(1)}, bf16[2,32,512]{2,1,0:T(8,128)(2,1)S(1)}, bf16[2,32,512]{2,1,0:T(8...) custom-call(s32[4]{0:T(128)S(1)} %copy-done.5, ...), custom_call_target="tpu_custom_call" | custom-call | flops 11500000256 | tf_op jit(solution)/shard_map/attend/pallas_call | solution.py:36
  38.9 3.2 %collective-permute-start.14 = (bf16[2,32,512]{2,1,0:T(8,128)(2,1)S(1)}, bf16[2,32,512]{2,1,0:T(8,128)(2,1)S(1)}, u32[]{:S(2)}, u32[]{:S(2)}) collective-permute-start(bf16[2,32,512]{2,1,0:T(8,128)(2,1)S(1)} %get-tuple-element.55), channel_id=1, source_target_pairs={{0,10},{1,11},{2,8},{3,9},{4,14},{5,15},{6,12},{7,13},{8,2},{9,3},... | collective-permute-start | bytes 196616 | tf_op jit(solution)/shard_map/ppermute | solution.py:390
  42.0 1.2 %collective-permute-start.15 = (bf16[2,32,512]{2,1,0:T(8,128)(2,1)S(1)}, bf16[2,32,512]{2,1,0:T(8,128)(2,1)S(1)}, u32[]{:S(2)}, u32[]{:S(2)}) collective-permute-start(bf16[2,32,512]{2,1,0:T(8,128)(2,1)S(1)} %get-tuple-element.56), channel_id=1, source_target_pairs={{0,2},{1,3},{2,0},{3,1},{4,6},{5,7},{6,4},{7,5},{8,10},{9,11},{10,... | collective-permute-start | bytes 196616 | tf_op jit(solution)/shard_map/ppermute | solution.py:390
  43.3 2.0 %collective-permute-start.16 = (bf16[2,32,512]{2,1,0:T(8,128)(2,1)S(1)}, bf16[2,32,512]{2,1,0:T(8,128)(2,1)S(1)}, u32[]{:S(2)}, u32[]{:S(2)}) collective-permute-start(bf16[2,32,512]{2,1,0:T(8,128)(2,1)S(1)} %get-tuple-element.57), channel_id=1, source_target_pairs={{0,12},{1,13},{2,14},{3,15},{4,8},{5,9},{6,10},{7,11},{8,4},{9,5},... | collective-permute-start | bytes 196616 | tf_op jit(solution)/shard_map/ppermute | solution.py:390
  45.4 3.1 %collective-permute-start.18 = (bf16[2,32,512]{2,1,0:T(8,128)(2,1)S(1)}, bf16[2,32,512]{2,1,0:T(8,128)(2,1)S(1)}, u32[]{:S(2)}, u32[]{:S(2)}) collective-permute-start(bf16[2,32,512]{2,1,0:T(8,128)(2,1)S(1)} %get-tuple-element.59), channel_id=1, source_target_pairs={{0,14},{1,15},{2,12},{3,13},{4,10},{5,11},{6,8},{7,9},{8,6},{9,7},... | collective-permute-start | bytes 196616 | tf_op jit(solution)/shard_map/ppermute | solution.py:390
  50.0 2.4 %collective-permute-done.18.refs_5_ = bf16[2,32,512]{2,1,0:T(8,128)(2,1)S(1)} collective-permute-done((bf16[2,32,512]{2,1,0:T(8,128)(2,1)S(1)}, bf16[2,32,512]{2,1,0:T(8,128)(2,1)S(1)}, u32[]{:S(2)}, u32[]{:S(2)}) %collective-permute-start.18) | collective-permute-done | bytes 65568 | tf_op jit(solution)/shard_map/ppermute | solution.py:390
  52.4 1.2 %collective-permute-done.19.refs_6_ = bf16[2,32,512]{2,1,0:T(8,128)(2,1)S(1)} collective-permute-done((bf16[2,32,512]{2,1,0:T(8,128)(2,1)S(1)}, bf16[2,32,512]{2,1,0:T(8,128)(2,1)S(1)}, u32[]{:S(2)}, u32[]{:S(2)}) %collective-permute-start.19) | collective-permute-done | bytes 65568 | tf_op jit(solution)/shard_map/ppermute | solution.py:390
  53.7 1.5 %collective-permute-done.20.refs_8_ = bf16[8,32,512]{2,1,0:T(8,128)(2,1)S(1)} collective-permute-done((bf16[8,32,512]{2,1,0:T(8,128)(2,1)S(1)}, bf16[8,32,512]{2,1,0:T(8,128)(2,1)S(1)}, u32[]{:S(2)}, u32[]{:S(2)}) %collective-permute-start.20) | collective-permute-done | bytes 262176 | tf_op jit(solution)/shard_map/ppermute | solution.py:390
  55.8 1.4 %terms.3 = (f32[32,3584]{1,0:T(8,128)S(1)}, bf16[32,3584]{1,0:T(8,128)(2,1)S(1)}) custom-call(bf16[64,1024]{1,0:T(8,128)(2,1)S(1)} %values.1.val_ref, bf16[1024,7168]{1,0:T(8,128)(2,1)S(1)} %bitcast.2), custom_call_target="tpu_custom_call" | custom-call | flops 6899999744 | tf_op jit(solution)/shard_map/terms/pallas_call | solution.py:36
  57.4 1.4 %terms.2 = (f32[32,3584]{1,0:T(8,128)S(1)}, bf16[32,3584]{1,0:T(8,128)(2,1)S(1)}) custom-call(bf16[64,1024]{1,0:T(8,128)(2,1)S(1)} %values.1.val_ref, bf16[1024,7168]{1,0:T(8,128)(2,1)S(1)} %bitcast.2), custom_call_target="tpu_custom_call" | custom-call | flops 6899999744 | tf_op jit(solution)/shard_map/terms/pallas_call | solution.py:36
  59.2 1.1 %collective-permute-start.25 = (bf16[8,3584]{1,0:T(8,128)(2,1)S(1)}, bf16[8,3584]{1,0:T(8,128)(2,1)S(1)}, u32[]{:S(2)}, u32[]{:S(2)}) collective-permute-start(bf16[8,3584]{1,0:T(8,128)(2,1)S(1)} %get-tuple-element.73), channel_id=1, source_target_pairs={{0,2},{1,3},{2,0},{3,1},{4,6},{5,7},{6,4},{7,5},{8,10},{9,11},{10,... | collective-permute-start | bytes 172040 | tf_op jit(solution)/shard_map/ppermute | solution.py:390
  60.4 1.1 %collective-permute-start.26 = (bf16[8,3584]{1,0:T(8,128)(2,1)S(1)}, bf16[8,3584]{1,0:T(8,128)(2,1)S(1)}, u32[]{:S(2)}, u32[]{:S(2)}) collective-permute-start(bf16[8,3584]{1,0:T(8,128)(2,1)S(1)} %get-tuple-element.74), channel_id=1, source_target_pairs={{0,2},{1,3},{2,0},{3,1},{4,6},{5,7},{6,4},{7,5},{8,10},{9,11},{10,... | collective-permute-start | bytes 172040 | tf_op jit(solution)/shard_map/ppermute | solution.py:390
  61.8 1.9 %collective-permute-done.25.refs_2_ = bf16[8,3584]{1,0:T(8,128)(2,1)S(1)} collective-permute-done((bf16[8,3584]{1,0:T(8,128)(2,1)S(1)}, bf16[8,3584]{1,0:T(8,128)(2,1)S(1)}, u32[]{:S(2)}, u32[]{:S(2)}) %collective-permute-start.25) | collective-permute-done | bytes 57376 | tf_op jit(solution)/shard_map/ppermute | solution.py:390
  63.7 1.1 %collective-permute-done.26.refs_3_ = bf16[8,3584]{1,0:T(8,128)(2,1)S(1)} collective-permute-done((bf16[8,3584]{1,0:T(8,128)(2,1)S(1)}, bf16[8,3584]{1,0:T(8,128)(2,1)S(1)}, u32[]{:S(2)}, u32[]{:S(2)}) %collective-permute-start.26) | collective-permute-done | bytes 57376 | tf_op jit(solution)/shard_map/ppermute | solution.py:390
  64.8 0.8 %collective-permute-start.27 = (bf16[4,7168]{1,0:T(4,128)(2,1)S(1)}, bf16[4,7168]{1,0:T(4,128)(2,1)S(1)}, u32[]{:S(2)}, u32[]{:S(2)}) collective-permute-start(bf16[4,7168]{1,0:T(4,128)(2,1)S(1)} %get-tuple-element.75), channel_id=1, source_target_pairs={{0,8},{1,9},{2,10},{3,11},{4,12},{5,13},{6,14},{7,15},{8,0},{9,1},... | collective-permute-start | bytes 172040 | tf_op jit(solution)/shard_map/ppermute | solution.py:390
  65.5 1.9 %collective-permute-start.28 = (bf16[4,7168]{1,0:T(4,128)(2,1)S(1)}, bf16[4,7168]{1,0:T(4,128)(2,1)S(1)}, u32[]{:S(2)}, u32[]{:S(2)}) collective-permute-start(bf16[4,7168]{1,0:T(4,128)(2,1)S(1)} %get-tuple-element.76), channel_id=1, source_target_pairs={{0,12},{1,13},{2,14},{3,15},{4,8},{5,9},{6,10},{7,11},{8,4},{9,5},... | collective-permute-start | bytes 172040 | tf_op jit(solution)/shard_map/ppermute | solution.py:390
  67.5 1.0 %collective-permute-start.24 = (bf16[4,7168]{1,0:T(4,128)(2,1)S(1)}, bf16[4,7168]{1,0:T(4,128)(2,1)S(1)}, u32[]{:S(2)}, u32[]{:S(2)}) collective-permute-start(bf16[4,7168]{1,0:T(4,128)(2,1)S(1)} %get-tuple-element.70), channel_id=1, source_target_pairs={{0,2},{1,3},{2,0},{3,1},{4,6},{5,7},{6,4},{7,5},{8,10},{9,11},{10,... | collective-permute-start | bytes 172040 | tf_op jit(solution)/shard_map/ppermute | solution.py:390
  68.6 3.4 %collective-permute-done.27.refs_2_ = bf16[4,7168]{1,0:T(4,128)(2,1)S(1)} collective-permute-done((bf16[4,7168]{1,0:T(4,128)(2,1)S(1)}, bf16[4,7168]{1,0:T(4,128)(2,1)S(1)}, u32[]{:S(2)}, u32[]{:S(2)}) %collective-permute-start.27) | collective-permute-done | bytes 57376 | tf_op jit(solution)/shard_map/ppermute | solution.py:390
  (71 shorter events, 7.5 us)
Async XLA Ops:
  0.0 14.2 %collective-permute-start.4 = (bf16[1536,1536]{1,0:T(8,128)(2,1)}, bf16[1536,1536]{1,0:T(8,128)(2,1)S(1)}, u32[]{:S(2)}, u32[]{:S(2)}) collective-permute-start(bf16[1536,1536]{1,0:T(8,128)(2,1)} %refs_4_.1), channel_id=1, source_target_pairs={{0,1},{1,0},{2,3},{3,2},{4,5},{5,4},{6,7},{7,6},{8,9},{9,8},{10,11... | collective-permute-start | bytes 14155784 | tf_op jit(solution)/shard_map/ppermute | solution.py:390
  0.5 13.7 %collective-permute-start.5 = (bf16[8,128,512]{2,1,0:T(8,128)(2,1)}, bf16[8,128,512]{2,1,0:T(8,128)(2,1)S(1)}, u32[]{:S(2)}, u32[]{:S(2)}) collective-permute-start(bf16[8,128,512]{2,1,0:T(8,128)(2,1)} %refs_5_.1), channel_id=1, source_target_pairs={{0,1},{1,0},{2,3},{3,2},{4,5},{5,4},{6,7},{7,6},{8,9},{9,8},{10,11... | collective-permute-start | bytes 3145736 | tf_op jit(solution)/shard_map/ppermute | solution.py:390
  0.5 4.8 %collective-permute-start = (bf16[4,1536]{1,0:T(4,128)(2,1)}, bf16[4,1536]{1,0:T(4,128)(2,1)S(1)}, u32[]{:S(2)}, u32[]{:S(2)}) collective-permute-start(bf16[4,1536]{1,0:T(4,128)(2,1)} %refs_0_.1), channel_id=1, source_target_pairs={{0,2},{1,3},{2,0},{3,1},{4,6},{5,7},{6,4},{7,5},{8,10},{9,11},{10,... | collective-permute-start | bytes 36872 | tf_op jit(solution)/shard_map/ppermute | solution.py:390
  5.4 23.8 %slice-start.4 = ((s8[7077888]{0:T(1024)(128)(4,1)}), s8[4194304]{0:T(1024)(128)(4,1)S(1)}, s32[]{:S(2)}) async-start(s8[7077888]{0:T(1024)(128)(4,1)} %bitcast.3), calls=%async_computation.4 | async-start | bytes 8388608
  5.4 23.8 %slice-start.5 = ((s8[7077888]{0:T(1024)(128)(4,1)}), s8[2883584]{0:T(1024)(128)(4,1)S(1)}, s32[]{:S(2)}) async-start(s8[7077888]{0:T(1024)(128)(4,1)} %bitcast.3), calls=%async_computation.5 | async-start | bytes 5767168
  5.4 5.0 %collective-permute-start.3 = (bf16[8,1536]{1,0:T(8,128)(2,1)S(1)}, bf16[8,1536]{1,0:T(8,128)(2,1)S(1)}, u32[]{:S(2)}, u32[]{:S(2)}) collective-permute-start(bf16[8,1536]{1,0:T(8,128)(2,1)S(1)} %get-tuple-element.45.refs_0_), channel_id=1, source_target_pairs={{0,8},{1,9},{2,10},{3,11},{4,12},{5,13},{6,14},{7,15},{8,0},{9,1},... | collective-permute-start | bytes 73736 | tf_op jit(solution)/shard_map/ppermute | solution.py:390
  8.6 5.6 %collective-permute-start.2 = (bf16[8,1536]{1,0:T(8,128)(2,1)S(1)}, bf16[8,1536]{1,0:T(8,128)(2,1)S(1)}, u32[]{:S(2)}, u32[]{:S(2)}) collective-permute-start(bf16[8,1536]{1,0:T(8,128)(2,1)S(1)} %get-tuple-element.45.refs_0_), channel_id=1, source_target_pairs={{0,12},{1,13},{2,14},{3,15},{4,8},{5,9},{6,10},{7,11},{8,4},{9,5},... | collective-permute-start | bytes 73736 | tf_op jit(solution)/shard_map/ppermute | solution.py:390
  9.9 4.3 %collective-permute-start.1 = (bf16[8,1536]{1,0:T(8,128)(2,1)S(1)}, bf16[8,1536]{1,0:T(8,128)(2,1)S(1)}, u32[]{:S(2)}, u32[]{:S(2)}) collective-permute-start(bf16[8,1536]{1,0:T(8,128)(2,1)S(1)} %get-tuple-element.45.refs_0_), channel_id=1, source_target_pairs={{0,4},{1,5},{2,6},{3,7},{4,0},{5,1},{6,2},{7,3},{8,12},{9,13},{10,... | collective-permute-start | bytes 73736 | tf_op jit(solution)/shard_map/ppermute | solution.py:390
  16.5 8.6 %collective-permute-start.6 = (bf16[2,144,128]{2,1,0:T(8,128)(2,1)S(1)}, bf16[2,144,128]{2,1,0:T(8,128)(2,1)S(1)}, u32[]{:S(2)}, u32[]{:S(2)}) collective-permute-start(bf16[2,144,128]{2,1,0:T(8,128)(2,1)S(1)} %get-tuple-element.47), channel_id=1, source_target_pairs={{0,8},{1,9},{2,10},{3,11},{4,12},{5,13},{6,14},{7,15},{8,0},{9,1},... | collective-permute-start | bytes 221192 | tf_op jit(solution)/shard_map/ppermute | solution.py:390
  17.8 11.3 %collective-permute-start.7 = (bf16[2,144,128]{2,1,0:T(8,128)(2,1)S(1)}, bf16[2,144,128]{2,1,0:T(8,128)(2,1)S(1)}, u32[]{:S(2)}, u32[]{:S(2)}) collective-permute-start(bf16[2,144,128]{2,1,0:T(8,128)(2,1)S(1)} %get-tuple-element.48), channel_id=1, source_target_pairs={{0,10},{1,11},{2,8},{3,9},{4,14},{5,15},{6,12},{7,13},{8,2},{9,3},... | collective-permute-start | bytes 221192 | tf_op jit(solution)/shard_map/ppermute | solution.py:390
  20.5 10.4 %collective-permute-start.8 = (bf16[2,144,128]{2,1,0:T(8,128)(2,1)S(1)}, bf16[2,144,128]{2,1,0:T(8,128)(2,1)S(1)}, u32[]{:S(2)}, u32[]{:S(2)}) collective-permute-start(bf16[2,144,128]{2,1,0:T(8,128)(2,1)S(1)} %get-tuple-element.49), channel_id=1, source_target_pairs={{0,2},{1,3},{2,0},{3,1},{4,6},{5,7},{6,4},{7,5},{8,10},{9,11},{10,... | collective-permute-start | bytes 221192 | tf_op jit(solution)/shard_map/ppermute | solution.py:390
  21.0 9.9 %collective-permute-start.9 = (bf16[2,144,128]{2,1,0:T(8,128)(2,1)S(1)}, bf16[2,144,128]{2,1,0:T(8,128)(2,1)S(1)}, u32[]{:S(2)}, u32[]{:S(2)}) collective-permute-start(bf16[2,144,128]{2,1,0:T(8,128)(2,1)S(1)} %get-tuple-element.50), channel_id=1, source_target_pairs={{0,12},{1,13},{2,14},{3,15},{4,8},{5,9},{6,10},{7,11},{8,4},{9,5},... | collective-permute-start | bytes 221192 | tf_op jit(solution)/shard_map/ppermute | solution.py:390
  23.0 7.9 %collective-permute-start.10 = (bf16[2,144,128]{2,1,0:T(8,128)(2,1)S(1)}, bf16[2,144,128]{2,1,0:T(8,128)(2,1)S(1)}, u32[]{:S(2)}, u32[]{:S(2)}) collective-permute-start(bf16[2,144,128]{2,1,0:T(8,128)(2,1)S(1)} %get-tuple-element.51), channel_id=1, source_target_pairs={{0,4},{1,5},{2,6},{3,7},{4,0},{5,1},{6,2},{7,3},{8,12},{9,13},{10,... | collective-permute-start | bytes 221192 | tf_op jit(solution)/shard_map/ppermute | solution.py:390
  25.1 7.0 %collective-permute-start.11 = (bf16[2,144,128]{2,1,0:T(8,128)(2,1)S(1)}, bf16[2,144,128]{2,1,0:T(8,128)(2,1)S(1)}, u32[]{:S(2)}, u32[]{:S(2)}) collective-permute-start(bf16[2,144,128]{2,1,0:T(8,128)(2,1)S(1)} %get-tuple-element.52), channel_id=1, source_target_pairs={{0,14},{1,15},{2,12},{3,13},{4,10},{5,11},{6,8},{7,9},{8,6},{9,7},... | collective-permute-start | bytes 221192 | tf_op jit(solution)/shard_map/ppermute | solution.py:390
  29.2 5.3 %collective-permute-start.12 = (bf16[2,144,128]{2,1,0:T(8,128)(2,1)S(1)}, bf16[2,144,128]{2,1,0:T(8,128)(2,1)S(1)}, u32[]{:S(2)}, u32[]{:S(2)}) collective-permute-start(bf16[2,144,128]{2,1,0:T(8,128)(2,1)S(1)} %get-tuple-element.53), channel_id=1, source_target_pairs={{0,6},{1,7},{2,4},{3,5},{4,2},{5,3},{6,0},{7,1},{8,14},{9,15},{10,... | collective-permute-start | bytes 221192 | tf_op jit(solution)/shard_map/ppermute | solution.py:390
  34.4 21.3 %slice-start.1 = ((s8[14680064]{0:T(1024)(128)(4,1)}), s8[4194304]{0:T(1024)(128)(4,1)S(1)}, s32[]{:S(2)}) async-start(s8[14680064]{0:T(1024)(128)(4,1)} %bitcast.1), calls=%async_computation.1 | async-start | bytes 8388608
  38.8 6.6 %collective-permute-start.13 = (bf16[2,32,512]{2,1,0:T(8,128)(2,1)S(1)}, bf16[2,32,512]{2,1,0:T(8,128)(2,1)S(1)}, u32[]{:S(2)}, u32[]{:S(2)}) collective-permute-start(bf16[2,32,512]{2,1,0:T(8,128)(2,1)S(1)} %get-tuple-element.54), channel_id=1, source_target_pairs={{0,8},{1,9},{2,10},{3,11},{4,12},{5,13},{6,14},{7,15},{8,0},{9,1},... | collective-permute-start | bytes 196616 | tf_op jit(solution)/shard_map/ppermute | solution.py:390
  38.9 9.6 %collective-permute-start.14 = (bf16[2,32,512]{2,1,0:T(8,128)(2,1)S(1)}, bf16[2,32,512]{2,1,0:T(8,128)(2,1)S(1)}, u32[]{:S(2)}, u32[]{:S(2)}) collective-permute-start(bf16[2,32,512]{2,1,0:T(8,128)(2,1)S(1)} %get-tuple-element.55), channel_id=1, source_target_pairs={{0,10},{1,11},{2,8},{3,9},{4,14},{5,15},{6,12},{7,13},{8,2},{9,3},... | collective-permute-start | bytes 196616 | tf_op jit(solution)/shard_map/ppermute | solution.py:390
  42.0 7.1 %collective-permute-start.15 = (bf16[2,32,512]{2,1,0:T(8,128)(2,1)S(1)}, bf16[2,32,512]{2,1,0:T(8,128)(2,1)S(1)}, u32[]{:S(2)}, u32[]{:S(2)}) collective-permute-start(bf16[2,32,512]{2,1,0:T(8,128)(2,1)S(1)} %get-tuple-element.56), channel_id=1, source_target_pairs={{0,2},{1,3},{2,0},{3,1},{4,6},{5,7},{6,4},{7,5},{8,10},{9,11},{10,... | collective-permute-start | bytes 196616 | tf_op jit(solution)/shard_map/ppermute | solution.py:390
  43.3 6.1 %collective-permute-start.16 = (bf16[2,32,512]{2,1,0:T(8,128)(2,1)S(1)}, bf16[2,32,512]{2,1,0:T(8,128)(2,1)S(1)}, u32[]{:S(2)}, u32[]{:S(2)}) collective-permute-start(bf16[2,32,512]{2,1,0:T(8,128)(2,1)S(1)} %get-tuple-element.57), channel_id=1, source_target_pairs={{0,12},{1,13},{2,14},{3,15},{4,8},{5,9},{6,10},{7,11},{8,4},{9,5},... | collective-permute-start | bytes 196616 | tf_op jit(solution)/shard_map/ppermute | solution.py:390
  45.3 4.7 %collective-permute-start.17 = (bf16[2,32,512]{2,1,0:T(8,128)(2,1)S(1)}, bf16[2,32,512]{2,1,0:T(8,128)(2,1)S(1)}, u32[]{:S(2)}, u32[]{:S(2)}) collective-permute-start(bf16[2,32,512]{2,1,0:T(8,128)(2,1)S(1)} %get-tuple-element.58), channel_id=1, source_target_pairs={{0,4},{1,5},{2,6},{3,7},{4,0},{5,1},{6,2},{7,3},{8,12},{9,13},{10,... | collective-permute-start | bytes 196616 | tf_op jit(solution)/shard_map/ppermute | solution.py:390
  45.4 7.1 %collective-permute-start.18 = (bf16[2,32,512]{2,1,0:T(8,128)(2,1)S(1)}, bf16[2,32,512]{2,1,0:T(8,128)(2,1)S(1)}, u32[]{:S(2)}, u32[]{:S(2)}) collective-permute-start(bf16[2,32,512]{2,1,0:T(8,128)(2,1)S(1)} %get-tuple-element.59), channel_id=1, source_target_pairs={{0,14},{1,15},{2,12},{3,13},{4,10},{5,11},{6,8},{7,9},{8,6},{9,7},... | collective-permute-start | bytes 196616 | tf_op jit(solution)/shard_map/ppermute | solution.py:390
  48.5 5.2 %collective-permute-start.19 = (bf16[2,32,512]{2,1,0:T(8,128)(2,1)S(1)}, bf16[2,32,512]{2,1,0:T(8,128)(2,1)S(1)}, u32[]{:S(2)}, u32[]{:S(2)}) collective-permute-start(bf16[2,32,512]{2,1,0:T(8,128)(2,1)S(1)} %get-tuple-element.60), channel_id=1, source_target_pairs={{0,6},{1,7},{2,4},{3,5},{4,2},{5,3},{6,0},{7,1},{8,14},{9,15},{10,... | collective-permute-start | bytes 196616 | tf_op jit(solution)/shard_map/ppermute | solution.py:390
  53.6 1.6 %collective-permute-start.20 = (bf16[8,32,512]{2,1,0:T(8,128)(2,1)S(1)}, bf16[8,32,512]{2,1,0:T(8,128)(2,1)S(1)}, u32[]{:S(2)}, u32[]{:S(2)}) collective-permute-start(bf16[8,32,512]{2,1,0:T(8,128)(2,1)S(1)} %regroup.1), channel_id=1, source_target_pairs={{0,1},{1,0},{2,3},{3,2},{4,5},{5,4},{6,7},{7,6},{8,9},{9,8},{10,11... | collective-permute-start | bytes 786440 | tf_op jit(solution)/shard_map/ppermute | solution.py:390
  57.1 2.0 %collective-permute-start.22 = (bf16[32,3584]{1,0:T(8,128)(2,1)S(1)}, bf16[32,3584]{1,0:T(8,128)(2,1)S(1)}, u32[]{:S(2)}, u32[]{:S(2)}) collective-permute-start(bf16[32,3584]{1,0:T(8,128)(2,1)S(1)} %get-tuple-element.65), channel_id=1, source_target_pairs={{0,1},{1,0},{2,3},{3,2},{4,5},{5,4},{6,7},{7,6},{8,9},{9,8},{10,11... | collective-permute-start | bytes 688136 | tf_op jit(solution)/shard_map/ppermute | solution.py:390
  58.7 1.6 %collective-permute-start.21 = (bf16[32,3584]{1,0:T(8,128)(2,1)S(1)}, bf16[32,3584]{1,0:T(8,128)(2,1)S(1)}, u32[]{:S(2)}, u32[]{:S(2)}) collective-permute-start(bf16[32,3584]{1,0:T(8,128)(2,1)S(1)} %get-tuple-element.63), channel_id=1, source_target_pairs={{0,1},{1,0},{2,3},{3,2},{4,5},{5,4},{6,7},{7,6},{8,9},{9,8},{10,11... | collective-permute-start | bytes 688136 | tf_op jit(solution)/shard_map/ppermute | solution.py:390
  59.2 4.4 %collective-permute-start.25 = (bf16[8,3584]{1,0:T(8,128)(2,1)S(1)}, bf16[8,3584]{1,0:T(8,128)(2,1)S(1)}, u32[]{:S(2)}, u32[]{:S(2)}) collective-permute-start(bf16[8,3584]{1,0:T(8,128)(2,1)S(1)} %get-tuple-element.73), channel_id=1, source_target_pairs={{0,2},{1,3},{2,0},{3,1},{4,6},{5,7},{6,4},{7,5},{8,10},{9,11},{10,... | collective-permute-start | bytes 172040 | tf_op jit(solution)/shard_map/ppermute | solution.py:390
  60.4 4.3 %collective-permute-start.26 = (bf16[8,3584]{1,0:T(8,128)(2,1)S(1)}, bf16[8,3584]{1,0:T(8,128)(2,1)S(1)}, u32[]{:S(2)}, u32[]{:S(2)}) collective-permute-start(bf16[8,3584]{1,0:T(8,128)(2,1)S(1)} %get-tuple-element.74), channel_id=1, source_target_pairs={{0,2},{1,3},{2,0},{3,1},{4,6},{5,7},{6,4},{7,5},{8,10},{9,11},{10,... | collective-permute-start | bytes 172040 | tf_op jit(solution)/shard_map/ppermute | solution.py:390
  61.5 6.0 %collective-permute-start.23 = (bf16[8,7168]{1,0:T(8,128)(2,1)S(1)}, bf16[8,7168]{1,0:T(8,128)(2,1)S(1)}, u32[]{:S(2)}, u32[]{:S(2)}) collective-permute-start(bf16[8,7168]{1,0:T(8,128)(2,1)S(1)} %get-tuple-element.68), channel_id=1, source_target_pairs={{0,4},{1,5},{2,6},{3,7},{4,0},{5,1},{6,2},{7,3},{8,12},{9,13},{10,... | collective-permute-start | bytes 344072 | tf_op jit(solution)/shard_map/ppermute | solution.py:390
  64.8 7.2 %collective-permute-start.27 = (bf16[4,7168]{1,0:T(4,128)(2,1)S(1)}, bf16[4,7168]{1,0:T(4,128)(2,1)S(1)}, u32[]{:S(2)}, u32[]{:S(2)}) collective-permute-start(bf16[4,7168]{1,0:T(4,128)(2,1)S(1)} %get-tuple-element.75), channel_id=1, source_target_pairs={{0,8},{1,9},{2,10},{3,11},{4,12},{5,13},{6,14},{7,15},{8,0},{9,1},... | collective-permute-start | bytes 172040 | tf_op jit(solution)/shard_map/ppermute | solution.py:390
  65.5 6.4 %collective-permute-start.28 = (bf16[4,7168]{1,0:T(4,128)(2,1)S(1)}, bf16[4,7168]{1,0:T(4,128)(2,1)S(1)}, u32[]{:S(2)}, u32[]{:S(2)}) collective-permute-start(bf16[4,7168]{1,0:T(4,128)(2,1)S(1)} %get-tuple-element.76), channel_id=1, source_target_pairs={{0,12},{1,13},{2,14},{3,15},{4,8},{5,9},{6,10},{7,11},{8,4},{9,5},... | collective-permute-start | bytes 172040 | tf_op jit(solution)/shard_map/ppermute | solution.py:390
  67.5 4.5 %collective-permute-start.24 = (bf16[4,7168]{1,0:T(4,128)(2,1)S(1)}, bf16[4,7168]{1,0:T(4,128)(2,1)S(1)}, u32[]{:S(2)}, u32[]{:S(2)}) collective-permute-start(bf16[4,7168]{1,0:T(4,128)(2,1)S(1)} %get-tuple-element.70), channel_id=1, source_target_pairs={{0,2},{1,3},{2,0},{3,1},{4,6},{5,7},{6,4},{7,5},{8,10},{9,11},{10,... | collective-permute-start | bytes 172040 | tf_op jit(solution)/shard_map/ppermute | solution.py:390
  (11 other events, 109.8 us)

commit v9 on v8

--- a/solution.py
+++ b/solution.py
@@ -51,6 +51,10 @@
 
 def shape(*dims, dtype=jnp.bfloat16):
     return jax.ShapeDtypeStruct(dims, dtype)
+
+
+def mask(k):
+    return k ^ (k.bit_count() & 1)
 
 
 def far_first(devices, step):
@@ -387,7 +391,8 @@
     def swap(block, k):
         if k == 0:
             return block
-        return lax.ppermute(block, "row", [(i, i ^ k) for i in range(devices)])
+        flip_bits = k if k == 1 else mask(k)
+        return lax.ppermute(block, "row", [(i, i ^ flip_bits) for i in range(devices)])
 
     far_weights = [swap(w_uq, 1), swap(w_uk, 1)]
     tables, near = join(rotary(lengths), [q_latent, swap(q_latent, 2)])

time: 72.8 us -> 73 us (level)
  waiting for transfers between devices: 23.9 us -> 25.1 us
  starting transfers between devices: 34.8 us -> 33.8 us
    ppermute x29, waiting for transfers between devices: 23.9 us -> 25.1 us  [swap(): lax.ppermute(block, 'row', [(i, i ^ flip_bits) for i in range(devices)])]
    ppermute x29, starting transfers between devices: 34.8 us -> 33.8 us  [swap(): lax.ppermute(block, 'row', [(i, i ^ flip_bits) for i in range(devices)])]
  transfers between devices with their start and end apart: 29 -> 29, of which waited for: 16 -> 14; matrix products, arithmetic and copies ran while one was open for 0% -> 0% of each run, Pallas kernels for 5% -> 5%
where the time goes in v9:
time: 73 us; the launch traced here: 72.9 us
  starting transfers between devices  33.8 us (46%)
  waiting for transfers between devices  25.1 us (34%)
  Pallas kernels  13 us (18%)
    ppermute x29, starting transfers between devices, swap(): lax.ppermute(block, 'row', [(i, i ^ flip_bits) for i in range(devices)])  33.8 us
    ppermute x29, waiting for transfers between devices, swap(): lax.ppermute(block, 'row', [(i, i ^ flip_bits) for i in range(devices)])  25.1 us
    pallas_call x14, Pallas kernels, run(): pl.pallas_call(kernel, out_shape=out_shape, in_specs=smem + [in_vmem()] *...  13 us
  transfers between devices with their start and end apart: 29, of which 14 were waited for; matrix products, arithmetic and copies ran while one was open for 0% of the time, Pallas kernels for 5%

profile of v9, /device:TPU:0, one launch (start us, length us, event | category | flops | bytes accessed | tf_op | source)
XLA Modules:
  0.0 72.9 jit_solution(16545490961284692329)
XLA Ops:
  0.5 2.6 %collective-permute-start = (bf16[4,1536]{1,0:T(4,128)(2,1)}, bf16[4,1536]{1,0:T(4,128)(2,1)S(1)}, u32[]{:S(2)}, u32[]{:S(2)}) collective-permute-start(bf16[4,1536]{1,0:T(4,128)(2,1)} %refs_0_.1), channel_id=1, source_target_pairs={{0,3},{1,2},{2,1},{3,0},{4,7},{5,6},{6,5},{7,4},{8,11},{9,10},{10,... | collective-permute-start | bytes 36872 | tf_op jit(solution)/shard_map/ppermute | solution.py:395
  3.2 0.7 copy-done.4
  4.8 2.9 %collective-permute-start.3 = (bf16[8,1536]{1,0:T(8,128)(2,1)S(1)}, bf16[8,1536]{1,0:T(8,128)(2,1)S(1)}, u32[]{:S(2)}, u32[]{:S(2)}) collective-permute-start(bf16[8,1536]{1,0:T(8,128)(2,1)S(1)} %get-tuple-element.45.refs_0_), channel_id=1, source_target_pairs={{0,9},{1,8},{2,11},{3,10},{4,13},{5,12},{6,15},{7,14},{8,1},{9,0},... | collective-permute-start | bytes 73736 | tf_op jit(solution)/shard_map/ppermute | solution.py:395
  7.7 1.4 %collective-permute-start.2 = (bf16[8,1536]{1,0:T(8,128)(2,1)S(1)}, bf16[8,1536]{1,0:T(8,128)(2,1)S(1)}, u32[]{:S(2)}, u32[]{:S(2)}) collective-permute-start(bf16[8,1536]{1,0:T(8,128)(2,1)S(1)} %get-tuple-element.45.refs_0_), channel_id=1, source_target_pairs={{0,12},{1,13},{2,14},{3,15},{4,8},{5,9},{6,10},{7,11},{8,4},{9,5},... | collective-permute-start | bytes 73736 | tf_op jit(solution)/shard_map/ppermute | solution.py:395
  9.3 4.2 %collective-permute-done.2.refs_2_ = bf16[8,1536]{1,0:T(8,128)(2,1)S(1)} collective-permute-done((bf16[8,1536]{1,0:T(8,128)(2,1)S(1)}, bf16[8,1536]{1,0:T(8,128)(2,1)S(1)}, u32[]{:S(2)}, u32[]{:S(2)}) %collective-permute-start.2) | collective-permute-done | bytes 24608 | tf_op jit(solution)/shard_map/ppermute | solution.py:395
  13.5 2.3 %project.1 = (bf16[2,144,128]{2,1,0:T(8,128)(2,1)S(1)}, bf16[2,144,128]{2,1,0:T(8,128)(2,1)S(1)}, bf16[2,144,128]{2,1,0:T(8,128)(2,1)S(1)}, bf16[2,144,128]{2,1,...) custom-call(bf16[8,1536]{1,0:T(8,128)(2,1)S(1)} %get-tuple-element.4, ...), custom_call_target="tpu_custom_call" | custom-call | flops 23000000512 | tf_op jit(solution)/shard_map/project/pallas_call | solution.py:36
  16.4 2.2 %collective-permute-start.7 = (bf16[2,144,128]{2,1,0:T(8,128)(2,1)S(1)}, bf16[2,144,128]{2,1,0:T(8,128)(2,1)S(1)}, u32[]{:S(2)}, u32[]{:S(2)}) collective-permute-start(bf16[2,144,128]{2,1,0:T(8,128)(2,1)S(1)} %get-tuple-element.48), channel_id=1, source_target_pairs={{0,10},{1,11},{2,8},{3,9},{4,14},{5,15},{6,12},{7,13},{8,2},{9,3},... | collective-permute-start | bytes 221192 | tf_op jit(solution)/shard_map/ppermute | solution.py:395
  18.6 1.1 %collective-permute-start.8 = (bf16[2,144,128]{2,1,0:T(8,128)(2,1)S(1)}, bf16[2,144,128]{2,1,0:T(8,128)(2,1)S(1)}, u32[]{:S(2)}, u32[]{:S(2)}) collective-permute-start(bf16[2,144,128]{2,1,0:T(8,128)(2,1)S(1)} %get-tuple-element.49), channel_id=1, source_target_pairs={{0,3},{1,2},{2,1},{3,0},{4,7},{5,6},{6,5},{7,4},{8,11},{9,10},{10,... | collective-permute-start | bytes 221192 | tf_op jit(solution)/shard_map/ppermute | solution.py:395
  19.7 1.6 %collective-permute-start.9 = (bf16[2,144,128]{2,1,0:T(8,128)(2,1)S(1)}, bf16[2,144,128]{2,1,0:T(8,128)(2,1)S(1)}, u32[]{:S(2)}, u32[]{:S(2)}) collective-permute-start(bf16[2,144,128]{2,1,0:T(8,128)(2,1)S(1)} %get-tuple-element.50), channel_id=1, source_target_pairs={{0,12},{1,13},{2,14},{3,15},{4,8},{5,9},{6,10},{7,11},{8,4},{9,5},... | collective-permute-start | bytes 221192 | tf_op jit(solution)/shard_map/ppermute | solution.py:395
  21.4 0.7 collective-permute-done.6.refs_0_
  22.1 6.0 %collective-permute-start.11 = (bf16[2,144,128]{2,1,0:T(8,128)(2,1)S(1)}, bf16[2,144,128]{2,1,0:T(8,128)(2,1)S(1)}, u32[]{:S(2)}, u32[]{:S(2)}) collective-permute-start(bf16[2,144,128]{2,1,0:T(8,128)(2,1)S(1)} %get-tuple-element.52), channel_id=1, source_target_pairs={{0,15},{1,14},{2,13},{3,12},{4,11},{5,10},{6,9},{7,8},{8,7},{9,6},... | collective-permute-start | bytes 221192 | tf_op jit(solution)/shard_map/ppermute | solution.py:395
  28.1 1.7 %flip.1.flip_ref = bf16[4,1536,512]{2,1,0:T(8,128)(2,1)S(1)} custom-call(bf16[4,576,1536]{2,1,0:T(8,128)(2,1)S(1)} %bitcast.5, bf16[2,144,128]{2,1,0:T(8,128)(2,1)S(1)} %get-tuple-element.46.after_ref.refs_7_), custom_call_target="tpu_custom_call" | custom-call | flops 4600000000 | tf_op jit(solution)/shard_map/flip/pallas_call | solution.py:36
  30.3 3.0 %collective-permute-done.12.refs_6_ = bf16[2,144,128]{2,1,0:T(8,128)(2,1)S(1)} collective-permute-done((bf16[2,144,128]{2,1,0:T(8,128)(2,1)S(1)}, bf16[2,144,128]{2,1,0:T(8,128)(2,1)S(1)}, u32[]{:S(2)}, u32[]{:S(2)}) %collective-permute-start.12) | collective-permute-done | bytes 73760 | tf_op jit(solution)/shard_map/ppermute | solution.py:395
  33.3 4.3 %attend.1 = (bf16[2,32,512]{2,1,0:T(8,128)(2,1)S(1)}, bf16[2,32,512]{2,1,0:T(8,128)(2,1)S(1)}, bf16[2,32,512]{2,1,0:T(8,128)(2,1)S(1)}, bf16[2,32,512]{2,1,0:T(8...) custom-call(s32[4]{0:T(128)S(1)} %copy-done.5, ...), custom_call_target="tpu_custom_call" | custom-call | flops 11500000256 | tf_op jit(solution)/shard_map/attend/pallas_call | solution.py:36
  37.7 1.0 %collective-permute-start.13 = (bf16[2,32,512]{2,1,0:T(8,128)(2,1)S(1)}, bf16[2,32,512]{2,1,0:T(8,128)(2,1)S(1)}, u32[]{:S(2)}, u32[]{:S(2)}) collective-permute-start(bf16[2,32,512]{2,1,0:T(8,128)(2,1)S(1)} %get-tuple-element.54), channel_id=1, source_target_pairs={{0,9},{1,8},{2,11},{3,10},{4,13},{5,12},{6,15},{7,14},{8,1},{9,0},... | collective-permute-start | bytes 196616 | tf_op jit(solution)/shard_map/ppermute | solution.py:395
  38.7 1.8 %collective-permute-start.14 = (bf16[2,32,512]{2,1,0:T(8,128)(2,1)S(1)}, bf16[2,32,512]{2,1,0:T(8,128)(2,1)S(1)}, u32[]{:S(2)}, u32[]{:S(2)}) collective-permute-start(bf16[2,32,512]{2,1,0:T(8,128)(2,1)S(1)} %get-tuple-element.55), channel_id=1, source_target_pairs={{0,10},{1,11},{2,8},{3,9},{4,14},{5,15},{6,12},{7,13},{8,2},{9,3},... | collective-permute-start | bytes 196616 | tf_op jit(solution)/shard_map/ppermute | solution.py:395
  40.5 1.1 %collective-permute-start.15 = (bf16[2,32,512]{2,1,0:T(8,128)(2,1)S(1)}, bf16[2,32,512]{2,1,0:T(8,128)(2,1)S(1)}, u32[]{:S(2)}, u32[]{:S(2)}) collective-permute-start(bf16[2,32,512]{2,1,0:T(8,128)(2,1)S(1)} %get-tuple-element.56), channel_id=1, source_target_pairs={{0,3},{1,2},{2,1},{3,0},{4,7},{5,6},{6,5},{7,4},{8,11},{9,10},{10,... | collective-permute-start | bytes 196616 | tf_op jit(solution)/shard_map/ppermute | solution.py:395
  41.6 2.4 %collective-permute-start.16 = (bf16[2,32,512]{2,1,0:T(8,128)(2,1)S(1)}, bf16[2,32,512]{2,1,0:T(8,128)(2,1)S(1)}, u32[]{:S(2)}, u32[]{:S(2)}) collective-permute-start(bf16[2,32,512]{2,1,0:T(8,128)(2,1)S(1)} %get-tuple-element.57), channel_id=1, source_target_pairs={{0,12},{1,13},{2,14},{3,15},{4,8},{5,9},{6,10},{7,11},{8,4},{9,5},... | collective-permute-start | bytes 196616 | tf_op jit(solution)/shard_map/ppermute | solution.py:395
  44.0 3.3 %collective-permute-start.18 = (bf16[2,32,512]{2,1,0:T(8,128)(2,1)S(1)}, bf16[2,32,512]{2,1,0:T(8,128)(2,1)S(1)}, u32[]{:S(2)}, u32[]{:S(2)}) collective-permute-start(bf16[2,32,512]{2,1,0:T(8,128)(2,1)S(1)} %get-tuple-element.59), channel_id=1, source_target_pairs={{0,15},{1,14},{2,13},{3,12},{4,11},{5,10},{6,9},{7,8},{8,7},{9,6},... | collective-permute-start | bytes 196616 | tf_op jit(solution)/shard_map/ppermute | solution.py:395
  47.3 1.7 %collective-permute-done.14.refs_1_ = bf16[2,32,512]{2,1,0:T(8,128)(2,1)S(1)} collective-permute-done((bf16[2,32,512]{2,1,0:T(8,128)(2,1)S(1)}, bf16[2,32,512]{2,1,0:T(8,128)(2,1)S(1)}, u32[]{:S(2)}, u32[]{:S(2)}) %collective-permute-start.14) | collective-permute-done | bytes 65568 | tf_op jit(solution)/shard_map/ppermute | solution.py:395
  49.4 1.7 %collective-permute-done.18.refs_5_ = bf16[2,32,512]{2,1,0:T(8,128)(2,1)S(1)} collective-permute-done((bf16[2,32,512]{2,1,0:T(8,128)(2,1)S(1)}, bf16[2,32,512]{2,1,0:T(8,128)(2,1)S(1)}, u32[]{:S(2)}, u32[]{:S(2)}) %collective-permute-start.18) | collective-permute-done | bytes 65568 | tf_op jit(solution)/shard_map/ppermute | solution.py:395
  51.1 3.1 %collective-permute-done.19.refs_6_ = bf16[2,32,512]{2,1,0:T(8,128)(2,1)S(1)} collective-permute-done((bf16[2,32,512]{2,1,0:T(8,128)(2,1)S(1)}, bf16[2,32,512]{2,1,0:T(8,128)(2,1)S(1)}, u32[]{:S(2)}, u32[]{:S(2)}) %collective-permute-start.19) | collective-permute-done | bytes 65568 | tf_op jit(solution)/shard_map/ppermute | solution.py:395
  54.3 1.5 %collective-permute-done.20.refs_8_ = bf16[8,32,512]{2,1,0:T(8,128)(2,1)S(1)} collective-permute-done((bf16[8,32,512]{2,1,0:T(8,128)(2,1)S(1)}, bf16[8,32,512]{2,1,0:T(8,128)(2,1)S(1)}, u32[]{:S(2)}, u32[]{:S(2)}) %collective-permute-start.20) | collective-permute-done | bytes 262176 | tf_op jit(solution)/shard_map/ppermute | solution.py:395
  56.3 1.4 %terms.3 = (f32[32,3584]{1,0:T(8,128)S(1)}, bf16[32,3584]{1,0:T(8,128)(2,1)S(1)}) custom-call(bf16[64,1024]{1,0:T(8,128)(2,1)S(1)} %values.1.val_ref, bf16[1024,7168]{1,0:T(8,128)(2,1)S(1)} %bitcast.2), custom_call_target="tpu_custom_call" | custom-call | flops 6899999744 | tf_op jit(solution)/shard_map/terms/pallas_call | solution.py:36
  57.9 1.4 %terms.2 = (f32[32,3584]{1,0:T(8,128)S(1)}, bf16[32,3584]{1,0:T(8,128)(2,1)S(1)}) custom-call(bf16[64,1024]{1,0:T(8,128)(2,1)S(1)} %values.1.val_ref, bf16[1024,7168]{1,0:T(8,128)(2,1)S(1)} %bitcast.2), custom_call_target="tpu_custom_call" | custom-call | flops 6899999744 | tf_op jit(solution)/shard_map/terms/pallas_call | solution.py:36
  60.9 0.8 %collective-permute-start.26 = (bf16[8,3584]{1,0:T(8,128)(2,1)S(1)}, bf16[8,3584]{1,0:T(8,128)(2,1)S(1)}, u32[]{:S(2)}, u32[]{:S(2)}) collective-permute-start(bf16[8,3584]{1,0:T(8,128)(2,1)S(1)} %get-tuple-element.74), channel_id=1, source_target_pairs={{0,3},{1,2},{2,1},{3,0},{4,7},{5,6},{6,5},{7,4},{8,11},{9,10},{10,... | collective-permute-start | bytes 172040 | tf_op jit(solution)/shard_map/ppermute | solution.py:395
  61.8 2.0 %collective-permute-done.25.refs_2_ = bf16[8,3584]{1,0:T(8,128)(2,1)S(1)} collective-permute-done((bf16[8,3584]{1,0:T(8,128)(2,1)S(1)}, bf16[8,3584]{1,0:T(8,128)(2,1)S(1)}, u32[]{:S(2)}, u32[]{:S(2)}) %collective-permute-start.25) | collective-permute-done | bytes 57376 | tf_op jit(solution)/shard_map/ppermute | solution.py:395
  63.8 1.2 %collective-permute-done.26.refs_3_ = bf16[8,3584]{1,0:T(8,128)(2,1)S(1)} collective-permute-done((bf16[8,3584]{1,0:T(8,128)(2,1)S(1)}, bf16[8,3584]{1,0:T(8,128)(2,1)S(1)}, u32[]{:S(2)}, u32[]{:S(2)}) %collective-permute-start.26) | collective-permute-done | bytes 57376 | tf_op jit(solution)/shard_map/ppermute | solution.py:395
  65.0 0.8 %collective-permute-start.27 = (bf16[4,7168]{1,0:T(4,128)(2,1)S(1)}, bf16[4,7168]{1,0:T(4,128)(2,1)S(1)}, u32[]{:S(2)}, u32[]{:S(2)}) collective-permute-start(bf16[4,7168]{1,0:T(4,128)(2,1)S(1)} %get-tuple-element.75), channel_id=1, source_target_pairs={{0,9},{1,8},{2,11},{3,10},{4,13},{5,12},{6,15},{7,14},{8,1},{9,0},... | collective-permute-start | bytes 172040 | tf_op jit(solution)/shard_map/ppermute | solution.py:395
  65.8 1.9 %collective-permute-start.28 = (bf16[4,7168]{1,0:T(4,128)(2,1)S(1)}, bf16[4,7168]{1,0:T(4,128)(2,1)S(1)}, u32[]{:S(2)}, u32[]{:S(2)}) collective-permute-start(bf16[4,7168]{1,0:T(4,128)(2,1)S(1)} %get-tuple-element.76), channel_id=1, source_target_pairs={{0,12},{1,13},{2,14},{3,15},{4,8},{5,9},{6,10},{7,11},{8,4},{9,5},... | collective-permute-start | bytes 172040 | tf_op jit(solution)/shard_map/ppermute | solution.py:395
  68.0 4.2 %collective-permute-done.27.refs_2_ = bf16[4,7168]{1,0:T(4,128)(2,1)S(1)} collective-permute-done((bf16[4,7168]{1,0:T(4,128)(2,1)S(1)}, bf16[4,7168]{1,0:T(4,128)(2,1)S(1)}, u32[]{:S(2)}, u32[]{:S(2)}) %collective-permute-start.27) | collective-permute-done | bytes 57376 | tf_op jit(solution)/shard_map/ppermute | solution.py:395
  72.2 0.7 last_sum.1
  (71 shorter events, 5.8 us)
Async XLA Ops:
  0.0 13.5 %collective-permute-start.4 = (bf16[1536,1536]{1,0:T(8,128)(2,1)}, bf16[1536,1536]{1,0:T(8,128)(2,1)S(1)}, u32[]{:S(2)}, u32[]{:S(2)}) collective-permute-start(bf16[1536,1536]{1,0:T(8,128)(2,1)} %refs_4_.1), channel_id=1, source_target_pairs={{0,1},{1,0},{2,3},{3,2},{4,5},{5,4},{6,7},{7,6},{8,9},{9,8},{10,11... | collective-permute-start | bytes 14155784 | tf_op jit(solution)/shard_map/ppermute | solution.py:395
  0.5 13.0 %collective-permute-start.5 = (bf16[8,128,512]{2,1,0:T(8,128)(2,1)}, bf16[8,128,512]{2,1,0:T(8,128)(2,1)S(1)}, u32[]{:S(2)}, u32[]{:S(2)}) collective-permute-start(bf16[8,128,512]{2,1,0:T(8,128)(2,1)} %refs_5_.1), channel_id=1, source_target_pairs={{0,1},{1,0},{2,3},{3,2},{4,5},{5,4},{6,7},{7,6},{8,9},{9,8},{10,11... | collective-permute-start | bytes 3145736 | tf_op jit(solution)/shard_map/ppermute | solution.py:395
  0.5 4.2 %collective-permute-start = (bf16[4,1536]{1,0:T(4,128)(2,1)}, bf16[4,1536]{1,0:T(4,128)(2,1)S(1)}, u32[]{:S(2)}, u32[]{:S(2)}) collective-permute-start(bf16[4,1536]{1,0:T(4,128)(2,1)} %refs_0_.1), channel_id=1, source_target_pairs={{0,3},{1,2},{2,1},{3,0},{4,7},{5,6},{6,5},{7,4},{8,11},{9,10},{10,... | collective-permute-start | bytes 36872 | tf_op jit(solution)/shard_map/ppermute | solution.py:395
  4.8 23.3 %slice-start.4 = ((s8[7077888]{0:T(1024)(128)(4,1)}), s8[4194304]{0:T(1024)(128)(4,1)S(1)}, s32[]{:S(2)}) async-start(s8[7077888]{0:T(1024)(128)(4,1)} %bitcast.3), calls=%async_computation.4 | async-start | bytes 8388608
  4.8 23.3 %slice-start.5 = ((s8[7077888]{0:T(1024)(128)(4,1)}), s8[2883584]{0:T(1024)(128)(4,1)S(1)}, s32[]{:S(2)}) async-start(s8[7077888]{0:T(1024)(128)(4,1)} %bitcast.3), calls=%async_computation.5 | async-start | bytes 5767168
  4.8 4.5 %collective-permute-start.3 = (bf16[8,1536]{1,0:T(8,128)(2,1)S(1)}, bf16[8,1536]{1,0:T(8,128)(2,1)S(1)}, u32[]{:S(2)}, u32[]{:S(2)}) collective-permute-start(bf16[8,1536]{1,0:T(8,128)(2,1)S(1)} %get-tuple-element.45.refs_0_), channel_id=1, source_target_pairs={{0,9},{1,8},{2,11},{3,10},{4,13},{5,12},{6,15},{7,14},{8,1},{9,0},... | collective-permute-start | bytes 73736 | tf_op jit(solution)/shard_map/ppermute | solution.py:395
  7.7 5.8 %collective-permute-start.2 = (bf16[8,1536]{1,0:T(8,128)(2,1)S(1)}, bf16[8,1536]{1,0:T(8,128)(2,1)S(1)}, u32[]{:S(2)}, u32[]{:S(2)}) collective-permute-start(bf16[8,1536]{1,0:T(8,128)(2,1)S(1)} %get-tuple-element.45.refs_0_), channel_id=1, source_target_pairs={{0,12},{1,13},{2,14},{3,15},{4,8},{5,9},{6,10},{7,11},{8,4},{9,5},... | collective-permute-start | bytes 73736 | tf_op jit(solution)/shard_map/ppermute | solution.py:395
  9.1 4.4 %collective-permute-start.1 = (bf16[8,1536]{1,0:T(8,128)(2,1)S(1)}, bf16[8,1536]{1,0:T(8,128)(2,1)S(1)}, u32[]{:S(2)}, u32[]{:S(2)}) collective-permute-start(bf16[8,1536]{1,0:T(8,128)(2,1)S(1)} %get-tuple-element.45.refs_0_), channel_id=1, source_target_pairs={{0,5},{1,4},{2,7},{3,6},{4,1},{5,0},{6,3},{7,2},{8,13},{9,12},{10,... | collective-permute-start | bytes 73736 | tf_op jit(solution)/shard_map/ppermute | solution.py:395
  15.8 6.2 %collective-permute-start.6 = (bf16[2,144,128]{2,1,0:T(8,128)(2,1)S(1)}, bf16[2,144,128]{2,1,0:T(8,128)(2,1)S(1)}, u32[]{:S(2)}, u32[]{:S(2)}) collective-permute-start(bf16[2,144,128]{2,1,0:T(8,128)(2,1)S(1)} %get-tuple-element.47), channel_id=1, source_target_pairs={{0,9},{1,8},{2,11},{3,10},{4,13},{5,12},{6,15},{7,14},{8,1},{9,0},... | collective-permute-start | bytes 221192 | tf_op jit(solution)/shard_map/ppermute | solution.py:395
  16.4 11.7 %collective-permute-start.7 = (bf16[2,144,128]{2,1,0:T(8,128)(2,1)S(1)}, bf16[2,144,128]{2,1,0:T(8,128)(2,1)S(1)}, u32[]{:S(2)}, u32[]{:S(2)}) collective-permute-start(bf16[2,144,128]{2,1,0:T(8,128)(2,1)S(1)} %get-tuple-element.48), channel_id=1, source_target_pairs={{0,10},{1,11},{2,8},{3,9},{4,14},{5,15},{6,12},{7,13},{8,2},{9,3},... | collective-permute-start | bytes 221192 | tf_op jit(solution)/shard_map/ppermute | solution.py:395
  18.6 11.2 %collective-permute-start.8 = (bf16[2,144,128]{2,1,0:T(8,128)(2,1)S(1)}, bf16[2,144,128]{2,1,0:T(8,128)(2,1)S(1)}, u32[]{:S(2)}, u32[]{:S(2)}) collective-permute-start(bf16[2,144,128]{2,1,0:T(8,128)(2,1)S(1)} %get-tuple-element.49), channel_id=1, source_target_pairs={{0,3},{1,2},{2,1},{3,0},{4,7},{5,6},{6,5},{7,4},{8,11},{9,10},{10,... | collective-permute-start | bytes 221192 | tf_op jit(solution)/shard_map/ppermute | solution.py:395
  19.7 10.1 %collective-permute-start.9 = (bf16[2,144,128]{2,1,0:T(8,128)(2,1)S(1)}, bf16[2,144,128]{2,1,0:T(8,128)(2,1)S(1)}, u32[]{:S(2)}, u32[]{:S(2)}) collective-permute-start(bf16[2,144,128]{2,1,0:T(8,128)(2,1)S(1)} %get-tuple-element.50), channel_id=1, source_target_pairs={{0,12},{1,13},{2,14},{3,15},{4,8},{5,9},{6,10},{7,11},{8,4},{9,5},... | collective-permute-start | bytes 221192 | tf_op jit(solution)/shard_map/ppermute | solution.py:395
  21.4 8.4 %collective-permute-start.10 = (bf16[2,144,128]{2,1,0:T(8,128)(2,1)S(1)}, bf16[2,144,128]{2,1,0:T(8,128)(2,1)S(1)}, u32[]{:S(2)}, u32[]{:S(2)}) collective-permute-start(bf16[2,144,128]{2,1,0:T(8,128)(2,1)S(1)} %get-tuple-element.51), channel_id=1, source_target_pairs={{0,5},{1,4},{2,7},{3,6},{4,1},{5,0},{6,3},{7,2},{8,13},{9,12},{10,... | collective-permute-start | bytes 221192 | tf_op jit(solution)/shard_map/ppermute | solution.py:395
  22.1 8.2 %collective-permute-start.11 = (bf16[2,144,128]{2,1,0:T(8,128)(2,1)S(1)}, bf16[2,144,128]{2,1,0:T(8,128)(2,1)S(1)}, u32[]{:S(2)}, u32[]{:S(2)}) collective-permute-start(bf16[2,144,128]{2,1,0:T(8,128)(2,1)S(1)} %get-tuple-element.52), channel_id=1, source_target_pairs={{0,15},{1,14},{2,13},{3,12},{4,11},{5,10},{6,9},{7,8},{8,7},{9,6},... | collective-permute-start | bytes 221192 | tf_op jit(solution)/shard_map/ppermute | solution.py:395
  28.1 5.3 %collective-permute-start.12 = (bf16[2,144,128]{2,1,0:T(8,128)(2,1)S(1)}, bf16[2,144,128]{2,1,0:T(8,128)(2,1)S(1)}, u32[]{:S(2)}, u32[]{:S(2)}) collective-permute-start(bf16[2,144,128]{2,1,0:T(8,128)(2,1)S(1)} %get-tuple-element.53), channel_id=1, source_target_pairs={{0,6},{1,7},{2,4},{3,5},{4,2},{5,3},{6,0},{7,1},{8,14},{9,15},{10,... | collective-permute-start | bytes 221192 | tf_op jit(solution)/shard_map/ppermute | solution.py:395
  33.3 23.0 %slice-start.1 = ((s8[14680064]{0:T(1024)(128)(4,1)}), s8[4194304]{0:T(1024)(128)(4,1)S(1)}, s32[]{:S(2)}) async-start(s8[14680064]{0:T(1024)(128)(4,1)} %bitcast.1), calls=%async_computation.1 | async-start | bytes 8388608
  37.7 6.3 %collective-permute-start.13 = (bf16[2,32,512]{2,1,0:T(8,128)(2,1)S(1)}, bf16[2,32,512]{2,1,0:T(8,128)(2,1)S(1)}, u32[]{:S(2)}, u32[]{:S(2)}) collective-permute-start(bf16[2,32,512]{2,1,0:T(8,128)(2,1)S(1)} %get-tuple-element.54), channel_id=1, source_target_pairs={{0,9},{1,8},{2,11},{3,10},{4,13},{5,12},{6,15},{7,14},{8,1},{9,0},... | collective-permute-start | bytes 196616 | tf_op jit(solution)/shard_map/ppermute | solution.py:395
  38.7 10.3 %collective-permute-start.14 = (bf16[2,32,512]{2,1,0:T(8,128)(2,1)S(1)}, bf16[2,32,512]{2,1,0:T(8,128)(2,1)S(1)}, u32[]{:S(2)}, u32[]{:S(2)}) collective-permute-start(bf16[2,32,512]{2,1,0:T(8,128)(2,1)S(1)} %get-tuple-element.55), channel_id=1, source_target_pairs={{0,10},{1,11},{2,8},{3,9},{4,14},{5,15},{6,12},{7,13},{8,2},{9,3},... | collective-permute-start | bytes 196616 | tf_op jit(solution)/shard_map/ppermute | solution.py:395
  40.5 8.5 %collective-permute-start.15 = (bf16[2,32,512]{2,1,0:T(8,128)(2,1)S(1)}, bf16[2,32,512]{2,1,0:T(8,128)(2,1)S(1)}, u32[]{:S(2)}, u32[]{:S(2)}) collective-permute-start(bf16[2,32,512]{2,1,0:T(8,128)(2,1)S(1)} %get-tuple-element.56), channel_id=1, source_target_pairs={{0,3},{1,2},{2,1},{3,0},{4,7},{5,6},{6,5},{7,4},{8,11},{9,10},{10,... | collective-permute-start | bytes 196616 | tf_op jit(solution)/shard_map/ppermute | solution.py:395
  41.6 7.4 %collective-permute-start.16 = (bf16[2,32,512]{2,1,0:T(8,128)(2,1)S(1)}, bf16[2,32,512]{2,1,0:T(8,128)(2,1)S(1)}, u32[]{:S(2)}, u32[]{:S(2)}) collective-permute-start(bf16[2,32,512]{2,1,0:T(8,128)(2,1)S(1)} %get-tuple-element.57), channel_id=1, source_target_pairs={{0,12},{1,13},{2,14},{3,15},{4,8},{5,9},{6,10},{7,11},{8,4},{9,5},... | collective-permute-start | bytes 196616 | tf_op jit(solution)/shard_map/ppermute | solution.py:395
  44.0 5.4 %collective-permute-start.17 = (bf16[2,32,512]{2,1,0:T(8,128)(2,1)S(1)}, bf16[2,32,512]{2,1,0:T(8,128)(2,1)S(1)}, u32[]{:S(2)}, u32[]{:S(2)}) collective-permute-start(bf16[2,32,512]{2,1,0:T(8,128)(2,1)S(1)} %get-tuple-element.58), channel_id=1, source_target_pairs={{0,5},{1,4},{2,7},{3,6},{4,1},{5,0},{6,3},{7,2},{8,13},{9,12},{10,... | collective-permute-start | bytes 196616 | tf_op jit(solution)/shard_map/ppermute | solution.py:395
  44.0 7.1 %collective-permute-start.18 = (bf16[2,32,512]{2,1,0:T(8,128)(2,1)S(1)}, bf16[2,32,512]{2,1,0:T(8,128)(2,1)S(1)}, u32[]{:S(2)}, u32[]{:S(2)}) collective-permute-start(bf16[2,32,512]{2,1,0:T(8,128)(2,1)S(1)} %get-tuple-element.59), channel_id=1, source_target_pairs={{0,15},{1,14},{2,13},{3,12},{4,11},{5,10},{6,9},{7,8},{8,7},{9,6},... | collective-permute-start | bytes 196616 | tf_op jit(solution)/shard_map/ppermute | solution.py:395
  49.0 5.2 %collective-permute-start.19 = (bf16[2,32,512]{2,1,0:T(8,128)(2,1)S(1)}, bf16[2,32,512]{2,1,0:T(8,128)(2,1)S(1)}, u32[]{:S(2)}, u32[]{:S(2)}) collective-permute-start(bf16[2,32,512]{2,1,0:T(8,128)(2,1)S(1)} %get-tuple-element.60), channel_id=1, source_target_pairs={{0,6},{1,7},{2,4},{3,5},{4,2},{5,3},{6,0},{7,1},{8,14},{9,15},{10,... | collective-permute-start | bytes 196616 | tf_op jit(solution)/shard_map/ppermute | solution.py:395
  54.2 1.6 %collective-permute-start.20 = (bf16[8,32,512]{2,1,0:T(8,128)(2,1)S(1)}, bf16[8,32,512]{2,1,0:T(8,128)(2,1)S(1)}, u32[]{:S(2)}, u32[]{:S(2)}) collective-permute-start(bf16[8,32,512]{2,1,0:T(8,128)(2,1)S(1)} %regroup.1), channel_id=1, source_target_pairs={{0,1},{1,0},{2,3},{3,2},{4,5},{5,4},{6,7},{7,6},{8,9},{9,8},{10,11... | collective-permute-start | bytes 786440 | tf_op jit(solution)/shard_map/ppermute | solution.py:395
  57.7 2.0 %collective-permute-start.22 = (bf16[32,3584]{1,0:T(8,128)(2,1)S(1)}, bf16[32,3584]{1,0:T(8,128)(2,1)S(1)}, u32[]{:S(2)}, u32[]{:S(2)}) collective-permute-start(bf16[32,3584]{1,0:T(8,128)(2,1)S(1)} %get-tuple-element.65), channel_id=1, source_target_pairs={{0,1},{1,0},{2,3},{3,2},{4,5},{5,4},{6,7},{7,6},{8,9},{9,8},{10,11... | collective-permute-start | bytes 688136 | tf_op jit(solution)/shard_map/ppermute | solution.py:395
  59.3 1.6 %collective-permute-start.21 = (bf16[32,3584]{1,0:T(8,128)(2,1)S(1)}, bf16[32,3584]{1,0:T(8,128)(2,1)S(1)}, u32[]{:S(2)}, u32[]{:S(2)}) collective-permute-start(bf16[32,3584]{1,0:T(8,128)(2,1)S(1)} %get-tuple-element.63), channel_id=1, source_target_pairs={{0,1},{1,0},{2,3},{3,2},{4,5},{5,4},{6,7},{7,6},{8,9},{9,8},{10,11... | collective-permute-start | bytes 688136 | tf_op jit(solution)/shard_map/ppermute | solution.py:395
  59.8 4.0 %collective-permute-start.25 = (bf16[8,3584]{1,0:T(8,128)(2,1)S(1)}, bf16[8,3584]{1,0:T(8,128)(2,1)S(1)}, u32[]{:S(2)}, u32[]{:S(2)}) collective-permute-start(bf16[8,3584]{1,0:T(8,128)(2,1)S(1)} %get-tuple-element.73), channel_id=1, source_target_pairs={{0,3},{1,2},{2,1},{3,0},{4,7},{5,6},{6,5},{7,4},{8,11},{9,10},{10,... | collective-permute-start | bytes 172040 | tf_op jit(solution)/shard_map/ppermute | solution.py:395
  60.9 4.0 %collective-permute-start.26 = (bf16[8,3584]{1,0:T(8,128)(2,1)S(1)}, bf16[8,3584]{1,0:T(8,128)(2,1)S(1)}, u32[]{:S(2)}, u32[]{:S(2)}) collective-permute-start(bf16[8,3584]{1,0:T(8,128)(2,1)S(1)} %get-tuple-element.74), channel_id=1, source_target_pairs={{0,3},{1,2},{2,1},{3,0},{4,7},{5,6},{6,5},{7,4},{8,11},{9,10},{10,... | collective-permute-start | bytes 172040 | tf_op jit(solution)/shard_map/ppermute | solution.py:395
  61.7 6.0 %collective-permute-start.23 = (bf16[8,7168]{1,0:T(8,128)(2,1)S(1)}, bf16[8,7168]{1,0:T(8,128)(2,1)S(1)}, u32[]{:S(2)}, u32[]{:S(2)}) collective-permute-start(bf16[8,7168]{1,0:T(8,128)(2,1)S(1)} %get-tuple-element.68), channel_id=1, source_target_pairs={{0,5},{1,4},{2,7},{3,6},{4,1},{5,0},{6,3},{7,2},{8,13},{9,12},{10,... | collective-permute-start | bytes 344072 | tf_op jit(solution)/shard_map/ppermute | solution.py:395
  65.0 7.2 %collective-permute-start.27 = (bf16[4,7168]{1,0:T(4,128)(2,1)S(1)}, bf16[4,7168]{1,0:T(4,128)(2,1)S(1)}, u32[]{:S(2)}, u32[]{:S(2)}) collective-permute-start(bf16[4,7168]{1,0:T(4,128)(2,1)S(1)} %get-tuple-element.75), channel_id=1, source_target_pairs={{0,9},{1,8},{2,11},{3,10},{4,13},{5,12},{6,15},{7,14},{8,1},{9,0},... | collective-permute-start | bytes 172040 | tf_op jit(solution)/shard_map/ppermute | solution.py:395
  65.8 6.4 %collective-permute-start.28 = (bf16[4,7168]{1,0:T(4,128)(2,1)S(1)}, bf16[4,7168]{1,0:T(4,128)(2,1)S(1)}, u32[]{:S(2)}, u32[]{:S(2)}) collective-permute-start(bf16[4,7168]{1,0:T(4,128)(2,1)S(1)} %get-tuple-element.76), channel_id=1, source_target_pairs={{0,12},{1,13},{2,14},{3,15},{4,8},{5,9},{6,10},{7,11},{8,4},{9,5},... | collective-permute-start | bytes 172040 | tf_op jit(solution)/shard_map/ppermute | solution.py:395
  67.8 4.4 %collective-permute-start.24 = (bf16[4,7168]{1,0:T(4,128)(2,1)S(1)}, bf16[4,7168]{1,0:T(4,128)(2,1)S(1)}, u32[]{:S(2)}, u32[]{:S(2)}) collective-permute-start(bf16[4,7168]{1,0:T(4,128)(2,1)S(1)} %get-tuple-element.70), channel_id=1, source_target_pairs={{0,3},{1,2},{2,1},{3,0},{4,7},{5,6},{6,5},{7,4},{8,11},{9,10},{10,... | collective-permute-start | bytes 172040 | tf_op jit(solution)/shard_map/ppermute | solution.py:395
  (11 other events, 113.6 us)

commit v10 on v9

--- a/solution.py
+++ b/solution.py
@@ -61,14 +61,16 @@
     return sorted(range(0, devices, step), key=lambda k: -k.bit_length())
 
 
+def far_chips(devices):
+    return [k for k in far_first(devices, 2) if k > Y + Z1]
+
+
 def chip_order(devices):
-    chips = far_first(devices, 2)
-    far = chips[: len(chips) // 2]
-    near = sorted(chips[len(chips) // 2 :])[1:]
-    mixed = far[:1]
-    for k, other in zip(far[1:], near):
-        mixed += [k, other]
-    return mixed + [0]
+    return [*far_chips(devices), Y, Y + Z1, Z1, 0]
+
+
+def message_sizes(devices):
+    return [1] * len(far_chips(devices)) + [2, 1, 1]
 
 
 def gathered_order(devices):
@@ -124,7 +126,8 @@
     wide = 2 * count // devices * heads
     width = NOPE + ROPE
     lane = lax.broadcasted_iota(jnp.int32, (wide // 2, LANES), 1)
-    order = chip_order(devices)
+    blocks = [(ref, 2 * i) for ref in out_refs for i in range(ref.shape[0] // 2)]
+    blocks = dict(zip(chip_order(devices), blocks))
     for core, (wq_ref, wk_ref) in enumerate(weights):
         projected = jnp.dot(piece, wq_ref[...], preferred_element_type=jnp.float32)
         for h in range(heads):
@@ -132,21 +135,22 @@
             absorbed = jnp.dot(
                 mine[:, :NOPE].astype(jnp.bfloat16), wk_ref[h], preferred_element_type=jnp.float32
             )
-            at = pl.ds(h, count, stride=heads)
+            spread = pl.ds(h, count, stride=heads)
             for c in range(PIECES):
-                lat_ref[core * PIECES + c, at, :] = absorbed[:, c * LANES : (c + 1) * LANES]
+                lat_ref[core * PIECES + c, spread, :] = absorbed[:, c * LANES : (c + 1) * LANES]
             pe = mine[:, NOPE:]
-            rot_ref[core, at, :] = jnp.concatenate([pe, pe], axis=-1)
+            rot_ref[core, spread, :] = jnp.concatenate([pe, pe], axis=-1)
         for place, k in enumerate(gathered_order(devices)):
-            out_ref = out_refs[order.index(k)]
+            out_ref, at = blocks[k]
+            at += core
             first = place * wide
             for c in range(PIECES):
-                out_ref[core, c * wide : (c + 1) * wide, :] = lat_ref[
+                out_ref[at, c * wide : (c + 1) * wide, :] = lat_ref[
                     core * PIECES + c, first : first + wide, :
                 ].astype(jnp.bfloat16)
             low = rot_ref[core, first : first + wide // 2, :]
             high = rot_ref[core, first + wide // 2 : first + wide, :]
-            out_ref[core, PIECES * wide :, :] = jnp.where(lane < ROPE, low, high).astype(
+            out_ref[at, PIECES * wide :, :] = jnp.where(lane < ROPE, low, high).astype(
                 jnp.bfloat16
             )
 
@@ -159,7 +163,8 @@
         pltpu.VMEM((2 * PIECES, count * heads, LANES), jnp.float32),
         pltpu.VMEM((2, count * heads, LANES), jnp.float32),
     ]
-    out = [shape(2, PIECES * wide + wide // 2, LANES)] * (devices // 2)
+    tall = PIECES * wide + wide // 2
+    out = [shape(2 * size, tall, LANES) for size in message_sizes(devices)]
     kernel = functools.partial(project_kernel, devices)
     return call(kernel, out, 20, "project", scratch)(*pieces, *[resident(w) for w in weights])
 
@@ -174,22 +179,35 @@
     return call(flip_kernel, shape(rows, maxlen, LAT), 4, "flip")(resident(keys), after)
 
 
-def attend_kernel(chips, len_ref, cos_ref, sin_ref, key_ref, flip_ref, new_ref, *refs):
-    q_refs = refs[:chips]
-    out_refs = refs[chips:]
+def forward_kernel(own_ref, passing_ref, out_ref):
+    out_ref[:2] = own_ref[...]
+    out_ref[2:] = passing_ref[2:]
+
+
+def forward(own, passing):
+    return call(forward_kernel, shape(4, *own.shape[1:]), 1, "forward")(own, passing)
+
+
+def arrived(refs):
+    blocks = []
+    for i, ref in enumerate(refs):
+        count = 2 if i == len(refs) - 3 else ref.shape[0]
+        blocks += [(ref, core) for core in range(count)]
+    return blocks
+
+
+def attend_kernel(sizes, len_ref, cos_ref, sin_ref, key_ref, flip_ref, new_ref, *refs):
+    blocks = arrived(refs[: len(sizes)])
+    out_refs = refs[len(sizes) :]
     rows, _, maxlen = key_ref.shape
     wide = out_refs[0].shape[1]
     heads = wide // rows
 
     def query_block(first):
-        blocks = [
-            ref[core, first : first + heads, :].astype(jnp.float32)
-            for ref in q_refs
-            for core in range(2)
-        ]
-        return jnp.concatenate(blocks, axis=0)
-
-    for r in range(rows):
+        parts = [ref[i, first : first + heads, :].astype(jnp.float32) for ref, i in blocks]
+        return jnp.concatenate(parts, axis=0)
+
+    def score(r):
         latent = jnp.concatenate(
             [query_block(c * wide + r * heads) for c in range(PIECES)], axis=-1
         )
@@ -207,7 +225,16 @@
         )
         scores += jnp.dot(rotated, key_ref[r, LAT:, :], preferred_element_type=jnp.float32)
         position = lax.broadcasted_iota(jnp.int32, (1, maxlen), 1)
-        scores = jnp.where(position < len_ref[r], scores, -jnp.inf)
+        return jnp.where(position < len_ref[r], scores, -jnp.inf), own
+
+    back = [(ref, i) for ref in out_refs for i in range(ref.shape[0])]
+    y_at = len(back) - 8
+    back = back[: y_at + 2] + back[y_at + 4 : y_at + 6] + back[y_at + 2 : y_at + 4] + back[-2:]
+    ahead = score(0)
+    for r in range(rows):
+        scores, own = ahead
+        if r + 1 < rows:
+            ahead = score(r + 1)
         peak = jnp.maximum(jnp.max(scores, axis=-1, keepdims=True), own)
         expo = jnp.exp2((scores - peak) * SCALE)
         own_expo = jnp.exp2((own - peak) * SCALE)
@@ -215,41 +242,52 @@
         weights = (expo * inverse).astype(jnp.bfloat16)
         own_weight = (own_expo * inverse).astype(jnp.bfloat16).astype(jnp.float32)
         summed = jnp.dot(weights, flip_ref[r], preferred_element_type=jnp.float32)
-        summed += own_weight * newest[:, :LAT]
-        for k in range(2 * chips):
-            out_refs[k // 2][k % 2, r * heads : (r + 1) * heads, :] = summed[
+        summed += own_weight * new_ref[r : r + 1, :LAT].astype(jnp.float32)
+        for k, (out_ref, i) in enumerate(back):
+            out_ref[i, r * heads : (r + 1) * heads, :] = summed[
                 k * heads : (k + 1) * heads, :
             ].astype(jnp.bfloat16)
 
 
-def attend(lengths, tables, keys, flipped, new_latent, messages, heads):
-    chips = len(messages)
-    kernel = functools.partial(attend_kernel, chips)
-    block = shape(2, keys.shape[0] * heads, LAT)
-    return call(kernel, [block] * chips, 2 + chips, "attend", scalars=1)(
+def attend(lengths, tables, keys, flipped, new_latent, messages, heads, devices):
+    sizes = message_sizes(devices)
+    out = [shape(2 * size, keys.shape[0] * heads, LAT) for size in sizes]
+    return call(functools.partial(attend_kernel, sizes), out, 10, "attend", scalars=1)(
         lengths, *tables, resident(keys), resident(flipped), new_latent, *messages
     )
 
 
+def early_kernel(passing_ref, own_ref, after_ref, out_ref):
+    out_ref[0] = passing_ref[1]
+    out_ref[1] = own_ref[1]
+
+
+def early(passing, own, after):
+    return call(early_kernel, shape(2, *own.shape[1:]), 4, "early")(passing, own, after)
+
+
 def regroup_kernel(*refs):
-    *in_refs, out_ref = refs
-    for j, ref in enumerate(in_refs):
-        out_ref[j] = ref[1]
-
-
-def regroup(messages):
+    *in_refs, early_ref, out_ref = refs
+    blocks = arrived(in_refs)[1::2]
+    blocks = [*blocks[:-4], (early_ref, 0), *blocks[-3:-1], (early_ref, 1)]
+    for j, (ref, i) in enumerate(blocks):
+        out_ref[j] = ref[i]
+
+
+def regroup(messages, ready, chips):
     _, wide, width = messages[0].shape
-    return call(regroup_kernel, shape(len(messages), wide, width), 1, "regroup")(*messages)
-
-
-def values_kernel(chips, *refs):
-    mine_refs = refs[:chips]
-    other_ref, wv_ref, val_ref, rows_ref = refs[chips:]
+    return call(regroup_kernel, shape(chips, wide, width), 1, "regroup")(*messages, ready)
+
+
+def values_kernel(*refs):
+    *in_refs, other_ref, wv_ref, val_ref, rows_ref = refs
+    mine = arrived(in_refs)[::2]
+    chips = len(mine)
     heads = wv_ref.shape[0]
     wide = other_ref.shape[1]
     for place in range(2 * chips):
-        block = mine_refs[place][0] if place < chips else other_ref[place - chips]
-        block = block.astype(jnp.float32)
+        ref, i = mine[place] if place < chips else (other_ref, place - chips)
+        block = ref[i].astype(jnp.float32)
         for c in range(PIECES):
             rows_ref[c, place * wide : (place + 1) * wide, :] = block[:, c * LANES : (c + 1) * LANES]
     count = val_ref.shape[0]
@@ -267,8 +305,7 @@
     heads = w_uv.shape[0]
     count = 2 * chips * wide // heads
     scratch = [pltpu.VMEM((PIECES, count * heads, LANES), jnp.float32)]
-    kernel = functools.partial(values_kernel, chips)
-    return call(kernel, shape(count, heads * VD), 3, "values", scratch)(
+    return call(values_kernel, shape(count, heads * VD), 3, "values", scratch)(
         *messages, other, resident(w_uv)
     )
 
@@ -295,7 +332,7 @@
 
 
 def places(devices, chips):
-    order = chip_order(devices)
+    order = [*far_chips(devices), Y, Z1, Y + Z1, 0]
     return [order.index(k) for k in chips]
 
 
@@ -385,7 +422,6 @@
 def on_device(q_latent, new_latent, cache, lengths, w_uq, w_uk, w_uv, w_o, devices):
     heads = w_uk.shape[0]
     rows = cache.shape[0]
-    order = chip_order(devices)
     zs = far_first(devices, 4)[::-1]
 
     def swap(block, k):
@@ -396,13 +432,24 @@
 
     far_weights = [swap(w_uq, 1), swap(w_uk, 1)]
     tables, near = join(rotary(lengths), [q_latent, swap(q_latent, 2)])
+    def exchange(messages):
+        *far, across, pair, own = messages
+        early = len(far) // 2
+        got = [swap(block, k) for block, k in zip(far[:early], far_k)]
+        passing = swap(across, Y)
+        got += [swap(block, k) for block, k in zip(far[early:], far_k[early:])]
+        sent = forward(pair, passing)
+        return [*got, passing, swap(sent, Z1), own], sent
+
+    far_k = far_chips(devices)
     messages = project([swap(near, z) for z in zs], [w_uq, w_uk, *far_weights], devices)
+    messages, sent = exchange(messages)
     keys = jnp.swapaxes(cache, 1, 2)
-    flipped = flip(keys, messages[-1])
-    messages = [swap(block, k) for k, block in zip(order, messages)]
-    latents = attend(lengths, tables, keys, flipped, new_latent, messages, heads)
-    latents = [swap(block, k) for k, block in zip(order, latents)]
-    values = head_values(latents, swap(regroup(latents), 1), w_uv)
+    flipped = flip(keys, sent)
+    latents = attend(lengths, tables, keys, flipped, new_latent, messages, heads, devices)
+    latents, sent = exchange(latents)
+    ready = early(latents[-3], latents[-1], sent)
+    values = head_values(latents, swap(regroup(latents, ready, devices // 2), 1), w_uv)
     keep, got, near = [], [], None
     for part in range(PARTS):
         mine, other = output_terms(values, w_o, part)

time: 73 us -> 71.8 us (0.984)
  starting transfers between devices: 33.8 us -> 30.7 us
  waiting for transfers between devices: 25.1 us -> 27.7 us
  Pallas kernels: 13 us -> 12.2 us
    ppermute x29 -> x27, starting transfers between devices: 33.8 us -> 30.7 us  [swap(): lax.ppermute(block, 'row', [(i, i ^ flip_bits) for i in range(devices)])]
    ppermute x29 -> x27, waiting for transfers between devices: 25.1 us -> 27.7 us  [swap(): lax.ppermute(block, 'row', [(i, i ^ flip_bits) for i in range(devices)])]
    pallas_call x14 -> x17, Pallas kernels: 13 us -> 12.2 us  [run(): pl.pallas_call(kernel, out_shape=out_shape, in_specs=smem + [in_vmem()] *...]
  transfers between devices with their start and end apart: 29 -> 27, of which waited for: 14 -> 13; matrix products, arithmetic and copies ran while one was open for 0% -> 0% of each run, Pallas kernels for 5% -> 5%
where the time goes in v10:
time: 71.8 us; the launch traced here: 71.6 us
  starting transfers between devices  30.7 us (43%)
  waiting for transfers between devices  27.7 us (39%)
  Pallas kernels  12.2 us (17%)
  local copies, waits for them, and re-layouts  0.72 us (1%)
    ppermute x27, starting transfers between devices, swap(): lax.ppermute(block, 'row', [(i, i ^ flip_bits) for i in range(devices)])  30.7 us
    ppermute x27, waiting for transfers between devices, swap(): lax.ppermute(block, 'row', [(i, i ^ flip_bits) for i in range(devices)])  27.7 us
    pallas_call x17, Pallas kernels, run(): pl.pallas_call(kernel, out_shape=out_shape, in_specs=smem + [in_vmem()] *...  12.2 us
  transfers between devices with their start and end apart: 27, of which 13 were waited for; matrix products, arithmetic and copies ran while one was open for 0% of the time, Pallas kernels for 5%

profile of v10, /device:TPU:0, one launch (start us, length us, event | category | flops | bytes accessed | tf_op | source)
XLA Modules:
  0.0 71.6 jit_solution(996039467329666374)
XLA Ops:
  0.5 2.6 %collective-permute-start = (bf16[4,1536]{1,0:T(4,128)(2,1)}, bf16[4,1536]{1,0:T(4,128)(2,1)S(1)}, u32[]{:S(2)}, u32[]{:S(2)}) collective-permute-start(bf16[4,1536]{1,0:T(4,128)(2,1)} %refs_0_.1), channel_id=1, source_target_pairs={{0,3},{1,2},{2,1},{3,0},{4,7},{5,6},{6,5},{7,4},{8,11},{9,10},{10,... | collective-permute-start | bytes 36872 | tf_op jit(solution)/shard_map/ppermute | solution.py:431
  3.2 0.7 copy-done.4
  4.8 2.9 %collective-permute-start.3 = (bf16[8,1536]{1,0:T(8,128)(2,1)S(1)}, bf16[8,1536]{1,0:T(8,128)(2,1)S(1)}, u32[]{:S(2)}, u32[]{:S(2)}) collective-permute-start(bf16[8,1536]{1,0:T(8,128)(2,1)S(1)} %get-tuple-element.43.refs_0_), channel_id=1, source_target_pairs={{0,9},{1,8},{2,11},{3,10},{4,13},{5,12},{6,15},{7,14},{8,1},{9,0},... | collective-permute-start | bytes 73736 | tf_op jit(solution)/shard_map/ppermute | solution.py:431
  7.7 1.4 %collective-permute-start.2 = (bf16[8,1536]{1,0:T(8,128)(2,1)S(1)}, bf16[8,1536]{1,0:T(8,128)(2,1)S(1)}, u32[]{:S(2)}, u32[]{:S(2)}) collective-permute-start(bf16[8,1536]{1,0:T(8,128)(2,1)S(1)} %get-tuple-element.43.refs_0_), channel_id=1, source_target_pairs={{0,12},{1,13},{2,14},{3,15},{4,8},{5,9},{6,10},{7,11},{8,4},{9,5},... | collective-permute-start | bytes 73736 | tf_op jit(solution)/shard_map/ppermute | solution.py:431
  9.3 4.2 %collective-permute-done.2.refs_2_ = bf16[8,1536]{1,0:T(8,128)(2,1)S(1)} collective-permute-done((bf16[8,1536]{1,0:T(8,128)(2,1)S(1)}, bf16[8,1536]{1,0:T(8,128)(2,1)S(1)}, u32[]{:S(2)}, u32[]{:S(2)}) %collective-permute-start.2) | collective-permute-done | bytes 24608 | tf_op jit(solution)/shard_map/ppermute | solution.py:431
  13.5 2.3 %project.1 = (bf16[2,144,128]{2,1,0:T(8,128)(2,1)S(1)}, bf16[2,144,128]{2,1,0:T(8,128)(2,1)S(1)}, bf16[2,144,128]{2,1,0:T(8,128)(2,1)S(1)}, bf16[2,144,128]{2,1,...) custom-call(bf16[8,1536]{1,0:T(8,128)(2,1)S(1)} %get-tuple-element.4, ...), custom_call_target="tpu_custom_call" | custom-call | flops 23000000512 | tf_op jit(solution)/shard_map/project/pallas_call | solution.py:36
  16.3 1.7 %collective-permute-start.7 = (bf16[2,144,128]{2,1,0:T(8,128)(2,1)S(1)}, bf16[2,144,128]{2,1,0:T(8,128)(2,1)S(1)}, u32[]{:S(2)}, u32[]{:S(2)}) collective-permute-start(bf16[2,144,128]{2,1,0:T(8,128)(2,1)S(1)} %get-tuple-element.46), channel_id=1, source_target_pairs={{0,9},{1,8},{2,11},{3,10},{4,13},{5,12},{6,15},{7,14},{8,1},{9,0},... | collective-permute-start | bytes 221192 | tf_op jit(solution)/shard_map/ppermute | solution.py:431
  17.9 2.1 %collective-permute-start.8 = (bf16[2,144,128]{2,1,0:T(8,128)(2,1)S(1)}, bf16[2,144,128]{2,1,0:T(8,128)(2,1)S(1)}, u32[]{:S(2)}, u32[]{:S(2)}) collective-permute-start(bf16[2,144,128]{2,1,0:T(8,128)(2,1)S(1)} %get-tuple-element.47), channel_id=1, source_target_pairs={{0,10},{1,11},{2,8},{3,9},{4,14},{5,15},{6,12},{7,13},{8,2},{9,3},... | collective-permute-start | bytes 221192 | tf_op jit(solution)/shard_map/ppermute | solution.py:431
  20.0 1.6 %collective-permute-start.9 = (bf16[2,144,128]{2,1,0:T(8,128)(2,1)S(1)}, bf16[2,144,128]{2,1,0:T(8,128)(2,1)S(1)}, u32[]{:S(2)}, u32[]{:S(2)}) collective-permute-start(bf16[2,144,128]{2,1,0:T(8,128)(2,1)S(1)} %get-tuple-element.48), channel_id=1, source_target_pairs={{0,12},{1,13},{2,14},{3,15},{4,8},{5,9},{6,10},{7,11},{8,4},{9,5},... | collective-permute-start | bytes 221192 | tf_op jit(solution)/shard_map/ppermute | solution.py:431
  21.6 1.4 %collective-permute-start.10 = (bf16[2,144,128]{2,1,0:T(8,128)(2,1)S(1)}, bf16[2,144,128]{2,1,0:T(8,128)(2,1)S(1)}, u32[]{:S(2)}, u32[]{:S(2)}) collective-permute-start(bf16[2,144,128]{2,1,0:T(8,128)(2,1)S(1)} %get-tuple-element.49), channel_id=1, source_target_pairs={{0,15},{1,14},{2,13},{3,12},{4,11},{5,10},{6,9},{7,8},{8,7},{9,6},... | collective-permute-start | bytes 221192 | tf_op jit(solution)/shard_map/ppermute | solution.py:431
  23.2 1.7 %flip.1.flip_ref = bf16[4,1536,512]{2,1,0:T(8,128)(2,1)S(1)} custom-call(bf16[4,576,1536]{2,1,0:T(8,128)(2,1)S(1)} %bitcast.5, bf16[4,144,128]{2,1,0:T(8,128)(2,1)S(1)} %forward.2.after_ref), custom_call_target="tpu_custom_call" | custom-call | flops 4600000000 | tf_op jit(solution)/shard_map/flip/pallas_call | solution.py:36
  24.9 1.4 %collective-permute-done.7.refs_0_ = bf16[2,144,128]{2,1,0:T(8,128)(2,1)S(1)} collective-permute-done((bf16[2,144,128]{2,1,0:T(8,128)(2,1)S(1)}, bf16[2,144,128]{2,1,0:T(8,128)(2,1)S(1)}, u32[]{:S(2)}, u32[]{:S(2)}) %collective-permute-start.7) | collective-permute-done | bytes 73760 | tf_op jit(solution)/shard_map/ppermute | solution.py:431
  26.3 3.4 %collective-permute-done.8.refs_1_ = bf16[2,144,128]{2,1,0:T(8,128)(2,1)S(1)} collective-permute-done((bf16[2,144,128]{2,1,0:T(8,128)(2,1)S(1)}, bf16[2,144,128]{2,1,0:T(8,128)(2,1)S(1)}, u32[]{:S(2)}, u32[]{:S(2)}) %collective-permute-start.8) | collective-permute-done | bytes 73760 | tf_op jit(solution)/shard_map/ppermute | solution.py:431
  29.7 2.9 %collective-permute-done.11.refs_5_ = bf16[4,144,128]{2,1,0:T(8,128)(2,1)S(1)} collective-permute-done((bf16[4,144,128]{2,1,0:T(8,128)(2,1)S(1)}, bf16[4,144,128]{2,1,0:T(8,128)(2,1)S(1)}, u32[]{:S(2)}, u32[]{:S(2)}) %collective-permute-start.11) | collective-permute-done | bytes 147488 | tf_op jit(solution)/shard_map/ppermute | solution.py:431
  32.6 3.4 %attend.1 = (bf16[2,32,512]{2,1,0:T(8,128)(2,1)S(1)}, bf16[2,32,512]{2,1,0:T(8,128)(2,1)S(1)}, bf16[2,32,512]{2,1,0:T(8,128)(2,1)S(1)}, bf16[2,32,512]{2,1,0:T(8...) custom-call(s32[4]{0:T(128)S(1)} %copy-done.5, ...), custom_call_target="tpu_custom_call" | custom-call | flops 11500000256 | tf_op jit(solution)/shard_map/attend/pallas_call | solution.py:36
  36.4 2.7 %collective-permute-start.12 = (bf16[2,32,512]{2,1,0:T(8,128)(2,1)S(1)}, bf16[2,32,512]{2,1,0:T(8,128)(2,1)S(1)}, u32[]{:S(2)}, u32[]{:S(2)}) collective-permute-start(bf16[2,32,512]{2,1,0:T(8,128)(2,1)S(1)} %get-tuple-element.51), channel_id=1, source_target_pairs={{0,9},{1,8},{2,11},{3,10},{4,13},{5,12},{6,15},{7,14},{8,1},{9,0},... | collective-permute-start | bytes 196616 | tf_op jit(solution)/shard_map/ppermute | solution.py:431
  39.1 1.2 %collective-permute-start.13 = (bf16[2,32,512]{2,1,0:T(8,128)(2,1)S(1)}, bf16[2,32,512]{2,1,0:T(8,128)(2,1)S(1)}, u32[]{:S(2)}, u32[]{:S(2)}) collective-permute-start(bf16[2,32,512]{2,1,0:T(8,128)(2,1)S(1)} %get-tuple-element.52), channel_id=1, source_target_pairs={{0,10},{1,11},{2,8},{3,9},{4,14},{5,15},{6,12},{7,13},{8,2},{9,3},... | collective-permute-start | bytes 196616 | tf_op jit(solution)/shard_map/ppermute | solution.py:431
  40.2 2.6 %collective-permute-start.14 = (bf16[2,32,512]{2,1,0:T(8,128)(2,1)S(1)}, bf16[2,32,512]{2,1,0:T(8,128)(2,1)S(1)}, u32[]{:S(2)}, u32[]{:S(2)}) collective-permute-start(bf16[2,32,512]{2,1,0:T(8,128)(2,1)S(1)} %get-tuple-element.53), channel_id=1, source_target_pairs={{0,12},{1,13},{2,14},{3,15},{4,8},{5,9},{6,10},{7,11},{8,4},{9,5},... | collective-permute-start | bytes 196616 | tf_op jit(solution)/shard_map/ppermute | solution.py:431
  43.7 4.7 %collective-permute-done.13.refs_1_ = bf16[2,32,512]{2,1,0:T(8,128)(2,1)S(1)} collective-permute-done((bf16[2,32,512]{2,1,0:T(8,128)(2,1)S(1)}, bf16[2,32,512]{2,1,0:T(8,128)(2,1)S(1)}, u32[]{:S(2)}, u32[]{:S(2)}) %collective-permute-start.13) | collective-permute-done | bytes 65568 | tf_op jit(solution)/shard_map/ppermute | solution.py:431
  48.3 1.6 %collective-permute-done.15.refs_3_ = bf16[2,32,512]{2,1,0:T(8,128)(2,1)S(1)} collective-permute-done((bf16[2,32,512]{2,1,0:T(8,128)(2,1)S(1)}, bf16[2,32,512]{2,1,0:T(8,128)(2,1)S(1)}, u32[]{:S(2)}, u32[]{:S(2)}) %collective-permute-start.15) | collective-permute-done | bytes 65568 | tf_op jit(solution)/shard_map/ppermute | solution.py:431
  50.0 1.3 %collective-permute-done.17.refs_5_ = bf16[4,32,512]{2,1,0:T(8,128)(2,1)S(1)} collective-permute-done((bf16[4,32,512]{2,1,0:T(8,128)(2,1)S(1)}, bf16[4,32,512]{2,1,0:T(8,128)(2,1)S(1)}, u32[]{:S(2)}, u32[]{:S(2)}) %collective-permute-start.17) | collective-permute-done | bytes 131104 | tf_op jit(solution)/shard_map/ppermute | solution.py:431
  51.5 1.4 %collective-permute-done.18.refs_7_ = bf16[8,32,512]{2,1,0:T(8,128)(2,1)S(1)} collective-permute-done((bf16[8,32,512]{2,1,0:T(8,128)(2,1)S(1)}, bf16[8,32,512]{2,1,0:T(8,128)(2,1)S(1)}, u32[]{:S(2)}, u32[]{:S(2)}) %collective-permute-start.18) | collective-permute-done | bytes 262176 | tf_op jit(solution)/shard_map/ppermute | solution.py:431
  53.4 1.4 %terms.3 = (f32[32,3584]{1,0:T(8,128)S(1)}, bf16[32,3584]{1,0:T(8,128)(2,1)S(1)}) custom-call(bf16[64,1024]{1,0:T(8,128)(2,1)S(1)} %values.1.val_ref, bf16[1024,7168]{1,0:T(8,128)(2,1)S(1)} %bitcast.2), custom_call_target="tpu_custom_call" | custom-call | flops 6899999744 | tf_op jit(solution)/shard_map/terms/pallas_call | solution.py:36
  55.0 1.4 %terms.2 = (f32[32,3584]{1,0:T(8,128)S(1)}, bf16[32,3584]{1,0:T(8,128)(2,1)S(1)}) custom-call(bf16[64,1024]{1,0:T(8,128)(2,1)S(1)} %values.1.val_ref, bf16[1024,7168]{1,0:T(8,128)(2,1)S(1)} %bitcast.2), custom_call_target="tpu_custom_call" | custom-call | flops 6899999744 | tf_op jit(solution)/shard_map/terms/pallas_call | solution.py:36
  56.9 1.5 %collective-permute-start.23 = (bf16[8,3584]{1,0:T(8,128)(2,1)S(1)}, bf16[8,3584]{1,0:T(8,128)(2,1)S(1)}, u32[]{:S(2)}, u32[]{:S(2)}) collective-permute-start(bf16[8,3584]{1,0:T(8,128)(2,1)S(1)} %get-tuple-element.69), channel_id=1, source_target_pairs={{0,3},{1,2},{2,1},{3,0},{4,7},{5,6},{6,5},{7,4},{8,11},{9,10},{10,... | collective-permute-start | bytes 172040 | tf_op jit(solution)/shard_map/ppermute | solution.py:431
  58.4 1.3 %collective-permute-start.24 = (bf16[8,3584]{1,0:T(8,128)(2,1)S(1)}, bf16[8,3584]{1,0:T(8,128)(2,1)S(1)}, u32[]{:S(2)}, u32[]{:S(2)}) collective-permute-start(bf16[8,3584]{1,0:T(8,128)(2,1)S(1)} %get-tuple-element.70), channel_id=1, source_target_pairs={{0,3},{1,2},{2,1},{3,0},{4,7},{5,6},{6,5},{7,4},{8,11},{9,10},{10,... | collective-permute-start | bytes 172040 | tf_op jit(solution)/shard_map/ppermute | solution.py:431
  59.7 0.6 collective-permute-start.21
  60.8 1.4 %collective-permute-done.24.refs_3_ = bf16[8,3584]{1,0:T(8,128)(2,1)S(1)} collective-permute-done((bf16[8,3584]{1,0:T(8,128)(2,1)S(1)}, bf16[8,3584]{1,0:T(8,128)(2,1)S(1)}, u32[]{:S(2)}, u32[]{:S(2)}) %collective-permute-start.24) | collective-permute-done | bytes 57376 | tf_op jit(solution)/shard_map/ppermute | solution.py:431
  62.3 2.6 %collective-permute-start.25 = (bf16[4,7168]{1,0:T(4,128)(2,1)S(1)}, bf16[4,7168]{1,0:T(4,128)(2,1)S(1)}, u32[]{:S(2)}, u32[]{:S(2)}) collective-permute-start(bf16[4,7168]{1,0:T(4,128)(2,1)S(1)} %get-tuple-element.71), channel_id=1, source_target_pairs={{0,9},{1,8},{2,11},{3,10},{4,13},{5,12},{6,15},{7,14},{8,1},{9,0},... | collective-permute-start | bytes 172040 | tf_op jit(solution)/shard_map/ppermute | solution.py:431
  64.9 1.4 %collective-permute-start.26 = (bf16[4,7168]{1,0:T(4,128)(2,1)S(1)}, bf16[4,7168]{1,0:T(4,128)(2,1)S(1)}, u32[]{:S(2)}, u32[]{:S(2)}) collective-permute-start(bf16[4,7168]{1,0:T(4,128)(2,1)S(1)} %get-tuple-element.72), channel_id=1, source_target_pairs={{0,12},{1,13},{2,14},{3,15},{4,8},{5,9},{6,10},{7,11},{8,4},{9,5},... | collective-permute-start | bytes 172040 | tf_op jit(solution)/shard_map/ppermute | solution.py:431
  66.9 4.1 %collective-permute-done.26.refs_3_ = bf16[4,7168]{1,0:T(4,128)(2,1)S(1)} collective-permute-done((bf16[4,7168]{1,0:T(4,128)(2,1)S(1)}, bf16[4,7168]{1,0:T(4,128)(2,1)S(1)}, u32[]{:S(2)}, u32[]{:S(2)}) %collective-permute-start.26) | collective-permute-done | bytes 57376 | tf_op jit(solution)/shard_map/ppermute | solution.py:431
  71.0 0.7 last_sum.1
  (70 shorter events, 6.0 us)
Async XLA Ops:
  0.0 13.5 %collective-permute-start.4 = (bf16[1536,1536]{1,0:T(8,128)(2,1)}, bf16[1536,1536]{1,0:T(8,128)(2,1)S(1)}, u32[]{:S(2)}, u32[]{:S(2)}) collective-permute-start(bf16[1536,1536]{1,0:T(8,128)(2,1)} %refs_4_.1), channel_id=1, source_target_pairs={{0,1},{1,0},{2,3},{3,2},{4,5},{5,4},{6,7},{7,6},{8,9},{9,8},{10,11... | collective-permute-start | bytes 14155784 | tf_op jit(solution)/shard_map/ppermute | solution.py:431
  0.5 13.0 %collective-permute-start.5 = (bf16[8,128,512]{2,1,0:T(8,128)(2,1)}, bf16[8,128,512]{2,1,0:T(8,128)(2,1)S(1)}, u32[]{:S(2)}, u32[]{:S(2)}) collective-permute-start(bf16[8,128,512]{2,1,0:T(8,128)(2,1)} %refs_5_.1), channel_id=1, source_target_pairs={{0,1},{1,0},{2,3},{3,2},{4,5},{5,4},{6,7},{7,6},{8,9},{9,8},{10,11... | collective-permute-start | bytes 3145736 | tf_op jit(solution)/shard_map/ppermute | solution.py:431
  0.5 4.2 %collective-permute-start = (bf16[4,1536]{1,0:T(4,128)(2,1)}, bf16[4,1536]{1,0:T(4,128)(2,1)S(1)}, u32[]{:S(2)}, u32[]{:S(2)}) collective-permute-start(bf16[4,1536]{1,0:T(4,128)(2,1)} %refs_0_.1), channel_id=1, source_target_pairs={{0,3},{1,2},{2,1},{3,0},{4,7},{5,6},{6,5},{7,4},{8,11},{9,10},{10,... | collective-permute-start | bytes 36872 | tf_op jit(solution)/shard_map/ppermute | solution.py:431
  4.8 18.4 %slice-start.4 = ((s8[7077888]{0:T(1024)(128)(4,1)}), s8[4194304]{0:T(1024)(128)(4,1)S(1)}, s32[]{:S(2)}) async-start(s8[7077888]{0:T(1024)(128)(4,1)} %bitcast.3), calls=%async_computation.4 | async-start | bytes 8388608
  4.8 18.4 %slice-start.5 = ((s8[7077888]{0:T(1024)(128)(4,1)}), s8[2883584]{0:T(1024)(128)(4,1)S(1)}, s32[]{:S(2)}) async-start(s8[7077888]{0:T(1024)(128)(4,1)} %bitcast.3), calls=%async_computation.5 | async-start | bytes 5767168
  4.8 4.5 %collective-permute-start.3 = (bf16[8,1536]{1,0:T(8,128)(2,1)S(1)}, bf16[8,1536]{1,0:T(8,128)(2,1)S(1)}, u32[]{:S(2)}, u32[]{:S(2)}) collective-permute-start(bf16[8,1536]{1,0:T(8,128)(2,1)S(1)} %get-tuple-element.43.refs_0_), channel_id=1, source_target_pairs={{0,9},{1,8},{2,11},{3,10},{4,13},{5,12},{6,15},{7,14},{8,1},{9,0},... | collective-permute-start | bytes 73736 | tf_op jit(solution)/shard_map/ppermute | solution.py:431
  7.7 5.8 %collective-permute-start.2 = (bf16[8,1536]{1,0:T(8,128)(2,1)S(1)}, bf16[8,1536]{1,0:T(8,128)(2,1)S(1)}, u32[]{:S(2)}, u32[]{:S(2)}) collective-permute-start(bf16[8,1536]{1,0:T(8,128)(2,1)S(1)} %get-tuple-element.43.refs_0_), channel_id=1, source_target_pairs={{0,12},{1,13},{2,14},{3,15},{4,8},{5,9},{6,10},{7,11},{8,4},{9,5},... | collective-permute-start | bytes 73736 | tf_op jit(solution)/shard_map/ppermute | solution.py:431
  9.1 4.4 %collective-permute-start.1 = (bf16[8,1536]{1,0:T(8,128)(2,1)S(1)}, bf16[8,1536]{1,0:T(8,128)(2,1)S(1)}, u32[]{:S(2)}, u32[]{:S(2)}) collective-permute-start(bf16[8,1536]{1,0:T(8,128)(2,1)S(1)} %get-tuple-element.43.refs_0_), channel_id=1, source_target_pairs={{0,5},{1,4},{2,7},{3,6},{4,1},{5,0},{6,3},{7,2},{8,13},{9,12},{10,... | collective-permute-start | bytes 73736 | tf_op jit(solution)/shard_map/ppermute | solution.py:431
  15.8 7.2 %collective-permute-start.6 = (bf16[4,144,128]{2,1,0:T(8,128)(2,1)S(1)}, bf16[4,144,128]{2,1,0:T(8,128)(2,1)S(1)}, u32[]{:S(2)}, u32[]{:S(2)}) collective-permute-start(bf16[4,144,128]{2,1,0:T(8,128)(2,1)S(1)} %get-tuple-element.45), channel_id=1, source_target_pairs={{0,3},{1,2},{2,1},{3,0},{4,7},{5,6},{6,5},{7,4},{8,11},{9,10},{10,... | collective-permute-start | bytes 442376 | tf_op jit(solution)/shard_map/ppermute | solution.py:431
  16.3 10.1 %collective-permute-start.7 = (bf16[2,144,128]{2,1,0:T(8,128)(2,1)S(1)}, bf16[2,144,128]{2,1,0:T(8,128)(2,1)S(1)}, u32[]{:S(2)}, u32[]{:S(2)}) collective-permute-start(bf16[2,144,128]{2,1,0:T(8,128)(2,1)S(1)} %get-tuple-element.46), channel_id=1, source_target_pairs={{0,9},{1,8},{2,11},{3,10},{4,13},{5,12},{6,15},{7,14},{8,1},{9,0},... | collective-permute-start | bytes 221192 | tf_op jit(solution)/shard_map/ppermute | solution.py:431
  17.9 11.8 %collective-permute-start.8 = (bf16[2,144,128]{2,1,0:T(8,128)(2,1)S(1)}, bf16[2,144,128]{2,1,0:T(8,128)(2,1)S(1)}, u32[]{:S(2)}, u32[]{:S(2)}) collective-permute-start(bf16[2,144,128]{2,1,0:T(8,128)(2,1)S(1)} %get-tuple-element.47), channel_id=1, source_target_pairs={{0,10},{1,11},{2,8},{3,9},{4,14},{5,15},{6,12},{7,13},{8,2},{9,3},... | collective-permute-start | bytes 221192 | tf_op jit(solution)/shard_map/ppermute | solution.py:431
  20.0 9.7 %collective-permute-start.9 = (bf16[2,144,128]{2,1,0:T(8,128)(2,1)S(1)}, bf16[2,144,128]{2,1,0:T(8,128)(2,1)S(1)}, u32[]{:S(2)}, u32[]{:S(2)}) collective-permute-start(bf16[2,144,128]{2,1,0:T(8,128)(2,1)S(1)} %get-tuple-element.48), channel_id=1, source_target_pairs={{0,12},{1,13},{2,14},{3,15},{4,8},{5,9},{6,10},{7,11},{8,4},{9,5},... | collective-permute-start | bytes 221192 | tf_op jit(solution)/shard_map/ppermute | solution.py:431
  21.6 8.1 %collective-permute-start.10 = (bf16[2,144,128]{2,1,0:T(8,128)(2,1)S(1)}, bf16[2,144,128]{2,1,0:T(8,128)(2,1)S(1)}, u32[]{:S(2)}, u32[]{:S(2)}) collective-permute-start(bf16[2,144,128]{2,1,0:T(8,128)(2,1)S(1)} %get-tuple-element.49), channel_id=1, source_target_pairs={{0,15},{1,14},{2,13},{3,12},{4,11},{5,10},{6,9},{7,8},{8,7},{9,6},... | collective-permute-start | bytes 221192 | tf_op jit(solution)/shard_map/ppermute | solution.py:431
  23.1 9.5 %collective-permute-start.11 = (bf16[4,144,128]{2,1,0:T(8,128)(2,1)S(1)}, bf16[4,144,128]{2,1,0:T(8,128)(2,1)S(1)}, u32[]{:S(2)}, u32[]{:S(2)}) collective-permute-start(bf16[4,144,128]{2,1,0:T(8,128)(2,1)S(1)} %forward.2.after_ref), channel_id=1, source_target_pairs={{0,5},{1,4},{2,7},{3,6},{4,1},{5,0},{6,3},{7,2},{8,13},{9,12},{10,... | collective-permute-start | bytes 442376 | tf_op jit(solution)/shard_map/ppermute | solution.py:431
  36.1 7.1 %collective-permute-start.16 = (bf16[4,32,512]{2,1,0:T(8,128)(2,1)S(1)}, bf16[4,32,512]{2,1,0:T(8,128)(2,1)S(1)}, u32[]{:S(2)}, u32[]{:S(2)}) collective-permute-start(bf16[4,32,512]{2,1,0:T(8,128)(2,1)S(1)} %get-tuple-element.55), channel_id=1, source_target_pairs={{0,3},{1,2},{2,1},{3,0},{4,7},{5,6},{6,5},{7,4},{8,11},{9,10},{10,... | collective-permute-start | bytes 393224 | tf_op jit(solution)/shard_map/ppermute | solution.py:431
  36.4 7.3 %collective-permute-start.12 = (bf16[2,32,512]{2,1,0:T(8,128)(2,1)S(1)}, bf16[2,32,512]{2,1,0:T(8,128)(2,1)S(1)}, u32[]{:S(2)}, u32[]{:S(2)}) collective-permute-start(bf16[2,32,512]{2,1,0:T(8,128)(2,1)S(1)} %get-tuple-element.51), channel_id=1, source_target_pairs={{0,9},{1,8},{2,11},{3,10},{4,13},{5,12},{6,15},{7,14},{8,1},{9,0},... | collective-permute-start | bytes 196616 | tf_op jit(solution)/shard_map/ppermute | solution.py:431
  39.1 9.3 %collective-permute-start.13 = (bf16[2,32,512]{2,1,0:T(8,128)(2,1)S(1)}, bf16[2,32,512]{2,1,0:T(8,128)(2,1)S(1)}, u32[]{:S(2)}, u32[]{:S(2)}) collective-permute-start(bf16[2,32,512]{2,1,0:T(8,128)(2,1)S(1)} %get-tuple-element.52), channel_id=1, source_target_pairs={{0,10},{1,11},{2,8},{3,9},{4,14},{5,15},{6,12},{7,13},{8,2},{9,3},... | collective-permute-start | bytes 196616 | tf_op jit(solution)/shard_map/ppermute | solution.py:431
  40.2 8.1 %collective-permute-start.14 = (bf16[2,32,512]{2,1,0:T(8,128)(2,1)S(1)}, bf16[2,32,512]{2,1,0:T(8,128)(2,1)S(1)}, u32[]{:S(2)}, u32[]{:S(2)}) collective-permute-start(bf16[2,32,512]{2,1,0:T(8,128)(2,1)S(1)} %get-tuple-element.53), channel_id=1, source_target_pairs={{0,12},{1,13},{2,14},{3,15},{4,8},{5,9},{6,10},{7,11},{8,4},{9,5},... | collective-permute-start | bytes 196616 | tf_op jit(solution)/shard_map/ppermute | solution.py:431
  42.9 7.1 %collective-permute-start.15 = (bf16[2,32,512]{2,1,0:T(8,128)(2,1)S(1)}, bf16[2,32,512]{2,1,0:T(8,128)(2,1)S(1)}, u32[]{:S(2)}, u32[]{:S(2)}) collective-permute-start(bf16[2,32,512]{2,1,0:T(8,128)(2,1)S(1)} %get-tuple-element.54), channel_id=1, source_target_pairs={{0,15},{1,14},{2,13},{3,12},{4,11},{5,10},{6,9},{7,8},{8,7},{9,6},... | collective-permute-start | bytes 196616 | tf_op jit(solution)/shard_map/ppermute | solution.py:431
  43.2 8.0 %collective-permute-start.17 = (bf16[4,32,512]{2,1,0:T(8,128)(2,1)S(1)}, bf16[4,32,512]{2,1,0:T(8,128)(2,1)S(1)}, u32[]{:S(2)}, u32[]{:S(2)}) collective-permute-start(bf16[4,32,512]{2,1,0:T(8,128)(2,1)S(1)} %forward.3.after_ref), channel_id=1, source_target_pairs={{0,5},{1,4},{2,7},{3,6},{4,1},{5,0},{6,3},{7,2},{8,13},{9,12},{10,... | collective-permute-start | bytes 393224 | tf_op jit(solution)/shard_map/ppermute | solution.py:431
  43.6 9.7 %slice-start = ((s8[14680064]{0:T(1024)(128)(4,1)}), s8[4194304]{0:T(1024)(128)(4,1)S(1)}, s32[]{:S(2)}) async-start(s8[14680064]{0:T(1024)(128)(4,1)} %bitcast.1), calls=%async_computation | async-start | bytes 8388608
  43.6 9.7 %slice-start.1 = ((s8[14680064]{0:T(1024)(128)(4,1)}), s8[4194304]{0:T(1024)(128)(4,1)S(1)}, s32[]{:S(2)}) async-start(s8[14680064]{0:T(1024)(128)(4,1)} %bitcast.1), calls=%async_computation.1 | async-start | bytes 8388608
  43.6 9.7 %slice-start.2 = ((s8[14680064]{0:T(1024)(128)(4,1)}), s8[4194304]{0:T(1024)(128)(4,1)S(1)}, s32[]{:S(2)}) async-start(s8[14680064]{0:T(1024)(128)(4,1)} %bitcast.1), calls=%async_computation.2 | async-start | bytes 8388608
  51.3 1.6 %collective-permute-start.18 = (bf16[8,32,512]{2,1,0:T(8,128)(2,1)S(1)}, bf16[8,32,512]{2,1,0:T(8,128)(2,1)S(1)}, u32[]{:S(2)}, u32[]{:S(2)}) collective-permute-start(bf16[8,32,512]{2,1,0:T(8,128)(2,1)S(1)} %regroup.1), channel_id=1, source_target_pairs={{0,1},{1,0},{2,3},{3,2},{4,5},{5,4},{6,7},{7,6},{8,9},{9,8},{10,11... | collective-permute-start | bytes 786440 | tf_op jit(solution)/shard_map/ppermute | solution.py:431
  54.8 2.0 %collective-permute-start.20 = (bf16[32,3584]{1,0:T(8,128)(2,1)S(1)}, bf16[32,3584]{1,0:T(8,128)(2,1)S(1)}, u32[]{:S(2)}, u32[]{:S(2)}) collective-permute-start(bf16[32,3584]{1,0:T(8,128)(2,1)S(1)} %get-tuple-element.61), channel_id=1, source_target_pairs={{0,1},{1,0},{2,3},{3,2},{4,5},{5,4},{6,7},{7,6},{8,9},{9,8},{10,11... | collective-permute-start | bytes 688136 | tf_op jit(solution)/shard_map/ppermute | solution.py:431
  56.4 2.0 %collective-permute-start.19 = (bf16[32,3584]{1,0:T(8,128)(2,1)S(1)}, bf16[32,3584]{1,0:T(8,128)(2,1)S(1)}, u32[]{:S(2)}, u32[]{:S(2)}) collective-permute-start(bf16[32,3584]{1,0:T(8,128)(2,1)S(1)} %get-tuple-element.59), channel_id=1, source_target_pairs={{0,1},{1,0},{2,3},{3,2},{4,5},{5,4},{6,7},{7,6},{8,9},{9,8},{10,11... | collective-permute-start | bytes 688136 | tf_op jit(solution)/shard_map/ppermute | solution.py:431
  56.9 4.0 %collective-permute-start.23 = (bf16[8,3584]{1,0:T(8,128)(2,1)S(1)}, bf16[8,3584]{1,0:T(8,128)(2,1)S(1)}, u32[]{:S(2)}, u32[]{:S(2)}) collective-permute-start(bf16[8,3584]{1,0:T(8,128)(2,1)S(1)} %get-tuple-element.69), channel_id=1, source_target_pairs={{0,3},{1,2},{2,1},{3,0},{4,7},{5,6},{6,5},{7,4},{8,11},{9,10},{10,... | collective-permute-start | bytes 172040 | tf_op jit(solution)/shard_map/ppermute | solution.py:431
  58.4 3.8 %collective-permute-start.24 = (bf16[8,3584]{1,0:T(8,128)(2,1)S(1)}, bf16[8,3584]{1,0:T(8,128)(2,1)S(1)}, u32[]{:S(2)}, u32[]{:S(2)}) collective-permute-start(bf16[8,3584]{1,0:T(8,128)(2,1)S(1)} %get-tuple-element.70), channel_id=1, source_target_pairs={{0,3},{1,2},{2,1},{3,0},{4,7},{5,6},{6,5},{7,4},{8,11},{9,10},{10,... | collective-permute-start | bytes 172040 | tf_op jit(solution)/shard_map/ppermute | solution.py:431
  59.7 6.6 %collective-permute-start.21 = (bf16[8,7168]{1,0:T(8,128)(2,1)S(1)}, bf16[8,7168]{1,0:T(8,128)(2,1)S(1)}, u32[]{:S(2)}, u32[]{:S(2)}) collective-permute-start(bf16[8,7168]{1,0:T(8,128)(2,1)S(1)} %get-tuple-element.64), channel_id=1, source_target_pairs={{0,5},{1,4},{2,7},{3,6},{4,1},{5,0},{6,3},{7,2},{8,13},{9,12},{10,... | collective-permute-start | bytes 344072 | tf_op jit(solution)/shard_map/ppermute | solution.py:431
  62.3 4.6 %collective-permute-start.25 = (bf16[4,7168]{1,0:T(4,128)(2,1)S(1)}, bf16[4,7168]{1,0:T(4,128)(2,1)S(1)}, u32[]{:S(2)}, u32[]{:S(2)}) collective-permute-start(bf16[4,7168]{1,0:T(4,128)(2,1)S(1)} %get-tuple-element.71), channel_id=1, source_target_pairs={{0,9},{1,8},{2,11},{3,10},{4,13},{5,12},{6,15},{7,14},{8,1},{9,0},... | collective-permute-start | bytes 172040 | tf_op jit(solution)/shard_map/ppermute | solution.py:431
  64.9 6.0 %collective-permute-start.26 = (bf16[4,7168]{1,0:T(4,128)(2,1)S(1)}, bf16[4,7168]{1,0:T(4,128)(2,1)S(1)}, u32[]{:S(2)}, u32[]{:S(2)}) collective-permute-start(bf16[4,7168]{1,0:T(4,128)(2,1)S(1)} %get-tuple-element.72), channel_id=1, source_target_pairs={{0,12},{1,13},{2,14},{3,15},{4,8},{5,9},{6,10},{7,11},{8,4},{9,5},... | collective-permute-start | bytes 172040 | tf_op jit(solution)/shard_map/ppermute | solution.py:431
  66.3 4.6 %collective-permute-start.22 = (bf16[4,7168]{1,0:T(4,128)(2,1)S(1)}, bf16[4,7168]{1,0:T(4,128)(2,1)S(1)}, u32[]{:S(2)}, u32[]{:S(2)}) collective-permute-start(bf16[4,7168]{1,0:T(4,128)(2,1)S(1)} %get-tuple-element.66), channel_id=1, source_target_pairs={{0,3},{1,2},{2,1},{3,0},{4,7},{5,6},{6,5},{7,4},{8,11},{9,10},{10,... | collective-permute-start | bytes 172040 | tf_op jit(solution)/shard_map/ppermute | solution.py:431
  (9 other events, 62.9 us)

commit v11 on v10

--- a/solution.py
+++ b/solution.py
@@ -51,10 +51,6 @@
 
 def shape(*dims, dtype=jnp.bfloat16):
     return jax.ShapeDtypeStruct(dims, dtype)
-
-
-def mask(k):
-    return k ^ (k.bit_count() & 1)
 
 
 def far_first(devices, step):
@@ -427,11 +423,11 @@
     def swap(block, k):
         if k == 0:
             return block
-        flip_bits = k if k == 1 else mask(k)
-        return lax.ppermute(block, "row", [(i, i ^ flip_bits) for i in range(devices)])
-
+        return lax.ppermute(block, "row", [(i, i ^ k) for i in range(devices)])
+
+    across = swap(q_latent, Y)
     far_weights = [swap(w_uq, 1), swap(w_uk, 1)]
-    tables, near = join(rotary(lengths), [q_latent, swap(q_latent, 2)])
+    tables, near = join(rotary(lengths), [q_latent, across])
     def exchange(messages):
         *far, across, pair, own = messages
         early = len(far) // 2

time: 71.8 us -> 70 us (0.975)
  waiting for transfers between devices: 27.7 us -> 21.1 us
  starting transfers between devices: 30.7 us -> 35.5 us
    ppermute x27, waiting for transfers between devices: 27.7 us -> 21.1 us  [swap(): return lax.ppermute(block, 'row', [(i, i ^ k) for i in range(devices)])]
    ppermute x27, starting transfers between devices: 30.7 us -> 35.5 us  [swap(): return lax.ppermute(block, 'row', [(i, i ^ k) for i in range(devices)])]
  transfers between devices with their start and end apart: 27 -> 27, of which waited for: 13 -> 15; matrix products, arithmetic and copies ran while one was open for 0% -> 0% of each run, Pallas kernels for 5% -> 6%
where the time goes in v11:
time: 70 us; the launch traced here: 69.9 us
  starting transfers between devices  35.5 us (51%)
  waiting for transfers between devices  21.1 us (30%)
  Pallas kernels  12.2 us (17%)
  local copies, waits for them, and re-layouts  0.73 us (1%)
    ppermute x27, starting transfers between devices, swap(): return lax.ppermute(block, 'row', [(i, i ^ k) for i in range(devices)])  35.5 us
    ppermute x27, waiting for transfers between devices, swap(): return lax.ppermute(block, 'row', [(i, i ^ k) for i in range(devices)])  21.1 us
    pallas_call x17, Pallas kernels, run(): pl.pallas_call(kernel, out_shape=out_shape, in_specs=smem + [in_vmem()] *...  12.2 us
  transfers between devices with their start and end apart: 27, of which 15 were waited for; matrix products, arithmetic and copies ran while one was open for 0% of the time, Pallas kernels for 6%

profile of v11, /device:TPU:0, one launch (start us, length us, event | category | flops | bytes accessed | tf_op | source)
XLA Modules:
  0.0 69.9 jit_solution(3868243722084613353)
XLA Ops:
  0.5 3.0 %collective-permute-start = (bf16[4,1536]{1,0:T(4,128)(2,1)}, bf16[4,1536]{1,0:T(4,128)(2,1)S(1)}, u32[]{:S(2)}, u32[]{:S(2)}) collective-permute-start(bf16[4,1536]{1,0:T(4,128)(2,1)} %refs_0_.1), channel_id=1, source_target_pairs={{0,2},{1,3},{2,0},{3,1},{4,6},{5,7},{6,4},{7,5},{8,10},{9,11},{10,... | collective-permute-start | bytes 36872 | tf_op jit(solution)/shard_map/ppermute | solution.py:426
  5.4 3.2 %collective-permute-start.3 = (bf16[8,1536]{1,0:T(8,128)(2,1)S(1)}, bf16[8,1536]{1,0:T(8,128)(2,1)S(1)}, u32[]{:S(2)}, u32[]{:S(2)}) collective-permute-start(bf16[8,1536]{1,0:T(8,128)(2,1)S(1)} %get-tuple-element.43.refs_0_), channel_id=1, source_target_pairs={{0,8},{1,9},{2,10},{3,11},{4,12},{5,13},{6,14},{7,15},{8,0},{9,1},... | collective-permute-start | bytes 73736 | tf_op jit(solution)/shard_map/ppermute | solution.py:426
  8.6 1.3 %collective-permute-start.2 = (bf16[8,1536]{1,0:T(8,128)(2,1)S(1)}, bf16[8,1536]{1,0:T(8,128)(2,1)S(1)}, u32[]{:S(2)}, u32[]{:S(2)}) collective-permute-start(bf16[8,1536]{1,0:T(8,128)(2,1)S(1)} %get-tuple-element.43.refs_0_), channel_id=1, source_target_pairs={{0,12},{1,13},{2,14},{3,15},{4,8},{5,9},{6,10},{7,11},{8,4},{9,5},... | collective-permute-start | bytes 73736 | tf_op jit(solution)/shard_map/ppermute | solution.py:426
  10.4 3.8 %collective-permute-done.2.refs_2_ = bf16[8,1536]{1,0:T(8,128)(2,1)S(1)} collective-permute-done((bf16[8,1536]{1,0:T(8,128)(2,1)S(1)}, bf16[8,1536]{1,0:T(8,128)(2,1)S(1)}, u32[]{:S(2)}, u32[]{:S(2)}) %collective-permute-start.2) | collective-permute-done | bytes 24608 | tf_op jit(solution)/shard_map/ppermute | solution.py:426
  14.2 2.3 %project.1 = (bf16[2,144,128]{2,1,0:T(8,128)(2,1)S(1)}, bf16[2,144,128]{2,1,0:T(8,128)(2,1)S(1)}, bf16[2,144,128]{2,1,0:T(8,128)(2,1)S(1)}, bf16[2,144,128]{2,1,...) custom-call(bf16[8,1536]{1,0:T(8,128)(2,1)S(1)} %get-tuple-element.4, ...), custom_call_target="tpu_custom_call" | custom-call | flops 23000000512 | tf_op jit(solution)/shard_map/project/pallas_call | solution.py:36
  16.5 1.6 %collective-permute-start.6 = (bf16[4,144,128]{2,1,0:T(8,128)(2,1)S(1)}, bf16[4,144,128]{2,1,0:T(8,128)(2,1)S(1)}, u32[]{:S(2)}, u32[]{:S(2)}) collective-permute-start(bf16[4,144,128]{2,1,0:T(8,128)(2,1)S(1)} %get-tuple-element.45), channel_id=1, source_target_pairs={{0,2},{1,3},{2,0},{3,1},{4,6},{5,7},{6,4},{7,5},{8,10},{9,11},{10,... | collective-permute-start | bytes 442376 | tf_op jit(solution)/shard_map/ppermute | solution.py:426
  18.1 1.2 %collective-permute-start.7 = (bf16[2,144,128]{2,1,0:T(8,128)(2,1)S(1)}, bf16[2,144,128]{2,1,0:T(8,128)(2,1)S(1)}, u32[]{:S(2)}, u32[]{:S(2)}) collective-permute-start(bf16[2,144,128]{2,1,0:T(8,128)(2,1)S(1)} %get-tuple-element.46), channel_id=1, source_target_pairs={{0,8},{1,9},{2,10},{3,11},{4,12},{5,13},{6,14},{7,15},{8,0},{9,1},... | collective-permute-start | bytes 221192 | tf_op jit(solution)/shard_map/ppermute | solution.py:426
  19.4 1.6 %collective-permute-start.8 = (bf16[2,144,128]{2,1,0:T(8,128)(2,1)S(1)}, bf16[2,144,128]{2,1,0:T(8,128)(2,1)S(1)}, u32[]{:S(2)}, u32[]{:S(2)}) collective-permute-start(bf16[2,144,128]{2,1,0:T(8,128)(2,1)S(1)} %get-tuple-element.47), channel_id=1, source_target_pairs={{0,10},{1,11},{2,8},{3,9},{4,14},{5,15},{6,12},{7,13},{8,2},{9,3},... | collective-permute-start | bytes 221192 | tf_op jit(solution)/shard_map/ppermute | solution.py:426
  21.0 2.0 %collective-permute-start.9 = (bf16[2,144,128]{2,1,0:T(8,128)(2,1)S(1)}, bf16[2,144,128]{2,1,0:T(8,128)(2,1)S(1)}, u32[]{:S(2)}, u32[]{:S(2)}) collective-permute-start(bf16[2,144,128]{2,1,0:T(8,128)(2,1)S(1)} %get-tuple-element.48), channel_id=1, source_target_pairs={{0,12},{1,13},{2,14},{3,15},{4,8},{5,9},{6,10},{7,11},{8,4},{9,5},... | collective-permute-start | bytes 221192 | tf_op jit(solution)/shard_map/ppermute | solution.py:426
  23.0 2.8 %collective-permute-start.10 = (bf16[2,144,128]{2,1,0:T(8,128)(2,1)S(1)}, bf16[2,144,128]{2,1,0:T(8,128)(2,1)S(1)}, u32[]{:S(2)}, u32[]{:S(2)}) collective-permute-start(bf16[2,144,128]{2,1,0:T(8,128)(2,1)S(1)} %get-tuple-element.49), channel_id=1, source_target_pairs={{0,14},{1,15},{2,12},{3,13},{4,10},{5,11},{6,8},{7,9},{8,6},{9,7},... | collective-permute-start | bytes 221192 | tf_op jit(solution)/shard_map/ppermute | solution.py:426
  25.9 1.7 %flip.1.flip_ref = bf16[4,1536,512]{2,1,0:T(8,128)(2,1)S(1)} custom-call(bf16[4,576,1536]{2,1,0:T(8,128)(2,1)S(1)} %bitcast.5, bf16[4,144,128]{2,1,0:T(8,128)(2,1)S(1)} %forward.2.after_ref), custom_call_target="tpu_custom_call" | custom-call | flops 4600000000 | tf_op jit(solution)/shard_map/flip/pallas_call | solution.py:36
  28.1 2.4 %collective-permute-done.8.refs_1_ = bf16[2,144,128]{2,1,0:T(8,128)(2,1)S(1)} collective-permute-done((bf16[2,144,128]{2,1,0:T(8,128)(2,1)S(1)}, bf16[2,144,128]{2,1,0:T(8,128)(2,1)S(1)}, u32[]{:S(2)}, u32[]{:S(2)}) %collective-permute-start.8) | collective-permute-done | bytes 73760 | tf_op jit(solution)/shard_map/ppermute | solution.py:426
  30.6 1.2 %collective-permute-done.11.refs_5_ = bf16[4,144,128]{2,1,0:T(8,128)(2,1)S(1)} collective-permute-done((bf16[4,144,128]{2,1,0:T(8,128)(2,1)S(1)}, bf16[4,144,128]{2,1,0:T(8,128)(2,1)S(1)}, u32[]{:S(2)}, u32[]{:S(2)}) %collective-permute-start.11) | collective-permute-done | bytes 147488 | tf_op jit(solution)/shard_map/ppermute | solution.py:426
  31.8 3.4 %attend.1 = (bf16[2,32,512]{2,1,0:T(8,128)(2,1)S(1)}, bf16[2,32,512]{2,1,0:T(8,128)(2,1)S(1)}, bf16[2,32,512]{2,1,0:T(8,128)(2,1)S(1)}, bf16[2,32,512]{2,1,0:T(8...) custom-call(s32[4]{0:T(128)S(1)} %copy-done.5, ...), custom_call_target="tpu_custom_call" | custom-call | flops 11500000256 | tf_op jit(solution)/shard_map/attend/pallas_call | solution.py:36
  35.2 0.8 %collective-permute-start.16 = (bf16[4,32,512]{2,1,0:T(8,128)(2,1)S(1)}, bf16[4,32,512]{2,1,0:T(8,128)(2,1)S(1)}, u32[]{:S(2)}, u32[]{:S(2)}) collective-permute-start(bf16[4,32,512]{2,1,0:T(8,128)(2,1)S(1)} %get-tuple-element.55), channel_id=1, source_target_pairs={{0,2},{1,3},{2,0},{3,1},{4,6},{5,7},{6,4},{7,5},{8,10},{9,11},{10,... | collective-permute-start | bytes 393224 | tf_op jit(solution)/shard_map/ppermute | solution.py:426
  36.0 2.5 %collective-permute-start.12 = (bf16[2,32,512]{2,1,0:T(8,128)(2,1)S(1)}, bf16[2,32,512]{2,1,0:T(8,128)(2,1)S(1)}, u32[]{:S(2)}, u32[]{:S(2)}) collective-permute-start(bf16[2,32,512]{2,1,0:T(8,128)(2,1)S(1)} %get-tuple-element.51), channel_id=1, source_target_pairs={{0,8},{1,9},{2,10},{3,11},{4,12},{5,13},{6,14},{7,15},{8,0},{9,1},... | collective-permute-start | bytes 196616 | tf_op jit(solution)/shard_map/ppermute | solution.py:426
  38.5 1.1 %collective-permute-start.13 = (bf16[2,32,512]{2,1,0:T(8,128)(2,1)S(1)}, bf16[2,32,512]{2,1,0:T(8,128)(2,1)S(1)}, u32[]{:S(2)}, u32[]{:S(2)}) collective-permute-start(bf16[2,32,512]{2,1,0:T(8,128)(2,1)S(1)} %get-tuple-element.52), channel_id=1, source_target_pairs={{0,10},{1,11},{2,8},{3,9},{4,14},{5,15},{6,12},{7,13},{8,2},{9,3},... | collective-permute-start | bytes 196616 | tf_op jit(solution)/shard_map/ppermute | solution.py:426
  39.7 2.6 %collective-permute-start.14 = (bf16[2,32,512]{2,1,0:T(8,128)(2,1)S(1)}, bf16[2,32,512]{2,1,0:T(8,128)(2,1)S(1)}, u32[]{:S(2)}, u32[]{:S(2)}) collective-permute-start(bf16[2,32,512]{2,1,0:T(8,128)(2,1)S(1)} %get-tuple-element.53), channel_id=1, source_target_pairs={{0,12},{1,13},{2,14},{3,15},{4,8},{5,9},{6,10},{7,11},{8,4},{9,5},... | collective-permute-start | bytes 196616 | tf_op jit(solution)/shard_map/ppermute | solution.py:426
  42.3 1.3 %collective-permute-start.15 = (bf16[2,32,512]{2,1,0:T(8,128)(2,1)S(1)}, bf16[2,32,512]{2,1,0:T(8,128)(2,1)S(1)}, u32[]{:S(2)}, u32[]{:S(2)}) collective-permute-start(bf16[2,32,512]{2,1,0:T(8,128)(2,1)S(1)} %get-tuple-element.54), channel_id=1, source_target_pairs={{0,14},{1,15},{2,12},{3,13},{4,10},{5,11},{6,8},{7,9},{8,6},{9,7},... | collective-permute-start | bytes 196616 | tf_op jit(solution)/shard_map/ppermute | solution.py:426
  43.9 4.3 %collective-permute-done.13.refs_1_ = bf16[2,32,512]{2,1,0:T(8,128)(2,1)S(1)} collective-permute-done((bf16[2,32,512]{2,1,0:T(8,128)(2,1)S(1)}, bf16[2,32,512]{2,1,0:T(8,128)(2,1)S(1)}, u32[]{:S(2)}, u32[]{:S(2)}) %collective-permute-start.13) | collective-permute-done | bytes 65568 | tf_op jit(solution)/shard_map/ppermute | solution.py:426
  48.2 1.2 %collective-permute-done.15.refs_3_ = bf16[2,32,512]{2,1,0:T(8,128)(2,1)S(1)} collective-permute-done((bf16[2,32,512]{2,1,0:T(8,128)(2,1)S(1)}, bf16[2,32,512]{2,1,0:T(8,128)(2,1)S(1)}, u32[]{:S(2)}, u32[]{:S(2)}) %collective-permute-start.15) | collective-permute-done | bytes 65568 | tf_op jit(solution)/shard_map/ppermute | solution.py:426
  49.6 1.5 %collective-permute-done.18.refs_7_ = bf16[8,32,512]{2,1,0:T(8,128)(2,1)S(1)} collective-permute-done((bf16[8,32,512]{2,1,0:T(8,128)(2,1)S(1)}, bf16[8,32,512]{2,1,0:T(8,128)(2,1)S(1)}, u32[]{:S(2)}, u32[]{:S(2)}) %collective-permute-start.18) | collective-permute-done | bytes 262176 | tf_op jit(solution)/shard_map/ppermute | solution.py:426
  51.6 1.4 %terms.3 = (f32[32,3584]{1,0:T(8,128)S(1)}, bf16[32,3584]{1,0:T(8,128)(2,1)S(1)}) custom-call(bf16[64,1024]{1,0:T(8,128)(2,1)S(1)} %values.1.val_ref, bf16[1024,7168]{1,0:T(8,128)(2,1)S(1)} %bitcast.2), custom_call_target="tpu_custom_call" | custom-call | flops 6899999744 | tf_op jit(solution)/shard_map/terms/pallas_call | solution.py:36
  53.2 1.4 %terms.2 = (f32[32,3584]{1,0:T(8,128)S(1)}, bf16[32,3584]{1,0:T(8,128)(2,1)S(1)}) custom-call(bf16[64,1024]{1,0:T(8,128)(2,1)S(1)} %values.1.val_ref, bf16[1024,7168]{1,0:T(8,128)(2,1)S(1)} %bitcast.2), custom_call_target="tpu_custom_call" | custom-call | flops 6899999744 | tf_op jit(solution)/shard_map/terms/pallas_call | solution.py:36
  55.1 1.6 %collective-permute-start.23 = (bf16[8,3584]{1,0:T(8,128)(2,1)S(1)}, bf16[8,3584]{1,0:T(8,128)(2,1)S(1)}, u32[]{:S(2)}, u32[]{:S(2)}) collective-permute-start(bf16[8,3584]{1,0:T(8,128)(2,1)S(1)} %get-tuple-element.69), channel_id=1, source_target_pairs={{0,2},{1,3},{2,0},{3,1},{4,6},{5,7},{6,4},{7,5},{8,10},{9,11},{10,... | collective-permute-start | bytes 172040 | tf_op jit(solution)/shard_map/ppermute | solution.py:426
  56.8 1.0 %collective-permute-start.24 = (bf16[8,3584]{1,0:T(8,128)(2,1)S(1)}, bf16[8,3584]{1,0:T(8,128)(2,1)S(1)}, u32[]{:S(2)}, u32[]{:S(2)}) collective-permute-start(bf16[8,3584]{1,0:T(8,128)(2,1)S(1)} %get-tuple-element.70), channel_id=1, source_target_pairs={{0,2},{1,3},{2,0},{3,1},{4,6},{5,7},{6,4},{7,5},{8,10},{9,11},{10,... | collective-permute-start | bytes 172040 | tf_op jit(solution)/shard_map/ppermute | solution.py:426
  57.9 1.3 %collective-permute-start.21 = (bf16[8,7168]{1,0:T(8,128)(2,1)S(1)}, bf16[8,7168]{1,0:T(8,128)(2,1)S(1)}, u32[]{:S(2)}, u32[]{:S(2)}) collective-permute-start(bf16[8,7168]{1,0:T(8,128)(2,1)S(1)} %get-tuple-element.64), channel_id=1, source_target_pairs={{0,4},{1,5},{2,6},{3,7},{4,0},{5,1},{6,2},{7,3},{8,12},{9,13},{10,... | collective-permute-start | bytes 344072 | tf_op jit(solution)/shard_map/ppermute | solution.py:426
  59.3 1.7 %collective-permute-done.24.refs_3_ = bf16[8,3584]{1,0:T(8,128)(2,1)S(1)} collective-permute-done((bf16[8,3584]{1,0:T(8,128)(2,1)S(1)}, bf16[8,3584]{1,0:T(8,128)(2,1)S(1)}, u32[]{:S(2)}, u32[]{:S(2)}) %collective-permute-start.24) | collective-permute-done | bytes 57376 | tf_op jit(solution)/shard_map/ppermute | solution.py:426
  61.1 1.6 %collective-permute-start.25 = (bf16[4,7168]{1,0:T(4,128)(2,1)S(1)}, bf16[4,7168]{1,0:T(4,128)(2,1)S(1)}, u32[]{:S(2)}, u32[]{:S(2)}) collective-permute-start(bf16[4,7168]{1,0:T(4,128)(2,1)S(1)} %get-tuple-element.71), channel_id=1, source_target_pairs={{0,8},{1,9},{2,10},{3,11},{4,12},{5,13},{6,14},{7,15},{8,0},{9,1},... | collective-permute-start | bytes 172040 | tf_op jit(solution)/shard_map/ppermute | solution.py:426
  62.7 2.2 %collective-permute-start.26 = (bf16[4,7168]{1,0:T(4,128)(2,1)S(1)}, bf16[4,7168]{1,0:T(4,128)(2,1)S(1)}, u32[]{:S(2)}, u32[]{:S(2)}) collective-permute-start(bf16[4,7168]{1,0:T(4,128)(2,1)S(1)} %get-tuple-element.72), channel_id=1, source_target_pairs={{0,12},{1,13},{2,14},{3,15},{4,8},{5,9},{6,10},{7,11},{8,4},{9,5},... | collective-permute-start | bytes 172040 | tf_op jit(solution)/shard_map/ppermute | solution.py:426
  64.9 1.0 %collective-permute-start.22 = (bf16[4,7168]{1,0:T(4,128)(2,1)S(1)}, bf16[4,7168]{1,0:T(4,128)(2,1)S(1)}, u32[]{:S(2)}, u32[]{:S(2)}) collective-permute-start(bf16[4,7168]{1,0:T(4,128)(2,1)S(1)} %get-tuple-element.66), channel_id=1, source_target_pairs={{0,2},{1,3},{2,0},{3,1},{4,6},{5,7},{6,4},{7,5},{8,10},{9,11},{10,... | collective-permute-start | bytes 172040 | tf_op jit(solution)/shard_map/ppermute | solution.py:426
  66.4 2.3 %collective-permute-done.26.refs_3_ = bf16[4,7168]{1,0:T(4,128)(2,1)S(1)} collective-permute-done((bf16[4,7168]{1,0:T(4,128)(2,1)S(1)}, bf16[4,7168]{1,0:T(4,128)(2,1)S(1)}, u32[]{:S(2)}, u32[]{:S(2)}) %collective-permute-start.26) | collective-permute-done | bytes 57376 | tf_op jit(solution)/shard_map/ppermute | solution.py:426
  (70 shorter events, 6.8 us)
Async XLA Ops:
  0.0 14.2 %collective-permute-start.4 = (bf16[1536,1536]{1,0:T(8,128)(2,1)}, bf16[1536,1536]{1,0:T(8,128)(2,1)S(1)}, u32[]{:S(2)}, u32[]{:S(2)}) collective-permute-start(bf16[1536,1536]{1,0:T(8,128)(2,1)} %refs_4_.1), channel_id=1, source_target_pairs={{0,1},{1,0},{2,3},{3,2},{4,5},{5,4},{6,7},{7,6},{8,9},{9,8},{10,11... | collective-permute-start | bytes 14155784 | tf_op jit(solution)/shard_map/ppermute | solution.py:426
  0.5 13.7 %collective-permute-start.5 = (bf16[8,128,512]{2,1,0:T(8,128)(2,1)}, bf16[8,128,512]{2,1,0:T(8,128)(2,1)S(1)}, u32[]{:S(2)}, u32[]{:S(2)}) collective-permute-start(bf16[8,128,512]{2,1,0:T(8,128)(2,1)} %refs_5_.1), channel_id=1, source_target_pairs={{0,1},{1,0},{2,3},{3,2},{4,5},{5,4},{6,7},{7,6},{8,9},{9,8},{10,11... | collective-permute-start | bytes 3145736 | tf_op jit(solution)/shard_map/ppermute | solution.py:426
  0.5 4.8 %collective-permute-start = (bf16[4,1536]{1,0:T(4,128)(2,1)}, bf16[4,1536]{1,0:T(4,128)(2,1)S(1)}, u32[]{:S(2)}, u32[]{:S(2)}) collective-permute-start(bf16[4,1536]{1,0:T(4,128)(2,1)} %refs_0_.1), channel_id=1, source_target_pairs={{0,2},{1,3},{2,0},{3,1},{4,6},{5,7},{6,4},{7,5},{8,10},{9,11},{10,... | collective-permute-start | bytes 36872 | tf_op jit(solution)/shard_map/ppermute | solution.py:426
  4.1 10.1 %slice-start.6 = ((s8[4718592]{0:T(1024)(128)(4,1)}), s8[4194304]{0:T(1024)(128)(4,1)S(1)}, s32[]{:S(2)}) async-start(s8[4718592]{0:T(1024)(128)(4,1)} %bitcast.7), calls=%async_computation.6 | async-start | bytes 8388608
  5.4 8.9 %slice-start.7 = ((s8[4718592]{0:T(1024)(128)(4,1)}), s8[524288]{0:T(1024)(128)(4,1)S(1)}, s32[]{:S(2)}) async-start(s8[4718592]{0:T(1024)(128)(4,1)} %bitcast.7), calls=%async_computation.7 | async-start | bytes 1048576
  5.4 8.9 %copy-start = (bf16[8,128,512]{2,1,0:T(8,128)(2,1)S(1)}, bf16[8,128,512]{2,1,0:T(8,128)(2,1)}, u32[]{:S(2)}) copy-start(bf16[8,128,512]{2,1,0:T(8,128)(2,1)} %refs_5_.1) | copy-start | bytes 3145732
  5.4 20.5 %slice-start.4 = ((s8[7077888]{0:T(1024)(128)(4,1)}), s8[4194304]{0:T(1024)(128)(4,1)S(1)}, s32[]{:S(2)}) async-start(s8[7077888]{0:T(1024)(128)(4,1)} %bitcast.3), calls=%async_computation.4 | async-start | bytes 8388608
  5.4 20.5 %slice-start.5 = ((s8[7077888]{0:T(1024)(128)(4,1)}), s8[2883584]{0:T(1024)(128)(4,1)S(1)}, s32[]{:S(2)}) async-start(s8[7077888]{0:T(1024)(128)(4,1)} %bitcast.3), calls=%async_computation.5 | async-start | bytes 5767168
  5.4 5.0 %collective-permute-start.3 = (bf16[8,1536]{1,0:T(8,128)(2,1)S(1)}, bf16[8,1536]{1,0:T(8,128)(2,1)S(1)}, u32[]{:S(2)}, u32[]{:S(2)}) collective-permute-start(bf16[8,1536]{1,0:T(8,128)(2,1)S(1)} %get-tuple-element.43.refs_0_), channel_id=1, source_target_pairs={{0,8},{1,9},{2,10},{3,11},{4,12},{5,13},{6,14},{7,15},{8,0},{9,1},... | collective-permute-start | bytes 73736 | tf_op jit(solution)/shard_map/ppermute | solution.py:426
  8.6 5.6 %collective-permute-start.2 = (bf16[8,1536]{1,0:T(8,128)(2,1)S(1)}, bf16[8,1536]{1,0:T(8,128)(2,1)S(1)}, u32[]{:S(2)}, u32[]{:S(2)}) collective-permute-start(bf16[8,1536]{1,0:T(8,128)(2,1)S(1)} %get-tuple-element.43.refs_0_), channel_id=1, source_target_pairs={{0,12},{1,13},{2,14},{3,15},{4,8},{5,9},{6,10},{7,11},{8,4},{9,5},... | collective-permute-start | bytes 73736 | tf_op jit(solution)/shard_map/ppermute | solution.py:426
  9.9 4.3 %collective-permute-start.1 = (bf16[8,1536]{1,0:T(8,128)(2,1)S(1)}, bf16[8,1536]{1,0:T(8,128)(2,1)S(1)}, u32[]{:S(2)}, u32[]{:S(2)}) collective-permute-start(bf16[8,1536]{1,0:T(8,128)(2,1)S(1)} %get-tuple-element.43.refs_0_), channel_id=1, source_target_pairs={{0,4},{1,5},{2,6},{3,7},{4,0},{5,1},{6,2},{7,3},{8,12},{9,13},{10,... | collective-permute-start | bytes 73736 | tf_op jit(solution)/shard_map/ppermute | solution.py:426
  16.5 9.2 %collective-permute-start.6 = (bf16[4,144,128]{2,1,0:T(8,128)(2,1)S(1)}, bf16[4,144,128]{2,1,0:T(8,128)(2,1)S(1)}, u32[]{:S(2)}, u32[]{:S(2)}) collective-permute-start(bf16[4,144,128]{2,1,0:T(8,128)(2,1)S(1)} %get-tuple-element.45), channel_id=1, source_target_pairs={{0,2},{1,3},{2,0},{3,1},{4,6},{5,7},{6,4},{7,5},{8,10},{9,11},{10,... | collective-permute-start | bytes 442376 | tf_op jit(solution)/shard_map/ppermute | solution.py:426
  18.1 10.0 %collective-permute-start.7 = (bf16[2,144,128]{2,1,0:T(8,128)(2,1)S(1)}, bf16[2,144,128]{2,1,0:T(8,128)(2,1)S(1)}, u32[]{:S(2)}, u32[]{:S(2)}) collective-permute-start(bf16[2,144,128]{2,1,0:T(8,128)(2,1)S(1)} %get-tuple-element.46), channel_id=1, source_target_pairs={{0,8},{1,9},{2,10},{3,11},{4,12},{5,13},{6,14},{7,15},{8,0},{9,1},... | collective-permute-start | bytes 221192 | tf_op jit(solution)/shard_map/ppermute | solution.py:426
  19.4 11.2 %collective-permute-start.8 = (bf16[2,144,128]{2,1,0:T(8,128)(2,1)S(1)}, bf16[2,144,128]{2,1,0:T(8,128)(2,1)S(1)}, u32[]{:S(2)}, u32[]{:S(2)}) collective-permute-start(bf16[2,144,128]{2,1,0:T(8,128)(2,1)S(1)} %get-tuple-element.47), channel_id=1, source_target_pairs={{0,10},{1,11},{2,8},{3,9},{4,14},{5,15},{6,12},{7,13},{8,2},{9,3},... | collective-permute-start | bytes 221192 | tf_op jit(solution)/shard_map/ppermute | solution.py:426
  21.0 9.6 %collective-permute-start.9 = (bf16[2,144,128]{2,1,0:T(8,128)(2,1)S(1)}, bf16[2,144,128]{2,1,0:T(8,128)(2,1)S(1)}, u32[]{:S(2)}, u32[]{:S(2)}) collective-permute-start(bf16[2,144,128]{2,1,0:T(8,128)(2,1)S(1)} %get-tuple-element.48), channel_id=1, source_target_pairs={{0,12},{1,13},{2,14},{3,15},{4,8},{5,9},{6,10},{7,11},{8,4},{9,5},... | collective-permute-start | bytes 221192 | tf_op jit(solution)/shard_map/ppermute | solution.py:426
  23.0 7.6 %collective-permute-start.10 = (bf16[2,144,128]{2,1,0:T(8,128)(2,1)S(1)}, bf16[2,144,128]{2,1,0:T(8,128)(2,1)S(1)}, u32[]{:S(2)}, u32[]{:S(2)}) collective-permute-start(bf16[2,144,128]{2,1,0:T(8,128)(2,1)S(1)} %get-tuple-element.49), channel_id=1, source_target_pairs={{0,14},{1,15},{2,12},{3,13},{4,10},{5,11},{6,8},{7,9},{8,6},{9,7},... | collective-permute-start | bytes 221192 | tf_op jit(solution)/shard_map/ppermute | solution.py:426
  25.8 6.0 %collective-permute-start.11 = (bf16[4,144,128]{2,1,0:T(8,128)(2,1)S(1)}, bf16[4,144,128]{2,1,0:T(8,128)(2,1)S(1)}, u32[]{:S(2)}, u32[]{:S(2)}) collective-permute-start(bf16[4,144,128]{2,1,0:T(8,128)(2,1)S(1)} %forward.2.after_ref), channel_id=1, source_target_pairs={{0,4},{1,5},{2,6},{3,7},{4,0},{5,1},{6,2},{7,3},{8,12},{9,13},{10,... | collective-permute-start | bytes 442376 | tf_op jit(solution)/shard_map/ppermute | solution.py:426
  35.2 8.4 %collective-permute-start.16 = (bf16[4,32,512]{2,1,0:T(8,128)(2,1)S(1)}, bf16[4,32,512]{2,1,0:T(8,128)(2,1)S(1)}, u32[]{:S(2)}, u32[]{:S(2)}) collective-permute-start(bf16[4,32,512]{2,1,0:T(8,128)(2,1)S(1)} %get-tuple-element.55), channel_id=1, source_target_pairs={{0,2},{1,3},{2,0},{3,1},{4,6},{5,7},{6,4},{7,5},{8,10},{9,11},{10,... | collective-permute-start | bytes 393224 | tf_op jit(solution)/shard_map/ppermute | solution.py:426
  36.0 7.9 %collective-permute-start.12 = (bf16[2,32,512]{2,1,0:T(8,128)(2,1)S(1)}, bf16[2,32,512]{2,1,0:T(8,128)(2,1)S(1)}, u32[]{:S(2)}, u32[]{:S(2)}) collective-permute-start(bf16[2,32,512]{2,1,0:T(8,128)(2,1)S(1)} %get-tuple-element.51), channel_id=1, source_target_pairs={{0,8},{1,9},{2,10},{3,11},{4,12},{5,13},{6,14},{7,15},{8,0},{9,1},... | collective-permute-start | bytes 196616 | tf_op jit(solution)/shard_map/ppermute | solution.py:426
  38.5 9.7 %collective-permute-start.13 = (bf16[2,32,512]{2,1,0:T(8,128)(2,1)S(1)}, bf16[2,32,512]{2,1,0:T(8,128)(2,1)S(1)}, u32[]{:S(2)}, u32[]{:S(2)}) collective-permute-start(bf16[2,32,512]{2,1,0:T(8,128)(2,1)S(1)} %get-tuple-element.52), channel_id=1, source_target_pairs={{0,10},{1,11},{2,8},{3,9},{4,14},{5,15},{6,12},{7,13},{8,2},{9,3},... | collective-permute-start | bytes 196616 | tf_op jit(solution)/shard_map/ppermute | solution.py:426
  39.7 8.6 %collective-permute-start.14 = (bf16[2,32,512]{2,1,0:T(8,128)(2,1)S(1)}, bf16[2,32,512]{2,1,0:T(8,128)(2,1)S(1)}, u32[]{:S(2)}, u32[]{:S(2)}) collective-permute-start(bf16[2,32,512]{2,1,0:T(8,128)(2,1)S(1)} %get-tuple-element.53), channel_id=1, source_target_pairs={{0,12},{1,13},{2,14},{3,15},{4,8},{5,9},{6,10},{7,11},{8,4},{9,5},... | collective-permute-start | bytes 196616 | tf_op jit(solution)/shard_map/ppermute | solution.py:426
  42.3 7.1 %collective-permute-start.15 = (bf16[2,32,512]{2,1,0:T(8,128)(2,1)S(1)}, bf16[2,32,512]{2,1,0:T(8,128)(2,1)S(1)}, u32[]{:S(2)}, u32[]{:S(2)}) collective-permute-start(bf16[2,32,512]{2,1,0:T(8,128)(2,1)S(1)} %get-tuple-element.54), channel_id=1, source_target_pairs={{0,14},{1,15},{2,12},{3,13},{4,10},{5,11},{6,8},{7,9},{8,6},{9,7},... | collective-permute-start | bytes 196616 | tf_op jit(solution)/shard_map/ppermute | solution.py:426
  43.7 5.8 %collective-permute-start.17 = (bf16[4,32,512]{2,1,0:T(8,128)(2,1)S(1)}, bf16[4,32,512]{2,1,0:T(8,128)(2,1)S(1)}, u32[]{:S(2)}, u32[]{:S(2)}) collective-permute-start(bf16[4,32,512]{2,1,0:T(8,128)(2,1)S(1)} %forward.3.after_ref), channel_id=1, source_target_pairs={{0,4},{1,5},{2,6},{3,7},{4,0},{5,1},{6,2},{7,3},{8,12},{9,13},{10,... | collective-permute-start | bytes 393224 | tf_op jit(solution)/shard_map/ppermute | solution.py:426
  49.5 1.6 %collective-permute-start.18 = (bf16[8,32,512]{2,1,0:T(8,128)(2,1)S(1)}, bf16[8,32,512]{2,1,0:T(8,128)(2,1)S(1)}, u32[]{:S(2)}, u32[]{:S(2)}) collective-permute-start(bf16[8,32,512]{2,1,0:T(8,128)(2,1)S(1)} %regroup.1), channel_id=1, source_target_pairs={{0,1},{1,0},{2,3},{3,2},{4,5},{5,4},{6,7},{7,6},{8,9},{9,8},{10,11... | collective-permute-start | bytes 786440 | tf_op jit(solution)/shard_map/ppermute | solution.py:426
  53.0 2.0 %collective-permute-start.20 = (bf16[32,3584]{1,0:T(8,128)(2,1)S(1)}, bf16[32,3584]{1,0:T(8,128)(2,1)S(1)}, u32[]{:S(2)}, u32[]{:S(2)}) collective-permute-start(bf16[32,3584]{1,0:T(8,128)(2,1)S(1)} %get-tuple-element.61), channel_id=1, source_target_pairs={{0,1},{1,0},{2,3},{3,2},{4,5},{5,4},{6,7},{7,6},{8,9},{9,8},{10,11... | collective-permute-start | bytes 688136 | tf_op jit(solution)/shard_map/ppermute | solution.py:426
  54.6 2.2 %collective-permute-start.19 = (bf16[32,3584]{1,0:T(8,128)(2,1)S(1)}, bf16[32,3584]{1,0:T(8,128)(2,1)S(1)}, u32[]{:S(2)}, u32[]{:S(2)}) collective-permute-start(bf16[32,3584]{1,0:T(8,128)(2,1)S(1)} %get-tuple-element.59), channel_id=1, source_target_pairs={{0,1},{1,0},{2,3},{3,2},{4,5},{5,4},{6,7},{7,6},{8,9},{9,8},{10,11... | collective-permute-start | bytes 688136 | tf_op jit(solution)/shard_map/ppermute | solution.py:426
  55.1 4.2 %collective-permute-start.23 = (bf16[8,3584]{1,0:T(8,128)(2,1)S(1)}, bf16[8,3584]{1,0:T(8,128)(2,1)S(1)}, u32[]{:S(2)}, u32[]{:S(2)}) collective-permute-start(bf16[8,3584]{1,0:T(8,128)(2,1)S(1)} %get-tuple-element.69), channel_id=1, source_target_pairs={{0,2},{1,3},{2,0},{3,1},{4,6},{5,7},{6,4},{7,5},{8,10},{9,11},{10,... | collective-permute-start | bytes 172040 | tf_op jit(solution)/shard_map/ppermute | solution.py:426
  56.8 4.2 %collective-permute-start.24 = (bf16[8,3584]{1,0:T(8,128)(2,1)S(1)}, bf16[8,3584]{1,0:T(8,128)(2,1)S(1)}, u32[]{:S(2)}, u32[]{:S(2)}) collective-permute-start(bf16[8,3584]{1,0:T(8,128)(2,1)S(1)} %get-tuple-element.70), channel_id=1, source_target_pairs={{0,2},{1,3},{2,0},{3,1},{4,6},{5,7},{6,4},{7,5},{8,10},{9,11},{10,... | collective-permute-start | bytes 172040 | tf_op jit(solution)/shard_map/ppermute | solution.py:426
  57.9 7.0 %collective-permute-start.21 = (bf16[8,7168]{1,0:T(8,128)(2,1)S(1)}, bf16[8,7168]{1,0:T(8,128)(2,1)S(1)}, u32[]{:S(2)}, u32[]{:S(2)}) collective-permute-start(bf16[8,7168]{1,0:T(8,128)(2,1)S(1)} %get-tuple-element.64), channel_id=1, source_target_pairs={{0,4},{1,5},{2,6},{3,7},{4,0},{5,1},{6,2},{7,3},{8,12},{9,13},{10,... | collective-permute-start | bytes 344072 | tf_op jit(solution)/shard_map/ppermute | solution.py:426
  61.1 5.3 %collective-permute-start.25 = (bf16[4,7168]{1,0:T(4,128)(2,1)S(1)}, bf16[4,7168]{1,0:T(4,128)(2,1)S(1)}, u32[]{:S(2)}, u32[]{:S(2)}) collective-permute-start(bf16[4,7168]{1,0:T(4,128)(2,1)S(1)} %get-tuple-element.71), channel_id=1, source_target_pairs={{0,8},{1,9},{2,10},{3,11},{4,12},{5,13},{6,14},{7,15},{8,0},{9,1},... | collective-permute-start | bytes 172040 | tf_op jit(solution)/shard_map/ppermute | solution.py:426
  62.7 6.0 %collective-permute-start.26 = (bf16[4,7168]{1,0:T(4,128)(2,1)S(1)}, bf16[4,7168]{1,0:T(4,128)(2,1)S(1)}, u32[]{:S(2)}, u32[]{:S(2)}) collective-permute-start(bf16[4,7168]{1,0:T(4,128)(2,1)S(1)} %get-tuple-element.72), channel_id=1, source_target_pairs={{0,12},{1,13},{2,14},{3,15},{4,8},{5,9},{6,10},{7,11},{8,4},{9,5},... | collective-permute-start | bytes 172040 | tf_op jit(solution)/shard_map/ppermute | solution.py:426
  64.9 4.2 %collective-permute-start.22 = (bf16[4,7168]{1,0:T(4,128)(2,1)S(1)}, bf16[4,7168]{1,0:T(4,128)(2,1)S(1)}, u32[]{:S(2)}, u32[]{:S(2)}) collective-permute-start(bf16[4,7168]{1,0:T(4,128)(2,1)S(1)} %get-tuple-element.66), channel_id=1, source_target_pairs={{0,2},{1,3},{2,0},{3,1},{4,6},{5,7},{6,4},{7,5},{8,10},{9,11},{10,... | collective-permute-start | bytes 172040 | tf_op jit(solution)/shard_map/ppermute | solution.py:426
  (9 other events, 50.6 us)

commit v12 on v8

--- a/solution.py
+++ b/solution.py
@@ -57,14 +57,21 @@
     return sorted(range(0, devices, step), key=lambda k: -k.bit_length())
 
 
-def chip_order(devices):
-    chips = far_first(devices, 2)
-    far = chips[: len(chips) // 2]
-    near = sorted(chips[len(chips) // 2 :])[1:]
-    mixed = far[:1]
-    for k, other in zip(far[1:], near):
-        mixed += [k, other]
-    return mixed + [0]
+def far_chips(devices):
+    return [k for k in far_first(devices, 2) if k > Y + Z1]
+
+
+def chip_orders(devices):
+    far, near = far_chips(devices), [Y, Z1, Y + Z1]
+    return [*near, *far, 0], [*far, *near, 0]
+
+
+def on_odd_core():
+    return lax.rem(lax.axis_index("row"), 2) == 1
+
+
+def block_at(odd, even_place, odd_place, size):
+    return pl.ds(pl.multiple_of(jnp.where(odd, odd_place, even_place) * size, size), size)
 
 
 def gathered_order(devices):
@@ -120,7 +127,9 @@
     wide = 2 * count // devices * heads
     width = NOPE + ROPE
     lane = lax.broadcasted_iota(jnp.int32, (wide // 2, LANES), 1)
-    order = chip_order(devices)
+    odd = on_odd_core()
+    gathered = gathered_order(devices)
+    orders = zip(*[[gathered.index(k) for k in order] for order in chip_orders(devices)])
     for core, (wq_ref, wk_ref) in enumerate(weights):
         projected = jnp.dot(piece, wq_ref[...], preferred_element_type=jnp.float32)
         for h in range(heads):
@@ -128,23 +137,21 @@
             absorbed = jnp.dot(
                 mine[:, :NOPE].astype(jnp.bfloat16), wk_ref[h], preferred_element_type=jnp.float32
             )
-            at = pl.ds(h, count, stride=heads)
+            spread = pl.ds(h, count, stride=heads)
             for c in range(PIECES):
-                lat_ref[core * PIECES + c, at, :] = absorbed[:, c * LANES : (c + 1) * LANES]
+                lat_ref[core * PIECES + c, spread, :] = absorbed[:, c * LANES : (c + 1) * LANES]
             pe = mine[:, NOPE:]
-            rot_ref[core, at, :] = jnp.concatenate([pe, pe], axis=-1)
-        for place, k in enumerate(gathered_order(devices)):
-            out_ref = out_refs[order.index(k)]
-            first = place * wide
+            rot_ref[core, spread, :] = jnp.concatenate([pe, pe], axis=-1)
+    for out_ref, (even_place, odd_place) in zip(out_refs, orders):
+        here = block_at(odd, even_place, odd_place, wide)
+        for core in range(2):
             for c in range(PIECES):
                 out_ref[core, c * wide : (c + 1) * wide, :] = lat_ref[
-                    core * PIECES + c, first : first + wide, :
+                    core * PIECES + c, here, :
                 ].astype(jnp.bfloat16)
-            low = rot_ref[core, first : first + wide // 2, :]
-            high = rot_ref[core, first + wide // 2 : first + wide, :]
-            out_ref[core, PIECES * wide :, :] = jnp.where(lane < ROPE, low, high).astype(
-                jnp.bfloat16
-            )
+            pair = rot_ref[core, here, :]
+            packed = jnp.where(lane < ROPE, pair[: wide // 2], pair[wide // 2 :])
+            out_ref[core, PIECES * wide :, :] = packed.astype(jnp.bfloat16)
 
 
 def project(pieces, weights, devices):
@@ -171,21 +178,17 @@
 
 
 def attend_kernel(chips, len_ref, cos_ref, sin_ref, key_ref, flip_ref, new_ref, *refs):
-    q_refs = refs[:chips]
+    blocks = [(ref, core) for ref in refs[:chips] for core in range(2)]
     out_refs = refs[chips:]
     rows, _, maxlen = key_ref.shape
     wide = out_refs[0].shape[1]
     heads = wide // rows
 
     def query_block(first):
-        blocks = [
-            ref[core, first : first + heads, :].astype(jnp.float32)
-            for ref in q_refs
-            for core in range(2)
-        ]
-        return jnp.concatenate(blocks, axis=0)
-
-    for r in range(rows):
+        parts = [ref[i, first : first + heads, :].astype(jnp.float32) for ref, i in blocks]
+        return jnp.concatenate(parts, axis=0)
+
+    def score(r):
         latent = jnp.concatenate(
             [query_block(c * wide + r * heads) for c in range(PIECES)], axis=-1
         )
@@ -203,7 +206,13 @@
         )
         scores += jnp.dot(rotated, key_ref[r, LAT:, :], preferred_element_type=jnp.float32)
         position = lax.broadcasted_iota(jnp.int32, (1, maxlen), 1)
-        scores = jnp.where(position < len_ref[r], scores, -jnp.inf)
+        return jnp.where(position < len_ref[r], scores, -jnp.inf), own
+
+    ahead = score(0)
+    for r in range(rows):
+        scores, own = ahead
+        if r + 1 < rows:
+            ahead = score(r + 1)
         peak = jnp.maximum(jnp.max(scores, axis=-1, keepdims=True), own)
         expo = jnp.exp2((scores - peak) * SCALE)
         own_expo = jnp.exp2((own - peak) * SCALE)
@@ -211,7 +220,7 @@
         weights = (expo * inverse).astype(jnp.bfloat16)
         own_weight = (own_expo * inverse).astype(jnp.bfloat16).astype(jnp.float32)
         summed = jnp.dot(weights, flip_ref[r], preferred_element_type=jnp.float32)
-        summed += own_weight * newest[:, :LAT]
+        summed += own_weight * new_ref[r : r + 1, :LAT].astype(jnp.float32)
         for k in range(2 * chips):
             out_refs[k // 2][k % 2, r * heads : (r + 1) * heads, :] = summed[
                 k * heads : (k + 1) * heads, :
@@ -220,9 +229,8 @@
 
 def attend(lengths, tables, keys, flipped, new_latent, messages, heads):
     chips = len(messages)
-    kernel = functools.partial(attend_kernel, chips)
-    block = shape(2, keys.shape[0] * heads, LAT)
-    return call(kernel, [block] * chips, 2 + chips, "attend", scalars=1)(
+    out = [shape(2, keys.shape[0] * heads, LAT)] * chips
+    return call(functools.partial(attend_kernel, chips), out, 10, "attend", scalars=1)(
         lengths, *tables, resident(keys), resident(flipped), new_latent, *messages
     )
 
@@ -238,16 +246,21 @@
     return call(regroup_kernel, shape(len(messages), wide, width), 1, "regroup")(*messages)
 
 
-def values_kernel(chips, *refs):
+def values_kernel(devices, *refs):
+    chips = devices // 2
     mine_refs = refs[:chips]
     other_ref, wv_ref, val_ref, rows_ref = refs[chips:]
     heads = wv_ref.shape[0]
     wide = other_ref.shape[1]
-    for place in range(2 * chips):
-        block = mine_refs[place][0] if place < chips else other_ref[place - chips]
-        block = block.astype(jnp.float32)
-        for c in range(PIECES):
-            rows_ref[c, place * wide : (place + 1) * wide, :] = block[:, c * LANES : (c + 1) * LANES]
+    odd = on_odd_core()
+    orders = [places(devices, order) for order in chip_orders(devices)]
+    for i, (even_place, odd_place) in enumerate(zip(*orders)):
+        mine = block_at(odd, even_place, odd_place, wide)
+        other = block_at(odd, chips + odd_place, chips + even_place, wide)
+        for where, block in ((mine, mine_refs[i][0]), (other, other_ref[i])):
+            block = block.astype(jnp.float32)
+            for c in range(PIECES):
+                rows_ref[c, where, :] = block[:, c * LANES : (c + 1) * LANES]
     count = val_ref.shape[0]
     for h in range(heads):
         chosen = jnp.concatenate(
@@ -258,12 +271,12 @@
         ).astype(jnp.bfloat16)
 
 
-def head_values(messages, other, w_uv):
+def head_values(messages, other, w_uv, devices):
     chips, wide, _ = other.shape
     heads = w_uv.shape[0]
     count = 2 * chips * wide // heads
     scratch = [pltpu.VMEM((PIECES, count * heads, LANES), jnp.float32)]
-    kernel = functools.partial(values_kernel, chips)
+    kernel = functools.partial(values_kernel, devices)
     return call(kernel, shape(count, heads * VD), 3, "values", scratch)(
         *messages, other, resident(w_uv)
     )
@@ -291,7 +304,7 @@
 
 
 def places(devices, chips):
-    order = chip_order(devices)
+    order = far_first(devices, 2)
     return [order.index(k) for k in chips]
 
 
@@ -381,7 +394,6 @@
 def on_device(q_latent, new_latent, cache, lengths, w_uq, w_uk, w_uv, w_o, devices):
     heads = w_uk.shape[0]
     rows = cache.shape[0]
-    order = chip_order(devices)
     zs = far_first(devices, 4)[::-1]
 
     def swap(block, k):
@@ -389,15 +401,23 @@
             return block
         return lax.ppermute(block, "row", [(i, i ^ k) for i in range(devices)])
 
+    across = swap(q_latent, Y)
     far_weights = [swap(w_uq, 1), swap(w_uk, 1)]
-    tables, near = join(rotary(lengths), [q_latent, swap(q_latent, 2)])
+    tables, near = join(rotary(lengths), [q_latent, across])
+    def exchange(messages):
+        got = []
+        for block, flips in zip(messages, zip(*chip_orders(devices))):
+            pairs = [(i, i ^ flips[i % 2]) for i in range(devices)]
+            got.append(lax.ppermute(block, "row", pairs) if any(flips) else block)
+        return got
+
     messages = project([swap(near, z) for z in zs], [w_uq, w_uk, *far_weights], devices)
     keys = jnp.swapaxes(cache, 1, 2)
     flipped = flip(keys, messages[-1])
-    messages = [swap(block, k) for k, block in zip(order, messages)]
+    messages = exchange(messages)
     latents = attend(lengths, tables, keys, flipped, new_latent, messages, heads)
-    latents = [swap(block, k) for k, block in zip(order, latents)]
-    values = head_values(latents, swap(regroup(latents), 1), w_uv)
+    latents = exchange(latents)
+    values = head_values(latents, swap(regroup(latents), 1), w_uv, devices)
     keep, got, near = [], [], None
     for part in range(PARTS):
         mine, other = output_terms(values, w_o, part)

time: 72.8 us -> 70.7 us (0.971)
  waiting for transfers between devices: 23.9 us -> 20 us
  starting transfers between devices: 34.8 us -> 37.3 us
  Pallas kernels: 13 us -> 12.2 us
    ppermute x0 -> x14, starting transfers between devices: none -> 22.4 us  [exchange(): got.append(lax.ppermute(block, 'row', pairs) if any(flips) else block)]
    ppermute x29 -> x15, starting transfers between devices: 34.8 us -> 14.9 us  [swap(): return lax.ppermute(block, 'row', [(i, i ^ k) for i in range(devices)])]
    ppermute x29 -> x15, waiting for transfers between devices: 23.9 us -> 12.5 us  [swap(): return lax.ppermute(block, 'row', [(i, i ^ k) for i in range(devices)])]
    ppermute x0 -> x14, waiting for transfers between devices: none -> 7.58 us  [exchange(): got.append(lax.ppermute(block, 'row', pairs) if any(flips) else block)]
    pallas_call x14, Pallas kernels: 13 us -> 12.2 us  [run(): pl.pallas_call(kernel, out_shape=out_shape, in_specs=smem + [in_vmem()] *...]
  transfers between devices with their start and end apart: 29 -> 29, of which waited for: 16 -> 12; matrix products, arithmetic and copies ran while one was open for 0% -> 0% of each run, Pallas kernels for 5% -> 5%
where the time goes in v12:
time: 70.7 us; the launch traced here: 70.5 us
  starting transfers between devices  37.3 us (53%)
  waiting for transfers between devices  20 us (28%)
  Pallas kernels  12.2 us (17%)
  local copies, waits for them, and re-layouts  0.71 us (1%)
    ppermute x14, starting transfers between devices, exchange(): got.append(lax.ppermute(block, 'row', pairs) if any(flips) else block)  22.4 us
    ppermute x15, starting transfers between devices, swap(): return lax.ppermute(block, 'row', [(i, i ^ k) for i in range(devices)])  14.9 us
    ppermute x15, waiting for transfers between devices, swap(): return lax.ppermute(block, 'row', [(i, i ^ k) for i in range(devices)])  12.5 us
    pallas_call x14, Pallas kernels, run(): pl.pallas_call(kernel, out_shape=out_shape, in_specs=smem + [in_vmem()] *...  12.2 us
    ppermute x14, waiting for transfers between devices, exchange(): got.append(lax.ppermute(block, 'row', pairs) if any(flips) else block)  7.58 us
  transfers between devices with their start and end apart: 29, of which 12 were waited for; matrix products, arithmetic and copies ran while one was open for 0% of the time, Pallas kernels for 5%

profile of v12, /device:TPU:0, one launch (start us, length us, event | category | flops | bytes accessed | tf_op | source)
XLA Modules:
  0.0 70.5 jit_solution(12961597865656366923)
XLA Ops:
  0.5 3.0 %collective-permute-start = (bf16[4,1536]{1,0:T(4,128)(2,1)}, bf16[4,1536]{1,0:T(4,128)(2,1)S(1)}, u32[]{:S(2)}, u32[]{:S(2)}) collective-permute-start(bf16[4,1536]{1,0:T(4,128)(2,1)} %refs_0_.1), channel_id=1, source_target_pairs={{0,2},{1,3},{2,0},{3,1},{4,6},{5,7},{6,4},{7,5},{8,10},{9,11},{10,... | collective-permute-start | bytes 36872 | tf_op jit(solution)/shard_map/ppermute | solution.py:402
  3.5 0.7 copy-done.4
  5.4 3.2 %collective-permute-start.3 = (bf16[8,1536]{1,0:T(8,128)(2,1)S(1)}, bf16[8,1536]{1,0:T(8,128)(2,1)S(1)}, u32[]{:S(2)}, u32[]{:S(2)}) collective-permute-start(bf16[8,1536]{1,0:T(8,128)(2,1)S(1)} %get-tuple-element.45.refs_0_), channel_id=1, source_target_pairs={{0,8},{1,9},{2,10},{3,11},{4,12},{5,13},{6,14},{7,15},{8,0},{9,1},... | collective-permute-start | bytes 73736 | tf_op jit(solution)/shard_map/ppermute | solution.py:402
  8.6 1.3 %collective-permute-start.2 = (bf16[8,1536]{1,0:T(8,128)(2,1)S(1)}, bf16[8,1536]{1,0:T(8,128)(2,1)S(1)}, u32[]{:S(2)}, u32[]{:S(2)}) collective-permute-start(bf16[8,1536]{1,0:T(8,128)(2,1)S(1)} %get-tuple-element.45.refs_0_), channel_id=1, source_target_pairs={{0,12},{1,13},{2,14},{3,15},{4,8},{5,9},{6,10},{7,11},{8,4},{9,5},... | collective-permute-start | bytes 73736 | tf_op jit(solution)/shard_map/ppermute | solution.py:402
  10.4 3.8 %collective-permute-done.2.refs_2_ = bf16[8,1536]{1,0:T(8,128)(2,1)S(1)} collective-permute-done((bf16[8,1536]{1,0:T(8,128)(2,1)S(1)}, bf16[8,1536]{1,0:T(8,128)(2,1)S(1)}, u32[]{:S(2)}, u32[]{:S(2)}) %collective-permute-start.2) | collective-permute-done | bytes 24608 | tf_op jit(solution)/shard_map/ppermute | solution.py:402
  14.2 2.3 %project.1 = (bf16[2,144,128]{2,1,0:T(8,128)(2,1)S(1)}, bf16[2,144,128]{2,1,0:T(8,128)(2,1)S(1)}, bf16[2,144,128]{2,1,0:T(8,128)(2,1)S(1)}, bf16[2,144,128]{2,1,...) custom-call(bf16[8,1536]{1,0:T(8,128)(2,1)S(1)} %get-tuple-element.4, ...), custom_call_target="tpu_custom_call" | custom-call | flops 23000000512 | tf_op jit(solution)/shard_map/project/pallas_call | solution.py:36
  16.6 1.6 %collective-permute-start.6 = (bf16[2,144,128]{2,1,0:T(8,128)(2,1)S(1)}, bf16[2,144,128]{2,1,0:T(8,128)(2,1)S(1)}, u32[]{:S(2)}, u32[]{:S(2)}) collective-permute-start(bf16[2,144,128]{2,1,0:T(8,128)(2,1)S(1)} %get-tuple-element.47), channel_id=1, source_target_pairs={{0,2},{1,9},{2,0},{3,11},{4,6},{5,13},{6,4},{7,15},{8,10},{9,1},{1... | collective-permute-start | bytes 221192 | tf_op jit(solution)/shard_map/ppermute | solution.py:411
  18.1 2.0 %collective-permute-start.8 = (bf16[2,144,128]{2,1,0:T(8,128)(2,1)S(1)}, bf16[2,144,128]{2,1,0:T(8,128)(2,1)S(1)}, u32[]{:S(2)}, u32[]{:S(2)}) collective-permute-start(bf16[2,144,128]{2,1,0:T(8,128)(2,1)S(1)} %get-tuple-element.49), channel_id=1, source_target_pairs={{0,6},{1,13},{2,4},{3,15},{4,2},{5,9},{6,0},{7,11},{8,14},{9,5},{1... | collective-permute-start | bytes 221192 | tf_op jit(solution)/shard_map/ppermute | solution.py:411
  20.1 1.2 %collective-permute-start.9 = (bf16[2,144,128]{2,1,0:T(8,128)(2,1)S(1)}, bf16[2,144,128]{2,1,0:T(8,128)(2,1)S(1)}, u32[]{:S(2)}, u32[]{:S(2)}) collective-permute-start(bf16[2,144,128]{2,1,0:T(8,128)(2,1)S(1)} %get-tuple-element.50), channel_id=1, source_target_pairs={{0,8},{1,15},{2,10},{3,13},{4,12},{5,11},{6,14},{7,9},{8,0},{9,7},... | collective-permute-start | bytes 221192 | tf_op jit(solution)/shard_map/ppermute | solution.py:411
  21.3 2.6 %collective-permute-start.10 = (bf16[2,144,128]{2,1,0:T(8,128)(2,1)S(1)}, bf16[2,144,128]{2,1,0:T(8,128)(2,1)S(1)}, u32[]{:S(2)}, u32[]{:S(2)}) collective-permute-start(bf16[2,144,128]{2,1,0:T(8,128)(2,1)S(1)} %get-tuple-element.51), channel_id=1, source_target_pairs={{0,10},{1,3},{2,8},{3,1},{4,14},{5,7},{6,12},{7,5},{8,2},{9,11},{1... | collective-permute-start | bytes 221192 | tf_op jit(solution)/shard_map/ppermute | solution.py:411
  24.0 2.0 %collective-permute-start.11 = (bf16[2,144,128]{2,1,0:T(8,128)(2,1)S(1)}, bf16[2,144,128]{2,1,0:T(8,128)(2,1)S(1)}, u32[]{:S(2)}, u32[]{:S(2)}) collective-permute-start(bf16[2,144,128]{2,1,0:T(8,128)(2,1)S(1)} %get-tuple-element.52), channel_id=1, source_target_pairs={{0,12},{1,5},{2,14},{3,7},{4,8},{5,1},{6,10},{7,3},{8,4},{9,13},{1... | collective-permute-start | bytes 221192 | tf_op jit(solution)/shard_map/ppermute | solution.py:411
  26.0 1.8 %collective-permute-start.12 = (bf16[2,144,128]{2,1,0:T(8,128)(2,1)S(1)}, bf16[2,144,128]{2,1,0:T(8,128)(2,1)S(1)}, u32[]{:S(2)}, u32[]{:S(2)}) collective-permute-start(bf16[2,144,128]{2,1,0:T(8,128)(2,1)S(1)} %get-tuple-element.53), channel_id=1, source_target_pairs={{0,14},{1,7},{2,12},{3,5},{4,10},{5,3},{6,8},{7,1},{8,6},{9,15},{1... | collective-permute-start | bytes 221192 | tf_op jit(solution)/shard_map/ppermute | solution.py:411
  27.8 1.7 %flip.1.flip_ref = bf16[4,1536,512]{2,1,0:T(8,128)(2,1)S(1)} custom-call(bf16[4,576,1536]{2,1,0:T(8,128)(2,1)S(1)} %bitcast.5, bf16[2,144,128]{2,1,0:T(8,128)(2,1)S(1)} %get-tuple-element.46.after_ref.refs_7_), custom_call_target="tpu_custom_call" | custom-call | flops 4600000000 | tf_op jit(solution)/shard_map/flip/pallas_call | solution.py:36
  30.1 2.9 %collective-permute-done.12.refs_6_ = bf16[2,144,128]{2,1,0:T(8,128)(2,1)S(1)} collective-permute-done((bf16[2,144,128]{2,1,0:T(8,128)(2,1)S(1)}, bf16[2,144,128]{2,1,0:T(8,128)(2,1)S(1)}, u32[]{:S(2)}, u32[]{:S(2)}) %collective-permute-start.12) | collective-permute-done | bytes 73760 | tf_op jit(solution)/shard_map/ppermute | solution.py:411
  33.1 3.6 %attend.1 = (bf16[2,32,512]{2,1,0:T(8,128)(2,1)S(1)}, bf16[2,32,512]{2,1,0:T(8,128)(2,1)S(1)}, bf16[2,32,512]{2,1,0:T(8,128)(2,1)S(1)}, bf16[2,32,512]{2,1,0:T(8...) custom-call(s32[4]{0:T(128)S(1)} %copy-done.5, ...), custom_call_target="tpu_custom_call" | custom-call | flops 11500000256 | tf_op jit(solution)/shard_map/attend/pallas_call | solution.py:36
  37.2 3.0 %collective-permute-start.15 = (bf16[2,32,512]{2,1,0:T(8,128)(2,1)S(1)}, bf16[2,32,512]{2,1,0:T(8,128)(2,1)S(1)}, u32[]{:S(2)}, u32[]{:S(2)}) collective-permute-start(bf16[2,32,512]{2,1,0:T(8,128)(2,1)S(1)} %get-tuple-element.56), channel_id=1, source_target_pairs={{0,6},{1,13},{2,4},{3,15},{4,2},{5,9},{6,0},{7,11},{8,14},{9,5},{1... | collective-permute-start | bytes 196616 | tf_op jit(solution)/shard_map/ppermute | solution.py:411
  40.6 2.5 %collective-permute-start.17 = (bf16[2,32,512]{2,1,0:T(8,128)(2,1)S(1)}, bf16[2,32,512]{2,1,0:T(8,128)(2,1)S(1)}, u32[]{:S(2)}, u32[]{:S(2)}) collective-permute-start(bf16[2,32,512]{2,1,0:T(8,128)(2,1)S(1)} %get-tuple-element.58), channel_id=1, source_target_pairs={{0,10},{1,3},{2,8},{3,1},{4,14},{5,7},{6,12},{7,5},{8,2},{9,11},{1... | collective-permute-start | bytes 196616 | tf_op jit(solution)/shard_map/ppermute | solution.py:411
  43.1 1.8 %collective-permute-start.18 = (bf16[2,32,512]{2,1,0:T(8,128)(2,1)S(1)}, bf16[2,32,512]{2,1,0:T(8,128)(2,1)S(1)}, u32[]{:S(2)}, u32[]{:S(2)}) collective-permute-start(bf16[2,32,512]{2,1,0:T(8,128)(2,1)S(1)} %get-tuple-element.59), channel_id=1, source_target_pairs={{0,12},{1,5},{2,14},{3,7},{4,8},{5,1},{6,10},{7,3},{8,4},{9,13},{1... | collective-permute-start | bytes 196616 | tf_op jit(solution)/shard_map/ppermute | solution.py:411
  44.9 3.0 %collective-permute-start.19 = (bf16[2,32,512]{2,1,0:T(8,128)(2,1)S(1)}, bf16[2,32,512]{2,1,0:T(8,128)(2,1)S(1)}, u32[]{:S(2)}, u32[]{:S(2)}) collective-permute-start(bf16[2,32,512]{2,1,0:T(8,128)(2,1)S(1)} %get-tuple-element.60), channel_id=1, source_target_pairs={{0,14},{1,7},{2,12},{3,5},{4,10},{5,3},{6,8},{7,1},{8,6},{9,15},{1... | collective-permute-start | bytes 196616 | tf_op jit(solution)/shard_map/ppermute | solution.py:411
  47.9 1.4 %collective-permute-done.18.refs_5_ = bf16[2,32,512]{2,1,0:T(8,128)(2,1)S(1)} collective-permute-done((bf16[2,32,512]{2,1,0:T(8,128)(2,1)S(1)}, bf16[2,32,512]{2,1,0:T(8,128)(2,1)S(1)}, u32[]{:S(2)}, u32[]{:S(2)}) %collective-permute-start.18) | collective-permute-done | bytes 65568 | tf_op jit(solution)/shard_map/ppermute | solution.py:411
  49.2 2.6 %collective-permute-done.19.refs_6_ = bf16[2,32,512]{2,1,0:T(8,128)(2,1)S(1)} collective-permute-done((bf16[2,32,512]{2,1,0:T(8,128)(2,1)S(1)}, bf16[2,32,512]{2,1,0:T(8,128)(2,1)S(1)}, u32[]{:S(2)}, u32[]{:S(2)}) %collective-permute-start.19) | collective-permute-done | bytes 65568 | tf_op jit(solution)/shard_map/ppermute | solution.py:411
  52.0 1.5 %collective-permute-done.20.refs_8_ = bf16[8,32,512]{2,1,0:T(8,128)(2,1)S(1)} collective-permute-done((bf16[8,32,512]{2,1,0:T(8,128)(2,1)S(1)}, bf16[8,32,512]{2,1,0:T(8,128)(2,1)S(1)}, u32[]{:S(2)}, u32[]{:S(2)}) %collective-permute-start.20) | collective-permute-done | bytes 262176 | tf_op jit(solution)/shard_map/ppermute | solution.py:402
  54.0 1.4 %terms.3 = (f32[32,3584]{1,0:T(8,128)S(1)}, bf16[32,3584]{1,0:T(8,128)(2,1)S(1)}) custom-call(bf16[64,1024]{1,0:T(8,128)(2,1)S(1)} %values.1.val_ref, bf16[1024,7168]{1,0:T(8,128)(2,1)S(1)} %bitcast.2), custom_call_target="tpu_custom_call" | custom-call | flops 6899999744 | tf_op jit(solution)/shard_map/terms/pallas_call | solution.py:36
  55.6 1.4 %terms.2 = (f32[32,3584]{1,0:T(8,128)S(1)}, bf16[32,3584]{1,0:T(8,128)(2,1)S(1)}) custom-call(bf16[64,1024]{1,0:T(8,128)(2,1)S(1)} %values.1.val_ref, bf16[1024,7168]{1,0:T(8,128)(2,1)S(1)} %bitcast.2), custom_call_target="tpu_custom_call" | custom-call | flops 6899999744 | tf_op jit(solution)/shard_map/terms/pallas_call | solution.py:36
  57.5 1.6 %collective-permute-start.25 = (bf16[8,3584]{1,0:T(8,128)(2,1)S(1)}, bf16[8,3584]{1,0:T(8,128)(2,1)S(1)}, u32[]{:S(2)}, u32[]{:S(2)}) collective-permute-start(bf16[8,3584]{1,0:T(8,128)(2,1)S(1)} %get-tuple-element.73), channel_id=1, source_target_pairs={{0,2},{1,3},{2,0},{3,1},{4,6},{5,7},{6,4},{7,5},{8,10},{9,11},{10,... | collective-permute-start | bytes 172040 | tf_op jit(solution)/shard_map/ppermute | solution.py:402
  59.1 1.1 %collective-permute-start.26 = (bf16[8,3584]{1,0:T(8,128)(2,1)S(1)}, bf16[8,3584]{1,0:T(8,128)(2,1)S(1)}, u32[]{:S(2)}, u32[]{:S(2)}) collective-permute-start(bf16[8,3584]{1,0:T(8,128)(2,1)S(1)} %get-tuple-element.74), channel_id=1, source_target_pairs={{0,2},{1,3},{2,0},{3,1},{4,6},{5,7},{6,4},{7,5},{8,10},{9,11},{10,... | collective-permute-start | bytes 172040 | tf_op jit(solution)/shard_map/ppermute | solution.py:402
  60.2 1.7 %collective-permute-done.25.refs_2_ = bf16[8,3584]{1,0:T(8,128)(2,1)S(1)} collective-permute-done((bf16[8,3584]{1,0:T(8,128)(2,1)S(1)}, bf16[8,3584]{1,0:T(8,128)(2,1)S(1)}, u32[]{:S(2)}, u32[]{:S(2)}) %collective-permute-start.25) | collective-permute-done | bytes 57376 | tf_op jit(solution)/shard_map/ppermute | solution.py:402
  61.9 1.5 %collective-permute-done.26.refs_3_ = bf16[8,3584]{1,0:T(8,128)(2,1)S(1)} collective-permute-done((bf16[8,3584]{1,0:T(8,128)(2,1)S(1)}, bf16[8,3584]{1,0:T(8,128)(2,1)S(1)}, u32[]{:S(2)}, u32[]{:S(2)}) %collective-permute-start.26) | collective-permute-done | bytes 57376 | tf_op jit(solution)/shard_map/ppermute | solution.py:402
  63.5 2.1 %collective-permute-start.28 = (bf16[4,7168]{1,0:T(4,128)(2,1)S(1)}, bf16[4,7168]{1,0:T(4,128)(2,1)S(1)}, u32[]{:S(2)}, u32[]{:S(2)}) collective-permute-start(bf16[4,7168]{1,0:T(4,128)(2,1)S(1)} %get-tuple-element.76), channel_id=1, source_target_pairs={{0,12},{1,13},{2,14},{3,15},{4,8},{5,9},{6,10},{7,11},{8,4},{9,5},... | collective-permute-start | bytes 172040 | tf_op jit(solution)/shard_map/ppermute | solution.py:402
  65.6 1.2 %collective-permute-start.24 = (bf16[4,7168]{1,0:T(4,128)(2,1)S(1)}, bf16[4,7168]{1,0:T(4,128)(2,1)S(1)}, u32[]{:S(2)}, u32[]{:S(2)}) collective-permute-start(bf16[4,7168]{1,0:T(4,128)(2,1)S(1)} %get-tuple-element.70), channel_id=1, source_target_pairs={{0,2},{1,3},{2,0},{3,1},{4,6},{5,7},{6,4},{7,5},{8,10},{9,11},{10,... | collective-permute-start | bytes 172040 | tf_op jit(solution)/shard_map/ppermute | solution.py:402
  66.8 3.0 %collective-permute-done.27.refs_2_ = bf16[4,7168]{1,0:T(4,128)(2,1)S(1)} collective-permute-done((bf16[4,7168]{1,0:T(4,128)(2,1)S(1)}, bf16[4,7168]{1,0:T(4,128)(2,1)S(1)}, u32[]{:S(2)}, u32[]{:S(2)}) %collective-permute-start.27) | collective-permute-done | bytes 57376 | tf_op jit(solution)/shard_map/ppermute | solution.py:402
  69.9 0.7 last_sum.1
  (71 shorter events, 5.5 us)
Async XLA Ops:
  0.0 14.2 %collective-permute-start.4 = (bf16[1536,1536]{1,0:T(8,128)(2,1)}, bf16[1536,1536]{1,0:T(8,128)(2,1)S(1)}, u32[]{:S(2)}, u32[]{:S(2)}) collective-permute-start(bf16[1536,1536]{1,0:T(8,128)(2,1)} %refs_4_.1), channel_id=1, source_target_pairs={{0,1},{1,0},{2,3},{3,2},{4,5},{5,4},{6,7},{7,6},{8,9},{9,8},{10,11... | collective-permute-start | bytes 14155784 | tf_op jit(solution)/shard_map/ppermute | solution.py:402
  0.5 13.7 %collective-permute-start.5 = (bf16[8,128,512]{2,1,0:T(8,128)(2,1)}, bf16[8,128,512]{2,1,0:T(8,128)(2,1)S(1)}, u32[]{:S(2)}, u32[]{:S(2)}) collective-permute-start(bf16[8,128,512]{2,1,0:T(8,128)(2,1)} %refs_5_.1), channel_id=1, source_target_pairs={{0,1},{1,0},{2,3},{3,2},{4,5},{5,4},{6,7},{7,6},{8,9},{9,8},{10,11... | collective-permute-start | bytes 3145736 | tf_op jit(solution)/shard_map/ppermute | solution.py:402
  0.5 4.8 %collective-permute-start = (bf16[4,1536]{1,0:T(4,128)(2,1)}, bf16[4,1536]{1,0:T(4,128)(2,1)S(1)}, u32[]{:S(2)}, u32[]{:S(2)}) collective-permute-start(bf16[4,1536]{1,0:T(4,128)(2,1)} %refs_0_.1), channel_id=1, source_target_pairs={{0,2},{1,3},{2,0},{3,1},{4,6},{5,7},{6,4},{7,5},{8,10},{9,11},{10,... | collective-permute-start | bytes 36872 | tf_op jit(solution)/shard_map/ppermute | solution.py:402
  5.4 22.4 %slice-start.4 = ((s8[7077888]{0:T(1024)(128)(4,1)}), s8[4194304]{0:T(1024)(128)(4,1)S(1)}, s32[]{:S(2)}) async-start(s8[7077888]{0:T(1024)(128)(4,1)} %bitcast.3), calls=%async_computation.4 | async-start | bytes 8388608
  5.4 22.4 %slice-start.5 = ((s8[7077888]{0:T(1024)(128)(4,1)}), s8[2883584]{0:T(1024)(128)(4,1)S(1)}, s32[]{:S(2)}) async-start(s8[7077888]{0:T(1024)(128)(4,1)} %bitcast.3), calls=%async_computation.5 | async-start | bytes 5767168
  5.4 5.0 %collective-permute-start.3 = (bf16[8,1536]{1,0:T(8,128)(2,1)S(1)}, bf16[8,1536]{1,0:T(8,128)(2,1)S(1)}, u32[]{:S(2)}, u32[]{:S(2)}) collective-permute-start(bf16[8,1536]{1,0:T(8,128)(2,1)S(1)} %get-tuple-element.45.refs_0_), channel_id=1, source_target_pairs={{0,8},{1,9},{2,10},{3,11},{4,12},{5,13},{6,14},{7,15},{8,0},{9,1},... | collective-permute-start | bytes 73736 | tf_op jit(solution)/shard_map/ppermute | solution.py:402
  8.6 5.6 %collective-permute-start.2 = (bf16[8,1536]{1,0:T(8,128)(2,1)S(1)}, bf16[8,1536]{1,0:T(8,128)(2,1)S(1)}, u32[]{:S(2)}, u32[]{:S(2)}) collective-permute-start(bf16[8,1536]{1,0:T(8,128)(2,1)S(1)} %get-tuple-element.45.refs_0_), channel_id=1, source_target_pairs={{0,12},{1,13},{2,14},{3,15},{4,8},{5,9},{6,10},{7,11},{8,4},{9,5},... | collective-permute-start | bytes 73736 | tf_op jit(solution)/shard_map/ppermute | solution.py:402
  9.9 4.3 %collective-permute-start.1 = (bf16[8,1536]{1,0:T(8,128)(2,1)S(1)}, bf16[8,1536]{1,0:T(8,128)(2,1)S(1)}, u32[]{:S(2)}, u32[]{:S(2)}) collective-permute-start(bf16[8,1536]{1,0:T(8,128)(2,1)S(1)} %get-tuple-element.45.refs_0_), channel_id=1, source_target_pairs={{0,4},{1,5},{2,6},{3,7},{4,0},{5,1},{6,2},{7,3},{8,12},{9,13},{10,... | collective-permute-start | bytes 73736 | tf_op jit(solution)/shard_map/ppermute | solution.py:402
  16.6 7.4 %collective-permute-start.6 = (bf16[2,144,128]{2,1,0:T(8,128)(2,1)S(1)}, bf16[2,144,128]{2,1,0:T(8,128)(2,1)S(1)}, u32[]{:S(2)}, u32[]{:S(2)}) collective-permute-start(bf16[2,144,128]{2,1,0:T(8,128)(2,1)S(1)} %get-tuple-element.47), channel_id=1, source_target_pairs={{0,2},{1,9},{2,0},{3,11},{4,6},{5,13},{6,4},{7,15},{8,10},{9,1},{1... | collective-permute-start | bytes 221192 | tf_op jit(solution)/shard_map/ppermute | solution.py:411
  18.1 7.9 %collective-permute-start.7 = (bf16[2,144,128]{2,1,0:T(8,128)(2,1)S(1)}, bf16[2,144,128]{2,1,0:T(8,128)(2,1)S(1)}, u32[]{:S(2)}, u32[]{:S(2)}) collective-permute-start(bf16[2,144,128]{2,1,0:T(8,128)(2,1)S(1)} %get-tuple-element.48), channel_id=1, source_target_pairs={{0,4},{1,11},{2,6},{3,9},{4,0},{5,15},{6,2},{7,13},{8,12},{9,3},{1... | collective-permute-start | bytes 221192 | tf_op jit(solution)/shard_map/ppermute | solution.py:411
  18.1 11.3 %collective-permute-start.8 = (bf16[2,144,128]{2,1,0:T(8,128)(2,1)S(1)}, bf16[2,144,128]{2,1,0:T(8,128)(2,1)S(1)}, u32[]{:S(2)}, u32[]{:S(2)}) collective-permute-start(bf16[2,144,128]{2,1,0:T(8,128)(2,1)S(1)} %get-tuple-element.49), channel_id=1, source_target_pairs={{0,6},{1,13},{2,4},{3,15},{4,2},{5,9},{6,0},{7,11},{8,14},{9,5},{1... | collective-permute-start | bytes 221192 | tf_op jit(solution)/shard_map/ppermute | solution.py:411
  20.1 9.4 %collective-permute-start.9 = (bf16[2,144,128]{2,1,0:T(8,128)(2,1)S(1)}, bf16[2,144,128]{2,1,0:T(8,128)(2,1)S(1)}, u32[]{:S(2)}, u32[]{:S(2)}) collective-permute-start(bf16[2,144,128]{2,1,0:T(8,128)(2,1)S(1)} %get-tuple-element.50), channel_id=1, source_target_pairs={{0,8},{1,15},{2,10},{3,13},{4,12},{5,11},{6,14},{7,9},{8,0},{9,7},... | collective-permute-start | bytes 221192 | tf_op jit(solution)/shard_map/ppermute | solution.py:411
  21.3 8.1 %collective-permute-start.10 = (bf16[2,144,128]{2,1,0:T(8,128)(2,1)S(1)}, bf16[2,144,128]{2,1,0:T(8,128)(2,1)S(1)}, u32[]{:S(2)}, u32[]{:S(2)}) collective-permute-start(bf16[2,144,128]{2,1,0:T(8,128)(2,1)S(1)} %get-tuple-element.51), channel_id=1, source_target_pairs={{0,10},{1,3},{2,8},{3,1},{4,14},{5,7},{6,12},{7,5},{8,2},{9,11},{1... | collective-permute-start | bytes 221192 | tf_op jit(solution)/shard_map/ppermute | solution.py:411
  24.0 6.2 %collective-permute-start.11 = (bf16[2,144,128]{2,1,0:T(8,128)(2,1)S(1)}, bf16[2,144,128]{2,1,0:T(8,128)(2,1)S(1)}, u32[]{:S(2)}, u32[]{:S(2)}) collective-permute-start(bf16[2,144,128]{2,1,0:T(8,128)(2,1)S(1)} %get-tuple-element.52), channel_id=1, source_target_pairs={{0,12},{1,5},{2,14},{3,7},{4,8},{5,1},{6,10},{7,3},{8,4},{9,13},{1... | collective-permute-start | bytes 221192 | tf_op jit(solution)/shard_map/ppermute | solution.py:411
  26.0 7.1 %collective-permute-start.12 = (bf16[2,144,128]{2,1,0:T(8,128)(2,1)S(1)}, bf16[2,144,128]{2,1,0:T(8,128)(2,1)S(1)}, u32[]{:S(2)}, u32[]{:S(2)}) collective-permute-start(bf16[2,144,128]{2,1,0:T(8,128)(2,1)S(1)} %get-tuple-element.53), channel_id=1, source_target_pairs={{0,14},{1,7},{2,12},{3,5},{4,10},{5,3},{6,8},{7,1},{8,6},{9,15},{1... | collective-permute-start | bytes 221192 | tf_op jit(solution)/shard_map/ppermute | solution.py:411
  33.1 20.9 %slice-start.1 = ((s8[14680064]{0:T(1024)(128)(4,1)}), s8[4194304]{0:T(1024)(128)(4,1)S(1)}, s32[]{:S(2)}) async-start(s8[14680064]{0:T(1024)(128)(4,1)} %bitcast.1), calls=%async_computation.1 | async-start | bytes 8388608
  36.7 6.4 %collective-permute-start.13 = (bf16[2,32,512]{2,1,0:T(8,128)(2,1)S(1)}, bf16[2,32,512]{2,1,0:T(8,128)(2,1)S(1)}, u32[]{:S(2)}, u32[]{:S(2)}) collective-permute-start(bf16[2,32,512]{2,1,0:T(8,128)(2,1)S(1)} %get-tuple-element.54), channel_id=1, source_target_pairs={{0,2},{1,9},{2,0},{3,11},{4,6},{5,13},{6,4},{7,15},{8,10},{9,1},{1... | collective-permute-start | bytes 196616 | tf_op jit(solution)/shard_map/ppermute | solution.py:411
  37.2 7.7 %collective-permute-start.14 = (bf16[2,32,512]{2,1,0:T(8,128)(2,1)S(1)}, bf16[2,32,512]{2,1,0:T(8,128)(2,1)S(1)}, u32[]{:S(2)}, u32[]{:S(2)}) collective-permute-start(bf16[2,32,512]{2,1,0:T(8,128)(2,1)S(1)} %get-tuple-element.55), channel_id=1, source_target_pairs={{0,4},{1,11},{2,6},{3,9},{4,0},{5,15},{6,2},{7,13},{8,12},{9,3},{1... | collective-permute-start | bytes 196616 | tf_op jit(solution)/shard_map/ppermute | solution.py:411
  37.2 10.6 %collective-permute-start.15 = (bf16[2,32,512]{2,1,0:T(8,128)(2,1)S(1)}, bf16[2,32,512]{2,1,0:T(8,128)(2,1)S(1)}, u32[]{:S(2)}, u32[]{:S(2)}) collective-permute-start(bf16[2,32,512]{2,1,0:T(8,128)(2,1)S(1)} %get-tuple-element.56), channel_id=1, source_target_pairs={{0,6},{1,13},{2,4},{3,15},{4,2},{5,9},{6,0},{7,11},{8,14},{9,5},{1... | collective-permute-start | bytes 196616 | tf_op jit(solution)/shard_map/ppermute | solution.py:411
  40.2 7.7 %collective-permute-start.16 = (bf16[2,32,512]{2,1,0:T(8,128)(2,1)S(1)}, bf16[2,32,512]{2,1,0:T(8,128)(2,1)S(1)}, u32[]{:S(2)}, u32[]{:S(2)}) collective-permute-start(bf16[2,32,512]{2,1,0:T(8,128)(2,1)S(1)} %get-tuple-element.57), channel_id=1, source_target_pairs={{0,8},{1,15},{2,10},{3,13},{4,12},{5,11},{6,14},{7,9},{8,0},{9,7},... | collective-permute-start | bytes 196616 | tf_op jit(solution)/shard_map/ppermute | solution.py:411
  40.6 7.3 %collective-permute-start.17 = (bf16[2,32,512]{2,1,0:T(8,128)(2,1)S(1)}, bf16[2,32,512]{2,1,0:T(8,128)(2,1)S(1)}, u32[]{:S(2)}, u32[]{:S(2)}) collective-permute-start(bf16[2,32,512]{2,1,0:T(8,128)(2,1)S(1)} %get-tuple-element.58), channel_id=1, source_target_pairs={{0,10},{1,3},{2,8},{3,1},{4,14},{5,7},{6,12},{7,5},{8,2},{9,11},{1... | collective-permute-start | bytes 196616 | tf_op jit(solution)/shard_map/ppermute | solution.py:411
  43.1 6.2 %collective-permute-start.18 = (bf16[2,32,512]{2,1,0:T(8,128)(2,1)S(1)}, bf16[2,32,512]{2,1,0:T(8,128)(2,1)S(1)}, u32[]{:S(2)}, u32[]{:S(2)}) collective-permute-start(bf16[2,32,512]{2,1,0:T(8,128)(2,1)S(1)} %get-tuple-element.59), channel_id=1, source_target_pairs={{0,12},{1,5},{2,14},{3,7},{4,8},{5,1},{6,10},{7,3},{8,4},{9,13},{1... | collective-permute-start | bytes 196616 | tf_op jit(solution)/shard_map/ppermute | solution.py:411
  44.9 7.0 %collective-permute-start.19 = (bf16[2,32,512]{2,1,0:T(8,128)(2,1)S(1)}, bf16[2,32,512]{2,1,0:T(8,128)(2,1)S(1)}, u32[]{:S(2)}, u32[]{:S(2)}) collective-permute-start(bf16[2,32,512]{2,1,0:T(8,128)(2,1)S(1)} %get-tuple-element.60), channel_id=1, source_target_pairs={{0,14},{1,7},{2,12},{3,5},{4,10},{5,3},{6,8},{7,1},{8,6},{9,15},{1... | collective-permute-start | bytes 196616 | tf_op jit(solution)/shard_map/ppermute | solution.py:411
  51.9 1.6 %collective-permute-start.20 = (bf16[8,32,512]{2,1,0:T(8,128)(2,1)S(1)}, bf16[8,32,512]{2,1,0:T(8,128)(2,1)S(1)}, u32[]{:S(2)}, u32[]{:S(2)}) collective-permute-start(bf16[8,32,512]{2,1,0:T(8,128)(2,1)S(1)} %regroup.1), channel_id=1, source_target_pairs={{0,1},{1,0},{2,3},{3,2},{4,5},{5,4},{6,7},{7,6},{8,9},{9,8},{10,11... | collective-permute-start | bytes 786440 | tf_op jit(solution)/shard_map/ppermute | solution.py:402
  55.4 2.0 %collective-permute-start.22 = (bf16[32,3584]{1,0:T(8,128)(2,1)S(1)}, bf16[32,3584]{1,0:T(8,128)(2,1)S(1)}, u32[]{:S(2)}, u32[]{:S(2)}) collective-permute-start(bf16[32,3584]{1,0:T(8,128)(2,1)S(1)} %get-tuple-element.65), channel_id=1, source_target_pairs={{0,1},{1,0},{2,3},{3,2},{4,5},{5,4},{6,7},{7,6},{8,9},{9,8},{10,11... | collective-permute-start | bytes 688136 | tf_op jit(solution)/shard_map/ppermute | solution.py:402
  57.0 2.1 %collective-permute-start.21 = (bf16[32,3584]{1,0:T(8,128)(2,1)S(1)}, bf16[32,3584]{1,0:T(8,128)(2,1)S(1)}, u32[]{:S(2)}, u32[]{:S(2)}) collective-permute-start(bf16[32,3584]{1,0:T(8,128)(2,1)S(1)} %get-tuple-element.63), channel_id=1, source_target_pairs={{0,1},{1,0},{2,3},{3,2},{4,5},{5,4},{6,7},{7,6},{8,9},{9,8},{10,11... | collective-permute-start | bytes 688136 | tf_op jit(solution)/shard_map/ppermute | solution.py:402
  57.5 4.4 %collective-permute-start.25 = (bf16[8,3584]{1,0:T(8,128)(2,1)S(1)}, bf16[8,3584]{1,0:T(8,128)(2,1)S(1)}, u32[]{:S(2)}, u32[]{:S(2)}) collective-permute-start(bf16[8,3584]{1,0:T(8,128)(2,1)S(1)} %get-tuple-element.73), channel_id=1, source_target_pairs={{0,2},{1,3},{2,0},{3,1},{4,6},{5,7},{6,4},{7,5},{8,10},{9,11},{10,... | collective-permute-start | bytes 172040 | tf_op jit(solution)/shard_map/ppermute | solution.py:402
  59.1 4.2 %collective-permute-start.26 = (bf16[8,3584]{1,0:T(8,128)(2,1)S(1)}, bf16[8,3584]{1,0:T(8,128)(2,1)S(1)}, u32[]{:S(2)}, u32[]{:S(2)}) collective-permute-start(bf16[8,3584]{1,0:T(8,128)(2,1)S(1)} %get-tuple-element.74), channel_id=1, source_target_pairs={{0,2},{1,3},{2,0},{3,1},{4,6},{5,7},{6,4},{7,5},{8,10},{9,11},{10,... | collective-permute-start | bytes 172040 | tf_op jit(solution)/shard_map/ppermute | solution.py:402
  60.2 5.4 %collective-permute-start.23 = (bf16[8,7168]{1,0:T(8,128)(2,1)S(1)}, bf16[8,7168]{1,0:T(8,128)(2,1)S(1)}, u32[]{:S(2)}, u32[]{:S(2)}) collective-permute-start(bf16[8,7168]{1,0:T(8,128)(2,1)S(1)} %get-tuple-element.68), channel_id=1, source_target_pairs={{0,4},{1,5},{2,6},{3,7},{4,0},{5,1},{6,2},{7,3},{8,12},{9,13},{10,... | collective-permute-start | bytes 344072 | tf_op jit(solution)/shard_map/ppermute | solution.py:402
  63.4 6.4 %collective-permute-start.27 = (bf16[4,7168]{1,0:T(4,128)(2,1)S(1)}, bf16[4,7168]{1,0:T(4,128)(2,1)S(1)}, u32[]{:S(2)}, u32[]{:S(2)}) collective-permute-start(bf16[4,7168]{1,0:T(4,128)(2,1)S(1)} %get-tuple-element.75), channel_id=1, source_target_pairs={{0,8},{1,9},{2,10},{3,11},{4,12},{5,13},{6,14},{7,15},{8,0},{9,1},... | collective-permute-start | bytes 172040 | tf_op jit(solution)/shard_map/ppermute | solution.py:402
  63.5 6.3 %collective-permute-start.28 = (bf16[4,7168]{1,0:T(4,128)(2,1)S(1)}, bf16[4,7168]{1,0:T(4,128)(2,1)S(1)}, u32[]{:S(2)}, u32[]{:S(2)}) collective-permute-start(bf16[4,7168]{1,0:T(4,128)(2,1)S(1)} %get-tuple-element.76), channel_id=1, source_target_pairs={{0,12},{1,13},{2,14},{3,15},{4,8},{5,9},{6,10},{7,11},{8,4},{9,5},... | collective-permute-start | bytes 172040 | tf_op jit(solution)/shard_map/ppermute | solution.py:402
  65.6 4.2 %collective-permute-start.24 = (bf16[4,7168]{1,0:T(4,128)(2,1)S(1)}, bf16[4,7168]{1,0:T(4,128)(2,1)S(1)}, u32[]{:S(2)}, u32[]{:S(2)}) collective-permute-start(bf16[4,7168]{1,0:T(4,128)(2,1)S(1)} %get-tuple-element.70), channel_id=1, source_target_pairs={{0,2},{1,3},{2,0},{3,1},{4,6},{5,7},{6,4},{7,5},{8,10},{9,11},{10,... | collective-permute-start | bytes 172040 | tf_op jit(solution)/shard_map/ppermute | solution.py:402
  (11 other events, 108.8 us)

commit v13 on v11

--- a/solution.py
+++ b/solution.py
@@ -20,6 +20,7 @@
 PARTS = 2
 Y = 2
 Z1 = 4
+NEAR = (Z1, Y + Z1, Y)
 
 
 def resident(x):
@@ -58,7 +59,8 @@
 
 
 def far_chips(devices):
-    return [k for k in far_first(devices, 2) if k > Y + Z1]
+    chips = [k for k in far_first(devices, 2) if k > Y + Z1]
+    return chips[:1] + chips[:0:-1]
 
 
 def chip_order(devices):
@@ -324,7 +326,7 @@
 
 
 def far_z(devices):
-    return [z for z in far_first(devices, Z1) if z > Z1]
+    return [z for z in far_first(devices, Z1) if z > Z1][::-1]
 
 
 def places(devices, chips):
@@ -344,22 +346,21 @@
 
 
 def last_part_kernel(rows, keep, give, near, mine_ref, other_ref, before_ref, *out_refs):
-    keep_ref, give_ref, local_ref, pair_ref = out_refs
+    keep_ref, give_ref, *near_refs = out_refs
     total = mine_ref[...] + other_ref[...].astype(jnp.float32)
     keep_ref[...] = pick(total, rows, keep)
     give_ref[...] = pick(total, rows, give).astype(give_ref.dtype)
-    here = pick(total, rows, near)
-    half, width = local_ref.shape[0], before_ref.shape[1]
-    for columns, block in ((slice(0, width), before_ref[...]), (slice(width, None), here)):
-        local_ref[:, columns] = block[:half]
-        pair_ref[:, columns] = block[half:].astype(pair_ref.dtype)
+    width = before_ref.shape[1]
+    for i, (j, out_ref) in enumerate(zip(near, near_refs)):
+        out_ref[:, :width] = before_ref[i * rows : (i + 1) * rows].astype(out_ref.dtype)
+        out_ref[:, width:] = total[j * rows : (j + 1) * rows].astype(out_ref.dtype)
 
 
 def core_sum(mine, other, before, rows, devices):
     count, width = mine.shape
     keep = places(devices, far_z(devices))
     give = places(devices, [z + Y for z in far_z(devices)])
-    near = places(devices, [0, Y, Z1, Z1 + Y])
+    near = places(devices, [0, *NEAR])
     far = len(keep) * rows
     out = (shape(far, width, dtype=jnp.float32), shape(far, width))
     if before is None:
@@ -368,7 +369,7 @@
         return call(kernel, out, 1, "core_sum")(mine, other)
     kernel = functools.partial(last_part_kernel, rows, keep, give, near)
     full = before.shape[1] + width
-    out += (shape(2 * rows, full, dtype=jnp.float32), shape(2 * rows, full))
+    out += (shape(rows, full, dtype=jnp.float32), *[shape(rows, full)] * len(NEAR))
     return call(kernel, out, 1, "core_sum")(mine, other, before)
 
 
@@ -392,19 +393,6 @@
     return call(far_sum_kernel, out, 1, "far_sum")(*mine, *other)
 
 
-def near_sum_kernel(mine_ref, other_ref, keep_ref, give_ref):
-    total = mine_ref[...] + other_ref[...].astype(jnp.float32)
-    rows = keep_ref.shape[0]
-    keep_ref[...] = total[:rows]
-    give_ref[...] = total[rows:].astype(give_ref.dtype)
-
-
-def near_sum(mine, other):
-    rows, width = mine.shape[0] // 2, mine.shape[1]
-    out = (shape(rows, width, dtype=jnp.float32), shape(rows, width))
-    return call(near_sum_kernel, out, 1, "near_sum")(mine, other)
-
-
 def last_sum_kernel(*refs):
     *in_refs, out_ref = refs
     terms = [ref[...].astype(jnp.float32) for ref in in_refs]
@@ -449,13 +437,13 @@
     keep, got, near = [], [], None
     for part in range(PARTS):
         mine, other = output_terms(values, w_o, part)
-        far_mine, far_other, near, *pair = core_sum(mine, swap(other, 1), near, rows, devices)
+        far_mine, far_other, near, *given = core_sum(mine, swap(other, 1), near, rows, devices)
         keep.append(far_mine)
         got.append(swap(far_other, Y))
-    local, across = near_sum(near, swap(pair[0], Z1))
+    given = [swap(block, k) for block, k in zip(given, NEAR)]
     far = far_sum(keep, got, rows)
     far = [swap(block, z) for z, block in zip(far_z(devices), far)]
-    return last_sum([local, swap(across, Y), *far])
+    return last_sum([near, *given, *far])
 
 
 def solution(mesh):

time: 70 us -> 70.1 us (level)
  waiting for transfers between devices: 21.1 us -> 22.6 us
  starting transfers between devices: 35.5 us -> 34.2 us
    ppermute x27 -> x28, waiting for transfers between devices: 21.1 us -> 22.6 us  [swap(): return lax.ppermute(block, 'row', [(i, i ^ k) for i in range(devices)])]
    ppermute x27 -> x28, starting transfers between devices: 35.5 us -> 34.2 us  [swap(): return lax.ppermute(block, 'row', [(i, i ^ k) for i in range(devices)])]
    pallas_call x17 -> x16, Pallas kernels: 12.2 us -> 12.2 us  [run(): pl.pallas_call(kernel, out_shape=out_shape, in_specs=smem + [in_vmem()] *...]
  transfers between devices with their start and end apart: 27 -> 28, of which waited for: 15 -> 12; matrix products, arithmetic and copies ran while one was open for 0% -> 0% of each run, Pallas kernels for 6% -> 6%
where the time goes in v13:
time: 70.1 us; the launch traced here: 70 us
  starting transfers between devices  34.2 us (49%)
  waiting for transfers between devices  22.6 us (32%)
  Pallas kernels  12.2 us (17%)
  local copies, waits for them, and re-layouts  0.72 us (1%)
    ppermute x28, starting transfers between devices, swap(): return lax.ppermute(block, 'row', [(i, i ^ k) for i in range(devices)])  34.2 us
    ppermute x28, waiting for transfers between devices, swap(): return lax.ppermute(block, 'row', [(i, i ^ k) for i in range(devices)])  22.6 us
    pallas_call x16, Pallas kernels, run(): pl.pallas_call(kernel, out_shape=out_shape, in_specs=smem + [in_vmem()] *...  12.2 us
  transfers between devices with their start and end apart: 28, of which 12 were waited for; matrix products, arithmetic and copies ran while one was open for 0% of the time, Pallas kernels for 6%

profile of v13, /device:TPU:0, one launch (start us, length us, event | category | flops | bytes accessed | tf_op | source)
XLA Modules:
  0.0 70.0 jit_solution(15305375085906257750)
XLA Ops:
  0.5 3.0 %collective-permute-start = (bf16[4,1536]{1,0:T(4,128)(2,1)}, bf16[4,1536]{1,0:T(4,128)(2,1)S(1)}, u32[]{:S(2)}, u32[]{:S(2)}) collective-permute-start(bf16[4,1536]{1,0:T(4,128)(2,1)} %refs_0_.1), channel_id=1, source_target_pairs={{0,2},{1,3},{2,0},{3,1},{4,6},{5,7},{6,4},{7,5},{8,10},{9,11},{10,... | collective-permute-start | bytes 36872 | tf_op jit(solution)/shard_map/ppermute | solution.py:414
  5.4 3.2 %collective-permute-start.3 = (bf16[8,1536]{1,0:T(8,128)(2,1)S(1)}, bf16[8,1536]{1,0:T(8,128)(2,1)S(1)}, u32[]{:S(2)}, u32[]{:S(2)}) collective-permute-start(bf16[8,1536]{1,0:T(8,128)(2,1)S(1)} %get-tuple-element.43.refs_0_), channel_id=1, source_target_pairs={{0,8},{1,9},{2,10},{3,11},{4,12},{5,13},{6,14},{7,15},{8,0},{9,1},... | collective-permute-start | bytes 73736 | tf_op jit(solution)/shard_map/ppermute | solution.py:414
  8.6 1.3 %collective-permute-start.2 = (bf16[8,1536]{1,0:T(8,128)(2,1)S(1)}, bf16[8,1536]{1,0:T(8,128)(2,1)S(1)}, u32[]{:S(2)}, u32[]{:S(2)}) collective-permute-start(bf16[8,1536]{1,0:T(8,128)(2,1)S(1)} %get-tuple-element.43.refs_0_), channel_id=1, source_target_pairs={{0,12},{1,13},{2,14},{3,15},{4,8},{5,9},{6,10},{7,11},{8,4},{9,5},... | collective-permute-start | bytes 73736 | tf_op jit(solution)/shard_map/ppermute | solution.py:414
  10.4 3.8 %collective-permute-done.2.refs_2_ = bf16[8,1536]{1,0:T(8,128)(2,1)S(1)} collective-permute-done((bf16[8,1536]{1,0:T(8,128)(2,1)S(1)}, bf16[8,1536]{1,0:T(8,128)(2,1)S(1)}, u32[]{:S(2)}, u32[]{:S(2)}) %collective-permute-start.2) | collective-permute-done | bytes 24608 | tf_op jit(solution)/shard_map/ppermute | solution.py:414
  14.2 2.3 %project.1 = (bf16[2,144,128]{2,1,0:T(8,128)(2,1)S(1)}, bf16[2,144,128]{2,1,0:T(8,128)(2,1)S(1)}, bf16[2,144,128]{2,1,0:T(8,128)(2,1)S(1)}, bf16[2,144,128]{2,1,...) custom-call(bf16[8,1536]{1,0:T(8,128)(2,1)S(1)} %get-tuple-element.4, ...), custom_call_target="tpu_custom_call" | custom-call | flops 23000000512 | tf_op jit(solution)/shard_map/project/pallas_call | solution.py:37
  16.5 1.6 %collective-permute-start.6 = (bf16[4,144,128]{2,1,0:T(8,128)(2,1)S(1)}, bf16[4,144,128]{2,1,0:T(8,128)(2,1)S(1)}, u32[]{:S(2)}, u32[]{:S(2)}) collective-permute-start(bf16[4,144,128]{2,1,0:T(8,128)(2,1)S(1)} %get-tuple-element.45), channel_id=1, source_target_pairs={{0,2},{1,3},{2,0},{3,1},{4,6},{5,7},{6,4},{7,5},{8,10},{9,11},{10,... | collective-permute-start | bytes 442376 | tf_op jit(solution)/shard_map/ppermute | solution.py:414
  18.1 1.2 %collective-permute-start.7 = (bf16[2,144,128]{2,1,0:T(8,128)(2,1)S(1)}, bf16[2,144,128]{2,1,0:T(8,128)(2,1)S(1)}, u32[]{:S(2)}, u32[]{:S(2)}) collective-permute-start(bf16[2,144,128]{2,1,0:T(8,128)(2,1)S(1)} %get-tuple-element.46), channel_id=1, source_target_pairs={{0,8},{1,9},{2,10},{3,11},{4,12},{5,13},{6,14},{7,15},{8,0},{9,1},... | collective-permute-start | bytes 221192 | tf_op jit(solution)/shard_map/ppermute | solution.py:414
  19.4 0.9 %collective-permute-start.8 = (bf16[2,144,128]{2,1,0:T(8,128)(2,1)S(1)}, bf16[2,144,128]{2,1,0:T(8,128)(2,1)S(1)}, u32[]{:S(2)}, u32[]{:S(2)}) collective-permute-start(bf16[2,144,128]{2,1,0:T(8,128)(2,1)S(1)} %get-tuple-element.47), channel_id=1, source_target_pairs={{0,14},{1,15},{2,12},{3,13},{4,10},{5,11},{6,8},{7,9},{8,6},{9,7},... | collective-permute-start | bytes 221192 | tf_op jit(solution)/shard_map/ppermute | solution.py:414
  20.2 2.9 %collective-permute-start.9 = (bf16[2,144,128]{2,1,0:T(8,128)(2,1)S(1)}, bf16[2,144,128]{2,1,0:T(8,128)(2,1)S(1)}, u32[]{:S(2)}, u32[]{:S(2)}) collective-permute-start(bf16[2,144,128]{2,1,0:T(8,128)(2,1)S(1)} %get-tuple-element.48), channel_id=1, source_target_pairs={{0,12},{1,13},{2,14},{3,15},{4,8},{5,9},{6,10},{7,11},{8,4},{9,5},... | collective-permute-start | bytes 221192 | tf_op jit(solution)/shard_map/ppermute | solution.py:414
  23.1 0.8 %collective-permute-start.10 = (bf16[2,144,128]{2,1,0:T(8,128)(2,1)S(1)}, bf16[2,144,128]{2,1,0:T(8,128)(2,1)S(1)}, u32[]{:S(2)}, u32[]{:S(2)}) collective-permute-start(bf16[2,144,128]{2,1,0:T(8,128)(2,1)S(1)} %get-tuple-element.49), channel_id=1, source_target_pairs={{0,10},{1,11},{2,8},{3,9},{4,14},{5,15},{6,12},{7,13},{8,2},{9,3},... | collective-permute-start | bytes 221192 | tf_op jit(solution)/shard_map/ppermute | solution.py:414
  24.0 1.7 %collective-permute-start.11 = (bf16[4,144,128]{2,1,0:T(8,128)(2,1)S(1)}, bf16[4,144,128]{2,1,0:T(8,128)(2,1)S(1)}, u32[]{:S(2)}, u32[]{:S(2)}) collective-permute-start(bf16[4,144,128]{2,1,0:T(8,128)(2,1)S(1)} %forward.2.after_ref), channel_id=1, source_target_pairs={{0,4},{1,5},{2,6},{3,7},{4,0},{5,1},{6,2},{7,3},{8,12},{9,13},{10,... | collective-permute-start | bytes 442376 | tf_op jit(solution)/shard_map/ppermute | solution.py:414
  25.7 1.7 %flip.1.flip_ref = bf16[4,1536,512]{2,1,0:T(8,128)(2,1)S(1)} custom-call(bf16[4,576,1536]{2,1,0:T(8,128)(2,1)S(1)} %bitcast.5, bf16[4,144,128]{2,1,0:T(8,128)(2,1)S(1)} %forward.2.after_ref), custom_call_target="tpu_custom_call" | custom-call | flops 4600000000 | tf_op jit(solution)/shard_map/flip/pallas_call | solution.py:37
  27.4 0.9 %collective-permute-done.7.refs_0_ = bf16[2,144,128]{2,1,0:T(8,128)(2,1)S(1)} collective-permute-done((bf16[2,144,128]{2,1,0:T(8,128)(2,1)S(1)}, bf16[2,144,128]{2,1,0:T(8,128)(2,1)S(1)}, u32[]{:S(2)}, u32[]{:S(2)}) %collective-permute-start.7) | collective-permute-done | bytes 73760 | tf_op jit(solution)/shard_map/ppermute | solution.py:414
  28.3 4.4 %collective-permute-done.10.refs_3_ = bf16[2,144,128]{2,1,0:T(8,128)(2,1)S(1)} collective-permute-done((bf16[2,144,128]{2,1,0:T(8,128)(2,1)S(1)}, bf16[2,144,128]{2,1,0:T(8,128)(2,1)S(1)}, u32[]{:S(2)}, u32[]{:S(2)}) %collective-permute-start.10) | collective-permute-done | bytes 73760 | tf_op jit(solution)/shard_map/ppermute | solution.py:414
  32.7 3.4 %attend.1 = (bf16[2,32,512]{2,1,0:T(8,128)(2,1)S(1)}, bf16[2,32,512]{2,1,0:T(8,128)(2,1)S(1)}, bf16[2,32,512]{2,1,0:T(8,128)(2,1)S(1)}, bf16[2,32,512]{2,1,0:T(8...) custom-call(s32[4]{0:T(128)S(1)} %copy-done.5, ...), custom_call_target="tpu_custom_call" | custom-call | flops 11500000256 | tf_op jit(solution)/shard_map/attend/pallas_call | solution.py:37
  36.8 2.6 %collective-permute-start.13 = (bf16[2,32,512]{2,1,0:T(8,128)(2,1)S(1)}, bf16[2,32,512]{2,1,0:T(8,128)(2,1)S(1)}, u32[]{:S(2)}, u32[]{:S(2)}) collective-permute-start(bf16[2,32,512]{2,1,0:T(8,128)(2,1)S(1)} %get-tuple-element.52), channel_id=1, source_target_pairs={{0,14},{1,15},{2,12},{3,13},{4,10},{5,11},{6,8},{7,9},{8,6},{9,7},... | collective-permute-start | bytes 196616 | tf_op jit(solution)/shard_map/ppermute | solution.py:414
  39.4 2.2 %collective-permute-start.14 = (bf16[2,32,512]{2,1,0:T(8,128)(2,1)S(1)}, bf16[2,32,512]{2,1,0:T(8,128)(2,1)S(1)}, u32[]{:S(2)}, u32[]{:S(2)}) collective-permute-start(bf16[2,32,512]{2,1,0:T(8,128)(2,1)S(1)} %get-tuple-element.53), channel_id=1, source_target_pairs={{0,12},{1,13},{2,14},{3,15},{4,8},{5,9},{6,10},{7,11},{8,4},{9,5},... | collective-permute-start | bytes 196616 | tf_op jit(solution)/shard_map/ppermute | solution.py:414
  41.6 1.0 %collective-permute-start.15 = (bf16[2,32,512]{2,1,0:T(8,128)(2,1)S(1)}, bf16[2,32,512]{2,1,0:T(8,128)(2,1)S(1)}, u32[]{:S(2)}, u32[]{:S(2)}) collective-permute-start(bf16[2,32,512]{2,1,0:T(8,128)(2,1)S(1)} %get-tuple-element.54), channel_id=1, source_target_pairs={{0,10},{1,11},{2,8},{3,9},{4,14},{5,15},{6,12},{7,13},{8,2},{9,3},... | collective-permute-start | bytes 196616 | tf_op jit(solution)/shard_map/ppermute | solution.py:414
  42.6 2.2 %collective-permute-start.17 = (bf16[4,32,512]{2,1,0:T(8,128)(2,1)S(1)}, bf16[4,32,512]{2,1,0:T(8,128)(2,1)S(1)}, u32[]{:S(2)}, u32[]{:S(2)}) collective-permute-start(bf16[4,32,512]{2,1,0:T(8,128)(2,1)S(1)} %forward.3.after_ref), channel_id=1, source_target_pairs={{0,4},{1,5},{2,6},{3,7},{4,0},{5,1},{6,2},{7,3},{8,12},{9,13},{10,... | collective-permute-start | bytes 393224 | tf_op jit(solution)/shard_map/ppermute | solution.py:414
  44.8 1.4 %collective-permute-done.12.refs_0_ = bf16[2,32,512]{2,1,0:T(8,128)(2,1)S(1)} collective-permute-done((bf16[2,32,512]{2,1,0:T(8,128)(2,1)S(1)}, bf16[2,32,512]{2,1,0:T(8,128)(2,1)S(1)}, u32[]{:S(2)}, u32[]{:S(2)}) %collective-permute-start.12) | collective-permute-done | bytes 65568 | tf_op jit(solution)/shard_map/ppermute | solution.py:414
  46.3 4.0 %collective-permute-done.15.refs_3_ = bf16[2,32,512]{2,1,0:T(8,128)(2,1)S(1)} collective-permute-done((bf16[2,32,512]{2,1,0:T(8,128)(2,1)S(1)}, bf16[2,32,512]{2,1,0:T(8,128)(2,1)S(1)}, u32[]{:S(2)}, u32[]{:S(2)}) %collective-permute-start.15) | collective-permute-done | bytes 65568 | tf_op jit(solution)/shard_map/ppermute | solution.py:414
  50.4 1.5 %collective-permute-done.18.refs_7_ = bf16[8,32,512]{2,1,0:T(8,128)(2,1)S(1)} collective-permute-done((bf16[8,32,512]{2,1,0:T(8,128)(2,1)S(1)}, bf16[8,32,512]{2,1,0:T(8,128)(2,1)S(1)}, u32[]{:S(2)}, u32[]{:S(2)}) %collective-permute-start.18) | collective-permute-done | bytes 262176 | tf_op jit(solution)/shard_map/ppermute | solution.py:414
  52.5 1.4 %terms.3 = (f32[32,3584]{1,0:T(8,128)S(1)}, bf16[32,3584]{1,0:T(8,128)(2,1)S(1)}) custom-call(bf16[64,1024]{1,0:T(8,128)(2,1)S(1)} %values.1.val_ref, bf16[1024,7168]{1,0:T(8,128)(2,1)S(1)} %bitcast.2), custom_call_target="tpu_custom_call" | custom-call | flops 6899999744 | tf_op jit(solution)/shard_map/terms/pallas_call | solution.py:37
  54.1 1.4 %terms.2 = (f32[32,3584]{1,0:T(8,128)S(1)}, bf16[32,3584]{1,0:T(8,128)(2,1)S(1)}) custom-call(bf16[64,1024]{1,0:T(8,128)(2,1)S(1)} %values.1.val_ref, bf16[1024,7168]{1,0:T(8,128)(2,1)S(1)} %bitcast.2), custom_call_target="tpu_custom_call" | custom-call | flops 6899999744 | tf_op jit(solution)/shard_map/terms/pallas_call | solution.py:37
  56.0 1.0 %collective-permute-start.24 = (bf16[8,3584]{1,0:T(8,128)(2,1)S(1)}, bf16[8,3584]{1,0:T(8,128)(2,1)S(1)}, u32[]{:S(2)}, u32[]{:S(2)}) collective-permute-start(bf16[8,3584]{1,0:T(8,128)(2,1)S(1)} %get-tuple-element.69), channel_id=1, source_target_pairs={{0,2},{1,3},{2,0},{3,1},{4,6},{5,7},{6,4},{7,5},{8,10},{9,11},{10,... | collective-permute-start | bytes 172040 | tf_op jit(solution)/shard_map/ppermute | solution.py:414
  57.1 1.1 %collective-permute-start.25 = (bf16[8,3584]{1,0:T(8,128)(2,1)S(1)}, bf16[8,3584]{1,0:T(8,128)(2,1)S(1)}, u32[]{:S(2)}, u32[]{:S(2)}) collective-permute-start(bf16[8,3584]{1,0:T(8,128)(2,1)S(1)} %get-tuple-element.70), channel_id=1, source_target_pairs={{0,2},{1,3},{2,0},{3,1},{4,6},{5,7},{6,4},{7,5},{8,10},{9,11},{10,... | collective-permute-start | bytes 172040 | tf_op jit(solution)/shard_map/ppermute | solution.py:414
  58.2 2.4 %collective-permute-start.22 = (bf16[4,7168]{1,0:T(4,128)(2,1)S(1)}, bf16[4,7168]{1,0:T(4,128)(2,1)S(1)}, u32[]{:S(2)}, u32[]{:S(2)}) collective-permute-start(bf16[4,7168]{1,0:T(4,128)(2,1)S(1)} %get-tuple-element.65), channel_id=1, source_target_pairs={{0,6},{1,7},{2,4},{3,5},{4,2},{5,3},{6,0},{7,1},{8,14},{9,15},{10,... | collective-permute-start | bytes 172040 | tf_op jit(solution)/shard_map/ppermute | solution.py:414
  60.6 1.0 %collective-permute-start.23 = (bf16[4,7168]{1,0:T(4,128)(2,1)S(1)}, bf16[4,7168]{1,0:T(4,128)(2,1)S(1)}, u32[]{:S(2)}, u32[]{:S(2)}) collective-permute-start(bf16[4,7168]{1,0:T(4,128)(2,1)S(1)} %get-tuple-element.66), channel_id=1, source_target_pairs={{0,2},{1,3},{2,0},{3,1},{4,6},{5,7},{6,4},{7,5},{8,10},{9,11},{10,... | collective-permute-start | bytes 172040 | tf_op jit(solution)/shard_map/ppermute | solution.py:414
  61.7 2.0 %collective-permute-start.26 = (bf16[4,7168]{1,0:T(4,128)(2,1)S(1)}, bf16[4,7168]{1,0:T(4,128)(2,1)S(1)}, u32[]{:S(2)}, u32[]{:S(2)}) collective-permute-start(bf16[4,7168]{1,0:T(4,128)(2,1)S(1)} %get-tuple-element.71), channel_id=1, source_target_pairs={{0,12},{1,13},{2,14},{3,15},{4,8},{5,9},{6,10},{7,11},{8,4},{9,5},... | collective-permute-start | bytes 172040 | tf_op jit(solution)/shard_map/ppermute | solution.py:414
  63.9 1.0 %collective-permute-done.23.refs_3_ = bf16[4,7168]{1,0:T(4,128)(2,1)S(1)} collective-permute-done((bf16[4,7168]{1,0:T(4,128)(2,1)S(1)}, bf16[4,7168]{1,0:T(4,128)(2,1)S(1)}, u32[]{:S(2)}, u32[]{:S(2)}) %collective-permute-start.23) | collective-permute-done | bytes 57376 | tf_op jit(solution)/shard_map/ppermute | solution.py:414
  64.8 3.0 %collective-permute-done.26.refs_4_ = bf16[4,7168]{1,0:T(4,128)(2,1)S(1)} collective-permute-done((bf16[4,7168]{1,0:T(4,128)(2,1)S(1)}, bf16[4,7168]{1,0:T(4,128)(2,1)S(1)}, u32[]{:S(2)}, u32[]{:S(2)}) %collective-permute-start.26) | collective-permute-done | bytes 57376 | tf_op jit(solution)/shard_map/ppermute | solution.py:414
  67.8 1.5 %collective-permute-done.27.refs_5_ = bf16[4,7168]{1,0:T(4,128)(2,1)S(1)} collective-permute-done((bf16[4,7168]{1,0:T(4,128)(2,1)S(1)}, bf16[4,7168]{1,0:T(4,128)(2,1)S(1)}, u32[]{:S(2)}, u32[]{:S(2)}) %collective-permute-start.27) | collective-permute-done | bytes 57376 | tf_op jit(solution)/shard_map/ppermute | solution.py:414
  (71 shorter events, 5.9 us)
Async XLA Ops:
  0.0 14.2 %collective-permute-start.4 = (bf16[1536,1536]{1,0:T(8,128)(2,1)}, bf16[1536,1536]{1,0:T(8,128)(2,1)S(1)}, u32[]{:S(2)}, u32[]{:S(2)}) collective-permute-start(bf16[1536,1536]{1,0:T(8,128)(2,1)} %refs_4_.1), channel_id=1, source_target_pairs={{0,1},{1,0},{2,3},{3,2},{4,5},{5,4},{6,7},{7,6},{8,9},{9,8},{10,11... | collective-permute-start | bytes 14155784 | tf_op jit(solution)/shard_map/ppermute | solution.py:414
  0.5 13.7 %collective-permute-start.5 = (bf16[8,128,512]{2,1,0:T(8,128)(2,1)}, bf16[8,128,512]{2,1,0:T(8,128)(2,1)S(1)}, u32[]{:S(2)}, u32[]{:S(2)}) collective-permute-start(bf16[8,128,512]{2,1,0:T(8,128)(2,1)} %refs_5_.1), channel_id=1, source_target_pairs={{0,1},{1,0},{2,3},{3,2},{4,5},{5,4},{6,7},{7,6},{8,9},{9,8},{10,11... | collective-permute-start | bytes 3145736 | tf_op jit(solution)/shard_map/ppermute | solution.py:414
  0.5 4.8 %collective-permute-start = (bf16[4,1536]{1,0:T(4,128)(2,1)}, bf16[4,1536]{1,0:T(4,128)(2,1)S(1)}, u32[]{:S(2)}, u32[]{:S(2)}) collective-permute-start(bf16[4,1536]{1,0:T(4,128)(2,1)} %refs_0_.1), channel_id=1, source_target_pairs={{0,2},{1,3},{2,0},{3,1},{4,6},{5,7},{6,4},{7,5},{8,10},{9,11},{10,... | collective-permute-start | bytes 36872 | tf_op jit(solution)/shard_map/ppermute | solution.py:414
  4.1 10.1 %slice-start.6 = ((s8[4718592]{0:T(1024)(128)(4,1)}), s8[4194304]{0:T(1024)(128)(4,1)S(1)}, s32[]{:S(2)}) async-start(s8[4718592]{0:T(1024)(128)(4,1)} %bitcast.7), calls=%async_computation.6 | async-start | bytes 8388608
  5.4 8.9 %copy-start = (bf16[8,128,512]{2,1,0:T(8,128)(2,1)S(1)}, bf16[8,128,512]{2,1,0:T(8,128)(2,1)}, u32[]{:S(2)}) copy-start(bf16[8,128,512]{2,1,0:T(8,128)(2,1)} %refs_5_.1) | copy-start | bytes 3145732
  5.4 20.3 %slice-start.4 = ((s8[7077888]{0:T(1024)(128)(4,1)}), s8[4194304]{0:T(1024)(128)(4,1)S(1)}, s32[]{:S(2)}) async-start(s8[7077888]{0:T(1024)(128)(4,1)} %bitcast.3), calls=%async_computation.4 | async-start | bytes 8388608
  5.4 20.3 %slice-start.5 = ((s8[7077888]{0:T(1024)(128)(4,1)}), s8[2883584]{0:T(1024)(128)(4,1)S(1)}, s32[]{:S(2)}) async-start(s8[7077888]{0:T(1024)(128)(4,1)} %bitcast.3), calls=%async_computation.5 | async-start | bytes 5767168
  5.4 5.0 %collective-permute-start.3 = (bf16[8,1536]{1,0:T(8,128)(2,1)S(1)}, bf16[8,1536]{1,0:T(8,128)(2,1)S(1)}, u32[]{:S(2)}, u32[]{:S(2)}) collective-permute-start(bf16[8,1536]{1,0:T(8,128)(2,1)S(1)} %get-tuple-element.43.refs_0_), channel_id=1, source_target_pairs={{0,8},{1,9},{2,10},{3,11},{4,12},{5,13},{6,14},{7,15},{8,0},{9,1},... | collective-permute-start | bytes 73736 | tf_op jit(solution)/shard_map/ppermute | solution.py:414
  8.6 5.6 %collective-permute-start.2 = (bf16[8,1536]{1,0:T(8,128)(2,1)S(1)}, bf16[8,1536]{1,0:T(8,128)(2,1)S(1)}, u32[]{:S(2)}, u32[]{:S(2)}) collective-permute-start(bf16[8,1536]{1,0:T(8,128)(2,1)S(1)} %get-tuple-element.43.refs_0_), channel_id=1, source_target_pairs={{0,12},{1,13},{2,14},{3,15},{4,8},{5,9},{6,10},{7,11},{8,4},{9,5},... | collective-permute-start | bytes 73736 | tf_op jit(solution)/shard_map/ppermute | solution.py:414
  9.9 4.3 %collective-permute-start.1 = (bf16[8,1536]{1,0:T(8,128)(2,1)S(1)}, bf16[8,1536]{1,0:T(8,128)(2,1)S(1)}, u32[]{:S(2)}, u32[]{:S(2)}) collective-permute-start(bf16[8,1536]{1,0:T(8,128)(2,1)S(1)} %get-tuple-element.43.refs_0_), channel_id=1, source_target_pairs={{0,4},{1,5},{2,6},{3,7},{4,0},{5,1},{6,2},{7,3},{8,12},{9,13},{10,... | collective-permute-start | bytes 73736 | tf_op jit(solution)/shard_map/ppermute | solution.py:414
  16.5 7.4 %collective-permute-start.6 = (bf16[4,144,128]{2,1,0:T(8,128)(2,1)S(1)}, bf16[4,144,128]{2,1,0:T(8,128)(2,1)S(1)}, u32[]{:S(2)}, u32[]{:S(2)}) collective-permute-start(bf16[4,144,128]{2,1,0:T(8,128)(2,1)S(1)} %get-tuple-element.45), channel_id=1, source_target_pairs={{0,2},{1,3},{2,0},{3,1},{4,6},{5,7},{6,4},{7,5},{8,10},{9,11},{10,... | collective-permute-start | bytes 442376 | tf_op jit(solution)/shard_map/ppermute | solution.py:414
  18.1 10.2 %collective-permute-start.7 = (bf16[2,144,128]{2,1,0:T(8,128)(2,1)S(1)}, bf16[2,144,128]{2,1,0:T(8,128)(2,1)S(1)}, u32[]{:S(2)}, u32[]{:S(2)}) collective-permute-start(bf16[2,144,128]{2,1,0:T(8,128)(2,1)S(1)} %get-tuple-element.46), channel_id=1, source_target_pairs={{0,8},{1,9},{2,10},{3,11},{4,12},{5,13},{6,14},{7,15},{8,0},{9,1},... | collective-permute-start | bytes 221192 | tf_op jit(solution)/shard_map/ppermute | solution.py:414
  19.4 9.0 %collective-permute-start.8 = (bf16[2,144,128]{2,1,0:T(8,128)(2,1)S(1)}, bf16[2,144,128]{2,1,0:T(8,128)(2,1)S(1)}, u32[]{:S(2)}, u32[]{:S(2)}) collective-permute-start(bf16[2,144,128]{2,1,0:T(8,128)(2,1)S(1)} %get-tuple-element.47), channel_id=1, source_target_pairs={{0,14},{1,15},{2,12},{3,13},{4,10},{5,11},{6,8},{7,9},{8,6},{9,7},... | collective-permute-start | bytes 221192 | tf_op jit(solution)/shard_map/ppermute | solution.py:414
  20.2 8.1 %collective-permute-start.9 = (bf16[2,144,128]{2,1,0:T(8,128)(2,1)S(1)}, bf16[2,144,128]{2,1,0:T(8,128)(2,1)S(1)}, u32[]{:S(2)}, u32[]{:S(2)}) collective-permute-start(bf16[2,144,128]{2,1,0:T(8,128)(2,1)S(1)} %get-tuple-element.48), channel_id=1, source_target_pairs={{0,12},{1,13},{2,14},{3,15},{4,8},{5,9},{6,10},{7,11},{8,4},{9,5},... | collective-permute-start | bytes 221192 | tf_op jit(solution)/shard_map/ppermute | solution.py:414
  23.1 9.6 %collective-permute-start.10 = (bf16[2,144,128]{2,1,0:T(8,128)(2,1)S(1)}, bf16[2,144,128]{2,1,0:T(8,128)(2,1)S(1)}, u32[]{:S(2)}, u32[]{:S(2)}) collective-permute-start(bf16[2,144,128]{2,1,0:T(8,128)(2,1)S(1)} %get-tuple-element.49), channel_id=1, source_target_pairs={{0,10},{1,11},{2,8},{3,9},{4,14},{5,15},{6,12},{7,13},{8,2},{9,3},... | collective-permute-start | bytes 221192 | tf_op jit(solution)/shard_map/ppermute | solution.py:414
  24.0 8.7 %collective-permute-start.11 = (bf16[4,144,128]{2,1,0:T(8,128)(2,1)S(1)}, bf16[4,144,128]{2,1,0:T(8,128)(2,1)S(1)}, u32[]{:S(2)}, u32[]{:S(2)}) collective-permute-start(bf16[4,144,128]{2,1,0:T(8,128)(2,1)S(1)} %forward.2.after_ref), channel_id=1, source_target_pairs={{0,4},{1,5},{2,6},{3,7},{4,0},{5,1},{6,2},{7,3},{8,12},{9,13},{10,... | collective-permute-start | bytes 442376 | tf_op jit(solution)/shard_map/ppermute | solution.py:414
  36.2 6.4 %collective-permute-start.16 = (bf16[4,32,512]{2,1,0:T(8,128)(2,1)S(1)}, bf16[4,32,512]{2,1,0:T(8,128)(2,1)S(1)}, u32[]{:S(2)}, u32[]{:S(2)}) collective-permute-start(bf16[4,32,512]{2,1,0:T(8,128)(2,1)S(1)} %get-tuple-element.55), channel_id=1, source_target_pairs={{0,2},{1,3},{2,0},{3,1},{4,6},{5,7},{6,4},{7,5},{8,10},{9,11},{10,... | collective-permute-start | bytes 393224 | tf_op jit(solution)/shard_map/ppermute | solution.py:414
  36.7 9.5 %collective-permute-start.12 = (bf16[2,32,512]{2,1,0:T(8,128)(2,1)S(1)}, bf16[2,32,512]{2,1,0:T(8,128)(2,1)S(1)}, u32[]{:S(2)}, u32[]{:S(2)}) collective-permute-start(bf16[2,32,512]{2,1,0:T(8,128)(2,1)S(1)} %get-tuple-element.51), channel_id=1, source_target_pairs={{0,8},{1,9},{2,10},{3,11},{4,12},{5,13},{6,14},{7,15},{8,0},{9,1},... | collective-permute-start | bytes 196616 | tf_op jit(solution)/shard_map/ppermute | solution.py:414
  36.8 9.5 %collective-permute-start.13 = (bf16[2,32,512]{2,1,0:T(8,128)(2,1)S(1)}, bf16[2,32,512]{2,1,0:T(8,128)(2,1)S(1)}, u32[]{:S(2)}, u32[]{:S(2)}) collective-permute-start(bf16[2,32,512]{2,1,0:T(8,128)(2,1)S(1)} %get-tuple-element.52), channel_id=1, source_target_pairs={{0,14},{1,15},{2,12},{3,13},{4,10},{5,11},{6,8},{7,9},{8,6},{9,7},... | collective-permute-start | bytes 196616 | tf_op jit(solution)/shard_map/ppermute | solution.py:414
  39.4 6.9 %collective-permute-start.14 = (bf16[2,32,512]{2,1,0:T(8,128)(2,1)S(1)}, bf16[2,32,512]{2,1,0:T(8,128)(2,1)S(1)}, u32[]{:S(2)}, u32[]{:S(2)}) collective-permute-start(bf16[2,32,512]{2,1,0:T(8,128)(2,1)S(1)} %get-tuple-element.53), channel_id=1, source_target_pairs={{0,12},{1,13},{2,14},{3,15},{4,8},{5,9},{6,10},{7,11},{8,4},{9,5},... | collective-permute-start | bytes 196616 | tf_op jit(solution)/shard_map/ppermute | solution.py:414
  41.6 8.7 %collective-permute-start.15 = (bf16[2,32,512]{2,1,0:T(8,128)(2,1)S(1)}, bf16[2,32,512]{2,1,0:T(8,128)(2,1)S(1)}, u32[]{:S(2)}, u32[]{:S(2)}) collective-permute-start(bf16[2,32,512]{2,1,0:T(8,128)(2,1)S(1)} %get-tuple-element.54), channel_id=1, source_target_pairs={{0,10},{1,11},{2,8},{3,9},{4,14},{5,15},{6,12},{7,13},{8,2},{9,3},... | collective-permute-start | bytes 196616 | tf_op jit(solution)/shard_map/ppermute | solution.py:414
  42.6 7.7 %collective-permute-start.17 = (bf16[4,32,512]{2,1,0:T(8,128)(2,1)S(1)}, bf16[4,32,512]{2,1,0:T(8,128)(2,1)S(1)}, u32[]{:S(2)}, u32[]{:S(2)}) collective-permute-start(bf16[4,32,512]{2,1,0:T(8,128)(2,1)S(1)} %forward.3.after_ref), channel_id=1, source_target_pairs={{0,4},{1,5},{2,6},{3,7},{4,0},{5,1},{6,2},{7,3},{8,12},{9,13},{10,... | collective-permute-start | bytes 393224 | tf_op jit(solution)/shard_map/ppermute | solution.py:414
  50.4 1.6 %collective-permute-start.18 = (bf16[8,32,512]{2,1,0:T(8,128)(2,1)S(1)}, bf16[8,32,512]{2,1,0:T(8,128)(2,1)S(1)}, u32[]{:S(2)}, u32[]{:S(2)}) collective-permute-start(bf16[8,32,512]{2,1,0:T(8,128)(2,1)S(1)} %regroup.1), channel_id=1, source_target_pairs={{0,1},{1,0},{2,3},{3,2},{4,5},{5,4},{6,7},{7,6},{8,9},{9,8},{10,11... | collective-permute-start | bytes 786440 | tf_op jit(solution)/shard_map/ppermute | solution.py:414
  53.9 2.0 %collective-permute-start.20 = (bf16[32,3584]{1,0:T(8,128)(2,1)S(1)}, bf16[32,3584]{1,0:T(8,128)(2,1)S(1)}, u32[]{:S(2)}, u32[]{:S(2)}) collective-permute-start(bf16[32,3584]{1,0:T(8,128)(2,1)S(1)} %get-tuple-element.61), channel_id=1, source_target_pairs={{0,1},{1,0},{2,3},{3,2},{4,5},{5,4},{6,7},{7,6},{8,9},{9,8},{10,11... | collective-permute-start | bytes 688136 | tf_op jit(solution)/shard_map/ppermute | solution.py:414
  55.4 1.6 %collective-permute-start.19 = (bf16[32,3584]{1,0:T(8,128)(2,1)S(1)}, bf16[32,3584]{1,0:T(8,128)(2,1)S(1)}, u32[]{:S(2)}, u32[]{:S(2)}) collective-permute-start(bf16[32,3584]{1,0:T(8,128)(2,1)S(1)} %get-tuple-element.59), channel_id=1, source_target_pairs={{0,1},{1,0},{2,3},{3,2},{4,5},{5,4},{6,7},{7,6},{8,9},{9,8},{10,11... | collective-permute-start | bytes 688136 | tf_op jit(solution)/shard_map/ppermute | solution.py:414
  56.0 5.7 %collective-permute-start.24 = (bf16[8,3584]{1,0:T(8,128)(2,1)S(1)}, bf16[8,3584]{1,0:T(8,128)(2,1)S(1)}, u32[]{:S(2)}, u32[]{:S(2)}) collective-permute-start(bf16[8,3584]{1,0:T(8,128)(2,1)S(1)} %get-tuple-element.69), channel_id=1, source_target_pairs={{0,2},{1,3},{2,0},{3,1},{4,6},{5,7},{6,4},{7,5},{8,10},{9,11},{10,... | collective-permute-start | bytes 172040 | tf_op jit(solution)/shard_map/ppermute | solution.py:414
  57.1 4.6 %collective-permute-start.25 = (bf16[8,3584]{1,0:T(8,128)(2,1)S(1)}, bf16[8,3584]{1,0:T(8,128)(2,1)S(1)}, u32[]{:S(2)}, u32[]{:S(2)}) collective-permute-start(bf16[8,3584]{1,0:T(8,128)(2,1)S(1)} %get-tuple-element.70), channel_id=1, source_target_pairs={{0,2},{1,3},{2,0},{3,1},{4,6},{5,7},{6,4},{7,5},{8,10},{9,11},{10,... | collective-permute-start | bytes 172040 | tf_op jit(solution)/shard_map/ppermute | solution.py:414
  58.2 5.5 %collective-permute-start.21 = (bf16[4,7168]{1,0:T(4,128)(2,1)S(1)}, bf16[4,7168]{1,0:T(4,128)(2,1)S(1)}, u32[]{:S(2)}, u32[]{:S(2)}) collective-permute-start(bf16[4,7168]{1,0:T(4,128)(2,1)S(1)} %get-tuple-element.64), channel_id=1, source_target_pairs={{0,4},{1,5},{2,6},{3,7},{4,0},{5,1},{6,2},{7,3},{8,12},{9,13},{10,... | collective-permute-start | bytes 172040 | tf_op jit(solution)/shard_map/ppermute | solution.py:414
  58.2 5.6 %collective-permute-start.22 = (bf16[4,7168]{1,0:T(4,128)(2,1)S(1)}, bf16[4,7168]{1,0:T(4,128)(2,1)S(1)}, u32[]{:S(2)}, u32[]{:S(2)}) collective-permute-start(bf16[4,7168]{1,0:T(4,128)(2,1)S(1)} %get-tuple-element.65), channel_id=1, source_target_pairs={{0,6},{1,7},{2,4},{3,5},{4,2},{5,3},{6,0},{7,1},{8,14},{9,15},{10,... | collective-permute-start | bytes 172040 | tf_op jit(solution)/shard_map/ppermute | solution.py:414
  60.6 4.2 %collective-permute-start.23 = (bf16[4,7168]{1,0:T(4,128)(2,1)S(1)}, bf16[4,7168]{1,0:T(4,128)(2,1)S(1)}, u32[]{:S(2)}, u32[]{:S(2)}) collective-permute-start(bf16[4,7168]{1,0:T(4,128)(2,1)S(1)} %get-tuple-element.66), channel_id=1, source_target_pairs={{0,2},{1,3},{2,0},{3,1},{4,6},{5,7},{6,4},{7,5},{8,10},{9,11},{10,... | collective-permute-start | bytes 172040 | tf_op jit(solution)/shard_map/ppermute | solution.py:414
  61.7 6.0 %collective-permute-start.26 = (bf16[4,7168]{1,0:T(4,128)(2,1)S(1)}, bf16[4,7168]{1,0:T(4,128)(2,1)S(1)}, u32[]{:S(2)}, u32[]{:S(2)}) collective-permute-start(bf16[4,7168]{1,0:T(4,128)(2,1)S(1)} %get-tuple-element.71), channel_id=1, source_target_pairs={{0,12},{1,13},{2,14},{3,15},{4,8},{5,9},{6,10},{7,11},{8,4},{9,5},... | collective-permute-start | bytes 172040 | tf_op jit(solution)/shard_map/ppermute | solution.py:414
  63.7 5.6 %collective-permute-start.27 = (bf16[4,7168]{1,0:T(4,128)(2,1)S(1)}, bf16[4,7168]{1,0:T(4,128)(2,1)S(1)}, u32[]{:S(2)}, u32[]{:S(2)}) collective-permute-start(bf16[4,7168]{1,0:T(4,128)(2,1)S(1)} %get-tuple-element.72), channel_id=1, source_target_pairs={{0,8},{1,9},{2,10},{3,11},{4,12},{5,13},{6,14},{7,15},{8,0},{9,1},... | collective-permute-start | bytes 172040 | tf_op jit(solution)/shard_map/ppermute | solution.py:414
  (10 other events, 61.1 us)

commit v14 on v12

--- a/solution.py
+++ b/solution.py
@@ -20,6 +20,8 @@
 PARTS = 2
 Y = 2
 Z1 = 4
+PASSED = Y + Z1
+NEAR = (Z1, PASSED, Y)
 
 
 def resident(x):
@@ -61,9 +63,16 @@
     return [k for k in far_first(devices, 2) if k > Y + Z1]
 
 
-def chip_orders(devices):
-    far, near = far_chips(devices), [Y, Z1, Y + Z1]
-    return [*near, *far, 0], [*far, *near, 0]
+def sent_orders(devices):
+    far = far_chips(devices)
+    even = [PASSED, Y, *far]
+    odd = [far[0], PASSED, far[1], Y, *far[2:]]
+    return [*even, Z1, 0], [*odd, Z1, 0]
+
+
+def arrived_orders(devices):
+    even, odd = sent_orders(devices)
+    return [*even[1:-1], PASSED, 0], [odd[0], *odd[2:-1], PASSED, 0]
 
 
 def on_odd_core():
@@ -129,7 +138,7 @@
     lane = lax.broadcasted_iota(jnp.int32, (wide // 2, LANES), 1)
     odd = on_odd_core()
     gathered = gathered_order(devices)
-    orders = zip(*[[gathered.index(k) for k in order] for order in chip_orders(devices)])
+    orders = zip(*[[gathered.index(k) for k in order] for order in sent_orders(devices)])
     for core, (wq_ref, wk_ref) in enumerate(weights):
         projected = jnp.dot(piece, wq_ref[...], preferred_element_type=jnp.float32)
         for h in range(heads):
@@ -177,9 +186,27 @@
     return call(flip_kernel, shape(rows, maxlen, LAT), 4, "flip")(resident(keys), after)
 
 
-def attend_kernel(chips, len_ref, cos_ref, sin_ref, key_ref, flip_ref, new_ref, *refs):
-    blocks = [(ref, core) for ref in refs[:chips] for core in range(2)]
-    out_refs = refs[chips:]
+def forward_kernel(pair_ref, first_ref, second_ref, sent_ref, kept_ref):
+    odd = on_odd_core()
+    first, second = first_ref[...], second_ref[...]
+    sent_ref[:2] = pair_ref[...]
+    sent_ref[2:] = jnp.where(odd, second, first)
+    kept_ref[...] = jnp.where(odd, first, second)
+
+
+def forward(pair, first, second):
+    out = (shape(4, *pair.shape[1:]), shape(*pair.shape))
+    return call(forward_kernel, out, 1, "forward")(pair, first, second)
+
+
+def arrived(refs):
+    return [(ref, i) for ref in refs for i in range(ref.shape[0])]
+
+
+def attend_kernel(count, len_ref, cos_ref, sin_ref, key_ref, flip_ref, new_ref, *refs):
+    blocks = arrived(refs[:count])
+    out_refs = refs[count:]
+    odd = on_odd_core()
     rows, _, maxlen = key_ref.shape
     wide = out_refs[0].shape[1]
     heads = wide // rows
@@ -208,6 +235,9 @@
         position = lax.broadcasted_iota(jnp.int32, (1, maxlen), 1)
         return jnp.where(position < len_ref[r], scores, -jnp.inf), own
 
+    straight = [(1 + i, out_ref) for i, out_ref in enumerate(out_refs[2:-1])]
+    straight.append((len(out_refs) - 1, out_refs[-1]))
+    passed = len(out_refs) - 2
     ahead = score(0)
     for r in range(rows):
         scores, own = ahead
@@ -221,43 +251,57 @@
         own_weight = (own_expo * inverse).astype(jnp.bfloat16).astype(jnp.float32)
         summed = jnp.dot(weights, flip_ref[r], preferred_element_type=jnp.float32)
         summed += own_weight * new_ref[r : r + 1, :LAT].astype(jnp.float32)
-        for k in range(2 * chips):
-            out_refs[k // 2][k % 2, r * heads : (r + 1) * heads, :] = summed[
-                k * heads : (k + 1) * heads, :
-            ].astype(jnp.bfloat16)
-
-
-def attend(lengths, tables, keys, flipped, new_latent, messages, heads):
-    chips = len(messages)
-    out = [shape(2, keys.shape[0] * heads, LAT)] * chips
-    return call(functools.partial(attend_kernel, chips), out, 10, "attend", scalars=1)(
+        summed = summed.astype(jnp.bfloat16)
+        for core in range(2):
+            at = slice(r * heads, (r + 1) * heads)
+            chip = [summed[k * heads : (k + 1) * heads, :] for k in range(core, len(blocks), 2)]
+            for k, out_ref in straight:
+                out_ref[core, at, :] = chip[k]
+            out_refs[0][core, at, :] = jnp.where(odd, chip[0], chip[passed])
+            out_refs[1][core, at, :] = jnp.where(odd, chip[passed], chip[0])
+
+
+def attend(lengths, tables, keys, flipped, new_latent, messages, heads, devices):
+    out = [shape(2, keys.shape[0] * heads, LAT)] * (devices // 2)
+    return call(functools.partial(attend_kernel, len(messages)), out, 10, "attend", scalars=1)(
         lengths, *tables, resident(keys), resident(flipped), new_latent, *messages
     )
 
 
+def early_kernel(own_ref, after_ref, out_ref):
+    out_ref[...] = own_ref[1]
+
+
+def early(own, after):
+    return call(early_kernel, shape(*own.shape[1:]), 4, "early")(own, after)
+
+
 def regroup_kernel(*refs):
-    *in_refs, out_ref = refs
-    for j, ref in enumerate(in_refs):
-        out_ref[j] = ref[1]
-
-
-def regroup(messages):
+    *in_refs, early_ref, out_ref = refs
+    blocks = arrived(in_refs)[1::2]
+    for j, (ref, i) in enumerate(blocks[:-1]):
+        out_ref[j] = ref[i]
+    out_ref[len(blocks) - 1] = early_ref[...]
+
+
+def regroup(messages, ready, chips):
     _, wide, width = messages[0].shape
-    return call(regroup_kernel, shape(len(messages), wide, width), 1, "regroup")(*messages)
+    return call(regroup_kernel, shape(chips, wide, width), 1, "regroup")(*messages, ready)
 
 
 def values_kernel(devices, *refs):
+    *in_refs, other_ref, wv_ref, val_ref, rows_ref = refs
     chips = devices // 2
-    mine_refs = refs[:chips]
-    other_ref, wv_ref, val_ref, rows_ref = refs[chips:]
     heads = wv_ref.shape[0]
     wide = other_ref.shape[1]
     odd = on_odd_core()
-    orders = [places(devices, order) for order in chip_orders(devices)]
+    orders = [places(devices, order) for order in arrived_orders(devices)]
+    mine_blocks = arrived(in_refs)[::2]
     for i, (even_place, odd_place) in enumerate(zip(*orders)):
+        ref, at = mine_blocks[i]
         mine = block_at(odd, even_place, odd_place, wide)
         other = block_at(odd, chips + odd_place, chips + even_place, wide)
-        for where, block in ((mine, mine_refs[i][0]), (other, other_ref[i])):
+        for where, block in ((mine, ref[at]), (other, other_ref[i])):
             block = block.astype(jnp.float32)
             for c in range(PIECES):
                 rows_ref[c, where, :] = block[:, c * LANES : (c + 1) * LANES]
@@ -300,7 +344,7 @@
 
 
 def far_z(devices):
-    return [z for z in far_first(devices, Z1) if z > Z1]
+    return [z for z in far_first(devices, Z1) if z > Z1][::-1]
 
 
 def places(devices, chips):
@@ -320,22 +364,21 @@
 
 
 def last_part_kernel(rows, keep, give, near, mine_ref, other_ref, before_ref, *out_refs):
-    keep_ref, give_ref, local_ref, pair_ref = out_refs
+    keep_ref, give_ref, *near_refs = out_refs
     total = mine_ref[...] + other_ref[...].astype(jnp.float32)
     keep_ref[...] = pick(total, rows, keep)
     give_ref[...] = pick(total, rows, give).astype(give_ref.dtype)
-    here = pick(total, rows, near)
-    half, width = local_ref.shape[0], before_ref.shape[1]
-    for columns, block in ((slice(0, width), before_ref[...]), (slice(width, None), here)):
-        local_ref[:, columns] = block[:half]
-        pair_ref[:, columns] = block[half:].astype(pair_ref.dtype)
+    width = before_ref.shape[1]
+    for i, (j, out_ref) in enumerate(zip(near, near_refs)):
+        out_ref[:, :width] = before_ref[i * rows : (i + 1) * rows].astype(out_ref.dtype)
+        out_ref[:, width:] = total[j * rows : (j + 1) * rows].astype(out_ref.dtype)
 
 
 def core_sum(mine, other, before, rows, devices):
     count, width = mine.shape
     keep = places(devices, far_z(devices))
     give = places(devices, [z + Y for z in far_z(devices)])
-    near = places(devices, [0, Y, Z1, Z1 + Y])
+    near = places(devices, [0, *NEAR])
     far = len(keep) * rows
     out = (shape(far, width, dtype=jnp.float32), shape(far, width))
     if before is None:
@@ -344,7 +387,7 @@
         return call(kernel, out, 1, "core_sum")(mine, other)
     kernel = functools.partial(last_part_kernel, rows, keep, give, near)
     full = before.shape[1] + width
-    out += (shape(2 * rows, full, dtype=jnp.float32), shape(2 * rows, full))
+    out += (shape(rows, full, dtype=jnp.float32), *[shape(rows, full)] * len(NEAR))
     return call(kernel, out, 1, "core_sum")(mine, other, before)
 
 
@@ -368,19 +411,6 @@
     return call(far_sum_kernel, out, 1, "far_sum")(*mine, *other)
 
 
-def near_sum_kernel(mine_ref, other_ref, keep_ref, give_ref):
-    total = mine_ref[...] + other_ref[...].astype(jnp.float32)
-    rows = keep_ref.shape[0]
-    keep_ref[...] = total[:rows]
-    give_ref[...] = total[rows:].astype(give_ref.dtype)
-
-
-def near_sum(mine, other):
-    rows, width = mine.shape[0] // 2, mine.shape[1]
-    out = (shape(rows, width, dtype=jnp.float32), shape(rows, width))
-    return call(near_sum_kernel, out, 1, "near_sum")(mine, other)
-
-
 def last_sum_kernel(*refs):
     *in_refs, out_ref = refs
     terms = [ref[...].astype(jnp.float32) for ref in in_refs]
@@ -405,29 +435,33 @@
     far_weights = [swap(w_uq, 1), swap(w_uk, 1)]
     tables, near = join(rotary(lengths), [q_latent, across])
     def exchange(messages):
+        *first, pair, own = messages
         got = []
-        for block, flips in zip(messages, zip(*chip_orders(devices))):
+        for block, chips in zip(first, zip(*sent_orders(devices))):
+            flips = [Y if k == PASSED else k for k in chips]
             pairs = [(i, i ^ flips[i % 2]) for i in range(devices)]
-            got.append(lax.ppermute(block, "row", pairs) if any(flips) else block)
-        return got
+            got.append(lax.ppermute(block, "row", pairs))
+        sent, kept = forward(pair, *got[:2])
+        return [kept, *got[2:], swap(sent, Z1), own], sent
 
     messages = project([swap(near, z) for z in zs], [w_uq, w_uk, *far_weights], devices)
+    messages, sent = exchange(messages)
     keys = jnp.swapaxes(cache, 1, 2)
-    flipped = flip(keys, messages[-1])
-    messages = exchange(messages)
-    latents = attend(lengths, tables, keys, flipped, new_latent, messages, heads)
-    latents = exchange(latents)
-    values = head_values(latents, swap(regroup(latents), 1), w_uv, devices)
+    flipped = flip(keys, sent)
+    latents = attend(lengths, tables, keys, flipped, new_latent, messages, heads, devices)
+    latents, sent = exchange(latents)
+    other = swap(regroup(latents, early(latents[-1], sent), devices // 2), 1)
+    values = head_values(latents, other, w_uv, devices)
     keep, got, near = [], [], None
     for part in range(PARTS):
         mine, other = output_terms(values, w_o, part)
-        far_mine, far_other, near, *pair = core_sum(mine, swap(other, 1), near, rows, devices)
+        far_mine, far_other, near, *given = core_sum(mine, swap(other, 1), near, rows, devices)
         keep.append(far_mine)
         got.append(swap(far_other, Y))
-    local, across = near_sum(near, swap(pair[0], Z1))
+    given = [swap(block, k) for block, k in zip(given, NEAR)]
     far = far_sum(keep, got, rows)
     far = [swap(block, z) for z, block in zip(far_z(devices), far)]
-    return last_sum([local, swap(across, Y), *far])
+    return last_sum([near, *given, *far])
 
 
 def solution(mesh):

time: 70.7 us -> 71.3 us (level)
  waiting for transfers between devices: 20 us -> 21.1 us
    ppermute x14 -> x12, starting transfers between devices: 22.4 us -> 19.5 us  [exchange(): got.append(lax.ppermute(block, 'row', pairs))]
    ppermute x15 -> x18, starting transfers between devices: 14.9 us -> 17.3 us  [swap(): return lax.ppermute(block, 'row', [(i, i ^ k) for i in range(devices)])]
    ppermute x14 -> x12, waiting for transfers between devices: 7.58 us -> 8.75 us  [exchange(): got.append(lax.ppermute(block, 'row', pairs))]
    ppermute x15 -> x18, waiting for transfers between devices: 12.5 us -> 12.4 us  [swap(): return lax.ppermute(block, 'row', [(i, i ^ k) for i in range(devices)])]
    pallas_call x14 -> x16, Pallas kernels: 12.2 us -> 12.2 us  [run(): pl.pallas_call(kernel, out_shape=out_shape, in_specs=smem + [in_vmem()] *...]
  transfers between devices with their start and end apart: 29 -> 30, of which waited for: 12 -> 15; matrix products, arithmetic and copies ran while one was open for 0% -> 0% of each run, Pallas kernels for 5% -> 6%
where the time goes in v14:
time: 71.3 us; the launch traced here: 71.2 us
  starting transfers between devices  36.8 us (52%)
  waiting for transfers between devices  21.1 us (30%)
  Pallas kernels  12.2 us (17%)
  local copies, waits for them, and re-layouts  0.73 us (1%)
    ppermute x12, starting transfers between devices, exchange(): got.append(lax.ppermute(block, 'row', pairs))  19.5 us
    ppermute x18, starting transfers between devices, swap(): return lax.ppermute(block, 'row', [(i, i ^ k) for i in range(devices)])  17.3 us
    ppermute x18, waiting for transfers between devices, swap(): return lax.ppermute(block, 'row', [(i, i ^ k) for i in range(devices)])  12.4 us
    pallas_call x16, Pallas kernels, run(): pl.pallas_call(kernel, out_shape=out_shape, in_specs=smem + [in_vmem()] *...  12.2 us
    ppermute x12, waiting for transfers between devices, exchange(): got.append(lax.ppermute(block, 'row', pairs))  8.75 us
  transfers between devices with their start and end apart: 30, of which 15 were waited for; matrix products, arithmetic and copies ran while one was open for 0% of the time, Pallas kernels for 6%

profile of v14, /device:TPU:0, one launch (start us, length us, event | category | flops | bytes accessed | tf_op | source)
XLA Modules:
  0.0 71.2 jit_solution(10928443509092876066)
XLA Ops:
  0.5 3.0 %collective-permute-start = (bf16[4,1536]{1,0:T(4,128)(2,1)}, bf16[4,1536]{1,0:T(4,128)(2,1)S(1)}, u32[]{:S(2)}, u32[]{:S(2)}) collective-permute-start(bf16[4,1536]{1,0:T(4,128)(2,1)} %refs_0_.1), channel_id=1, source_target_pairs={{0,2},{1,3},{2,0},{3,1},{4,6},{5,7},{6,4},{7,5},{8,10},{9,11},{10,... | collective-permute-start | bytes 36872 | tf_op jit(solution)/shard_map/ppermute | solution.py:432
  5.4 3.2 %collective-permute-start.3 = (bf16[8,1536]{1,0:T(8,128)(2,1)S(1)}, bf16[8,1536]{1,0:T(8,128)(2,1)S(1)}, u32[]{:S(2)}, u32[]{:S(2)}) collective-permute-start(bf16[8,1536]{1,0:T(8,128)(2,1)S(1)} %get-tuple-element.49.refs_0_), channel_id=1, source_target_pairs={{0,8},{1,9},{2,10},{3,11},{4,12},{5,13},{6,14},{7,15},{8,0},{9,1},... | collective-permute-start | bytes 73736 | tf_op jit(solution)/shard_map/ppermute | solution.py:432
  8.6 1.3 %collective-permute-start.2 = (bf16[8,1536]{1,0:T(8,128)(2,1)S(1)}, bf16[8,1536]{1,0:T(8,128)(2,1)S(1)}, u32[]{:S(2)}, u32[]{:S(2)}) collective-permute-start(bf16[8,1536]{1,0:T(8,128)(2,1)S(1)} %get-tuple-element.49.refs_0_), channel_id=1, source_target_pairs={{0,12},{1,13},{2,14},{3,15},{4,8},{5,9},{6,10},{7,11},{8,4},{9,5},... | collective-permute-start | bytes 73736 | tf_op jit(solution)/shard_map/ppermute | solution.py:432
  10.4 3.8 %collective-permute-done.2.refs_2_ = bf16[8,1536]{1,0:T(8,128)(2,1)S(1)} collective-permute-done((bf16[8,1536]{1,0:T(8,128)(2,1)S(1)}, bf16[8,1536]{1,0:T(8,128)(2,1)S(1)}, u32[]{:S(2)}, u32[]{:S(2)}) %collective-permute-start.2) | collective-permute-done | bytes 24608 | tf_op jit(solution)/shard_map/ppermute | solution.py:432
  14.2 2.3 %project.1 = (bf16[2,144,128]{2,1,0:T(8,128)(2,1)S(1)}, bf16[2,144,128]{2,1,0:T(8,128)(2,1)S(1)}, bf16[2,144,128]{2,1,0:T(8,128)(2,1)S(1)}, bf16[2,144,128]{2,1,...) custom-call(bf16[8,1536]{1,0:T(8,128)(2,1)S(1)} %get-tuple-element.4, ...), custom_call_target="tpu_custom_call" | custom-call | flops 23000000512 | tf_op jit(solution)/shard_map/project/pallas_call | solution.py:38
  16.6 1.6 %collective-permute-start.6 = (bf16[2,144,128]{2,1,0:T(8,128)(2,1)S(1)}, bf16[2,144,128]{2,1,0:T(8,128)(2,1)S(1)}, u32[]{:S(2)}, u32[]{:S(2)}) collective-permute-start(bf16[2,144,128]{2,1,0:T(8,128)(2,1)S(1)} %get-tuple-element.51), channel_id=1, source_target_pairs={{0,2},{1,9},{2,0},{3,11},{4,6},{5,13},{6,4},{7,15},{8,10},{9,1},{1... | collective-permute-start | bytes 221192 | tf_op jit(solution)/shard_map/ppermute | solution.py:443
  18.6 1.2 %collective-permute-start.8 = (bf16[2,144,128]{2,1,0:T(8,128)(2,1)S(1)}, bf16[2,144,128]{2,1,0:T(8,128)(2,1)S(1)}, u32[]{:S(2)}, u32[]{:S(2)}) collective-permute-start(bf16[2,144,128]{2,1,0:T(8,128)(2,1)S(1)} %get-tuple-element.55), channel_id=1, source_target_pairs={{0,8},{1,11},{2,10},{3,9},{4,12},{5,15},{6,14},{7,13},{8,0},{9,3},... | collective-permute-start | bytes 221192 | tf_op jit(solution)/shard_map/ppermute | solution.py:443
  19.9 2.6 %collective-permute-start.9 = (bf16[2,144,128]{2,1,0:T(8,128)(2,1)S(1)}, bf16[2,144,128]{2,1,0:T(8,128)(2,1)S(1)}, u32[]{:S(2)}, u32[]{:S(2)}) collective-permute-start(bf16[2,144,128]{2,1,0:T(8,128)(2,1)S(1)} %get-tuple-element.56), channel_id=1, source_target_pairs={{0,10},{1,3},{2,8},{3,1},{4,14},{5,7},{6,12},{7,5},{8,2},{9,11},{1... | collective-permute-start | bytes 221192 | tf_op jit(solution)/shard_map/ppermute | solution.py:443
  22.5 2.0 %collective-permute-start.10 = (bf16[2,144,128]{2,1,0:T(8,128)(2,1)S(1)}, bf16[2,144,128]{2,1,0:T(8,128)(2,1)S(1)}, u32[]{:S(2)}, u32[]{:S(2)}) collective-permute-start(bf16[2,144,128]{2,1,0:T(8,128)(2,1)S(1)} %get-tuple-element.57), channel_id=1, source_target_pairs={{0,12},{1,13},{2,14},{3,15},{4,8},{5,9},{6,10},{7,11},{8,4},{9,5},... | collective-permute-start | bytes 221192 | tf_op jit(solution)/shard_map/ppermute | solution.py:443
  24.5 1.8 %collective-permute-start.11 = (bf16[2,144,128]{2,1,0:T(8,128)(2,1)S(1)}, bf16[2,144,128]{2,1,0:T(8,128)(2,1)S(1)}, u32[]{:S(2)}, u32[]{:S(2)}) collective-permute-start(bf16[2,144,128]{2,1,0:T(8,128)(2,1)S(1)} %get-tuple-element.58), channel_id=1, source_target_pairs={{0,14},{1,15},{2,12},{3,13},{4,10},{5,11},{6,8},{7,9},{8,6},{9,7},... | collective-permute-start | bytes 221192 | tf_op jit(solution)/shard_map/ppermute | solution.py:443
  26.5 1.7 %flip.1.flip_ref = bf16[4,1536,512]{2,1,0:T(8,128)(2,1)S(1)} custom-call(bf16[4,576,1536]{2,1,0:T(8,128)(2,1)S(1)} %bitcast.5, bf16[4,144,128]{2,1,0:T(8,128)(2,1)S(1)} %get-tuple-element.53.after_ref), custom_call_target="tpu_custom_call" | custom-call | flops 4600000000 | tf_op jit(solution)/shard_map/flip/pallas_call | solution.py:38
  28.2 2.0 %collective-permute-done.9.refs_2_ = bf16[2,144,128]{2,1,0:T(8,128)(2,1)S(1)} collective-permute-done((bf16[2,144,128]{2,1,0:T(8,128)(2,1)S(1)}, bf16[2,144,128]{2,1,0:T(8,128)(2,1)S(1)}, u32[]{:S(2)}, u32[]{:S(2)}) %collective-permute-start.9) | collective-permute-done | bytes 73760 | tf_op jit(solution)/shard_map/ppermute | solution.py:443
  30.2 1.5 %collective-permute-done.11.refs_4_ = bf16[2,144,128]{2,1,0:T(8,128)(2,1)S(1)} collective-permute-done((bf16[2,144,128]{2,1,0:T(8,128)(2,1)S(1)}, bf16[2,144,128]{2,1,0:T(8,128)(2,1)S(1)}, u32[]{:S(2)}, u32[]{:S(2)}) %collective-permute-start.11) | collective-permute-done | bytes 73760 | tf_op jit(solution)/shard_map/ppermute | solution.py:443
  32.3 3.4 %attend.1 = (bf16[2,32,512]{2,1,0:T(8,128)(2,1)S(1)}, bf16[2,32,512]{2,1,0:T(8,128)(2,1)S(1)}, bf16[2,32,512]{2,1,0:T(8,128)(2,1)S(1)}, bf16[2,32,512]{2,1,0:T(8...) custom-call(s32[4]{0:T(128)S(1)} %copy-done.5, ...), custom_call_target="tpu_custom_call" | custom-call | flops 11500000256 | tf_op jit(solution)/shard_map/attend/pallas_call | solution.py:38
  35.8 1.6 %collective-permute-start.13 = (bf16[2,32,512]{2,1,0:T(8,128)(2,1)S(1)}, bf16[2,32,512]{2,1,0:T(8,128)(2,1)S(1)}, u32[]{:S(2)}, u32[]{:S(2)}) collective-permute-start(bf16[2,32,512]{2,1,0:T(8,128)(2,1)S(1)} %get-tuple-element.61), channel_id=1, source_target_pairs={{0,2},{1,9},{2,0},{3,11},{4,6},{5,13},{6,4},{7,15},{8,10},{9,1},{1... | collective-permute-start | bytes 196616 | tf_op jit(solution)/shard_map/ppermute | solution.py:443
  37.9 1.1 %collective-permute-start.15 = (bf16[2,32,512]{2,1,0:T(8,128)(2,1)S(1)}, bf16[2,32,512]{2,1,0:T(8,128)(2,1)S(1)}, u32[]{:S(2)}, u32[]{:S(2)}) collective-permute-start(bf16[2,32,512]{2,1,0:T(8,128)(2,1)S(1)} %get-tuple-element.64), channel_id=1, source_target_pairs={{0,8},{1,11},{2,10},{3,9},{4,12},{5,15},{6,14},{7,13},{8,0},{9,3},... | collective-permute-start | bytes 196616 | tf_op jit(solution)/shard_map/ppermute | solution.py:443
  38.9 2.8 %collective-permute-start.16 = (bf16[2,32,512]{2,1,0:T(8,128)(2,1)S(1)}, bf16[2,32,512]{2,1,0:T(8,128)(2,1)S(1)}, u32[]{:S(2)}, u32[]{:S(2)}) collective-permute-start(bf16[2,32,512]{2,1,0:T(8,128)(2,1)S(1)} %get-tuple-element.65), channel_id=1, source_target_pairs={{0,10},{1,3},{2,8},{3,1},{4,14},{5,7},{6,12},{7,5},{8,2},{9,11},{1... | collective-permute-start | bytes 196616 | tf_op jit(solution)/shard_map/ppermute | solution.py:443
  41.7 2.1 %collective-permute-start.17 = (bf16[2,32,512]{2,1,0:T(8,128)(2,1)S(1)}, bf16[2,32,512]{2,1,0:T(8,128)(2,1)S(1)}, u32[]{:S(2)}, u32[]{:S(2)}) collective-permute-start(bf16[2,32,512]{2,1,0:T(8,128)(2,1)S(1)} %get-tuple-element.66), channel_id=1, source_target_pairs={{0,12},{1,13},{2,14},{3,15},{4,8},{5,9},{6,10},{7,11},{8,4},{9,5},... | collective-permute-start | bytes 196616 | tf_op jit(solution)/shard_map/ppermute | solution.py:443
  43.8 1.7 %collective-permute-start.18 = (bf16[2,32,512]{2,1,0:T(8,128)(2,1)S(1)}, bf16[2,32,512]{2,1,0:T(8,128)(2,1)S(1)}, u32[]{:S(2)}, u32[]{:S(2)}) collective-permute-start(bf16[2,32,512]{2,1,0:T(8,128)(2,1)S(1)} %get-tuple-element.67), channel_id=1, source_target_pairs={{0,14},{1,15},{2,12},{3,13},{4,10},{5,11},{6,8},{7,9},{8,6},{9,7},... | collective-permute-start | bytes 196616 | tf_op jit(solution)/shard_map/ppermute | solution.py:443
  45.7 2.8 %collective-permute-done.16.refs_2_ = bf16[2,32,512]{2,1,0:T(8,128)(2,1)S(1)} collective-permute-done((bf16[2,32,512]{2,1,0:T(8,128)(2,1)S(1)}, bf16[2,32,512]{2,1,0:T(8,128)(2,1)S(1)}, u32[]{:S(2)}, u32[]{:S(2)}) %collective-permute-start.16) | collective-permute-done | bytes 65568 | tf_op jit(solution)/shard_map/ppermute | solution.py:443
  48.6 2.3 %collective-permute-done.18.refs_4_ = bf16[2,32,512]{2,1,0:T(8,128)(2,1)S(1)} collective-permute-done((bf16[2,32,512]{2,1,0:T(8,128)(2,1)S(1)}, bf16[2,32,512]{2,1,0:T(8,128)(2,1)S(1)}, u32[]{:S(2)}, u32[]{:S(2)}) %collective-permute-start.18) | collective-permute-done | bytes 65568 | tf_op jit(solution)/shard_map/ppermute | solution.py:443
  51.1 1.5 %collective-permute-done.20.refs_7_ = bf16[8,32,512]{2,1,0:T(8,128)(2,1)S(1)} collective-permute-done((bf16[8,32,512]{2,1,0:T(8,128)(2,1)S(1)}, bf16[8,32,512]{2,1,0:T(8,128)(2,1)S(1)}, u32[]{:S(2)}, u32[]{:S(2)}) %collective-permute-start.20) | collective-permute-done | bytes 262176 | tf_op jit(solution)/shard_map/ppermute | solution.py:432
  53.1 1.4 %terms.3 = (f32[32,3584]{1,0:T(8,128)S(1)}, bf16[32,3584]{1,0:T(8,128)(2,1)S(1)}) custom-call(bf16[64,1024]{1,0:T(8,128)(2,1)S(1)} %values.1.val_ref, bf16[1024,7168]{1,0:T(8,128)(2,1)S(1)} %bitcast.2), custom_call_target="tpu_custom_call" | custom-call | flops 6899999744 | tf_op jit(solution)/shard_map/terms/pallas_call | solution.py:38
  54.7 1.4 %terms.2 = (f32[32,3584]{1,0:T(8,128)S(1)}, bf16[32,3584]{1,0:T(8,128)(2,1)S(1)}) custom-call(bf16[64,1024]{1,0:T(8,128)(2,1)S(1)} %values.1.val_ref, bf16[1024,7168]{1,0:T(8,128)(2,1)S(1)} %bitcast.2), custom_call_target="tpu_custom_call" | custom-call | flops 6899999744 | tf_op jit(solution)/shard_map/terms/pallas_call | solution.py:38
  56.6 1.9 %collective-permute-start.26 = (bf16[8,3584]{1,0:T(8,128)(2,1)S(1)}, bf16[8,3584]{1,0:T(8,128)(2,1)S(1)}, u32[]{:S(2)}, u32[]{:S(2)}) collective-permute-start(bf16[8,3584]{1,0:T(8,128)(2,1)S(1)} %get-tuple-element.81), channel_id=1, source_target_pairs={{0,2},{1,3},{2,0},{3,1},{4,6},{5,7},{6,4},{7,5},{8,10},{9,11},{10,... | collective-permute-start | bytes 172040 | tf_op jit(solution)/shard_map/ppermute | solution.py:432
  58.5 1.0 %collective-permute-start.27 = (bf16[8,3584]{1,0:T(8,128)(2,1)S(1)}, bf16[8,3584]{1,0:T(8,128)(2,1)S(1)}, u32[]{:S(2)}, u32[]{:S(2)}) collective-permute-start(bf16[8,3584]{1,0:T(8,128)(2,1)S(1)} %get-tuple-element.82), channel_id=1, source_target_pairs={{0,2},{1,3},{2,0},{3,1},{4,6},{5,7},{6,4},{7,5},{8,10},{9,11},{10,... | collective-permute-start | bytes 172040 | tf_op jit(solution)/shard_map/ppermute | solution.py:432
  59.6 2.5 %collective-permute-start.24 = (bf16[4,7168]{1,0:T(4,128)(2,1)S(1)}, bf16[4,7168]{1,0:T(4,128)(2,1)S(1)}, u32[]{:S(2)}, u32[]{:S(2)}) collective-permute-start(bf16[4,7168]{1,0:T(4,128)(2,1)S(1)} %get-tuple-element.77), channel_id=1, source_target_pairs={{0,6},{1,7},{2,4},{3,5},{4,2},{5,3},{6,0},{7,1},{8,14},{9,15},{10,... | collective-permute-start | bytes 172040 | tf_op jit(solution)/shard_map/ppermute | solution.py:432
  62.1 1.0 %collective-permute-start.25 = (bf16[4,7168]{1,0:T(4,128)(2,1)S(1)}, bf16[4,7168]{1,0:T(4,128)(2,1)S(1)}, u32[]{:S(2)}, u32[]{:S(2)}) collective-permute-start(bf16[4,7168]{1,0:T(4,128)(2,1)S(1)} %get-tuple-element.78), channel_id=1, source_target_pairs={{0,2},{1,3},{2,0},{3,1},{4,6},{5,7},{6,4},{7,5},{8,10},{9,11},{10,... | collective-permute-start | bytes 172040 | tf_op jit(solution)/shard_map/ppermute | solution.py:432
  63.1 1.9 %collective-permute-start.28 = (bf16[4,7168]{1,0:T(4,128)(2,1)S(1)}, bf16[4,7168]{1,0:T(4,128)(2,1)S(1)}, u32[]{:S(2)}, u32[]{:S(2)}) collective-permute-start(bf16[4,7168]{1,0:T(4,128)(2,1)S(1)} %get-tuple-element.83), channel_id=1, source_target_pairs={{0,12},{1,13},{2,14},{3,15},{4,8},{5,9},{6,10},{7,11},{8,4},{9,5},... | collective-permute-start | bytes 172040 | tf_op jit(solution)/shard_map/ppermute | solution.py:432
  65.1 1.2 %collective-permute-done.25.refs_3_ = bf16[4,7168]{1,0:T(4,128)(2,1)S(1)} collective-permute-done((bf16[4,7168]{1,0:T(4,128)(2,1)S(1)}, bf16[4,7168]{1,0:T(4,128)(2,1)S(1)}, u32[]{:S(2)}, u32[]{:S(2)}) %collective-permute-start.25) | collective-permute-done | bytes 57376 | tf_op jit(solution)/shard_map/ppermute | solution.py:432
  66.3 2.9 %collective-permute-done.28.refs_4_ = bf16[4,7168]{1,0:T(4,128)(2,1)S(1)} collective-permute-done((bf16[4,7168]{1,0:T(4,128)(2,1)S(1)}, bf16[4,7168]{1,0:T(4,128)(2,1)S(1)}, u32[]{:S(2)}, u32[]{:S(2)}) %collective-permute-start.28) | collective-permute-done | bytes 57376 | tf_op jit(solution)/shard_map/ppermute | solution.py:432
  69.2 1.4 %collective-permute-done.29.refs_5_ = bf16[4,7168]{1,0:T(4,128)(2,1)S(1)} collective-permute-done((bf16[4,7168]{1,0:T(4,128)(2,1)S(1)}, bf16[4,7168]{1,0:T(4,128)(2,1)S(1)}, u32[]{:S(2)}, u32[]{:S(2)}) %collective-permute-start.29) | collective-permute-done | bytes 57376 | tf_op jit(solution)/shard_map/ppermute | solution.py:432
  (75 shorter events, 7.1 us)
Async XLA Ops:
  0.0 14.2 %collective-permute-start.4 = (bf16[1536,1536]{1,0:T(8,128)(2,1)}, bf16[1536,1536]{1,0:T(8,128)(2,1)S(1)}, u32[]{:S(2)}, u32[]{:S(2)}) collective-permute-start(bf16[1536,1536]{1,0:T(8,128)(2,1)} %refs_4_.1), channel_id=1, source_target_pairs={{0,1},{1,0},{2,3},{3,2},{4,5},{5,4},{6,7},{7,6},{8,9},{9,8},{10,11... | collective-permute-start | bytes 14155784 | tf_op jit(solution)/shard_map/ppermute | solution.py:432
  0.5 13.7 %collective-permute-start.5 = (bf16[8,128,512]{2,1,0:T(8,128)(2,1)}, bf16[8,128,512]{2,1,0:T(8,128)(2,1)S(1)}, u32[]{:S(2)}, u32[]{:S(2)}) collective-permute-start(bf16[8,128,512]{2,1,0:T(8,128)(2,1)} %refs_5_.1), channel_id=1, source_target_pairs={{0,1},{1,0},{2,3},{3,2},{4,5},{5,4},{6,7},{7,6},{8,9},{9,8},{10,11... | collective-permute-start | bytes 3145736 | tf_op jit(solution)/shard_map/ppermute | solution.py:432
  0.5 4.8 %collective-permute-start = (bf16[4,1536]{1,0:T(4,128)(2,1)}, bf16[4,1536]{1,0:T(4,128)(2,1)S(1)}, u32[]{:S(2)}, u32[]{:S(2)}) collective-permute-start(bf16[4,1536]{1,0:T(4,128)(2,1)} %refs_0_.1), channel_id=1, source_target_pairs={{0,2},{1,3},{2,0},{3,1},{4,6},{5,7},{6,4},{7,5},{8,10},{9,11},{10,... | collective-permute-start | bytes 36872 | tf_op jit(solution)/shard_map/ppermute | solution.py:432
  5.4 21.0 %slice-start.4 = ((s8[7077888]{0:T(1024)(128)(4,1)}), s8[4194304]{0:T(1024)(128)(4,1)S(1)}, s32[]{:S(2)}) async-start(s8[7077888]{0:T(1024)(128)(4,1)} %bitcast.3), calls=%async_computation.4 | async-start | bytes 8388608
  5.4 21.0 %slice-start.5 = ((s8[7077888]{0:T(1024)(128)(4,1)}), s8[2883584]{0:T(1024)(128)(4,1)S(1)}, s32[]{:S(2)}) async-start(s8[7077888]{0:T(1024)(128)(4,1)} %bitcast.3), calls=%async_computation.5 | async-start | bytes 5767168
  5.4 5.0 %collective-permute-start.3 = (bf16[8,1536]{1,0:T(8,128)(2,1)S(1)}, bf16[8,1536]{1,0:T(8,128)(2,1)S(1)}, u32[]{:S(2)}, u32[]{:S(2)}) collective-permute-start(bf16[8,1536]{1,0:T(8,128)(2,1)S(1)} %get-tuple-element.49.refs_0_), channel_id=1, source_target_pairs={{0,8},{1,9},{2,10},{3,11},{4,12},{5,13},{6,14},{7,15},{8,0},{9,1},... | collective-permute-start | bytes 73736 | tf_op jit(solution)/shard_map/ppermute | solution.py:432
  8.6 5.6 %collective-permute-start.2 = (bf16[8,1536]{1,0:T(8,128)(2,1)S(1)}, bf16[8,1536]{1,0:T(8,128)(2,1)S(1)}, u32[]{:S(2)}, u32[]{:S(2)}) collective-permute-start(bf16[8,1536]{1,0:T(8,128)(2,1)S(1)} %get-tuple-element.49.refs_0_), channel_id=1, source_target_pairs={{0,12},{1,13},{2,14},{3,15},{4,8},{5,9},{6,10},{7,11},{8,4},{9,5},... | collective-permute-start | bytes 73736 | tf_op jit(solution)/shard_map/ppermute | solution.py:432
  9.9 4.3 %collective-permute-start.1 = (bf16[8,1536]{1,0:T(8,128)(2,1)S(1)}, bf16[8,1536]{1,0:T(8,128)(2,1)S(1)}, u32[]{:S(2)}, u32[]{:S(2)}) collective-permute-start(bf16[8,1536]{1,0:T(8,128)(2,1)S(1)} %get-tuple-element.49.refs_0_), channel_id=1, source_target_pairs={{0,4},{1,5},{2,6},{3,7},{4,0},{5,1},{6,2},{7,3},{8,12},{9,13},{10,... | collective-permute-start | bytes 73736 | tf_op jit(solution)/shard_map/ppermute | solution.py:432
  16.6 8.0 %collective-permute-start.6 = (bf16[2,144,128]{2,1,0:T(8,128)(2,1)S(1)}, bf16[2,144,128]{2,1,0:T(8,128)(2,1)S(1)}, u32[]{:S(2)}, u32[]{:S(2)}) collective-permute-start(bf16[2,144,128]{2,1,0:T(8,128)(2,1)S(1)} %get-tuple-element.51), channel_id=1, source_target_pairs={{0,2},{1,9},{2,0},{3,11},{4,6},{5,13},{6,4},{7,15},{8,10},{9,1},{1... | collective-permute-start | bytes 221192 | tf_op jit(solution)/shard_map/ppermute | solution.py:443
  18.1 8.2 %collective-permute-start.7 = (bf16[2,144,128]{2,1,0:T(8,128)(2,1)S(1)}, bf16[2,144,128]{2,1,0:T(8,128)(2,1)S(1)}, u32[]{:S(2)}, u32[]{:S(2)}) collective-permute-start(bf16[2,144,128]{2,1,0:T(8,128)(2,1)S(1)} %get-tuple-element.52), channel_id=1, source_target_pairs={{0,2},{1,3},{2,0},{3,1},{4,6},{5,7},{6,4},{7,5},{8,10},{9,11},{10,... | collective-permute-start | bytes 221192 | tf_op jit(solution)/shard_map/ppermute | solution.py:443
  18.6 9.6 %collective-permute-start.8 = (bf16[2,144,128]{2,1,0:T(8,128)(2,1)S(1)}, bf16[2,144,128]{2,1,0:T(8,128)(2,1)S(1)}, u32[]{:S(2)}, u32[]{:S(2)}) collective-permute-start(bf16[2,144,128]{2,1,0:T(8,128)(2,1)S(1)} %get-tuple-element.55), channel_id=1, source_target_pairs={{0,8},{1,11},{2,10},{3,9},{4,12},{5,15},{6,14},{7,13},{8,0},{9,3},... | collective-permute-start | bytes 221192 | tf_op jit(solution)/shard_map/ppermute | solution.py:443
  19.9 10.4 %collective-permute-start.9 = (bf16[2,144,128]{2,1,0:T(8,128)(2,1)S(1)}, bf16[2,144,128]{2,1,0:T(8,128)(2,1)S(1)}, u32[]{:S(2)}, u32[]{:S(2)}) collective-permute-start(bf16[2,144,128]{2,1,0:T(8,128)(2,1)S(1)} %get-tuple-element.56), channel_id=1, source_target_pairs={{0,10},{1,3},{2,8},{3,1},{4,14},{5,7},{6,12},{7,5},{8,2},{9,11},{1... | collective-permute-start | bytes 221192 | tf_op jit(solution)/shard_map/ppermute | solution.py:443
  22.5 7.7 %collective-permute-start.10 = (bf16[2,144,128]{2,1,0:T(8,128)(2,1)S(1)}, bf16[2,144,128]{2,1,0:T(8,128)(2,1)S(1)}, u32[]{:S(2)}, u32[]{:S(2)}) collective-permute-start(bf16[2,144,128]{2,1,0:T(8,128)(2,1)S(1)} %get-tuple-element.57), channel_id=1, source_target_pairs={{0,12},{1,13},{2,14},{3,15},{4,8},{5,9},{6,10},{7,11},{8,4},{9,5},... | collective-permute-start | bytes 221192 | tf_op jit(solution)/shard_map/ppermute | solution.py:443
  24.5 7.2 %collective-permute-start.11 = (bf16[2,144,128]{2,1,0:T(8,128)(2,1)S(1)}, bf16[2,144,128]{2,1,0:T(8,128)(2,1)S(1)}, u32[]{:S(2)}, u32[]{:S(2)}) collective-permute-start(bf16[2,144,128]{2,1,0:T(8,128)(2,1)S(1)} %get-tuple-element.58), channel_id=1, source_target_pairs={{0,14},{1,15},{2,12},{3,13},{4,10},{5,11},{6,8},{7,9},{8,6},{9,7},... | collective-permute-start | bytes 221192 | tf_op jit(solution)/shard_map/ppermute | solution.py:443
  26.3 6.0 %collective-permute-start.12 = (bf16[4,144,128]{2,1,0:T(8,128)(2,1)S(1)}, bf16[4,144,128]{2,1,0:T(8,128)(2,1)S(1)}, u32[]{:S(2)}, u32[]{:S(2)}) collective-permute-start(bf16[4,144,128]{2,1,0:T(8,128)(2,1)S(1)} %get-tuple-element.53.after_ref), channel_id=1, source_target_pairs={{0,4},{1,5},{2,6},{3,7},{4,0},{5,1},{6,2},{7,3},{8,12},{9,13},{10,... | collective-permute-start | bytes 442376 | tf_op jit(solution)/shard_map/ppermute | solution.py:432
  35.8 8.1 %collective-permute-start.13 = (bf16[2,32,512]{2,1,0:T(8,128)(2,1)S(1)}, bf16[2,32,512]{2,1,0:T(8,128)(2,1)S(1)}, u32[]{:S(2)}, u32[]{:S(2)}) collective-permute-start(bf16[2,32,512]{2,1,0:T(8,128)(2,1)S(1)} %get-tuple-element.61), channel_id=1, source_target_pairs={{0,2},{1,9},{2,0},{3,11},{4,6},{5,13},{6,4},{7,15},{8,10},{9,1},{1... | collective-permute-start | bytes 196616 | tf_op jit(solution)/shard_map/ppermute | solution.py:443
  37.4 8.2 %collective-permute-start.14 = (bf16[2,32,512]{2,1,0:T(8,128)(2,1)S(1)}, bf16[2,32,512]{2,1,0:T(8,128)(2,1)S(1)}, u32[]{:S(2)}, u32[]{:S(2)}) collective-permute-start(bf16[2,32,512]{2,1,0:T(8,128)(2,1)S(1)} %get-tuple-element.62), channel_id=1, source_target_pairs={{0,2},{1,3},{2,0},{3,1},{4,6},{5,7},{6,4},{7,5},{8,10},{9,11},{10,... | collective-permute-start | bytes 196616 | tf_op jit(solution)/shard_map/ppermute | solution.py:443
  37.9 7.8 %collective-permute-start.15 = (bf16[2,32,512]{2,1,0:T(8,128)(2,1)S(1)}, bf16[2,32,512]{2,1,0:T(8,128)(2,1)S(1)}, u32[]{:S(2)}, u32[]{:S(2)}) collective-permute-start(bf16[2,32,512]{2,1,0:T(8,128)(2,1)S(1)} %get-tuple-element.64), channel_id=1, source_target_pairs={{0,8},{1,11},{2,10},{3,9},{4,12},{5,15},{6,14},{7,13},{8,0},{9,3},... | collective-permute-start | bytes 196616 | tf_op jit(solution)/shard_map/ppermute | solution.py:443
  38.9 9.6 %collective-permute-start.16 = (bf16[2,32,512]{2,1,0:T(8,128)(2,1)S(1)}, bf16[2,32,512]{2,1,0:T(8,128)(2,1)S(1)}, u32[]{:S(2)}, u32[]{:S(2)}) collective-permute-start(bf16[2,32,512]{2,1,0:T(8,128)(2,1)S(1)} %get-tuple-element.65), channel_id=1, source_target_pairs={{0,10},{1,3},{2,8},{3,1},{4,14},{5,7},{6,12},{7,5},{8,2},{9,11},{1... | collective-permute-start | bytes 196616 | tf_op jit(solution)/shard_map/ppermute | solution.py:443
  41.7 6.8 %collective-permute-start.17 = (bf16[2,32,512]{2,1,0:T(8,128)(2,1)S(1)}, bf16[2,32,512]{2,1,0:T(8,128)(2,1)S(1)}, u32[]{:S(2)}, u32[]{:S(2)}) collective-permute-start(bf16[2,32,512]{2,1,0:T(8,128)(2,1)S(1)} %get-tuple-element.66), channel_id=1, source_target_pairs={{0,12},{1,13},{2,14},{3,15},{4,8},{5,9},{6,10},{7,11},{8,4},{9,5},... | collective-permute-start | bytes 196616 | tf_op jit(solution)/shard_map/ppermute | solution.py:443
  43.8 7.0 %collective-permute-start.18 = (bf16[2,32,512]{2,1,0:T(8,128)(2,1)S(1)}, bf16[2,32,512]{2,1,0:T(8,128)(2,1)S(1)}, u32[]{:S(2)}, u32[]{:S(2)}) collective-permute-start(bf16[2,32,512]{2,1,0:T(8,128)(2,1)S(1)} %get-tuple-element.67), channel_id=1, source_target_pairs={{0,14},{1,15},{2,12},{3,13},{4,10},{5,11},{6,8},{7,9},{8,6},{9,7},... | collective-permute-start | bytes 196616 | tf_op jit(solution)/shard_map/ppermute | solution.py:443
  45.5 5.4 %collective-permute-start.19 = (bf16[4,32,512]{2,1,0:T(8,128)(2,1)S(1)}, bf16[4,32,512]{2,1,0:T(8,128)(2,1)S(1)}, u32[]{:S(2)}, u32[]{:S(2)}) collective-permute-start(bf16[4,32,512]{2,1,0:T(8,128)(2,1)S(1)} %get-tuple-element.68.after_ref), channel_id=1, source_target_pairs={{0,4},{1,5},{2,6},{3,7},{4,0},{5,1},{6,2},{7,3},{8,12},{9,13},{10,... | collective-permute-start | bytes 393224 | tf_op jit(solution)/shard_map/ppermute | solution.py:432
  51.0 1.6 %collective-permute-start.20 = (bf16[8,32,512]{2,1,0:T(8,128)(2,1)S(1)}, bf16[8,32,512]{2,1,0:T(8,128)(2,1)S(1)}, u32[]{:S(2)}, u32[]{:S(2)}) collective-permute-start(bf16[8,32,512]{2,1,0:T(8,128)(2,1)S(1)} %regroup.1), channel_id=1, source_target_pairs={{0,1},{1,0},{2,3},{3,2},{4,5},{5,4},{6,7},{7,6},{8,9},{9,8},{10,11... | collective-permute-start | bytes 786440 | tf_op jit(solution)/shard_map/ppermute | solution.py:432
  54.5 2.0 %collective-permute-start.22 = (bf16[32,3584]{1,0:T(8,128)(2,1)S(1)}, bf16[32,3584]{1,0:T(8,128)(2,1)S(1)}, u32[]{:S(2)}, u32[]{:S(2)}) collective-permute-start(bf16[32,3584]{1,0:T(8,128)(2,1)S(1)} %get-tuple-element.73), channel_id=1, source_target_pairs={{0,1},{1,0},{2,3},{3,2},{4,5},{5,4},{6,7},{7,6},{8,9},{9,8},{10,11... | collective-permute-start | bytes 688136 | tf_op jit(solution)/shard_map/ppermute | solution.py:432
  56.1 2.4 %collective-permute-start.21 = (bf16[32,3584]{1,0:T(8,128)(2,1)S(1)}, bf16[32,3584]{1,0:T(8,128)(2,1)S(1)}, u32[]{:S(2)}, u32[]{:S(2)}) collective-permute-start(bf16[32,3584]{1,0:T(8,128)(2,1)S(1)} %get-tuple-element.71), channel_id=1, source_target_pairs={{0,1},{1,0},{2,3},{3,2},{4,5},{5,4},{6,7},{7,6},{8,9},{9,8},{10,11... | collective-permute-start | bytes 688136 | tf_op jit(solution)/shard_map/ppermute | solution.py:432
  56.6 6.5 %collective-permute-start.26 = (bf16[8,3584]{1,0:T(8,128)(2,1)S(1)}, bf16[8,3584]{1,0:T(8,128)(2,1)S(1)}, u32[]{:S(2)}, u32[]{:S(2)}) collective-permute-start(bf16[8,3584]{1,0:T(8,128)(2,1)S(1)} %get-tuple-element.81), channel_id=1, source_target_pairs={{0,2},{1,3},{2,0},{3,1},{4,6},{5,7},{6,4},{7,5},{8,10},{9,11},{10,... | collective-permute-start | bytes 172040 | tf_op jit(solution)/shard_map/ppermute | solution.py:432
  58.5 4.5 %collective-permute-start.27 = (bf16[8,3584]{1,0:T(8,128)(2,1)S(1)}, bf16[8,3584]{1,0:T(8,128)(2,1)S(1)}, u32[]{:S(2)}, u32[]{:S(2)}) collective-permute-start(bf16[8,3584]{1,0:T(8,128)(2,1)S(1)} %get-tuple-element.82), channel_id=1, source_target_pairs={{0,2},{1,3},{2,0},{3,1},{4,6},{5,7},{6,4},{7,5},{8,10},{9,11},{10,... | collective-permute-start | bytes 172040 | tf_op jit(solution)/shard_map/ppermute | solution.py:432
  59.6 5.4 %collective-permute-start.23 = (bf16[4,7168]{1,0:T(4,128)(2,1)S(1)}, bf16[4,7168]{1,0:T(4,128)(2,1)S(1)}, u32[]{:S(2)}, u32[]{:S(2)}) collective-permute-start(bf16[4,7168]{1,0:T(4,128)(2,1)S(1)} %get-tuple-element.76), channel_id=1, source_target_pairs={{0,4},{1,5},{2,6},{3,7},{4,0},{5,1},{6,2},{7,3},{8,12},{9,13},{10,... | collective-permute-start | bytes 172040 | tf_op jit(solution)/shard_map/ppermute | solution.py:432
  59.6 5.5 %collective-permute-start.24 = (bf16[4,7168]{1,0:T(4,128)(2,1)S(1)}, bf16[4,7168]{1,0:T(4,128)(2,1)S(1)}, u32[]{:S(2)}, u32[]{:S(2)}) collective-permute-start(bf16[4,7168]{1,0:T(4,128)(2,1)S(1)} %get-tuple-element.77), channel_id=1, source_target_pairs={{0,6},{1,7},{2,4},{3,5},{4,2},{5,3},{6,0},{7,1},{8,14},{9,15},{10,... | collective-permute-start | bytes 172040 | tf_op jit(solution)/shard_map/ppermute | solution.py:432
  62.1 4.2 %collective-permute-start.25 = (bf16[4,7168]{1,0:T(4,128)(2,1)S(1)}, bf16[4,7168]{1,0:T(4,128)(2,1)S(1)}, u32[]{:S(2)}, u32[]{:S(2)}) collective-permute-start(bf16[4,7168]{1,0:T(4,128)(2,1)S(1)} %get-tuple-element.78), channel_id=1, source_target_pairs={{0,2},{1,3},{2,0},{3,1},{4,6},{5,7},{6,4},{7,5},{8,10},{9,11},{10,... | collective-permute-start | bytes 172040 | tf_op jit(solution)/shard_map/ppermute | solution.py:432
  63.1 6.0 %collective-permute-start.28 = (bf16[4,7168]{1,0:T(4,128)(2,1)S(1)}, bf16[4,7168]{1,0:T(4,128)(2,1)S(1)}, u32[]{:S(2)}, u32[]{:S(2)}) collective-permute-start(bf16[4,7168]{1,0:T(4,128)(2,1)S(1)} %get-tuple-element.83), channel_id=1, source_target_pairs={{0,12},{1,13},{2,14},{3,15},{4,8},{5,9},{6,10},{7,11},{8,4},{9,5},... | collective-permute-start | bytes 172040 | tf_op jit(solution)/shard_map/ppermute | solution.py:432
  65.0 5.5 %collective-permute-start.29 = (bf16[4,7168]{1,0:T(4,128)(2,1)S(1)}, bf16[4,7168]{1,0:T(4,128)(2,1)S(1)}, u32[]{:S(2)}, u32[]{:S(2)}) collective-permute-start(bf16[4,7168]{1,0:T(4,128)(2,1)S(1)} %get-tuple-element.84), channel_id=1, source_target_pairs={{0,8},{1,9},{2,10},{3,11},{4,12},{5,13},{6,14},{7,15},{8,0},{9,1},... | collective-permute-start | bytes 172040 | tf_op jit(solution)/shard_map/ppermute | solution.py:432
  (12 other events, 76.9 us)

commit v15 on v13

--- a/solution.py
+++ b/solution.py
@@ -59,8 +59,7 @@
 
 
 def far_chips(devices):
-    chips = [k for k in far_first(devices, 2) if k > Y + Z1]
-    return chips[:1] + chips[:0:-1]
+    return [k for k in far_first(devices, 2) if k > Y + Z1]
 
 
 def chip_order(devices):
@@ -277,52 +276,51 @@
     return call(regroup_kernel, shape(chips, wide, width), 1, "regroup")(*messages, ready)
 
 
-def values_kernel(*refs):
-    *in_refs, other_ref, wv_ref, val_ref, rows_ref = refs
-    mine = arrived(in_refs)[::2]
-    chips = len(mine)
+def values_kernel(count, *refs):
+    blocks = arrived(refs[:count])
+    blocks = blocks[::2] if count > 1 else blocks
+    wv_ref, val_ref, rows_ref = refs[count], *refs[-2:]
     heads = wv_ref.shape[0]
-    wide = other_ref.shape[1]
-    for place in range(2 * chips):
-        ref, i = mine[place] if place < chips else (other_ref, place - chips)
+    for place, (ref, i) in enumerate(blocks):
         block = ref[i].astype(jnp.float32)
+        wide = block.shape[0]
         for c in range(PIECES):
             rows_ref[c, place * wide : (place + 1) * wide, :] = block[:, c * LANES : (c + 1) * LANES]
-    count = val_ref.shape[0]
+    total = val_ref.shape[0]
     for h in range(heads):
         chosen = jnp.concatenate(
-            [rows_ref[c, pl.ds(h, count, stride=heads), :] for c in range(PIECES)], axis=-1
+            [rows_ref[c, pl.ds(h, total, stride=heads), :] for c in range(PIECES)], axis=-1
         )
         val_ref[:, h * VD : (h + 1) * VD] = jnp.dot(
             chosen.astype(jnp.bfloat16), wv_ref[h], preferred_element_type=jnp.float32
         ).astype(jnp.bfloat16)
 
 
-def head_values(messages, other, w_uv):
-    chips, wide, _ = other.shape
+def head_values(messages, w_uv, chips, *after):
     heads = w_uv.shape[0]
-    count = 2 * chips * wide // heads
+    count = chips * messages[0].shape[1] // heads
     scratch = [pltpu.VMEM((PIECES, count * heads, LANES), jnp.float32)]
-    return call(values_kernel, shape(count, heads * VD), 3, "values", scratch)(
-        *messages, other, resident(w_uv)
+    kernel = functools.partial(values_kernel, len(messages))
+    return call(kernel, shape(count, heads * VD), 2, "values", scratch)(
+        *messages, resident(w_uv), *after
     )
 
 
-def terms_kernel(start, val_ref, wo_ref, mine_ref, other_ref):
-    half, width = mine_ref.shape
-    terms = jnp.dot(
-        val_ref[...], wo_ref[:, start : start + width], preferred_element_type=jnp.float32
-    )
-    mine_ref[...] = terms[:half]
-    other_ref[...] = terms[half:].astype(jnp.bfloat16)
-
-
-def output_terms(values, w_o, part):
-    half = values.shape[0] // 2
+def terms_kernel(start, *refs):
+    *val_refs, wo_ref = refs[: len(refs) // 2 + 1]
+    out_refs = refs[len(refs) // 2 + 1 :]
+    half, width = out_refs[0].shape
+    values = jnp.concatenate([ref[...] for ref in val_refs], axis=0)
+    terms = jnp.dot(values, wo_ref[:, start : start + width], preferred_element_type=jnp.float32)
+    for i, out_ref in enumerate(out_refs):
+        out_ref[...] = terms[i * half : (i + 1) * half].astype(out_ref.dtype)
+
+
+def output_terms(values, types, w_o, part):
     width = w_o.shape[1] // PARTS
-    out = (shape(half, width, dtype=jnp.float32), shape(half, width))
+    out = [shape(v.shape[0], width, dtype=t) for v, t in zip(values, types)]
     kernel = functools.partial(terms_kernel, part * width)
-    return call(kernel, out, 6, "terms")(values, resident(w_o))
+    return call(kernel, out, 3 * len(values), "terms")(*values, resident(w_o))
 
 
 def far_z(devices):
@@ -433,10 +431,17 @@
     latents = attend(lengths, tables, keys, flipped, new_latent, messages, heads, devices)
     latents, sent = exchange(latents)
     ready = early(latents[-3], latents[-1], sent)
-    values = head_values(latents, swap(regroup(latents, ready, devices // 2), 1), w_uv)
+    other = swap(regroup(latents, ready, devices // 2), 1)
+    here, there = jnp.float32, jnp.bfloat16
+    mine_values = head_values(latents, w_uv, devices // 2)
+    early_mine = output_terms([mine_values], [here], w_o, 0)
+    other_values = head_values([other], w_uv, devices // 2, *early_mine)
     keep, got, near = [], [], None
     for part in range(PARTS):
-        mine, other = output_terms(values, w_o, part)
+        if part == 0:
+            mine, other = *early_mine, *output_terms([other_values], [there], w_o, 0)
+        else:
+            mine, other = output_terms([mine_values, other_values], [here, there], w_o, part)
         far_mine, far_other, near, *given = core_sum(mine, swap(other, 1), near, rows, devices)
         keep.append(far_mine)
         got.append(swap(far_other, Y))

time: 70.1 us -> 71.3 us (1.017)
  waiting for transfers between devices: 22.6 us -> 19.6 us
  Pallas kernels: 12.2 us -> 13.7 us
  starting transfers between devices: 34.2 us -> 35.7 us
  local copies, waits for them, and re-layouts: 0.72 us -> 1.85 us
    ppermute x28, waiting for transfers between devices: 22.6 us -> 19.6 us  [swap(): return lax.ppermute(block, 'row', [(i, i ^ k) for i in range(devices)])]
    pallas_call x16 -> x18, Pallas kernels: 12.2 us -> 13.7 us  [run(): pl.pallas_call(kernel, out_shape=out_shape, in_specs=smem + [in_vmem()] *...]
    ppermute x28, starting transfers between devices: 34.2 us -> 35.7 us  [swap(): return lax.ppermute(block, 'row', [(i, i ^ k) for i in range(devices)])]
    unnamed x28, local copies, waits for them, and re-layouts: 0.72 us -> 1.85 us
  transfers between devices with their start and end apart: 28 -> 28, of which waited for: 12 -> 12; matrix products, arithmetic and copies ran while one was open for 0% -> 0% of each run, Pallas kernels for 6% -> 8%
where the time goes in v15:
time: 71.3 us; the launch traced here: 71.2 us
  starting transfers between devices  35.7 us (50%)
  waiting for transfers between devices  19.6 us (27%)
  Pallas kernels  13.7 us (19%)
  local copies, waits for them, and re-layouts  1.85 us (3%)
    ppermute x28, starting transfers between devices, swap(): return lax.ppermute(block, 'row', [(i, i ^ k) for i in range(devices)])  35.7 us
    ppermute x28, waiting for transfers between devices, swap(): return lax.ppermute(block, 'row', [(i, i ^ k) for i in range(devices)])  19.6 us
    pallas_call x18, Pallas kernels, run(): pl.pallas_call(kernel, out_shape=out_shape, in_specs=smem + [in_vmem()] *...  13.7 us
    unnamed x28, local copies, waits for them, and re-layouts  1.85 us
  transfers between devices with their start and end apart: 28, of which 12 were waited for; matrix products, arithmetic and copies ran while one was open for 0% of the time, Pallas kernels for 8%

profile of v15, /device:TPU:0, one launch (start us, length us, event | category | flops | bytes accessed | tf_op | source)
XLA Modules:
  0.0 71.2 jit_solution(14559290086065940106)
XLA Ops:
  0.5 3.0 %collective-permute-start = (bf16[4,1536]{1,0:T(4,128)(2,1)}, bf16[4,1536]{1,0:T(4,128)(2,1)S(1)}, u32[]{:S(2)}, u32[]{:S(2)}) collective-permute-start(bf16[4,1536]{1,0:T(4,128)(2,1)} %refs_0_.1), channel_id=1, source_target_pairs={{0,2},{1,3},{2,0},{3,1},{4,6},{5,7},{6,4},{7,5},{8,10},{9,11},{10,... | collective-permute-start | bytes 36872 | tf_op jit(solution)/shard_map/ppermute | solution.py:412
  5.4 3.2 %collective-permute-start.3 = (bf16[8,1536]{1,0:T(8,128)(2,1)S(1)}, bf16[8,1536]{1,0:T(8,128)(2,1)S(1)}, u32[]{:S(2)}, u32[]{:S(2)}) collective-permute-start(bf16[8,1536]{1,0:T(8,128)(2,1)S(1)} %get-tuple-element.41.refs_0_), channel_id=1, source_target_pairs={{0,8},{1,9},{2,10},{3,11},{4,12},{5,13},{6,14},{7,15},{8,0},{9,1},... | collective-permute-start | bytes 73736 | tf_op jit(solution)/shard_map/ppermute | solution.py:412
  8.6 1.3 %collective-permute-start.2 = (bf16[8,1536]{1,0:T(8,128)(2,1)S(1)}, bf16[8,1536]{1,0:T(8,128)(2,1)S(1)}, u32[]{:S(2)}, u32[]{:S(2)}) collective-permute-start(bf16[8,1536]{1,0:T(8,128)(2,1)S(1)} %get-tuple-element.41.refs_0_), channel_id=1, source_target_pairs={{0,12},{1,13},{2,14},{3,15},{4,8},{5,9},{6,10},{7,11},{8,4},{9,5},... | collective-permute-start | bytes 73736 | tf_op jit(solution)/shard_map/ppermute | solution.py:412
  10.4 3.8 %collective-permute-done.2.refs_2_ = bf16[8,1536]{1,0:T(8,128)(2,1)S(1)} collective-permute-done((bf16[8,1536]{1,0:T(8,128)(2,1)S(1)}, bf16[8,1536]{1,0:T(8,128)(2,1)S(1)}, u32[]{:S(2)}, u32[]{:S(2)}) %collective-permute-start.2) | collective-permute-done | bytes 24608 | tf_op jit(solution)/shard_map/ppermute | solution.py:412
  14.2 2.3 %project.1 = (bf16[2,144,128]{2,1,0:T(8,128)(2,1)S(1)}, bf16[2,144,128]{2,1,0:T(8,128)(2,1)S(1)}, bf16[2,144,128]{2,1,0:T(8,128)(2,1)S(1)}, bf16[2,144,128]{2,1,...) custom-call(bf16[8,1536]{1,0:T(8,128)(2,1)S(1)} %get-tuple-element.4, ...), custom_call_target="tpu_custom_call" | custom-call | flops 23000000512 | tf_op jit(solution)/shard_map/project/pallas_call | solution.py:37
  16.5 1.6 %collective-permute-start.6 = (bf16[4,144,128]{2,1,0:T(8,128)(2,1)S(1)}, bf16[4,144,128]{2,1,0:T(8,128)(2,1)S(1)}, u32[]{:S(2)}, u32[]{:S(2)}) collective-permute-start(bf16[4,144,128]{2,1,0:T(8,128)(2,1)S(1)} %get-tuple-element.43), channel_id=1, source_target_pairs={{0,2},{1,3},{2,0},{3,1},{4,6},{5,7},{6,4},{7,5},{8,10},{9,11},{10,... | collective-permute-start | bytes 442376 | tf_op jit(solution)/shard_map/ppermute | solution.py:412
  18.1 1.2 %collective-permute-start.7 = (bf16[2,144,128]{2,1,0:T(8,128)(2,1)S(1)}, bf16[2,144,128]{2,1,0:T(8,128)(2,1)S(1)}, u32[]{:S(2)}, u32[]{:S(2)}) collective-permute-start(bf16[2,144,128]{2,1,0:T(8,128)(2,1)S(1)} %get-tuple-element.44), channel_id=1, source_target_pairs={{0,8},{1,9},{2,10},{3,11},{4,12},{5,13},{6,14},{7,15},{8,0},{9,1},... | collective-permute-start | bytes 221192 | tf_op jit(solution)/shard_map/ppermute | solution.py:412
  19.4 1.6 %collective-permute-start.8 = (bf16[2,144,128]{2,1,0:T(8,128)(2,1)S(1)}, bf16[2,144,128]{2,1,0:T(8,128)(2,1)S(1)}, u32[]{:S(2)}, u32[]{:S(2)}) collective-permute-start(bf16[2,144,128]{2,1,0:T(8,128)(2,1)S(1)} %get-tuple-element.45), channel_id=1, source_target_pairs={{0,10},{1,11},{2,8},{3,9},{4,14},{5,15},{6,12},{7,13},{8,2},{9,3},... | collective-permute-start | bytes 221192 | tf_op jit(solution)/shard_map/ppermute | solution.py:412
  21.0 2.0 %collective-permute-start.9 = (bf16[2,144,128]{2,1,0:T(8,128)(2,1)S(1)}, bf16[2,144,128]{2,1,0:T(8,128)(2,1)S(1)}, u32[]{:S(2)}, u32[]{:S(2)}) collective-permute-start(bf16[2,144,128]{2,1,0:T(8,128)(2,1)S(1)} %get-tuple-element.46), channel_id=1, source_target_pairs={{0,12},{1,13},{2,14},{3,15},{4,8},{5,9},{6,10},{7,11},{8,4},{9,5},... | collective-permute-start | bytes 221192 | tf_op jit(solution)/shard_map/ppermute | solution.py:412
  23.0 2.8 %collective-permute-start.10 = (bf16[2,144,128]{2,1,0:T(8,128)(2,1)S(1)}, bf16[2,144,128]{2,1,0:T(8,128)(2,1)S(1)}, u32[]{:S(2)}, u32[]{:S(2)}) collective-permute-start(bf16[2,144,128]{2,1,0:T(8,128)(2,1)S(1)} %get-tuple-element.47), channel_id=1, source_target_pairs={{0,14},{1,15},{2,12},{3,13},{4,10},{5,11},{6,8},{7,9},{8,6},{9,7},... | collective-permute-start | bytes 221192 | tf_op jit(solution)/shard_map/ppermute | solution.py:412
  25.9 1.7 %flip.1.flip_ref = bf16[4,1536,512]{2,1,0:T(8,128)(2,1)S(1)} custom-call(bf16[4,576,1536]{2,1,0:T(8,128)(2,1)S(1)} %bitcast.5, bf16[4,144,128]{2,1,0:T(8,128)(2,1)S(1)} %forward.2.after_ref), custom_call_target="tpu_custom_call" | custom-call | flops 4600000000 | tf_op jit(solution)/shard_map/flip/pallas_call | solution.py:37
  28.1 2.4 %collective-permute-done.8.refs_1_ = bf16[2,144,128]{2,1,0:T(8,128)(2,1)S(1)} collective-permute-done((bf16[2,144,128]{2,1,0:T(8,128)(2,1)S(1)}, bf16[2,144,128]{2,1,0:T(8,128)(2,1)S(1)}, u32[]{:S(2)}, u32[]{:S(2)}) %collective-permute-start.8) | collective-permute-done | bytes 73760 | tf_op jit(solution)/shard_map/ppermute | solution.py:412
  30.6 1.2 %collective-permute-done.11.refs_5_ = bf16[4,144,128]{2,1,0:T(8,128)(2,1)S(1)} collective-permute-done((bf16[4,144,128]{2,1,0:T(8,128)(2,1)S(1)}, bf16[4,144,128]{2,1,0:T(8,128)(2,1)S(1)}, u32[]{:S(2)}, u32[]{:S(2)}) %collective-permute-start.11) | collective-permute-done | bytes 147488 | tf_op jit(solution)/shard_map/ppermute | solution.py:412
  31.8 3.4 %attend.1 = (bf16[2,32,512]{2,1,0:T(8,128)(2,1)S(1)}, bf16[2,32,512]{2,1,0:T(8,128)(2,1)S(1)}, bf16[2,32,512]{2,1,0:T(8,128)(2,1)S(1)}, bf16[2,32,512]{2,1,0:T(8...) custom-call(s32[4]{0:T(128)S(1)} %copy-done.5, ...), custom_call_target="tpu_custom_call" | custom-call | flops 11500000256 | tf_op jit(solution)/shard_map/attend/pallas_call | solution.py:37
  36.0 2.5 %collective-permute-start.12 = (bf16[2,32,512]{2,1,0:T(8,128)(2,1)S(1)}, bf16[2,32,512]{2,1,0:T(8,128)(2,1)S(1)}, u32[]{:S(2)}, u32[]{:S(2)}) collective-permute-start(bf16[2,32,512]{2,1,0:T(8,128)(2,1)S(1)} %get-tuple-element.49), channel_id=1, source_target_pairs={{0,8},{1,9},{2,10},{3,11},{4,12},{5,13},{6,14},{7,15},{8,0},{9,1},... | collective-permute-start | bytes 196616 | tf_op jit(solution)/shard_map/ppermute | solution.py:412
  38.5 1.1 %collective-permute-start.13 = (bf16[2,32,512]{2,1,0:T(8,128)(2,1)S(1)}, bf16[2,32,512]{2,1,0:T(8,128)(2,1)S(1)}, u32[]{:S(2)}, u32[]{:S(2)}) collective-permute-start(bf16[2,32,512]{2,1,0:T(8,128)(2,1)S(1)} %get-tuple-element.50), channel_id=1, source_target_pairs={{0,10},{1,11},{2,8},{3,9},{4,14},{5,15},{6,12},{7,13},{8,2},{9,3},... | collective-permute-start | bytes 196616 | tf_op jit(solution)/shard_map/ppermute | solution.py:412
  39.7 2.6 %collective-permute-start.14 = (bf16[2,32,512]{2,1,0:T(8,128)(2,1)S(1)}, bf16[2,32,512]{2,1,0:T(8,128)(2,1)S(1)}, u32[]{:S(2)}, u32[]{:S(2)}) collective-permute-start(bf16[2,32,512]{2,1,0:T(8,128)(2,1)S(1)} %get-tuple-element.51), channel_id=1, source_target_pairs={{0,12},{1,13},{2,14},{3,15},{4,8},{5,9},{6,10},{7,11},{8,4},{9,5},... | collective-permute-start | bytes 196616 | tf_op jit(solution)/shard_map/ppermute | solution.py:412
  42.3 1.3 %collective-permute-start.15 = (bf16[2,32,512]{2,1,0:T(8,128)(2,1)S(1)}, bf16[2,32,512]{2,1,0:T(8,128)(2,1)S(1)}, u32[]{:S(2)}, u32[]{:S(2)}) collective-permute-start(bf16[2,32,512]{2,1,0:T(8,128)(2,1)S(1)} %get-tuple-element.52), channel_id=1, source_target_pairs={{0,14},{1,15},{2,12},{3,13},{4,10},{5,11},{6,8},{7,9},{8,6},{9,7},... | collective-permute-start | bytes 196616 | tf_op jit(solution)/shard_map/ppermute | solution.py:412
  43.9 4.3 %collective-permute-done.13.refs_1_ = bf16[2,32,512]{2,1,0:T(8,128)(2,1)S(1)} collective-permute-done((bf16[2,32,512]{2,1,0:T(8,128)(2,1)S(1)}, bf16[2,32,512]{2,1,0:T(8,128)(2,1)S(1)}, u32[]{:S(2)}, u32[]{:S(2)}) %collective-permute-start.13) | collective-permute-done | bytes 65568 | tf_op jit(solution)/shard_map/ppermute | solution.py:412
  48.2 1.2 %collective-permute-done.15.refs_3_ = bf16[2,32,512]{2,1,0:T(8,128)(2,1)S(1)} collective-permute-done((bf16[2,32,512]{2,1,0:T(8,128)(2,1)S(1)}, bf16[2,32,512]{2,1,0:T(8,128)(2,1)S(1)}, u32[]{:S(2)}, u32[]{:S(2)}) %collective-permute-start.15) | collective-permute-done | bytes 65568 | tf_op jit(solution)/shard_map/ppermute | solution.py:412
  49.9 1.1 %slice-done.3 = s8[2097152]{0:T(1024)(128)(4,1)S(1)} async-done(((s8[14680064]{0:T(1024)(128)(4,1)}), s8[2097152]{0:T(1024)(128)(4,1)S(1)}, s32[]{:S(2)}) %slice-start.3) | async-done | bytes 2097176
  51.1 1.4 %terms.3.refs_2_.mine_ref = f32[32,3584]{1,0:T(8,128)S(1)} custom-call(bf16[32,1024]{1,0:T(8,128)(2,1)S(1)} %values.2.refs_0_, bf16[1024,7168]{1,0:T(8,128)(2,1)S(1)} %bitcast.2), custom_call_target="tpu_custom_call" | custom-call | flops 3449999872 | tf_op jit(solution)/shard_map/terms/pallas_call | solution.py:37
  52.8 1.4 %terms.5 = bf16[32,3584]{1,0:T(8,128)(2,1)S(1)} custom-call(bf16[32,1024]{1,0:T(8,128)(2,1)S(1)} %values.3.refs_1_.refs_0_, bf16[1024,7168]{1,0:T(8,128)(2,1)S(1)} %bitcast.2), custom_call_target="tpu_custom_call" | custom-call | flops 3449999872 | tf_op jit(solution)/shard_map/terms/pallas_call | solution.py:37
  54.1 1.4 %terms.4 = (f32[32,3584]{1,0:T(8,128)S(1)}, bf16[32,3584]{1,0:T(8,128)(2,1)S(1)}) custom-call(bf16[32,1024]{1,0:T(8,128)(2,1)S(1)} %values.2.refs_0_, bf16[32,1024]{1,0:T(8,128)(2,1)S(1)} %values.3.refs_1_.refs_0_, bf16[1024,7168]{1,0:T(8,128)(2,1)S(1)} %bitcast.2), custom_call_target="tpu_custom_call" | custom-call | flops 6899999744 | tf_op jit(solution)/shard_map/terms/pallas_call | solution.py:37
  56.2 1.6 %collective-permute-start.24 = (bf16[8,3584]{1,0:T(8,128)(2,1)S(1)}, bf16[8,3584]{1,0:T(8,128)(2,1)S(1)}, u32[]{:S(2)}, u32[]{:S(2)}) collective-permute-start(bf16[8,3584]{1,0:T(8,128)(2,1)S(1)} %get-tuple-element.65), channel_id=1, source_target_pairs={{0,2},{1,3},{2,0},{3,1},{4,6},{5,7},{6,4},{7,5},{8,10},{9,11},{10,... | collective-permute-start | bytes 172040 | tf_op jit(solution)/shard_map/ppermute | solution.py:412
  57.9 1.0 %collective-permute-start.25 = (bf16[8,3584]{1,0:T(8,128)(2,1)S(1)}, bf16[8,3584]{1,0:T(8,128)(2,1)S(1)}, u32[]{:S(2)}, u32[]{:S(2)}) collective-permute-start(bf16[8,3584]{1,0:T(8,128)(2,1)S(1)} %get-tuple-element.66), channel_id=1, source_target_pairs={{0,2},{1,3},{2,0},{3,1},{4,6},{5,7},{6,4},{7,5},{8,10},{9,11},{10,... | collective-permute-start | bytes 172040 | tf_op jit(solution)/shard_map/ppermute | solution.py:412
  59.0 1.3 %collective-permute-start.21 = (bf16[4,7168]{1,0:T(4,128)(2,1)S(1)}, bf16[4,7168]{1,0:T(4,128)(2,1)S(1)}, u32[]{:S(2)}, u32[]{:S(2)}) collective-permute-start(bf16[4,7168]{1,0:T(4,128)(2,1)S(1)} %get-tuple-element.60), channel_id=1, source_target_pairs={{0,4},{1,5},{2,6},{3,7},{4,0},{5,1},{6,2},{7,3},{8,12},{9,13},{10,... | collective-permute-start | bytes 172040 | tf_op jit(solution)/shard_map/ppermute | solution.py:412
  60.3 1.2 %collective-permute-start.22 = (bf16[4,7168]{1,0:T(4,128)(2,1)S(1)}, bf16[4,7168]{1,0:T(4,128)(2,1)S(1)}, u32[]{:S(2)}, u32[]{:S(2)}) collective-permute-start(bf16[4,7168]{1,0:T(4,128)(2,1)S(1)} %get-tuple-element.61), channel_id=1, source_target_pairs={{0,6},{1,7},{2,4},{3,5},{4,2},{5,3},{6,0},{7,1},{8,14},{9,15},{10,... | collective-permute-start | bytes 172040 | tf_op jit(solution)/shard_map/ppermute | solution.py:412
  61.5 1.0 %collective-permute-start.23 = (bf16[4,7168]{1,0:T(4,128)(2,1)S(1)}, bf16[4,7168]{1,0:T(4,128)(2,1)S(1)}, u32[]{:S(2)}, u32[]{:S(2)}) collective-permute-start(bf16[4,7168]{1,0:T(4,128)(2,1)S(1)} %get-tuple-element.62), channel_id=1, source_target_pairs={{0,2},{1,3},{2,0},{3,1},{4,6},{5,7},{6,4},{7,5},{8,10},{9,11},{10,... | collective-permute-start | bytes 172040 | tf_op jit(solution)/shard_map/ppermute | solution.py:412
  62.5 2.2 %collective-permute-start.26 = (bf16[4,7168]{1,0:T(4,128)(2,1)S(1)}, bf16[4,7168]{1,0:T(4,128)(2,1)S(1)}, u32[]{:S(2)}, u32[]{:S(2)}) collective-permute-start(bf16[4,7168]{1,0:T(4,128)(2,1)S(1)} %get-tuple-element.67), channel_id=1, source_target_pairs={{0,12},{1,13},{2,14},{3,15},{4,8},{5,9},{6,10},{7,11},{8,4},{9,5},... | collective-permute-start | bytes 172040 | tf_op jit(solution)/shard_map/ppermute | solution.py:412
  66.0 2.7 %collective-permute-done.26.refs_4_ = bf16[4,7168]{1,0:T(4,128)(2,1)S(1)} collective-permute-done((bf16[4,7168]{1,0:T(4,128)(2,1)S(1)}, bf16[4,7168]{1,0:T(4,128)(2,1)S(1)}, u32[]{:S(2)}, u32[]{:S(2)}) %collective-permute-start.26) | collective-permute-done | bytes 57376 | tf_op jit(solution)/shard_map/ppermute | solution.py:412
  68.6 1.9 %collective-permute-done.27.refs_5_ = bf16[4,7168]{1,0:T(4,128)(2,1)S(1)} collective-permute-done((bf16[4,7168]{1,0:T(4,128)(2,1)S(1)}, bf16[4,7168]{1,0:T(4,128)(2,1)S(1)}, u32[]{:S(2)}, u32[]{:S(2)}) %collective-permute-start.27) | collective-permute-done | bytes 57376 | tf_op jit(solution)/shard_map/ppermute | solution.py:412
  (73 shorter events, 7.9 us)
Async XLA Ops:
  0.0 14.2 %collective-permute-start.4 = (bf16[1536,1536]{1,0:T(8,128)(2,1)}, bf16[1536,1536]{1,0:T(8,128)(2,1)S(1)}, u32[]{:S(2)}, u32[]{:S(2)}) collective-permute-start(bf16[1536,1536]{1,0:T(8,128)(2,1)} %refs_4_.1), channel_id=1, source_target_pairs={{0,1},{1,0},{2,3},{3,2},{4,5},{5,4},{6,7},{7,6},{8,9},{9,8},{10,11... | collective-permute-start | bytes 14155784 | tf_op jit(solution)/shard_map/ppermute | solution.py:412
  0.5 13.7 %collective-permute-start.5 = (bf16[8,128,512]{2,1,0:T(8,128)(2,1)}, bf16[8,128,512]{2,1,0:T(8,128)(2,1)S(1)}, u32[]{:S(2)}, u32[]{:S(2)}) collective-permute-start(bf16[8,128,512]{2,1,0:T(8,128)(2,1)} %refs_5_.1), channel_id=1, source_target_pairs={{0,1},{1,0},{2,3},{3,2},{4,5},{5,4},{6,7},{7,6},{8,9},{9,8},{10,11... | collective-permute-start | bytes 3145736 | tf_op jit(solution)/shard_map/ppermute | solution.py:412
  0.5 4.8 %collective-permute-start = (bf16[4,1536]{1,0:T(4,128)(2,1)}, bf16[4,1536]{1,0:T(4,128)(2,1)S(1)}, u32[]{:S(2)}, u32[]{:S(2)}) collective-permute-start(bf16[4,1536]{1,0:T(4,128)(2,1)} %refs_0_.1), channel_id=1, source_target_pairs={{0,2},{1,3},{2,0},{3,1},{4,6},{5,7},{6,4},{7,5},{8,10},{9,11},{10,... | collective-permute-start | bytes 36872 | tf_op jit(solution)/shard_map/ppermute | solution.py:412
  4.1 10.1 %slice-start.6 = ((s8[4718592]{0:T(1024)(128)(4,1)}), s8[4194304]{0:T(1024)(128)(4,1)S(1)}, s32[]{:S(2)}) async-start(s8[4718592]{0:T(1024)(128)(4,1)} %bitcast.7), calls=%async_computation.6 | async-start | bytes 8388608
  5.4 8.9 %copy-start = (bf16[8,128,512]{2,1,0:T(8,128)(2,1)S(1)}, bf16[8,128,512]{2,1,0:T(8,128)(2,1)}, u32[]{:S(2)}) copy-start(bf16[8,128,512]{2,1,0:T(8,128)(2,1)} %refs_5_.1) | copy-start | bytes 3145732
  5.4 20.5 %slice-start.4 = ((s8[7077888]{0:T(1024)(128)(4,1)}), s8[4194304]{0:T(1024)(128)(4,1)S(1)}, s32[]{:S(2)}) async-start(s8[7077888]{0:T(1024)(128)(4,1)} %bitcast.3), calls=%async_computation.4 | async-start | bytes 8388608
  5.4 20.5 %slice-start.5 = ((s8[7077888]{0:T(1024)(128)(4,1)}), s8[2883584]{0:T(1024)(128)(4,1)S(1)}, s32[]{:S(2)}) async-start(s8[7077888]{0:T(1024)(128)(4,1)} %bitcast.3), calls=%async_computation.5 | async-start | bytes 5767168
  5.4 5.0 %collective-permute-start.3 = (bf16[8,1536]{1,0:T(8,128)(2,1)S(1)}, bf16[8,1536]{1,0:T(8,128)(2,1)S(1)}, u32[]{:S(2)}, u32[]{:S(2)}) collective-permute-start(bf16[8,1536]{1,0:T(8,128)(2,1)S(1)} %get-tuple-element.41.refs_0_), channel_id=1, source_target_pairs={{0,8},{1,9},{2,10},{3,11},{4,12},{5,13},{6,14},{7,15},{8,0},{9,1},... | collective-permute-start | bytes 73736 | tf_op jit(solution)/shard_map/ppermute | solution.py:412
  8.6 5.6 %collective-permute-start.2 = (bf16[8,1536]{1,0:T(8,128)(2,1)S(1)}, bf16[8,1536]{1,0:T(8,128)(2,1)S(1)}, u32[]{:S(2)}, u32[]{:S(2)}) collective-permute-start(bf16[8,1536]{1,0:T(8,128)(2,1)S(1)} %get-tuple-element.41.refs_0_), channel_id=1, source_target_pairs={{0,12},{1,13},{2,14},{3,15},{4,8},{5,9},{6,10},{7,11},{8,4},{9,5},... | collective-permute-start | bytes 73736 | tf_op jit(solution)/shard_map/ppermute | solution.py:412
  9.9 4.3 %collective-permute-start.1 = (bf16[8,1536]{1,0:T(8,128)(2,1)S(1)}, bf16[8,1536]{1,0:T(8,128)(2,1)S(1)}, u32[]{:S(2)}, u32[]{:S(2)}) collective-permute-start(bf16[8,1536]{1,0:T(8,128)(2,1)S(1)} %get-tuple-element.41.refs_0_), channel_id=1, source_target_pairs={{0,4},{1,5},{2,6},{3,7},{4,0},{5,1},{6,2},{7,3},{8,12},{9,13},{10,... | collective-permute-start | bytes 73736 | tf_op jit(solution)/shard_map/ppermute | solution.py:412
  16.5 9.2 %collective-permute-start.6 = (bf16[4,144,128]{2,1,0:T(8,128)(2,1)S(1)}, bf16[4,144,128]{2,1,0:T(8,128)(2,1)S(1)}, u32[]{:S(2)}, u32[]{:S(2)}) collective-permute-start(bf16[4,144,128]{2,1,0:T(8,128)(2,1)S(1)} %get-tuple-element.43), channel_id=1, source_target_pairs={{0,2},{1,3},{2,0},{3,1},{4,6},{5,7},{6,4},{7,5},{8,10},{9,11},{10,... | collective-permute-start | bytes 442376 | tf_op jit(solution)/shard_map/ppermute | solution.py:412
  18.1 10.0 %collective-permute-start.7 = (bf16[2,144,128]{2,1,0:T(8,128)(2,1)S(1)}, bf16[2,144,128]{2,1,0:T(8,128)(2,1)S(1)}, u32[]{:S(2)}, u32[]{:S(2)}) collective-permute-start(bf16[2,144,128]{2,1,0:T(8,128)(2,1)S(1)} %get-tuple-element.44), channel_id=1, source_target_pairs={{0,8},{1,9},{2,10},{3,11},{4,12},{5,13},{6,14},{7,15},{8,0},{9,1},... | collective-permute-start | bytes 221192 | tf_op jit(solution)/shard_map/ppermute | solution.py:412
  19.4 11.2 %collective-permute-start.8 = (bf16[2,144,128]{2,1,0:T(8,128)(2,1)S(1)}, bf16[2,144,128]{2,1,0:T(8,128)(2,1)S(1)}, u32[]{:S(2)}, u32[]{:S(2)}) collective-permute-start(bf16[2,144,128]{2,1,0:T(8,128)(2,1)S(1)} %get-tuple-element.45), channel_id=1, source_target_pairs={{0,10},{1,11},{2,8},{3,9},{4,14},{5,15},{6,12},{7,13},{8,2},{9,3},... | collective-permute-start | bytes 221192 | tf_op jit(solution)/shard_map/ppermute | solution.py:412
  21.0 9.6 %collective-permute-start.9 = (bf16[2,144,128]{2,1,0:T(8,128)(2,1)S(1)}, bf16[2,144,128]{2,1,0:T(8,128)(2,1)S(1)}, u32[]{:S(2)}, u32[]{:S(2)}) collective-permute-start(bf16[2,144,128]{2,1,0:T(8,128)(2,1)S(1)} %get-tuple-element.46), channel_id=1, source_target_pairs={{0,12},{1,13},{2,14},{3,15},{4,8},{5,9},{6,10},{7,11},{8,4},{9,5},... | collective-permute-start | bytes 221192 | tf_op jit(solution)/shard_map/ppermute | solution.py:412
  23.0 7.6 %collective-permute-start.10 = (bf16[2,144,128]{2,1,0:T(8,128)(2,1)S(1)}, bf16[2,144,128]{2,1,0:T(8,128)(2,1)S(1)}, u32[]{:S(2)}, u32[]{:S(2)}) collective-permute-start(bf16[2,144,128]{2,1,0:T(8,128)(2,1)S(1)} %get-tuple-element.47), channel_id=1, source_target_pairs={{0,14},{1,15},{2,12},{3,13},{4,10},{5,11},{6,8},{7,9},{8,6},{9,7},... | collective-permute-start | bytes 221192 | tf_op jit(solution)/shard_map/ppermute | solution.py:412
  25.8 6.0 %collective-permute-start.11 = (bf16[4,144,128]{2,1,0:T(8,128)(2,1)S(1)}, bf16[4,144,128]{2,1,0:T(8,128)(2,1)S(1)}, u32[]{:S(2)}, u32[]{:S(2)}) collective-permute-start(bf16[4,144,128]{2,1,0:T(8,128)(2,1)S(1)} %forward.2.after_ref), channel_id=1, source_target_pairs={{0,4},{1,5},{2,6},{3,7},{4,0},{5,1},{6,2},{7,3},{8,12},{9,13},{10,... | collective-permute-start | bytes 442376 | tf_op jit(solution)/shard_map/ppermute | solution.py:412
  35.2 8.4 %collective-permute-start.16 = (bf16[4,32,512]{2,1,0:T(8,128)(2,1)S(1)}, bf16[4,32,512]{2,1,0:T(8,128)(2,1)S(1)}, u32[]{:S(2)}, u32[]{:S(2)}) collective-permute-start(bf16[4,32,512]{2,1,0:T(8,128)(2,1)S(1)} %get-tuple-element.53), channel_id=1, source_target_pairs={{0,2},{1,3},{2,0},{3,1},{4,6},{5,7},{6,4},{7,5},{8,10},{9,11},{10,... | collective-permute-start | bytes 393224 | tf_op jit(solution)/shard_map/ppermute | solution.py:412
  36.0 7.9 %collective-permute-start.12 = (bf16[2,32,512]{2,1,0:T(8,128)(2,1)S(1)}, bf16[2,32,512]{2,1,0:T(8,128)(2,1)S(1)}, u32[]{:S(2)}, u32[]{:S(2)}) collective-permute-start(bf16[2,32,512]{2,1,0:T(8,128)(2,1)S(1)} %get-tuple-element.49), channel_id=1, source_target_pairs={{0,8},{1,9},{2,10},{3,11},{4,12},{5,13},{6,14},{7,15},{8,0},{9,1},... | collective-permute-start | bytes 196616 | tf_op jit(solution)/shard_map/ppermute | solution.py:412
  38.5 9.7 %collective-permute-start.13 = (bf16[2,32,512]{2,1,0:T(8,128)(2,1)S(1)}, bf16[2,32,512]{2,1,0:T(8,128)(2,1)S(1)}, u32[]{:S(2)}, u32[]{:S(2)}) collective-permute-start(bf16[2,32,512]{2,1,0:T(8,128)(2,1)S(1)} %get-tuple-element.50), channel_id=1, source_target_pairs={{0,10},{1,11},{2,8},{3,9},{4,14},{5,15},{6,12},{7,13},{8,2},{9,3},... | collective-permute-start | bytes 196616 | tf_op jit(solution)/shard_map/ppermute | solution.py:412
  39.7 8.6 %collective-permute-start.14 = (bf16[2,32,512]{2,1,0:T(8,128)(2,1)S(1)}, bf16[2,32,512]{2,1,0:T(8,128)(2,1)S(1)}, u32[]{:S(2)}, u32[]{:S(2)}) collective-permute-start(bf16[2,32,512]{2,1,0:T(8,128)(2,1)S(1)} %get-tuple-element.51), channel_id=1, source_target_pairs={{0,12},{1,13},{2,14},{3,15},{4,8},{5,9},{6,10},{7,11},{8,4},{9,5},... | collective-permute-start | bytes 196616 | tf_op jit(solution)/shard_map/ppermute | solution.py:412
  42.3 7.1 %collective-permute-start.15 = (bf16[2,32,512]{2,1,0:T(8,128)(2,1)S(1)}, bf16[2,32,512]{2,1,0:T(8,128)(2,1)S(1)}, u32[]{:S(2)}, u32[]{:S(2)}) collective-permute-start(bf16[2,32,512]{2,1,0:T(8,128)(2,1)S(1)} %get-tuple-element.52), channel_id=1, source_target_pairs={{0,14},{1,15},{2,12},{3,13},{4,10},{5,11},{6,8},{7,9},{8,6},{9,7},... | collective-permute-start | bytes 196616 | tf_op jit(solution)/shard_map/ppermute | solution.py:412
  43.7 5.8 %collective-permute-start.17 = (bf16[4,32,512]{2,1,0:T(8,128)(2,1)S(1)}, bf16[4,32,512]{2,1,0:T(8,128)(2,1)S(1)}, u32[]{:S(2)}, u32[]{:S(2)}) collective-permute-start(bf16[4,32,512]{2,1,0:T(8,128)(2,1)S(1)} %forward.3.after_ref), channel_id=1, source_target_pairs={{0,4},{1,5},{2,6},{3,7},{4,0},{5,1},{6,2},{7,3},{8,12},{9,13},{10,... | collective-permute-start | bytes 393224 | tf_op jit(solution)/shard_map/ppermute | solution.py:412
  49.5 2.9 %collective-permute-start.18 = (bf16[8,32,512]{2,1,0:T(8,128)(2,1)S(1)}, bf16[8,32,512]{2,1,0:T(8,128)(2,1)S(1)}, u32[]{:S(2)}, u32[]{:S(2)}) collective-permute-start(bf16[8,32,512]{2,1,0:T(8,128)(2,1)S(1)} %regroup.1), channel_id=1, source_target_pairs={{0,1},{1,0},{2,3},{3,2},{4,5},{5,4},{6,7},{7,6},{8,9},{9,8},{10,11... | collective-permute-start | bytes 786440 | tf_op jit(solution)/shard_map/ppermute | solution.py:412
  54.1 2.0 %collective-permute-start.20 = (bf16[32,3584]{1,0:T(8,128)(2,1)S(1)}, bf16[32,3584]{1,0:T(8,128)(2,1)S(1)}, u32[]{:S(2)}, u32[]{:S(2)}) collective-permute-start(bf16[32,3584]{1,0:T(8,128)(2,1)S(1)} %terms.5), channel_id=1, source_target_pairs={{0,1},{1,0},{2,3},{3,2},{4,5},{5,4},{6,7},{7,6},{8,9},{9,8},{10,11... | collective-permute-start | bytes 688136 | tf_op jit(solution)/shard_map/ppermute | solution.py:412
  55.5 2.3 %collective-permute-start.19 = (bf16[32,3584]{1,0:T(8,128)(2,1)S(1)}, bf16[32,3584]{1,0:T(8,128)(2,1)S(1)}, u32[]{:S(2)}, u32[]{:S(2)}) collective-permute-start(bf16[32,3584]{1,0:T(8,128)(2,1)S(1)} %get-tuple-element.57), channel_id=1, source_target_pairs={{0,1},{1,0},{2,3},{3,2},{4,5},{5,4},{6,7},{7,6},{8,9},{9,8},{10,11... | collective-permute-start | bytes 688136 | tf_op jit(solution)/shard_map/ppermute | solution.py:412
  56.2 6.3 %collective-permute-start.24 = (bf16[8,3584]{1,0:T(8,128)(2,1)S(1)}, bf16[8,3584]{1,0:T(8,128)(2,1)S(1)}, u32[]{:S(2)}, u32[]{:S(2)}) collective-permute-start(bf16[8,3584]{1,0:T(8,128)(2,1)S(1)} %get-tuple-element.65), channel_id=1, source_target_pairs={{0,2},{1,3},{2,0},{3,1},{4,6},{5,7},{6,4},{7,5},{8,10},{9,11},{10,... | collective-permute-start | bytes 172040 | tf_op jit(solution)/shard_map/ppermute | solution.py:412
  57.9 4.5 %collective-permute-start.25 = (bf16[8,3584]{1,0:T(8,128)(2,1)S(1)}, bf16[8,3584]{1,0:T(8,128)(2,1)S(1)}, u32[]{:S(2)}, u32[]{:S(2)}) collective-permute-start(bf16[8,3584]{1,0:T(8,128)(2,1)S(1)} %get-tuple-element.66), channel_id=1, source_target_pairs={{0,2},{1,3},{2,0},{3,1},{4,6},{5,7},{6,4},{7,5},{8,10},{9,11},{10,... | collective-permute-start | bytes 172040 | tf_op jit(solution)/shard_map/ppermute | solution.py:412
  59.0 6.4 %collective-permute-start.21 = (bf16[4,7168]{1,0:T(4,128)(2,1)S(1)}, bf16[4,7168]{1,0:T(4,128)(2,1)S(1)}, u32[]{:S(2)}, u32[]{:S(2)}) collective-permute-start(bf16[4,7168]{1,0:T(4,128)(2,1)S(1)} %get-tuple-element.60), channel_id=1, source_target_pairs={{0,4},{1,5},{2,6},{3,7},{4,0},{5,1},{6,2},{7,3},{8,12},{9,13},{10,... | collective-permute-start | bytes 172040 | tf_op jit(solution)/shard_map/ppermute | solution.py:412
  60.3 5.1 %collective-permute-start.22 = (bf16[4,7168]{1,0:T(4,128)(2,1)S(1)}, bf16[4,7168]{1,0:T(4,128)(2,1)S(1)}, u32[]{:S(2)}, u32[]{:S(2)}) collective-permute-start(bf16[4,7168]{1,0:T(4,128)(2,1)S(1)} %get-tuple-element.61), channel_id=1, source_target_pairs={{0,6},{1,7},{2,4},{3,5},{4,2},{5,3},{6,0},{7,1},{8,14},{9,15},{10,... | collective-permute-start | bytes 172040 | tf_op jit(solution)/shard_map/ppermute | solution.py:412
  61.5 4.5 %collective-permute-start.23 = (bf16[4,7168]{1,0:T(4,128)(2,1)S(1)}, bf16[4,7168]{1,0:T(4,128)(2,1)S(1)}, u32[]{:S(2)}, u32[]{:S(2)}) collective-permute-start(bf16[4,7168]{1,0:T(4,128)(2,1)S(1)} %get-tuple-element.62), channel_id=1, source_target_pairs={{0,2},{1,3},{2,0},{3,1},{4,6},{5,7},{6,4},{7,5},{8,10},{9,11},{10,... | collective-permute-start | bytes 172040 | tf_op jit(solution)/shard_map/ppermute | solution.py:412
  62.5 6.1 %collective-permute-start.26 = (bf16[4,7168]{1,0:T(4,128)(2,1)S(1)}, bf16[4,7168]{1,0:T(4,128)(2,1)S(1)}, u32[]{:S(2)}, u32[]{:S(2)}) collective-permute-start(bf16[4,7168]{1,0:T(4,128)(2,1)S(1)} %get-tuple-element.67), channel_id=1, source_target_pairs={{0,12},{1,13},{2,14},{3,15},{4,8},{5,9},{6,10},{7,11},{8,4},{9,5},... | collective-permute-start | bytes 172040 | tf_op jit(solution)/shard_map/ppermute | solution.py:412
  64.7 5.8 %collective-permute-start.27 = (bf16[4,7168]{1,0:T(4,128)(2,1)S(1)}, bf16[4,7168]{1,0:T(4,128)(2,1)S(1)}, u32[]{:S(2)}, u32[]{:S(2)}) collective-permute-start(bf16[4,7168]{1,0:T(4,128)(2,1)S(1)} %get-tuple-element.68), channel_id=1, source_target_pairs={{0,8},{1,9},{2,10},{3,11},{4,12},{5,13},{6,14},{7,15},{8,0},{9,1},... | collective-permute-start | bytes 172040 | tf_op jit(solution)/shard_map/ppermute | solution.py:412
  (10 other events, 52.5 us)

commit v16 on v13

--- a/solution.py
+++ b/solution.py
@@ -59,8 +59,7 @@
 
 
 def far_chips(devices):
-    chips = [k for k in far_first(devices, 2) if k > Y + Z1]
-    return chips[:1] + chips[:0:-1]
+    return [k for k in far_first(devices, 2) if k > Y + Z1]
 
 
 def chip_order(devices):
@@ -93,6 +92,14 @@
 def rotary(lengths):
     table = shape(lengths.shape[0], ROPE, dtype=jnp.float32)
     return call(rotary_kernel, (table, table), 3, "rotary", scalars=1)(lengths)
+
+
+def stage_kernel(in_ref, out_ref):
+    out_ref[...] = in_ref[...]
+
+
+def stage(block):
+    return call(stage_kernel, shape(*block.shape), 1, "stage")(block)
 
 
 def join_kernel(cos_ref, sin_ref, *refs):
@@ -413,9 +420,10 @@
             return block
         return lax.ppermute(block, "row", [(i, i ^ k) for i in range(devices)])
 
-    across = swap(q_latent, Y)
+    own_rows = stage(q_latent)
+    across = swap(own_rows, Y)
     far_weights = [swap(w_uq, 1), swap(w_uk, 1)]
-    tables, near = join(rotary(lengths), [q_latent, across])
+    tables, near = join(rotary(lengths), [own_rows, across])
     def exchange(messages):
         *far, across, pair, own = messages
         early = len(far) // 2

time: 70.1 us -> 70.5 us (level)
  waiting for transfers between devices: 22.6 us -> 21.4 us
  starting transfers between devices: 34.2 us -> 35 us
  local copies, waits for them, and re-layouts: 0.72 us -> 1.43 us
    ppermute x28, waiting for transfers between devices: 22.6 us -> 21.4 us  [swap(): return lax.ppermute(block, 'row', [(i, i ^ k) for i in range(devices)])]
    ppermute x28, starting transfers between devices: 34.2 us -> 35 us  [swap(): return lax.ppermute(block, 'row', [(i, i ^ k) for i in range(devices)])]
    unnamed x28, local copies, waits for them, and re-layouts: 0.72 us -> 1.43 us
    pallas_call x16 -> x17, Pallas kernels: 12.2 us -> 12.1 us  [run(): pl.pallas_call(kernel, out_shape=out_shape, in_specs=smem + [in_vmem()] *...]
  transfers between devices with their start and end apart: 28 -> 28, of which waited for: 12 -> 13; matrix products, arithmetic and copies ran while one was open for 0% -> 0% of each run, Pallas kernels for 6% -> 6%
where the time goes in v16:
time: 70.5 us; the launch traced here: 70.3 us
  starting transfers between devices  35 us (50%)
  waiting for transfers between devices  21.4 us (30%)
  Pallas kernels  12.1 us (17%)
  local copies, waits for them, and re-layouts  1.43 us (2%)
    ppermute x28, starting transfers between devices, swap(): return lax.ppermute(block, 'row', [(i, i ^ k) for i in range(devices)])  35 us
    ppermute x28, waiting for transfers between devices, swap(): return lax.ppermute(block, 'row', [(i, i ^ k) for i in range(devices)])  21.4 us
    pallas_call x17, Pallas kernels, run(): pl.pallas_call(kernel, out_shape=out_shape, in_specs=smem + [in_vmem()] *...  12.1 us
    unnamed x28, local copies, waits for them, and re-layouts  1.43 us
  transfers between devices with their start and end apart: 28, of which 13 were waited for; matrix products, arithmetic and copies ran while one was open for 0% of the time, Pallas kernels for 6%

profile of v16, /device:TPU:0, one launch (start us, length us, event | category | flops | bytes accessed | tf_op | source)
XLA Modules:
  0.0 70.3 jit_solution(1952745962447002700)
XLA Ops:
  1.2 3.0 %collective-permute-start = (bf16[4,1536]{1,0:T(4,128)(2,1)S(1)}, bf16[4,1536]{1,0:T(4,128)(2,1)S(1)}, u32[]{:S(2)}, u32[]{:S(2)}) collective-permute-start(bf16[4,1536]{1,0:T(4,128)(2,1)S(1)} %stage.1.refs_0_), channel_id=1, source_target_pairs={{0,2},{1,3},{2,0},{3,1},{4,6},{5,7},{6,4},{7,5},{8,10},{9,11},{10,... | collective-permute-start | bytes 36872 | tf_op jit(solution)/shard_map/ppermute | solution.py:421
  5.9 3.2 %collective-permute-start.3 = (bf16[8,1536]{1,0:T(8,128)(2,1)S(1)}, bf16[8,1536]{1,0:T(8,128)(2,1)S(1)}, u32[]{:S(2)}, u32[]{:S(2)}) collective-permute-start(bf16[8,1536]{1,0:T(8,128)(2,1)S(1)} %get-tuple-element.43.refs_0_), channel_id=1, source_target_pairs={{0,8},{1,9},{2,10},{3,11},{4,12},{5,13},{6,14},{7,15},{8,0},{9,1},... | collective-permute-start | bytes 73736 | tf_op jit(solution)/shard_map/ppermute | solution.py:421
  9.1 1.3 %collective-permute-start.2 = (bf16[8,1536]{1,0:T(8,128)(2,1)S(1)}, bf16[8,1536]{1,0:T(8,128)(2,1)S(1)}, u32[]{:S(2)}, u32[]{:S(2)}) collective-permute-start(bf16[8,1536]{1,0:T(8,128)(2,1)S(1)} %get-tuple-element.43.refs_0_), channel_id=1, source_target_pairs={{0,12},{1,13},{2,14},{3,15},{4,8},{5,9},{6,10},{7,11},{8,4},{9,5},... | collective-permute-start | bytes 73736 | tf_op jit(solution)/shard_map/ppermute | solution.py:421
  10.9 3.8 %collective-permute-done.2.refs_2_ = bf16[8,1536]{1,0:T(8,128)(2,1)S(1)} collective-permute-done((bf16[8,1536]{1,0:T(8,128)(2,1)S(1)}, bf16[8,1536]{1,0:T(8,128)(2,1)S(1)}, u32[]{:S(2)}, u32[]{:S(2)}) %collective-permute-start.2) | collective-permute-done | bytes 24608 | tf_op jit(solution)/shard_map/ppermute | solution.py:421
  14.7 2.3 %project.1 = (bf16[2,144,128]{2,1,0:T(8,128)(2,1)S(1)}, bf16[2,144,128]{2,1,0:T(8,128)(2,1)S(1)}, bf16[2,144,128]{2,1,0:T(8,128)(2,1)S(1)}, bf16[2,144,128]{2,1,...) custom-call(bf16[8,1536]{1,0:T(8,128)(2,1)S(1)} %get-tuple-element.4, ...), custom_call_target="tpu_custom_call" | custom-call | flops 23000000512 | tf_op jit(solution)/shard_map/project/pallas_call | solution.py:37
  17.0 1.6 %collective-permute-start.6 = (bf16[4,144,128]{2,1,0:T(8,128)(2,1)S(1)}, bf16[4,144,128]{2,1,0:T(8,128)(2,1)S(1)}, u32[]{:S(2)}, u32[]{:S(2)}) collective-permute-start(bf16[4,144,128]{2,1,0:T(8,128)(2,1)S(1)} %get-tuple-element.45), channel_id=1, source_target_pairs={{0,2},{1,3},{2,0},{3,1},{4,6},{5,7},{6,4},{7,5},{8,10},{9,11},{10,... | collective-permute-start | bytes 442376 | tf_op jit(solution)/shard_map/ppermute | solution.py:421
  18.6 1.2 %collective-permute-start.7 = (bf16[2,144,128]{2,1,0:T(8,128)(2,1)S(1)}, bf16[2,144,128]{2,1,0:T(8,128)(2,1)S(1)}, u32[]{:S(2)}, u32[]{:S(2)}) collective-permute-start(bf16[2,144,128]{2,1,0:T(8,128)(2,1)S(1)} %get-tuple-element.46), channel_id=1, source_target_pairs={{0,8},{1,9},{2,10},{3,11},{4,12},{5,13},{6,14},{7,15},{8,0},{9,1},... | collective-permute-start | bytes 221192 | tf_op jit(solution)/shard_map/ppermute | solution.py:421
  19.8 1.6 %collective-permute-start.8 = (bf16[2,144,128]{2,1,0:T(8,128)(2,1)S(1)}, bf16[2,144,128]{2,1,0:T(8,128)(2,1)S(1)}, u32[]{:S(2)}, u32[]{:S(2)}) collective-permute-start(bf16[2,144,128]{2,1,0:T(8,128)(2,1)S(1)} %get-tuple-element.47), channel_id=1, source_target_pairs={{0,10},{1,11},{2,8},{3,9},{4,14},{5,15},{6,12},{7,13},{8,2},{9,3},... | collective-permute-start | bytes 221192 | tf_op jit(solution)/shard_map/ppermute | solution.py:421
  21.5 2.0 %collective-permute-start.9 = (bf16[2,144,128]{2,1,0:T(8,128)(2,1)S(1)}, bf16[2,144,128]{2,1,0:T(8,128)(2,1)S(1)}, u32[]{:S(2)}, u32[]{:S(2)}) collective-permute-start(bf16[2,144,128]{2,1,0:T(8,128)(2,1)S(1)} %get-tuple-element.48), channel_id=1, source_target_pairs={{0,12},{1,13},{2,14},{3,15},{4,8},{5,9},{6,10},{7,11},{8,4},{9,5},... | collective-permute-start | bytes 221192 | tf_op jit(solution)/shard_map/ppermute | solution.py:421
  23.5 2.8 %collective-permute-start.10 = (bf16[2,144,128]{2,1,0:T(8,128)(2,1)S(1)}, bf16[2,144,128]{2,1,0:T(8,128)(2,1)S(1)}, u32[]{:S(2)}, u32[]{:S(2)}) collective-permute-start(bf16[2,144,128]{2,1,0:T(8,128)(2,1)S(1)} %get-tuple-element.49), channel_id=1, source_target_pairs={{0,14},{1,15},{2,12},{3,13},{4,10},{5,11},{6,8},{7,9},{8,6},{9,7},... | collective-permute-start | bytes 221192 | tf_op jit(solution)/shard_map/ppermute | solution.py:421
  26.4 1.7 %flip.1.flip_ref = bf16[4,1536,512]{2,1,0:T(8,128)(2,1)S(1)} custom-call(bf16[4,576,1536]{2,1,0:T(8,128)(2,1)S(1)} %bitcast.5, bf16[4,144,128]{2,1,0:T(8,128)(2,1)S(1)} %forward.2.after_ref), custom_call_target="tpu_custom_call" | custom-call | flops 4600000000 | tf_op jit(solution)/shard_map/flip/pallas_call | solution.py:37
  28.1 2.9 %collective-permute-done.8.refs_1_ = bf16[2,144,128]{2,1,0:T(8,128)(2,1)S(1)} collective-permute-done((bf16[2,144,128]{2,1,0:T(8,128)(2,1)S(1)}, bf16[2,144,128]{2,1,0:T(8,128)(2,1)S(1)}, u32[]{:S(2)}, u32[]{:S(2)}) %collective-permute-start.8) | collective-permute-done | bytes 73760 | tf_op jit(solution)/shard_map/ppermute | solution.py:421
  31.0 1.2 %collective-permute-done.11.refs_5_ = bf16[4,144,128]{2,1,0:T(8,128)(2,1)S(1)} collective-permute-done((bf16[4,144,128]{2,1,0:T(8,128)(2,1)S(1)}, bf16[4,144,128]{2,1,0:T(8,128)(2,1)S(1)}, u32[]{:S(2)}, u32[]{:S(2)}) %collective-permute-start.11) | collective-permute-done | bytes 147488 | tf_op jit(solution)/shard_map/ppermute | solution.py:421
  32.3 3.4 %attend.1 = (bf16[2,32,512]{2,1,0:T(8,128)(2,1)S(1)}, bf16[2,32,512]{2,1,0:T(8,128)(2,1)S(1)}, bf16[2,32,512]{2,1,0:T(8,128)(2,1)S(1)}, bf16[2,32,512]{2,1,0:T(8...) custom-call(s32[4]{0:T(128)S(1)} %copy-done.5, ...), custom_call_target="tpu_custom_call" | custom-call | flops 11500000256 | tf_op jit(solution)/shard_map/attend/pallas_call | solution.py:37
  36.5 2.0 %collective-permute-start.12 = (bf16[2,32,512]{2,1,0:T(8,128)(2,1)S(1)}, bf16[2,32,512]{2,1,0:T(8,128)(2,1)S(1)}, u32[]{:S(2)}, u32[]{:S(2)}) collective-permute-start(bf16[2,32,512]{2,1,0:T(8,128)(2,1)S(1)} %get-tuple-element.51), channel_id=1, source_target_pairs={{0,8},{1,9},{2,10},{3,11},{4,12},{5,13},{6,14},{7,15},{8,0},{9,1},... | collective-permute-start | bytes 196616 | tf_op jit(solution)/shard_map/ppermute | solution.py:421
  38.5 1.6 %collective-permute-start.13 = (bf16[2,32,512]{2,1,0:T(8,128)(2,1)S(1)}, bf16[2,32,512]{2,1,0:T(8,128)(2,1)S(1)}, u32[]{:S(2)}, u32[]{:S(2)}) collective-permute-start(bf16[2,32,512]{2,1,0:T(8,128)(2,1)S(1)} %get-tuple-element.52), channel_id=1, source_target_pairs={{0,10},{1,11},{2,8},{3,9},{4,14},{5,15},{6,12},{7,13},{8,2},{9,3},... | collective-permute-start | bytes 196616 | tf_op jit(solution)/shard_map/ppermute | solution.py:421
  40.2 2.2 %collective-permute-start.14 = (bf16[2,32,512]{2,1,0:T(8,128)(2,1)S(1)}, bf16[2,32,512]{2,1,0:T(8,128)(2,1)S(1)}, u32[]{:S(2)}, u32[]{:S(2)}) collective-permute-start(bf16[2,32,512]{2,1,0:T(8,128)(2,1)S(1)} %get-tuple-element.53), channel_id=1, source_target_pairs={{0,12},{1,13},{2,14},{3,15},{4,8},{5,9},{6,10},{7,11},{8,4},{9,5},... | collective-permute-start | bytes 196616 | tf_op jit(solution)/shard_map/ppermute | solution.py:421
  42.3 1.8 %collective-permute-start.15 = (bf16[2,32,512]{2,1,0:T(8,128)(2,1)S(1)}, bf16[2,32,512]{2,1,0:T(8,128)(2,1)S(1)}, u32[]{:S(2)}, u32[]{:S(2)}) collective-permute-start(bf16[2,32,512]{2,1,0:T(8,128)(2,1)S(1)} %get-tuple-element.54), channel_id=1, source_target_pairs={{0,14},{1,15},{2,12},{3,13},{4,10},{5,11},{6,8},{7,9},{8,6},{9,7},... | collective-permute-start | bytes 196616 | tf_op jit(solution)/shard_map/ppermute | solution.py:421
  44.3 1.4 %collective-permute-done.12.refs_0_ = bf16[2,32,512]{2,1,0:T(8,128)(2,1)S(1)} collective-permute-done((bf16[2,32,512]{2,1,0:T(8,128)(2,1)S(1)}, bf16[2,32,512]{2,1,0:T(8,128)(2,1)S(1)}, u32[]{:S(2)}, u32[]{:S(2)}) %collective-permute-start.12) | collective-permute-done | bytes 65568 | tf_op jit(solution)/shard_map/ppermute | solution.py:421
  45.7 1.9 %collective-permute-done.13.refs_1_ = bf16[2,32,512]{2,1,0:T(8,128)(2,1)S(1)} collective-permute-done((bf16[2,32,512]{2,1,0:T(8,128)(2,1)S(1)}, bf16[2,32,512]{2,1,0:T(8,128)(2,1)S(1)}, u32[]{:S(2)}, u32[]{:S(2)}) %collective-permute-start.13) | collective-permute-done | bytes 65568 | tf_op jit(solution)/shard_map/ppermute | solution.py:421
  47.6 1.8 %collective-permute-done.15.refs_3_ = bf16[2,32,512]{2,1,0:T(8,128)(2,1)S(1)} collective-permute-done((bf16[2,32,512]{2,1,0:T(8,128)(2,1)S(1)}, bf16[2,32,512]{2,1,0:T(8,128)(2,1)S(1)}, u32[]{:S(2)}, u32[]{:S(2)}) %collective-permute-start.15) | collective-permute-done | bytes 65568 | tf_op jit(solution)/shard_map/ppermute | solution.py:421
  49.9 1.5 %collective-permute-done.18.refs_7_ = bf16[8,32,512]{2,1,0:T(8,128)(2,1)S(1)} collective-permute-done((bf16[8,32,512]{2,1,0:T(8,128)(2,1)S(1)}, bf16[8,32,512]{2,1,0:T(8,128)(2,1)S(1)}, u32[]{:S(2)}, u32[]{:S(2)}) %collective-permute-start.18) | collective-permute-done | bytes 262176 | tf_op jit(solution)/shard_map/ppermute | solution.py:421
  51.9 1.4 %terms.3 = (f32[32,3584]{1,0:T(8,128)S(1)}, bf16[32,3584]{1,0:T(8,128)(2,1)S(1)}) custom-call(bf16[64,1024]{1,0:T(8,128)(2,1)S(1)} %values.1.val_ref, bf16[1024,7168]{1,0:T(8,128)(2,1)S(1)} %bitcast.2), custom_call_target="tpu_custom_call" | custom-call | flops 6899999744 | tf_op jit(solution)/shard_map/terms/pallas_call | solution.py:37
  53.5 1.4 %terms.2 = (f32[32,3584]{1,0:T(8,128)S(1)}, bf16[32,3584]{1,0:T(8,128)(2,1)S(1)}) custom-call(bf16[64,1024]{1,0:T(8,128)(2,1)S(1)} %values.1.val_ref, bf16[1024,7168]{1,0:T(8,128)(2,1)S(1)} %bitcast.2), custom_call_target="tpu_custom_call" | custom-call | flops 6899999744 | tf_op jit(solution)/shard_map/terms/pallas_call | solution.py:37
  55.4 1.5 %collective-permute-start.24 = (bf16[8,3584]{1,0:T(8,128)(2,1)S(1)}, bf16[8,3584]{1,0:T(8,128)(2,1)S(1)}, u32[]{:S(2)}, u32[]{:S(2)}) collective-permute-start(bf16[8,3584]{1,0:T(8,128)(2,1)S(1)} %get-tuple-element.69), channel_id=1, source_target_pairs={{0,2},{1,3},{2,0},{3,1},{4,6},{5,7},{6,4},{7,5},{8,10},{9,11},{10,... | collective-permute-start | bytes 172040 | tf_op jit(solution)/shard_map/ppermute | solution.py:421
  57.0 1.0 %collective-permute-start.25 = (bf16[8,3584]{1,0:T(8,128)(2,1)S(1)}, bf16[8,3584]{1,0:T(8,128)(2,1)S(1)}, u32[]{:S(2)}, u32[]{:S(2)}) collective-permute-start(bf16[8,3584]{1,0:T(8,128)(2,1)S(1)} %get-tuple-element.70), channel_id=1, source_target_pairs={{0,2},{1,3},{2,0},{3,1},{4,6},{5,7},{6,4},{7,5},{8,10},{9,11},{10,... | collective-permute-start | bytes 172040 | tf_op jit(solution)/shard_map/ppermute | solution.py:421
  58.7 1.9 %collective-permute-start.22 = (bf16[4,7168]{1,0:T(4,128)(2,1)S(1)}, bf16[4,7168]{1,0:T(4,128)(2,1)S(1)}, u32[]{:S(2)}, u32[]{:S(2)}) collective-permute-start(bf16[4,7168]{1,0:T(4,128)(2,1)S(1)} %get-tuple-element.65), channel_id=1, source_target_pairs={{0,6},{1,7},{2,4},{3,5},{4,2},{5,3},{6,0},{7,1},{8,14},{9,15},{10,... | collective-permute-start | bytes 172040 | tf_op jit(solution)/shard_map/ppermute | solution.py:421
  60.6 1.0 %collective-permute-start.23 = (bf16[4,7168]{1,0:T(4,128)(2,1)S(1)}, bf16[4,7168]{1,0:T(4,128)(2,1)S(1)}, u32[]{:S(2)}, u32[]{:S(2)}) collective-permute-start(bf16[4,7168]{1,0:T(4,128)(2,1)S(1)} %get-tuple-element.66), channel_id=1, source_target_pairs={{0,2},{1,3},{2,0},{3,1},{4,6},{5,7},{6,4},{7,5},{8,10},{9,11},{10,... | collective-permute-start | bytes 172040 | tf_op jit(solution)/shard_map/ppermute | solution.py:421
  61.6 1.9 %collective-permute-start.26 = (bf16[4,7168]{1,0:T(4,128)(2,1)S(1)}, bf16[4,7168]{1,0:T(4,128)(2,1)S(1)}, u32[]{:S(2)}, u32[]{:S(2)}) collective-permute-start(bf16[4,7168]{1,0:T(4,128)(2,1)S(1)} %get-tuple-element.71), channel_id=1, source_target_pairs={{0,12},{1,13},{2,14},{3,15},{4,8},{5,9},{6,10},{7,11},{8,4},{9,5},... | collective-permute-start | bytes 172040 | tf_op jit(solution)/shard_map/ppermute | solution.py:421
  63.8 1.0 %collective-permute-done.23.refs_3_ = bf16[4,7168]{1,0:T(4,128)(2,1)S(1)} collective-permute-done((bf16[4,7168]{1,0:T(4,128)(2,1)S(1)}, bf16[4,7168]{1,0:T(4,128)(2,1)S(1)}, u32[]{:S(2)}, u32[]{:S(2)}) %collective-permute-start.23) | collective-permute-done | bytes 57376 | tf_op jit(solution)/shard_map/ppermute | solution.py:421
  64.7 2.9 %collective-permute-done.26.refs_4_ = bf16[4,7168]{1,0:T(4,128)(2,1)S(1)} collective-permute-done((bf16[4,7168]{1,0:T(4,128)(2,1)S(1)}, bf16[4,7168]{1,0:T(4,128)(2,1)S(1)}, u32[]{:S(2)}, u32[]{:S(2)}) %collective-permute-start.26) | collective-permute-done | bytes 57376 | tf_op jit(solution)/shard_map/ppermute | solution.py:421
  67.6 2.0 %collective-permute-done.27.refs_5_ = bf16[4,7168]{1,0:T(4,128)(2,1)S(1)} collective-permute-done((bf16[4,7168]{1,0:T(4,128)(2,1)S(1)}, bf16[4,7168]{1,0:T(4,128)(2,1)S(1)}, u32[]{:S(2)}, u32[]{:S(2)}) %collective-permute-start.27) | collective-permute-done | bytes 57376 | tf_op jit(solution)/shard_map/ppermute | solution.py:421
  (72 shorter events, 7.7 us)
Async XLA Ops:
  0.0 14.7 %collective-permute-start.4 = (bf16[1536,1536]{1,0:T(8,128)(2,1)}, bf16[1536,1536]{1,0:T(8,128)(2,1)S(1)}, u32[]{:S(2)}, u32[]{:S(2)}) collective-permute-start(bf16[1536,1536]{1,0:T(8,128)(2,1)} %refs_4_.1), channel_id=1, source_target_pairs={{0,1},{1,0},{2,3},{3,2},{4,5},{5,4},{6,7},{7,6},{8,9},{9,8},{10,11... | collective-permute-start | bytes 14155784 | tf_op jit(solution)/shard_map/ppermute | solution.py:421
  0.5 14.2 %collective-permute-start.5 = (bf16[8,128,512]{2,1,0:T(8,128)(2,1)}, bf16[8,128,512]{2,1,0:T(8,128)(2,1)S(1)}, u32[]{:S(2)}, u32[]{:S(2)}) collective-permute-start(bf16[8,128,512]{2,1,0:T(8,128)(2,1)} %refs_5_.1), channel_id=1, source_target_pairs={{0,1},{1,0},{2,3},{3,2},{4,5},{5,4},{6,7},{7,6},{8,9},{9,8},{10,11... | collective-permute-start | bytes 3145736 | tf_op jit(solution)/shard_map/ppermute | solution.py:421
  1.2 4.6 %collective-permute-start = (bf16[4,1536]{1,0:T(4,128)(2,1)S(1)}, bf16[4,1536]{1,0:T(4,128)(2,1)S(1)}, u32[]{:S(2)}, u32[]{:S(2)}) collective-permute-start(bf16[4,1536]{1,0:T(4,128)(2,1)S(1)} %stage.1.refs_0_), channel_id=1, source_target_pairs={{0,2},{1,3},{2,0},{3,1},{4,6},{5,7},{6,4},{7,5},{8,10},{9,11},{10,... | collective-permute-start | bytes 36872 | tf_op jit(solution)/shard_map/ppermute | solution.py:421
  4.8 9.9 %slice-start.6 = ((s8[4718592]{0:T(1024)(128)(4,1)}), s8[4194304]{0:T(1024)(128)(4,1)S(1)}, s32[]{:S(2)}) async-start(s8[4718592]{0:T(1024)(128)(4,1)} %bitcast.7), calls=%async_computation.6 | async-start | bytes 8388608
  5.9 8.9 %copy-start = (bf16[8,128,512]{2,1,0:T(8,128)(2,1)S(1)}, bf16[8,128,512]{2,1,0:T(8,128)(2,1)}, u32[]{:S(2)}) copy-start(bf16[8,128,512]{2,1,0:T(8,128)(2,1)} %refs_5_.1) | copy-start | bytes 3145732
  5.9 20.5 %slice-start.4 = ((s8[7077888]{0:T(1024)(128)(4,1)}), s8[4194304]{0:T(1024)(128)(4,1)S(1)}, s32[]{:S(2)}) async-start(s8[7077888]{0:T(1024)(128)(4,1)} %bitcast.3), calls=%async_computation.4 | async-start | bytes 8388608
  5.9 20.5 %slice-start.5 = ((s8[7077888]{0:T(1024)(128)(4,1)}), s8[2883584]{0:T(1024)(128)(4,1)S(1)}, s32[]{:S(2)}) async-start(s8[7077888]{0:T(1024)(128)(4,1)} %bitcast.3), calls=%async_computation.5 | async-start | bytes 5767168
  5.9 5.0 %collective-permute-start.3 = (bf16[8,1536]{1,0:T(8,128)(2,1)S(1)}, bf16[8,1536]{1,0:T(8,128)(2,1)S(1)}, u32[]{:S(2)}, u32[]{:S(2)}) collective-permute-start(bf16[8,1536]{1,0:T(8,128)(2,1)S(1)} %get-tuple-element.43.refs_0_), channel_id=1, source_target_pairs={{0,8},{1,9},{2,10},{3,11},{4,12},{5,13},{6,14},{7,15},{8,0},{9,1},... | collective-permute-start | bytes 73736 | tf_op jit(solution)/shard_map/ppermute | solution.py:421
  9.1 5.6 %collective-permute-start.2 = (bf16[8,1536]{1,0:T(8,128)(2,1)S(1)}, bf16[8,1536]{1,0:T(8,128)(2,1)S(1)}, u32[]{:S(2)}, u32[]{:S(2)}) collective-permute-start(bf16[8,1536]{1,0:T(8,128)(2,1)S(1)} %get-tuple-element.43.refs_0_), channel_id=1, source_target_pairs={{0,12},{1,13},{2,14},{3,15},{4,8},{5,9},{6,10},{7,11},{8,4},{9,5},... | collective-permute-start | bytes 73736 | tf_op jit(solution)/shard_map/ppermute | solution.py:421
  10.4 4.3 %collective-permute-start.1 = (bf16[8,1536]{1,0:T(8,128)(2,1)S(1)}, bf16[8,1536]{1,0:T(8,128)(2,1)S(1)}, u32[]{:S(2)}, u32[]{:S(2)}) collective-permute-start(bf16[8,1536]{1,0:T(8,128)(2,1)S(1)} %get-tuple-element.43.refs_0_), channel_id=1, source_target_pairs={{0,4},{1,5},{2,6},{3,7},{4,0},{5,1},{6,2},{7,3},{8,12},{9,13},{10,... | collective-permute-start | bytes 73736 | tf_op jit(solution)/shard_map/ppermute | solution.py:421
  17.0 9.2 %collective-permute-start.6 = (bf16[4,144,128]{2,1,0:T(8,128)(2,1)S(1)}, bf16[4,144,128]{2,1,0:T(8,128)(2,1)S(1)}, u32[]{:S(2)}, u32[]{:S(2)}) collective-permute-start(bf16[4,144,128]{2,1,0:T(8,128)(2,1)S(1)} %get-tuple-element.45), channel_id=1, source_target_pairs={{0,2},{1,3},{2,0},{3,1},{4,6},{5,7},{6,4},{7,5},{8,10},{9,11},{10,... | collective-permute-start | bytes 442376 | tf_op jit(solution)/shard_map/ppermute | solution.py:421
  18.6 9.5 %collective-permute-start.7 = (bf16[2,144,128]{2,1,0:T(8,128)(2,1)S(1)}, bf16[2,144,128]{2,1,0:T(8,128)(2,1)S(1)}, u32[]{:S(2)}, u32[]{:S(2)}) collective-permute-start(bf16[2,144,128]{2,1,0:T(8,128)(2,1)S(1)} %get-tuple-element.46), channel_id=1, source_target_pairs={{0,8},{1,9},{2,10},{3,11},{4,12},{5,13},{6,14},{7,15},{8,0},{9,1},... | collective-permute-start | bytes 221192 | tf_op jit(solution)/shard_map/ppermute | solution.py:421
  19.8 11.2 %collective-permute-start.8 = (bf16[2,144,128]{2,1,0:T(8,128)(2,1)S(1)}, bf16[2,144,128]{2,1,0:T(8,128)(2,1)S(1)}, u32[]{:S(2)}, u32[]{:S(2)}) collective-permute-start(bf16[2,144,128]{2,1,0:T(8,128)(2,1)S(1)} %get-tuple-element.47), channel_id=1, source_target_pairs={{0,10},{1,11},{2,8},{3,9},{4,14},{5,15},{6,12},{7,13},{8,2},{9,3},... | collective-permute-start | bytes 221192 | tf_op jit(solution)/shard_map/ppermute | solution.py:421
  21.5 9.5 %collective-permute-start.9 = (bf16[2,144,128]{2,1,0:T(8,128)(2,1)S(1)}, bf16[2,144,128]{2,1,0:T(8,128)(2,1)S(1)}, u32[]{:S(2)}, u32[]{:S(2)}) collective-permute-start(bf16[2,144,128]{2,1,0:T(8,128)(2,1)S(1)} %get-tuple-element.48), channel_id=1, source_target_pairs={{0,12},{1,13},{2,14},{3,15},{4,8},{5,9},{6,10},{7,11},{8,4},{9,5},... | collective-permute-start | bytes 221192 | tf_op jit(solution)/shard_map/ppermute | solution.py:421
  23.5 7.5 %collective-permute-start.10 = (bf16[2,144,128]{2,1,0:T(8,128)(2,1)S(1)}, bf16[2,144,128]{2,1,0:T(8,128)(2,1)S(1)}, u32[]{:S(2)}, u32[]{:S(2)}) collective-permute-start(bf16[2,144,128]{2,1,0:T(8,128)(2,1)S(1)} %get-tuple-element.49), channel_id=1, source_target_pairs={{0,14},{1,15},{2,12},{3,13},{4,10},{5,11},{6,8},{7,9},{8,6},{9,7},... | collective-permute-start | bytes 221192 | tf_op jit(solution)/shard_map/ppermute | solution.py:421
  26.3 6.0 %collective-permute-start.11 = (bf16[4,144,128]{2,1,0:T(8,128)(2,1)S(1)}, bf16[4,144,128]{2,1,0:T(8,128)(2,1)S(1)}, u32[]{:S(2)}, u32[]{:S(2)}) collective-permute-start(bf16[4,144,128]{2,1,0:T(8,128)(2,1)S(1)} %forward.2.after_ref), channel_id=1, source_target_pairs={{0,4},{1,5},{2,6},{3,7},{4,0},{5,1},{6,2},{7,3},{8,12},{9,13},{10,... | collective-permute-start | bytes 442376 | tf_op jit(solution)/shard_map/ppermute | solution.py:421
  35.7 8.4 %collective-permute-start.16 = (bf16[4,32,512]{2,1,0:T(8,128)(2,1)S(1)}, bf16[4,32,512]{2,1,0:T(8,128)(2,1)S(1)}, u32[]{:S(2)}, u32[]{:S(2)}) collective-permute-start(bf16[4,32,512]{2,1,0:T(8,128)(2,1)S(1)} %get-tuple-element.55), channel_id=1, source_target_pairs={{0,2},{1,3},{2,0},{3,1},{4,6},{5,7},{6,4},{7,5},{8,10},{9,11},{10,... | collective-permute-start | bytes 393224 | tf_op jit(solution)/shard_map/ppermute | solution.py:421
  36.5 9.2 %collective-permute-start.12 = (bf16[2,32,512]{2,1,0:T(8,128)(2,1)S(1)}, bf16[2,32,512]{2,1,0:T(8,128)(2,1)S(1)}, u32[]{:S(2)}, u32[]{:S(2)}) collective-permute-start(bf16[2,32,512]{2,1,0:T(8,128)(2,1)S(1)} %get-tuple-element.51), channel_id=1, source_target_pairs={{0,8},{1,9},{2,10},{3,11},{4,12},{5,13},{6,14},{7,15},{8,0},{9,1},... | collective-permute-start | bytes 196616 | tf_op jit(solution)/shard_map/ppermute | solution.py:421
  38.5 9.1 %collective-permute-start.13 = (bf16[2,32,512]{2,1,0:T(8,128)(2,1)S(1)}, bf16[2,32,512]{2,1,0:T(8,128)(2,1)S(1)}, u32[]{:S(2)}, u32[]{:S(2)}) collective-permute-start(bf16[2,32,512]{2,1,0:T(8,128)(2,1)S(1)} %get-tuple-element.52), channel_id=1, source_target_pairs={{0,10},{1,11},{2,8},{3,9},{4,14},{5,15},{6,12},{7,13},{8,2},{9,3},... | collective-permute-start | bytes 196616 | tf_op jit(solution)/shard_map/ppermute | solution.py:421
  40.2 7.5 %collective-permute-start.14 = (bf16[2,32,512]{2,1,0:T(8,128)(2,1)S(1)}, bf16[2,32,512]{2,1,0:T(8,128)(2,1)S(1)}, u32[]{:S(2)}, u32[]{:S(2)}) collective-permute-start(bf16[2,32,512]{2,1,0:T(8,128)(2,1)S(1)} %get-tuple-element.53), channel_id=1, source_target_pairs={{0,12},{1,13},{2,14},{3,15},{4,8},{5,9},{6,10},{7,11},{8,4},{9,5},... | collective-permute-start | bytes 196616 | tf_op jit(solution)/shard_map/ppermute | solution.py:421
  42.3 7.1 %collective-permute-start.15 = (bf16[2,32,512]{2,1,0:T(8,128)(2,1)S(1)}, bf16[2,32,512]{2,1,0:T(8,128)(2,1)S(1)}, u32[]{:S(2)}, u32[]{:S(2)}) collective-permute-start(bf16[2,32,512]{2,1,0:T(8,128)(2,1)S(1)} %get-tuple-element.54), channel_id=1, source_target_pairs={{0,14},{1,15},{2,12},{3,13},{4,10},{5,11},{6,8},{7,9},{8,6},{9,7},... | collective-permute-start | bytes 196616 | tf_op jit(solution)/shard_map/ppermute | solution.py:421
  44.2 5.6 %collective-permute-start.17 = (bf16[4,32,512]{2,1,0:T(8,128)(2,1)S(1)}, bf16[4,32,512]{2,1,0:T(8,128)(2,1)S(1)}, u32[]{:S(2)}, u32[]{:S(2)}) collective-permute-start(bf16[4,32,512]{2,1,0:T(8,128)(2,1)S(1)} %forward.3.after_ref), channel_id=1, source_target_pairs={{0,4},{1,5},{2,6},{3,7},{4,0},{5,1},{6,2},{7,3},{8,12},{9,13},{10,... | collective-permute-start | bytes 393224 | tf_op jit(solution)/shard_map/ppermute | solution.py:421
  49.8 1.6 %collective-permute-start.18 = (bf16[8,32,512]{2,1,0:T(8,128)(2,1)S(1)}, bf16[8,32,512]{2,1,0:T(8,128)(2,1)S(1)}, u32[]{:S(2)}, u32[]{:S(2)}) collective-permute-start(bf16[8,32,512]{2,1,0:T(8,128)(2,1)S(1)} %regroup.1), channel_id=1, source_target_pairs={{0,1},{1,0},{2,3},{3,2},{4,5},{5,4},{6,7},{7,6},{8,9},{9,8},{10,11... | collective-permute-start | bytes 786440 | tf_op jit(solution)/shard_map/ppermute | solution.py:421
  53.3 2.0 %collective-permute-start.20 = (bf16[32,3584]{1,0:T(8,128)(2,1)S(1)}, bf16[32,3584]{1,0:T(8,128)(2,1)S(1)}, u32[]{:S(2)}, u32[]{:S(2)}) collective-permute-start(bf16[32,3584]{1,0:T(8,128)(2,1)S(1)} %get-tuple-element.61), channel_id=1, source_target_pairs={{0,1},{1,0},{2,3},{3,2},{4,5},{5,4},{6,7},{7,6},{8,9},{9,8},{10,11... | collective-permute-start | bytes 688136 | tf_op jit(solution)/shard_map/ppermute | solution.py:421
  54.9 2.1 %collective-permute-start.19 = (bf16[32,3584]{1,0:T(8,128)(2,1)S(1)}, bf16[32,3584]{1,0:T(8,128)(2,1)S(1)}, u32[]{:S(2)}, u32[]{:S(2)}) collective-permute-start(bf16[32,3584]{1,0:T(8,128)(2,1)S(1)} %get-tuple-element.59), channel_id=1, source_target_pairs={{0,1},{1,0},{2,3},{3,2},{4,5},{5,4},{6,7},{7,6},{8,9},{9,8},{10,11... | collective-permute-start | bytes 688136 | tf_op jit(solution)/shard_map/ppermute | solution.py:421
  55.4 6.2 %collective-permute-start.24 = (bf16[8,3584]{1,0:T(8,128)(2,1)S(1)}, bf16[8,3584]{1,0:T(8,128)(2,1)S(1)}, u32[]{:S(2)}, u32[]{:S(2)}) collective-permute-start(bf16[8,3584]{1,0:T(8,128)(2,1)S(1)} %get-tuple-element.69), channel_id=1, source_target_pairs={{0,2},{1,3},{2,0},{3,1},{4,6},{5,7},{6,4},{7,5},{8,10},{9,11},{10,... | collective-permute-start | bytes 172040 | tf_op jit(solution)/shard_map/ppermute | solution.py:421
  57.0 4.5 %collective-permute-start.25 = (bf16[8,3584]{1,0:T(8,128)(2,1)S(1)}, bf16[8,3584]{1,0:T(8,128)(2,1)S(1)}, u32[]{:S(2)}, u32[]{:S(2)}) collective-permute-start(bf16[8,3584]{1,0:T(8,128)(2,1)S(1)} %get-tuple-element.70), channel_id=1, source_target_pairs={{0,2},{1,3},{2,0},{3,1},{4,6},{5,7},{6,4},{7,5},{8,10},{9,11},{10,... | collective-permute-start | bytes 172040 | tf_op jit(solution)/shard_map/ppermute | solution.py:421
  58.0 5.7 %collective-permute-start.21 = (bf16[4,7168]{1,0:T(4,128)(2,1)S(1)}, bf16[4,7168]{1,0:T(4,128)(2,1)S(1)}, u32[]{:S(2)}, u32[]{:S(2)}) collective-permute-start(bf16[4,7168]{1,0:T(4,128)(2,1)S(1)} %get-tuple-element.64), channel_id=1, source_target_pairs={{0,4},{1,5},{2,6},{3,7},{4,0},{5,1},{6,2},{7,3},{8,12},{9,13},{10,... | collective-permute-start | bytes 172040 | tf_op jit(solution)/shard_map/ppermute | solution.py:421
  58.7 5.1 %collective-permute-start.22 = (bf16[4,7168]{1,0:T(4,128)(2,1)S(1)}, bf16[4,7168]{1,0:T(4,128)(2,1)S(1)}, u32[]{:S(2)}, u32[]{:S(2)}) collective-permute-start(bf16[4,7168]{1,0:T(4,128)(2,1)S(1)} %get-tuple-element.65), channel_id=1, source_target_pairs={{0,6},{1,7},{2,4},{3,5},{4,2},{5,3},{6,0},{7,1},{8,14},{9,15},{10,... | collective-permute-start | bytes 172040 | tf_op jit(solution)/shard_map/ppermute | solution.py:421
  60.6 4.2 %collective-permute-start.23 = (bf16[4,7168]{1,0:T(4,128)(2,1)S(1)}, bf16[4,7168]{1,0:T(4,128)(2,1)S(1)}, u32[]{:S(2)}, u32[]{:S(2)}) collective-permute-start(bf16[4,7168]{1,0:T(4,128)(2,1)S(1)} %get-tuple-element.66), channel_id=1, source_target_pairs={{0,2},{1,3},{2,0},{3,1},{4,6},{5,7},{6,4},{7,5},{8,10},{9,11},{10,... | collective-permute-start | bytes 172040 | tf_op jit(solution)/shard_map/ppermute | solution.py:421
  61.6 6.0 %collective-permute-start.26 = (bf16[4,7168]{1,0:T(4,128)(2,1)S(1)}, bf16[4,7168]{1,0:T(4,128)(2,1)S(1)}, u32[]{:S(2)}, u32[]{:S(2)}) collective-permute-start(bf16[4,7168]{1,0:T(4,128)(2,1)S(1)} %get-tuple-element.71), channel_id=1, source_target_pairs={{0,12},{1,13},{2,14},{3,15},{4,8},{5,9},{6,10},{7,11},{8,4},{9,5},... | collective-permute-start | bytes 172040 | tf_op jit(solution)/shard_map/ppermute | solution.py:421
  63.5 6.1 %collective-permute-start.27 = (bf16[4,7168]{1,0:T(4,128)(2,1)S(1)}, bf16[4,7168]{1,0:T(4,128)(2,1)S(1)}, u32[]{:S(2)}, u32[]{:S(2)}) collective-permute-start(bf16[4,7168]{1,0:T(4,128)(2,1)S(1)} %get-tuple-element.72), channel_id=1, source_target_pairs={{0,8},{1,9},{2,10},{3,11},{4,12},{5,13},{6,14},{7,15},{8,0},{9,1},... | collective-permute-start | bytes 172040 | tf_op jit(solution)/shard_map/ppermute | solution.py:421
  (10 other events, 54.0 us)

commit v17 on v13

--- a/solution.py
+++ b/solution.py
@@ -59,8 +59,7 @@
 
 
 def far_chips(devices):
-    chips = [k for k in far_first(devices, 2) if k > Y + Z1]
-    return chips[:1] + chips[:0:-1]
+    return [k for k in far_first(devices, 2) if k > Y + Z1]
 
 
 def chip_order(devices):
@@ -69,6 +68,15 @@
 
 def message_sizes(devices):
     return [1] * len(far_chips(devices)) + [2, 1, 1]
+
+
+def on_odd_core():
+    return lax.rem(lax.axis_index("row"), 2) == 1
+
+
+def flip_rows(key_ref, out_ref):
+    for r in range(key_ref.shape[0]):
+        out_ref[r] = key_ref[r, :LAT, :].T
 
 
 def gathered_order(devices):
@@ -115,9 +123,15 @@
     pieces = devices // 4
     q_refs = refs[:pieces]
     weights = (refs[pieces : pieces + 2], refs[pieces + 2 : pieces + 4])
-    lat_ref, rot_ref = refs[-2:]
-    out_refs = refs[pieces + 4 : -2]
+    key_ref = refs[pieces + 4]
+    flip_ref, lat_ref, rot_ref = refs[-3:]
+    out_refs = refs[pieces + 5 : -3]
     heads = weights[0][1].shape[0]
+
+    @pl.when(jnp.logical_not(on_odd_core()))
+    def _():
+        flip_rows(key_ref, flip_ref)
+
     piece = jnp.concatenate([ref[...].astype(jnp.float32) for ref in q_refs], axis=0)
     piece = piece.astype(jnp.bfloat16)
     count = piece.shape[0]
@@ -153,7 +167,7 @@
             )
 
 
-def project(pieces, weights, devices):
+def project(pieces, weights, keys, devices):
     heads = weights[1].shape[0]
     count = len(pieces) * pieces[0].shape[0]
     wide = 2 * count // devices * heads
@@ -164,17 +178,26 @@
     tall = PIECES * wide + wide // 2
     out = [shape(2 * size, tall, LANES) for size in message_sizes(devices)]
     kernel = functools.partial(project_kernel, devices)
-    return call(kernel, out, 20, "project", scratch)(*pieces, *[resident(w) for w in weights])
-
-
-def flip_kernel(key_ref, after_ref, out_ref):
-    for r in range(key_ref.shape[0]):
-        out_ref[r] = key_ref[r, :LAT, :].T
-
-
-def flip(keys, after):
-    rows, _, maxlen = keys.shape
-    return call(flip_kernel, shape(rows, maxlen, LAT), 4, "flip")(resident(keys), after)
+    out.append(shape(keys.shape[0], keys.shape[2], LAT))
+    args = (*pieces, *[resident(w) for w in weights], resident(keys))
+    return call(kernel, out, 20, "project", scratch)(*args)
+
+
+def flip_kernel(key_ref, flipped_ref, after_ref, out_ref):
+    odd = on_odd_core()
+
+    @pl.when(odd)
+    def _():
+        flip_rows(key_ref, out_ref)
+
+    @pl.when(jnp.logical_not(odd))
+    def _():
+        out_ref[...] = flipped_ref[...]
+
+
+def flip(keys, flipped, after):
+    out = shape(*flipped.shape)
+    return call(flip_kernel, out, 4, "flip")(resident(keys), resident(flipped), after)
 
 
 def forward_kernel(own_ref, passing_ref, out_ref):
@@ -426,10 +449,11 @@
         return [*got, passing, swap(sent, Z1), own], sent
 
     far_k = far_chips(devices)
-    messages = project([swap(near, z) for z in zs], [w_uq, w_uk, *far_weights], devices)
+    keys = jnp.swapaxes(cache, 1, 2)
+    pieces = [swap(near, z) for z in zs]
+    *messages, flipped = project(pieces, [w_uq, w_uk, *far_weights], keys, devices)
     messages, sent = exchange(messages)
-    keys = jnp.swapaxes(cache, 1, 2)
-    flipped = flip(keys, sent)
+    flipped = flip(keys, flipped, sent)
     latents = attend(lengths, tables, keys, flipped, new_latent, messages, heads, devices)
     latents, sent = exchange(latents)
     ready = early(latents[-3], latents[-1], sent)

time: 70.1 us -> 71 us (1.013)
  transfers between devices with their start and end apart: 28 -> 28, of which waited for: 12 -> 14; matrix products, arithmetic and copies ran while one was open for 0% -> 0% of each run, Pallas kernels for 6% -> 4%
where the time goes in v17:
time: 71 us; the launch traced here: 70.8 us
  starting transfers between devices  34.7 us (49%)
  waiting for transfers between devices  22.4 us (32%)
  Pallas kernels  12.6 us (18%)
  local copies, waits for them, and re-layouts  0.72 us (1%)
    ppermute x28, starting transfers between devices, swap(): return lax.ppermute(block, 'row', [(i, i ^ k) for i in range(devices)])  34.7 us
    ppermute x28, waiting for transfers between devices, swap(): return lax.ppermute(block, 'row', [(i, i ^ k) for i in range(devices)])  22.4 us
    pallas_call x16, Pallas kernels, run(): pl.pallas_call(kernel, out_shape=out_shape, in_specs=smem + [in_vmem()] *...  12.6 us
  transfers between devices with their start and end apart: 28, of which 14 were waited for; matrix products, arithmetic and copies ran while one was open for 0% of the time, Pallas kernels for 4%

profile of v17, /device:TPU:0, one launch (start us, length us, event | category | flops | bytes accessed | tf_op | source)
XLA Modules:
  0.0 70.8 jit_solution(3437487204249650282)
XLA Ops:
  0.5 3.0 %collective-permute-start = (bf16[4,1536]{1,0:T(4,128)(2,1)}, bf16[4,1536]{1,0:T(4,128)(2,1)S(1)}, u32[]{:S(2)}, u32[]{:S(2)}) collective-permute-start(bf16[4,1536]{1,0:T(4,128)(2,1)} %refs_0_.1), channel_id=1, source_target_pairs={{0,2},{1,3},{2,0},{3,1},{4,6},{5,7},{6,4},{7,5},{8,10},{9,11},{10,... | collective-permute-start | bytes 36872 | tf_op jit(solution)/shard_map/ppermute | solution.py:437
  5.4 3.2 %collective-permute-start.3 = (bf16[8,1536]{1,0:T(8,128)(2,1)S(1)}, bf16[8,1536]{1,0:T(8,128)(2,1)S(1)}, u32[]{:S(2)}, u32[]{:S(2)}) collective-permute-start(bf16[8,1536]{1,0:T(8,128)(2,1)S(1)} %get-tuple-element.44.refs_0_), channel_id=1, source_target_pairs={{0,8},{1,9},{2,10},{3,11},{4,12},{5,13},{6,14},{7,15},{8,0},{9,1},... | collective-permute-start | bytes 73736 | tf_op jit(solution)/shard_map/ppermute | solution.py:437
  8.6 1.3 %collective-permute-start.2 = (bf16[8,1536]{1,0:T(8,128)(2,1)S(1)}, bf16[8,1536]{1,0:T(8,128)(2,1)S(1)}, u32[]{:S(2)}, u32[]{:S(2)}) collective-permute-start(bf16[8,1536]{1,0:T(8,128)(2,1)S(1)} %get-tuple-element.44.refs_0_), channel_id=1, source_target_pairs={{0,12},{1,13},{2,14},{3,15},{4,8},{5,9},{6,10},{7,11},{8,4},{9,5},... | collective-permute-start | bytes 73736 | tf_op jit(solution)/shard_map/ppermute | solution.py:437
  10.4 3.8 %collective-permute-done.2.refs_2_ = bf16[8,1536]{1,0:T(8,128)(2,1)S(1)} collective-permute-done((bf16[8,1536]{1,0:T(8,128)(2,1)S(1)}, bf16[8,1536]{1,0:T(8,128)(2,1)S(1)}, u32[]{:S(2)}, u32[]{:S(2)}) %collective-permute-start.2) | collective-permute-done | bytes 24608 | tf_op jit(solution)/shard_map/ppermute | solution.py:437
  14.3 4.0 %project.1 = (bf16[2,144,128]{2,1,0:T(8,128)(2,1)S(1)}, bf16[2,144,128]{2,1,0:T(8,128)(2,1)S(1)}, bf16[2,144,128]{2,1,0:T(8,128)(2,1)S(1)}, bf16[2,144,128]{2,1,...) custom-call(bf16[8,1536]{1,0:T(8,128)(2,1)S(1)} %get-tuple-element.4, ...), custom_call_target="tpu_custom_call" | custom-call | flops 23000000512 | tf_op jit(solution)/shard_map/project/pallas_call | solution.py:37
  18.2 1.6 %collective-permute-start.6 = (bf16[4,144,128]{2,1,0:T(8,128)(2,1)S(1)}, bf16[4,144,128]{2,1,0:T(8,128)(2,1)S(1)}, u32[]{:S(2)}, u32[]{:S(2)}) collective-permute-start(bf16[4,144,128]{2,1,0:T(8,128)(2,1)S(1)} %get-tuple-element.47), channel_id=1, source_target_pairs={{0,2},{1,3},{2,0},{3,1},{4,6},{5,7},{6,4},{7,5},{8,10},{9,11},{10,... | collective-permute-start | bytes 442376 | tf_op jit(solution)/shard_map/ppermute | solution.py:437
  19.8 1.2 %collective-permute-start.7 = (bf16[2,144,128]{2,1,0:T(8,128)(2,1)S(1)}, bf16[2,144,128]{2,1,0:T(8,128)(2,1)S(1)}, u32[]{:S(2)}, u32[]{:S(2)}) collective-permute-start(bf16[2,144,128]{2,1,0:T(8,128)(2,1)S(1)} %get-tuple-element.48), channel_id=1, source_target_pairs={{0,8},{1,9},{2,10},{3,11},{4,12},{5,13},{6,14},{7,15},{8,0},{9,1},... | collective-permute-start | bytes 221192 | tf_op jit(solution)/shard_map/ppermute | solution.py:437
  21.1 1.6 %collective-permute-start.8 = (bf16[2,144,128]{2,1,0:T(8,128)(2,1)S(1)}, bf16[2,144,128]{2,1,0:T(8,128)(2,1)S(1)}, u32[]{:S(2)}, u32[]{:S(2)}) collective-permute-start(bf16[2,144,128]{2,1,0:T(8,128)(2,1)S(1)} %get-tuple-element.49), channel_id=1, source_target_pairs={{0,10},{1,11},{2,8},{3,9},{4,14},{5,15},{6,12},{7,13},{8,2},{9,3},... | collective-permute-start | bytes 221192 | tf_op jit(solution)/shard_map/ppermute | solution.py:437
  22.7 2.0 %collective-permute-start.9 = (bf16[2,144,128]{2,1,0:T(8,128)(2,1)S(1)}, bf16[2,144,128]{2,1,0:T(8,128)(2,1)S(1)}, u32[]{:S(2)}, u32[]{:S(2)}) collective-permute-start(bf16[2,144,128]{2,1,0:T(8,128)(2,1)S(1)} %get-tuple-element.50), channel_id=1, source_target_pairs={{0,12},{1,13},{2,14},{3,15},{4,8},{5,9},{6,10},{7,11},{8,4},{9,5},... | collective-permute-start | bytes 221192 | tf_op jit(solution)/shard_map/ppermute | solution.py:437
  24.7 2.8 %collective-permute-start.10 = (bf16[2,144,128]{2,1,0:T(8,128)(2,1)S(1)}, bf16[2,144,128]{2,1,0:T(8,128)(2,1)S(1)}, u32[]{:S(2)}, u32[]{:S(2)}) collective-permute-start(bf16[2,144,128]{2,1,0:T(8,128)(2,1)S(1)} %get-tuple-element.51), channel_id=1, source_target_pairs={{0,14},{1,15},{2,12},{3,13},{4,10},{5,11},{6,8},{7,9},{8,6},{9,7},... | collective-permute-start | bytes 221192 | tf_op jit(solution)/shard_map/ppermute | solution.py:437
  28.0 2.2 %collective-permute-done.8.refs_1_ = bf16[2,144,128]{2,1,0:T(8,128)(2,1)S(1)} collective-permute-done((bf16[2,144,128]{2,1,0:T(8,128)(2,1)S(1)}, bf16[2,144,128]{2,1,0:T(8,128)(2,1)S(1)}, u32[]{:S(2)}, u32[]{:S(2)}) %collective-permute-start.8) | collective-permute-done | bytes 73760 | tf_op jit(solution)/shard_map/ppermute | solution.py:437
  30.3 1.7 %collective-permute-done.10.refs_3_ = bf16[2,144,128]{2,1,0:T(8,128)(2,1)S(1)} collective-permute-done((bf16[2,144,128]{2,1,0:T(8,128)(2,1)S(1)}, bf16[2,144,128]{2,1,0:T(8,128)(2,1)S(1)}, u32[]{:S(2)}, u32[]{:S(2)}) %collective-permute-start.10) | collective-permute-done | bytes 73760 | tf_op jit(solution)/shard_map/ppermute | solution.py:437
  32.0 1.4 %collective-permute-done.11.refs_5_ = bf16[4,144,128]{2,1,0:T(8,128)(2,1)S(1)} collective-permute-done((bf16[4,144,128]{2,1,0:T(8,128)(2,1)S(1)}, bf16[4,144,128]{2,1,0:T(8,128)(2,1)S(1)}, u32[]{:S(2)}, u32[]{:S(2)}) %collective-permute-start.11) | collective-permute-done | bytes 147488 | tf_op jit(solution)/shard_map/ppermute | solution.py:437
  33.4 3.5 %attend.1 = (bf16[2,32,512]{2,1,0:T(8,128)(2,1)S(1)}, bf16[2,32,512]{2,1,0:T(8,128)(2,1)S(1)}, bf16[2,32,512]{2,1,0:T(8,128)(2,1)S(1)}, bf16[2,32,512]{2,1,0:T(8...) custom-call(s32[4]{0:T(128)S(1)} %copy-done.5, ...), custom_call_target="tpu_custom_call" | custom-call | flops 11500000256 | tf_op jit(solution)/shard_map/attend/pallas_call | solution.py:37
  37.6 1.1 %collective-permute-start.12 = (bf16[2,32,512]{2,1,0:T(8,128)(2,1)S(1)}, bf16[2,32,512]{2,1,0:T(8,128)(2,1)S(1)}, u32[]{:S(2)}, u32[]{:S(2)}) collective-permute-start(bf16[2,32,512]{2,1,0:T(8,128)(2,1)S(1)} %get-tuple-element.53), channel_id=1, source_target_pairs={{0,8},{1,9},{2,10},{3,11},{4,12},{5,13},{6,14},{7,15},{8,0},{9,1},... | collective-permute-start | bytes 196616 | tf_op jit(solution)/shard_map/ppermute | solution.py:437
  38.7 2.7 %collective-permute-start.13 = (bf16[2,32,512]{2,1,0:T(8,128)(2,1)S(1)}, bf16[2,32,512]{2,1,0:T(8,128)(2,1)S(1)}, u32[]{:S(2)}, u32[]{:S(2)}) collective-permute-start(bf16[2,32,512]{2,1,0:T(8,128)(2,1)S(1)} %get-tuple-element.54), channel_id=1, source_target_pairs={{0,10},{1,11},{2,8},{3,9},{4,14},{5,15},{6,12},{7,13},{8,2},{9,3},... | collective-permute-start | bytes 196616 | tf_op jit(solution)/shard_map/ppermute | solution.py:437
  41.4 1.9 %collective-permute-start.14 = (bf16[2,32,512]{2,1,0:T(8,128)(2,1)S(1)}, bf16[2,32,512]{2,1,0:T(8,128)(2,1)S(1)}, u32[]{:S(2)}, u32[]{:S(2)}) collective-permute-start(bf16[2,32,512]{2,1,0:T(8,128)(2,1)S(1)} %get-tuple-element.55), channel_id=1, source_target_pairs={{0,12},{1,13},{2,14},{3,15},{4,8},{5,9},{6,10},{7,11},{8,4},{9,5},... | collective-permute-start | bytes 196616 | tf_op jit(solution)/shard_map/ppermute | solution.py:437
  43.3 1.9 %collective-permute-start.15 = (bf16[2,32,512]{2,1,0:T(8,128)(2,1)S(1)}, bf16[2,32,512]{2,1,0:T(8,128)(2,1)S(1)}, u32[]{:S(2)}, u32[]{:S(2)}) collective-permute-start(bf16[2,32,512]{2,1,0:T(8,128)(2,1)S(1)} %get-tuple-element.56), channel_id=1, source_target_pairs={{0,14},{1,15},{2,12},{3,13},{4,10},{5,11},{6,8},{7,9},{8,6},{9,7},... | collective-permute-start | bytes 196616 | tf_op jit(solution)/shard_map/ppermute | solution.py:437
  45.4 1.0 %collective-permute-done.13.refs_1_ = bf16[2,32,512]{2,1,0:T(8,128)(2,1)S(1)} collective-permute-done((bf16[2,32,512]{2,1,0:T(8,128)(2,1)S(1)}, bf16[2,32,512]{2,1,0:T(8,128)(2,1)S(1)}, u32[]{:S(2)}, u32[]{:S(2)}) %collective-permute-start.13) | collective-permute-done | bytes 65568 | tf_op jit(solution)/shard_map/ppermute | solution.py:437
  46.4 1.1 %collective-permute-done.14.refs_2_ = bf16[2,32,512]{2,1,0:T(8,128)(2,1)S(1)} collective-permute-done((bf16[2,32,512]{2,1,0:T(8,128)(2,1)S(1)}, bf16[2,32,512]{2,1,0:T(8,128)(2,1)S(1)}, u32[]{:S(2)}, u32[]{:S(2)}) %collective-permute-start.14) | collective-permute-done | bytes 65568 | tf_op jit(solution)/shard_map/ppermute | solution.py:437
  47.6 2.8 %collective-permute-done.15.refs_3_ = bf16[2,32,512]{2,1,0:T(8,128)(2,1)S(1)} collective-permute-done((bf16[2,32,512]{2,1,0:T(8,128)(2,1)S(1)}, bf16[2,32,512]{2,1,0:T(8,128)(2,1)S(1)}, u32[]{:S(2)}, u32[]{:S(2)}) %collective-permute-start.15) | collective-permute-done | bytes 65568 | tf_op jit(solution)/shard_map/ppermute | solution.py:437
  50.8 1.5 %collective-permute-done.18.refs_7_ = bf16[8,32,512]{2,1,0:T(8,128)(2,1)S(1)} collective-permute-done((bf16[8,32,512]{2,1,0:T(8,128)(2,1)S(1)}, bf16[8,32,512]{2,1,0:T(8,128)(2,1)S(1)}, u32[]{:S(2)}, u32[]{:S(2)}) %collective-permute-start.18) | collective-permute-done | bytes 262176 | tf_op jit(solution)/shard_map/ppermute | solution.py:437
  52.9 1.4 %terms.3 = (f32[32,3584]{1,0:T(8,128)S(1)}, bf16[32,3584]{1,0:T(8,128)(2,1)S(1)}) custom-call(bf16[64,1024]{1,0:T(8,128)(2,1)S(1)} %values.1.val_ref, bf16[1024,7168]{1,0:T(8,128)(2,1)S(1)} %bitcast.7), custom_call_target="tpu_custom_call" | custom-call | flops 6899999744 | tf_op jit(solution)/shard_map/terms/pallas_call | solution.py:37
  54.5 1.4 %terms.2 = (f32[32,3584]{1,0:T(8,128)S(1)}, bf16[32,3584]{1,0:T(8,128)(2,1)S(1)}) custom-call(bf16[64,1024]{1,0:T(8,128)(2,1)S(1)} %values.1.val_ref, bf16[1024,7168]{1,0:T(8,128)(2,1)S(1)} %bitcast.7), custom_call_target="tpu_custom_call" | custom-call | flops 6899999744 | tf_op jit(solution)/shard_map/terms/pallas_call | solution.py:37
  56.4 1.6 %collective-permute-start.24 = (bf16[8,3584]{1,0:T(8,128)(2,1)S(1)}, bf16[8,3584]{1,0:T(8,128)(2,1)S(1)}, u32[]{:S(2)}, u32[]{:S(2)}) collective-permute-start(bf16[8,3584]{1,0:T(8,128)(2,1)S(1)} %get-tuple-element.71), channel_id=1, source_target_pairs={{0,2},{1,3},{2,0},{3,1},{4,6},{5,7},{6,4},{7,5},{8,10},{9,11},{10,... | collective-permute-start | bytes 172040 | tf_op jit(solution)/shard_map/ppermute | solution.py:437
  58.0 1.0 %collective-permute-start.25 = (bf16[8,3584]{1,0:T(8,128)(2,1)S(1)}, bf16[8,3584]{1,0:T(8,128)(2,1)S(1)}, u32[]{:S(2)}, u32[]{:S(2)}) collective-permute-start(bf16[8,3584]{1,0:T(8,128)(2,1)S(1)} %get-tuple-element.72), channel_id=1, source_target_pairs={{0,2},{1,3},{2,0},{3,1},{4,6},{5,7},{6,4},{7,5},{8,10},{9,11},{10,... | collective-permute-start | bytes 172040 | tf_op jit(solution)/shard_map/ppermute | solution.py:437
  59.3 2.3 %collective-permute-start.22 = (bf16[4,7168]{1,0:T(4,128)(2,1)S(1)}, bf16[4,7168]{1,0:T(4,128)(2,1)S(1)}, u32[]{:S(2)}, u32[]{:S(2)}) collective-permute-start(bf16[4,7168]{1,0:T(4,128)(2,1)S(1)} %get-tuple-element.67), channel_id=1, source_target_pairs={{0,6},{1,7},{2,4},{3,5},{4,2},{5,3},{6,0},{7,1},{8,14},{9,15},{10,... | collective-permute-start | bytes 172040 | tf_op jit(solution)/shard_map/ppermute | solution.py:437
  61.6 1.0 %collective-permute-start.23 = (bf16[4,7168]{1,0:T(4,128)(2,1)S(1)}, bf16[4,7168]{1,0:T(4,128)(2,1)S(1)}, u32[]{:S(2)}, u32[]{:S(2)}) collective-permute-start(bf16[4,7168]{1,0:T(4,128)(2,1)S(1)} %get-tuple-element.68), channel_id=1, source_target_pairs={{0,2},{1,3},{2,0},{3,1},{4,6},{5,7},{6,4},{7,5},{8,10},{9,11},{10,... | collective-permute-start | bytes 172040 | tf_op jit(solution)/shard_map/ppermute | solution.py:437
  62.6 2.0 %collective-permute-start.26 = (bf16[4,7168]{1,0:T(4,128)(2,1)S(1)}, bf16[4,7168]{1,0:T(4,128)(2,1)S(1)}, u32[]{:S(2)}, u32[]{:S(2)}) collective-permute-start(bf16[4,7168]{1,0:T(4,128)(2,1)S(1)} %get-tuple-element.73), channel_id=1, source_target_pairs={{0,12},{1,13},{2,14},{3,15},{4,8},{5,9},{6,10},{7,11},{8,4},{9,5},... | collective-permute-start | bytes 172040 | tf_op jit(solution)/shard_map/ppermute | solution.py:437
  64.6 1.2 %collective-permute-done.23.refs_3_ = bf16[4,7168]{1,0:T(4,128)(2,1)S(1)} collective-permute-done((bf16[4,7168]{1,0:T(4,128)(2,1)S(1)}, bf16[4,7168]{1,0:T(4,128)(2,1)S(1)}, u32[]{:S(2)}, u32[]{:S(2)}) %collective-permute-start.23) | collective-permute-done | bytes 57376 | tf_op jit(solution)/shard_map/ppermute | solution.py:437
  65.8 2.9 %collective-permute-done.26.refs_4_ = bf16[4,7168]{1,0:T(4,128)(2,1)S(1)} collective-permute-done((bf16[4,7168]{1,0:T(4,128)(2,1)S(1)}, bf16[4,7168]{1,0:T(4,128)(2,1)S(1)}, u32[]{:S(2)}, u32[]{:S(2)}) %collective-permute-start.26) | collective-permute-done | bytes 57376 | tf_op jit(solution)/shard_map/ppermute | solution.py:437
  68.7 1.5 %collective-permute-done.27.refs_5_ = bf16[4,7168]{1,0:T(4,128)(2,1)S(1)} collective-permute-done((bf16[4,7168]{1,0:T(4,128)(2,1)S(1)}, bf16[4,7168]{1,0:T(4,128)(2,1)S(1)}, u32[]{:S(2)}, u32[]{:S(2)}) %collective-permute-start.27) | collective-permute-done | bytes 57376 | tf_op jit(solution)/shard_map/ppermute | solution.py:437
  (71 shorter events, 6.9 us)
Async XLA Ops:
  0.0 14.2 %collective-permute-start.4 = (bf16[1536,1536]{1,0:T(8,128)(2,1)}, bf16[1536,1536]{1,0:T(8,128)(2,1)S(1)}, u32[]{:S(2)}, u32[]{:S(2)}) collective-permute-start(bf16[1536,1536]{1,0:T(8,128)(2,1)} %refs_4_.1), channel_id=1, source_target_pairs={{0,1},{1,0},{2,3},{3,2},{4,5},{5,4},{6,7},{7,6},{8,9},{9,8},{10,11... | collective-permute-start | bytes 14155784 | tf_op jit(solution)/shard_map/ppermute | solution.py:437
  0.5 13.7 %collective-permute-start.5 = (bf16[8,128,512]{2,1,0:T(8,128)(2,1)}, bf16[8,128,512]{2,1,0:T(8,128)(2,1)S(1)}, u32[]{:S(2)}, u32[]{:S(2)}) collective-permute-start(bf16[8,128,512]{2,1,0:T(8,128)(2,1)} %refs_5_.1), channel_id=1, source_target_pairs={{0,1},{1,0},{2,3},{3,2},{4,5},{5,4},{6,7},{7,6},{8,9},{9,8},{10,11... | collective-permute-start | bytes 3145736 | tf_op jit(solution)/shard_map/ppermute | solution.py:437
  0.5 4.8 %collective-permute-start = (bf16[4,1536]{1,0:T(4,128)(2,1)}, bf16[4,1536]{1,0:T(4,128)(2,1)S(1)}, u32[]{:S(2)}, u32[]{:S(2)}) collective-permute-start(bf16[4,1536]{1,0:T(4,128)(2,1)} %refs_0_.1), channel_id=1, source_target_pairs={{0,2},{1,3},{2,0},{3,1},{4,6},{5,7},{6,4},{7,5},{8,10},{9,11},{10,... | collective-permute-start | bytes 36872 | tf_op jit(solution)/shard_map/ppermute | solution.py:437
  4.1 10.1 %slice-start = ((s8[7077888]{0:T(1024)(128)(4,1)}), s8[4194304]{0:T(1024)(128)(4,1)S(1)}, s32[]{:S(2)}) async-start(s8[7077888]{0:T(1024)(128)(4,1)} %bitcast.1), calls=%async_computation | async-start | bytes 8388608
  4.1 10.1 %slice-start.6 = ((s8[4718592]{0:T(1024)(128)(4,1)}), s8[4194304]{0:T(1024)(128)(4,1)S(1)}, s32[]{:S(2)}) async-start(s8[4718592]{0:T(1024)(128)(4,1)} %bitcast.8), calls=%async_computation.6 | async-start | bytes 8388608
  5.4 8.9 %slice-start.7 = ((s8[4718592]{0:T(1024)(128)(4,1)}), s8[524288]{0:T(1024)(128)(4,1)S(1)}, s32[]{:S(2)}) async-start(s8[4718592]{0:T(1024)(128)(4,1)} %bitcast.8), calls=%async_computation.7 | async-start | bytes 1048576
  5.4 8.9 %copy-start = (bf16[8,128,512]{2,1,0:T(8,128)(2,1)S(1)}, bf16[8,128,512]{2,1,0:T(8,128)(2,1)}, u32[]{:S(2)}) copy-start(bf16[8,128,512]{2,1,0:T(8,128)(2,1)} %refs_5_.1) | copy-start | bytes 3145732
  5.4 5.0 %collective-permute-start.3 = (bf16[8,1536]{1,0:T(8,128)(2,1)S(1)}, bf16[8,1536]{1,0:T(8,128)(2,1)S(1)}, u32[]{:S(2)}, u32[]{:S(2)}) collective-permute-start(bf16[8,1536]{1,0:T(8,128)(2,1)S(1)} %get-tuple-element.44.refs_0_), channel_id=1, source_target_pairs={{0,8},{1,9},{2,10},{3,11},{4,12},{5,13},{6,14},{7,15},{8,0},{9,1},... | collective-permute-start | bytes 73736 | tf_op jit(solution)/shard_map/ppermute | solution.py:437
  8.6 5.6 %collective-permute-start.2 = (bf16[8,1536]{1,0:T(8,128)(2,1)S(1)}, bf16[8,1536]{1,0:T(8,128)(2,1)S(1)}, u32[]{:S(2)}, u32[]{:S(2)}) collective-permute-start(bf16[8,1536]{1,0:T(8,128)(2,1)S(1)} %get-tuple-element.44.refs_0_), channel_id=1, source_target_pairs={{0,12},{1,13},{2,14},{3,15},{4,8},{5,9},{6,10},{7,11},{8,4},{9,5},... | collective-permute-start | bytes 73736 | tf_op jit(solution)/shard_map/ppermute | solution.py:437
  9.9 4.3 %collective-permute-start.1 = (bf16[8,1536]{1,0:T(8,128)(2,1)S(1)}, bf16[8,1536]{1,0:T(8,128)(2,1)S(1)}, u32[]{:S(2)}, u32[]{:S(2)}) collective-permute-start(bf16[8,1536]{1,0:T(8,128)(2,1)S(1)} %get-tuple-element.44.refs_0_), channel_id=1, source_target_pairs={{0,4},{1,5},{2,6},{3,7},{4,0},{5,1},{6,2},{7,3},{8,12},{9,13},{10,... | collective-permute-start | bytes 73736 | tf_op jit(solution)/shard_map/ppermute | solution.py:437
  18.2 9.2 %collective-permute-start.6 = (bf16[4,144,128]{2,1,0:T(8,128)(2,1)S(1)}, bf16[4,144,128]{2,1,0:T(8,128)(2,1)S(1)}, u32[]{:S(2)}, u32[]{:S(2)}) collective-permute-start(bf16[4,144,128]{2,1,0:T(8,128)(2,1)S(1)} %get-tuple-element.47), channel_id=1, source_target_pairs={{0,2},{1,3},{2,0},{3,1},{4,6},{5,7},{6,4},{7,5},{8,10},{9,11},{10,... | collective-permute-start | bytes 442376 | tf_op jit(solution)/shard_map/ppermute | solution.py:437
  19.8 8.2 %collective-permute-start.7 = (bf16[2,144,128]{2,1,0:T(8,128)(2,1)S(1)}, bf16[2,144,128]{2,1,0:T(8,128)(2,1)S(1)}, u32[]{:S(2)}, u32[]{:S(2)}) collective-permute-start(bf16[2,144,128]{2,1,0:T(8,128)(2,1)S(1)} %get-tuple-element.48), channel_id=1, source_target_pairs={{0,8},{1,9},{2,10},{3,11},{4,12},{5,13},{6,14},{7,15},{8,0},{9,1},... | collective-permute-start | bytes 221192 | tf_op jit(solution)/shard_map/ppermute | solution.py:437
  21.1 9.2 %collective-permute-start.8 = (bf16[2,144,128]{2,1,0:T(8,128)(2,1)S(1)}, bf16[2,144,128]{2,1,0:T(8,128)(2,1)S(1)}, u32[]{:S(2)}, u32[]{:S(2)}) collective-permute-start(bf16[2,144,128]{2,1,0:T(8,128)(2,1)S(1)} %get-tuple-element.49), channel_id=1, source_target_pairs={{0,10},{1,11},{2,8},{3,9},{4,14},{5,15},{6,12},{7,13},{8,2},{9,3},... | collective-permute-start | bytes 221192 | tf_op jit(solution)/shard_map/ppermute | solution.py:437
  22.7 7.6 %collective-permute-start.9 = (bf16[2,144,128]{2,1,0:T(8,128)(2,1)S(1)}, bf16[2,144,128]{2,1,0:T(8,128)(2,1)S(1)}, u32[]{:S(2)}, u32[]{:S(2)}) collective-permute-start(bf16[2,144,128]{2,1,0:T(8,128)(2,1)S(1)} %get-tuple-element.50), channel_id=1, source_target_pairs={{0,12},{1,13},{2,14},{3,15},{4,8},{5,9},{6,10},{7,11},{8,4},{9,5},... | collective-permute-start | bytes 221192 | tf_op jit(solution)/shard_map/ppermute | solution.py:437
  24.7 7.3 %collective-permute-start.10 = (bf16[2,144,128]{2,1,0:T(8,128)(2,1)S(1)}, bf16[2,144,128]{2,1,0:T(8,128)(2,1)S(1)}, u32[]{:S(2)}, u32[]{:S(2)}) collective-permute-start(bf16[2,144,128]{2,1,0:T(8,128)(2,1)S(1)} %get-tuple-element.51), channel_id=1, source_target_pairs={{0,14},{1,15},{2,12},{3,13},{4,10},{5,11},{6,8},{7,9},{8,6},{9,7},... | collective-permute-start | bytes 221192 | tf_op jit(solution)/shard_map/ppermute | solution.py:437
  27.5 5.9 %collective-permute-start.11 = (bf16[4,144,128]{2,1,0:T(8,128)(2,1)S(1)}, bf16[4,144,128]{2,1,0:T(8,128)(2,1)S(1)}, u32[]{:S(2)}, u32[]{:S(2)}) collective-permute-start(bf16[4,144,128]{2,1,0:T(8,128)(2,1)S(1)} %forward.2.after_ref), channel_id=1, source_target_pairs={{0,4},{1,5},{2,6},{3,7},{4,0},{5,1},{6,2},{7,3},{8,12},{9,13},{10,... | collective-permute-start | bytes 442376 | tf_op jit(solution)/shard_map/ppermute | solution.py:437
  36.9 8.3 %collective-permute-start.16 = (bf16[4,32,512]{2,1,0:T(8,128)(2,1)S(1)}, bf16[4,32,512]{2,1,0:T(8,128)(2,1)S(1)}, u32[]{:S(2)}, u32[]{:S(2)}) collective-permute-start(bf16[4,32,512]{2,1,0:T(8,128)(2,1)S(1)} %get-tuple-element.57), channel_id=1, source_target_pairs={{0,2},{1,3},{2,0},{3,1},{4,6},{5,7},{6,4},{7,5},{8,10},{9,11},{10,... | collective-permute-start | bytes 393224 | tf_op jit(solution)/shard_map/ppermute | solution.py:437
  37.6 7.8 %collective-permute-start.12 = (bf16[2,32,512]{2,1,0:T(8,128)(2,1)S(1)}, bf16[2,32,512]{2,1,0:T(8,128)(2,1)S(1)}, u32[]{:S(2)}, u32[]{:S(2)}) collective-permute-start(bf16[2,32,512]{2,1,0:T(8,128)(2,1)S(1)} %get-tuple-element.53), channel_id=1, source_target_pairs={{0,8},{1,9},{2,10},{3,11},{4,12},{5,13},{6,14},{7,15},{8,0},{9,1},... | collective-permute-start | bytes 196616 | tf_op jit(solution)/shard_map/ppermute | solution.py:437
  38.7 7.7 %collective-permute-start.13 = (bf16[2,32,512]{2,1,0:T(8,128)(2,1)S(1)}, bf16[2,32,512]{2,1,0:T(8,128)(2,1)S(1)}, u32[]{:S(2)}, u32[]{:S(2)}) collective-permute-start(bf16[2,32,512]{2,1,0:T(8,128)(2,1)S(1)} %get-tuple-element.54), channel_id=1, source_target_pairs={{0,10},{1,11},{2,8},{3,9},{4,14},{5,15},{6,12},{7,13},{8,2},{9,3},... | collective-permute-start | bytes 196616 | tf_op jit(solution)/shard_map/ppermute | solution.py:437
  41.4 6.2 %collective-permute-start.14 = (bf16[2,32,512]{2,1,0:T(8,128)(2,1)S(1)}, bf16[2,32,512]{2,1,0:T(8,128)(2,1)S(1)}, u32[]{:S(2)}, u32[]{:S(2)}) collective-permute-start(bf16[2,32,512]{2,1,0:T(8,128)(2,1)S(1)} %get-tuple-element.55), channel_id=1, source_target_pairs={{0,12},{1,13},{2,14},{3,15},{4,8},{5,9},{6,10},{7,11},{8,4},{9,5},... | collective-permute-start | bytes 196616 | tf_op jit(solution)/shard_map/ppermute | solution.py:437
  43.3 7.0 %collective-permute-start.15 = (bf16[2,32,512]{2,1,0:T(8,128)(2,1)S(1)}, bf16[2,32,512]{2,1,0:T(8,128)(2,1)S(1)}, u32[]{:S(2)}, u32[]{:S(2)}) collective-permute-start(bf16[2,32,512]{2,1,0:T(8,128)(2,1)S(1)} %get-tuple-element.56), channel_id=1, source_target_pairs={{0,14},{1,15},{2,12},{3,13},{4,10},{5,11},{6,8},{7,9},{8,6},{9,7},... | collective-permute-start | bytes 196616 | tf_op jit(solution)/shard_map/ppermute | solution.py:437
  45.3 5.4 %collective-permute-start.17 = (bf16[4,32,512]{2,1,0:T(8,128)(2,1)S(1)}, bf16[4,32,512]{2,1,0:T(8,128)(2,1)S(1)}, u32[]{:S(2)}, u32[]{:S(2)}) collective-permute-start(bf16[4,32,512]{2,1,0:T(8,128)(2,1)S(1)} %forward.3.after_ref), channel_id=1, source_target_pairs={{0,4},{1,5},{2,6},{3,7},{4,0},{5,1},{6,2},{7,3},{8,12},{9,13},{10,... | collective-permute-start | bytes 393224 | tf_op jit(solution)/shard_map/ppermute | solution.py:437
  50.8 1.6 %collective-permute-start.18 = (bf16[8,32,512]{2,1,0:T(8,128)(2,1)S(1)}, bf16[8,32,512]{2,1,0:T(8,128)(2,1)S(1)}, u32[]{:S(2)}, u32[]{:S(2)}) collective-permute-start(bf16[8,32,512]{2,1,0:T(8,128)(2,1)S(1)} %regroup.1), channel_id=1, source_target_pairs={{0,1},{1,0},{2,3},{3,2},{4,5},{5,4},{6,7},{7,6},{8,9},{9,8},{10,11... | collective-permute-start | bytes 786440 | tf_op jit(solution)/shard_map/ppermute | solution.py:437
  54.3 2.0 %collective-permute-start.20 = (bf16[32,3584]{1,0:T(8,128)(2,1)S(1)}, bf16[32,3584]{1,0:T(8,128)(2,1)S(1)}, u32[]{:S(2)}, u32[]{:S(2)}) collective-permute-start(bf16[32,3584]{1,0:T(8,128)(2,1)S(1)} %get-tuple-element.63), channel_id=1, source_target_pairs={{0,1},{1,0},{2,3},{3,2},{4,5},{5,4},{6,7},{7,6},{8,9},{9,8},{10,11... | collective-permute-start | bytes 688136 | tf_op jit(solution)/shard_map/ppermute | solution.py:437
  55.8 2.1 %collective-permute-start.19 = (bf16[32,3584]{1,0:T(8,128)(2,1)S(1)}, bf16[32,3584]{1,0:T(8,128)(2,1)S(1)}, u32[]{:S(2)}, u32[]{:S(2)}) collective-permute-start(bf16[32,3584]{1,0:T(8,128)(2,1)S(1)} %get-tuple-element.61), channel_id=1, source_target_pairs={{0,1},{1,0},{2,3},{3,2},{4,5},{5,4},{6,7},{7,6},{8,9},{9,8},{10,11... | collective-permute-start | bytes 688136 | tf_op jit(solution)/shard_map/ppermute | solution.py:437
  56.4 6.2 %collective-permute-start.24 = (bf16[8,3584]{1,0:T(8,128)(2,1)S(1)}, bf16[8,3584]{1,0:T(8,128)(2,1)S(1)}, u32[]{:S(2)}, u32[]{:S(2)}) collective-permute-start(bf16[8,3584]{1,0:T(8,128)(2,1)S(1)} %get-tuple-element.71), channel_id=1, source_target_pairs={{0,2},{1,3},{2,0},{3,1},{4,6},{5,7},{6,4},{7,5},{8,10},{9,11},{10,... | collective-permute-start | bytes 172040 | tf_op jit(solution)/shard_map/ppermute | solution.py:437
  58.0 4.5 %collective-permute-start.25 = (bf16[8,3584]{1,0:T(8,128)(2,1)S(1)}, bf16[8,3584]{1,0:T(8,128)(2,1)S(1)}, u32[]{:S(2)}, u32[]{:S(2)}) collective-permute-start(bf16[8,3584]{1,0:T(8,128)(2,1)S(1)} %get-tuple-element.72), channel_id=1, source_target_pairs={{0,2},{1,3},{2,0},{3,1},{4,6},{5,7},{6,4},{7,5},{8,10},{9,11},{10,... | collective-permute-start | bytes 172040 | tf_op jit(solution)/shard_map/ppermute | solution.py:437
  59.1 5.5 %collective-permute-start.21 = (bf16[4,7168]{1,0:T(4,128)(2,1)S(1)}, bf16[4,7168]{1,0:T(4,128)(2,1)S(1)}, u32[]{:S(2)}, u32[]{:S(2)}) collective-permute-start(bf16[4,7168]{1,0:T(4,128)(2,1)S(1)} %get-tuple-element.66), channel_id=1, source_target_pairs={{0,4},{1,5},{2,6},{3,7},{4,0},{5,1},{6,2},{7,3},{8,12},{9,13},{10,... | collective-permute-start | bytes 172040 | tf_op jit(solution)/shard_map/ppermute | solution.py:437
  59.3 5.3 %collective-permute-start.22 = (bf16[4,7168]{1,0:T(4,128)(2,1)S(1)}, bf16[4,7168]{1,0:T(4,128)(2,1)S(1)}, u32[]{:S(2)}, u32[]{:S(2)}) collective-permute-start(bf16[4,7168]{1,0:T(4,128)(2,1)S(1)} %get-tuple-element.67), channel_id=1, source_target_pairs={{0,6},{1,7},{2,4},{3,5},{4,2},{5,3},{6,0},{7,1},{8,14},{9,15},{10,... | collective-permute-start | bytes 172040 | tf_op jit(solution)/shard_map/ppermute | solution.py:437
  61.6 4.2 %collective-permute-start.23 = (bf16[4,7168]{1,0:T(4,128)(2,1)S(1)}, bf16[4,7168]{1,0:T(4,128)(2,1)S(1)}, u32[]{:S(2)}, u32[]{:S(2)}) collective-permute-start(bf16[4,7168]{1,0:T(4,128)(2,1)S(1)} %get-tuple-element.68), channel_id=1, source_target_pairs={{0,2},{1,3},{2,0},{3,1},{4,6},{5,7},{6,4},{7,5},{8,10},{9,11},{10,... | collective-permute-start | bytes 172040 | tf_op jit(solution)/shard_map/ppermute | solution.py:437
  62.6 6.0 %collective-permute-start.26 = (bf16[4,7168]{1,0:T(4,128)(2,1)S(1)}, bf16[4,7168]{1,0:T(4,128)(2,1)S(1)}, u32[]{:S(2)}, u32[]{:S(2)}) collective-permute-start(bf16[4,7168]{1,0:T(4,128)(2,1)S(1)} %get-tuple-element.73), channel_id=1, source_target_pairs={{0,12},{1,13},{2,14},{3,15},{4,8},{5,9},{6,10},{7,11},{8,4},{9,5},... | collective-permute-start | bytes 172040 | tf_op jit(solution)/shard_map/ppermute | solution.py:437
  64.6 5.6 %collective-permute-start.27 = (bf16[4,7168]{1,0:T(4,128)(2,1)S(1)}, bf16[4,7168]{1,0:T(4,128)(2,1)S(1)}, u32[]{:S(2)}, u32[]{:S(2)}) collective-permute-start(bf16[4,7168]{1,0:T(4,128)(2,1)S(1)} %get-tuple-element.74), channel_id=1, source_target_pairs={{0,8},{1,9},{2,10},{3,11},{4,12},{5,13},{6,14},{7,15},{8,0},{9,1},... | collective-permute-start | bytes 172040 | tf_op jit(solution)/shard_map/ppermute | solution.py:437
  (10 other events, 58.0 us)

commit v18 on v13

--- a/solution.py
+++ b/solution.py
@@ -59,8 +59,7 @@
 
 
 def far_chips(devices):
-    chips = [k for k in far_first(devices, 2) if k > Y + Z1]
-    return chips[:1] + chips[:0:-1]
+    return [k for k in far_first(devices, 2) if k > Y + Z1]
 
 
 def chip_order(devices):

time: 70.1 us -> 70.2 us (level)
  starting transfers between devices: 34.2 us -> 35.8 us
  waiting for transfers between devices: 22.6 us -> 21.1 us
    ppermute x28, starting transfers between devices: 34.2 us -> 35.8 us  [swap(): return lax.ppermute(block, 'row', [(i, i ^ k) for i in range(devices)])]
    ppermute x28, waiting for transfers between devices: 22.6 us -> 21.1 us  [swap(): return lax.ppermute(block, 'row', [(i, i ^ k) for i in range(devices)])]
  transfers between devices with their start and end apart: 28 -> 28, of which waited for: 12 -> 13; matrix products, arithmetic and copies ran while one was open for 0% -> 0% of each run, Pallas kernels for 6% -> 6%
where the time goes in v18:
time: 70.2 us; the launch traced here: 70.1 us
  starting transfers between devices  35.8 us (51%)
  waiting for transfers between devices  21.1 us (30%)
  Pallas kernels  12.2 us (17%)
  local copies, waits for them, and re-layouts  0.73 us (1%)
    ppermute x28, starting transfers between devices, swap(): return lax.ppermute(block, 'row', [(i, i ^ k) for i in range(devices)])  35.8 us
    ppermute x28, waiting for transfers between devices, swap(): return lax.ppermute(block, 'row', [(i, i ^ k) for i in range(devices)])  21.1 us
    pallas_call x16, Pallas kernels, run(): pl.pallas_call(kernel, out_shape=out_shape, in_specs=smem + [in_vmem()] *...  12.2 us
  transfers between devices with their start and end apart: 28, of which 13 were waited for; matrix products, arithmetic and copies ran while one was open for 0% of the time, Pallas kernels for 6%

profile of v18, /device:TPU:0, one launch (start us, length us, event | category | flops | bytes accessed | tf_op | source)
XLA Modules:
  0.0 70.1 jit_solution(7619625152966071398)
XLA Ops:
  0.5 3.0 %collective-permute-start = (bf16[4,1536]{1,0:T(4,128)(2,1)}, bf16[4,1536]{1,0:T(4,128)(2,1)S(1)}, u32[]{:S(2)}, u32[]{:S(2)}) collective-permute-start(bf16[4,1536]{1,0:T(4,128)(2,1)} %refs_0_.1), channel_id=1, source_target_pairs={{0,2},{1,3},{2,0},{3,1},{4,6},{5,7},{6,4},{7,5},{8,10},{9,11},{10,... | collective-permute-start | bytes 36872 | tf_op jit(solution)/shard_map/ppermute | solution.py:413
  5.4 3.2 %collective-permute-start.3 = (bf16[8,1536]{1,0:T(8,128)(2,1)S(1)}, bf16[8,1536]{1,0:T(8,128)(2,1)S(1)}, u32[]{:S(2)}, u32[]{:S(2)}) collective-permute-start(bf16[8,1536]{1,0:T(8,128)(2,1)S(1)} %get-tuple-element.43.refs_0_), channel_id=1, source_target_pairs={{0,8},{1,9},{2,10},{3,11},{4,12},{5,13},{6,14},{7,15},{8,0},{9,1},... | collective-permute-start | bytes 73736 | tf_op jit(solution)/shard_map/ppermute | solution.py:413
  8.6 1.3 %collective-permute-start.2 = (bf16[8,1536]{1,0:T(8,128)(2,1)S(1)}, bf16[8,1536]{1,0:T(8,128)(2,1)S(1)}, u32[]{:S(2)}, u32[]{:S(2)}) collective-permute-start(bf16[8,1536]{1,0:T(8,128)(2,1)S(1)} %get-tuple-element.43.refs_0_), channel_id=1, source_target_pairs={{0,12},{1,13},{2,14},{3,15},{4,8},{5,9},{6,10},{7,11},{8,4},{9,5},... | collective-permute-start | bytes 73736 | tf_op jit(solution)/shard_map/ppermute | solution.py:413
  10.4 3.8 %collective-permute-done.2.refs_2_ = bf16[8,1536]{1,0:T(8,128)(2,1)S(1)} collective-permute-done((bf16[8,1536]{1,0:T(8,128)(2,1)S(1)}, bf16[8,1536]{1,0:T(8,128)(2,1)S(1)}, u32[]{:S(2)}, u32[]{:S(2)}) %collective-permute-start.2) | collective-permute-done | bytes 24608 | tf_op jit(solution)/shard_map/ppermute | solution.py:413
  14.2 2.3 %project.1 = (bf16[2,144,128]{2,1,0:T(8,128)(2,1)S(1)}, bf16[2,144,128]{2,1,0:T(8,128)(2,1)S(1)}, bf16[2,144,128]{2,1,0:T(8,128)(2,1)S(1)}, bf16[2,144,128]{2,1,...) custom-call(bf16[8,1536]{1,0:T(8,128)(2,1)S(1)} %get-tuple-element.4, ...), custom_call_target="tpu_custom_call" | custom-call | flops 23000000512 | tf_op jit(solution)/shard_map/project/pallas_call | solution.py:37
  16.5 1.6 %collective-permute-start.6 = (bf16[4,144,128]{2,1,0:T(8,128)(2,1)S(1)}, bf16[4,144,128]{2,1,0:T(8,128)(2,1)S(1)}, u32[]{:S(2)}, u32[]{:S(2)}) collective-permute-start(bf16[4,144,128]{2,1,0:T(8,128)(2,1)S(1)} %get-tuple-element.45), channel_id=1, source_target_pairs={{0,2},{1,3},{2,0},{3,1},{4,6},{5,7},{6,4},{7,5},{8,10},{9,11},{10,... | collective-permute-start | bytes 442376 | tf_op jit(solution)/shard_map/ppermute | solution.py:413
  18.1 1.2 %collective-permute-start.7 = (bf16[2,144,128]{2,1,0:T(8,128)(2,1)S(1)}, bf16[2,144,128]{2,1,0:T(8,128)(2,1)S(1)}, u32[]{:S(2)}, u32[]{:S(2)}) collective-permute-start(bf16[2,144,128]{2,1,0:T(8,128)(2,1)S(1)} %get-tuple-element.46), channel_id=1, source_target_pairs={{0,8},{1,9},{2,10},{3,11},{4,12},{5,13},{6,14},{7,15},{8,0},{9,1},... | collective-permute-start | bytes 221192 | tf_op jit(solution)/shard_map/ppermute | solution.py:413
  19.4 1.6 %collective-permute-start.8 = (bf16[2,144,128]{2,1,0:T(8,128)(2,1)S(1)}, bf16[2,144,128]{2,1,0:T(8,128)(2,1)S(1)}, u32[]{:S(2)}, u32[]{:S(2)}) collective-permute-start(bf16[2,144,128]{2,1,0:T(8,128)(2,1)S(1)} %get-tuple-element.47), channel_id=1, source_target_pairs={{0,10},{1,11},{2,8},{3,9},{4,14},{5,15},{6,12},{7,13},{8,2},{9,3},... | collective-permute-start | bytes 221192 | tf_op jit(solution)/shard_map/ppermute | solution.py:413
  21.0 2.0 %collective-permute-start.9 = (bf16[2,144,128]{2,1,0:T(8,128)(2,1)S(1)}, bf16[2,144,128]{2,1,0:T(8,128)(2,1)S(1)}, u32[]{:S(2)}, u32[]{:S(2)}) collective-permute-start(bf16[2,144,128]{2,1,0:T(8,128)(2,1)S(1)} %get-tuple-element.48), channel_id=1, source_target_pairs={{0,12},{1,13},{2,14},{3,15},{4,8},{5,9},{6,10},{7,11},{8,4},{9,5},... | collective-permute-start | bytes 221192 | tf_op jit(solution)/shard_map/ppermute | solution.py:413
  23.0 2.8 %collective-permute-start.10 = (bf16[2,144,128]{2,1,0:T(8,128)(2,1)S(1)}, bf16[2,144,128]{2,1,0:T(8,128)(2,1)S(1)}, u32[]{:S(2)}, u32[]{:S(2)}) collective-permute-start(bf16[2,144,128]{2,1,0:T(8,128)(2,1)S(1)} %get-tuple-element.49), channel_id=1, source_target_pairs={{0,14},{1,15},{2,12},{3,13},{4,10},{5,11},{6,8},{7,9},{8,6},{9,7},... | collective-permute-start | bytes 221192 | tf_op jit(solution)/shard_map/ppermute | solution.py:413
  25.9 1.7 %flip.1.flip_ref = bf16[4,1536,512]{2,1,0:T(8,128)(2,1)S(1)} custom-call(bf16[4,576,1536]{2,1,0:T(8,128)(2,1)S(1)} %bitcast.5, bf16[4,144,128]{2,1,0:T(8,128)(2,1)S(1)} %forward.2.after_ref), custom_call_target="tpu_custom_call" | custom-call | flops 4600000000 | tf_op jit(solution)/shard_map/flip/pallas_call | solution.py:37
  28.1 2.4 %collective-permute-done.8.refs_1_ = bf16[2,144,128]{2,1,0:T(8,128)(2,1)S(1)} collective-permute-done((bf16[2,144,128]{2,1,0:T(8,128)(2,1)S(1)}, bf16[2,144,128]{2,1,0:T(8,128)(2,1)S(1)}, u32[]{:S(2)}, u32[]{:S(2)}) %collective-permute-start.8) | collective-permute-done | bytes 73760 | tf_op jit(solution)/shard_map/ppermute | solution.py:413
  30.6 1.2 %collective-permute-done.11.refs_5_ = bf16[4,144,128]{2,1,0:T(8,128)(2,1)S(1)} collective-permute-done((bf16[4,144,128]{2,1,0:T(8,128)(2,1)S(1)}, bf16[4,144,128]{2,1,0:T(8,128)(2,1)S(1)}, u32[]{:S(2)}, u32[]{:S(2)}) %collective-permute-start.11) | collective-permute-done | bytes 147488 | tf_op jit(solution)/shard_map/ppermute | solution.py:413
  31.8 3.4 %attend.1 = (bf16[2,32,512]{2,1,0:T(8,128)(2,1)S(1)}, bf16[2,32,512]{2,1,0:T(8,128)(2,1)S(1)}, bf16[2,32,512]{2,1,0:T(8,128)(2,1)S(1)}, bf16[2,32,512]{2,1,0:T(8...) custom-call(s32[4]{0:T(128)S(1)} %copy-done.5, ...), custom_call_target="tpu_custom_call" | custom-call | flops 11500000256 | tf_op jit(solution)/shard_map/attend/pallas_call | solution.py:37
  35.2 0.8 %collective-permute-start.16 = (bf16[4,32,512]{2,1,0:T(8,128)(2,1)S(1)}, bf16[4,32,512]{2,1,0:T(8,128)(2,1)S(1)}, u32[]{:S(2)}, u32[]{:S(2)}) collective-permute-start(bf16[4,32,512]{2,1,0:T(8,128)(2,1)S(1)} %get-tuple-element.55), channel_id=1, source_target_pairs={{0,2},{1,3},{2,0},{3,1},{4,6},{5,7},{6,4},{7,5},{8,10},{9,11},{10,... | collective-permute-start | bytes 393224 | tf_op jit(solution)/shard_map/ppermute | solution.py:413
  36.0 2.5 %collective-permute-start.12 = (bf16[2,32,512]{2,1,0:T(8,128)(2,1)S(1)}, bf16[2,32,512]{2,1,0:T(8,128)(2,1)S(1)}, u32[]{:S(2)}, u32[]{:S(2)}) collective-permute-start(bf16[2,32,512]{2,1,0:T(8,128)(2,1)S(1)} %get-tuple-element.51), channel_id=1, source_target_pairs={{0,8},{1,9},{2,10},{3,11},{4,12},{5,13},{6,14},{7,15},{8,0},{9,1},... | collective-permute-start | bytes 196616 | tf_op jit(solution)/shard_map/ppermute | solution.py:413
  38.5 1.1 %collective-permute-start.13 = (bf16[2,32,512]{2,1,0:T(8,128)(2,1)S(1)}, bf16[2,32,512]{2,1,0:T(8,128)(2,1)S(1)}, u32[]{:S(2)}, u32[]{:S(2)}) collective-permute-start(bf16[2,32,512]{2,1,0:T(8,128)(2,1)S(1)} %get-tuple-element.52), channel_id=1, source_target_pairs={{0,10},{1,11},{2,8},{3,9},{4,14},{5,15},{6,12},{7,13},{8,2},{9,3},... | collective-permute-start | bytes 196616 | tf_op jit(solution)/shard_map/ppermute | solution.py:413
  39.7 2.6 %collective-permute-start.14 = (bf16[2,32,512]{2,1,0:T(8,128)(2,1)S(1)}, bf16[2,32,512]{2,1,0:T(8,128)(2,1)S(1)}, u32[]{:S(2)}, u32[]{:S(2)}) collective-permute-start(bf16[2,32,512]{2,1,0:T(8,128)(2,1)S(1)} %get-tuple-element.53), channel_id=1, source_target_pairs={{0,12},{1,13},{2,14},{3,15},{4,8},{5,9},{6,10},{7,11},{8,4},{9,5},... | collective-permute-start | bytes 196616 | tf_op jit(solution)/shard_map/ppermute | solution.py:413
  42.3 1.3 %collective-permute-start.15 = (bf16[2,32,512]{2,1,0:T(8,128)(2,1)S(1)}, bf16[2,32,512]{2,1,0:T(8,128)(2,1)S(1)}, u32[]{:S(2)}, u32[]{:S(2)}) collective-permute-start(bf16[2,32,512]{2,1,0:T(8,128)(2,1)S(1)} %get-tuple-element.54), channel_id=1, source_target_pairs={{0,14},{1,15},{2,12},{3,13},{4,10},{5,11},{6,8},{7,9},{8,6},{9,7},... | collective-permute-start | bytes 196616 | tf_op jit(solution)/shard_map/ppermute | solution.py:413
  43.9 4.3 %collective-permute-done.13.refs_1_ = bf16[2,32,512]{2,1,0:T(8,128)(2,1)S(1)} collective-permute-done((bf16[2,32,512]{2,1,0:T(8,128)(2,1)S(1)}, bf16[2,32,512]{2,1,0:T(8,128)(2,1)S(1)}, u32[]{:S(2)}, u32[]{:S(2)}) %collective-permute-start.13) | collective-permute-done | bytes 65568 | tf_op jit(solution)/shard_map/ppermute | solution.py:413
  48.2 1.2 %collective-permute-done.15.refs_3_ = bf16[2,32,512]{2,1,0:T(8,128)(2,1)S(1)} collective-permute-done((bf16[2,32,512]{2,1,0:T(8,128)(2,1)S(1)}, bf16[2,32,512]{2,1,0:T(8,128)(2,1)S(1)}, u32[]{:S(2)}, u32[]{:S(2)}) %collective-permute-start.15) | collective-permute-done | bytes 65568 | tf_op jit(solution)/shard_map/ppermute | solution.py:413
  49.6 1.5 %collective-permute-done.18.refs_7_ = bf16[8,32,512]{2,1,0:T(8,128)(2,1)S(1)} collective-permute-done((bf16[8,32,512]{2,1,0:T(8,128)(2,1)S(1)}, bf16[8,32,512]{2,1,0:T(8,128)(2,1)S(1)}, u32[]{:S(2)}, u32[]{:S(2)}) %collective-permute-start.18) | collective-permute-done | bytes 262176 | tf_op jit(solution)/shard_map/ppermute | solution.py:413
  51.6 1.4 %terms.3 = (f32[32,3584]{1,0:T(8,128)S(1)}, bf16[32,3584]{1,0:T(8,128)(2,1)S(1)}) custom-call(bf16[64,1024]{1,0:T(8,128)(2,1)S(1)} %values.1.val_ref, bf16[1024,7168]{1,0:T(8,128)(2,1)S(1)} %bitcast.2), custom_call_target="tpu_custom_call" | custom-call | flops 6899999744 | tf_op jit(solution)/shard_map/terms/pallas_call | solution.py:37
  53.2 1.4 %terms.2 = (f32[32,3584]{1,0:T(8,128)S(1)}, bf16[32,3584]{1,0:T(8,128)(2,1)S(1)}) custom-call(bf16[64,1024]{1,0:T(8,128)(2,1)S(1)} %values.1.val_ref, bf16[1024,7168]{1,0:T(8,128)(2,1)S(1)} %bitcast.2), custom_call_target="tpu_custom_call" | custom-call | flops 6899999744 | tf_op jit(solution)/shard_map/terms/pallas_call | solution.py:37
  55.1 1.6 %collective-permute-start.24 = (bf16[8,3584]{1,0:T(8,128)(2,1)S(1)}, bf16[8,3584]{1,0:T(8,128)(2,1)S(1)}, u32[]{:S(2)}, u32[]{:S(2)}) collective-permute-start(bf16[8,3584]{1,0:T(8,128)(2,1)S(1)} %get-tuple-element.69), channel_id=1, source_target_pairs={{0,2},{1,3},{2,0},{3,1},{4,6},{5,7},{6,4},{7,5},{8,10},{9,11},{10,... | collective-permute-start | bytes 172040 | tf_op jit(solution)/shard_map/ppermute | solution.py:413
  56.8 1.0 %collective-permute-start.25 = (bf16[8,3584]{1,0:T(8,128)(2,1)S(1)}, bf16[8,3584]{1,0:T(8,128)(2,1)S(1)}, u32[]{:S(2)}, u32[]{:S(2)}) collective-permute-start(bf16[8,3584]{1,0:T(8,128)(2,1)S(1)} %get-tuple-element.70), channel_id=1, source_target_pairs={{0,2},{1,3},{2,0},{3,1},{4,6},{5,7},{6,4},{7,5},{8,10},{9,11},{10,... | collective-permute-start | bytes 172040 | tf_op jit(solution)/shard_map/ppermute | solution.py:413
  57.9 1.3 %collective-permute-start.21 = (bf16[4,7168]{1,0:T(4,128)(2,1)S(1)}, bf16[4,7168]{1,0:T(4,128)(2,1)S(1)}, u32[]{:S(2)}, u32[]{:S(2)}) collective-permute-start(bf16[4,7168]{1,0:T(4,128)(2,1)S(1)} %get-tuple-element.64), channel_id=1, source_target_pairs={{0,4},{1,5},{2,6},{3,7},{4,0},{5,1},{6,2},{7,3},{8,12},{9,13},{10,... | collective-permute-start | bytes 172040 | tf_op jit(solution)/shard_map/ppermute | solution.py:413
  59.2 1.2 %collective-permute-start.22 = (bf16[4,7168]{1,0:T(4,128)(2,1)S(1)}, bf16[4,7168]{1,0:T(4,128)(2,1)S(1)}, u32[]{:S(2)}, u32[]{:S(2)}) collective-permute-start(bf16[4,7168]{1,0:T(4,128)(2,1)S(1)} %get-tuple-element.65), channel_id=1, source_target_pairs={{0,6},{1,7},{2,4},{3,5},{4,2},{5,3},{6,0},{7,1},{8,14},{9,15},{10,... | collective-permute-start | bytes 172040 | tf_op jit(solution)/shard_map/ppermute | solution.py:413
  60.4 1.0 %collective-permute-start.23 = (bf16[4,7168]{1,0:T(4,128)(2,1)S(1)}, bf16[4,7168]{1,0:T(4,128)(2,1)S(1)}, u32[]{:S(2)}, u32[]{:S(2)}) collective-permute-start(bf16[4,7168]{1,0:T(4,128)(2,1)S(1)} %get-tuple-element.66), channel_id=1, source_target_pairs={{0,2},{1,3},{2,0},{3,1},{4,6},{5,7},{6,4},{7,5},{8,10},{9,11},{10,... | collective-permute-start | bytes 172040 | tf_op jit(solution)/shard_map/ppermute | solution.py:413
  61.4 2.2 %collective-permute-start.26 = (bf16[4,7168]{1,0:T(4,128)(2,1)S(1)}, bf16[4,7168]{1,0:T(4,128)(2,1)S(1)}, u32[]{:S(2)}, u32[]{:S(2)}) collective-permute-start(bf16[4,7168]{1,0:T(4,128)(2,1)S(1)} %get-tuple-element.71), channel_id=1, source_target_pairs={{0,12},{1,13},{2,14},{3,15},{4,8},{5,9},{6,10},{7,11},{8,4},{9,5},... | collective-permute-start | bytes 172040 | tf_op jit(solution)/shard_map/ppermute | solution.py:413
  64.9 2.6 %collective-permute-done.26.refs_4_ = bf16[4,7168]{1,0:T(4,128)(2,1)S(1)} collective-permute-done((bf16[4,7168]{1,0:T(4,128)(2,1)S(1)}, bf16[4,7168]{1,0:T(4,128)(2,1)S(1)}, u32[]{:S(2)}, u32[]{:S(2)}) %collective-permute-start.26) | collective-permute-done | bytes 57376 | tf_op jit(solution)/shard_map/ppermute | solution.py:413
  67.5 1.9 %collective-permute-done.27.refs_5_ = bf16[4,7168]{1,0:T(4,128)(2,1)S(1)} collective-permute-done((bf16[4,7168]{1,0:T(4,128)(2,1)S(1)}, bf16[4,7168]{1,0:T(4,128)(2,1)S(1)}, u32[]{:S(2)}, u32[]{:S(2)}) %collective-permute-start.27) | collective-permute-done | bytes 57376 | tf_op jit(solution)/shard_map/ppermute | solution.py:413
  (71 shorter events, 7.0 us)
Async XLA Ops:
  0.0 14.2 %collective-permute-start.4 = (bf16[1536,1536]{1,0:T(8,128)(2,1)}, bf16[1536,1536]{1,0:T(8,128)(2,1)S(1)}, u32[]{:S(2)}, u32[]{:S(2)}) collective-permute-start(bf16[1536,1536]{1,0:T(8,128)(2,1)} %refs_4_.1), channel_id=1, source_target_pairs={{0,1},{1,0},{2,3},{3,2},{4,5},{5,4},{6,7},{7,6},{8,9},{9,8},{10,11... | collective-permute-start | bytes 14155784 | tf_op jit(solution)/shard_map/ppermute | solution.py:413
  0.5 13.7 %collective-permute-start.5 = (bf16[8,128,512]{2,1,0:T(8,128)(2,1)}, bf16[8,128,512]{2,1,0:T(8,128)(2,1)S(1)}, u32[]{:S(2)}, u32[]{:S(2)}) collective-permute-start(bf16[8,128,512]{2,1,0:T(8,128)(2,1)} %refs_5_.1), channel_id=1, source_target_pairs={{0,1},{1,0},{2,3},{3,2},{4,5},{5,4},{6,7},{7,6},{8,9},{9,8},{10,11... | collective-permute-start | bytes 3145736 | tf_op jit(solution)/shard_map/ppermute | solution.py:413
  0.5 4.8 %collective-permute-start = (bf16[4,1536]{1,0:T(4,128)(2,1)}, bf16[4,1536]{1,0:T(4,128)(2,1)S(1)}, u32[]{:S(2)}, u32[]{:S(2)}) collective-permute-start(bf16[4,1536]{1,0:T(4,128)(2,1)} %refs_0_.1), channel_id=1, source_target_pairs={{0,2},{1,3},{2,0},{3,1},{4,6},{5,7},{6,4},{7,5},{8,10},{9,11},{10,... | collective-permute-start | bytes 36872 | tf_op jit(solution)/shard_map/ppermute | solution.py:413
  4.1 10.1 %slice-start.6 = ((s8[4718592]{0:T(1024)(128)(4,1)}), s8[4194304]{0:T(1024)(128)(4,1)S(1)}, s32[]{:S(2)}) async-start(s8[4718592]{0:T(1024)(128)(4,1)} %bitcast.7), calls=%async_computation.6 | async-start | bytes 8388608
  5.4 8.9 %copy-start = (bf16[8,128,512]{2,1,0:T(8,128)(2,1)S(1)}, bf16[8,128,512]{2,1,0:T(8,128)(2,1)}, u32[]{:S(2)}) copy-start(bf16[8,128,512]{2,1,0:T(8,128)(2,1)} %refs_5_.1) | copy-start | bytes 3145732
  5.4 20.5 %slice-start.4 = ((s8[7077888]{0:T(1024)(128)(4,1)}), s8[4194304]{0:T(1024)(128)(4,1)S(1)}, s32[]{:S(2)}) async-start(s8[7077888]{0:T(1024)(128)(4,1)} %bitcast.3), calls=%async_computation.4 | async-start | bytes 8388608
  5.4 20.5 %slice-start.5 = ((s8[7077888]{0:T(1024)(128)(4,1)}), s8[2883584]{0:T(1024)(128)(4,1)S(1)}, s32[]{:S(2)}) async-start(s8[7077888]{0:T(1024)(128)(4,1)} %bitcast.3), calls=%async_computation.5 | async-start | bytes 5767168
  5.4 5.0 %collective-permute-start.3 = (bf16[8,1536]{1,0:T(8,128)(2,1)S(1)}, bf16[8,1536]{1,0:T(8,128)(2,1)S(1)}, u32[]{:S(2)}, u32[]{:S(2)}) collective-permute-start(bf16[8,1536]{1,0:T(8,128)(2,1)S(1)} %get-tuple-element.43.refs_0_), channel_id=1, source_target_pairs={{0,8},{1,9},{2,10},{3,11},{4,12},{5,13},{6,14},{7,15},{8,0},{9,1},... | collective-permute-start | bytes 73736 | tf_op jit(solution)/shard_map/ppermute | solution.py:413
  8.6 5.6 %collective-permute-start.2 = (bf16[8,1536]{1,0:T(8,128)(2,1)S(1)}, bf16[8,1536]{1,0:T(8,128)(2,1)S(1)}, u32[]{:S(2)}, u32[]{:S(2)}) collective-permute-start(bf16[8,1536]{1,0:T(8,128)(2,1)S(1)} %get-tuple-element.43.refs_0_), channel_id=1, source_target_pairs={{0,12},{1,13},{2,14},{3,15},{4,8},{5,9},{6,10},{7,11},{8,4},{9,5},... | collective-permute-start | bytes 73736 | tf_op jit(solution)/shard_map/ppermute | solution.py:413
  9.9 4.3 %collective-permute-start.1 = (bf16[8,1536]{1,0:T(8,128)(2,1)S(1)}, bf16[8,1536]{1,0:T(8,128)(2,1)S(1)}, u32[]{:S(2)}, u32[]{:S(2)}) collective-permute-start(bf16[8,1536]{1,0:T(8,128)(2,1)S(1)} %get-tuple-element.43.refs_0_), channel_id=1, source_target_pairs={{0,4},{1,5},{2,6},{3,7},{4,0},{5,1},{6,2},{7,3},{8,12},{9,13},{10,... | collective-permute-start | bytes 73736 | tf_op jit(solution)/shard_map/ppermute | solution.py:413
  16.5 9.2 %collective-permute-start.6 = (bf16[4,144,128]{2,1,0:T(8,128)(2,1)S(1)}, bf16[4,144,128]{2,1,0:T(8,128)(2,1)S(1)}, u32[]{:S(2)}, u32[]{:S(2)}) collective-permute-start(bf16[4,144,128]{2,1,0:T(8,128)(2,1)S(1)} %get-tuple-element.45), channel_id=1, source_target_pairs={{0,2},{1,3},{2,0},{3,1},{4,6},{5,7},{6,4},{7,5},{8,10},{9,11},{10,... | collective-permute-start | bytes 442376 | tf_op jit(solution)/shard_map/ppermute | solution.py:413
  18.1 10.0 %collective-permute-start.7 = (bf16[2,144,128]{2,1,0:T(8,128)(2,1)S(1)}, bf16[2,144,128]{2,1,0:T(8,128)(2,1)S(1)}, u32[]{:S(2)}, u32[]{:S(2)}) collective-permute-start(bf16[2,144,128]{2,1,0:T(8,128)(2,1)S(1)} %get-tuple-element.46), channel_id=1, source_target_pairs={{0,8},{1,9},{2,10},{3,11},{4,12},{5,13},{6,14},{7,15},{8,0},{9,1},... | collective-permute-start | bytes 221192 | tf_op jit(solution)/shard_map/ppermute | solution.py:413
  19.4 11.2 %collective-permute-start.8 = (bf16[2,144,128]{2,1,0:T(8,128)(2,1)S(1)}, bf16[2,144,128]{2,1,0:T(8,128)(2,1)S(1)}, u32[]{:S(2)}, u32[]{:S(2)}) collective-permute-start(bf16[2,144,128]{2,1,0:T(8,128)(2,1)S(1)} %get-tuple-element.47), channel_id=1, source_target_pairs={{0,10},{1,11},{2,8},{3,9},{4,14},{5,15},{6,12},{7,13},{8,2},{9,3},... | collective-permute-start | bytes 221192 | tf_op jit(solution)/shard_map/ppermute | solution.py:413
  21.0 9.6 %collective-permute-start.9 = (bf16[2,144,128]{2,1,0:T(8,128)(2,1)S(1)}, bf16[2,144,128]{2,1,0:T(8,128)(2,1)S(1)}, u32[]{:S(2)}, u32[]{:S(2)}) collective-permute-start(bf16[2,144,128]{2,1,0:T(8,128)(2,1)S(1)} %get-tuple-element.48), channel_id=1, source_target_pairs={{0,12},{1,13},{2,14},{3,15},{4,8},{5,9},{6,10},{7,11},{8,4},{9,5},... | collective-permute-start | bytes 221192 | tf_op jit(solution)/shard_map/ppermute | solution.py:413
  23.0 7.6 %collective-permute-start.10 = (bf16[2,144,128]{2,1,0:T(8,128)(2,1)S(1)}, bf16[2,144,128]{2,1,0:T(8,128)(2,1)S(1)}, u32[]{:S(2)}, u32[]{:S(2)}) collective-permute-start(bf16[2,144,128]{2,1,0:T(8,128)(2,1)S(1)} %get-tuple-element.49), channel_id=1, source_target_pairs={{0,14},{1,15},{2,12},{3,13},{4,10},{5,11},{6,8},{7,9},{8,6},{9,7},... | collective-permute-start | bytes 221192 | tf_op jit(solution)/shard_map/ppermute | solution.py:413
  25.8 6.0 %collective-permute-start.11 = (bf16[4,144,128]{2,1,0:T(8,128)(2,1)S(1)}, bf16[4,144,128]{2,1,0:T(8,128)(2,1)S(1)}, u32[]{:S(2)}, u32[]{:S(2)}) collective-permute-start(bf16[4,144,128]{2,1,0:T(8,128)(2,1)S(1)} %forward.2.after_ref), channel_id=1, source_target_pairs={{0,4},{1,5},{2,6},{3,7},{4,0},{5,1},{6,2},{7,3},{8,12},{9,13},{10,... | collective-permute-start | bytes 442376 | tf_op jit(solution)/shard_map/ppermute | solution.py:413
  35.2 8.4 %collective-permute-start.16 = (bf16[4,32,512]{2,1,0:T(8,128)(2,1)S(1)}, bf16[4,32,512]{2,1,0:T(8,128)(2,1)S(1)}, u32[]{:S(2)}, u32[]{:S(2)}) collective-permute-start(bf16[4,32,512]{2,1,0:T(8,128)(2,1)S(1)} %get-tuple-element.55), channel_id=1, source_target_pairs={{0,2},{1,3},{2,0},{3,1},{4,6},{5,7},{6,4},{7,5},{8,10},{9,11},{10,... | collective-permute-start | bytes 393224 | tf_op jit(solution)/shard_map/ppermute | solution.py:413
  36.0 7.9 %collective-permute-start.12 = (bf16[2,32,512]{2,1,0:T(8,128)(2,1)S(1)}, bf16[2,32,512]{2,1,0:T(8,128)(2,1)S(1)}, u32[]{:S(2)}, u32[]{:S(2)}) collective-permute-start(bf16[2,32,512]{2,1,0:T(8,128)(2,1)S(1)} %get-tuple-element.51), channel_id=1, source_target_pairs={{0,8},{1,9},{2,10},{3,11},{4,12},{5,13},{6,14},{7,15},{8,0},{9,1},... | collective-permute-start | bytes 196616 | tf_op jit(solution)/shard_map/ppermute | solution.py:413
  38.5 9.7 %collective-permute-start.13 = (bf16[2,32,512]{2,1,0:T(8,128)(2,1)S(1)}, bf16[2,32,512]{2,1,0:T(8,128)(2,1)S(1)}, u32[]{:S(2)}, u32[]{:S(2)}) collective-permute-start(bf16[2,32,512]{2,1,0:T(8,128)(2,1)S(1)} %get-tuple-element.52), channel_id=1, source_target_pairs={{0,10},{1,11},{2,8},{3,9},{4,14},{5,15},{6,12},{7,13},{8,2},{9,3},... | collective-permute-start | bytes 196616 | tf_op jit(solution)/shard_map/ppermute | solution.py:413
  39.7 8.6 %collective-permute-start.14 = (bf16[2,32,512]{2,1,0:T(8,128)(2,1)S(1)}, bf16[2,32,512]{2,1,0:T(8,128)(2,1)S(1)}, u32[]{:S(2)}, u32[]{:S(2)}) collective-permute-start(bf16[2,32,512]{2,1,0:T(8,128)(2,1)S(1)} %get-tuple-element.53), channel_id=1, source_target_pairs={{0,12},{1,13},{2,14},{3,15},{4,8},{5,9},{6,10},{7,11},{8,4},{9,5},... | collective-permute-start | bytes 196616 | tf_op jit(solution)/shard_map/ppermute | solution.py:413
  42.3 7.1 %collective-permute-start.15 = (bf16[2,32,512]{2,1,0:T(8,128)(2,1)S(1)}, bf16[2,32,512]{2,1,0:T(8,128)(2,1)S(1)}, u32[]{:S(2)}, u32[]{:S(2)}) collective-permute-start(bf16[2,32,512]{2,1,0:T(8,128)(2,1)S(1)} %get-tuple-element.54), channel_id=1, source_target_pairs={{0,14},{1,15},{2,12},{3,13},{4,10},{5,11},{6,8},{7,9},{8,6},{9,7},... | collective-permute-start | bytes 196616 | tf_op jit(solution)/shard_map/ppermute | solution.py:413
  43.7 5.8 %collective-permute-start.17 = (bf16[4,32,512]{2,1,0:T(8,128)(2,1)S(1)}, bf16[4,32,512]{2,1,0:T(8,128)(2,1)S(1)}, u32[]{:S(2)}, u32[]{:S(2)}) collective-permute-start(bf16[4,32,512]{2,1,0:T(8,128)(2,1)S(1)} %forward.3.after_ref), channel_id=1, source_target_pairs={{0,4},{1,5},{2,6},{3,7},{4,0},{5,1},{6,2},{7,3},{8,12},{9,13},{10,... | collective-permute-start | bytes 393224 | tf_op jit(solution)/shard_map/ppermute | solution.py:413
  49.5 1.6 %collective-permute-start.18 = (bf16[8,32,512]{2,1,0:T(8,128)(2,1)S(1)}, bf16[8,32,512]{2,1,0:T(8,128)(2,1)S(1)}, u32[]{:S(2)}, u32[]{:S(2)}) collective-permute-start(bf16[8,32,512]{2,1,0:T(8,128)(2,1)S(1)} %regroup.1), channel_id=1, source_target_pairs={{0,1},{1,0},{2,3},{3,2},{4,5},{5,4},{6,7},{7,6},{8,9},{9,8},{10,11... | collective-permute-start | bytes 786440 | tf_op jit(solution)/shard_map/ppermute | solution.py:413
  53.0 2.0 %collective-permute-start.20 = (bf16[32,3584]{1,0:T(8,128)(2,1)S(1)}, bf16[32,3584]{1,0:T(8,128)(2,1)S(1)}, u32[]{:S(2)}, u32[]{:S(2)}) collective-permute-start(bf16[32,3584]{1,0:T(8,128)(2,1)S(1)} %get-tuple-element.61), channel_id=1, source_target_pairs={{0,1},{1,0},{2,3},{3,2},{4,5},{5,4},{6,7},{7,6},{8,9},{9,8},{10,11... | collective-permute-start | bytes 688136 | tf_op jit(solution)/shard_map/ppermute | solution.py:413
  54.6 2.2 %collective-permute-start.19 = (bf16[32,3584]{1,0:T(8,128)(2,1)S(1)}, bf16[32,3584]{1,0:T(8,128)(2,1)S(1)}, u32[]{:S(2)}, u32[]{:S(2)}) collective-permute-start(bf16[32,3584]{1,0:T(8,128)(2,1)S(1)} %get-tuple-element.59), channel_id=1, source_target_pairs={{0,1},{1,0},{2,3},{3,2},{4,5},{5,4},{6,7},{7,6},{8,9},{9,8},{10,11... | collective-permute-start | bytes 688136 | tf_op jit(solution)/shard_map/ppermute | solution.py:413
  55.1 6.3 %collective-permute-start.24 = (bf16[8,3584]{1,0:T(8,128)(2,1)S(1)}, bf16[8,3584]{1,0:T(8,128)(2,1)S(1)}, u32[]{:S(2)}, u32[]{:S(2)}) collective-permute-start(bf16[8,3584]{1,0:T(8,128)(2,1)S(1)} %get-tuple-element.69), channel_id=1, source_target_pairs={{0,2},{1,3},{2,0},{3,1},{4,6},{5,7},{6,4},{7,5},{8,10},{9,11},{10,... | collective-permute-start | bytes 172040 | tf_op jit(solution)/shard_map/ppermute | solution.py:413
  56.8 4.5 %collective-permute-start.25 = (bf16[8,3584]{1,0:T(8,128)(2,1)S(1)}, bf16[8,3584]{1,0:T(8,128)(2,1)S(1)}, u32[]{:S(2)}, u32[]{:S(2)}) collective-permute-start(bf16[8,3584]{1,0:T(8,128)(2,1)S(1)} %get-tuple-element.70), channel_id=1, source_target_pairs={{0,2},{1,3},{2,0},{3,1},{4,6},{5,7},{6,4},{7,5},{8,10},{9,11},{10,... | collective-permute-start | bytes 172040 | tf_op jit(solution)/shard_map/ppermute | solution.py:413
  57.9 6.4 %collective-permute-start.21 = (bf16[4,7168]{1,0:T(4,128)(2,1)S(1)}, bf16[4,7168]{1,0:T(4,128)(2,1)S(1)}, u32[]{:S(2)}, u32[]{:S(2)}) collective-permute-start(bf16[4,7168]{1,0:T(4,128)(2,1)S(1)} %get-tuple-element.64), channel_id=1, source_target_pairs={{0,4},{1,5},{2,6},{3,7},{4,0},{5,1},{6,2},{7,3},{8,12},{9,13},{10,... | collective-permute-start | bytes 172040 | tf_op jit(solution)/shard_map/ppermute | solution.py:413
  59.2 5.1 %collective-permute-start.22 = (bf16[4,7168]{1,0:T(4,128)(2,1)S(1)}, bf16[4,7168]{1,0:T(4,128)(2,1)S(1)}, u32[]{:S(2)}, u32[]{:S(2)}) collective-permute-start(bf16[4,7168]{1,0:T(4,128)(2,1)S(1)} %get-tuple-element.65), channel_id=1, source_target_pairs={{0,6},{1,7},{2,4},{3,5},{4,2},{5,3},{6,0},{7,1},{8,14},{9,15},{10,... | collective-permute-start | bytes 172040 | tf_op jit(solution)/shard_map/ppermute | solution.py:413
  60.4 4.5 %collective-permute-start.23 = (bf16[4,7168]{1,0:T(4,128)(2,1)S(1)}, bf16[4,7168]{1,0:T(4,128)(2,1)S(1)}, u32[]{:S(2)}, u32[]{:S(2)}) collective-permute-start(bf16[4,7168]{1,0:T(4,128)(2,1)S(1)} %get-tuple-element.66), channel_id=1, source_target_pairs={{0,2},{1,3},{2,0},{3,1},{4,6},{5,7},{6,4},{7,5},{8,10},{9,11},{10,... | collective-permute-start | bytes 172040 | tf_op jit(solution)/shard_map/ppermute | solution.py:413
  61.4 6.1 %collective-permute-start.26 = (bf16[4,7168]{1,0:T(4,128)(2,1)S(1)}, bf16[4,7168]{1,0:T(4,128)(2,1)S(1)}, u32[]{:S(2)}, u32[]{:S(2)}) collective-permute-start(bf16[4,7168]{1,0:T(4,128)(2,1)S(1)} %get-tuple-element.71), channel_id=1, source_target_pairs={{0,12},{1,13},{2,14},{3,15},{4,8},{5,9},{6,10},{7,11},{8,4},{9,5},... | collective-permute-start | bytes 172040 | tf_op jit(solution)/shard_map/ppermute | solution.py:413
  63.6 5.8 %collective-permute-start.27 = (bf16[4,7168]{1,0:T(4,128)(2,1)S(1)}, bf16[4,7168]{1,0:T(4,128)(2,1)S(1)}, u32[]{:S(2)}, u32[]{:S(2)}) collective-permute-start(bf16[4,7168]{1,0:T(4,128)(2,1)S(1)} %get-tuple-element.72), channel_id=1, source_target_pairs={{0,8},{1,9},{2,10},{3,11},{4,12},{5,13},{6,14},{7,15},{8,0},{9,1},... | collective-permute-start | bytes 172040 | tf_op jit(solution)/shard_map/ppermute | solution.py:413
  (10 other events, 59.5 us)

commit v19 on v13

--- a/solution.py
+++ b/solution.py
@@ -218,10 +218,8 @@
         own = jnp.sum(latent * newest[:, :LAT], axis=-1, keepdims=True) + jnp.sum(
             rotated.astype(jnp.float32) * newest[:, LAT:], axis=-1, keepdims=True
         )
-        scores = jnp.dot(
-            latent.astype(jnp.bfloat16), key_ref[r, :LAT, :], preferred_element_type=jnp.float32
-        )
-        scores += jnp.dot(rotated, key_ref[r, LAT:, :], preferred_element_type=jnp.float32)
+        query = jnp.concatenate([latent.astype(jnp.bfloat16), rotated], axis=-1)
+        scores = jnp.dot(query, key_ref[r], preferred_element_type=jnp.float32)
         position = lax.broadcasted_iota(jnp.int32, (1, maxlen), 1)
         return jnp.where(position < len_ref[r], scores, -jnp.inf), own
 

time: 70.1 us -> 70.2 us (level)
  transfers between devices with their start and end apart: 28 -> 28, of which waited for: 12 -> 13; matrix products, arithmetic and copies ran while one was open for 0% -> 0% of each run, Pallas kernels for 6% -> 6%
where the time goes in v19:
time: 70.2 us; the launch traced here: 70 us
  starting transfers between devices  34.2 us (49%)
  waiting for transfers between devices  22.6 us (32%)
  Pallas kernels  12.2 us (17%)
  local copies, waits for them, and re-layouts  0.72 us (1%)
    ppermute x28, starting transfers between devices, swap(): return lax.ppermute(block, 'row', [(i, i ^ k) for i in range(devices)])  34.2 us
    ppermute x28, waiting for transfers between devices, swap(): return lax.ppermute(block, 'row', [(i, i ^ k) for i in range(devices)])  22.6 us
    pallas_call x16, Pallas kernels, run(): pl.pallas_call(kernel, out_shape=out_shape, in_specs=smem + [in_vmem()] *...  12.2 us
  transfers between devices with their start and end apart: 28, of which 13 were waited for; matrix products, arithmetic and copies ran while one was open for 0% of the time, Pallas kernels for 6%

profile of v19, /device:TPU:0, one launch (start us, length us, event | category | flops | bytes accessed | tf_op | source)
XLA Modules:
  0.0 70.0 jit_solution(7664354619626266993)
XLA Ops:
  0.5 3.0 %collective-permute-start = (bf16[4,1536]{1,0:T(4,128)(2,1)}, bf16[4,1536]{1,0:T(4,128)(2,1)S(1)}, u32[]{:S(2)}, u32[]{:S(2)}) collective-permute-start(bf16[4,1536]{1,0:T(4,128)(2,1)} %refs_0_.1), channel_id=1, source_target_pairs={{0,2},{1,3},{2,0},{3,1},{4,6},{5,7},{6,4},{7,5},{8,10},{9,11},{10,... | collective-permute-start | bytes 36872 | tf_op jit(solution)/shard_map/ppermute | solution.py:412
  5.4 3.2 %collective-permute-start.3 = (bf16[8,1536]{1,0:T(8,128)(2,1)S(1)}, bf16[8,1536]{1,0:T(8,128)(2,1)S(1)}, u32[]{:S(2)}, u32[]{:S(2)}) collective-permute-start(bf16[8,1536]{1,0:T(8,128)(2,1)S(1)} %get-tuple-element.43.refs_0_), channel_id=1, source_target_pairs={{0,8},{1,9},{2,10},{3,11},{4,12},{5,13},{6,14},{7,15},{8,0},{9,1},... | collective-permute-start | bytes 73736 | tf_op jit(solution)/shard_map/ppermute | solution.py:412
  8.6 1.3 %collective-permute-start.2 = (bf16[8,1536]{1,0:T(8,128)(2,1)S(1)}, bf16[8,1536]{1,0:T(8,128)(2,1)S(1)}, u32[]{:S(2)}, u32[]{:S(2)}) collective-permute-start(bf16[8,1536]{1,0:T(8,128)(2,1)S(1)} %get-tuple-element.43.refs_0_), channel_id=1, source_target_pairs={{0,12},{1,13},{2,14},{3,15},{4,8},{5,9},{6,10},{7,11},{8,4},{9,5},... | collective-permute-start | bytes 73736 | tf_op jit(solution)/shard_map/ppermute | solution.py:412
  10.4 3.8 %collective-permute-done.2.refs_2_ = bf16[8,1536]{1,0:T(8,128)(2,1)S(1)} collective-permute-done((bf16[8,1536]{1,0:T(8,128)(2,1)S(1)}, bf16[8,1536]{1,0:T(8,128)(2,1)S(1)}, u32[]{:S(2)}, u32[]{:S(2)}) %collective-permute-start.2) | collective-permute-done | bytes 24608 | tf_op jit(solution)/shard_map/ppermute | solution.py:412
  14.2 2.3 %project.1 = (bf16[2,144,128]{2,1,0:T(8,128)(2,1)S(1)}, bf16[2,144,128]{2,1,0:T(8,128)(2,1)S(1)}, bf16[2,144,128]{2,1,0:T(8,128)(2,1)S(1)}, bf16[2,144,128]{2,1,...) custom-call(bf16[8,1536]{1,0:T(8,128)(2,1)S(1)} %get-tuple-element.4, ...), custom_call_target="tpu_custom_call" | custom-call | flops 23000000512 | tf_op jit(solution)/shard_map/project/pallas_call | solution.py:37
  16.5 1.6 %collective-permute-start.6 = (bf16[4,144,128]{2,1,0:T(8,128)(2,1)S(1)}, bf16[4,144,128]{2,1,0:T(8,128)(2,1)S(1)}, u32[]{:S(2)}, u32[]{:S(2)}) collective-permute-start(bf16[4,144,128]{2,1,0:T(8,128)(2,1)S(1)} %get-tuple-element.45), channel_id=1, source_target_pairs={{0,2},{1,3},{2,0},{3,1},{4,6},{5,7},{6,4},{7,5},{8,10},{9,11},{10,... | collective-permute-start | bytes 442376 | tf_op jit(solution)/shard_map/ppermute | solution.py:412
  18.1 1.2 %collective-permute-start.7 = (bf16[2,144,128]{2,1,0:T(8,128)(2,1)S(1)}, bf16[2,144,128]{2,1,0:T(8,128)(2,1)S(1)}, u32[]{:S(2)}, u32[]{:S(2)}) collective-permute-start(bf16[2,144,128]{2,1,0:T(8,128)(2,1)S(1)} %get-tuple-element.46), channel_id=1, source_target_pairs={{0,8},{1,9},{2,10},{3,11},{4,12},{5,13},{6,14},{7,15},{8,0},{9,1},... | collective-permute-start | bytes 221192 | tf_op jit(solution)/shard_map/ppermute | solution.py:412
  19.4 0.9 %collective-permute-start.8 = (bf16[2,144,128]{2,1,0:T(8,128)(2,1)S(1)}, bf16[2,144,128]{2,1,0:T(8,128)(2,1)S(1)}, u32[]{:S(2)}, u32[]{:S(2)}) collective-permute-start(bf16[2,144,128]{2,1,0:T(8,128)(2,1)S(1)} %get-tuple-element.47), channel_id=1, source_target_pairs={{0,14},{1,15},{2,12},{3,13},{4,10},{5,11},{6,8},{7,9},{8,6},{9,7},... | collective-permute-start | bytes 221192 | tf_op jit(solution)/shard_map/ppermute | solution.py:412
  20.2 2.9 %collective-permute-start.9 = (bf16[2,144,128]{2,1,0:T(8,128)(2,1)S(1)}, bf16[2,144,128]{2,1,0:T(8,128)(2,1)S(1)}, u32[]{:S(2)}, u32[]{:S(2)}) collective-permute-start(bf16[2,144,128]{2,1,0:T(8,128)(2,1)S(1)} %get-tuple-element.48), channel_id=1, source_target_pairs={{0,12},{1,13},{2,14},{3,15},{4,8},{5,9},{6,10},{7,11},{8,4},{9,5},... | collective-permute-start | bytes 221192 | tf_op jit(solution)/shard_map/ppermute | solution.py:412
  23.1 0.8 %collective-permute-start.10 = (bf16[2,144,128]{2,1,0:T(8,128)(2,1)S(1)}, bf16[2,144,128]{2,1,0:T(8,128)(2,1)S(1)}, u32[]{:S(2)}, u32[]{:S(2)}) collective-permute-start(bf16[2,144,128]{2,1,0:T(8,128)(2,1)S(1)} %get-tuple-element.49), channel_id=1, source_target_pairs={{0,10},{1,11},{2,8},{3,9},{4,14},{5,15},{6,12},{7,13},{8,2},{9,3},... | collective-permute-start | bytes 221192 | tf_op jit(solution)/shard_map/ppermute | solution.py:412
  24.0 1.7 %collective-permute-start.11 = (bf16[4,144,128]{2,1,0:T(8,128)(2,1)S(1)}, bf16[4,144,128]{2,1,0:T(8,128)(2,1)S(1)}, u32[]{:S(2)}, u32[]{:S(2)}) collective-permute-start(bf16[4,144,128]{2,1,0:T(8,128)(2,1)S(1)} %forward.2.after_ref), channel_id=1, source_target_pairs={{0,4},{1,5},{2,6},{3,7},{4,0},{5,1},{6,2},{7,3},{8,12},{9,13},{10,... | collective-permute-start | bytes 442376 | tf_op jit(solution)/shard_map/ppermute | solution.py:412
  25.7 1.7 %flip.1.flip_ref = bf16[4,1536,512]{2,1,0:T(8,128)(2,1)S(1)} custom-call(bf16[4,576,1536]{2,1,0:T(8,128)(2,1)S(1)} %bitcast.5, bf16[4,144,128]{2,1,0:T(8,128)(2,1)S(1)} %forward.2.after_ref), custom_call_target="tpu_custom_call" | custom-call | flops 4600000000 | tf_op jit(solution)/shard_map/flip/pallas_call | solution.py:37
  27.4 0.9 %collective-permute-done.7.refs_0_ = bf16[2,144,128]{2,1,0:T(8,128)(2,1)S(1)} collective-permute-done((bf16[2,144,128]{2,1,0:T(8,128)(2,1)S(1)}, bf16[2,144,128]{2,1,0:T(8,128)(2,1)S(1)}, u32[]{:S(2)}, u32[]{:S(2)}) %collective-permute-start.7) | collective-permute-done | bytes 73760 | tf_op jit(solution)/shard_map/ppermute | solution.py:412
  28.3 4.4 %collective-permute-done.10.refs_3_ = bf16[2,144,128]{2,1,0:T(8,128)(2,1)S(1)} collective-permute-done((bf16[2,144,128]{2,1,0:T(8,128)(2,1)S(1)}, bf16[2,144,128]{2,1,0:T(8,128)(2,1)S(1)}, u32[]{:S(2)}, u32[]{:S(2)}) %collective-permute-start.10) | collective-permute-done | bytes 73760 | tf_op jit(solution)/shard_map/ppermute | solution.py:412
  32.7 3.5 %attend.1 = (bf16[2,32,512]{2,1,0:T(8,128)(2,1)S(1)}, bf16[2,32,512]{2,1,0:T(8,128)(2,1)S(1)}, bf16[2,32,512]{2,1,0:T(8,128)(2,1)S(1)}, bf16[2,32,512]{2,1,0:T(8...) custom-call(s32[4]{0:T(128)S(1)} %copy-done.5, ...), custom_call_target="tpu_custom_call" | custom-call | flops 11500000256 | tf_op jit(solution)/shard_map/attend/pallas_call | solution.py:37
  36.9 2.6 %collective-permute-start.13 = (bf16[2,32,512]{2,1,0:T(8,128)(2,1)S(1)}, bf16[2,32,512]{2,1,0:T(8,128)(2,1)S(1)}, u32[]{:S(2)}, u32[]{:S(2)}) collective-permute-start(bf16[2,32,512]{2,1,0:T(8,128)(2,1)S(1)} %get-tuple-element.52), channel_id=1, source_target_pairs={{0,14},{1,15},{2,12},{3,13},{4,10},{5,11},{6,8},{7,9},{8,6},{9,7},... | collective-permute-start | bytes 196616 | tf_op jit(solution)/shard_map/ppermute | solution.py:412
  39.5 2.2 %collective-permute-start.14 = (bf16[2,32,512]{2,1,0:T(8,128)(2,1)S(1)}, bf16[2,32,512]{2,1,0:T(8,128)(2,1)S(1)}, u32[]{:S(2)}, u32[]{:S(2)}) collective-permute-start(bf16[2,32,512]{2,1,0:T(8,128)(2,1)S(1)} %get-tuple-element.53), channel_id=1, source_target_pairs={{0,12},{1,13},{2,14},{3,15},{4,8},{5,9},{6,10},{7,11},{8,4},{9,5},... | collective-permute-start | bytes 196616 | tf_op jit(solution)/shard_map/ppermute | solution.py:412
  41.7 1.0 %collective-permute-start.15 = (bf16[2,32,512]{2,1,0:T(8,128)(2,1)S(1)}, bf16[2,32,512]{2,1,0:T(8,128)(2,1)S(1)}, u32[]{:S(2)}, u32[]{:S(2)}) collective-permute-start(bf16[2,32,512]{2,1,0:T(8,128)(2,1)S(1)} %get-tuple-element.54), channel_id=1, source_target_pairs={{0,10},{1,11},{2,8},{3,9},{4,14},{5,15},{6,12},{7,13},{8,2},{9,3},... | collective-permute-start | bytes 196616 | tf_op jit(solution)/shard_map/ppermute | solution.py:412
  42.7 2.2 %collective-permute-start.17 = (bf16[4,32,512]{2,1,0:T(8,128)(2,1)S(1)}, bf16[4,32,512]{2,1,0:T(8,128)(2,1)S(1)}, u32[]{:S(2)}, u32[]{:S(2)}) collective-permute-start(bf16[4,32,512]{2,1,0:T(8,128)(2,1)S(1)} %forward.3.after_ref), channel_id=1, source_target_pairs={{0,4},{1,5},{2,6},{3,7},{4,0},{5,1},{6,2},{7,3},{8,12},{9,13},{10,... | collective-permute-start | bytes 393224 | tf_op jit(solution)/shard_map/ppermute | solution.py:412
  44.9 1.4 %collective-permute-done.12.refs_0_ = bf16[2,32,512]{2,1,0:T(8,128)(2,1)S(1)} collective-permute-done((bf16[2,32,512]{2,1,0:T(8,128)(2,1)S(1)}, bf16[2,32,512]{2,1,0:T(8,128)(2,1)S(1)}, u32[]{:S(2)}, u32[]{:S(2)}) %collective-permute-start.12) | collective-permute-done | bytes 65568 | tf_op jit(solution)/shard_map/ppermute | solution.py:412
  46.3 4.1 %collective-permute-done.15.refs_3_ = bf16[2,32,512]{2,1,0:T(8,128)(2,1)S(1)} collective-permute-done((bf16[2,32,512]{2,1,0:T(8,128)(2,1)S(1)}, bf16[2,32,512]{2,1,0:T(8,128)(2,1)S(1)}, u32[]{:S(2)}, u32[]{:S(2)}) %collective-permute-start.15) | collective-permute-done | bytes 65568 | tf_op jit(solution)/shard_map/ppermute | solution.py:412
  50.5 1.5 %collective-permute-done.18.refs_7_ = bf16[8,32,512]{2,1,0:T(8,128)(2,1)S(1)} collective-permute-done((bf16[8,32,512]{2,1,0:T(8,128)(2,1)S(1)}, bf16[8,32,512]{2,1,0:T(8,128)(2,1)S(1)}, u32[]{:S(2)}, u32[]{:S(2)}) %collective-permute-start.18) | collective-permute-done | bytes 262176 | tf_op jit(solution)/shard_map/ppermute | solution.py:412
  52.6 1.4 %terms.3 = (f32[32,3584]{1,0:T(8,128)S(1)}, bf16[32,3584]{1,0:T(8,128)(2,1)S(1)}) custom-call(bf16[64,1024]{1,0:T(8,128)(2,1)S(1)} %values.1.val_ref, bf16[1024,7168]{1,0:T(8,128)(2,1)S(1)} %bitcast.2), custom_call_target="tpu_custom_call" | custom-call | flops 6899999744 | tf_op jit(solution)/shard_map/terms/pallas_call | solution.py:37
  54.1 1.4 %terms.2 = (f32[32,3584]{1,0:T(8,128)S(1)}, bf16[32,3584]{1,0:T(8,128)(2,1)S(1)}) custom-call(bf16[64,1024]{1,0:T(8,128)(2,1)S(1)} %values.1.val_ref, bf16[1024,7168]{1,0:T(8,128)(2,1)S(1)} %bitcast.2), custom_call_target="tpu_custom_call" | custom-call | flops 6899999744 | tf_op jit(solution)/shard_map/terms/pallas_call | solution.py:37
  56.0 1.0 %collective-permute-start.24 = (bf16[8,3584]{1,0:T(8,128)(2,1)S(1)}, bf16[8,3584]{1,0:T(8,128)(2,1)S(1)}, u32[]{:S(2)}, u32[]{:S(2)}) collective-permute-start(bf16[8,3584]{1,0:T(8,128)(2,1)S(1)} %get-tuple-element.69), channel_id=1, source_target_pairs={{0,2},{1,3},{2,0},{3,1},{4,6},{5,7},{6,4},{7,5},{8,10},{9,11},{10,... | collective-permute-start | bytes 172040 | tf_op jit(solution)/shard_map/ppermute | solution.py:412
  57.2 1.1 %collective-permute-start.25 = (bf16[8,3584]{1,0:T(8,128)(2,1)S(1)}, bf16[8,3584]{1,0:T(8,128)(2,1)S(1)}, u32[]{:S(2)}, u32[]{:S(2)}) collective-permute-start(bf16[8,3584]{1,0:T(8,128)(2,1)S(1)} %get-tuple-element.70), channel_id=1, source_target_pairs={{0,2},{1,3},{2,0},{3,1},{4,6},{5,7},{6,4},{7,5},{8,10},{9,11},{10,... | collective-permute-start | bytes 172040 | tf_op jit(solution)/shard_map/ppermute | solution.py:412
  58.3 2.4 %collective-permute-start.22 = (bf16[4,7168]{1,0:T(4,128)(2,1)S(1)}, bf16[4,7168]{1,0:T(4,128)(2,1)S(1)}, u32[]{:S(2)}, u32[]{:S(2)}) collective-permute-start(bf16[4,7168]{1,0:T(4,128)(2,1)S(1)} %get-tuple-element.65), channel_id=1, source_target_pairs={{0,6},{1,7},{2,4},{3,5},{4,2},{5,3},{6,0},{7,1},{8,14},{9,15},{10,... | collective-permute-start | bytes 172040 | tf_op jit(solution)/shard_map/ppermute | solution.py:412
  60.7 1.0 %collective-permute-start.23 = (bf16[4,7168]{1,0:T(4,128)(2,1)S(1)}, bf16[4,7168]{1,0:T(4,128)(2,1)S(1)}, u32[]{:S(2)}, u32[]{:S(2)}) collective-permute-start(bf16[4,7168]{1,0:T(4,128)(2,1)S(1)} %get-tuple-element.66), channel_id=1, source_target_pairs={{0,2},{1,3},{2,0},{3,1},{4,6},{5,7},{6,4},{7,5},{8,10},{9,11},{10,... | collective-permute-start | bytes 172040 | tf_op jit(solution)/shard_map/ppermute | solution.py:412
  61.8 1.9 %collective-permute-start.26 = (bf16[4,7168]{1,0:T(4,128)(2,1)S(1)}, bf16[4,7168]{1,0:T(4,128)(2,1)S(1)}, u32[]{:S(2)}, u32[]{:S(2)}) collective-permute-start(bf16[4,7168]{1,0:T(4,128)(2,1)S(1)} %get-tuple-element.71), channel_id=1, source_target_pairs={{0,12},{1,13},{2,14},{3,15},{4,8},{5,9},{6,10},{7,11},{8,4},{9,5},... | collective-permute-start | bytes 172040 | tf_op jit(solution)/shard_map/ppermute | solution.py:412
  63.9 1.0 %collective-permute-done.23.refs_3_ = bf16[4,7168]{1,0:T(4,128)(2,1)S(1)} collective-permute-done((bf16[4,7168]{1,0:T(4,128)(2,1)S(1)}, bf16[4,7168]{1,0:T(4,128)(2,1)S(1)}, u32[]{:S(2)}, u32[]{:S(2)}) %collective-permute-start.23) | collective-permute-done | bytes 57376 | tf_op jit(solution)/shard_map/ppermute | solution.py:412
  64.9 3.0 %collective-permute-done.26.refs_4_ = bf16[4,7168]{1,0:T(4,128)(2,1)S(1)} collective-permute-done((bf16[4,7168]{1,0:T(4,128)(2,1)S(1)}, bf16[4,7168]{1,0:T(4,128)(2,1)S(1)}, u32[]{:S(2)}, u32[]{:S(2)}) %collective-permute-start.26) | collective-permute-done | bytes 57376 | tf_op jit(solution)/shard_map/ppermute | solution.py:412
  67.9 1.5 %collective-permute-done.27.refs_5_ = bf16[4,7168]{1,0:T(4,128)(2,1)S(1)} collective-permute-done((bf16[4,7168]{1,0:T(4,128)(2,1)S(1)}, bf16[4,7168]{1,0:T(4,128)(2,1)S(1)}, u32[]{:S(2)}, u32[]{:S(2)}) %collective-permute-start.27) | collective-permute-done | bytes 57376 | tf_op jit(solution)/shard_map/ppermute | solution.py:412
  (71 shorter events, 5.9 us)
Async XLA Ops:
  0.0 14.2 %collective-permute-start.4 = (bf16[1536,1536]{1,0:T(8,128)(2,1)}, bf16[1536,1536]{1,0:T(8,128)(2,1)S(1)}, u32[]{:S(2)}, u32[]{:S(2)}) collective-permute-start(bf16[1536,1536]{1,0:T(8,128)(2,1)} %refs_4_.1), channel_id=1, source_target_pairs={{0,1},{1,0},{2,3},{3,2},{4,5},{5,4},{6,7},{7,6},{8,9},{9,8},{10,11... | collective-permute-start | bytes 14155784 | tf_op jit(solution)/shard_map/ppermute | solution.py:412
  0.5 13.7 %collective-permute-start.5 = (bf16[8,128,512]{2,1,0:T(8,128)(2,1)}, bf16[8,128,512]{2,1,0:T(8,128)(2,1)S(1)}, u32[]{:S(2)}, u32[]{:S(2)}) collective-permute-start(bf16[8,128,512]{2,1,0:T(8,128)(2,1)} %refs_5_.1), channel_id=1, source_target_pairs={{0,1},{1,0},{2,3},{3,2},{4,5},{5,4},{6,7},{7,6},{8,9},{9,8},{10,11... | collective-permute-start | bytes 3145736 | tf_op jit(solution)/shard_map/ppermute | solution.py:412
  0.5 4.8 %collective-permute-start = (bf16[4,1536]{1,0:T(4,128)(2,1)}, bf16[4,1536]{1,0:T(4,128)(2,1)S(1)}, u32[]{:S(2)}, u32[]{:S(2)}) collective-permute-start(bf16[4,1536]{1,0:T(4,128)(2,1)} %refs_0_.1), channel_id=1, source_target_pairs={{0,2},{1,3},{2,0},{3,1},{4,6},{5,7},{6,4},{7,5},{8,10},{9,11},{10,... | collective-permute-start | bytes 36872 | tf_op jit(solution)/shard_map/ppermute | solution.py:412
  4.1 10.1 %slice-start.6 = ((s8[4718592]{0:T(1024)(128)(4,1)}), s8[4194304]{0:T(1024)(128)(4,1)S(1)}, s32[]{:S(2)}) async-start(s8[4718592]{0:T(1024)(128)(4,1)} %bitcast.7), calls=%async_computation.6 | async-start | bytes 8388608
  5.4 8.9 %copy-start = (bf16[8,128,512]{2,1,0:T(8,128)(2,1)S(1)}, bf16[8,128,512]{2,1,0:T(8,128)(2,1)}, u32[]{:S(2)}) copy-start(bf16[8,128,512]{2,1,0:T(8,128)(2,1)} %refs_5_.1) | copy-start | bytes 3145732
  5.4 20.3 %slice-start.4 = ((s8[7077888]{0:T(1024)(128)(4,1)}), s8[4194304]{0:T(1024)(128)(4,1)S(1)}, s32[]{:S(2)}) async-start(s8[7077888]{0:T(1024)(128)(4,1)} %bitcast.3), calls=%async_computation.4 | async-start | bytes 8388608
  5.4 20.3 %slice-start.5 = ((s8[7077888]{0:T(1024)(128)(4,1)}), s8[2883584]{0:T(1024)(128)(4,1)S(1)}, s32[]{:S(2)}) async-start(s8[7077888]{0:T(1024)(128)(4,1)} %bitcast.3), calls=%async_computation.5 | async-start | bytes 5767168
  5.4 5.0 %collective-permute-start.3 = (bf16[8,1536]{1,0:T(8,128)(2,1)S(1)}, bf16[8,1536]{1,0:T(8,128)(2,1)S(1)}, u32[]{:S(2)}, u32[]{:S(2)}) collective-permute-start(bf16[8,1536]{1,0:T(8,128)(2,1)S(1)} %get-tuple-element.43.refs_0_), channel_id=1, source_target_pairs={{0,8},{1,9},{2,10},{3,11},{4,12},{5,13},{6,14},{7,15},{8,0},{9,1},... | collective-permute-start | bytes 73736 | tf_op jit(solution)/shard_map/ppermute | solution.py:412
  8.6 5.6 %collective-permute-start.2 = (bf16[8,1536]{1,0:T(8,128)(2,1)S(1)}, bf16[8,1536]{1,0:T(8,128)(2,1)S(1)}, u32[]{:S(2)}, u32[]{:S(2)}) collective-permute-start(bf16[8,1536]{1,0:T(8,128)(2,1)S(1)} %get-tuple-element.43.refs_0_), channel_id=1, source_target_pairs={{0,12},{1,13},{2,14},{3,15},{4,8},{5,9},{6,10},{7,11},{8,4},{9,5},... | collective-permute-start | bytes 73736 | tf_op jit(solution)/shard_map/ppermute | solution.py:412
  9.9 4.3 %collective-permute-start.1 = (bf16[8,1536]{1,0:T(8,128)(2,1)S(1)}, bf16[8,1536]{1,0:T(8,128)(2,1)S(1)}, u32[]{:S(2)}, u32[]{:S(2)}) collective-permute-start(bf16[8,1536]{1,0:T(8,128)(2,1)S(1)} %get-tuple-element.43.refs_0_), channel_id=1, source_target_pairs={{0,4},{1,5},{2,6},{3,7},{4,0},{5,1},{6,2},{7,3},{8,12},{9,13},{10,... | collective-permute-start | bytes 73736 | tf_op jit(solution)/shard_map/ppermute | solution.py:412
  16.5 7.4 %collective-permute-start.6 = (bf16[4,144,128]{2,1,0:T(8,128)(2,1)S(1)}, bf16[4,144,128]{2,1,0:T(8,128)(2,1)S(1)}, u32[]{:S(2)}, u32[]{:S(2)}) collective-permute-start(bf16[4,144,128]{2,1,0:T(8,128)(2,1)S(1)} %get-tuple-element.45), channel_id=1, source_target_pairs={{0,2},{1,3},{2,0},{3,1},{4,6},{5,7},{6,4},{7,5},{8,10},{9,11},{10,... | collective-permute-start | bytes 442376 | tf_op jit(solution)/shard_map/ppermute | solution.py:412
  18.1 10.2 %collective-permute-start.7 = (bf16[2,144,128]{2,1,0:T(8,128)(2,1)S(1)}, bf16[2,144,128]{2,1,0:T(8,128)(2,1)S(1)}, u32[]{:S(2)}, u32[]{:S(2)}) collective-permute-start(bf16[2,144,128]{2,1,0:T(8,128)(2,1)S(1)} %get-tuple-element.46), channel_id=1, source_target_pairs={{0,8},{1,9},{2,10},{3,11},{4,12},{5,13},{6,14},{7,15},{8,0},{9,1},... | collective-permute-start | bytes 221192 | tf_op jit(solution)/shard_map/ppermute | solution.py:412
  19.4 9.0 %collective-permute-start.8 = (bf16[2,144,128]{2,1,0:T(8,128)(2,1)S(1)}, bf16[2,144,128]{2,1,0:T(8,128)(2,1)S(1)}, u32[]{:S(2)}, u32[]{:S(2)}) collective-permute-start(bf16[2,144,128]{2,1,0:T(8,128)(2,1)S(1)} %get-tuple-element.47), channel_id=1, source_target_pairs={{0,14},{1,15},{2,12},{3,13},{4,10},{5,11},{6,8},{7,9},{8,6},{9,7},... | collective-permute-start | bytes 221192 | tf_op jit(solution)/shard_map/ppermute | solution.py:412
  20.2 8.1 %collective-permute-start.9 = (bf16[2,144,128]{2,1,0:T(8,128)(2,1)S(1)}, bf16[2,144,128]{2,1,0:T(8,128)(2,1)S(1)}, u32[]{:S(2)}, u32[]{:S(2)}) collective-permute-start(bf16[2,144,128]{2,1,0:T(8,128)(2,1)S(1)} %get-tuple-element.48), channel_id=1, source_target_pairs={{0,12},{1,13},{2,14},{3,15},{4,8},{5,9},{6,10},{7,11},{8,4},{9,5},... | collective-permute-start | bytes 221192 | tf_op jit(solution)/shard_map/ppermute | solution.py:412
  23.1 9.6 %collective-permute-start.10 = (bf16[2,144,128]{2,1,0:T(8,128)(2,1)S(1)}, bf16[2,144,128]{2,1,0:T(8,128)(2,1)S(1)}, u32[]{:S(2)}, u32[]{:S(2)}) collective-permute-start(bf16[2,144,128]{2,1,0:T(8,128)(2,1)S(1)} %get-tuple-element.49), channel_id=1, source_target_pairs={{0,10},{1,11},{2,8},{3,9},{4,14},{5,15},{6,12},{7,13},{8,2},{9,3},... | collective-permute-start | bytes 221192 | tf_op jit(solution)/shard_map/ppermute | solution.py:412
  24.0 8.7 %collective-permute-start.11 = (bf16[4,144,128]{2,1,0:T(8,128)(2,1)S(1)}, bf16[4,144,128]{2,1,0:T(8,128)(2,1)S(1)}, u32[]{:S(2)}, u32[]{:S(2)}) collective-permute-start(bf16[4,144,128]{2,1,0:T(8,128)(2,1)S(1)} %forward.2.after_ref), channel_id=1, source_target_pairs={{0,4},{1,5},{2,6},{3,7},{4,0},{5,1},{6,2},{7,3},{8,12},{9,13},{10,... | collective-permute-start | bytes 442376 | tf_op jit(solution)/shard_map/ppermute | solution.py:412
  36.2 6.4 %collective-permute-start.16 = (bf16[4,32,512]{2,1,0:T(8,128)(2,1)S(1)}, bf16[4,32,512]{2,1,0:T(8,128)(2,1)S(1)}, u32[]{:S(2)}, u32[]{:S(2)}) collective-permute-start(bf16[4,32,512]{2,1,0:T(8,128)(2,1)S(1)} %get-tuple-element.55), channel_id=1, source_target_pairs={{0,2},{1,3},{2,0},{3,1},{4,6},{5,7},{6,4},{7,5},{8,10},{9,11},{10,... | collective-permute-start | bytes 393224 | tf_op jit(solution)/shard_map/ppermute | solution.py:412
  36.8 9.5 %collective-permute-start.12 = (bf16[2,32,512]{2,1,0:T(8,128)(2,1)S(1)}, bf16[2,32,512]{2,1,0:T(8,128)(2,1)S(1)}, u32[]{:S(2)}, u32[]{:S(2)}) collective-permute-start(bf16[2,32,512]{2,1,0:T(8,128)(2,1)S(1)} %get-tuple-element.51), channel_id=1, source_target_pairs={{0,8},{1,9},{2,10},{3,11},{4,12},{5,13},{6,14},{7,15},{8,0},{9,1},... | collective-permute-start | bytes 196616 | tf_op jit(solution)/shard_map/ppermute | solution.py:412
  36.9 9.5 %collective-permute-start.13 = (bf16[2,32,512]{2,1,0:T(8,128)(2,1)S(1)}, bf16[2,32,512]{2,1,0:T(8,128)(2,1)S(1)}, u32[]{:S(2)}, u32[]{:S(2)}) collective-permute-start(bf16[2,32,512]{2,1,0:T(8,128)(2,1)S(1)} %get-tuple-element.52), channel_id=1, source_target_pairs={{0,14},{1,15},{2,12},{3,13},{4,10},{5,11},{6,8},{7,9},{8,6},{9,7},... | collective-permute-start | bytes 196616 | tf_op jit(solution)/shard_map/ppermute | solution.py:412
  39.5 6.9 %collective-permute-start.14 = (bf16[2,32,512]{2,1,0:T(8,128)(2,1)S(1)}, bf16[2,32,512]{2,1,0:T(8,128)(2,1)S(1)}, u32[]{:S(2)}, u32[]{:S(2)}) collective-permute-start(bf16[2,32,512]{2,1,0:T(8,128)(2,1)S(1)} %get-tuple-element.53), channel_id=1, source_target_pairs={{0,12},{1,13},{2,14},{3,15},{4,8},{5,9},{6,10},{7,11},{8,4},{9,5},... | collective-permute-start | bytes 196616 | tf_op jit(solution)/shard_map/ppermute | solution.py:412
  41.7 8.7 %collective-permute-start.15 = (bf16[2,32,512]{2,1,0:T(8,128)(2,1)S(1)}, bf16[2,32,512]{2,1,0:T(8,128)(2,1)S(1)}, u32[]{:S(2)}, u32[]{:S(2)}) collective-permute-start(bf16[2,32,512]{2,1,0:T(8,128)(2,1)S(1)} %get-tuple-element.54), channel_id=1, source_target_pairs={{0,10},{1,11},{2,8},{3,9},{4,14},{5,15},{6,12},{7,13},{8,2},{9,3},... | collective-permute-start | bytes 196616 | tf_op jit(solution)/shard_map/ppermute | solution.py:412
  42.7 7.7 %collective-permute-start.17 = (bf16[4,32,512]{2,1,0:T(8,128)(2,1)S(1)}, bf16[4,32,512]{2,1,0:T(8,128)(2,1)S(1)}, u32[]{:S(2)}, u32[]{:S(2)}) collective-permute-start(bf16[4,32,512]{2,1,0:T(8,128)(2,1)S(1)} %forward.3.after_ref), channel_id=1, source_target_pairs={{0,4},{1,5},{2,6},{3,7},{4,0},{5,1},{6,2},{7,3},{8,12},{9,13},{10,... | collective-permute-start | bytes 393224 | tf_op jit(solution)/shard_map/ppermute | solution.py:412
  50.4 1.6 %collective-permute-start.18 = (bf16[8,32,512]{2,1,0:T(8,128)(2,1)S(1)}, bf16[8,32,512]{2,1,0:T(8,128)(2,1)S(1)}, u32[]{:S(2)}, u32[]{:S(2)}) collective-permute-start(bf16[8,32,512]{2,1,0:T(8,128)(2,1)S(1)} %regroup.1), channel_id=1, source_target_pairs={{0,1},{1,0},{2,3},{3,2},{4,5},{5,4},{6,7},{7,6},{8,9},{9,8},{10,11... | collective-permute-start | bytes 786440 | tf_op jit(solution)/shard_map/ppermute | solution.py:412
  53.9 2.0 %collective-permute-start.20 = (bf16[32,3584]{1,0:T(8,128)(2,1)S(1)}, bf16[32,3584]{1,0:T(8,128)(2,1)S(1)}, u32[]{:S(2)}, u32[]{:S(2)}) collective-permute-start(bf16[32,3584]{1,0:T(8,128)(2,1)S(1)} %get-tuple-element.61), channel_id=1, source_target_pairs={{0,1},{1,0},{2,3},{3,2},{4,5},{5,4},{6,7},{7,6},{8,9},{9,8},{10,11... | collective-permute-start | bytes 688136 | tf_op jit(solution)/shard_map/ppermute | solution.py:412
  55.5 1.6 %collective-permute-start.19 = (bf16[32,3584]{1,0:T(8,128)(2,1)S(1)}, bf16[32,3584]{1,0:T(8,128)(2,1)S(1)}, u32[]{:S(2)}, u32[]{:S(2)}) collective-permute-start(bf16[32,3584]{1,0:T(8,128)(2,1)S(1)} %get-tuple-element.59), channel_id=1, source_target_pairs={{0,1},{1,0},{2,3},{3,2},{4,5},{5,4},{6,7},{7,6},{8,9},{9,8},{10,11... | collective-permute-start | bytes 688136 | tf_op jit(solution)/shard_map/ppermute | solution.py:412
  56.0 5.7 %collective-permute-start.24 = (bf16[8,3584]{1,0:T(8,128)(2,1)S(1)}, bf16[8,3584]{1,0:T(8,128)(2,1)S(1)}, u32[]{:S(2)}, u32[]{:S(2)}) collective-permute-start(bf16[8,3584]{1,0:T(8,128)(2,1)S(1)} %get-tuple-element.69), channel_id=1, source_target_pairs={{0,2},{1,3},{2,0},{3,1},{4,6},{5,7},{6,4},{7,5},{8,10},{9,11},{10,... | collective-permute-start | bytes 172040 | tf_op jit(solution)/shard_map/ppermute | solution.py:412
  57.2 4.6 %collective-permute-start.25 = (bf16[8,3584]{1,0:T(8,128)(2,1)S(1)}, bf16[8,3584]{1,0:T(8,128)(2,1)S(1)}, u32[]{:S(2)}, u32[]{:S(2)}) collective-permute-start(bf16[8,3584]{1,0:T(8,128)(2,1)S(1)} %get-tuple-element.70), channel_id=1, source_target_pairs={{0,2},{1,3},{2,0},{3,1},{4,6},{5,7},{6,4},{7,5},{8,10},{9,11},{10,... | collective-permute-start | bytes 172040 | tf_op jit(solution)/shard_map/ppermute | solution.py:412
  58.3 5.5 %collective-permute-start.21 = (bf16[4,7168]{1,0:T(4,128)(2,1)S(1)}, bf16[4,7168]{1,0:T(4,128)(2,1)S(1)}, u32[]{:S(2)}, u32[]{:S(2)}) collective-permute-start(bf16[4,7168]{1,0:T(4,128)(2,1)S(1)} %get-tuple-element.64), channel_id=1, source_target_pairs={{0,4},{1,5},{2,6},{3,7},{4,0},{5,1},{6,2},{7,3},{8,12},{9,13},{10,... | collective-permute-start | bytes 172040 | tf_op jit(solution)/shard_map/ppermute | solution.py:412
  58.3 5.6 %collective-permute-start.22 = (bf16[4,7168]{1,0:T(4,128)(2,1)S(1)}, bf16[4,7168]{1,0:T(4,128)(2,1)S(1)}, u32[]{:S(2)}, u32[]{:S(2)}) collective-permute-start(bf16[4,7168]{1,0:T(4,128)(2,1)S(1)} %get-tuple-element.65), channel_id=1, source_target_pairs={{0,6},{1,7},{2,4},{3,5},{4,2},{5,3},{6,0},{7,1},{8,14},{9,15},{10,... | collective-permute-start | bytes 172040 | tf_op jit(solution)/shard_map/ppermute | solution.py:412
  60.7 4.2 %collective-permute-start.23 = (bf16[4,7168]{1,0:T(4,128)(2,1)S(1)}, bf16[4,7168]{1,0:T(4,128)(2,1)S(1)}, u32[]{:S(2)}, u32[]{:S(2)}) collective-permute-start(bf16[4,7168]{1,0:T(4,128)(2,1)S(1)} %get-tuple-element.66), channel_id=1, source_target_pairs={{0,2},{1,3},{2,0},{3,1},{4,6},{5,7},{6,4},{7,5},{8,10},{9,11},{10,... | collective-permute-start | bytes 172040 | tf_op jit(solution)/shard_map/ppermute | solution.py:412
  61.8 6.0 %collective-permute-start.26 = (bf16[4,7168]{1,0:T(4,128)(2,1)S(1)}, bf16[4,7168]{1,0:T(4,128)(2,1)S(1)}, u32[]{:S(2)}, u32[]{:S(2)}) collective-permute-start(bf16[4,7168]{1,0:T(4,128)(2,1)S(1)} %get-tuple-element.71), channel_id=1, source_target_pairs={{0,12},{1,13},{2,14},{3,15},{4,8},{5,9},{6,10},{7,11},{8,4},{9,5},... | collective-permute-start | bytes 172040 | tf_op jit(solution)/shard_map/ppermute | solution.py:412
  63.8 5.6 %collective-permute-start.27 = (bf16[4,7168]{1,0:T(4,128)(2,1)S(1)}, bf16[4,7168]{1,0:T(4,128)(2,1)S(1)}, u32[]{:S(2)}, u32[]{:S(2)}) collective-permute-start(bf16[4,7168]{1,0:T(4,128)(2,1)S(1)} %get-tuple-element.72), channel_id=1, source_target_pairs={{0,8},{1,9},{2,10},{3,11},{4,12},{5,13},{6,14},{7,15},{8,0},{9,1},... | collective-permute-start | bytes 172040 | tf_op jit(solution)/shard_map/ppermute | solution.py:412
  (10 other events, 61.1 us)

commit v20 on v15

--- a/solution.py
+++ b/solution.py
@@ -254,32 +254,17 @@
     )
 
 
-def early_kernel(passing_ref, own_ref, after_ref, out_ref):
-    out_ref[0] = passing_ref[1]
-    out_ref[1] = own_ref[1]
-
-
-def early(passing, own, after):
-    return call(early_kernel, shape(2, *own.shape[1:]), 4, "early")(passing, own, after)
-
-
-def regroup_kernel(*refs):
-    *in_refs, early_ref, out_ref = refs
-    blocks = arrived(in_refs)[1::2]
-    blocks = [*blocks[:-4], (early_ref, 0), *blocks[-3:-1], (early_ref, 1)]
-    for j, (ref, i) in enumerate(blocks):
-        out_ref[j] = ref[i]
-
-
-def regroup(messages, ready, chips):
-    _, wide, width = messages[0].shape
-    return call(regroup_kernel, shape(chips, wide, width), 1, "regroup")(*messages, ready)
-
-
-def values_kernel(count, *refs):
-    blocks = arrived(refs[:count])
-    blocks = blocks[::2] if count > 1 else blocks
-    wv_ref, val_ref, rows_ref = refs[count], *refs[-2:]
+def early_kernel(own_ref, after_ref, out_ref):
+    out_ref[...] = own_ref[...]
+
+
+def early(own, after):
+    return call(early_kernel, shape(*own.shape), 4, "early")(own, after)
+
+
+def values_kernel(count, core, *refs):
+    blocks = arrived(refs[:count])[core::2]
+    wv_ref, val_ref, rows_ref = refs[count:]
     heads = wv_ref.shape[0]
     for place, (ref, i) in enumerate(blocks):
         block = ref[i].astype(jnp.float32)
@@ -296,14 +281,12 @@
         ).astype(jnp.bfloat16)
 
 
-def head_values(messages, w_uv, chips, *after):
+def head_values(messages, w_uv, core, chips):
     heads = w_uv.shape[0]
     count = chips * messages[0].shape[1] // heads
     scratch = [pltpu.VMEM((PIECES, count * heads, LANES), jnp.float32)]
-    kernel = functools.partial(values_kernel, len(messages))
-    return call(kernel, shape(count, heads * VD), 2, "values", scratch)(
-        *messages, resident(w_uv), *after
-    )
+    kernel = functools.partial(values_kernel, len(messages), core)
+    return call(kernel, shape(count, heads * VD), 2, "values", scratch)(*messages, resident(w_uv))
 
 
 def terms_kernel(start, *refs):
@@ -428,20 +411,18 @@
     messages, sent = exchange(messages)
     keys = jnp.swapaxes(cache, 1, 2)
     flipped = flip(keys, sent)
+    far_wv = swap(w_uv, 1)
     latents = attend(lengths, tables, keys, flipped, new_latent, messages, heads, devices)
     latents, sent = exchange(latents)
-    ready = early(latents[-3], latents[-1], sent)
-    other = swap(regroup(latents, ready, devices // 2), 1)
-    here, there = jnp.float32, jnp.bfloat16
-    mine_values = head_values(latents, w_uv, devices // 2)
-    early_mine = output_terms([mine_values], [here], w_o, 0)
-    other_values = head_values([other], w_uv, devices // 2, *early_mine)
+    latents[-1] = early(latents[-1], sent)
+    other_values = head_values(latents, far_wv, 1, devices // 2)
+    other_values = swap(other_values, 1)
+    mine_values = head_values(latents, w_uv, 0, devices // 2)
     keep, got, near = [], [], None
     for part in range(PARTS):
-        if part == 0:
-            mine, other = *early_mine, *output_terms([other_values], [there], w_o, 0)
-        else:
-            mine, other = output_terms([mine_values, other_values], [here, there], w_o, part)
+        mine, other = output_terms(
+            [mine_values, other_values], [jnp.float32, jnp.bfloat16], w_o, part
+        )
         far_mine, far_other, near, *given = core_sum(mine, swap(other, 1), near, rows, devices)
         keep.append(far_mine)
         got.append(swap(far_other, Y))

time: 71.3 us -> 71.9 us (level)
  waiting for transfers between devices: 19.6 us -> 23 us
  Pallas kernels: 13.7 us -> 12.3 us
  local copies, waits for them, and re-layouts: 1.85 us -> 0.98 us
    ppermute x28 -> x29, waiting for transfers between devices: 19.6 us -> 23 us  [swap(): return lax.ppermute(block, 'row', [(i, i ^ k) for i in range(devices)])]
    pallas_call x18 -> x16, Pallas kernels: 13.7 us -> 12.3 us  [run(): pl.pallas_call(kernel, out_shape=out_shape, in_specs=smem + [in_vmem()] *...]
    unnamed x28, local copies, waits for them, and re-layouts: 1.85 us -> 0.98 us
    ppermute x28 -> x29, starting transfers between devices: 35.7 us -> 35.1 us  [swap(): return lax.ppermute(block, 'row', [(i, i ^ k) for i in range(devices)])]
  transfers between devices with their start and end apart: 28 -> 29, of which waited for: 12 -> 15; matrix products, arithmetic and copies ran while one was open for 0% -> 0% of each run, Pallas kernels for 8% -> 11%
where the time goes in v20:
time: 71.9 us; the launch traced here: 71.7 us
  starting transfers between devices  35.1 us (49%)
  waiting for transfers between devices  23 us (32%)
  Pallas kernels  12.3 us (17%)
  local copies, waits for them, and re-layouts  0.98 us (1%)
    ppermute x29, starting transfers between devices, swap(): return lax.ppermute(block, 'row', [(i, i ^ k) for i in range(devices)])  35.1 us
    ppermute x29, waiting for transfers between devices, swap(): return lax.ppermute(block, 'row', [(i, i ^ k) for i in range(devices)])  23 us
    pallas_call x16, Pallas kernels, run(): pl.pallas_call(kernel, out_shape=out_shape, in_specs=smem + [in_vmem()] *...  12.3 us
  transfers between devices with their start and end apart: 29, of which 15 were waited for; matrix products, arithmetic and copies ran while one was open for 0% of the time, Pallas kernels for 11%

profile of v20, /device:TPU:0, one launch (start us, length us, event | category | flops | bytes accessed | tf_op | source)
XLA Modules:
  0.0 71.7 jit_solution(6012557618204669536)
XLA Ops:
  0.5 3.0 %collective-permute-start = (bf16[4,1536]{1,0:T(4,128)(2,1)}, bf16[4,1536]{1,0:T(4,128)(2,1)S(1)}, u32[]{:S(2)}, u32[]{:S(2)}) collective-permute-start(bf16[4,1536]{1,0:T(4,128)(2,1)} %refs_0_.1), channel_id=1, source_target_pairs={{0,2},{1,3},{2,0},{3,1},{4,6},{5,7},{6,4},{7,5},{8,10},{9,11},{10,... | collective-permute-start | bytes 36872 | tf_op jit(solution)/shard_map/ppermute | solution.py:395
  5.4 2.1 %collective-permute-start.1 = (bf16[8,1536]{1,0:T(8,128)(2,1)S(1)}, bf16[8,1536]{1,0:T(8,128)(2,1)S(1)}, u32[]{:S(2)}, u32[]{:S(2)}) collective-permute-start(bf16[8,1536]{1,0:T(8,128)(2,1)S(1)} %get-tuple-element.43.refs_0_), channel_id=1, source_target_pairs={{0,4},{1,5},{2,6},{3,7},{4,0},{5,1},{6,2},{7,3},{8,12},{9,13},{10,... | collective-permute-start | bytes 73736 | tf_op jit(solution)/shard_map/ppermute | solution.py:395
  7.6 2.5 %collective-permute-start.2 = (bf16[8,1536]{1,0:T(8,128)(2,1)S(1)}, bf16[8,1536]{1,0:T(8,128)(2,1)S(1)}, u32[]{:S(2)}, u32[]{:S(2)}) collective-permute-start(bf16[8,1536]{1,0:T(8,128)(2,1)S(1)} %get-tuple-element.43.refs_0_), channel_id=1, source_target_pairs={{0,12},{1,13},{2,14},{3,15},{4,8},{5,9},{6,10},{7,11},{8,4},{9,5},... | collective-permute-start | bytes 73736 | tf_op jit(solution)/shard_map/ppermute | solution.py:395
  10.1 3.0 %collective-permute-done.2.refs_2_ = bf16[8,1536]{1,0:T(8,128)(2,1)S(1)} collective-permute-done((bf16[8,1536]{1,0:T(8,128)(2,1)S(1)}, bf16[8,1536]{1,0:T(8,128)(2,1)S(1)}, u32[]{:S(2)}, u32[]{:S(2)}) %collective-permute-start.2) | collective-permute-done | bytes 24608 | tf_op jit(solution)/shard_map/ppermute | solution.py:395
  13.2 1.8 %collective-permute-done.3.refs_3_ = bf16[8,1536]{1,0:T(8,128)(2,1)S(1)} collective-permute-done((bf16[8,1536]{1,0:T(8,128)(2,1)S(1)}, bf16[8,1536]{1,0:T(8,128)(2,1)S(1)}, u32[]{:S(2)}, u32[]{:S(2)}) %collective-permute-start.3) | collective-permute-done | bytes 24608 | tf_op jit(solution)/shard_map/ppermute | solution.py:395
  15.1 2.3 %project.1 = (bf16[2,144,128]{2,1,0:T(8,128)(2,1)S(1)}, bf16[2,144,128]{2,1,0:T(8,128)(2,1)S(1)}, bf16[2,144,128]{2,1,0:T(8,128)(2,1)S(1)}, bf16[2,144,128]{2,1,...) custom-call(bf16[8,1536]{1,0:T(8,128)(2,1)S(1)} %get-tuple-element.4, ...), custom_call_target="tpu_custom_call" | custom-call | flops 23000000512 | tf_op jit(solution)/shard_map/project/pallas_call | solution.py:37
  17.3 1.6 %collective-permute-start.6 = (bf16[4,144,128]{2,1,0:T(8,128)(2,1)S(1)}, bf16[4,144,128]{2,1,0:T(8,128)(2,1)S(1)}, u32[]{:S(2)}, u32[]{:S(2)}) collective-permute-start(bf16[4,144,128]{2,1,0:T(8,128)(2,1)S(1)} %get-tuple-element.45), channel_id=1, source_target_pairs={{0,2},{1,3},{2,0},{3,1},{4,6},{5,7},{6,4},{7,5},{8,10},{9,11},{10,... | collective-permute-start | bytes 442376 | tf_op jit(solution)/shard_map/ppermute | solution.py:395
  18.9 1.1 %collective-permute-start.10 = (bf16[2,144,128]{2,1,0:T(8,128)(2,1)S(1)}, bf16[2,144,128]{2,1,0:T(8,128)(2,1)S(1)}, u32[]{:S(2)}, u32[]{:S(2)}) collective-permute-start(bf16[2,144,128]{2,1,0:T(8,128)(2,1)S(1)} %get-tuple-element.49), channel_id=1, source_target_pairs={{0,14},{1,15},{2,12},{3,13},{4,10},{5,11},{6,8},{7,9},{8,6},{9,7},... | collective-permute-start | bytes 221192 | tf_op jit(solution)/shard_map/ppermute | solution.py:395
  20.9 3.1 %collective-permute-start.8 = (bf16[2,144,128]{2,1,0:T(8,128)(2,1)S(1)}, bf16[2,144,128]{2,1,0:T(8,128)(2,1)S(1)}, u32[]{:S(2)}, u32[]{:S(2)}) collective-permute-start(bf16[2,144,128]{2,1,0:T(8,128)(2,1)S(1)} %get-tuple-element.47), channel_id=1, source_target_pairs={{0,10},{1,11},{2,8},{3,9},{4,14},{5,15},{6,12},{7,13},{8,2},{9,3},... | collective-permute-start | bytes 221192 | tf_op jit(solution)/shard_map/ppermute | solution.py:395
  23.9 2.7 %collective-permute-start.9 = (bf16[2,144,128]{2,1,0:T(8,128)(2,1)S(1)}, bf16[2,144,128]{2,1,0:T(8,128)(2,1)S(1)}, u32[]{:S(2)}, u32[]{:S(2)}) collective-permute-start(bf16[2,144,128]{2,1,0:T(8,128)(2,1)S(1)} %get-tuple-element.48), channel_id=1, source_target_pairs={{0,12},{1,13},{2,14},{3,15},{4,8},{5,9},{6,10},{7,11},{8,4},{9,5},... | collective-permute-start | bytes 221192 | tf_op jit(solution)/shard_map/ppermute | solution.py:395
  26.7 1.7 %flip.1.flip_ref = bf16[4,1536,512]{2,1,0:T(8,128)(2,1)S(1)} custom-call(bf16[4,576,1536]{2,1,0:T(8,128)(2,1)S(1)} %bitcast.5, bf16[4,144,128]{2,1,0:T(8,128)(2,1)S(1)} %forward.2.after_ref), custom_call_target="tpu_custom_call" | custom-call | flops 4600000000 | tf_op jit(solution)/shard_map/flip/pallas_call | solution.py:37
  28.6 1.7 %collective-permute-done.7.refs_0_ = bf16[2,144,128]{2,1,0:T(8,128)(2,1)S(1)} collective-permute-done((bf16[2,144,128]{2,1,0:T(8,128)(2,1)S(1)}, bf16[2,144,128]{2,1,0:T(8,128)(2,1)S(1)}, u32[]{:S(2)}, u32[]{:S(2)}) %collective-permute-start.7) | collective-permute-done | bytes 73760 | tf_op jit(solution)/shard_map/ppermute | solution.py:395
  30.3 2.1 %collective-permute-done.8.refs_1_ = bf16[2,144,128]{2,1,0:T(8,128)(2,1)S(1)} collective-permute-done((bf16[2,144,128]{2,1,0:T(8,128)(2,1)S(1)}, bf16[2,144,128]{2,1,0:T(8,128)(2,1)S(1)}, u32[]{:S(2)}, u32[]{:S(2)}) %collective-permute-start.8) | collective-permute-done | bytes 73760 | tf_op jit(solution)/shard_map/ppermute | solution.py:395
  32.6 3.4 %attend.1 = (bf16[2,32,512]{2,1,0:T(8,128)(2,1)S(1)}, bf16[2,32,512]{2,1,0:T(8,128)(2,1)S(1)}, bf16[2,32,512]{2,1,0:T(8,128)(2,1)S(1)}, bf16[2,32,512]{2,1,0:T(8...) custom-call(s32[4]{0:T(128)S(1)} %copy-done.5, ...), custom_call_target="tpu_custom_call" | custom-call | flops 11500000256 | tf_op jit(solution)/shard_map/attend/pallas_call | solution.py:37
  36.1 1.4 %collective-permute-start.16 = (bf16[4,32,512]{2,1,0:T(8,128)(2,1)S(1)}, bf16[4,32,512]{2,1,0:T(8,128)(2,1)S(1)}, u32[]{:S(2)}, u32[]{:S(2)}) collective-permute-start(bf16[4,32,512]{2,1,0:T(8,128)(2,1)S(1)} %get-tuple-element.55), channel_id=1, source_target_pairs={{0,2},{1,3},{2,0},{3,1},{4,6},{5,7},{6,4},{7,5},{8,10},{9,11},{10,... | collective-permute-start | bytes 393224 | tf_op jit(solution)/shard_map/ppermute | solution.py:395
  37.4 1.3 %collective-permute-start.12 = (bf16[2,32,512]{2,1,0:T(8,128)(2,1)S(1)}, bf16[2,32,512]{2,1,0:T(8,128)(2,1)S(1)}, u32[]{:S(2)}, u32[]{:S(2)}) collective-permute-start(bf16[2,32,512]{2,1,0:T(8,128)(2,1)S(1)} %get-tuple-element.51), channel_id=1, source_target_pairs={{0,8},{1,9},{2,10},{3,11},{4,12},{5,13},{6,14},{7,15},{8,0},{9,1},... | collective-permute-start | bytes 196616 | tf_op jit(solution)/shard_map/ppermute | solution.py:395
  38.8 1.8 %collective-permute-start.13 = (bf16[2,32,512]{2,1,0:T(8,128)(2,1)S(1)}, bf16[2,32,512]{2,1,0:T(8,128)(2,1)S(1)}, u32[]{:S(2)}, u32[]{:S(2)}) collective-permute-start(bf16[2,32,512]{2,1,0:T(8,128)(2,1)S(1)} %get-tuple-element.52), channel_id=1, source_target_pairs={{0,10},{1,11},{2,8},{3,9},{4,14},{5,15},{6,12},{7,13},{8,2},{9,3},... | collective-permute-start | bytes 196616 | tf_op jit(solution)/shard_map/ppermute | solution.py:395
  40.5 2.3 %collective-permute-start.14 = (bf16[2,32,512]{2,1,0:T(8,128)(2,1)S(1)}, bf16[2,32,512]{2,1,0:T(8,128)(2,1)S(1)}, u32[]{:S(2)}, u32[]{:S(2)}) collective-permute-start(bf16[2,32,512]{2,1,0:T(8,128)(2,1)S(1)} %get-tuple-element.53), channel_id=1, source_target_pairs={{0,12},{1,13},{2,14},{3,15},{4,8},{5,9},{6,10},{7,11},{8,4},{9,5},... | collective-permute-start | bytes 196616 | tf_op jit(solution)/shard_map/ppermute | solution.py:395
  42.8 2.2 %collective-permute-start.15 = (bf16[2,32,512]{2,1,0:T(8,128)(2,1)S(1)}, bf16[2,32,512]{2,1,0:T(8,128)(2,1)S(1)}, u32[]{:S(2)}, u32[]{:S(2)}) collective-permute-start(bf16[2,32,512]{2,1,0:T(8,128)(2,1)S(1)} %get-tuple-element.54), channel_id=1, source_target_pairs={{0,14},{1,15},{2,12},{3,13},{4,10},{5,11},{6,8},{7,9},{8,6},{9,7},... | collective-permute-start | bytes 196616 | tf_op jit(solution)/shard_map/ppermute | solution.py:395
  45.2 1.5 %collective-permute-done.12.refs_0_ = bf16[2,32,512]{2,1,0:T(8,128)(2,1)S(1)} collective-permute-done((bf16[2,32,512]{2,1,0:T(8,128)(2,1)S(1)}, bf16[2,32,512]{2,1,0:T(8,128)(2,1)S(1)}, u32[]{:S(2)}, u32[]{:S(2)}) %collective-permute-start.12) | collective-permute-done | bytes 65568 | tf_op jit(solution)/shard_map/ppermute | solution.py:395
  46.7 1.4 %collective-permute-done.13.refs_1_ = bf16[2,32,512]{2,1,0:T(8,128)(2,1)S(1)} collective-permute-done((bf16[2,32,512]{2,1,0:T(8,128)(2,1)S(1)}, bf16[2,32,512]{2,1,0:T(8,128)(2,1)S(1)}, u32[]{:S(2)}, u32[]{:S(2)}) %collective-permute-start.13) | collective-permute-done | bytes 65568 | tf_op jit(solution)/shard_map/ppermute | solution.py:395
  48.2 1.8 %collective-permute-done.15.refs_3_ = bf16[2,32,512]{2,1,0:T(8,128)(2,1)S(1)} collective-permute-done((bf16[2,32,512]{2,1,0:T(8,128)(2,1)S(1)}, bf16[2,32,512]{2,1,0:T(8,128)(2,1)S(1)}, u32[]{:S(2)}, u32[]{:S(2)}) %collective-permute-start.15) | collective-permute-done | bytes 65568 | tf_op jit(solution)/shard_map/ppermute | solution.py:395
  51.6 0.9 %collective-permute-done.19.refs_1_ = bf16[32,1024]{1,0:T(8,128)(2,1)S(1)} collective-permute-done((bf16[32,1024]{1,0:T(8,128)(2,1)S(1)}, bf16[32,1024]{1,0:T(8,128)(2,1)S(1)}, u32[]{:S(2)}, u32[]{:S(2)}) %collective-permute-start.19) | collective-permute-done | bytes 65568 | tf_op jit(solution)/shard_map/ppermute | solution.py:395
  52.8 1.4 %terms.3 = (f32[32,3584]{1,0:T(8,128)S(1)}, bf16[32,3584]{1,0:T(8,128)(2,1)S(1)}) custom-call(bf16[32,1024]{1,0:T(8,128)(2,1)S(1)} %values.2.refs_0_, bf16[32,1024]{1,0:T(8,128)(2,1)S(1)} %collective-permute-done.19.refs_1_, bf16[1024,7168]{1,0:T(8,128)(2,1)S(1)} %bitcast.2), custom_call_target="tpu_custom_call" | custom-call | flops 6899999744 | tf_op jit(solution)/shard_map/terms/pallas_call | solution.py:37
  54.2 1.4 %terms.2 = (f32[32,3584]{1,0:T(8,128)S(1)}, bf16[32,3584]{1,0:T(8,128)(2,1)S(1)}) custom-call(bf16[32,1024]{1,0:T(8,128)(2,1)S(1)} %values.2.refs_0_, bf16[32,1024]{1,0:T(8,128)(2,1)S(1)} %collective-permute-done.19.refs_1_, bf16[1024,7168]{1,0:T(8,128)(2,1)S(1)} %bitcast.2), custom_call_target="tpu_custom_call" | custom-call | flops 6899999744 | tf_op jit(solution)/shard_map/terms/pallas_call | solution.py:37
  56.3 1.0 %collective-permute-done.20.other_ref = bf16[32,3584]{1,0:T(8,128)(2,1)S(1)} collective-permute-done((bf16[32,3584]{1,0:T(8,128)(2,1)S(1)}, bf16[32,3584]{1,0:T(8,128)(2,1)S(1)}, u32[]{:S(2)}, u32[]{:S(2)}) %collective-permute-start.20) | collective-permute-done | bytes 229408 | tf_op jit(solution)/shard_map/ppermute | solution.py:395
  58.2 1.3 %collective-permute-start.25 = (bf16[8,3584]{1,0:T(8,128)(2,1)S(1)}, bf16[8,3584]{1,0:T(8,128)(2,1)S(1)}, u32[]{:S(2)}, u32[]{:S(2)}) collective-permute-start(bf16[8,3584]{1,0:T(8,128)(2,1)S(1)} %get-tuple-element.69), channel_id=1, source_target_pairs={{0,2},{1,3},{2,0},{3,1},{4,6},{5,7},{6,4},{7,5},{8,10},{9,11},{10,... | collective-permute-start | bytes 172040 | tf_op jit(solution)/shard_map/ppermute | solution.py:395
  60.1 1.5 %collective-permute-start.23 = (bf16[4,7168]{1,0:T(4,128)(2,1)S(1)}, bf16[4,7168]{1,0:T(4,128)(2,1)S(1)}, u32[]{:S(2)}, u32[]{:S(2)}) collective-permute-start(bf16[4,7168]{1,0:T(4,128)(2,1)S(1)} %get-tuple-element.65), channel_id=1, source_target_pairs={{0,6},{1,7},{2,4},{3,5},{4,2},{5,3},{6,0},{7,1},{8,14},{9,15},{10,... | collective-permute-start | bytes 172040 | tf_op jit(solution)/shard_map/ppermute | solution.py:395
  61.7 1.3 %collective-permute-start.24 = (bf16[4,7168]{1,0:T(4,128)(2,1)S(1)}, bf16[4,7168]{1,0:T(4,128)(2,1)S(1)}, u32[]{:S(2)}, u32[]{:S(2)}) collective-permute-start(bf16[4,7168]{1,0:T(4,128)(2,1)S(1)} %get-tuple-element.66), channel_id=1, source_target_pairs={{0,2},{1,3},{2,0},{3,1},{4,6},{5,7},{6,4},{7,5},{8,10},{9,11},{10,... | collective-permute-start | bytes 172040 | tf_op jit(solution)/shard_map/ppermute | solution.py:395
  63.0 1.9 %collective-permute-start.27 = (bf16[4,7168]{1,0:T(4,128)(2,1)S(1)}, bf16[4,7168]{1,0:T(4,128)(2,1)S(1)}, u32[]{:S(2)}, u32[]{:S(2)}) collective-permute-start(bf16[4,7168]{1,0:T(4,128)(2,1)S(1)} %get-tuple-element.71), channel_id=1, source_target_pairs={{0,12},{1,13},{2,14},{3,15},{4,8},{5,9},{6,10},{7,11},{8,4},{9,5},... | collective-permute-start | bytes 172040 | tf_op jit(solution)/shard_map/ppermute | solution.py:395
  65.8 3.2 %collective-permute-done.27.refs_4_ = bf16[4,7168]{1,0:T(4,128)(2,1)S(1)} collective-permute-done((bf16[4,7168]{1,0:T(4,128)(2,1)S(1)}, bf16[4,7168]{1,0:T(4,128)(2,1)S(1)}, u32[]{:S(2)}, u32[]{:S(2)}) %collective-permute-start.27) | collective-permute-done | bytes 57376 | tf_op jit(solution)/shard_map/ppermute | solution.py:395
  69.1 2.0 %collective-permute-done.28.refs_5_ = bf16[4,7168]{1,0:T(4,128)(2,1)S(1)} collective-permute-done((bf16[4,7168]{1,0:T(4,128)(2,1)S(1)}, bf16[4,7168]{1,0:T(4,128)(2,1)S(1)}, u32[]{:S(2)}, u32[]{:S(2)}) %collective-permute-start.28) | collective-permute-done | bytes 57376 | tf_op jit(solution)/shard_map/ppermute | solution.py:395
  (73 shorter events, 9.7 us)
Async XLA Ops:
  0.0 15.0 %collective-permute-start.4 = (bf16[1536,1536]{1,0:T(8,128)(2,1)}, bf16[1536,1536]{1,0:T(8,128)(2,1)S(1)}, u32[]{:S(2)}, u32[]{:S(2)}) collective-permute-start(bf16[1536,1536]{1,0:T(8,128)(2,1)} %refs_4_.1), channel_id=1, source_target_pairs={{0,1},{1,0},{2,3},{3,2},{4,5},{5,4},{6,7},{7,6},{8,9},{9,8},{10,11... | collective-permute-start | bytes 14155784 | tf_op jit(solution)/shard_map/ppermute | solution.py:395
  0.5 14.6 %collective-permute-start.5 = (bf16[8,128,512]{2,1,0:T(8,128)(2,1)}, bf16[8,128,512]{2,1,0:T(8,128)(2,1)S(1)}, u32[]{:S(2)}, u32[]{:S(2)}) collective-permute-start(bf16[8,128,512]{2,1,0:T(8,128)(2,1)} %refs_5_.1), channel_id=1, source_target_pairs={{0,1},{1,0},{2,3},{3,2},{4,5},{5,4},{6,7},{7,6},{8,9},{9,8},{10,11... | collective-permute-start | bytes 3145736 | tf_op jit(solution)/shard_map/ppermute | solution.py:395
  0.5 4.8 %collective-permute-start = (bf16[4,1536]{1,0:T(4,128)(2,1)}, bf16[4,1536]{1,0:T(4,128)(2,1)S(1)}, u32[]{:S(2)}, u32[]{:S(2)}) collective-permute-start(bf16[4,1536]{1,0:T(4,128)(2,1)} %refs_0_.1), channel_id=1, source_target_pairs={{0,2},{1,3},{2,0},{3,1},{4,6},{5,7},{6,4},{7,5},{8,10},{9,11},{10,... | collective-permute-start | bytes 36872 | tf_op jit(solution)/shard_map/ppermute | solution.py:395
  4.1 10.9 %slice-start.6 = ((s8[4718592]{0:T(1024)(128)(4,1)}), s8[4194304]{0:T(1024)(128)(4,1)S(1)}, s32[]{:S(2)}) async-start(s8[4718592]{0:T(1024)(128)(4,1)} %bitcast.7), calls=%async_computation.6 | async-start | bytes 8388608
  5.4 21.3 %slice-start.4 = ((s8[7077888]{0:T(1024)(128)(4,1)}), s8[4194304]{0:T(1024)(128)(4,1)S(1)}, s32[]{:S(2)}) async-start(s8[7077888]{0:T(1024)(128)(4,1)} %bitcast.3), calls=%async_computation.4 | async-start | bytes 8388608
  5.4 21.3 %slice-start.5 = ((s8[7077888]{0:T(1024)(128)(4,1)}), s8[2883584]{0:T(1024)(128)(4,1)S(1)}, s32[]{:S(2)}) async-start(s8[7077888]{0:T(1024)(128)(4,1)} %bitcast.3), calls=%async_computation.5 | async-start | bytes 5767168
  5.4 4.7 %collective-permute-start.1 = (bf16[8,1536]{1,0:T(8,128)(2,1)S(1)}, bf16[8,1536]{1,0:T(8,128)(2,1)S(1)}, u32[]{:S(2)}, u32[]{:S(2)}) collective-permute-start(bf16[8,1536]{1,0:T(8,128)(2,1)S(1)} %get-tuple-element.43.refs_0_), channel_id=1, source_target_pairs={{0,4},{1,5},{2,6},{3,7},{4,0},{5,1},{6,2},{7,3},{8,12},{9,13},{10,... | collective-permute-start | bytes 73736 | tf_op jit(solution)/shard_map/ppermute | solution.py:395
  7.6 5.6 %collective-permute-start.2 = (bf16[8,1536]{1,0:T(8,128)(2,1)S(1)}, bf16[8,1536]{1,0:T(8,128)(2,1)S(1)}, u32[]{:S(2)}, u32[]{:S(2)}) collective-permute-start(bf16[8,1536]{1,0:T(8,128)(2,1)S(1)} %get-tuple-element.43.refs_0_), channel_id=1, source_target_pairs={{0,12},{1,13},{2,14},{3,15},{4,8},{5,9},{6,10},{7,11},{8,4},{9,5},... | collective-permute-start | bytes 73736 | tf_op jit(solution)/shard_map/ppermute | solution.py:395
  10.0 5.0 %collective-permute-start.3 = (bf16[8,1536]{1,0:T(8,128)(2,1)S(1)}, bf16[8,1536]{1,0:T(8,128)(2,1)S(1)}, u32[]{:S(2)}, u32[]{:S(2)}) collective-permute-start(bf16[8,1536]{1,0:T(8,128)(2,1)S(1)} %get-tuple-element.43.refs_0_), channel_id=1, source_target_pairs={{0,8},{1,9},{2,10},{3,11},{4,12},{5,13},{6,14},{7,15},{8,0},{9,1},... | collective-permute-start | bytes 73736 | tf_op jit(solution)/shard_map/ppermute | solution.py:395
  17.3 9.2 %collective-permute-start.6 = (bf16[4,144,128]{2,1,0:T(8,128)(2,1)S(1)}, bf16[4,144,128]{2,1,0:T(8,128)(2,1)S(1)}, u32[]{:S(2)}, u32[]{:S(2)}) collective-permute-start(bf16[4,144,128]{2,1,0:T(8,128)(2,1)S(1)} %get-tuple-element.45), channel_id=1, source_target_pairs={{0,2},{1,3},{2,0},{3,1},{4,6},{5,7},{6,4},{7,5},{8,10},{9,11},{10,... | collective-permute-start | bytes 442376 | tf_op jit(solution)/shard_map/ppermute | solution.py:395
  18.9 9.5 %collective-permute-start.10 = (bf16[2,144,128]{2,1,0:T(8,128)(2,1)S(1)}, bf16[2,144,128]{2,1,0:T(8,128)(2,1)S(1)}, u32[]{:S(2)}, u32[]{:S(2)}) collective-permute-start(bf16[2,144,128]{2,1,0:T(8,128)(2,1)S(1)} %get-tuple-element.49), channel_id=1, source_target_pairs={{0,14},{1,15},{2,12},{3,13},{4,10},{5,11},{6,8},{7,9},{8,6},{9,7},... | collective-permute-start | bytes 221192 | tf_op jit(solution)/shard_map/ppermute | solution.py:395
  20.0 10.2 %collective-permute-start.7 = (bf16[2,144,128]{2,1,0:T(8,128)(2,1)S(1)}, bf16[2,144,128]{2,1,0:T(8,128)(2,1)S(1)}, u32[]{:S(2)}, u32[]{:S(2)}) collective-permute-start(bf16[2,144,128]{2,1,0:T(8,128)(2,1)S(1)} %get-tuple-element.46), channel_id=1, source_target_pairs={{0,8},{1,9},{2,10},{3,11},{4,12},{5,13},{6,14},{7,15},{8,0},{9,1},... | collective-permute-start | bytes 221192 | tf_op jit(solution)/shard_map/ppermute | solution.py:395
  20.9 11.5 %collective-permute-start.8 = (bf16[2,144,128]{2,1,0:T(8,128)(2,1)S(1)}, bf16[2,144,128]{2,1,0:T(8,128)(2,1)S(1)}, u32[]{:S(2)}, u32[]{:S(2)}) collective-permute-start(bf16[2,144,128]{2,1,0:T(8,128)(2,1)S(1)} %get-tuple-element.47), channel_id=1, source_target_pairs={{0,10},{1,11},{2,8},{3,9},{4,14},{5,15},{6,12},{7,13},{8,2},{9,3},... | collective-permute-start | bytes 221192 | tf_op jit(solution)/shard_map/ppermute | solution.py:395
  23.9 8.4 %collective-permute-start.9 = (bf16[2,144,128]{2,1,0:T(8,128)(2,1)S(1)}, bf16[2,144,128]{2,1,0:T(8,128)(2,1)S(1)}, u32[]{:S(2)}, u32[]{:S(2)}) collective-permute-start(bf16[2,144,128]{2,1,0:T(8,128)(2,1)S(1)} %get-tuple-element.48), channel_id=1, source_target_pairs={{0,12},{1,13},{2,14},{3,15},{4,8},{5,9},{6,10},{7,11},{8,4},{9,5},... | collective-permute-start | bytes 221192 | tf_op jit(solution)/shard_map/ppermute | solution.py:395
  26.6 6.0 %collective-permute-start.11 = (bf16[4,144,128]{2,1,0:T(8,128)(2,1)S(1)}, bf16[4,144,128]{2,1,0:T(8,128)(2,1)S(1)}, u32[]{:S(2)}, u32[]{:S(2)}) collective-permute-start(bf16[4,144,128]{2,1,0:T(8,128)(2,1)S(1)} %forward.2.after_ref), channel_id=1, source_target_pairs={{0,4},{1,5},{2,6},{3,7},{4,0},{5,1},{6,2},{7,3},{8,12},{9,13},{10,... | collective-permute-start | bytes 442376 | tf_op jit(solution)/shard_map/ppermute | solution.py:395
  28.5 16.6 %collective-permute-start.18 = (bf16[8,512,128]{2,1,0:T(8,128)(2,1)S(1)}, bf16[8,512,128]{2,1,0:T(8,128)(2,1)S(1)}, u32[]{:S(2)}, u32[]{:S(2)}) collective-permute-start(bf16[8,512,128]{2,1,0:T(8,128)(2,1)S(1)} %copy-done.1), channel_id=1, source_target_pairs={{0,1},{1,0},{2,3},{3,2},{4,5},{5,4},{6,7},{7,6},{8,9},{9,8},{10,11... | collective-permute-start | bytes 3145736 | tf_op jit(solution)/shard_map/ppermute | solution.py:395
  36.1 6.8 %collective-permute-start.16 = (bf16[4,32,512]{2,1,0:T(8,128)(2,1)S(1)}, bf16[4,32,512]{2,1,0:T(8,128)(2,1)S(1)}, u32[]{:S(2)}, u32[]{:S(2)}) collective-permute-start(bf16[4,32,512]{2,1,0:T(8,128)(2,1)S(1)} %get-tuple-element.55), channel_id=1, source_target_pairs={{0,2},{1,3},{2,0},{3,1},{4,6},{5,7},{6,4},{7,5},{8,10},{9,11},{10,... | collective-permute-start | bytes 393224 | tf_op jit(solution)/shard_map/ppermute | solution.py:395
  37.4 9.3 %collective-permute-start.12 = (bf16[2,32,512]{2,1,0:T(8,128)(2,1)S(1)}, bf16[2,32,512]{2,1,0:T(8,128)(2,1)S(1)}, u32[]{:S(2)}, u32[]{:S(2)}) collective-permute-start(bf16[2,32,512]{2,1,0:T(8,128)(2,1)S(1)} %get-tuple-element.51), channel_id=1, source_target_pairs={{0,8},{1,9},{2,10},{3,11},{4,12},{5,13},{6,14},{7,15},{8,0},{9,1},... | collective-permute-start | bytes 196616 | tf_op jit(solution)/shard_map/ppermute | solution.py:395
  38.8 9.4 %collective-permute-start.13 = (bf16[2,32,512]{2,1,0:T(8,128)(2,1)S(1)}, bf16[2,32,512]{2,1,0:T(8,128)(2,1)S(1)}, u32[]{:S(2)}, u32[]{:S(2)}) collective-permute-start(bf16[2,32,512]{2,1,0:T(8,128)(2,1)S(1)} %get-tuple-element.52), channel_id=1, source_target_pairs={{0,10},{1,11},{2,8},{3,9},{4,14},{5,15},{6,12},{7,13},{8,2},{9,3},... | collective-permute-start | bytes 196616 | tf_op jit(solution)/shard_map/ppermute | solution.py:395
  40.5 7.6 %collective-permute-start.14 = (bf16[2,32,512]{2,1,0:T(8,128)(2,1)S(1)}, bf16[2,32,512]{2,1,0:T(8,128)(2,1)S(1)}, u32[]{:S(2)}, u32[]{:S(2)}) collective-permute-start(bf16[2,32,512]{2,1,0:T(8,128)(2,1)S(1)} %get-tuple-element.53), channel_id=1, source_target_pairs={{0,12},{1,13},{2,14},{3,15},{4,8},{5,9},{6,10},{7,11},{8,4},{9,5},... | collective-permute-start | bytes 196616 | tf_op jit(solution)/shard_map/ppermute | solution.py:395
  42.8 7.1 %collective-permute-start.15 = (bf16[2,32,512]{2,1,0:T(8,128)(2,1)S(1)}, bf16[2,32,512]{2,1,0:T(8,128)(2,1)S(1)}, u32[]{:S(2)}, u32[]{:S(2)}) collective-permute-start(bf16[2,32,512]{2,1,0:T(8,128)(2,1)S(1)} %get-tuple-element.54), channel_id=1, source_target_pairs={{0,14},{1,15},{2,12},{3,13},{4,10},{5,11},{6,8},{7,9},{8,6},{9,7},... | collective-permute-start | bytes 196616 | tf_op jit(solution)/shard_map/ppermute | solution.py:395
  45.1 5.7 %collective-permute-start.17 = (bf16[4,32,512]{2,1,0:T(8,128)(2,1)S(1)}, bf16[4,32,512]{2,1,0:T(8,128)(2,1)S(1)}, u32[]{:S(2)}, u32[]{:S(2)}) collective-permute-start(bf16[4,32,512]{2,1,0:T(8,128)(2,1)S(1)} %forward.3.after_ref), channel_id=1, source_target_pairs={{0,4},{1,5},{2,6},{3,7},{4,0},{5,1},{6,2},{7,3},{8,12},{9,13},{10,... | collective-permute-start | bytes 393224 | tf_op jit(solution)/shard_map/ppermute | solution.py:395
  51.2 1.3 %collective-permute-start.19 = (bf16[32,1024]{1,0:T(8,128)(2,1)S(1)}, bf16[32,1024]{1,0:T(8,128)(2,1)S(1)}, u32[]{:S(2)}, u32[]{:S(2)}) collective-permute-start(bf16[32,1024]{1,0:T(8,128)(2,1)S(1)} %values.3), channel_id=1, source_target_pairs={{0,1},{1,0},{2,3},{3,2},{4,5},{5,4},{6,7},{7,6},{8,9},{9,8},{10,11... | collective-permute-start | bytes 196616 | tf_op jit(solution)/shard_map/ppermute | solution.py:395
  54.1 2.0 %collective-permute-start.21 = (bf16[32,3584]{1,0:T(8,128)(2,1)S(1)}, bf16[32,3584]{1,0:T(8,128)(2,1)S(1)}, u32[]{:S(2)}, u32[]{:S(2)}) collective-permute-start(bf16[32,3584]{1,0:T(8,128)(2,1)S(1)} %get-tuple-element.61), channel_id=1, source_target_pairs={{0,1},{1,0},{2,3},{3,2},{4,5},{5,4},{6,7},{7,6},{8,9},{9,8},{10,11... | collective-permute-start | bytes 688136 | tf_op jit(solution)/shard_map/ppermute | solution.py:395
  55.6 1.7 %collective-permute-start.20 = (bf16[32,3584]{1,0:T(8,128)(2,1)S(1)}, bf16[32,3584]{1,0:T(8,128)(2,1)S(1)}, u32[]{:S(2)}, u32[]{:S(2)}) collective-permute-start(bf16[32,3584]{1,0:T(8,128)(2,1)S(1)} %get-tuple-element.59), channel_id=1, source_target_pairs={{0,1},{1,0},{2,3},{3,2},{4,5},{5,4},{6,7},{7,6},{8,9},{9,8},{10,11... | collective-permute-start | bytes 688136 | tf_op jit(solution)/shard_map/ppermute | solution.py:395
  57.4 5.6 %collective-permute-start.26 = (bf16[8,3584]{1,0:T(8,128)(2,1)S(1)}, bf16[8,3584]{1,0:T(8,128)(2,1)S(1)}, u32[]{:S(2)}, u32[]{:S(2)}) collective-permute-start(bf16[8,3584]{1,0:T(8,128)(2,1)S(1)} %get-tuple-element.70), channel_id=1, source_target_pairs={{0,2},{1,3},{2,0},{3,1},{4,6},{5,7},{6,4},{7,5},{8,10},{9,11},{10,... | collective-permute-start | bytes 172040 | tf_op jit(solution)/shard_map/ppermute | solution.py:395
  58.2 4.8 %collective-permute-start.25 = (bf16[8,3584]{1,0:T(8,128)(2,1)S(1)}, bf16[8,3584]{1,0:T(8,128)(2,1)S(1)}, u32[]{:S(2)}, u32[]{:S(2)}) collective-permute-start(bf16[8,3584]{1,0:T(8,128)(2,1)S(1)} %get-tuple-element.69), channel_id=1, source_target_pairs={{0,2},{1,3},{2,0},{3,1},{4,6},{5,7},{6,4},{7,5},{8,10},{9,11},{10,... | collective-permute-start | bytes 172040 | tf_op jit(solution)/shard_map/ppermute | solution.py:395
  59.5 5.7 %collective-permute-start.22 = (bf16[4,7168]{1,0:T(4,128)(2,1)S(1)}, bf16[4,7168]{1,0:T(4,128)(2,1)S(1)}, u32[]{:S(2)}, u32[]{:S(2)}) collective-permute-start(bf16[4,7168]{1,0:T(4,128)(2,1)S(1)} %get-tuple-element.64), channel_id=1, source_target_pairs={{0,4},{1,5},{2,6},{3,7},{4,0},{5,1},{6,2},{7,3},{8,12},{9,13},{10,... | collective-permute-start | bytes 172040 | tf_op jit(solution)/shard_map/ppermute | solution.py:395
  60.1 5.1 %collective-permute-start.23 = (bf16[4,7168]{1,0:T(4,128)(2,1)S(1)}, bf16[4,7168]{1,0:T(4,128)(2,1)S(1)}, u32[]{:S(2)}, u32[]{:S(2)}) collective-permute-start(bf16[4,7168]{1,0:T(4,128)(2,1)S(1)} %get-tuple-element.65), channel_id=1, source_target_pairs={{0,6},{1,7},{2,4},{3,5},{4,2},{5,3},{6,0},{7,1},{8,14},{9,15},{10,... | collective-permute-start | bytes 172040 | tf_op jit(solution)/shard_map/ppermute | solution.py:395
  61.7 4.2 %collective-permute-start.24 = (bf16[4,7168]{1,0:T(4,128)(2,1)S(1)}, bf16[4,7168]{1,0:T(4,128)(2,1)S(1)}, u32[]{:S(2)}, u32[]{:S(2)}) collective-permute-start(bf16[4,7168]{1,0:T(4,128)(2,1)S(1)} %get-tuple-element.66), channel_id=1, source_target_pairs={{0,2},{1,3},{2,0},{3,1},{4,6},{5,7},{6,4},{7,5},{8,10},{9,11},{10,... | collective-permute-start | bytes 172040 | tf_op jit(solution)/shard_map/ppermute | solution.py:395
  63.0 6.0 %collective-permute-start.27 = (bf16[4,7168]{1,0:T(4,128)(2,1)S(1)}, bf16[4,7168]{1,0:T(4,128)(2,1)S(1)}, u32[]{:S(2)}, u32[]{:S(2)}) collective-permute-start(bf16[4,7168]{1,0:T(4,128)(2,1)S(1)} %get-tuple-element.71), channel_id=1, source_target_pairs={{0,12},{1,13},{2,14},{3,15},{4,8},{5,9},{6,10},{7,11},{8,4},{9,5},... | collective-permute-start | bytes 172040 | tf_op jit(solution)/shard_map/ppermute | solution.py:395
  64.9 6.1 %collective-permute-start.28 = (bf16[4,7168]{1,0:T(4,128)(2,1)S(1)}, bf16[4,7168]{1,0:T(4,128)(2,1)S(1)}, u32[]{:S(2)}, u32[]{:S(2)}) collective-permute-start(bf16[4,7168]{1,0:T(4,128)(2,1)S(1)} %get-tuple-element.72), channel_id=1, source_target_pairs={{0,8},{1,9},{2,10},{3,11},{4,12},{5,13},{6,14},{7,15},{8,0},{9,1},... | collective-permute-start | bytes 172040 | tf_op jit(solution)/shard_map/ppermute | solution.py:395
  (11 other events, 62.4 us)

commit v21 on v13

--- a/solution.py
+++ b/solution.py
@@ -60,7 +60,7 @@
 
 def far_chips(devices):
     chips = [k for k in far_first(devices, 2) if k > Y + Z1]
-    return chips[:1] + chips[:0:-1]
+    return [k for k in chips if not k & Y] + [k for k in chips if k & Y]
 
 
 def chip_order(devices):

time: 70.1 us -> 69.9 us (level)
    ppermute x28, waiting for transfers between devices: 22.6 us -> 21.9 us  [swap(): return lax.ppermute(block, 'row', [(i, i ^ k) for i in range(devices)])]
  transfers between devices with their start and end apart: 28 -> 28, of which waited for: 12 -> 13; matrix products, arithmetic and copies ran while one was open for 0% -> 0% of each run, Pallas kernels for 6% -> 6%
where the time goes in v21:
time: 69.9 us; the launch traced here: 69.7 us
  starting transfers between devices  34.7 us (50%)
  waiting for transfers between devices  21.9 us (31%)
  Pallas kernels  12.1 us (17%)
  local copies, waits for them, and re-layouts  0.72 us (1%)
    ppermute x28, starting transfers between devices, swap(): return lax.ppermute(block, 'row', [(i, i ^ k) for i in range(devices)])  34.7 us
    ppermute x28, waiting for transfers between devices, swap(): return lax.ppermute(block, 'row', [(i, i ^ k) for i in range(devices)])  21.9 us
    pallas_call x16, Pallas kernels, run(): pl.pallas_call(kernel, out_shape=out_shape, in_specs=smem + [in_vmem()] *...  12.1 us
  transfers between devices with their start and end apart: 28, of which 13 were waited for; matrix products, arithmetic and copies ran while one was open for 0% of the time, Pallas kernels for 6%

profile of v21, /device:TPU:0, one launch (start us, length us, event | category | flops | bytes accessed | tf_op | source)
XLA Modules:
  0.0 69.7 jit_solution(17028158611499518288)
XLA Ops:
  0.5 3.0 %collective-permute-start = (bf16[4,1536]{1,0:T(4,128)(2,1)}, bf16[4,1536]{1,0:T(4,128)(2,1)S(1)}, u32[]{:S(2)}, u32[]{:S(2)}) collective-permute-start(bf16[4,1536]{1,0:T(4,128)(2,1)} %refs_0_.1), channel_id=1, source_target_pairs={{0,2},{1,3},{2,0},{3,1},{4,6},{5,7},{6,4},{7,5},{8,10},{9,11},{10,... | collective-permute-start | bytes 36872 | tf_op jit(solution)/shard_map/ppermute | solution.py:414
  5.4 3.2 %collective-permute-start.3 = (bf16[8,1536]{1,0:T(8,128)(2,1)S(1)}, bf16[8,1536]{1,0:T(8,128)(2,1)S(1)}, u32[]{:S(2)}, u32[]{:S(2)}) collective-permute-start(bf16[8,1536]{1,0:T(8,128)(2,1)S(1)} %get-tuple-element.43.refs_0_), channel_id=1, source_target_pairs={{0,8},{1,9},{2,10},{3,11},{4,12},{5,13},{6,14},{7,15},{8,0},{9,1},... | collective-permute-start | bytes 73736 | tf_op jit(solution)/shard_map/ppermute | solution.py:414
  8.6 1.3 %collective-permute-start.2 = (bf16[8,1536]{1,0:T(8,128)(2,1)S(1)}, bf16[8,1536]{1,0:T(8,128)(2,1)S(1)}, u32[]{:S(2)}, u32[]{:S(2)}) collective-permute-start(bf16[8,1536]{1,0:T(8,128)(2,1)S(1)} %get-tuple-element.43.refs_0_), channel_id=1, source_target_pairs={{0,12},{1,13},{2,14},{3,15},{4,8},{5,9},{6,10},{7,11},{8,4},{9,5},... | collective-permute-start | bytes 73736 | tf_op jit(solution)/shard_map/ppermute | solution.py:414
  10.4 3.8 %collective-permute-done.2.refs_2_ = bf16[8,1536]{1,0:T(8,128)(2,1)S(1)} collective-permute-done((bf16[8,1536]{1,0:T(8,128)(2,1)S(1)}, bf16[8,1536]{1,0:T(8,128)(2,1)S(1)}, u32[]{:S(2)}, u32[]{:S(2)}) %collective-permute-start.2) | collective-permute-done | bytes 24608 | tf_op jit(solution)/shard_map/ppermute | solution.py:414
  14.2 2.3 %project.1 = (bf16[2,144,128]{2,1,0:T(8,128)(2,1)S(1)}, bf16[2,144,128]{2,1,0:T(8,128)(2,1)S(1)}, bf16[2,144,128]{2,1,0:T(8,128)(2,1)S(1)}, bf16[2,144,128]{2,1,...) custom-call(bf16[8,1536]{1,0:T(8,128)(2,1)S(1)} %get-tuple-element.4, ...), custom_call_target="tpu_custom_call" | custom-call | flops 23000000512 | tf_op jit(solution)/shard_map/project/pallas_call | solution.py:37
  16.5 1.6 %collective-permute-start.6 = (bf16[4,144,128]{2,1,0:T(8,128)(2,1)S(1)}, bf16[4,144,128]{2,1,0:T(8,128)(2,1)S(1)}, u32[]{:S(2)}, u32[]{:S(2)}) collective-permute-start(bf16[4,144,128]{2,1,0:T(8,128)(2,1)S(1)} %get-tuple-element.45), channel_id=1, source_target_pairs={{0,2},{1,3},{2,0},{3,1},{4,6},{5,7},{6,4},{7,5},{8,10},{9,11},{10,... | collective-permute-start | bytes 442376 | tf_op jit(solution)/shard_map/ppermute | solution.py:414
  18.1 1.2 %collective-permute-start.7 = (bf16[2,144,128]{2,1,0:T(8,128)(2,1)S(1)}, bf16[2,144,128]{2,1,0:T(8,128)(2,1)S(1)}, u32[]{:S(2)}, u32[]{:S(2)}) collective-permute-start(bf16[2,144,128]{2,1,0:T(8,128)(2,1)S(1)} %get-tuple-element.46), channel_id=1, source_target_pairs={{0,8},{1,9},{2,10},{3,11},{4,12},{5,13},{6,14},{7,15},{8,0},{9,1},... | collective-permute-start | bytes 221192 | tf_op jit(solution)/shard_map/ppermute | solution.py:414
  19.4 0.9 %collective-permute-start.8 = (bf16[2,144,128]{2,1,0:T(8,128)(2,1)S(1)}, bf16[2,144,128]{2,1,0:T(8,128)(2,1)S(1)}, u32[]{:S(2)}, u32[]{:S(2)}) collective-permute-start(bf16[2,144,128]{2,1,0:T(8,128)(2,1)S(1)} %get-tuple-element.47), channel_id=1, source_target_pairs={{0,12},{1,13},{2,14},{3,15},{4,8},{5,9},{6,10},{7,11},{8,4},{9,5},... | collective-permute-start | bytes 221192 | tf_op jit(solution)/shard_map/ppermute | solution.py:414
  20.3 1.8 %collective-permute-start.9 = (bf16[2,144,128]{2,1,0:T(8,128)(2,1)S(1)}, bf16[2,144,128]{2,1,0:T(8,128)(2,1)S(1)}, u32[]{:S(2)}, u32[]{:S(2)}) collective-permute-start(bf16[2,144,128]{2,1,0:T(8,128)(2,1)S(1)} %get-tuple-element.48), channel_id=1, source_target_pairs={{0,10},{1,11},{2,8},{3,9},{4,14},{5,15},{6,12},{7,13},{8,2},{9,3},... | collective-permute-start | bytes 221192 | tf_op jit(solution)/shard_map/ppermute | solution.py:414
  22.1 2.8 %collective-permute-start.10 = (bf16[2,144,128]{2,1,0:T(8,128)(2,1)S(1)}, bf16[2,144,128]{2,1,0:T(8,128)(2,1)S(1)}, u32[]{:S(2)}, u32[]{:S(2)}) collective-permute-start(bf16[2,144,128]{2,1,0:T(8,128)(2,1)S(1)} %get-tuple-element.49), channel_id=1, source_target_pairs={{0,14},{1,15},{2,12},{3,13},{4,10},{5,11},{6,8},{7,9},{8,6},{9,7},... | collective-permute-start | bytes 221192 | tf_op jit(solution)/shard_map/ppermute | solution.py:414
  25.0 1.7 %flip.1.flip_ref = bf16[4,1536,512]{2,1,0:T(8,128)(2,1)S(1)} custom-call(bf16[4,576,1536]{2,1,0:T(8,128)(2,1)S(1)} %bitcast.5, bf16[4,144,128]{2,1,0:T(8,128)(2,1)S(1)} %forward.2.after_ref), custom_call_target="tpu_custom_call" | custom-call | flops 4600000000 | tf_op jit(solution)/shard_map/flip/pallas_call | solution.py:37
  26.7 1.2 %collective-permute-done.7.refs_0_ = bf16[2,144,128]{2,1,0:T(8,128)(2,1)S(1)} collective-permute-done((bf16[2,144,128]{2,1,0:T(8,128)(2,1)S(1)}, bf16[2,144,128]{2,1,0:T(8,128)(2,1)S(1)}, u32[]{:S(2)}, u32[]{:S(2)}) %collective-permute-start.7) | collective-permute-done | bytes 73760 | tf_op jit(solution)/shard_map/ppermute | solution.py:414
  28.0 3.1 %collective-permute-done.9.refs_2_ = bf16[2,144,128]{2,1,0:T(8,128)(2,1)S(1)} collective-permute-done((bf16[2,144,128]{2,1,0:T(8,128)(2,1)S(1)}, bf16[2,144,128]{2,1,0:T(8,128)(2,1)S(1)}, u32[]{:S(2)}, u32[]{:S(2)}) %collective-permute-start.9) | collective-permute-done | bytes 73760 | tf_op jit(solution)/shard_map/ppermute | solution.py:414
  31.8 3.4 %attend.1 = (bf16[2,32,512]{2,1,0:T(8,128)(2,1)S(1)}, bf16[2,32,512]{2,1,0:T(8,128)(2,1)S(1)}, bf16[2,32,512]{2,1,0:T(8,128)(2,1)S(1)}, bf16[2,32,512]{2,1,0:T(8...) custom-call(s32[4]{0:T(128)S(1)} %copy-done.5, ...), custom_call_target="tpu_custom_call" | custom-call | flops 11500000256 | tf_op jit(solution)/shard_map/attend/pallas_call | solution.py:37
  36.2 2.4 %collective-permute-start.12 = (bf16[2,32,512]{2,1,0:T(8,128)(2,1)S(1)}, bf16[2,32,512]{2,1,0:T(8,128)(2,1)S(1)}, u32[]{:S(2)}, u32[]{:S(2)}) collective-permute-start(bf16[2,32,512]{2,1,0:T(8,128)(2,1)S(1)} %get-tuple-element.51), channel_id=1, source_target_pairs={{0,8},{1,9},{2,10},{3,11},{4,12},{5,13},{6,14},{7,15},{8,0},{9,1},... | collective-permute-start | bytes 196616 | tf_op jit(solution)/shard_map/ppermute | solution.py:414
  38.5 1.2 %collective-permute-start.13 = (bf16[2,32,512]{2,1,0:T(8,128)(2,1)S(1)}, bf16[2,32,512]{2,1,0:T(8,128)(2,1)S(1)}, u32[]{:S(2)}, u32[]{:S(2)}) collective-permute-start(bf16[2,32,512]{2,1,0:T(8,128)(2,1)S(1)} %get-tuple-element.52), channel_id=1, source_target_pairs={{0,12},{1,13},{2,14},{3,15},{4,8},{5,9},{6,10},{7,11},{8,4},{9,5},... | collective-permute-start | bytes 196616 | tf_op jit(solution)/shard_map/ppermute | solution.py:414
  39.8 1.1 %collective-permute-start.14 = (bf16[2,32,512]{2,1,0:T(8,128)(2,1)S(1)}, bf16[2,32,512]{2,1,0:T(8,128)(2,1)S(1)}, u32[]{:S(2)}, u32[]{:S(2)}) collective-permute-start(bf16[2,32,512]{2,1,0:T(8,128)(2,1)S(1)} %get-tuple-element.53), channel_id=1, source_target_pairs={{0,10},{1,11},{2,8},{3,9},{4,14},{5,15},{6,12},{7,13},{8,2},{9,3},... | collective-permute-start | bytes 196616 | tf_op jit(solution)/shard_map/ppermute | solution.py:414
  40.9 2.1 %collective-permute-start.15 = (bf16[2,32,512]{2,1,0:T(8,128)(2,1)S(1)}, bf16[2,32,512]{2,1,0:T(8,128)(2,1)S(1)}, u32[]{:S(2)}, u32[]{:S(2)}) collective-permute-start(bf16[2,32,512]{2,1,0:T(8,128)(2,1)S(1)} %get-tuple-element.54), channel_id=1, source_target_pairs={{0,14},{1,15},{2,12},{3,13},{4,10},{5,11},{6,8},{7,9},{8,6},{9,7},... | collective-permute-start | bytes 196616 | tf_op jit(solution)/shard_map/ppermute | solution.py:414
  42.9 1.3 %collective-permute-start.17 = (bf16[4,32,512]{2,1,0:T(8,128)(2,1)S(1)}, bf16[4,32,512]{2,1,0:T(8,128)(2,1)S(1)}, u32[]{:S(2)}, u32[]{:S(2)}) collective-permute-start(bf16[4,32,512]{2,1,0:T(8,128)(2,1)S(1)} %forward.3.after_ref), channel_id=1, source_target_pairs={{0,4},{1,5},{2,6},{3,7},{4,0},{5,1},{6,2},{7,3},{8,12},{9,13},{10,... | collective-permute-start | bytes 393224 | tf_op jit(solution)/shard_map/ppermute | solution.py:414
  44.3 1.9 %collective-permute-done.12.refs_0_ = bf16[2,32,512]{2,1,0:T(8,128)(2,1)S(1)} collective-permute-done((bf16[2,32,512]{2,1,0:T(8,128)(2,1)S(1)}, bf16[2,32,512]{2,1,0:T(8,128)(2,1)S(1)}, u32[]{:S(2)}, u32[]{:S(2)}) %collective-permute-start.12) | collective-permute-done | bytes 65568 | tf_op jit(solution)/shard_map/ppermute | solution.py:414
  46.2 3.3 %collective-permute-done.14.refs_2_ = bf16[2,32,512]{2,1,0:T(8,128)(2,1)S(1)} collective-permute-done((bf16[2,32,512]{2,1,0:T(8,128)(2,1)S(1)}, bf16[2,32,512]{2,1,0:T(8,128)(2,1)S(1)}, u32[]{:S(2)}, u32[]{:S(2)}) %collective-permute-start.14) | collective-permute-done | bytes 65568 | tf_op jit(solution)/shard_map/ppermute | solution.py:414
  49.6 1.5 %collective-permute-done.18.refs_7_ = bf16[8,32,512]{2,1,0:T(8,128)(2,1)S(1)} collective-permute-done((bf16[8,32,512]{2,1,0:T(8,128)(2,1)S(1)}, bf16[8,32,512]{2,1,0:T(8,128)(2,1)S(1)}, u32[]{:S(2)}, u32[]{:S(2)}) %collective-permute-start.18) | collective-permute-done | bytes 262176 | tf_op jit(solution)/shard_map/ppermute | solution.py:414
  51.7 1.4 %terms.3 = (f32[32,3584]{1,0:T(8,128)S(1)}, bf16[32,3584]{1,0:T(8,128)(2,1)S(1)}) custom-call(bf16[64,1024]{1,0:T(8,128)(2,1)S(1)} %values.1.val_ref, bf16[1024,7168]{1,0:T(8,128)(2,1)S(1)} %bitcast.2), custom_call_target="tpu_custom_call" | custom-call | flops 6899999744 | tf_op jit(solution)/shard_map/terms/pallas_call | solution.py:37
  53.3 1.4 %terms.2 = (f32[32,3584]{1,0:T(8,128)S(1)}, bf16[32,3584]{1,0:T(8,128)(2,1)S(1)}) custom-call(bf16[64,1024]{1,0:T(8,128)(2,1)S(1)} %values.1.val_ref, bf16[1024,7168]{1,0:T(8,128)(2,1)S(1)} %bitcast.2), custom_call_target="tpu_custom_call" | custom-call | flops 6899999744 | tf_op jit(solution)/shard_map/terms/pallas_call | solution.py:37
  55.2 1.2 %collective-permute-start.24 = (bf16[8,3584]{1,0:T(8,128)(2,1)S(1)}, bf16[8,3584]{1,0:T(8,128)(2,1)S(1)}, u32[]{:S(2)}, u32[]{:S(2)}) collective-permute-start(bf16[8,3584]{1,0:T(8,128)(2,1)S(1)} %get-tuple-element.69), channel_id=1, source_target_pairs={{0,2},{1,3},{2,0},{3,1},{4,6},{5,7},{6,4},{7,5},{8,10},{9,11},{10,... | collective-permute-start | bytes 172040 | tf_op jit(solution)/shard_map/ppermute | solution.py:414
  56.4 1.1 %collective-permute-start.25 = (bf16[8,3584]{1,0:T(8,128)(2,1)S(1)}, bf16[8,3584]{1,0:T(8,128)(2,1)S(1)}, u32[]{:S(2)}, u32[]{:S(2)}) collective-permute-start(bf16[8,3584]{1,0:T(8,128)(2,1)S(1)} %get-tuple-element.70), channel_id=1, source_target_pairs={{0,2},{1,3},{2,0},{3,1},{4,6},{5,7},{6,4},{7,5},{8,10},{9,11},{10,... | collective-permute-start | bytes 172040 | tf_op jit(solution)/shard_map/ppermute | solution.py:414
  57.5 1.2 %collective-permute-start.21 = (bf16[4,7168]{1,0:T(4,128)(2,1)S(1)}, bf16[4,7168]{1,0:T(4,128)(2,1)S(1)}, u32[]{:S(2)}, u32[]{:S(2)}) collective-permute-start(bf16[4,7168]{1,0:T(4,128)(2,1)S(1)} %get-tuple-element.64), channel_id=1, source_target_pairs={{0,4},{1,5},{2,6},{3,7},{4,0},{5,1},{6,2},{7,3},{8,12},{9,13},{10,... | collective-permute-start | bytes 172040 | tf_op jit(solution)/shard_map/ppermute | solution.py:414
  58.7 1.3 %collective-permute-start.22 = (bf16[4,7168]{1,0:T(4,128)(2,1)S(1)}, bf16[4,7168]{1,0:T(4,128)(2,1)S(1)}, u32[]{:S(2)}, u32[]{:S(2)}) collective-permute-start(bf16[4,7168]{1,0:T(4,128)(2,1)S(1)} %get-tuple-element.65), channel_id=1, source_target_pairs={{0,6},{1,7},{2,4},{3,5},{4,2},{5,3},{6,0},{7,1},{8,14},{9,15},{10,... | collective-permute-start | bytes 172040 | tf_op jit(solution)/shard_map/ppermute | solution.py:414
  60.0 1.0 %collective-permute-start.23 = (bf16[4,7168]{1,0:T(4,128)(2,1)S(1)}, bf16[4,7168]{1,0:T(4,128)(2,1)S(1)}, u32[]{:S(2)}, u32[]{:S(2)}) collective-permute-start(bf16[4,7168]{1,0:T(4,128)(2,1)S(1)} %get-tuple-element.66), channel_id=1, source_target_pairs={{0,2},{1,3},{2,0},{3,1},{4,6},{5,7},{6,4},{7,5},{8,10},{9,11},{10,... | collective-permute-start | bytes 172040 | tf_op jit(solution)/shard_map/ppermute | solution.py:414
  61.0 1.8 %collective-permute-start.26 = (bf16[4,7168]{1,0:T(4,128)(2,1)S(1)}, bf16[4,7168]{1,0:T(4,128)(2,1)S(1)}, u32[]{:S(2)}, u32[]{:S(2)}) collective-permute-start(bf16[4,7168]{1,0:T(4,128)(2,1)S(1)} %get-tuple-element.71), channel_id=1, source_target_pairs={{0,12},{1,13},{2,14},{3,15},{4,8},{5,9},{6,10},{7,11},{8,4},{9,5},... | collective-permute-start | bytes 172040 | tf_op jit(solution)/shard_map/ppermute | solution.py:414
  64.4 2.7 %collective-permute-done.26.refs_4_ = bf16[4,7168]{1,0:T(4,128)(2,1)S(1)} collective-permute-done((bf16[4,7168]{1,0:T(4,128)(2,1)S(1)}, bf16[4,7168]{1,0:T(4,128)(2,1)S(1)}, u32[]{:S(2)}, u32[]{:S(2)}) %collective-permute-start.26) | collective-permute-done | bytes 57376 | tf_op jit(solution)/shard_map/ppermute | solution.py:414
  67.1 2.0 %collective-permute-done.27.refs_5_ = bf16[4,7168]{1,0:T(4,128)(2,1)S(1)} collective-permute-done((bf16[4,7168]{1,0:T(4,128)(2,1)S(1)}, bf16[4,7168]{1,0:T(4,128)(2,1)S(1)}, u32[]{:S(2)}, u32[]{:S(2)}) %collective-permute-start.27) | collective-permute-done | bytes 57376 | tf_op jit(solution)/shard_map/ppermute | solution.py:414
  (71 shorter events, 8.3 us)
Async XLA Ops:
  0.0 14.2 %collective-permute-start.4 = (bf16[1536,1536]{1,0:T(8,128)(2,1)}, bf16[1536,1536]{1,0:T(8,128)(2,1)S(1)}, u32[]{:S(2)}, u32[]{:S(2)}) collective-permute-start(bf16[1536,1536]{1,0:T(8,128)(2,1)} %refs_4_.1), channel_id=1, source_target_pairs={{0,1},{1,0},{2,3},{3,2},{4,5},{5,4},{6,7},{7,6},{8,9},{9,8},{10,11... | collective-permute-start | bytes 14155784 | tf_op jit(solution)/shard_map/ppermute | solution.py:414
  0.5 13.7 %collective-permute-start.5 = (bf16[8,128,512]{2,1,0:T(8,128)(2,1)}, bf16[8,128,512]{2,1,0:T(8,128)(2,1)S(1)}, u32[]{:S(2)}, u32[]{:S(2)}) collective-permute-start(bf16[8,128,512]{2,1,0:T(8,128)(2,1)} %refs_5_.1), channel_id=1, source_target_pairs={{0,1},{1,0},{2,3},{3,2},{4,5},{5,4},{6,7},{7,6},{8,9},{9,8},{10,11... | collective-permute-start | bytes 3145736 | tf_op jit(solution)/shard_map/ppermute | solution.py:414
  0.5 4.8 %collective-permute-start = (bf16[4,1536]{1,0:T(4,128)(2,1)}, bf16[4,1536]{1,0:T(4,128)(2,1)S(1)}, u32[]{:S(2)}, u32[]{:S(2)}) collective-permute-start(bf16[4,1536]{1,0:T(4,128)(2,1)} %refs_0_.1), channel_id=1, source_target_pairs={{0,2},{1,3},{2,0},{3,1},{4,6},{5,7},{6,4},{7,5},{8,10},{9,11},{10,... | collective-permute-start | bytes 36872 | tf_op jit(solution)/shard_map/ppermute | solution.py:414
  4.1 10.1 %slice-start.6 = ((s8[4718592]{0:T(1024)(128)(4,1)}), s8[4194304]{0:T(1024)(128)(4,1)S(1)}, s32[]{:S(2)}) async-start(s8[4718592]{0:T(1024)(128)(4,1)} %bitcast.7), calls=%async_computation.6 | async-start | bytes 8388608
  5.4 8.9 %copy-start = (bf16[8,128,512]{2,1,0:T(8,128)(2,1)S(1)}, bf16[8,128,512]{2,1,0:T(8,128)(2,1)}, u32[]{:S(2)}) copy-start(bf16[8,128,512]{2,1,0:T(8,128)(2,1)} %refs_5_.1) | copy-start | bytes 3145732
  5.4 19.6 %slice-start.4 = ((s8[7077888]{0:T(1024)(128)(4,1)}), s8[4194304]{0:T(1024)(128)(4,1)S(1)}, s32[]{:S(2)}) async-start(s8[7077888]{0:T(1024)(128)(4,1)} %bitcast.3), calls=%async_computation.4 | async-start | bytes 8388608
  5.4 19.6 %slice-start.5 = ((s8[7077888]{0:T(1024)(128)(4,1)}), s8[2883584]{0:T(1024)(128)(4,1)S(1)}, s32[]{:S(2)}) async-start(s8[7077888]{0:T(1024)(128)(4,1)} %bitcast.3), calls=%async_computation.5 | async-start | bytes 5767168
  5.4 5.0 %collective-permute-start.3 = (bf16[8,1536]{1,0:T(8,128)(2,1)S(1)}, bf16[8,1536]{1,0:T(8,128)(2,1)S(1)}, u32[]{:S(2)}, u32[]{:S(2)}) collective-permute-start(bf16[8,1536]{1,0:T(8,128)(2,1)S(1)} %get-tuple-element.43.refs_0_), channel_id=1, source_target_pairs={{0,8},{1,9},{2,10},{3,11},{4,12},{5,13},{6,14},{7,15},{8,0},{9,1},... | collective-permute-start | bytes 73736 | tf_op jit(solution)/shard_map/ppermute | solution.py:414
  8.6 5.6 %collective-permute-start.2 = (bf16[8,1536]{1,0:T(8,128)(2,1)S(1)}, bf16[8,1536]{1,0:T(8,128)(2,1)S(1)}, u32[]{:S(2)}, u32[]{:S(2)}) collective-permute-start(bf16[8,1536]{1,0:T(8,128)(2,1)S(1)} %get-tuple-element.43.refs_0_), channel_id=1, source_target_pairs={{0,12},{1,13},{2,14},{3,15},{4,8},{5,9},{6,10},{7,11},{8,4},{9,5},... | collective-permute-start | bytes 73736 | tf_op jit(solution)/shard_map/ppermute | solution.py:414
  9.9 4.3 %collective-permute-start.1 = (bf16[8,1536]{1,0:T(8,128)(2,1)S(1)}, bf16[8,1536]{1,0:T(8,128)(2,1)S(1)}, u32[]{:S(2)}, u32[]{:S(2)}) collective-permute-start(bf16[8,1536]{1,0:T(8,128)(2,1)S(1)} %get-tuple-element.43.refs_0_), channel_id=1, source_target_pairs={{0,4},{1,5},{2,6},{3,7},{4,0},{5,1},{6,2},{7,3},{8,12},{9,13},{10,... | collective-permute-start | bytes 73736 | tf_op jit(solution)/shard_map/ppermute | solution.py:414
  16.5 8.3 %collective-permute-start.6 = (bf16[4,144,128]{2,1,0:T(8,128)(2,1)S(1)}, bf16[4,144,128]{2,1,0:T(8,128)(2,1)S(1)}, u32[]{:S(2)}, u32[]{:S(2)}) collective-permute-start(bf16[4,144,128]{2,1,0:T(8,128)(2,1)S(1)} %get-tuple-element.45), channel_id=1, source_target_pairs={{0,2},{1,3},{2,0},{3,1},{4,6},{5,7},{6,4},{7,5},{8,10},{9,11},{10,... | collective-permute-start | bytes 442376 | tf_op jit(solution)/shard_map/ppermute | solution.py:414
  18.1 9.9 %collective-permute-start.7 = (bf16[2,144,128]{2,1,0:T(8,128)(2,1)S(1)}, bf16[2,144,128]{2,1,0:T(8,128)(2,1)S(1)}, u32[]{:S(2)}, u32[]{:S(2)}) collective-permute-start(bf16[2,144,128]{2,1,0:T(8,128)(2,1)S(1)} %get-tuple-element.46), channel_id=1, source_target_pairs={{0,8},{1,9},{2,10},{3,11},{4,12},{5,13},{6,14},{7,15},{8,0},{9,1},... | collective-permute-start | bytes 221192 | tf_op jit(solution)/shard_map/ppermute | solution.py:414
  19.4 8.6 %collective-permute-start.8 = (bf16[2,144,128]{2,1,0:T(8,128)(2,1)S(1)}, bf16[2,144,128]{2,1,0:T(8,128)(2,1)S(1)}, u32[]{:S(2)}, u32[]{:S(2)}) collective-permute-start(bf16[2,144,128]{2,1,0:T(8,128)(2,1)S(1)} %get-tuple-element.47), channel_id=1, source_target_pairs={{0,12},{1,13},{2,14},{3,15},{4,8},{5,9},{6,10},{7,11},{8,4},{9,5},... | collective-permute-start | bytes 221192 | tf_op jit(solution)/shard_map/ppermute | solution.py:414
  20.3 10.8 %collective-permute-start.9 = (bf16[2,144,128]{2,1,0:T(8,128)(2,1)S(1)}, bf16[2,144,128]{2,1,0:T(8,128)(2,1)S(1)}, u32[]{:S(2)}, u32[]{:S(2)}) collective-permute-start(bf16[2,144,128]{2,1,0:T(8,128)(2,1)S(1)} %get-tuple-element.48), channel_id=1, source_target_pairs={{0,10},{1,11},{2,8},{3,9},{4,14},{5,15},{6,12},{7,13},{8,2},{9,3},... | collective-permute-start | bytes 221192 | tf_op jit(solution)/shard_map/ppermute | solution.py:414
  22.1 9.0 %collective-permute-start.10 = (bf16[2,144,128]{2,1,0:T(8,128)(2,1)S(1)}, bf16[2,144,128]{2,1,0:T(8,128)(2,1)S(1)}, u32[]{:S(2)}, u32[]{:S(2)}) collective-permute-start(bf16[2,144,128]{2,1,0:T(8,128)(2,1)S(1)} %get-tuple-element.49), channel_id=1, source_target_pairs={{0,14},{1,15},{2,12},{3,13},{4,10},{5,11},{6,8},{7,9},{8,6},{9,7},... | collective-permute-start | bytes 221192 | tf_op jit(solution)/shard_map/ppermute | solution.py:414
  24.9 6.9 %collective-permute-start.11 = (bf16[4,144,128]{2,1,0:T(8,128)(2,1)S(1)}, bf16[4,144,128]{2,1,0:T(8,128)(2,1)S(1)}, u32[]{:S(2)}, u32[]{:S(2)}) collective-permute-start(bf16[4,144,128]{2,1,0:T(8,128)(2,1)S(1)} %forward.2.after_ref), channel_id=1, source_target_pairs={{0,4},{1,5},{2,6},{3,7},{4,0},{5,1},{6,2},{7,3},{8,12},{9,13},{10,... | collective-permute-start | bytes 442376 | tf_op jit(solution)/shard_map/ppermute | solution.py:414
  35.2 7.7 %collective-permute-start.16 = (bf16[4,32,512]{2,1,0:T(8,128)(2,1)S(1)}, bf16[4,32,512]{2,1,0:T(8,128)(2,1)S(1)}, u32[]{:S(2)}, u32[]{:S(2)}) collective-permute-start(bf16[4,32,512]{2,1,0:T(8,128)(2,1)S(1)} %get-tuple-element.55), channel_id=1, source_target_pairs={{0,2},{1,3},{2,0},{3,1},{4,6},{5,7},{6,4},{7,5},{8,10},{9,11},{10,... | collective-permute-start | bytes 393224 | tf_op jit(solution)/shard_map/ppermute | solution.py:414
  36.2 10.0 %collective-permute-start.12 = (bf16[2,32,512]{2,1,0:T(8,128)(2,1)S(1)}, bf16[2,32,512]{2,1,0:T(8,128)(2,1)S(1)}, u32[]{:S(2)}, u32[]{:S(2)}) collective-permute-start(bf16[2,32,512]{2,1,0:T(8,128)(2,1)S(1)} %get-tuple-element.51), channel_id=1, source_target_pairs={{0,8},{1,9},{2,10},{3,11},{4,12},{5,13},{6,14},{7,15},{8,0},{9,1},... | collective-permute-start | bytes 196616 | tf_op jit(solution)/shard_map/ppermute | solution.py:414
  38.5 7.6 %collective-permute-start.13 = (bf16[2,32,512]{2,1,0:T(8,128)(2,1)S(1)}, bf16[2,32,512]{2,1,0:T(8,128)(2,1)S(1)}, u32[]{:S(2)}, u32[]{:S(2)}) collective-permute-start(bf16[2,32,512]{2,1,0:T(8,128)(2,1)S(1)} %get-tuple-element.52), channel_id=1, source_target_pairs={{0,12},{1,13},{2,14},{3,15},{4,8},{5,9},{6,10},{7,11},{8,4},{9,5},... | collective-permute-start | bytes 196616 | tf_op jit(solution)/shard_map/ppermute | solution.py:414
  39.8 9.8 %collective-permute-start.14 = (bf16[2,32,512]{2,1,0:T(8,128)(2,1)S(1)}, bf16[2,32,512]{2,1,0:T(8,128)(2,1)S(1)}, u32[]{:S(2)}, u32[]{:S(2)}) collective-permute-start(bf16[2,32,512]{2,1,0:T(8,128)(2,1)S(1)} %get-tuple-element.53), channel_id=1, source_target_pairs={{0,10},{1,11},{2,8},{3,9},{4,14},{5,15},{6,12},{7,13},{8,2},{9,3},... | collective-permute-start | bytes 196616 | tf_op jit(solution)/shard_map/ppermute | solution.py:414
  40.9 8.7 %collective-permute-start.15 = (bf16[2,32,512]{2,1,0:T(8,128)(2,1)S(1)}, bf16[2,32,512]{2,1,0:T(8,128)(2,1)S(1)}, u32[]{:S(2)}, u32[]{:S(2)}) collective-permute-start(bf16[2,32,512]{2,1,0:T(8,128)(2,1)S(1)} %get-tuple-element.54), channel_id=1, source_target_pairs={{0,14},{1,15},{2,12},{3,13},{4,10},{5,11},{6,8},{7,9},{8,6},{9,7},... | collective-permute-start | bytes 196616 | tf_op jit(solution)/shard_map/ppermute | solution.py:414
  42.9 6.6 %collective-permute-start.17 = (bf16[4,32,512]{2,1,0:T(8,128)(2,1)S(1)}, bf16[4,32,512]{2,1,0:T(8,128)(2,1)S(1)}, u32[]{:S(2)}, u32[]{:S(2)}) collective-permute-start(bf16[4,32,512]{2,1,0:T(8,128)(2,1)S(1)} %forward.3.after_ref), channel_id=1, source_target_pairs={{0,4},{1,5},{2,6},{3,7},{4,0},{5,1},{6,2},{7,3},{8,12},{9,13},{10,... | collective-permute-start | bytes 393224 | tf_op jit(solution)/shard_map/ppermute | solution.py:414
  49.6 1.6 %collective-permute-start.18 = (bf16[8,32,512]{2,1,0:T(8,128)(2,1)S(1)}, bf16[8,32,512]{2,1,0:T(8,128)(2,1)S(1)}, u32[]{:S(2)}, u32[]{:S(2)}) collective-permute-start(bf16[8,32,512]{2,1,0:T(8,128)(2,1)S(1)} %regroup.1), channel_id=1, source_target_pairs={{0,1},{1,0},{2,3},{3,2},{4,5},{5,4},{6,7},{7,6},{8,9},{9,8},{10,11... | collective-permute-start | bytes 786440 | tf_op jit(solution)/shard_map/ppermute | solution.py:414
  53.1 2.0 %collective-permute-start.20 = (bf16[32,3584]{1,0:T(8,128)(2,1)S(1)}, bf16[32,3584]{1,0:T(8,128)(2,1)S(1)}, u32[]{:S(2)}, u32[]{:S(2)}) collective-permute-start(bf16[32,3584]{1,0:T(8,128)(2,1)S(1)} %get-tuple-element.61), channel_id=1, source_target_pairs={{0,1},{1,0},{2,3},{3,2},{4,5},{5,4},{6,7},{7,6},{8,9},{9,8},{10,11... | collective-permute-start | bytes 688136 | tf_op jit(solution)/shard_map/ppermute | solution.py:414
  54.6 1.7 %collective-permute-start.19 = (bf16[32,3584]{1,0:T(8,128)(2,1)S(1)}, bf16[32,3584]{1,0:T(8,128)(2,1)S(1)}, u32[]{:S(2)}, u32[]{:S(2)}) collective-permute-start(bf16[32,3584]{1,0:T(8,128)(2,1)S(1)} %get-tuple-element.59), channel_id=1, source_target_pairs={{0,1},{1,0},{2,3},{3,2},{4,5},{5,4},{6,7},{7,6},{8,9},{9,8},{10,11... | collective-permute-start | bytes 688136 | tf_op jit(solution)/shard_map/ppermute | solution.py:414
  55.2 5.8 %collective-permute-start.24 = (bf16[8,3584]{1,0:T(8,128)(2,1)S(1)}, bf16[8,3584]{1,0:T(8,128)(2,1)S(1)}, u32[]{:S(2)}, u32[]{:S(2)}) collective-permute-start(bf16[8,3584]{1,0:T(8,128)(2,1)S(1)} %get-tuple-element.69), channel_id=1, source_target_pairs={{0,2},{1,3},{2,0},{3,1},{4,6},{5,7},{6,4},{7,5},{8,10},{9,11},{10,... | collective-permute-start | bytes 172040 | tf_op jit(solution)/shard_map/ppermute | solution.py:414
  56.4 4.5 %collective-permute-start.25 = (bf16[8,3584]{1,0:T(8,128)(2,1)S(1)}, bf16[8,3584]{1,0:T(8,128)(2,1)S(1)}, u32[]{:S(2)}, u32[]{:S(2)}) collective-permute-start(bf16[8,3584]{1,0:T(8,128)(2,1)S(1)} %get-tuple-element.70), channel_id=1, source_target_pairs={{0,2},{1,3},{2,0},{3,1},{4,6},{5,7},{6,4},{7,5},{8,10},{9,11},{10,... | collective-permute-start | bytes 172040 | tf_op jit(solution)/shard_map/ppermute | solution.py:414
  57.5 6.2 %collective-permute-start.21 = (bf16[4,7168]{1,0:T(4,128)(2,1)S(1)}, bf16[4,7168]{1,0:T(4,128)(2,1)S(1)}, u32[]{:S(2)}, u32[]{:S(2)}) collective-permute-start(bf16[4,7168]{1,0:T(4,128)(2,1)S(1)} %get-tuple-element.64), channel_id=1, source_target_pairs={{0,4},{1,5},{2,6},{3,7},{4,0},{5,1},{6,2},{7,3},{8,12},{9,13},{10,... | collective-permute-start | bytes 172040 | tf_op jit(solution)/shard_map/ppermute | solution.py:414
  58.7 5.1 %collective-permute-start.22 = (bf16[4,7168]{1,0:T(4,128)(2,1)S(1)}, bf16[4,7168]{1,0:T(4,128)(2,1)S(1)}, u32[]{:S(2)}, u32[]{:S(2)}) collective-permute-start(bf16[4,7168]{1,0:T(4,128)(2,1)S(1)} %get-tuple-element.65), channel_id=1, source_target_pairs={{0,6},{1,7},{2,4},{3,5},{4,2},{5,3},{6,0},{7,1},{8,14},{9,15},{10,... | collective-permute-start | bytes 172040 | tf_op jit(solution)/shard_map/ppermute | solution.py:414
  60.0 4.4 %collective-permute-start.23 = (bf16[4,7168]{1,0:T(4,128)(2,1)S(1)}, bf16[4,7168]{1,0:T(4,128)(2,1)S(1)}, u32[]{:S(2)}, u32[]{:S(2)}) collective-permute-start(bf16[4,7168]{1,0:T(4,128)(2,1)S(1)} %get-tuple-element.66), channel_id=1, source_target_pairs={{0,2},{1,3},{2,0},{3,1},{4,6},{5,7},{6,4},{7,5},{8,10},{9,11},{10,... | collective-permute-start | bytes 172040 | tf_op jit(solution)/shard_map/ppermute | solution.py:414
  61.0 6.0 %collective-permute-start.26 = (bf16[4,7168]{1,0:T(4,128)(2,1)S(1)}, bf16[4,7168]{1,0:T(4,128)(2,1)S(1)}, u32[]{:S(2)}, u32[]{:S(2)}) collective-permute-start(bf16[4,7168]{1,0:T(4,128)(2,1)S(1)} %get-tuple-element.71), channel_id=1, source_target_pairs={{0,12},{1,13},{2,14},{3,15},{4,8},{5,9},{6,10},{7,11},{8,4},{9,5},... | collective-permute-start | bytes 172040 | tf_op jit(solution)/shard_map/ppermute | solution.py:414
  62.8 6.2 %collective-permute-start.27 = (bf16[4,7168]{1,0:T(4,128)(2,1)S(1)}, bf16[4,7168]{1,0:T(4,128)(2,1)S(1)}, u32[]{:S(2)}, u32[]{:S(2)}) collective-permute-start(bf16[4,7168]{1,0:T(4,128)(2,1)S(1)} %get-tuple-element.72), channel_id=1, source_target_pairs={{0,8},{1,9},{2,10},{3,11},{4,12},{5,13},{6,14},{7,15},{8,0},{9,1},... | collective-permute-start | bytes 172040 | tf_op jit(solution)/shard_map/ppermute | solution.py:414
  (10 other events, 59.8 us)

commit v22 on v21

--- a/solution.py
+++ b/solution.py
@@ -60,7 +60,7 @@
 
 def far_chips(devices):
     chips = [k for k in far_first(devices, 2) if k > Y + Z1]
-    return [k for k in chips if not k & Y] + [k for k in chips if k & Y]
+    return [k for k in chips if not k & Y] + [k for k in chips[::-1] if k & Y]
 
 
 def chip_order(devices):

time: 69.9 us -> 69.5 us (level)
  waiting for transfers between devices: 21.9 us -> 20.1 us
  starting transfers between devices: 34.7 us -> 36.1 us
    ppermute x28, waiting for transfers between devices: 21.9 us -> 20.1 us  [swap(): return lax.ppermute(block, 'row', [(i, i ^ k) for i in range(devices)])]
    ppermute x28, starting transfers between devices: 34.7 us -> 36.1 us  [swap(): return lax.ppermute(block, 'row', [(i, i ^ k) for i in range(devices)])]
  transfers between devices with their start and end apart: 28 -> 28, of which waited for: 13 -> 12; matrix products, arithmetic and copies ran while one was open for 0% -> 0% of each run, Pallas kernels for 6% -> 6%
where the time goes in v22:
time: 69.5 us; the launch traced here: 69.4 us
  starting transfers between devices  36.1 us (52%)
  waiting for transfers between devices  20.1 us (29%)
  Pallas kernels  12.1 us (17%)
  local copies, waits for them, and re-layouts  0.72 us (1%)
    ppermute x28, starting transfers between devices, swap(): return lax.ppermute(block, 'row', [(i, i ^ k) for i in range(devices)])  36.1 us
    ppermute x28, waiting for transfers between devices, swap(): return lax.ppermute(block, 'row', [(i, i ^ k) for i in range(devices)])  20.1 us
    pallas_call x16, Pallas kernels, run(): pl.pallas_call(kernel, out_shape=out_shape, in_specs=smem + [in_vmem()] *...  12.1 us
  transfers between devices with their start and end apart: 28, of which 12 were waited for; matrix products, arithmetic and copies ran while one was open for 0% of the time, Pallas kernels for 6%

profile of v22, /device:TPU:0, one launch (start us, length us, event | category | flops | bytes accessed | tf_op | source)
XLA Modules:
  0.0 69.4 jit_solution(8183442432092346027)
XLA Ops:
  0.5 3.0 %collective-permute-start = (bf16[4,1536]{1,0:T(4,128)(2,1)}, bf16[4,1536]{1,0:T(4,128)(2,1)S(1)}, u32[]{:S(2)}, u32[]{:S(2)}) collective-permute-start(bf16[4,1536]{1,0:T(4,128)(2,1)} %refs_0_.1), channel_id=1, source_target_pairs={{0,2},{1,3},{2,0},{3,1},{4,6},{5,7},{6,4},{7,5},{8,10},{9,11},{10,... | collective-permute-start | bytes 36872 | tf_op jit(solution)/shard_map/ppermute | solution.py:414
  5.4 3.2 %collective-permute-start.3 = (bf16[8,1536]{1,0:T(8,128)(2,1)S(1)}, bf16[8,1536]{1,0:T(8,128)(2,1)S(1)}, u32[]{:S(2)}, u32[]{:S(2)}) collective-permute-start(bf16[8,1536]{1,0:T(8,128)(2,1)S(1)} %get-tuple-element.43.refs_0_), channel_id=1, source_target_pairs={{0,8},{1,9},{2,10},{3,11},{4,12},{5,13},{6,14},{7,15},{8,0},{9,1},... | collective-permute-start | bytes 73736 | tf_op jit(solution)/shard_map/ppermute | solution.py:414
  8.6 1.3 %collective-permute-start.2 = (bf16[8,1536]{1,0:T(8,128)(2,1)S(1)}, bf16[8,1536]{1,0:T(8,128)(2,1)S(1)}, u32[]{:S(2)}, u32[]{:S(2)}) collective-permute-start(bf16[8,1536]{1,0:T(8,128)(2,1)S(1)} %get-tuple-element.43.refs_0_), channel_id=1, source_target_pairs={{0,12},{1,13},{2,14},{3,15},{4,8},{5,9},{6,10},{7,11},{8,4},{9,5},... | collective-permute-start | bytes 73736 | tf_op jit(solution)/shard_map/ppermute | solution.py:414
  10.4 3.8 %collective-permute-done.2.refs_2_ = bf16[8,1536]{1,0:T(8,128)(2,1)S(1)} collective-permute-done((bf16[8,1536]{1,0:T(8,128)(2,1)S(1)}, bf16[8,1536]{1,0:T(8,128)(2,1)S(1)}, u32[]{:S(2)}, u32[]{:S(2)}) %collective-permute-start.2) | collective-permute-done | bytes 24608 | tf_op jit(solution)/shard_map/ppermute | solution.py:414
  14.2 2.3 %project.1 = (bf16[2,144,128]{2,1,0:T(8,128)(2,1)S(1)}, bf16[2,144,128]{2,1,0:T(8,128)(2,1)S(1)}, bf16[2,144,128]{2,1,0:T(8,128)(2,1)S(1)}, bf16[2,144,128]{2,1,...) custom-call(bf16[8,1536]{1,0:T(8,128)(2,1)S(1)} %get-tuple-element.4, ...), custom_call_target="tpu_custom_call" | custom-call | flops 23000000512 | tf_op jit(solution)/shard_map/project/pallas_call | solution.py:37
  16.5 1.6 %collective-permute-start.6 = (bf16[4,144,128]{2,1,0:T(8,128)(2,1)S(1)}, bf16[4,144,128]{2,1,0:T(8,128)(2,1)S(1)}, u32[]{:S(2)}, u32[]{:S(2)}) collective-permute-start(bf16[4,144,128]{2,1,0:T(8,128)(2,1)S(1)} %get-tuple-element.45), channel_id=1, source_target_pairs={{0,2},{1,3},{2,0},{3,1},{4,6},{5,7},{6,4},{7,5},{8,10},{9,11},{10,... | collective-permute-start | bytes 442376 | tf_op jit(solution)/shard_map/ppermute | solution.py:414
  18.1 1.2 %collective-permute-start.7 = (bf16[2,144,128]{2,1,0:T(8,128)(2,1)S(1)}, bf16[2,144,128]{2,1,0:T(8,128)(2,1)S(1)}, u32[]{:S(2)}, u32[]{:S(2)}) collective-permute-start(bf16[2,144,128]{2,1,0:T(8,128)(2,1)S(1)} %get-tuple-element.46), channel_id=1, source_target_pairs={{0,8},{1,9},{2,10},{3,11},{4,12},{5,13},{6,14},{7,15},{8,0},{9,1},... | collective-permute-start | bytes 221192 | tf_op jit(solution)/shard_map/ppermute | solution.py:414
  20.3 2.8 %collective-permute-start.9 = (bf16[2,144,128]{2,1,0:T(8,128)(2,1)S(1)}, bf16[2,144,128]{2,1,0:T(8,128)(2,1)S(1)}, u32[]{:S(2)}, u32[]{:S(2)}) collective-permute-start(bf16[2,144,128]{2,1,0:T(8,128)(2,1)S(1)} %get-tuple-element.48), channel_id=1, source_target_pairs={{0,14},{1,15},{2,12},{3,13},{4,10},{5,11},{6,8},{7,9},{8,6},{9,7},... | collective-permute-start | bytes 221192 | tf_op jit(solution)/shard_map/ppermute | solution.py:414
  24.0 1.7 %collective-permute-start.11 = (bf16[4,144,128]{2,1,0:T(8,128)(2,1)S(1)}, bf16[4,144,128]{2,1,0:T(8,128)(2,1)S(1)}, u32[]{:S(2)}, u32[]{:S(2)}) collective-permute-start(bf16[4,144,128]{2,1,0:T(8,128)(2,1)S(1)} %forward.2.after_ref), channel_id=1, source_target_pairs={{0,4},{1,5},{2,6},{3,7},{4,0},{5,1},{6,2},{7,3},{8,12},{9,13},{10,... | collective-permute-start | bytes 442376 | tf_op jit(solution)/shard_map/ppermute | solution.py:414
  25.7 1.7 %flip.1.flip_ref = bf16[4,1536,512]{2,1,0:T(8,128)(2,1)S(1)} custom-call(bf16[4,576,1536]{2,1,0:T(8,128)(2,1)S(1)} %bitcast.5, bf16[4,144,128]{2,1,0:T(8,128)(2,1)S(1)} %forward.2.after_ref), custom_call_target="tpu_custom_call" | custom-call | flops 4600000000 | tf_op jit(solution)/shard_map/flip/pallas_call | solution.py:37
  27.4 1.0 %collective-permute-done.7.refs_0_ = bf16[2,144,128]{2,1,0:T(8,128)(2,1)S(1)} collective-permute-done((bf16[2,144,128]{2,1,0:T(8,128)(2,1)S(1)}, bf16[2,144,128]{2,1,0:T(8,128)(2,1)S(1)}, u32[]{:S(2)}, u32[]{:S(2)}) %collective-permute-start.7) | collective-permute-done | bytes 73760 | tf_op jit(solution)/shard_map/ppermute | solution.py:414
  28.4 3.4 %collective-permute-done.10.refs_3_ = bf16[2,144,128]{2,1,0:T(8,128)(2,1)S(1)} collective-permute-done((bf16[2,144,128]{2,1,0:T(8,128)(2,1)S(1)}, bf16[2,144,128]{2,1,0:T(8,128)(2,1)S(1)}, u32[]{:S(2)}, u32[]{:S(2)}) %collective-permute-start.10) | collective-permute-done | bytes 73760 | tf_op jit(solution)/shard_map/ppermute | solution.py:414
  31.8 3.4 %attend.1 = (bf16[2,32,512]{2,1,0:T(8,128)(2,1)S(1)}, bf16[2,32,512]{2,1,0:T(8,128)(2,1)S(1)}, bf16[2,32,512]{2,1,0:T(8,128)(2,1)S(1)}, bf16[2,32,512]{2,1,0:T(8...) custom-call(s32[4]{0:T(128)S(1)} %copy-done.5, ...), custom_call_target="tpu_custom_call" | custom-call | flops 11500000256 | tf_op jit(solution)/shard_map/attend/pallas_call | solution.py:37
  35.2 1.6 %collective-permute-start.16 = (bf16[4,32,512]{2,1,0:T(8,128)(2,1)S(1)}, bf16[4,32,512]{2,1,0:T(8,128)(2,1)S(1)}, u32[]{:S(2)}, u32[]{:S(2)}) collective-permute-start(bf16[4,32,512]{2,1,0:T(8,128)(2,1)S(1)} %get-tuple-element.55), channel_id=1, source_target_pairs={{0,2},{1,3},{2,0},{3,1},{4,6},{5,7},{6,4},{7,5},{8,10},{9,11},{10,... | collective-permute-start | bytes 393224 | tf_op jit(solution)/shard_map/ppermute | solution.py:414
  36.8 1.0 %collective-permute-start.12 = (bf16[2,32,512]{2,1,0:T(8,128)(2,1)S(1)}, bf16[2,32,512]{2,1,0:T(8,128)(2,1)S(1)}, u32[]{:S(2)}, u32[]{:S(2)}) collective-permute-start(bf16[2,32,512]{2,1,0:T(8,128)(2,1)S(1)} %get-tuple-element.51), channel_id=1, source_target_pairs={{0,8},{1,9},{2,10},{3,11},{4,12},{5,13},{6,14},{7,15},{8,0},{9,1},... | collective-permute-start | bytes 196616 | tf_op jit(solution)/shard_map/ppermute | solution.py:414
  37.8 1.7 %collective-permute-start.13 = (bf16[2,32,512]{2,1,0:T(8,128)(2,1)S(1)}, bf16[2,32,512]{2,1,0:T(8,128)(2,1)S(1)}, u32[]{:S(2)}, u32[]{:S(2)}) collective-permute-start(bf16[2,32,512]{2,1,0:T(8,128)(2,1)S(1)} %get-tuple-element.52), channel_id=1, source_target_pairs={{0,12},{1,13},{2,14},{3,15},{4,8},{5,9},{6,10},{7,11},{8,4},{9,5},... | collective-permute-start | bytes 196616 | tf_op jit(solution)/shard_map/ppermute | solution.py:414
  39.4 2.1 %collective-permute-start.14 = (bf16[2,32,512]{2,1,0:T(8,128)(2,1)S(1)}, bf16[2,32,512]{2,1,0:T(8,128)(2,1)S(1)}, u32[]{:S(2)}, u32[]{:S(2)}) collective-permute-start(bf16[2,32,512]{2,1,0:T(8,128)(2,1)S(1)} %get-tuple-element.53), channel_id=1, source_target_pairs={{0,14},{1,15},{2,12},{3,13},{4,10},{5,11},{6,8},{7,9},{8,6},{9,7},... | collective-permute-start | bytes 196616 | tf_op jit(solution)/shard_map/ppermute | solution.py:414
  41.5 1.1 %collective-permute-start.15 = (bf16[2,32,512]{2,1,0:T(8,128)(2,1)S(1)}, bf16[2,32,512]{2,1,0:T(8,128)(2,1)S(1)}, u32[]{:S(2)}, u32[]{:S(2)}) collective-permute-start(bf16[2,32,512]{2,1,0:T(8,128)(2,1)S(1)} %get-tuple-element.54), channel_id=1, source_target_pairs={{0,10},{1,11},{2,8},{3,9},{4,14},{5,15},{6,12},{7,13},{8,2},{9,3},... | collective-permute-start | bytes 196616 | tf_op jit(solution)/shard_map/ppermute | solution.py:414
  42.7 2.2 %collective-permute-start.17 = (bf16[4,32,512]{2,1,0:T(8,128)(2,1)S(1)}, bf16[4,32,512]{2,1,0:T(8,128)(2,1)S(1)}, u32[]{:S(2)}, u32[]{:S(2)}) collective-permute-start(bf16[4,32,512]{2,1,0:T(8,128)(2,1)S(1)} %forward.3.after_ref), channel_id=1, source_target_pairs={{0,4},{1,5},{2,6},{3,7},{4,0},{5,1},{6,2},{7,3},{8,12},{9,13},{10,... | collective-permute-start | bytes 393224 | tf_op jit(solution)/shard_map/ppermute | solution.py:414
  44.8 1.1 %collective-permute-done.12.refs_0_ = bf16[2,32,512]{2,1,0:T(8,128)(2,1)S(1)} collective-permute-done((bf16[2,32,512]{2,1,0:T(8,128)(2,1)S(1)}, bf16[2,32,512]{2,1,0:T(8,128)(2,1)S(1)}, u32[]{:S(2)}, u32[]{:S(2)}) %collective-permute-start.12) | collective-permute-done | bytes 65568 | tf_op jit(solution)/shard_map/ppermute | solution.py:414
  46.0 1.1 %collective-permute-done.14.refs_2_ = bf16[2,32,512]{2,1,0:T(8,128)(2,1)S(1)} collective-permute-done((bf16[2,32,512]{2,1,0:T(8,128)(2,1)S(1)}, bf16[2,32,512]{2,1,0:T(8,128)(2,1)S(1)}, u32[]{:S(2)}, u32[]{:S(2)}) %collective-permute-start.14) | collective-permute-done | bytes 65568 | tf_op jit(solution)/shard_map/ppermute | solution.py:414
  47.1 2.3 %collective-permute-done.15.refs_3_ = bf16[2,32,512]{2,1,0:T(8,128)(2,1)S(1)} collective-permute-done((bf16[2,32,512]{2,1,0:T(8,128)(2,1)S(1)}, bf16[2,32,512]{2,1,0:T(8,128)(2,1)S(1)}, u32[]{:S(2)}, u32[]{:S(2)}) %collective-permute-start.15) | collective-permute-done | bytes 65568 | tf_op jit(solution)/shard_map/ppermute | solution.py:414
  49.5 1.5 %collective-permute-done.18.refs_7_ = bf16[8,32,512]{2,1,0:T(8,128)(2,1)S(1)} collective-permute-done((bf16[8,32,512]{2,1,0:T(8,128)(2,1)S(1)}, bf16[8,32,512]{2,1,0:T(8,128)(2,1)S(1)}, u32[]{:S(2)}, u32[]{:S(2)}) %collective-permute-start.18) | collective-permute-done | bytes 262176 | tf_op jit(solution)/shard_map/ppermute | solution.py:414
  51.5 1.4 %terms.3 = (f32[32,3584]{1,0:T(8,128)S(1)}, bf16[32,3584]{1,0:T(8,128)(2,1)S(1)}) custom-call(bf16[64,1024]{1,0:T(8,128)(2,1)S(1)} %values.1.val_ref, bf16[1024,7168]{1,0:T(8,128)(2,1)S(1)} %bitcast.2), custom_call_target="tpu_custom_call" | custom-call | flops 6899999744 | tf_op jit(solution)/shard_map/terms/pallas_call | solution.py:37
  53.1 1.4 %terms.2 = (f32[32,3584]{1,0:T(8,128)S(1)}, bf16[32,3584]{1,0:T(8,128)(2,1)S(1)}) custom-call(bf16[64,1024]{1,0:T(8,128)(2,1)S(1)} %values.1.val_ref, bf16[1024,7168]{1,0:T(8,128)(2,1)S(1)} %bitcast.2), custom_call_target="tpu_custom_call" | custom-call | flops 6899999744 | tf_op jit(solution)/shard_map/terms/pallas_call | solution.py:37
  55.0 1.5 %collective-permute-start.24 = (bf16[8,3584]{1,0:T(8,128)(2,1)S(1)}, bf16[8,3584]{1,0:T(8,128)(2,1)S(1)}, u32[]{:S(2)}, u32[]{:S(2)}) collective-permute-start(bf16[8,3584]{1,0:T(8,128)(2,1)S(1)} %get-tuple-element.69), channel_id=1, source_target_pairs={{0,2},{1,3},{2,0},{3,1},{4,6},{5,7},{6,4},{7,5},{8,10},{9,11},{10,... | collective-permute-start | bytes 172040 | tf_op jit(solution)/shard_map/ppermute | solution.py:414
  56.6 1.1 %collective-permute-start.25 = (bf16[8,3584]{1,0:T(8,128)(2,1)S(1)}, bf16[8,3584]{1,0:T(8,128)(2,1)S(1)}, u32[]{:S(2)}, u32[]{:S(2)}) collective-permute-start(bf16[8,3584]{1,0:T(8,128)(2,1)S(1)} %get-tuple-element.70), channel_id=1, source_target_pairs={{0,2},{1,3},{2,0},{3,1},{4,6},{5,7},{6,4},{7,5},{8,10},{9,11},{10,... | collective-permute-start | bytes 172040 | tf_op jit(solution)/shard_map/ppermute | solution.py:414
  57.6 2.5 %collective-permute-start.22 = (bf16[4,7168]{1,0:T(4,128)(2,1)S(1)}, bf16[4,7168]{1,0:T(4,128)(2,1)S(1)}, u32[]{:S(2)}, u32[]{:S(2)}) collective-permute-start(bf16[4,7168]{1,0:T(4,128)(2,1)S(1)} %get-tuple-element.65), channel_id=1, source_target_pairs={{0,6},{1,7},{2,4},{3,5},{4,2},{5,3},{6,0},{7,1},{8,14},{9,15},{10,... | collective-permute-start | bytes 172040 | tf_op jit(solution)/shard_map/ppermute | solution.py:414
  60.1 1.0 %collective-permute-start.23 = (bf16[4,7168]{1,0:T(4,128)(2,1)S(1)}, bf16[4,7168]{1,0:T(4,128)(2,1)S(1)}, u32[]{:S(2)}, u32[]{:S(2)}) collective-permute-start(bf16[4,7168]{1,0:T(4,128)(2,1)S(1)} %get-tuple-element.66), channel_id=1, source_target_pairs={{0,2},{1,3},{2,0},{3,1},{4,6},{5,7},{6,4},{7,5},{8,10},{9,11},{10,... | collective-permute-start | bytes 172040 | tf_op jit(solution)/shard_map/ppermute | solution.py:414
  61.1 2.5 %collective-permute-start.26 = (bf16[4,7168]{1,0:T(4,128)(2,1)S(1)}, bf16[4,7168]{1,0:T(4,128)(2,1)S(1)}, u32[]{:S(2)}, u32[]{:S(2)}) collective-permute-start(bf16[4,7168]{1,0:T(4,128)(2,1)S(1)} %get-tuple-element.71), channel_id=1, source_target_pairs={{0,12},{1,13},{2,14},{3,15},{4,8},{5,9},{6,10},{7,11},{8,4},{9,5},... | collective-permute-start | bytes 172040 | tf_op jit(solution)/shard_map/ppermute | solution.py:414
  64.3 3.0 %collective-permute-done.26.refs_4_ = bf16[4,7168]{1,0:T(4,128)(2,1)S(1)} collective-permute-done((bf16[4,7168]{1,0:T(4,128)(2,1)S(1)}, bf16[4,7168]{1,0:T(4,128)(2,1)S(1)}, u32[]{:S(2)}, u32[]{:S(2)}) %collective-permute-start.26) | collective-permute-done | bytes 57376 | tf_op jit(solution)/shard_map/ppermute | solution.py:414
  67.3 1.4 %collective-permute-done.27.refs_5_ = bf16[4,7168]{1,0:T(4,128)(2,1)S(1)} collective-permute-done((bf16[4,7168]{1,0:T(4,128)(2,1)S(1)}, bf16[4,7168]{1,0:T(4,128)(2,1)S(1)}, u32[]{:S(2)}, u32[]{:S(2)}) %collective-permute-start.27) | collective-permute-done | bytes 57376 | tf_op jit(solution)/shard_map/ppermute | solution.py:414
  (71 shorter events, 7.5 us)
Async XLA Ops:
  0.0 14.2 %collective-permute-start.4 = (bf16[1536,1536]{1,0:T(8,128)(2,1)}, bf16[1536,1536]{1,0:T(8,128)(2,1)S(1)}, u32[]{:S(2)}, u32[]{:S(2)}) collective-permute-start(bf16[1536,1536]{1,0:T(8,128)(2,1)} %refs_4_.1), channel_id=1, source_target_pairs={{0,1},{1,0},{2,3},{3,2},{4,5},{5,4},{6,7},{7,6},{8,9},{9,8},{10,11... | collective-permute-start | bytes 14155784 | tf_op jit(solution)/shard_map/ppermute | solution.py:414
  0.5 13.7 %collective-permute-start.5 = (bf16[8,128,512]{2,1,0:T(8,128)(2,1)}, bf16[8,128,512]{2,1,0:T(8,128)(2,1)S(1)}, u32[]{:S(2)}, u32[]{:S(2)}) collective-permute-start(bf16[8,128,512]{2,1,0:T(8,128)(2,1)} %refs_5_.1), channel_id=1, source_target_pairs={{0,1},{1,0},{2,3},{3,2},{4,5},{5,4},{6,7},{7,6},{8,9},{9,8},{10,11... | collective-permute-start | bytes 3145736 | tf_op jit(solution)/shard_map/ppermute | solution.py:414
  0.5 4.8 %collective-permute-start = (bf16[4,1536]{1,0:T(4,128)(2,1)}, bf16[4,1536]{1,0:T(4,128)(2,1)S(1)}, u32[]{:S(2)}, u32[]{:S(2)}) collective-permute-start(bf16[4,1536]{1,0:T(4,128)(2,1)} %refs_0_.1), channel_id=1, source_target_pairs={{0,2},{1,3},{2,0},{3,1},{4,6},{5,7},{6,4},{7,5},{8,10},{9,11},{10,... | collective-permute-start | bytes 36872 | tf_op jit(solution)/shard_map/ppermute | solution.py:414
  4.1 10.1 %slice-start.6 = ((s8[4718592]{0:T(1024)(128)(4,1)}), s8[4194304]{0:T(1024)(128)(4,1)S(1)}, s32[]{:S(2)}) async-start(s8[4718592]{0:T(1024)(128)(4,1)} %bitcast.7), calls=%async_computation.6 | async-start | bytes 8388608
  5.4 8.9 %copy-start = (bf16[8,128,512]{2,1,0:T(8,128)(2,1)S(1)}, bf16[8,128,512]{2,1,0:T(8,128)(2,1)}, u32[]{:S(2)}) copy-start(bf16[8,128,512]{2,1,0:T(8,128)(2,1)} %refs_5_.1) | copy-start | bytes 3145732
  5.4 20.3 %slice-start.4 = ((s8[7077888]{0:T(1024)(128)(4,1)}), s8[4194304]{0:T(1024)(128)(4,1)S(1)}, s32[]{:S(2)}) async-start(s8[7077888]{0:T(1024)(128)(4,1)} %bitcast.3), calls=%async_computation.4 | async-start | bytes 8388608
  5.4 20.3 %slice-start.5 = ((s8[7077888]{0:T(1024)(128)(4,1)}), s8[2883584]{0:T(1024)(128)(4,1)S(1)}, s32[]{:S(2)}) async-start(s8[7077888]{0:T(1024)(128)(4,1)} %bitcast.3), calls=%async_computation.5 | async-start | bytes 5767168
  5.4 5.0 %collective-permute-start.3 = (bf16[8,1536]{1,0:T(8,128)(2,1)S(1)}, bf16[8,1536]{1,0:T(8,128)(2,1)S(1)}, u32[]{:S(2)}, u32[]{:S(2)}) collective-permute-start(bf16[8,1536]{1,0:T(8,128)(2,1)S(1)} %get-tuple-element.43.refs_0_), channel_id=1, source_target_pairs={{0,8},{1,9},{2,10},{3,11},{4,12},{5,13},{6,14},{7,15},{8,0},{9,1},... | collective-permute-start | bytes 73736 | tf_op jit(solution)/shard_map/ppermute | solution.py:414
  8.6 5.6 %collective-permute-start.2 = (bf16[8,1536]{1,0:T(8,128)(2,1)S(1)}, bf16[8,1536]{1,0:T(8,128)(2,1)S(1)}, u32[]{:S(2)}, u32[]{:S(2)}) collective-permute-start(bf16[8,1536]{1,0:T(8,128)(2,1)S(1)} %get-tuple-element.43.refs_0_), channel_id=1, source_target_pairs={{0,12},{1,13},{2,14},{3,15},{4,8},{5,9},{6,10},{7,11},{8,4},{9,5},... | collective-permute-start | bytes 73736 | tf_op jit(solution)/shard_map/ppermute | solution.py:414
  9.9 4.3 %collective-permute-start.1 = (bf16[8,1536]{1,0:T(8,128)(2,1)S(1)}, bf16[8,1536]{1,0:T(8,128)(2,1)S(1)}, u32[]{:S(2)}, u32[]{:S(2)}) collective-permute-start(bf16[8,1536]{1,0:T(8,128)(2,1)S(1)} %get-tuple-element.43.refs_0_), channel_id=1, source_target_pairs={{0,4},{1,5},{2,6},{3,7},{4,0},{5,1},{6,2},{7,3},{8,12},{9,13},{10,... | collective-permute-start | bytes 73736 | tf_op jit(solution)/shard_map/ppermute | solution.py:414
  16.5 7.4 %collective-permute-start.6 = (bf16[4,144,128]{2,1,0:T(8,128)(2,1)S(1)}, bf16[4,144,128]{2,1,0:T(8,128)(2,1)S(1)}, u32[]{:S(2)}, u32[]{:S(2)}) collective-permute-start(bf16[4,144,128]{2,1,0:T(8,128)(2,1)S(1)} %get-tuple-element.45), channel_id=1, source_target_pairs={{0,2},{1,3},{2,0},{3,1},{4,6},{5,7},{6,4},{7,5},{8,10},{9,11},{10,... | collective-permute-start | bytes 442376 | tf_op jit(solution)/shard_map/ppermute | solution.py:414
  18.1 10.3 %collective-permute-start.7 = (bf16[2,144,128]{2,1,0:T(8,128)(2,1)S(1)}, bf16[2,144,128]{2,1,0:T(8,128)(2,1)S(1)}, u32[]{:S(2)}, u32[]{:S(2)}) collective-permute-start(bf16[2,144,128]{2,1,0:T(8,128)(2,1)S(1)} %get-tuple-element.46), channel_id=1, source_target_pairs={{0,8},{1,9},{2,10},{3,11},{4,12},{5,13},{6,14},{7,15},{8,0},{9,1},... | collective-permute-start | bytes 221192 | tf_op jit(solution)/shard_map/ppermute | solution.py:414
  19.4 9.0 %collective-permute-start.8 = (bf16[2,144,128]{2,1,0:T(8,128)(2,1)S(1)}, bf16[2,144,128]{2,1,0:T(8,128)(2,1)S(1)}, u32[]{:S(2)}, u32[]{:S(2)}) collective-permute-start(bf16[2,144,128]{2,1,0:T(8,128)(2,1)S(1)} %get-tuple-element.47), channel_id=1, source_target_pairs={{0,12},{1,13},{2,14},{3,15},{4,8},{5,9},{6,10},{7,11},{8,4},{9,5},... | collective-permute-start | bytes 221192 | tf_op jit(solution)/shard_map/ppermute | solution.py:414
  20.3 8.1 %collective-permute-start.9 = (bf16[2,144,128]{2,1,0:T(8,128)(2,1)S(1)}, bf16[2,144,128]{2,1,0:T(8,128)(2,1)S(1)}, u32[]{:S(2)}, u32[]{:S(2)}) collective-permute-start(bf16[2,144,128]{2,1,0:T(8,128)(2,1)S(1)} %get-tuple-element.48), channel_id=1, source_target_pairs={{0,14},{1,15},{2,12},{3,13},{4,10},{5,11},{6,8},{7,9},{8,6},{9,7},... | collective-permute-start | bytes 221192 | tf_op jit(solution)/shard_map/ppermute | solution.py:414
  23.1 8.6 %collective-permute-start.10 = (bf16[2,144,128]{2,1,0:T(8,128)(2,1)S(1)}, bf16[2,144,128]{2,1,0:T(8,128)(2,1)S(1)}, u32[]{:S(2)}, u32[]{:S(2)}) collective-permute-start(bf16[2,144,128]{2,1,0:T(8,128)(2,1)S(1)} %get-tuple-element.49), channel_id=1, source_target_pairs={{0,10},{1,11},{2,8},{3,9},{4,14},{5,15},{6,12},{7,13},{8,2},{9,3},... | collective-permute-start | bytes 221192 | tf_op jit(solution)/shard_map/ppermute | solution.py:414
  24.0 7.8 %collective-permute-start.11 = (bf16[4,144,128]{2,1,0:T(8,128)(2,1)S(1)}, bf16[4,144,128]{2,1,0:T(8,128)(2,1)S(1)}, u32[]{:S(2)}, u32[]{:S(2)}) collective-permute-start(bf16[4,144,128]{2,1,0:T(8,128)(2,1)S(1)} %forward.2.after_ref), channel_id=1, source_target_pairs={{0,4},{1,5},{2,6},{3,7},{4,0},{5,1},{6,2},{7,3},{8,12},{9,13},{10,... | collective-permute-start | bytes 442376 | tf_op jit(solution)/shard_map/ppermute | solution.py:414
  35.2 7.4 %collective-permute-start.16 = (bf16[4,32,512]{2,1,0:T(8,128)(2,1)S(1)}, bf16[4,32,512]{2,1,0:T(8,128)(2,1)S(1)}, u32[]{:S(2)}, u32[]{:S(2)}) collective-permute-start(bf16[4,32,512]{2,1,0:T(8,128)(2,1)S(1)} %get-tuple-element.55), channel_id=1, source_target_pairs={{0,2},{1,3},{2,0},{3,1},{4,6},{5,7},{6,4},{7,5},{8,10},{9,11},{10,... | collective-permute-start | bytes 393224 | tf_op jit(solution)/shard_map/ppermute | solution.py:414
  36.8 9.2 %collective-permute-start.12 = (bf16[2,32,512]{2,1,0:T(8,128)(2,1)S(1)}, bf16[2,32,512]{2,1,0:T(8,128)(2,1)S(1)}, u32[]{:S(2)}, u32[]{:S(2)}) collective-permute-start(bf16[2,32,512]{2,1,0:T(8,128)(2,1)S(1)} %get-tuple-element.51), channel_id=1, source_target_pairs={{0,8},{1,9},{2,10},{3,11},{4,12},{5,13},{6,14},{7,15},{8,0},{9,1},... | collective-permute-start | bytes 196616 | tf_op jit(solution)/shard_map/ppermute | solution.py:414
  37.8 8.2 %collective-permute-start.13 = (bf16[2,32,512]{2,1,0:T(8,128)(2,1)S(1)}, bf16[2,32,512]{2,1,0:T(8,128)(2,1)S(1)}, u32[]{:S(2)}, u32[]{:S(2)}) collective-permute-start(bf16[2,32,512]{2,1,0:T(8,128)(2,1)S(1)} %get-tuple-element.52), channel_id=1, source_target_pairs={{0,12},{1,13},{2,14},{3,15},{4,8},{5,9},{6,10},{7,11},{8,4},{9,5},... | collective-permute-start | bytes 196616 | tf_op jit(solution)/shard_map/ppermute | solution.py:414
  39.4 7.6 %collective-permute-start.14 = (bf16[2,32,512]{2,1,0:T(8,128)(2,1)S(1)}, bf16[2,32,512]{2,1,0:T(8,128)(2,1)S(1)}, u32[]{:S(2)}, u32[]{:S(2)}) collective-permute-start(bf16[2,32,512]{2,1,0:T(8,128)(2,1)S(1)} %get-tuple-element.53), channel_id=1, source_target_pairs={{0,14},{1,15},{2,12},{3,13},{4,10},{5,11},{6,8},{7,9},{8,6},{9,7},... | collective-permute-start | bytes 196616 | tf_op jit(solution)/shard_map/ppermute | solution.py:414
  41.5 7.8 %collective-permute-start.15 = (bf16[2,32,512]{2,1,0:T(8,128)(2,1)S(1)}, bf16[2,32,512]{2,1,0:T(8,128)(2,1)S(1)}, u32[]{:S(2)}, u32[]{:S(2)}) collective-permute-start(bf16[2,32,512]{2,1,0:T(8,128)(2,1)S(1)} %get-tuple-element.54), channel_id=1, source_target_pairs={{0,10},{1,11},{2,8},{3,9},{4,14},{5,15},{6,12},{7,13},{8,2},{9,3},... | collective-permute-start | bytes 196616 | tf_op jit(solution)/shard_map/ppermute | solution.py:414
  42.7 6.7 %collective-permute-start.17 = (bf16[4,32,512]{2,1,0:T(8,128)(2,1)S(1)}, bf16[4,32,512]{2,1,0:T(8,128)(2,1)S(1)}, u32[]{:S(2)}, u32[]{:S(2)}) collective-permute-start(bf16[4,32,512]{2,1,0:T(8,128)(2,1)S(1)} %forward.3.after_ref), channel_id=1, source_target_pairs={{0,4},{1,5},{2,6},{3,7},{4,0},{5,1},{6,2},{7,3},{8,12},{9,13},{10,... | collective-permute-start | bytes 393224 | tf_op jit(solution)/shard_map/ppermute | solution.py:414
  49.4 1.6 %collective-permute-start.18 = (bf16[8,32,512]{2,1,0:T(8,128)(2,1)S(1)}, bf16[8,32,512]{2,1,0:T(8,128)(2,1)S(1)}, u32[]{:S(2)}, u32[]{:S(2)}) collective-permute-start(bf16[8,32,512]{2,1,0:T(8,128)(2,1)S(1)} %regroup.1), channel_id=1, source_target_pairs={{0,1},{1,0},{2,3},{3,2},{4,5},{5,4},{6,7},{7,6},{8,9},{9,8},{10,11... | collective-permute-start | bytes 786440 | tf_op jit(solution)/shard_map/ppermute | solution.py:414
  52.9 2.0 %collective-permute-start.20 = (bf16[32,3584]{1,0:T(8,128)(2,1)S(1)}, bf16[32,3584]{1,0:T(8,128)(2,1)S(1)}, u32[]{:S(2)}, u32[]{:S(2)}) collective-permute-start(bf16[32,3584]{1,0:T(8,128)(2,1)S(1)} %get-tuple-element.61), channel_id=1, source_target_pairs={{0,1},{1,0},{2,3},{3,2},{4,5},{5,4},{6,7},{7,6},{8,9},{9,8},{10,11... | collective-permute-start | bytes 688136 | tf_op jit(solution)/shard_map/ppermute | solution.py:414
  54.5 2.0 %collective-permute-start.19 = (bf16[32,3584]{1,0:T(8,128)(2,1)S(1)}, bf16[32,3584]{1,0:T(8,128)(2,1)S(1)}, u32[]{:S(2)}, u32[]{:S(2)}) collective-permute-start(bf16[32,3584]{1,0:T(8,128)(2,1)S(1)} %get-tuple-element.59), channel_id=1, source_target_pairs={{0,1},{1,0},{2,3},{3,2},{4,5},{5,4},{6,7},{7,6},{8,9},{9,8},{10,11... | collective-permute-start | bytes 688136 | tf_op jit(solution)/shard_map/ppermute | solution.py:414
  55.0 6.1 %collective-permute-start.24 = (bf16[8,3584]{1,0:T(8,128)(2,1)S(1)}, bf16[8,3584]{1,0:T(8,128)(2,1)S(1)}, u32[]{:S(2)}, u32[]{:S(2)}) collective-permute-start(bf16[8,3584]{1,0:T(8,128)(2,1)S(1)} %get-tuple-element.69), channel_id=1, source_target_pairs={{0,2},{1,3},{2,0},{3,1},{4,6},{5,7},{6,4},{7,5},{8,10},{9,11},{10,... | collective-permute-start | bytes 172040 | tf_op jit(solution)/shard_map/ppermute | solution.py:414
  56.6 4.6 %collective-permute-start.25 = (bf16[8,3584]{1,0:T(8,128)(2,1)S(1)}, bf16[8,3584]{1,0:T(8,128)(2,1)S(1)}, u32[]{:S(2)}, u32[]{:S(2)}) collective-permute-start(bf16[8,3584]{1,0:T(8,128)(2,1)S(1)} %get-tuple-element.70), channel_id=1, source_target_pairs={{0,2},{1,3},{2,0},{3,1},{4,6},{5,7},{6,4},{7,5},{8,10},{9,11},{10,... | collective-permute-start | bytes 172040 | tf_op jit(solution)/shard_map/ppermute | solution.py:414
  57.6 6.0 %collective-permute-start.21 = (bf16[4,7168]{1,0:T(4,128)(2,1)S(1)}, bf16[4,7168]{1,0:T(4,128)(2,1)S(1)}, u32[]{:S(2)}, u32[]{:S(2)}) collective-permute-start(bf16[4,7168]{1,0:T(4,128)(2,1)S(1)} %get-tuple-element.64), channel_id=1, source_target_pairs={{0,4},{1,5},{2,6},{3,7},{4,0},{5,1},{6,2},{7,3},{8,12},{9,13},{10,... | collective-permute-start | bytes 172040 | tf_op jit(solution)/shard_map/ppermute | solution.py:414
  57.6 6.0 %collective-permute-start.22 = (bf16[4,7168]{1,0:T(4,128)(2,1)S(1)}, bf16[4,7168]{1,0:T(4,128)(2,1)S(1)}, u32[]{:S(2)}, u32[]{:S(2)}) collective-permute-start(bf16[4,7168]{1,0:T(4,128)(2,1)S(1)} %get-tuple-element.65), channel_id=1, source_target_pairs={{0,6},{1,7},{2,4},{3,5},{4,2},{5,3},{6,0},{7,1},{8,14},{9,15},{10,... | collective-permute-start | bytes 172040 | tf_op jit(solution)/shard_map/ppermute | solution.py:414
  60.1 4.2 %collective-permute-start.23 = (bf16[4,7168]{1,0:T(4,128)(2,1)S(1)}, bf16[4,7168]{1,0:T(4,128)(2,1)S(1)}, u32[]{:S(2)}, u32[]{:S(2)}) collective-permute-start(bf16[4,7168]{1,0:T(4,128)(2,1)S(1)} %get-tuple-element.66), channel_id=1, source_target_pairs={{0,2},{1,3},{2,0},{3,1},{4,6},{5,7},{6,4},{7,5},{8,10},{9,11},{10,... | collective-permute-start | bytes 172040 | tf_op jit(solution)/shard_map/ppermute | solution.py:414
  61.1 6.1 %collective-permute-start.26 = (bf16[4,7168]{1,0:T(4,128)(2,1)S(1)}, bf16[4,7168]{1,0:T(4,128)(2,1)S(1)}, u32[]{:S(2)}, u32[]{:S(2)}) collective-permute-start(bf16[4,7168]{1,0:T(4,128)(2,1)S(1)} %get-tuple-element.71), channel_id=1, source_target_pairs={{0,12},{1,13},{2,14},{3,15},{4,8},{5,9},{6,10},{7,11},{8,4},{9,5},... | collective-permute-start | bytes 172040 | tf_op jit(solution)/shard_map/ppermute | solution.py:414
  63.6 5.1 %collective-permute-start.27 = (bf16[4,7168]{1,0:T(4,128)(2,1)S(1)}, bf16[4,7168]{1,0:T(4,128)(2,1)S(1)}, u32[]{:S(2)}, u32[]{:S(2)}) collective-permute-start(bf16[4,7168]{1,0:T(4,128)(2,1)S(1)} %get-tuple-element.72), channel_id=1, source_target_pairs={{0,8},{1,9},{2,10},{3,11},{4,12},{5,13},{6,14},{7,15},{8,0},{9,1},... | collective-permute-start | bytes 172040 | tf_op jit(solution)/shard_map/ppermute | solution.py:414
  (10 other events, 55.3 us)

commit v23 on v22

--- a/solution.py
+++ b/solution.py
@@ -60,7 +60,7 @@
 
 def far_chips(devices):
     chips = [k for k in far_first(devices, 2) if k > Y + Z1]
-    return [k for k in chips if not k & Y] + [k for k in chips[::-1] if k & Y]
+    return [k for k in chips[::-1] if not k & Y] + [k for k in chips if k & Y]
 
 
 def chip_order(devices):

time: 69.5 us -> 69.8 us (level)
  waiting for transfers between devices: 20.1 us -> 22 us
  starting transfers between devices: 36.1 us -> 34.4 us
    ppermute x28, waiting for transfers between devices: 20.1 us -> 22 us  [swap(): return lax.ppermute(block, 'row', [(i, i ^ k) for i in range(devices)])]
    ppermute x28, starting transfers between devices: 36.1 us -> 34.4 us  [swap(): return lax.ppermute(block, 'row', [(i, i ^ k) for i in range(devices)])]
  transfers between devices with their start and end apart: 28 -> 28, of which waited for: 12 -> 15; matrix products, arithmetic and copies ran while one was open for 0% -> 0% of each run, Pallas kernels for 6% -> 6%
where the time goes in v23:
time: 69.8 us; the launch traced here: 69.7 us
  starting transfers between devices  34.4 us (49%)
  waiting for transfers between devices  22 us (32%)
  Pallas kernels  12.2 us (17%)
  local copies, waits for them, and re-layouts  0.73 us (1%)
    ppermute x28, starting transfers between devices, swap(): return lax.ppermute(block, 'row', [(i, i ^ k) for i in range(devices)])  34.4 us
    ppermute x28, waiting for transfers between devices, swap(): return lax.ppermute(block, 'row', [(i, i ^ k) for i in range(devices)])  22 us
    pallas_call x16, Pallas kernels, run(): pl.pallas_call(kernel, out_shape=out_shape, in_specs=smem + [in_vmem()] *...  12.2 us
  transfers between devices with their start and end apart: 28, of which 15 were waited for; matrix products, arithmetic and copies ran while one was open for 0% of the time, Pallas kernels for 6%

profile of v23, /device:TPU:0, one launch (start us, length us, event | category | flops | bytes accessed | tf_op | source)
XLA Modules:
  0.0 69.7 jit_solution(10700625326738883870)
XLA Ops:
  0.5 3.0 %collective-permute-start = (bf16[4,1536]{1,0:T(4,128)(2,1)}, bf16[4,1536]{1,0:T(4,128)(2,1)S(1)}, u32[]{:S(2)}, u32[]{:S(2)}) collective-permute-start(bf16[4,1536]{1,0:T(4,128)(2,1)} %refs_0_.1), channel_id=1, source_target_pairs={{0,2},{1,3},{2,0},{3,1},{4,6},{5,7},{6,4},{7,5},{8,10},{9,11},{10,... | collective-permute-start | bytes 36872 | tf_op jit(solution)/shard_map/ppermute | solution.py:414
  5.4 3.2 %collective-permute-start.3 = (bf16[8,1536]{1,0:T(8,128)(2,1)S(1)}, bf16[8,1536]{1,0:T(8,128)(2,1)S(1)}, u32[]{:S(2)}, u32[]{:S(2)}) collective-permute-start(bf16[8,1536]{1,0:T(8,128)(2,1)S(1)} %get-tuple-element.43.refs_0_), channel_id=1, source_target_pairs={{0,8},{1,9},{2,10},{3,11},{4,12},{5,13},{6,14},{7,15},{8,0},{9,1},... | collective-permute-start | bytes 73736 | tf_op jit(solution)/shard_map/ppermute | solution.py:414
  8.6 1.3 %collective-permute-start.2 = (bf16[8,1536]{1,0:T(8,128)(2,1)S(1)}, bf16[8,1536]{1,0:T(8,128)(2,1)S(1)}, u32[]{:S(2)}, u32[]{:S(2)}) collective-permute-start(bf16[8,1536]{1,0:T(8,128)(2,1)S(1)} %get-tuple-element.43.refs_0_), channel_id=1, source_target_pairs={{0,12},{1,13},{2,14},{3,15},{4,8},{5,9},{6,10},{7,11},{8,4},{9,5},... | collective-permute-start | bytes 73736 | tf_op jit(solution)/shard_map/ppermute | solution.py:414
  10.4 3.8 %collective-permute-done.2.refs_2_ = bf16[8,1536]{1,0:T(8,128)(2,1)S(1)} collective-permute-done((bf16[8,1536]{1,0:T(8,128)(2,1)S(1)}, bf16[8,1536]{1,0:T(8,128)(2,1)S(1)}, u32[]{:S(2)}, u32[]{:S(2)}) %collective-permute-start.2) | collective-permute-done | bytes 24608 | tf_op jit(solution)/shard_map/ppermute | solution.py:414
  14.2 2.3 %project.1 = (bf16[2,144,128]{2,1,0:T(8,128)(2,1)S(1)}, bf16[2,144,128]{2,1,0:T(8,128)(2,1)S(1)}, bf16[2,144,128]{2,1,0:T(8,128)(2,1)S(1)}, bf16[2,144,128]{2,1,...) custom-call(bf16[8,1536]{1,0:T(8,128)(2,1)S(1)} %get-tuple-element.4, ...), custom_call_target="tpu_custom_call" | custom-call | flops 23000000512 | tf_op jit(solution)/shard_map/project/pallas_call | solution.py:37
  16.5 1.6 %collective-permute-start.6 = (bf16[4,144,128]{2,1,0:T(8,128)(2,1)S(1)}, bf16[4,144,128]{2,1,0:T(8,128)(2,1)S(1)}, u32[]{:S(2)}, u32[]{:S(2)}) collective-permute-start(bf16[4,144,128]{2,1,0:T(8,128)(2,1)S(1)} %get-tuple-element.45), channel_id=1, source_target_pairs={{0,2},{1,3},{2,0},{3,1},{4,6},{5,7},{6,4},{7,5},{8,10},{9,11},{10,... | collective-permute-start | bytes 442376 | tf_op jit(solution)/shard_map/ppermute | solution.py:414
  18.1 2.0 %collective-permute-start.7 = (bf16[2,144,128]{2,1,0:T(8,128)(2,1)S(1)}, bf16[2,144,128]{2,1,0:T(8,128)(2,1)S(1)}, u32[]{:S(2)}, u32[]{:S(2)}) collective-permute-start(bf16[2,144,128]{2,1,0:T(8,128)(2,1)S(1)} %get-tuple-element.46), channel_id=1, source_target_pairs={{0,12},{1,13},{2,14},{3,15},{4,8},{5,9},{6,10},{7,11},{8,4},{9,5},... | collective-permute-start | bytes 221192 | tf_op jit(solution)/shard_map/ppermute | solution.py:414
  20.1 2.9 %collective-permute-start.9 = (bf16[2,144,128]{2,1,0:T(8,128)(2,1)S(1)}, bf16[2,144,128]{2,1,0:T(8,128)(2,1)S(1)}, u32[]{:S(2)}, u32[]{:S(2)}) collective-permute-start(bf16[2,144,128]{2,1,0:T(8,128)(2,1)S(1)} %get-tuple-element.48), channel_id=1, source_target_pairs={{0,10},{1,11},{2,8},{3,9},{4,14},{5,15},{6,12},{7,13},{8,2},{9,3},... | collective-permute-start | bytes 221192 | tf_op jit(solution)/shard_map/ppermute | solution.py:414
  23.0 2.8 %collective-permute-start.10 = (bf16[2,144,128]{2,1,0:T(8,128)(2,1)S(1)}, bf16[2,144,128]{2,1,0:T(8,128)(2,1)S(1)}, u32[]{:S(2)}, u32[]{:S(2)}) collective-permute-start(bf16[2,144,128]{2,1,0:T(8,128)(2,1)S(1)} %get-tuple-element.49), channel_id=1, source_target_pairs={{0,14},{1,15},{2,12},{3,13},{4,10},{5,11},{6,8},{7,9},{8,6},{9,7},... | collective-permute-start | bytes 221192 | tf_op jit(solution)/shard_map/ppermute | solution.py:414
  25.9 1.7 %flip.1.flip_ref = bf16[4,1536,512]{2,1,0:T(8,128)(2,1)S(1)} custom-call(bf16[4,576,1536]{2,1,0:T(8,128)(2,1)S(1)} %bitcast.5, bf16[4,144,128]{2,1,0:T(8,128)(2,1)S(1)} %forward.2.after_ref), custom_call_target="tpu_custom_call" | custom-call | flops 4600000000 | tf_op jit(solution)/shard_map/flip/pallas_call | solution.py:37
  27.6 0.8 %collective-permute-done.8.refs_1_ = bf16[2,144,128]{2,1,0:T(8,128)(2,1)S(1)} collective-permute-done((bf16[2,144,128]{2,1,0:T(8,128)(2,1)S(1)}, bf16[2,144,128]{2,1,0:T(8,128)(2,1)S(1)}, u32[]{:S(2)}, u32[]{:S(2)}) %collective-permute-start.8) | collective-permute-done | bytes 73760 | tf_op jit(solution)/shard_map/ppermute | solution.py:414
  28.4 2.5 %collective-permute-done.9.refs_2_ = bf16[2,144,128]{2,1,0:T(8,128)(2,1)S(1)} collective-permute-done((bf16[2,144,128]{2,1,0:T(8,128)(2,1)S(1)}, bf16[2,144,128]{2,1,0:T(8,128)(2,1)S(1)}, u32[]{:S(2)}, u32[]{:S(2)}) %collective-permute-start.9) | collective-permute-done | bytes 73760 | tf_op jit(solution)/shard_map/ppermute | solution.py:414
  30.9 1.1 %collective-permute-done.11.refs_5_ = bf16[4,144,128]{2,1,0:T(8,128)(2,1)S(1)} collective-permute-done((bf16[4,144,128]{2,1,0:T(8,128)(2,1)S(1)}, bf16[4,144,128]{2,1,0:T(8,128)(2,1)S(1)}, u32[]{:S(2)}, u32[]{:S(2)}) %collective-permute-start.11) | collective-permute-done | bytes 147488 | tf_op jit(solution)/shard_map/ppermute | solution.py:414
  32.0 3.4 %attend.1 = (bf16[2,32,512]{2,1,0:T(8,128)(2,1)S(1)}, bf16[2,32,512]{2,1,0:T(8,128)(2,1)S(1)}, bf16[2,32,512]{2,1,0:T(8,128)(2,1)S(1)}, bf16[2,32,512]{2,1,0:T(8...) custom-call(s32[4]{0:T(128)S(1)} %copy-done.5, ...), custom_call_target="tpu_custom_call" | custom-call | flops 11500000256 | tf_op jit(solution)/shard_map/attend/pallas_call | solution.py:37
  35.5 0.8 %collective-permute-start.16 = (bf16[4,32,512]{2,1,0:T(8,128)(2,1)S(1)}, bf16[4,32,512]{2,1,0:T(8,128)(2,1)S(1)}, u32[]{:S(2)}, u32[]{:S(2)}) collective-permute-start(bf16[4,32,512]{2,1,0:T(8,128)(2,1)S(1)} %get-tuple-element.55), channel_id=1, source_target_pairs={{0,2},{1,3},{2,0},{3,1},{4,6},{5,7},{6,4},{7,5},{8,10},{9,11},{10,... | collective-permute-start | bytes 393224 | tf_op jit(solution)/shard_map/ppermute | solution.py:414
  36.3 2.3 %collective-permute-start.12 = (bf16[2,32,512]{2,1,0:T(8,128)(2,1)S(1)}, bf16[2,32,512]{2,1,0:T(8,128)(2,1)S(1)}, u32[]{:S(2)}, u32[]{:S(2)}) collective-permute-start(bf16[2,32,512]{2,1,0:T(8,128)(2,1)S(1)} %get-tuple-element.51), channel_id=1, source_target_pairs={{0,12},{1,13},{2,14},{3,15},{4,8},{5,9},{6,10},{7,11},{8,4},{9,5},... | collective-permute-start | bytes 196616 | tf_op jit(solution)/shard_map/ppermute | solution.py:414
  38.8 3.8 %collective-permute-start.14 = (bf16[2,32,512]{2,1,0:T(8,128)(2,1)S(1)}, bf16[2,32,512]{2,1,0:T(8,128)(2,1)S(1)}, u32[]{:S(2)}, u32[]{:S(2)}) collective-permute-start(bf16[2,32,512]{2,1,0:T(8,128)(2,1)S(1)} %get-tuple-element.53), channel_id=1, source_target_pairs={{0,10},{1,11},{2,8},{3,9},{4,14},{5,15},{6,12},{7,13},{8,2},{9,3},... | collective-permute-start | bytes 196616 | tf_op jit(solution)/shard_map/ppermute | solution.py:414
  42.5 1.4 %collective-permute-start.15 = (bf16[2,32,512]{2,1,0:T(8,128)(2,1)S(1)}, bf16[2,32,512]{2,1,0:T(8,128)(2,1)S(1)}, u32[]{:S(2)}, u32[]{:S(2)}) collective-permute-start(bf16[2,32,512]{2,1,0:T(8,128)(2,1)S(1)} %get-tuple-element.54), channel_id=1, source_target_pairs={{0,14},{1,15},{2,12},{3,13},{4,10},{5,11},{6,8},{7,9},{8,6},{9,7},... | collective-permute-start | bytes 196616 | tf_op jit(solution)/shard_map/ppermute | solution.py:414
  44.1 3.0 %collective-permute-done.13.refs_1_ = bf16[2,32,512]{2,1,0:T(8,128)(2,1)S(1)} collective-permute-done((bf16[2,32,512]{2,1,0:T(8,128)(2,1)S(1)}, bf16[2,32,512]{2,1,0:T(8,128)(2,1)S(1)}, u32[]{:S(2)}, u32[]{:S(2)}) %collective-permute-start.13) | collective-permute-done | bytes 65568 | tf_op jit(solution)/shard_map/ppermute | solution.py:414
  47.1 1.1 %collective-permute-done.14.refs_2_ = bf16[2,32,512]{2,1,0:T(8,128)(2,1)S(1)} collective-permute-done((bf16[2,32,512]{2,1,0:T(8,128)(2,1)S(1)}, bf16[2,32,512]{2,1,0:T(8,128)(2,1)S(1)}, u32[]{:S(2)}, u32[]{:S(2)}) %collective-permute-start.14) | collective-permute-done | bytes 65568 | tf_op jit(solution)/shard_map/ppermute | solution.py:414
  48.2 1.4 %collective-permute-done.15.refs_3_ = bf16[2,32,512]{2,1,0:T(8,128)(2,1)S(1)} collective-permute-done((bf16[2,32,512]{2,1,0:T(8,128)(2,1)S(1)}, bf16[2,32,512]{2,1,0:T(8,128)(2,1)S(1)}, u32[]{:S(2)}, u32[]{:S(2)}) %collective-permute-start.15) | collective-permute-done | bytes 65568 | tf_op jit(solution)/shard_map/ppermute | solution.py:414
  50.1 1.5 %collective-permute-done.18.refs_7_ = bf16[8,32,512]{2,1,0:T(8,128)(2,1)S(1)} collective-permute-done((bf16[8,32,512]{2,1,0:T(8,128)(2,1)S(1)}, bf16[8,32,512]{2,1,0:T(8,128)(2,1)S(1)}, u32[]{:S(2)}, u32[]{:S(2)}) %collective-permute-start.18) | collective-permute-done | bytes 262176 | tf_op jit(solution)/shard_map/ppermute | solution.py:414
  52.1 1.4 %terms.3 = (f32[32,3584]{1,0:T(8,128)S(1)}, bf16[32,3584]{1,0:T(8,128)(2,1)S(1)}) custom-call(bf16[64,1024]{1,0:T(8,128)(2,1)S(1)} %values.1.val_ref, bf16[1024,7168]{1,0:T(8,128)(2,1)S(1)} %bitcast.2), custom_call_target="tpu_custom_call" | custom-call | flops 6899999744 | tf_op jit(solution)/shard_map/terms/pallas_call | solution.py:37
  53.7 1.4 %terms.2 = (f32[32,3584]{1,0:T(8,128)S(1)}, bf16[32,3584]{1,0:T(8,128)(2,1)S(1)}) custom-call(bf16[64,1024]{1,0:T(8,128)(2,1)S(1)} %values.1.val_ref, bf16[1024,7168]{1,0:T(8,128)(2,1)S(1)} %bitcast.2), custom_call_target="tpu_custom_call" | custom-call | flops 6899999744 | tf_op jit(solution)/shard_map/terms/pallas_call | solution.py:37
  55.6 1.1 %collective-permute-start.24 = (bf16[8,3584]{1,0:T(8,128)(2,1)S(1)}, bf16[8,3584]{1,0:T(8,128)(2,1)S(1)}, u32[]{:S(2)}, u32[]{:S(2)}) collective-permute-start(bf16[8,3584]{1,0:T(8,128)(2,1)S(1)} %get-tuple-element.69), channel_id=1, source_target_pairs={{0,2},{1,3},{2,0},{3,1},{4,6},{5,7},{6,4},{7,5},{8,10},{9,11},{10,... | collective-permute-start | bytes 172040 | tf_op jit(solution)/shard_map/ppermute | solution.py:414
  56.8 1.1 %collective-permute-start.25 = (bf16[8,3584]{1,0:T(8,128)(2,1)S(1)}, bf16[8,3584]{1,0:T(8,128)(2,1)S(1)}, u32[]{:S(2)}, u32[]{:S(2)}) collective-permute-start(bf16[8,3584]{1,0:T(8,128)(2,1)S(1)} %get-tuple-element.70), channel_id=1, source_target_pairs={{0,2},{1,3},{2,0},{3,1},{4,6},{5,7},{6,4},{7,5},{8,10},{9,11},{10,... | collective-permute-start | bytes 172040 | tf_op jit(solution)/shard_map/ppermute | solution.py:414
  58.1 2.2 %collective-permute-start.22 = (bf16[4,7168]{1,0:T(4,128)(2,1)S(1)}, bf16[4,7168]{1,0:T(4,128)(2,1)S(1)}, u32[]{:S(2)}, u32[]{:S(2)}) collective-permute-start(bf16[4,7168]{1,0:T(4,128)(2,1)S(1)} %get-tuple-element.65), channel_id=1, source_target_pairs={{0,6},{1,7},{2,4},{3,5},{4,2},{5,3},{6,0},{7,1},{8,14},{9,15},{10,... | collective-permute-start | bytes 172040 | tf_op jit(solution)/shard_map/ppermute | solution.py:414
  60.3 1.0 %collective-permute-start.23 = (bf16[4,7168]{1,0:T(4,128)(2,1)S(1)}, bf16[4,7168]{1,0:T(4,128)(2,1)S(1)}, u32[]{:S(2)}, u32[]{:S(2)}) collective-permute-start(bf16[4,7168]{1,0:T(4,128)(2,1)S(1)} %get-tuple-element.66), channel_id=1, source_target_pairs={{0,2},{1,3},{2,0},{3,1},{4,6},{5,7},{6,4},{7,5},{8,10},{9,11},{10,... | collective-permute-start | bytes 172040 | tf_op jit(solution)/shard_map/ppermute | solution.py:414
  61.4 2.1 %collective-permute-start.26 = (bf16[4,7168]{1,0:T(4,128)(2,1)S(1)}, bf16[4,7168]{1,0:T(4,128)(2,1)S(1)}, u32[]{:S(2)}, u32[]{:S(2)}) collective-permute-start(bf16[4,7168]{1,0:T(4,128)(2,1)S(1)} %get-tuple-element.71), channel_id=1, source_target_pairs={{0,12},{1,13},{2,14},{3,15},{4,8},{5,9},{6,10},{7,11},{8,4},{9,5},... | collective-permute-start | bytes 172040 | tf_op jit(solution)/shard_map/ppermute | solution.py:414
  63.5 1.0 %collective-permute-done.23.refs_3_ = bf16[4,7168]{1,0:T(4,128)(2,1)S(1)} collective-permute-done((bf16[4,7168]{1,0:T(4,128)(2,1)S(1)}, bf16[4,7168]{1,0:T(4,128)(2,1)S(1)}, u32[]{:S(2)}, u32[]{:S(2)}) %collective-permute-start.23) | collective-permute-done | bytes 57376 | tf_op jit(solution)/shard_map/ppermute | solution.py:414
  64.5 2.9 %collective-permute-done.26.refs_4_ = bf16[4,7168]{1,0:T(4,128)(2,1)S(1)} collective-permute-done((bf16[4,7168]{1,0:T(4,128)(2,1)S(1)}, bf16[4,7168]{1,0:T(4,128)(2,1)S(1)}, u32[]{:S(2)}, u32[]{:S(2)}) %collective-permute-start.26) | collective-permute-done | bytes 57376 | tf_op jit(solution)/shard_map/ppermute | solution.py:414
  67.4 1.6 %collective-permute-done.27.refs_5_ = bf16[4,7168]{1,0:T(4,128)(2,1)S(1)} collective-permute-done((bf16[4,7168]{1,0:T(4,128)(2,1)S(1)}, bf16[4,7168]{1,0:T(4,128)(2,1)S(1)}, u32[]{:S(2)}, u32[]{:S(2)}) %collective-permute-start.27) | collective-permute-done | bytes 57376 | tf_op jit(solution)/shard_map/ppermute | solution.py:414
  (71 shorter events, 6.0 us)
Async XLA Ops:
  0.0 14.2 %collective-permute-start.4 = (bf16[1536,1536]{1,0:T(8,128)(2,1)}, bf16[1536,1536]{1,0:T(8,128)(2,1)S(1)}, u32[]{:S(2)}, u32[]{:S(2)}) collective-permute-start(bf16[1536,1536]{1,0:T(8,128)(2,1)} %refs_4_.1), channel_id=1, source_target_pairs={{0,1},{1,0},{2,3},{3,2},{4,5},{5,4},{6,7},{7,6},{8,9},{9,8},{10,11... | collective-permute-start | bytes 14155784 | tf_op jit(solution)/shard_map/ppermute | solution.py:414
  0.5 13.7 %collective-permute-start.5 = (bf16[8,128,512]{2,1,0:T(8,128)(2,1)}, bf16[8,128,512]{2,1,0:T(8,128)(2,1)S(1)}, u32[]{:S(2)}, u32[]{:S(2)}) collective-permute-start(bf16[8,128,512]{2,1,0:T(8,128)(2,1)} %refs_5_.1), channel_id=1, source_target_pairs={{0,1},{1,0},{2,3},{3,2},{4,5},{5,4},{6,7},{7,6},{8,9},{9,8},{10,11... | collective-permute-start | bytes 3145736 | tf_op jit(solution)/shard_map/ppermute | solution.py:414
  0.5 4.8 %collective-permute-start = (bf16[4,1536]{1,0:T(4,128)(2,1)}, bf16[4,1536]{1,0:T(4,128)(2,1)S(1)}, u32[]{:S(2)}, u32[]{:S(2)}) collective-permute-start(bf16[4,1536]{1,0:T(4,128)(2,1)} %refs_0_.1), channel_id=1, source_target_pairs={{0,2},{1,3},{2,0},{3,1},{4,6},{5,7},{6,4},{7,5},{8,10},{9,11},{10,... | collective-permute-start | bytes 36872 | tf_op jit(solution)/shard_map/ppermute | solution.py:414
  4.1 10.1 %slice-start.6 = ((s8[4718592]{0:T(1024)(128)(4,1)}), s8[4194304]{0:T(1024)(128)(4,1)S(1)}, s32[]{:S(2)}) async-start(s8[4718592]{0:T(1024)(128)(4,1)} %bitcast.7), calls=%async_computation.6 | async-start | bytes 8388608
  5.4 8.9 %copy-start = (bf16[8,128,512]{2,1,0:T(8,128)(2,1)S(1)}, bf16[8,128,512]{2,1,0:T(8,128)(2,1)}, u32[]{:S(2)}) copy-start(bf16[8,128,512]{2,1,0:T(8,128)(2,1)} %refs_5_.1) | copy-start | bytes 3145732
  5.4 20.5 %slice-start.4 = ((s8[7077888]{0:T(1024)(128)(4,1)}), s8[4194304]{0:T(1024)(128)(4,1)S(1)}, s32[]{:S(2)}) async-start(s8[7077888]{0:T(1024)(128)(4,1)} %bitcast.3), calls=%async_computation.4 | async-start | bytes 8388608
  5.4 20.5 %slice-start.5 = ((s8[7077888]{0:T(1024)(128)(4,1)}), s8[2883584]{0:T(1024)(128)(4,1)S(1)}, s32[]{:S(2)}) async-start(s8[7077888]{0:T(1024)(128)(4,1)} %bitcast.3), calls=%async_computation.5 | async-start | bytes 5767168
  5.4 5.0 %collective-permute-start.3 = (bf16[8,1536]{1,0:T(8,128)(2,1)S(1)}, bf16[8,1536]{1,0:T(8,128)(2,1)S(1)}, u32[]{:S(2)}, u32[]{:S(2)}) collective-permute-start(bf16[8,1536]{1,0:T(8,128)(2,1)S(1)} %get-tuple-element.43.refs_0_), channel_id=1, source_target_pairs={{0,8},{1,9},{2,10},{3,11},{4,12},{5,13},{6,14},{7,15},{8,0},{9,1},... | collective-permute-start | bytes 73736 | tf_op jit(solution)/shard_map/ppermute | solution.py:414
  8.6 5.6 %collective-permute-start.2 = (bf16[8,1536]{1,0:T(8,128)(2,1)S(1)}, bf16[8,1536]{1,0:T(8,128)(2,1)S(1)}, u32[]{:S(2)}, u32[]{:S(2)}) collective-permute-start(bf16[8,1536]{1,0:T(8,128)(2,1)S(1)} %get-tuple-element.43.refs_0_), channel_id=1, source_target_pairs={{0,12},{1,13},{2,14},{3,15},{4,8},{5,9},{6,10},{7,11},{8,4},{9,5},... | collective-permute-start | bytes 73736 | tf_op jit(solution)/shard_map/ppermute | solution.py:414
  9.9 4.3 %collective-permute-start.1 = (bf16[8,1536]{1,0:T(8,128)(2,1)S(1)}, bf16[8,1536]{1,0:T(8,128)(2,1)S(1)}, u32[]{:S(2)}, u32[]{:S(2)}) collective-permute-start(bf16[8,1536]{1,0:T(8,128)(2,1)S(1)} %get-tuple-element.43.refs_0_), channel_id=1, source_target_pairs={{0,4},{1,5},{2,6},{3,7},{4,0},{5,1},{6,2},{7,3},{8,12},{9,13},{10,... | collective-permute-start | bytes 73736 | tf_op jit(solution)/shard_map/ppermute | solution.py:414
  16.5 9.2 %collective-permute-start.6 = (bf16[4,144,128]{2,1,0:T(8,128)(2,1)S(1)}, bf16[4,144,128]{2,1,0:T(8,128)(2,1)S(1)}, u32[]{:S(2)}, u32[]{:S(2)}) collective-permute-start(bf16[4,144,128]{2,1,0:T(8,128)(2,1)S(1)} %get-tuple-element.45), channel_id=1, source_target_pairs={{0,2},{1,3},{2,0},{3,1},{4,6},{5,7},{6,4},{7,5},{8,10},{9,11},{10,... | collective-permute-start | bytes 442376 | tf_op jit(solution)/shard_map/ppermute | solution.py:414
  18.1 9.5 %collective-permute-start.7 = (bf16[2,144,128]{2,1,0:T(8,128)(2,1)S(1)}, bf16[2,144,128]{2,1,0:T(8,128)(2,1)S(1)}, u32[]{:S(2)}, u32[]{:S(2)}) collective-permute-start(bf16[2,144,128]{2,1,0:T(8,128)(2,1)S(1)} %get-tuple-element.46), channel_id=1, source_target_pairs={{0,12},{1,13},{2,14},{3,15},{4,8},{5,9},{6,10},{7,11},{8,4},{9,5},... | collective-permute-start | bytes 221192 | tf_op jit(solution)/shard_map/ppermute | solution.py:414
  20.1 8.3 %collective-permute-start.8 = (bf16[2,144,128]{2,1,0:T(8,128)(2,1)S(1)}, bf16[2,144,128]{2,1,0:T(8,128)(2,1)S(1)}, u32[]{:S(2)}, u32[]{:S(2)}) collective-permute-start(bf16[2,144,128]{2,1,0:T(8,128)(2,1)S(1)} %get-tuple-element.47), channel_id=1, source_target_pairs={{0,8},{1,9},{2,10},{3,11},{4,12},{5,13},{6,14},{7,15},{8,0},{9,1},... | collective-permute-start | bytes 221192 | tf_op jit(solution)/shard_map/ppermute | solution.py:414
  20.1 10.8 %collective-permute-start.9 = (bf16[2,144,128]{2,1,0:T(8,128)(2,1)S(1)}, bf16[2,144,128]{2,1,0:T(8,128)(2,1)S(1)}, u32[]{:S(2)}, u32[]{:S(2)}) collective-permute-start(bf16[2,144,128]{2,1,0:T(8,128)(2,1)S(1)} %get-tuple-element.48), channel_id=1, source_target_pairs={{0,10},{1,11},{2,8},{3,9},{4,14},{5,15},{6,12},{7,13},{8,2},{9,3},... | collective-permute-start | bytes 221192 | tf_op jit(solution)/shard_map/ppermute | solution.py:414
  23.0 7.9 %collective-permute-start.10 = (bf16[2,144,128]{2,1,0:T(8,128)(2,1)S(1)}, bf16[2,144,128]{2,1,0:T(8,128)(2,1)S(1)}, u32[]{:S(2)}, u32[]{:S(2)}) collective-permute-start(bf16[2,144,128]{2,1,0:T(8,128)(2,1)S(1)} %get-tuple-element.49), channel_id=1, source_target_pairs={{0,14},{1,15},{2,12},{3,13},{4,10},{5,11},{6,8},{7,9},{8,6},{9,7},... | collective-permute-start | bytes 221192 | tf_op jit(solution)/shard_map/ppermute | solution.py:414
  25.8 6.3 %collective-permute-start.11 = (bf16[4,144,128]{2,1,0:T(8,128)(2,1)S(1)}, bf16[4,144,128]{2,1,0:T(8,128)(2,1)S(1)}, u32[]{:S(2)}, u32[]{:S(2)}) collective-permute-start(bf16[4,144,128]{2,1,0:T(8,128)(2,1)S(1)} %forward.2.after_ref), channel_id=1, source_target_pairs={{0,4},{1,5},{2,6},{3,7},{4,0},{5,1},{6,2},{7,3},{8,12},{9,13},{10,... | collective-permute-start | bytes 442376 | tf_op jit(solution)/shard_map/ppermute | solution.py:414
  35.5 8.4 %collective-permute-start.16 = (bf16[4,32,512]{2,1,0:T(8,128)(2,1)S(1)}, bf16[4,32,512]{2,1,0:T(8,128)(2,1)S(1)}, u32[]{:S(2)}, u32[]{:S(2)}) collective-permute-start(bf16[4,32,512]{2,1,0:T(8,128)(2,1)S(1)} %get-tuple-element.55), channel_id=1, source_target_pairs={{0,2},{1,3},{2,0},{3,1},{4,6},{5,7},{6,4},{7,5},{8,10},{9,11},{10,... | collective-permute-start | bytes 393224 | tf_op jit(solution)/shard_map/ppermute | solution.py:414
  36.3 7.8 %collective-permute-start.12 = (bf16[2,32,512]{2,1,0:T(8,128)(2,1)S(1)}, bf16[2,32,512]{2,1,0:T(8,128)(2,1)S(1)}, u32[]{:S(2)}, u32[]{:S(2)}) collective-permute-start(bf16[2,32,512]{2,1,0:T(8,128)(2,1)S(1)} %get-tuple-element.51), channel_id=1, source_target_pairs={{0,12},{1,13},{2,14},{3,15},{4,8},{5,9},{6,10},{7,11},{8,4},{9,5},... | collective-permute-start | bytes 196616 | tf_op jit(solution)/shard_map/ppermute | solution.py:414
  38.6 8.5 %collective-permute-start.13 = (bf16[2,32,512]{2,1,0:T(8,128)(2,1)S(1)}, bf16[2,32,512]{2,1,0:T(8,128)(2,1)S(1)}, u32[]{:S(2)}, u32[]{:S(2)}) collective-permute-start(bf16[2,32,512]{2,1,0:T(8,128)(2,1)S(1)} %get-tuple-element.52), channel_id=1, source_target_pairs={{0,8},{1,9},{2,10},{3,11},{4,12},{5,13},{6,14},{7,15},{8,0},{9,1},... | collective-permute-start | bytes 196616 | tf_op jit(solution)/shard_map/ppermute | solution.py:414
  38.8 9.5 %collective-permute-start.14 = (bf16[2,32,512]{2,1,0:T(8,128)(2,1)S(1)}, bf16[2,32,512]{2,1,0:T(8,128)(2,1)S(1)}, u32[]{:S(2)}, u32[]{:S(2)}) collective-permute-start(bf16[2,32,512]{2,1,0:T(8,128)(2,1)S(1)} %get-tuple-element.53), channel_id=1, source_target_pairs={{0,10},{1,11},{2,8},{3,9},{4,14},{5,15},{6,12},{7,13},{8,2},{9,3},... | collective-permute-start | bytes 196616 | tf_op jit(solution)/shard_map/ppermute | solution.py:414
  42.5 7.1 %collective-permute-start.15 = (bf16[2,32,512]{2,1,0:T(8,128)(2,1)S(1)}, bf16[2,32,512]{2,1,0:T(8,128)(2,1)S(1)}, u32[]{:S(2)}, u32[]{:S(2)}) collective-permute-start(bf16[2,32,512]{2,1,0:T(8,128)(2,1)S(1)} %get-tuple-element.54), channel_id=1, source_target_pairs={{0,14},{1,15},{2,12},{3,13},{4,10},{5,11},{6,8},{7,9},{8,6},{9,7},... | collective-permute-start | bytes 196616 | tf_op jit(solution)/shard_map/ppermute | solution.py:414
  44.0 6.0 %collective-permute-start.17 = (bf16[4,32,512]{2,1,0:T(8,128)(2,1)S(1)}, bf16[4,32,512]{2,1,0:T(8,128)(2,1)S(1)}, u32[]{:S(2)}, u32[]{:S(2)}) collective-permute-start(bf16[4,32,512]{2,1,0:T(8,128)(2,1)S(1)} %forward.3.after_ref), channel_id=1, source_target_pairs={{0,4},{1,5},{2,6},{3,7},{4,0},{5,1},{6,2},{7,3},{8,12},{9,13},{10,... | collective-permute-start | bytes 393224 | tf_op jit(solution)/shard_map/ppermute | solution.py:414
  50.0 1.6 %collective-permute-start.18 = (bf16[8,32,512]{2,1,0:T(8,128)(2,1)S(1)}, bf16[8,32,512]{2,1,0:T(8,128)(2,1)S(1)}, u32[]{:S(2)}, u32[]{:S(2)}) collective-permute-start(bf16[8,32,512]{2,1,0:T(8,128)(2,1)S(1)} %regroup.1), channel_id=1, source_target_pairs={{0,1},{1,0},{2,3},{3,2},{4,5},{5,4},{6,7},{7,6},{8,9},{9,8},{10,11... | collective-permute-start | bytes 786440 | tf_op jit(solution)/shard_map/ppermute | solution.py:414
  53.5 2.0 %collective-permute-start.20 = (bf16[32,3584]{1,0:T(8,128)(2,1)S(1)}, bf16[32,3584]{1,0:T(8,128)(2,1)S(1)}, u32[]{:S(2)}, u32[]{:S(2)}) collective-permute-start(bf16[32,3584]{1,0:T(8,128)(2,1)S(1)} %get-tuple-element.61), channel_id=1, source_target_pairs={{0,1},{1,0},{2,3},{3,2},{4,5},{5,4},{6,7},{7,6},{8,9},{9,8},{10,11... | collective-permute-start | bytes 688136 | tf_op jit(solution)/shard_map/ppermute | solution.py:414
  55.1 1.6 %collective-permute-start.19 = (bf16[32,3584]{1,0:T(8,128)(2,1)S(1)}, bf16[32,3584]{1,0:T(8,128)(2,1)S(1)}, u32[]{:S(2)}, u32[]{:S(2)}) collective-permute-start(bf16[32,3584]{1,0:T(8,128)(2,1)S(1)} %get-tuple-element.59), channel_id=1, source_target_pairs={{0,1},{1,0},{2,3},{3,2},{4,5},{5,4},{6,7},{7,6},{8,9},{9,8},{10,11... | collective-permute-start | bytes 688136 | tf_op jit(solution)/shard_map/ppermute | solution.py:414
  55.6 5.7 %collective-permute-start.24 = (bf16[8,3584]{1,0:T(8,128)(2,1)S(1)}, bf16[8,3584]{1,0:T(8,128)(2,1)S(1)}, u32[]{:S(2)}, u32[]{:S(2)}) collective-permute-start(bf16[8,3584]{1,0:T(8,128)(2,1)S(1)} %get-tuple-element.69), channel_id=1, source_target_pairs={{0,2},{1,3},{2,0},{3,1},{4,6},{5,7},{6,4},{7,5},{8,10},{9,11},{10,... | collective-permute-start | bytes 172040 | tf_op jit(solution)/shard_map/ppermute | solution.py:414
  56.8 4.6 %collective-permute-start.25 = (bf16[8,3584]{1,0:T(8,128)(2,1)S(1)}, bf16[8,3584]{1,0:T(8,128)(2,1)S(1)}, u32[]{:S(2)}, u32[]{:S(2)}) collective-permute-start(bf16[8,3584]{1,0:T(8,128)(2,1)S(1)} %get-tuple-element.70), channel_id=1, source_target_pairs={{0,2},{1,3},{2,0},{3,1},{4,6},{5,7},{6,4},{7,5},{8,10},{9,11},{10,... | collective-permute-start | bytes 172040 | tf_op jit(solution)/shard_map/ppermute | solution.py:414
  57.8 5.6 %collective-permute-start.21 = (bf16[4,7168]{1,0:T(4,128)(2,1)S(1)}, bf16[4,7168]{1,0:T(4,128)(2,1)S(1)}, u32[]{:S(2)}, u32[]{:S(2)}) collective-permute-start(bf16[4,7168]{1,0:T(4,128)(2,1)S(1)} %get-tuple-element.64), channel_id=1, source_target_pairs={{0,4},{1,5},{2,6},{3,7},{4,0},{5,1},{6,2},{7,3},{8,12},{9,13},{10,... | collective-permute-start | bytes 172040 | tf_op jit(solution)/shard_map/ppermute | solution.py:414
  58.1 5.4 %collective-permute-start.22 = (bf16[4,7168]{1,0:T(4,128)(2,1)S(1)}, bf16[4,7168]{1,0:T(4,128)(2,1)S(1)}, u32[]{:S(2)}, u32[]{:S(2)}) collective-permute-start(bf16[4,7168]{1,0:T(4,128)(2,1)S(1)} %get-tuple-element.65), channel_id=1, source_target_pairs={{0,6},{1,7},{2,4},{3,5},{4,2},{5,3},{6,0},{7,1},{8,14},{9,15},{10,... | collective-permute-start | bytes 172040 | tf_op jit(solution)/shard_map/ppermute | solution.py:414
  60.3 4.2 %collective-permute-start.23 = (bf16[4,7168]{1,0:T(4,128)(2,1)S(1)}, bf16[4,7168]{1,0:T(4,128)(2,1)S(1)}, u32[]{:S(2)}, u32[]{:S(2)}) collective-permute-start(bf16[4,7168]{1,0:T(4,128)(2,1)S(1)} %get-tuple-element.66), channel_id=1, source_target_pairs={{0,2},{1,3},{2,0},{3,1},{4,6},{5,7},{6,4},{7,5},{8,10},{9,11},{10,... | collective-permute-start | bytes 172040 | tf_op jit(solution)/shard_map/ppermute | solution.py:414
  61.4 6.0 %collective-permute-start.26 = (bf16[4,7168]{1,0:T(4,128)(2,1)S(1)}, bf16[4,7168]{1,0:T(4,128)(2,1)S(1)}, u32[]{:S(2)}, u32[]{:S(2)}) collective-permute-start(bf16[4,7168]{1,0:T(4,128)(2,1)S(1)} %get-tuple-element.71), channel_id=1, source_target_pairs={{0,12},{1,13},{2,14},{3,15},{4,8},{5,9},{6,10},{7,11},{8,4},{9,5},... | collective-permute-start | bytes 172040 | tf_op jit(solution)/shard_map/ppermute | solution.py:414
  63.4 5.6 %collective-permute-start.27 = (bf16[4,7168]{1,0:T(4,128)(2,1)S(1)}, bf16[4,7168]{1,0:T(4,128)(2,1)S(1)}, u32[]{:S(2)}, u32[]{:S(2)}) collective-permute-start(bf16[4,7168]{1,0:T(4,128)(2,1)S(1)} %get-tuple-element.72), channel_id=1, source_target_pairs={{0,8},{1,9},{2,10},{3,11},{4,12},{5,13},{6,14},{7,15},{8,0},{9,1},... | collective-permute-start | bytes 172040 | tf_op jit(solution)/shard_map/ppermute | solution.py:414
  (10 other events, 60.9 us)
